TPU v7x, 32 devices: a whole 2x2x4 slice. The times are simulated.
32 devices in a mesh: groups: 2 (over y), row: 4 (over z), col: 2 (over x), depth: 2 (over core).
Axes of the slice: x: 2, y: 2, z: 4, core: 2. Of those that a mesh axis runs over, the one named last changes fastest.
Arguments:
- environment: bfloat16 [4, 2, 2048, 2048], P(('groups', 'depth'), None, 'row', 'col'), parts along dimension 0, may hold values from -6 to 6
- site_tensor: bfloat16 [4, 2048, 2, 2048], P('groups', 'row', None, 'col'), parts along dimension 0, may hold values from -0.09375 to 0.09375
- mpo: float32 [4, 2, 2, 2], P('groups'), parts along dimension 0, may hold values from -3 to 3
Outputs:
- new_environment: float32 [4, 2, 2048, 2048], P('groups', None, 'row', ('col', 'depth')), parts along dimension 0
There are 2 independent parts, one for each index of `groups`. A program takes and returns all parts, laid end to end along the dimension named above; each array names one. Nothing has to cross between parts.
All inputs are finite; a program needn't handle non-finite values.
Results may differ from a plain program's by a relative error of at most 0.003.
Values may be sent and summed in bfloat16 or wider, within the bound.
No kernel may reach another device: no remote copies, remote signals or barrier semaphores. Data moves between devices by JAX's collectives and lax.ppermute only.
A program may use at most 128 MiB of HBM per device.

v0:
```python
import jax
import jax.numpy as jnp
from jax import lax
from jax.sharding import PartitionSpec as P


def env_right(piece):
    real_part = piece[:, 0]
    imag_part = piece[:, 1]
    top_half = jnp.concatenate([real_part, imag_part], axis=2)
    low_half = jnp.concatenate([imag_part, -real_part], axis=2)
    return jnp.concatenate([top_half, low_half], axis=1)


def on_device(environment, site_tensor, mpo):
    highest = lax.Precision.HIGHEST
    w_local, col_count = (environment.shape[0], environment.shape[3])
    phys_count, row_count = (site_tensor.shape[0], site_tensor.shape[1])
    mpo_count = mpo.shape[1]
    depth_count = lax.axis_size("depth")
    t_local = phys_count // depth_count
    depth_pos = lax.axis_index("depth")
    t_first = depth_pos * t_local
    mpo_mine = lax.dynamic_slice_in_dim(mpo, depth_pos * w_local, w_local, 0)
    wide_site = lax.all_gather(site_tensor, "col", axis=3, tiled=True)
    own_site = lax.dynamic_slice_in_dim(site_tensor, t_first, t_local, 0)
    piece = lax.all_gather(environment, "row", axis=2, tiled=True)
    piece_rows = piece.shape[2]
    site_block = wide_site
    site_block = site_block.reshape(phys_count * row_count, 2 * piece_rows)
    contracted = jnp.einsum(
        "mk,wkn->wmn", site_block, env_right(piece), preferred_element_type=jnp.float32
    )
    g_local = contracted.reshape(w_local, phys_count, row_count, 2, col_count)
    g_local = jnp.transpose(g_local, (0, 1, 3, 2, 4))
    q_terms = jnp.einsum("wvst,wspxc->vtpxc", mpo_mine, g_local, precision=highest)
    q_mine = lax.psum_scatter(q_terms, "depth", scatter_dimension=1, tiled=True)
    q_low = q_mine.astype(jnp.bfloat16)
    q_real = q_low[:, :, 0]
    q_imag = q_low[:, :, 1]
    real_rows = jnp.stack([q_real, -q_imag], axis=2)
    imag_rows = jnp.stack([q_imag, q_real], axis=2)
    left_q = jnp.stack([real_rows, imag_rows], axis=1)
    left_q = jnp.transpose(left_q, (0, 1, 4, 2, 3, 5))
    left_q = left_q.reshape(mpo_count * 2 * row_count, t_local, 2, col_count)
    partial_env = lax.dot_general(
        left_q,
        lax.all_gather(own_site, "row", axis=1, tiled=True),
        (((1, 2, 3), (0, 2, 3)), ((), ())),
        preferred_element_type=jnp.float32,
    )
    partial_env = partial_env.reshape(mpo_count, 2, row_count, partial_env.shape[1])
    return lax.psum_scatter(partial_env, ("col", "depth"), scatter_dimension=3, tiled=True)


def solution(mesh):
    placed = (
        P(("groups", "depth"), None, "row", "col"),
        P("groups", "row", None, "col"),
        P("groups", None, None, None),
    )
    return jax.shard_map(
        on_device,
        mesh=mesh,
        in_specs=placed,
        out_specs=P("groups", None, "row", ("col", "depth")),
        check_vma=False,
    )
```

profile of v0, /device:TPU:1, one launch (start us, length us, event | category | flops | bytes accessed | tf_op | source)
XLA Modules:
  0.0 740.5 jit_solution(4638841427905685294)
XLA Ops:
  6.5 0.0 copy-start
  6.5 0.0 all-gather.6.cloned.1.call-start
  6.5 0.7 all-gather.6.cloned.1.call-update
  7.3 0.0 all-gather.4.cloned.1.call-start
  7.3 0.7 all-gather.4.cloned.1.call-update
  8.0 0.0 reduce-scatter.3.cloned.1.call-start
  8.1 106.9 %all-gather.6.cloned.1.call-done = bf16[2,512,2,2048]{3,2,1,0:T(2,128)(2,1)} async-done(((bf16[2,512,2,1024]{3,2,1,0:T(2,128)(2,1)}), bf16[2,512,2,2048]{3,2,1,0:T(2,128)(2,1)}) %all-gather.6.cloned.1.call-update) | async-done | bytes 8388624 | tf_op jit(solution)/shard_map/all_gather | solution.py:25
  115.0 12.6 %copy.32 = bf16[128,8,2,2048]{3,1,2,0:T(8,128)(2,1)} copy(bf16[128,8,2,2048]{3,2,1,0:T(2,128)(2,1)} %bitcast.65) | data formatting | bytes 16777216
  127.6 138.8 %all-gather.4.cloned.1.call-done = bf16[1,2,2048,1024]{3,2,1,0:T(8,128)(2,1)} async-done(((bf16[1,2,512,1024]{3,2,1,0:T(8,128)(2,1)}), bf16[1,2,2048,1024]{3,2,1,0:T(8,128)(2,1)}) %all-gather.4.cloned.1.call-update) | async-done | bytes 8388624 | tf_op jit(solution)/shard_map/all_gather | solution.py:27
  266.4 0.0 copy-start.2
  266.4 7.0 slice_bitcast_fusion.1
  273.4 1.8 copy-done.2
  275.2 2.3 fusion.22
  277.5 33.1 %fusion.16 = f32[1,1024,2048]{1,2,0:T(8,128)} fusion(bf16[1024,4096]{1,0:T(8,128)(2,1)} %bitcast.66, bf16[1,2048,1024]{2,1,0:T(8,128)(2,1)} %fusion.22, bf16[1,2048,1024]{2,1,0:T(8,128)(2,1)} %get-tuple-element.6, bf16[1,2048,1024]{2,1,0:T(8,128)(2,1)} %get-tuple-element.5), kind=kOutput, calls=%fused_computation.16 | convolution fusion | flops 17246978048 | bytes 29360128 | tf_op jit(solution)/shard_map/mk,wkn->wmn/dot_general | solution.py:31
  310.5 11.8 %reshape.43 = f32[1,2,512,2,1024]{2,1,4,3,0:T(2,128)} reshape(f32[1,1024,2048]{1,2,0:T(8,128)} %fusion.16) | data formatting | bytes 16777216 | tf_op jit(solution)/shard_map/reshape | solution.py:34
  322.3 17.1 %copy.20 = f32[1,2,512,2,1024]{4,1,2,3,0:T(2,128)} copy(f32[1,2,512,2,1024]{2,1,4,3,0:T(2,128)} %reshape.43) | data formatting | bytes 16777216 | tf_op jit(solution)/shard_map/reshape | solution.py:34
  339.4 0.0 copy-done
  339.4 58.0 %fusion.11 = f32[2,2,2,512,1024]{4,1,3,2,0:T(2,128)S(1)} fusion(f32[1,2,512,2,1024]{4,1,2,3,0:T(2,128)} %copy.20, f32[2,2,2,2]{3,2,1,0:T(2,128)S(1)} %copy-done, s32[]{:T(128)S(6)} %select_n.4), kind=kOutput, calls=%fused_computation.13 | convolution fusion | flops 100663296 | bytes 25167876 | tf_op jit(solution)/shard_map/wvst,wspxc->vtpxc/dot_general | solution.py:36
  397.4 11.0 %copy.22 = f32[2,2,2,512,1024]{4,3,2,0,1:T(8,128)} copy(f32[2,2,2,512,1024]{4,1,3,2,0:T(2,128)S(1)} %fusion.11) | data formatting | bytes 33554432 | tf_op jit(solution)/shard_map/wvst,wspxc->vtpxc/dot_general | solution.py:36
  408.3 0.0 reduce-scatter.3.cloned.1.call-update
  408.4 0.0 all-gather.8.cloned.1.call-start
  408.4 3.0 constant_dynamic-slice_fusion
  411.5 1.9 copy.31
  413.4 0.0 all-gather.8.cloned.1.call-update
  413.4 0.0 reduce-scatter.5.cloned.1.call-start
  413.5 19.7 %reduce-scatter.3.cloned.1.call-done = f32[2,1,2,512,1024]{4,3,2,0,1:T(8,128)} async-done(((f32[2,2,2,512,1024]{4,3,2,0,1:T(8,128)}), f32[2,1,2,512,1024]{4,3,2,0,1:T(8,128)}) %reduce-scatter.3.cloned.1.call-update) | async-done | bytes 8388624 | tf_op jit(solution)/shard_map/reduce_scatter | solution.py:37
  433.2 4.0 convert_element_type.3
  437.2 0.4 slice_negate_fusion
  437.7 4.0 maximum_bitcast_fusion.8
  441.6 143.8 %all-gather.8.cloned.1.call-done = bf16[1,2048,2,1024]{3,1,2,0:T(8,128)(2,1)} async-done(((bf16[1,512,2,1024]{3,1,2,0:T(8,128)(2,1)}), bf16[1,2048,2,1024]{3,1,2,0:T(8,128)(2,1)}) %all-gather.8.cloned.1.call-update) | async-done | bytes 8388624 | tf_op jit(solution)/shard_map/all_gather | solution.py:48
  585.4 24.4 %fusion.13 = f32[2,2,512,2048]{3,2,1,0:T(8,128)} fusion(bf16[1,2048,2,1024]{3,1,2,0:T(8,128)(2,1)} %all-gather.8.cloned.1.call-done, bf16[2,1,1,2,512,1024]{5,4,3,1,0,2:T(8,128)(2,1)} %get-tuple-element.11, bf16[2,1,1,2,512,1024]{5,4,3,1,0,2:T(8,128)(2,1)} %get-tuple-element.10), kind=kOutput, calls=%fused_computation.15 | convolution fusion | flops 17184063488 | bytes 33554432 | tf_op jit(solution)/shard_map/dot_general | solution.py:46
  609.8 0.0 reduce-scatter.5.cloned.1.call-update
  609.8 0.0 copy-start.1
  609.8 124.2 %reduce-scatter.5.cloned.1.call-done = f32[2,2,512,512]{3,2,1,0:T(8,128)} async-done(((f32[2,2,512,2048]{3,2,1,0:T(8,128)}), f32[2,2,512,512]{3,2,1,0:T(8,128)}) %reduce-scatter.5.cloned.1.call-update) | async-done | bytes 4194320 | tf_op jit(solution)/shard_map/reduce_scatter | solution.py:53
  734.0 0.0 copy-done.1
Async XLA Ops:
  6.5 332.9 %copy-start = (f32[2,2,2,2]{3,2,1,0:T(2,128)S(1)}, f32[2,2,2,2]{3,2,1,0:T(2,128)}, u32[]{:S(2)}) copy-start(f32[2,2,2,2]{3,2,1,0:T(2,128)} %param.5) | copy-start | bytes 196
  6.5 108.4 %all-gather.6.cloned.1.call-start = ((), (), s32[]{:S(2)}) async-start(), calls=%async_computation.3 | async-start | bytes 12582912 | tf_op jit(solution)/shard_map/all_gather | solution.py:25
  7.3 259.2 %all-gather.4.cloned.1.call-start = ((), (), s32[]{:S(2)}) async-start(), calls=%async_computation.2 | async-start | bytes 10485760 | tf_op jit(solution)/shard_map/all_gather | solution.py:27
  8.0 425.2 %reduce-scatter.3.cloned.1.call-start = ((), (), s32[]{:S(2)}) async-start(), calls=%async_computation.4 | async-start | bytes 25165824 | tf_op jit(solution)/shard_map/reduce_scatter | solution.py:37
  266.4 8.8 %copy-start.2 = (bf16[1,2,2048,1024]{3,2,1,0:T(8,128)(2,1)S(1)}, bf16[1,2,2048,1024]{3,2,1,0:T(8,128)(2,1)}, u32[]{:S(2)}) copy-start(bf16[1,2,2048,1024]{3,2,1,0:T(8,128)(2,1)} %all-gather.4.cloned.1.call-done) | copy-start | bytes 25165828
  408.4 177.0 %all-gather.8.cloned.1.call-start = ((), (), s32[]{:S(2)}) async-start(), calls=%async_computation.5 | async-start | bytes 10485760 | tf_op jit(solution)/shard_map/all_gather | solution.py:48
  413.4 320.6 %reduce-scatter.5.cloned.1.call-start = ((), (), s32[]{:S(2)}) async-start(), calls=%async_computation.6 | async-start | bytes 20971520 | tf_op jit(solution)/shard_map/reduce_scatter | solution.py:53
  609.8 124.2 %copy-start.1 = (f32[2,2,2,2]{3,2,1,0:T(2,128)S(1)}, f32[2,2,2,2]{3,2,1,0:T(2,128)}, u32[]{:S(2)}) copy-start(f32[2,2,2,2]{3,2,1,0:T(2,128)} %param.5) | copy-start | bytes 196
Sparse Core Ops, SparseCore 0:
  8.9 106.0 all-gather.5
  116.5 149.8 all-gather.3
  408.5 24.6 reduce-scatter.2
  434.7 150.6 all-gather.7
  609.9 124.0 reduce-scatter.4
where the time goes:
time: 742 us; the launch traced here: 741 us
  waiting for transfers between devices  535 us (72%)
  matrix products  115 us (15%)
  local copies, waits for them, and re-layouts  66.2 us (9%)
  between operations  13.2 us (2%)
  other arithmetic  10.7 us (1%)
    all_gather x1, waiting for transfers between devices, on_device(): lax.all_gather(own_site, 'row', axis=1, tiled=True)  144 us
    all_gather x1, waiting for transfers between devices, on_device(): piece = lax.all_gather(environment, 'row', axis=2, tiled=True)  139 us
    reduce_scatter x1, waiting for transfers between devices, on_device(): lax.psum_scatter(partial_env, ('col', 'depth'), scatter_dimension=3, tile...  124 us
    all_gather x1, waiting for transfers between devices, on_device(): wide_site = lax.all_gather(site_tensor, 'col', axis=3, tiled=True)  107 us
    dot_general x1, matrix products, on_device(): jnp.einsum('wvst,wspxc->vtpxc', mpo_mine, g_local, precision=highest)  58 us
    dot_general x1, matrix products, on_device(): jnp.einsum('mk,wkn->wmn', site_block, env_right(piece), preferred_element...  33.1 us
    reshape x2, local copies, waits for them, and re-layouts, on_device(): g_local = contracted.reshape(w_local, phys_count, row_count, 2, col_count)  28.9 us
    dot_general x1, matrix products, on_device(): lax.dot_general(left_q, lax.all_gather(own_site, 'row', axis=1, tiled=Tru...  24.4 us
  transfers between devices with their start and end apart: 5, of which 5 were waited for; matrix products, arithmetic and copies ran while one was open for 4% of the time, Pallas kernels for 0%

commit v1 on v0

v1 whole, which is shorter than its diff:
```python
from functools import partial
import jax
import jax.numpy as jnp
from jax import lax
from jax.experimental import pallas as pl
from jax.experimental.pallas import tpu as pltpu
from jax.sharding import PartitionSpec as P

F32 = jnp.float32
BF16 = jnp.bfloat16
VMEM_BYTES = 48 * 1024 * 1024


def params(steps):
    return pltpu.CompilerParams(
        dimension_semantics=("arbitrary",) * steps, vmem_limit_bytes=VMEM_BYTES
    )


def mul(left, right):
    return jnp.dot(left, right, preferred_element_type=F32)


def mul_t(left, right):
    return lax.dot_general(left, right, (((1,), (1,)), ((), ())), preferred_element_type=F32)


def first_kernel(site_ref, own_ref, sib_ref, *rest):
    out_ref = rest[-1]
    real, imag = site_ref[0, 0], site_ref[0, 1]
    for which, env_ref in enumerate((own_ref, sib_ref)):
        env_real, env_imag = env_ref[0, 0], env_ref[0, 1]
        g_real = mul(real, env_real) + mul(imag, env_imag)
        g_imag = mul(real, env_imag) - mul(imag, env_real)
        if len(rest) == 2:
            g_real = g_real + rest[0][which, 0, 0, 0]
            g_imag = g_imag + rest[0][which, 0, 0, 1]
        out_ref[which, 0, 0, 0] = g_real
        out_ref[which, 0, 0, 1] = g_imag


def first_product(site, own, sib, total):
    phys, _, rows, depth = site.shape
    w_local, _, _, cols = own.shape
    total_spec = pl.BlockSpec((2, 1, 1, 2, rows, cols), lambda s, w: (0, w, s, 0, 0, 0))
    env_spec = pl.BlockSpec((1, 2, depth, cols), lambda s, w: (w, 0, 0, 0))
    args = (site, own, sib) + (() if total is None else (total,))
    shape = (2, w_local, phys, 2, rows, cols)
    return pl.pallas_call(
        first_kernel,
        grid=(phys, w_local),
        in_specs=[pl.BlockSpec((1, 2, rows, depth), lambda s, w: (s, 0, 0, 0)), env_spec, env_spec]
        + ([] if total is None else [total_spec]),
        out_specs=total_spec,
        out_shape=jax.ShapeDtypeStruct(shape, F32),
        input_output_aliases={} if total is None else {3: 0},
        compiler_params=params(2),
        cost_estimate=pl.CostEstimate(
            flops=16 * w_local * phys * rows * depth * cols,
            bytes_accessed=32 * w_local * phys * rows * cols,
            transcendentals=0,
        ),
        name="first_product",
    )(*args)


def mix_kernel(mpo_ref, g_ref, q_ref):
    _, w_local, phys = g_ref.shape[:3]
    mpo_count = q_ref.shape[0]
    for v in range(mpo_count):
        for t in range(phys):
            total = None
            for which in range(2):
                for w in range(w_local):
                    for s in range(phys):
                        term = mpo_ref[which * w_local + w, v, s, t] * g_ref[which, w, s, 0]
                        total = term if total is None else total + term
            q_ref[v, t, 0] = total.astype(BF16)


def mix(mpo, g):
    _, w_local, phys, _, rows, cols = g.shape
    mpo_count = mpo.shape[1]
    tile = min(rows, 64)
    return pl.pallas_call(
        mix_kernel,
        grid=(2, rows // tile),
        in_specs=[
            pl.BlockSpec(memory_space=pltpu.SMEM),
            pl.BlockSpec((2, w_local, phys, 1, tile, cols), lambda p, i: (0, 0, 0, p, i, 0)),
        ],
        out_specs=pl.BlockSpec((mpo_count, phys, 1, tile, cols), lambda p, i: (0, 0, p, i, 0)),
        out_shape=jax.ShapeDtypeStruct((mpo_count, phys, 2, rows, cols), BF16),
        compiler_params=params(2),
        cost_estimate=pl.CostEstimate(
            flops=4 * w_local * phys * phys * mpo_count * 2 * rows * cols,
            bytes_accessed=g.size * 4 + mpo_count * phys * 4 * rows * cols,
            transcendentals=0,
        ),
        name="mix",
    )(mpo, g)


def second_kernel(q_ref, site_ref, wide_ref, low_ref):
    out_real, out_imag = 0.0, 0.0
    for t in range(q_ref.shape[1]):
        q_real, q_imag = q_ref[0, t, 0], q_ref[0, t, 1]
        real, imag = site_ref[t, 0], site_ref[t, 1]
        out_real += mul_t(q_real, real) - mul_t(q_imag, imag)
        out_imag += mul_t(q_real, imag) + mul_t(q_imag, real)
    wide_ref[0, 0] = out_real
    wide_ref[0, 1] = out_imag
    low_ref[0, 0] = out_real.astype(BF16)
    low_ref[0, 1] = out_imag.astype(BF16)


def second_product(q, site):
    mpo_count, phys, _, rows, cols = q.shape
    y_rows = site.shape[2]
    out_spec = pl.BlockSpec((1, 2, rows, y_rows), lambda v: (v, 0, 0, 0))
    shape = (mpo_count, 2, rows, y_rows)
    return pl.pallas_call(
        second_kernel,
        grid=(mpo_count,),
        in_specs=[
            pl.BlockSpec((1, phys, 2, rows, cols), lambda v: (v, 0, 0, 0, 0)),
            pl.BlockSpec((phys, 2, y_rows, cols), lambda v: (0, 0, 0, 0)),
        ],
        out_specs=[out_spec, out_spec],
        out_shape=[jax.ShapeDtypeStruct(shape, F32), jax.ShapeDtypeStruct(shape, BF16)],
        compiler_params=params(1),
        cost_estimate=pl.CostEstimate(
            flops=8 * mpo_count * phys * rows * y_rows * cols,
            bytes_accessed=q.size * 2 + site.size * 2 + 12 * mpo_count * rows * y_rows,
            transcendentals=0,
        ),
        name="second_product",
    )(q, site)


def after(value, *earlier):
    return lax.optimization_barrier((value,) + earlier)[0]


def shift(value, axis, count):
    return lax.ppermute(value, axis, [(i, (i + 1) % count) for i in range(count)])


def swap(value):
    return lax.ppermute(value, "depth", [(0, 1), (1, 0)])


def on_device(environment, site_tensor, mpo):
    row_count, col_count = lax.axis_size("row"), lax.axis_size("col")
    row, col, depth = (lax.axis_index(axis) for axis in ("row", "col", "depth"))
    w_local, _, rows, half = environment.shape
    phys = site_tensor.shape[0]
    cols = half // 2
    pieces = col_count * 2
    bond = pieces * cols

    env_own = lax.dynamic_slice_in_dim(environment, depth * cols, cols, 3)
    env_sib = swap(lax.dynamic_slice_in_dim(environment, (1 - depth) * cols, cols, 3))
    mpo_mine = jnp.concatenate(
        [
            lax.dynamic_slice_in_dim(mpo, depth * w_local, w_local, 0),
            lax.dynamic_slice_in_dim(mpo, (1 - depth) * w_local, w_local, 0),
        ],
        axis=0,
    )
    planar = jnp.transpose(site_tensor.reshape(phys, rows, 2, 2, cols), (3, 0, 2, 1, 4))
    site_own = lax.dynamic_index_in_dim(planar, depth, 0, keepdims=False)

    by_col = [planar]
    travelling = site_own
    for _ in range(col_count - 1):
        travelling = shift(travelling, "col", col_count)
        sibling = swap(travelling)
        pair = jnp.stack([travelling, sibling])
        by_col.append(jnp.where(depth == 0, pair, pair[::-1]))
    site_pieces = jnp.concatenate(by_col, axis=0)

    def piece_at(index):
        there = lax.rem(col - index // 2 + col_count, col_count)
        return lax.dynamic_index_in_dim(site_pieces, there * 2 + index % 2, 0, keepdims=False)

    ring = row_count == pieces

    total = None
    if ring:
        own, sib = env_own, env_sib
        for step in range(row_count):
            block = lax.rem(row - step + row_count, row_count)
            total = first_product(piece_at(block), own, sib, total)
            if step < row_count - 1:
                own, sib = shift(own, "row", row_count), shift(sib, "row", row_count)
    else:
        own = lax.all_gather(env_own, "row", axis=2, tiled=True)
        sib = lax.all_gather(env_sib, "row", axis=2, tiled=True)
        for index in range(pieces):
            block = slice(index * cols, (index + 1) * cols)
            total = first_product(piece_at(index), own[:, :, block], sib[:, :, block], total)
    q = mix(mpo_mine, total)

    if not ring:
        site_all = lax.all_gather(site_own, "row", axis=2, tiled=True)
        parts = []
        for index in range(pieces):
            block = slice(index * cols, (index + 1) * cols)
            parts.append(second_product(q, site_all[:, :, block])[0])
        return lax.psum_scatter(
            jnp.concatenate(parts, axis=3), ("col", "depth"), scatter_dimension=3, tiled=True
        )

    axes = ("row", "col", "depth")
    place = lambda r, c, d: (r * col_count + c) * 2 + d
    chunks = 2
    y_rows = rows // chunks
    mine = col * 2 + depth
    outs = []
    for chunk in range(chunks):
        travelling = site_own[:, :, chunk * y_rows : (chunk + 1) * y_rows]
        travelling = after(travelling, own)
        out = None
        for step in range(row_count):
            target = [(r - step) % row_count for r in range(row_count)]
            wide, low = second_product(q, travelling)
            if step < row_count - 1:
                travelling = shift(travelling, "row", row_count)
            low = lax.ppermute(
                low,
                axes,
                [
                    (place(r, c, 1 - target[r] % 2), place(r, c, target[r] % 2))
                    for r in range(row_count)
                    for c in range(col_count)
                ],
            )
            wide = wide + low.astype(F32)
            low = wide.astype(BF16)
            for away in range(1, col_count):
                came = lax.ppermute(
                    low,
                    axes,
                    [
                        (
                            place(r, (target[r] // 2 + away) % col_count, target[r] % 2),
                            place(r, target[r] // 2, target[r] % 2),
                        )
                        for r in range(row_count)
                    ],
                )
                wide = wide + came.astype(F32)
            if out is None:
                out = wide
            else:
                out = jnp.where(mine == lax.rem(row - step + row_count, row_count), wide, out)
        outs.append(out)
    return jnp.concatenate(outs, axis=3)


def solution(mesh):
    placed = (
        P(("groups", "depth"), None, "row", "col"),
        P("groups", "row", None, "col"),
        P("groups", None, None, None),
    )
    return jax.shard_map(
        on_device,
        mesh=mesh,
        in_specs=placed,
        out_specs=P("groups", None, "row", ("col", "depth")),
        check_vma=False,
    )
```

time: 742 us -> 395 us (0.53)
  waiting for transfers between devices: 535 us -> 186 us
  matrix products: 115 us -> 0 us
  Pallas kernels: 0 us -> 85.3 us
  starting transfers between devices: 0.16 us -> 50.3 us
  local copies, waits for them, and re-layouts: 66.2 us -> 32.2 us
  other arithmetic: 10.7 us -> 38.9 us
  between operations: 13.2 us -> 0.36 us
    all_gather x3 -> x0, waiting for transfers between devices: 389 us -> none  [the longest x1 144 us: on_device(): lax.all_gather(own_site, 'row', axis=1, tiled=True)]
    ppermute x0 -> x31, waiting for transfers between devices: none -> 186 us  [the longest x13 165 us: shift(): lax.ppermute(value, axis, [(i, (i + 1) % count) for i in range(count)])]
    reduce_scatter x2 -> x0, waiting for transfers between devices: 144 us -> none  [the longest x1 124 us: on_device(): lax.psum_scatter(partial_env, ('col', 'depth'), scatter_dimension=3, tile...]
    dot_general x3 -> x0, matrix products: 115 us -> none  [the longest x1 58 us: on_device(): jnp.einsum('wvst,wspxc->vtpxc', mpo_mine, g_local, precision=highest)]
    pallas_call x0 -> x13, Pallas kernels: none -> 85.3 us  [the longest x8 40.3 us: second_product(): pl.pallas_call(second_kernel, grid=(mpo_count,), in_specs=[pl.BlockSpec((...]
    ppermute x0 -> x31, starting transfers between devices: none -> 50.3 us  [the longest x8 25.7 us: on_device(): lax.ppermute(low, axes, [(place(r, c, 1 - target[r] % 2), place(r, c, tar...]
    reshape x2 -> x1, local copies, waits for them, and re-layouts: 28.9 us -> 7.27 us  [on_device(): site_tensor.reshape(phys, rows, 2, 2, cols)]
    convert_element_type x1 -> x8, other arithmetic: 4.04 us -> 17.5 us  [on_device(): low = wide.astype(BF16)]
  transfers between devices with their start and end apart: 5 -> 31, of which waited for: 5 -> 12; matrix products, arithmetic and copies ran while one was open for 4% -> 8% of each run, Pallas kernels for 0% -> 22%
where the time goes in v1:
time: 395 us; the launch traced here: 393 us
  waiting for transfers between devices  186 us (47%)
  Pallas kernels  85.3 us (22%)
  starting transfers between devices  50.3 us (13%)
  other arithmetic  38.9 us (10%)
  local copies, waits for them, and re-layouts  32.2 us (8%)
    ppermute x13, waiting for transfers between devices, shift(): lax.ppermute(value, axis, [(i, (i + 1) % count) for i in range(count)])  165 us
    pallas_call x8, Pallas kernels, second_product(): pl.pallas_call(second_kernel, grid=(mpo_count,), in_specs=[pl.BlockSpec((...  40.3 us
    pallas_call x4, Pallas kernels, first_product(): pl.pallas_call(first_kernel, grid=(phys, w_local), in_specs=[pl.BlockSpec...  34.7 us
    ppermute x8, starting transfers between devices, on_device(): lax.ppermute(low, axes, [(place(r, c, 1 - target[r] % 2), place(r, c, tar...  25.7 us
    ppermute x8, waiting for transfers between devices, on_device(): lax.ppermute(low, axes, [(place(r, (target[r] // 2 + away) % col_count, t...  20.9 us
    unnamed x47, local copies, waits for them, and re-layouts  19.9 us
    convert_element_type x8, other arithmetic, on_device(): low = wide.astype(BF16)  17.5 us
    ppermute x8, starting transfers between devices, on_device(): lax.ppermute(low, axes, [(place(r, (target[r] // 2 + away) % col_count, t...  17.4 us
  transfers between devices with their start and end apart: 31, of which 12 were waited for; matrix products, arithmetic and copies ran while one was open for 8% of the time, Pallas kernels for 22%

profile of v1, /device:TPU:1, one launch (start us, length us, event | category | flops | bytes accessed | tf_op | source)
XLA Modules:
  0.0 393.3 jit_solution(10538460064982012571)
XLA Ops:
  0.0 11.1 %copy.7 = bf16[2,512,2,1024]{1,3,2,0:T(8,128)(2,1)} copy(bf16[2,512,2,1024]{3,2,1,0:T(2,128)(2,1)} %param.4) | data formatting | bytes 8388608 | tf_op args[1]
  11.1 7.3 %copy.8 = bf16[2,512,2,2,512]{4,1,2,0,3:T(8,128)(2,1)} copy(bf16[2,512,2,2,512]{1,4,3,2,0:T(8,128)(2,1)} %bitcast.17) | data formatting | bytes 8388608 | tf_op jit(solution)/shard_map/reshape | solution.py:171
  18.4 3.2 dynamic-slice_bitcast_fusion
  21.6 2.0 collective-permute-start
  23.9 1.3 collective-permute-start.2
  25.2 1.2 collective-permute-start.5
  26.5 23.1 %collective-permute-done.2.own_ref = bf16[1,2,512,512]{3,2,1,0:T(8,128)(2,1)S(1)} collective-permute-done((bf16[1,2,512,512]{3,2,1,0:T(8,128)(2,1)S(1)}, bf16[1,2,512,512]{3,2,1,0:T(8,128)(2,1)S(1)}, u32[]{:S(2)}, u32[]{:S(2)}) %collective-permute-start.2) | collective-permute-done | bytes 1048608 | tf_op jit(solution)/shard_map/ppermute | solution.py:146
  51.3 18.0 %collective-permute-done = bf16[2,2,512,512]{3,2,1,0:T(8,128)(2,1)} collective-permute-done((bf16[2,2,512,512]{3,2,1,0:T(8,128)(2,1)}, bf16[2,2,512,512]{3,2,1,0:T(8,128)(2,1)}, u32[]{:S(2)}, u32[]{:S(2)}) %collective-permute-start) | collective-permute-done | bytes 2097184 | tf_op jit(solution)/shard_map/ppermute | solution.py:146
  69.3 1.2 collective-permute-start.1
  70.5 3.7 collective-permute-done.3.own_ref
  74.2 22.6 %collective-permute-done.6.sib_ref = bf16[1,2,512,512]{3,2,1,0:T(8,128)(2,1)} collective-permute-done((bf16[1,2,512,512]{3,2,1,0:T(8,128)(2,1)S(1)}, bf16[1,2,512,512]{3,2,1,0:T(8,128)(2,1)}, u32[]{:S(2)}, u32[]{:S(2)}) %collective-permute-start.6) | collective-permute-done | bytes 1048608 | tf_op jit(solution)/shard_map/ppermute | solution.py:146
  96.8 1.7 fusion.16
  98.5 20.8 %collective-permute-done.4.own_ref = bf16[1,2,512,512]{3,2,1,0:T(8,128)(2,1)} collective-permute-done((bf16[1,2,512,512]{3,2,1,0:T(8,128)(2,1)S(1)}, bf16[1,2,512,512]{3,2,1,0:T(8,128)(2,1)}, u32[]{:S(2)}, u32[]{:S(2)}) %collective-permute-start.4) | collective-permute-done | bytes 1048608 | tf_op jit(solution)/shard_map/ppermute | solution.py:146
  119.3 22.5 %collective-permute-done.7.sib_ref = bf16[1,2,512,512]{3,2,1,0:T(8,128)(2,1)} collective-permute-done((bf16[1,2,512,512]{3,2,1,0:T(8,128)(2,1)}, bf16[1,2,512,512]{3,2,1,0:T(8,128)(2,1)}, u32[]{:S(2)}, u32[]{:S(2)}) %collective-permute-start.7) | collective-permute-done | bytes 1048608 | tf_op jit(solution)/shard_map/ppermute | solution.py:146
  141.7 2.6 pad_maximum_fusion
  145.3 1.2 copy-done.17
  146.5 3.0 fusion.1
  149.6 14.6 %collective-permute-done.9.site_ref = bf16[2,2,256,512]{3,2,1,0:T(8,128)(2,1)} collective-permute-done((bf16[2,2,256,512]{3,2,1,0:T(8,128)(2,1)S(1)}, bf16[2,2,256,512]{3,2,1,0:T(8,128)(2,1)}, u32[]{:S(2)}, u32[]{:S(2)}) %collective-permute-start.9) | collective-permute-done | bytes 1048608 | tf_op jit(solution)/shard_map/ppermute | solution.py:146
  164.2 6.8 %first_product.4.rest_0_ = f32[2,1,2,2,512,512]{5,4,3,2,1,0:T(8,128)} custom-call(bf16[2,2,512,512]{3,2,1,0:T(8,128)(2,1)S(1)} %get-tuple-element.41.site_ref, bf16[1,2,512,512]{3,2,1,0:T(8,128)(2,1)S(1)} %get-tuple-element.48.own_ref, bf16[1,2,512,512]{3,2,1,0:T(8,128)(2,1)S(1)} %copy-done.12), custom_call_target="tpu_custom_call" | custom-call | flops 4294967296 | bytes 16777216 | tf_op jit(solution)/shard_map/first_product/pallas_call | solution.py:49
  171.0 9.3 %first_product.5.rest_0_ = f32[2,1,2,2,512,512]{5,4,3,2,1,0:T(8,128)} custom-call(bf16[2,2,512,512]{3,2,1,0:T(8,128)(2,1)S(1)} %get-tuple-element.44.site_ref, bf16[1,2,512,512]{3,2,1,0:T(8,128)(2,1)S(1)} %collective-permute-done.2.own_ref, bf16[1,2,512,512]{3,2,1,0:T(8,128)(2,1)} %collective-permute-done.6.sib_ref, ...), custom_call_target="tpu_custom_call", output_to_operand_aliasing={{}: (3, {})} | custom-call | flops 4294967296 | bytes 16777216 | tf_op jit(solution)/shard_map/first_product/pallas_call | solution.py:49
  180.3 9.3 %first_product.6.rest_0_ = f32[2,1,2,2,512,512]{5,4,3,2,1,0:T(8,128)} custom-call(bf16[2,2,512,512]{3,2,1,0:T(8,128)(2,1)S(1)} %get-tuple-element.43.site_ref, bf16[1,2,512,512]{3,2,1,0:T(8,128)(2,1)S(1)} %collective-permute-done.3.own_ref, bf16[1,2,512,512]{3,2,1,0:T(8,128)(2,1)} %collective-permute-done.7.sib_ref, ...), custom_call_target="tpu_custom_call", output_to_operand_aliasing={{}: (3, {})} | custom-call | flops 4294967296 | bytes 16777216 | tf_op jit(solution)/shard_map/first_product/pallas_call | solution.py:49
  189.6 19.4 %collective-permute-done.8.sib_ref = bf16[1,2,512,512]{3,2,1,0:T(8,128)(2,1)S(1)} collective-permute-done((bf16[1,2,512,512]{3,2,1,0:T(8,128)(2,1)}, bf16[1,2,512,512]{3,2,1,0:T(8,128)(2,1)S(1)}, u32[]{:S(2)}, u32[]{:S(2)}) %collective-permute-start.8) | collective-permute-done | bytes 1048608 | tf_op jit(solution)/shard_map/ppermute | solution.py:146
  209.0 9.3 %first_product.7.g_ref = f32[2,1,2,2,512,512]{5,4,3,2,1,0:T(8,128)} custom-call(bf16[2,2,512,512]{3,2,1,0:T(8,128)(2,1)S(1)} %get-tuple-element.42.site_ref, bf16[1,2,512,512]{3,2,1,0:T(8,128)(2,1)} %collective-permute-done.4.own_ref, bf16[1,2,512,512]{3,2,1,0:T(8,128)(2,1)S(1)} %collective-permute-done.8.sib_ref, ...), custom_call_target="tpu_custom_call", output_to_operand_aliasing={{}: (3, {})} | custom-call | flops 4294967296 | bytes 16777216 | tf_op jit(solution)/shard_map/first_product/pallas_call | solution.py:49
  218.3 10.3 %mix.1.q_ref = bf16[2,2,2,512,512]{4,3,2,1,0:T(8,128)(2,1)S(1)} custom-call(f32[2,2,2,2]{3,2,1,0:T(2,128)S(1)} %pad_maximum_fusion.2.mpo_ref, f32[2,1,2,2,512,512]{5,4,3,2,1,0:T(8,128)} %first_product.7.g_ref), custom_call_target="tpu_custom_call" | custom-call | flops 16777216 | bytes 12582912 | tf_op jit(solution)/shard_map/mix/pallas_call | solution.py:85
  228.7 2.0 copy-done.10
  230.7 5.3 %second_product.10 = (f32[2,2,512,256]{3,2,1,0:T(8,128)S(1)}, bf16[2,2,512,256]{3,2,1,0:T(8,128)(2,1)}) custom-call(bf16[2,2,2,512,512]{4,3,2,1,0:T(8,128)(2,1)} %copy-done.10, bf16[2,2,256,512]{3,2,1,0:T(8,128)(2,1)} %collective-permute-done.9.site_ref), custom_call_target="tpu_custom_call" | custom-call | flops 2147483648 | bytes 8388608 | tf_op jit(solution)/shard_map/second_product/pallas_call | solution.py:122
  235.9 1.3 collective-permute-start.16
  237.2 5.0 %second_product.11 = (f32[2,2,512,256]{3,2,1,0:T(8,128)S(1)}, bf16[2,2,512,256]{3,2,1,0:T(8,128)(2,1)}) custom-call(bf16[2,2,2,512,512]{4,3,2,1,0:T(8,128)(2,1)} %copy-done.10, bf16[2,2,256,512]{3,2,1,0:T(8,128)(2,1)S(1)} %get-tuple-element.23.site_ref), custom_call_target="tpu_custom_call" | custom-call | flops 2147483648 | bytes 8388608 | tf_op jit(solution)/shard_map/second_product/pallas_call | solution.py:122
  242.2 8.9 %collective-permute-start.18 = (bf16[2,2,512,256]{3,2,1,0:T(8,128)(2,1)}, bf16[2,2,512,256]{3,2,1,0:T(8,128)(2,1)}, u32[]{:S(2)}, u32[]{:S(2)}) collective-permute-start(bf16[2,2,512,256]{3,2,1,0:T(8,128)(2,1)} %get-tuple-element.31), channel_id=1, source_target_pairs={{1,0},{3,2},{4,5},{6,7},{9,8},{11,10},{12,13},{14,15},{17,16},{19,... | collective-permute-start | bytes 3145736 | tf_op jit(solution)/shard_map/ppermute | solution.py:230
  251.1 5.3 %second_product.14 = (f32[2,2,512,256]{3,2,1,0:T(8,128)S(1)}, bf16[2,2,512,256]{3,2,1,0:T(8,128)(2,1)}) custom-call(bf16[2,2,2,512,512]{4,3,2,1,0:T(8,128)(2,1)} %copy-done.10, bf16[2,2,256,512]{3,2,1,0:T(8,128)(2,1)} %collective-permute-done.20.site_ref), custom_call_target="tpu_custom_call" | custom-call | flops 2147483648 | bytes 8388608 | tf_op jit(solution)/shard_map/second_product/pallas_call | solution.py:122
  256.4 1.3 collective-permute-start.27
  258.3 4.2 %second_product.15 = (f32[2,2,512,256]{3,2,1,0:T(8,128)S(1)}, bf16[2,2,512,256]{3,2,1,0:T(8,128)(2,1)S(1)}) custom-call(bf16[2,2,2,512,512]{4,3,2,1,0:T(8,128)(2,1)} %copy-done.10, bf16[2,2,256,512]{3,2,1,0:T(8,128)(2,1)S(1)} %get-tuple-element.32.site_ref), custom_call_target="tpu_custom_call" | custom-call | flops 2147483648 | bytes 8388608 | tf_op jit(solution)/shard_map/second_product/pallas_call | solution.py:122
  262.6 6.1 %second_product.9 = (f32[2,2,512,256]{3,2,1,0:T(8,128)S(1)}, bf16[2,2,512,256]{3,2,1,0:T(8,128)(2,1)}) custom-call(bf16[2,2,2,512,512]{4,3,2,1,0:T(8,128)(2,1)} %copy-done.10, bf16[2,2,256,512]{3,2,1,0:T(8,128)(2,1)} %collective-permute-done.10.site_ref), custom_call_target="tpu_custom_call" | custom-call | flops 2147483648 | bytes 8388608 | tf_op jit(solution)/shard_map/second_product/pallas_call | solution.py:122
  268.6 4.3 %collective-permute-start.29 = (bf16[2,2,512,256]{3,2,1,0:T(8,128)(2,1)S(1)}, bf16[2,2,512,256]{3,2,1,0:T(8,128)(2,1)}, u32[]{:S(2)}, u32[]{:S(2)}) collective-permute-start(bf16[2,2,512,256]{3,2,1,0:T(8,128)(2,1)S(1)} %get-tuple-element.40), channel_id=1, source_target_pairs={{1,0},{3,2},{4,5},{6,7},{9,8},{11,10},{12,13},{14,15},{17,16},{19,... | collective-permute-start | bytes 3145736 | tf_op jit(solution)/shard_map/ppermute | solution.py:230
  273.0 2.5 fusion.10
  275.4 2.3 collective-permute-start.14
  278.3 2.4 fusion.11
  280.8 20.0 %collective-permute-done.11.site_ref = bf16[2,2,256,512]{3,2,1,0:T(8,128)(2,1)S(1)} collective-permute-done((bf16[2,2,256,512]{3,2,1,0:T(8,128)(2,1)}, bf16[2,2,256,512]{3,2,1,0:T(8,128)(2,1)S(1)}, u32[]{:S(2)}, u32[]{:S(2)}) %collective-permute-start.11) | collective-permute-done | bytes 1048608 | tf_op jit(solution)/shard_map/ppermute | solution.py:146
  301.8 1.2 copy-done.14
  303.1 5.0 %second_product.8 = (f32[2,2,512,256]{3,2,1,0:T(8,128)S(1)}, bf16[2,2,512,256]{3,2,1,0:T(8,128)(2,1)}) custom-call(bf16[2,2,2,512,512]{4,3,2,1,0:T(8,128)(2,1)} %copy-done.10, bf16[2,2,256,512]{3,2,1,0:T(8,128)(2,1)S(1)} %copy-done.14), custom_call_target="tpu_custom_call" | custom-call | flops 2147483648 | bytes 8388608 | tf_op jit(solution)/shard_map/second_product/pallas_call | solution.py:122
  308.0 1.3 collective-permute-start.12
  309.3 5.3 %second_product.13 = (f32[2,2,512,256]{3,2,1,0:T(8,128)S(1)}, bf16[2,2,512,256]{3,2,1,0:T(8,128)(2,1)}) custom-call(bf16[2,2,2,512,512]{4,3,2,1,0:T(8,128)(2,1)} %copy-done.10, bf16[2,2,256,512]{3,2,1,0:T(8,128)(2,1)} %collective-permute-done.21.site_ref), custom_call_target="tpu_custom_call" | custom-call | flops 2147483648 | bytes 8388608 | tf_op jit(solution)/shard_map/second_product/pallas_call | solution.py:122
  314.6 5.0 %collective-permute-start.25 = (bf16[2,2,512,256]{3,2,1,0:T(8,128)(2,1)}, bf16[2,2,512,256]{3,2,1,0:T(8,128)(2,1)}, u32[]{:S(2)}, u32[]{:S(2)}) collective-permute-start(bf16[2,2,512,256]{3,2,1,0:T(8,128)(2,1)} %get-tuple-element.36), channel_id=1, source_target_pairs={{1,0},{3,2},{4,5},{6,7},{9,8},{11,10},{12,13},{14,15},{17,16},{19,... | collective-permute-start | bytes 3145736 | tf_op jit(solution)/shard_map/ppermute | solution.py:230
  319.6 2.4 fusion.14
  323.1 3.1 collective-permute-start.17
  326.2 1.2 copy-done.16
  327.4 4.2 %second_product.12 = (f32[2,2,512,256]{3,2,1,0:T(8,128)S(1)}, bf16[2,2,512,256]{3,2,1,0:T(8,128)(2,1)S(1)}) custom-call(bf16[2,2,2,512,512]{4,3,2,1,0:T(8,128)(2,1)} %copy-done.10, bf16[2,2,256,512]{3,2,1,0:T(8,128)(2,1)S(1)} %copy-done.16), custom_call_target="tpu_custom_call" | custom-call | flops 2147483648 | bytes 8388608 | tf_op jit(solution)/shard_map/second_product/pallas_call | solution.py:122
  331.7 1.3 collective-permute-start.23
  333.0 1.6 fusion.9
  335.3 1.6 collective-permute-start.15
  337.0 2.4 fusion.8
  339.4 1.3 collective-permute-start.13
  340.7 2.5 fusion.15
  343.2 2.4 fusion.13
  345.7 6.0 %collective-permute-start.28 = (bf16[2,2,512,256]{3,2,1,0:T(8,128)(2,1)}, bf16[2,2,512,256]{3,2,1,0:T(8,128)(2,1)}, u32[]{:S(2)}, u32[]{:S(2)}) collective-permute-start(bf16[2,2,512,256]{3,2,1,0:T(8,128)(2,1)} %fusion.14), channel_id=1, source_target_pairs={{1,3},{6,4},{11,9},{12,14},{17,19},{22,20},{27,25},{28,30}} | collective-permute-start | bytes 3145736 | tf_op jit(solution)/shard_map/ppermute | solution.py:242
  351.6 1.2 fusion.12
  352.9 1.7 collective-permute-start.30
  354.5 1.7 collective-permute-start.26
  356.3 1.3 collective-permute-start.24
  357.6 9.1 %collective-permute-done.13 = bf16[2,2,512,256]{3,2,1,0:T(8,128)(2,1)} collective-permute-done((bf16[2,2,512,256]{3,2,1,0:T(8,128)(2,1)}, bf16[2,2,512,256]{3,2,1,0:T(8,128)(2,1)}, u32[]{:S(2)}, u32[]{:S(2)}) %collective-permute-start.13) | collective-permute-done | bytes 1048608 | tf_op jit(solution)/shard_map/ppermute | solution.py:242
  366.7 7.1 %select_select_fusion.1 = f32[2,2,512,256]{3,2,1,0:T(8,128)S(1)} fusion(bf16[2,2,512,256]{3,2,1,0:T(8,128)(2,1)S(1)} %collective-permute-done.19, bf16[2,2,512,256]{3,2,1,0:T(8,128)(2,1)} %collective-permute-done.17, bf16[2,2,512,256]{3,2,1,0:T(8,128)(2,1)} %collective-permute-done.15, bf16[2,2,512,256]{3,2,1,0:T(8,128)(2,1)} %collective-permute-done.13, ...), kind=kLoop, calls=%fused_computation.24 | loop fusion | flops 9961472 | bytes 18874372 | tf_op jit(solution)/shard_map/jit(_where)/select_n | solution.py:257
  373.9 11.7 %collective-permute-done.24 = bf16[2,2,512,256]{3,2,1,0:T(8,128)(2,1)} collective-permute-done((bf16[2,2,512,256]{3,2,1,0:T(8,128)(2,1)}, bf16[2,2,512,256]{3,2,1,0:T(8,128)(2,1)}, u32[]{:S(2)}, u32[]{:S(2)}) %collective-permute-start.24) | collective-permute-done | bytes 1048608 | tf_op jit(solution)/shard_map/ppermute | solution.py:242
  385.6 5.1 %select_select_fusion = f32[2,2,512,256]{3,2,1,0:T(8,128)S(1)} fusion(bf16[2,2,512,256]{3,2,1,0:T(8,128)(2,1)} %collective-permute-done.30, bf16[2,2,512,256]{3,2,1,0:T(8,128)(2,1)} %collective-permute-done.28, bf16[2,2,512,256]{3,2,1,0:T(8,128)(2,1)} %collective-permute-done.26, bf16[2,2,512,256]{3,2,1,0:T(8,128)(2,1)} %collective-permute-done.24, ...), kind=kLoop, calls=%fused_computation.19 | loop fusion | flops 9961472 | bytes 18874372 | tf_op jit(solution)/shard_map/jit(_where)/select_n | solution.py:257
  390.7 2.7 pad_maximum_fusion.1
  (78 shorter events, 7.1 us)
Async XLA Ops:
  18.4 5.2 %copy-start.20 = (bf16[1,2,512,1024]{3,2,1,0:T(8,128)(2,1)S(1)}, bf16[1,2,512,1024]{3,2,1,0:T(8,128)(2,1)}, u32[]{:S(2)}) copy-start(bf16[1,2,512,1024]{3,2,1,0:T(8,128)(2,1)} %param.3) | copy-start | bytes 6291460
  21.6 47.7 %collective-permute-start = (bf16[2,2,512,512]{3,2,1,0:T(8,128)(2,1)}, bf16[2,2,512,512]{3,2,1,0:T(8,128)(2,1)}, u32[]{:S(2)}, u32[]{:S(2)}) collective-permute-start(bf16[2,2,512,512]{3,2,1,0:T(8,128)(2,1)} %dynamic-slice_bitcast_fusion), channel_id=1, source_target_pairs={{0,2},{2,0},{1,3},{3,1},{4,6},{6,4},{5,7},{7,5},{8,10},{10,8},{9,1... | collective-permute-start | bytes 6291464 | tf_op jit(solution)/shard_map/ppermute | solution.py:146
  23.6 73.2 %copy-start.22 = (f32[2,2,2,2]{3,2,1,0:T(2,128)S(1)}, f32[2,2,2,2]{3,2,1,0:T(2,128)}, u32[]{:S(2)}) copy-start(f32[2,2,2,2]{3,2,1,0:T(2,128)} %param.5) | copy-start | bytes 196
  23.9 25.7 %collective-permute-start.2 = (bf16[1,2,512,512]{3,2,1,0:T(8,128)(2,1)S(1)}, bf16[1,2,512,512]{3,2,1,0:T(8,128)(2,1)S(1)}, u32[]{:S(2)}, u32[]{:S(2)}) collective-permute-start(bf16[1,2,512,512]{3,2,1,0:T(8,128)(2,1)S(1)} %get-tuple-element.48.own_ref), channel_id=1, source_target_pairs={{0,4},{4,8},{8,12},{12,0},{1,5},{5,9},{9,13},{13,1},{2,6},{6,10},{... | collective-permute-start | bytes 3145736 | tf_op jit(solution)/shard_map/ppermute | solution.py:146
  25.2 24.3 %collective-permute-start.5 = (bf16[1,2,512,512]{3,2,1,0:T(8,128)(2,1)S(1)}, bf16[1,2,512,512]{3,2,1,0:T(8,128)(2,1)S(1)}, u32[]{:S(2)}, u32[]{:S(2)}) collective-permute-start(bf16[1,2,512,512]{3,2,1,0:T(8,128)(2,1)S(1)} %get-tuple-element.47), channel_id=1, source_target_pairs={{0,1},{1,0},{2,3},{3,2},{4,5},{5,4},{6,7},{7,6},{8,9},{9,8},{10,11... | collective-permute-start | bytes 3145736 | tf_op jit(solution)/shard_map/ppermute | solution.py:150
  49.6 24.7 %collective-permute-start.3 = (bf16[1,2,512,512]{3,2,1,0:T(8,128)(2,1)S(1)}, bf16[1,2,512,512]{3,2,1,0:T(8,128)(2,1)S(1)}, u32[]{:S(2)}, u32[]{:S(2)}) collective-permute-start(bf16[1,2,512,512]{3,2,1,0:T(8,128)(2,1)S(1)} %collective-permute-done.2.own_ref), channel_id=1, source_target_pairs={{0,4},{4,8},{8,12},{12,0},{1,5},{5,9},{9,13},{13,1},{2,6},{6,10},{... | collective-permute-start | bytes 3145736 | tf_op jit(solution)/shard_map/ppermute | solution.py:146
  49.6 47.2 %collective-permute-start.6 = (bf16[1,2,512,512]{3,2,1,0:T(8,128)(2,1)S(1)}, bf16[1,2,512,512]{3,2,1,0:T(8,128)(2,1)}, u32[]{:S(2)}, u32[]{:S(2)}) collective-permute-start(bf16[1,2,512,512]{3,2,1,0:T(8,128)(2,1)S(1)} %collective-permute-done.5.sib_ref), channel_id=1, source_target_pairs={{0,4},{4,8},{8,12},{12,0},{1,5},{5,9},{9,13},{13,1},{2,6},{6,10},{... | collective-permute-start | bytes 3145736 | tf_op jit(solution)/shard_map/ppermute | solution.py:146
  50.3 1.0 copy-start.11
  69.3 72.4 %collective-permute-start.1 = (bf16[2,2,512,512]{3,2,1,0:T(8,128)(2,1)}, bf16[2,2,512,512]{3,2,1,0:T(8,128)(2,1)}, u32[]{:S(2)}, u32[]{:S(2)}) collective-permute-start(bf16[2,2,512,512]{3,2,1,0:T(8,128)(2,1)} %collective-permute-done), channel_id=1, source_target_pairs={{0,1},{1,0},{2,3},{3,2},{4,5},{5,4},{6,7},{7,6},{8,9},{9,8},{10,11... | collective-permute-start | bytes 6291464 | tf_op jit(solution)/shard_map/ppermute | solution.py:150
  74.2 45.0 %collective-permute-start.4 = (bf16[1,2,512,512]{3,2,1,0:T(8,128)(2,1)S(1)}, bf16[1,2,512,512]{3,2,1,0:T(8,128)(2,1)}, u32[]{:S(2)}, u32[]{:S(2)}) collective-permute-start(bf16[1,2,512,512]{3,2,1,0:T(8,128)(2,1)S(1)} %collective-permute-done.3.own_ref), channel_id=1, source_target_pairs={{0,4},{4,8},{8,12},{12,0},{1,5},{5,9},{9,13},{13,1},{2,6},{6,10},{... | collective-permute-start | bytes 3145736 | tf_op jit(solution)/shard_map/ppermute | solution.py:146
  96.8 44.9 %collective-permute-start.7 = (bf16[1,2,512,512]{3,2,1,0:T(8,128)(2,1)}, bf16[1,2,512,512]{3,2,1,0:T(8,128)(2,1)}, u32[]{:S(2)}, u32[]{:S(2)}) collective-permute-start(bf16[1,2,512,512]{3,2,1,0:T(8,128)(2,1)} %collective-permute-done.6.sib_ref), channel_id=1, source_target_pairs={{0,4},{4,8},{8,12},{12,0},{1,5},{5,9},{9,13},{13,1},{2,6},{6,10},{... | collective-permute-start | bytes 3145736 | tf_op jit(solution)/shard_map/ppermute | solution.py:146
  119.3 44.9 %collective-permute-start.9 = (bf16[2,2,256,512]{3,2,1,0:T(8,128)(2,1)S(1)}, bf16[2,2,256,512]{3,2,1,0:T(8,128)(2,1)}, u32[]{:S(2)}, u32[]{:S(2)}) collective-permute-start(bf16[2,2,256,512]{3,2,1,0:T(8,128)(2,1)S(1)} %get-tuple-element.23.site_ref), channel_id=1, source_target_pairs={{0,4},{4,8},{8,12},{12,0},{1,5},{5,9},{9,13},{13,1},{2,6},{6,10},{... | collective-permute-start | bytes 3145736 | tf_op jit(solution)/shard_map/ppermute | solution.py:146
  119.3 131.9 %collective-permute-start.20 = (bf16[2,2,256,512]{3,2,1,0:T(8,128)(2,1)S(1)}, bf16[2,2,256,512]{3,2,1,0:T(8,128)(2,1)}, u32[]{:S(2)}, u32[]{:S(2)}) collective-permute-start(bf16[2,2,256,512]{3,2,1,0:T(8,128)(2,1)S(1)} %get-tuple-element.32.site_ref), channel_id=1, source_target_pairs={{0,4},{4,8},{8,12},{12,0},{1,5},{5,9},{9,13},{13,1},{2,6},{6,10},{... | collective-permute-start | bytes 3145736 | tf_op jit(solution)/shard_map/ppermute | solution.py:146
  141.7 67.3 %collective-permute-start.8 = (bf16[1,2,512,512]{3,2,1,0:T(8,128)(2,1)}, bf16[1,2,512,512]{3,2,1,0:T(8,128)(2,1)S(1)}, u32[]{:S(2)}, u32[]{:S(2)}) collective-permute-start(bf16[1,2,512,512]{3,2,1,0:T(8,128)(2,1)} %collective-permute-done.7.sib_ref), channel_id=1, source_target_pairs={{0,4},{4,8},{8,12},{12,0},{1,5},{5,9},{9,13},{13,1},{2,6},{6,10},{... | collective-permute-start | bytes 3145736 | tf_op jit(solution)/shard_map/ppermute | solution.py:146
  144.3 2.2 copy-start.17
  146.5 17.7 %copy-start.12 = (bf16[1,2,512,512]{3,2,1,0:T(8,128)(2,1)S(1)}, bf16[1,2,512,512]{3,2,1,0:T(8,128)(2,1)}, u32[]{:S(2)}) copy-start(bf16[1,2,512,512]{3,2,1,0:T(8,128)(2,1)} %copy-done.11) | copy-start | bytes 3145732
  164.2 93.5 %collective-permute-start.10 = (bf16[2,2,256,512]{3,2,1,0:T(8,128)(2,1)}, bf16[2,2,256,512]{3,2,1,0:T(8,128)(2,1)}, u32[]{:S(2)}, u32[]{:S(2)}) collective-permute-start(bf16[2,2,256,512]{3,2,1,0:T(8,128)(2,1)} %collective-permute-done.9.site_ref), channel_id=1, source_target_pairs={{0,4},{4,8},{8,12},{12,0},{1,5},{5,9},{9,13},{13,1},{2,6},{6,10},{... | collective-permute-start | bytes 3145736 | tf_op jit(solution)/shard_map/ppermute | solution.py:146
  228.7 2.0 copy-start.10
  235.9 37.0 %copy-start = (f32[2,2,512,256]{3,2,1,0:T(8,128)}, f32[2,2,512,256]{3,2,1,0:T(8,128)S(1)}, u32[]{:S(2)}) copy-start(f32[2,2,512,256]{3,2,1,0:T(8,128)S(1)} %get-tuple-element.28) | copy-start | bytes 6291460
  235.9 32.7 %collective-permute-start.16 = (bf16[2,2,512,256]{3,2,1,0:T(8,128)(2,1)}, bf16[2,2,512,256]{3,2,1,0:T(8,128)(2,1)}, u32[]{:S(2)}, u32[]{:S(2)}) collective-permute-start(bf16[2,2,512,256]{3,2,1,0:T(8,128)(2,1)} %get-tuple-element.29), channel_id=1, source_target_pairs={{0,1},{2,3},{5,4},{7,6},{8,9},{10,11},{13,12},{15,14},{16,17},{18,... | collective-permute-start | bytes 3145736 | tf_op jit(solution)/shard_map/ppermute | solution.py:230
  242.2 36.1 %copy-start.1 = (f32[2,2,512,256]{3,2,1,0:T(8,128)}, f32[2,2,512,256]{3,2,1,0:T(8,128)S(1)}, u32[]{:S(2)}) copy-start(f32[2,2,512,256]{3,2,1,0:T(8,128)S(1)} %get-tuple-element.30) | copy-start | bytes 6291460
  242.2 33.2 %collective-permute-start.18 = (bf16[2,2,512,256]{3,2,1,0:T(8,128)(2,1)}, bf16[2,2,512,256]{3,2,1,0:T(8,128)(2,1)}, u32[]{:S(2)}, u32[]{:S(2)}) collective-permute-start(bf16[2,2,512,256]{3,2,1,0:T(8,128)(2,1)} %get-tuple-element.31), channel_id=1, source_target_pairs={{1,0},{3,2},{4,5},{6,7},{9,8},{11,10},{12,13},{14,15},{17,16},{19,... | collective-permute-start | bytes 3145736 | tf_op jit(solution)/shard_map/ppermute | solution.py:230
  251.1 27.2 %collective-permute-start.21 = (bf16[2,2,256,512]{3,2,1,0:T(8,128)(2,1)}, bf16[2,2,256,512]{3,2,1,0:T(8,128)(2,1)}, u32[]{:S(2)}, u32[]{:S(2)}) collective-permute-start(bf16[2,2,256,512]{3,2,1,0:T(8,128)(2,1)} %collective-permute-done.20.site_ref), channel_id=1, source_target_pairs={{0,4},{4,8},{8,12},{12,0},{1,5},{5,9},{9,13},{13,1},{2,6},{6,10},{... | collective-permute-start | bytes 3145736 | tf_op jit(solution)/shard_map/ppermute | solution.py:146
  256.4 58.2 %collective-permute-start.27 = (bf16[2,2,512,256]{3,2,1,0:T(8,128)(2,1)}, bf16[2,2,512,256]{3,2,1,0:T(8,128)(2,1)}, u32[]{:S(2)}, u32[]{:S(2)}) collective-permute-start(bf16[2,2,512,256]{3,2,1,0:T(8,128)(2,1)} %get-tuple-element.38), channel_id=1, source_target_pairs={{0,1},{2,3},{5,4},{7,6},{8,9},{10,11},{13,12},{15,14},{16,17},{18,... | collective-permute-start | bytes 3145736 | tf_op jit(solution)/shard_map/ppermute | solution.py:230
  257.7 43.1 %collective-permute-start.11 = (bf16[2,2,256,512]{3,2,1,0:T(8,128)(2,1)}, bf16[2,2,256,512]{3,2,1,0:T(8,128)(2,1)S(1)}, u32[]{:S(2)}, u32[]{:S(2)}) collective-permute-start(bf16[2,2,256,512]{3,2,1,0:T(8,128)(2,1)} %collective-permute-done.10.site_ref), channel_id=1, source_target_pairs={{0,4},{4,8},{8,12},{12,0},{1,5},{5,9},{9,13},{13,1},{2,6},{6,10},{... | collective-permute-start | bytes 3145736 | tf_op jit(solution)/shard_map/ppermute | solution.py:146
  262.6 78.2 %copy-start.2 = (f32[2,2,512,256]{3,2,1,0:T(8,128)}, f32[2,2,512,256]{3,2,1,0:T(8,128)S(1)}, u32[]{:S(2)}) copy-start(f32[2,2,512,256]{3,2,1,0:T(8,128)S(1)} %get-tuple-element.39) | copy-start | bytes 6291460
  268.6 64.3 %copy-start.4 = (f32[2,2,512,256]{3,2,1,0:T(8,128)}, f32[2,2,512,256]{3,2,1,0:T(8,128)S(1)}, u32[]{:S(2)}) copy-start(f32[2,2,512,256]{3,2,1,0:T(8,128)S(1)} %get-tuple-element.26) | copy-start | bytes 6291460
  268.6 65.9 %collective-permute-start.29 = (bf16[2,2,512,256]{3,2,1,0:T(8,128)(2,1)S(1)}, bf16[2,2,512,256]{3,2,1,0:T(8,128)(2,1)}, u32[]{:S(2)}, u32[]{:S(2)}) collective-permute-start(bf16[2,2,512,256]{3,2,1,0:T(8,128)(2,1)S(1)} %get-tuple-element.40), channel_id=1, source_target_pairs={{1,0},{3,2},{4,5},{6,7},{9,8},{11,10},{12,13},{14,15},{17,16},{19,... | collective-permute-start | bytes 3145736 | tf_op jit(solution)/shard_map/ppermute | solution.py:230
  275.4 56.2 %collective-permute-start.14 = (bf16[2,2,512,256]{3,2,1,0:T(8,128)(2,1)}, bf16[2,2,512,256]{3,2,1,0:T(8,128)(2,1)}, u32[]{:S(2)}, u32[]{:S(2)}) collective-permute-start(bf16[2,2,512,256]{3,2,1,0:T(8,128)(2,1)} %get-tuple-element.27), channel_id=1, source_target_pairs={{1,0},{3,2},{4,5},{6,7},{9,8},{11,10},{12,13},{14,15},{17,16},{19,... | collective-permute-start | bytes 3145736 | tf_op jit(solution)/shard_map/ppermute | solution.py:230
  278.3 43.7 %collective-permute-start.22 = (bf16[2,2,256,512]{3,2,1,0:T(8,128)(2,1)}, bf16[2,2,256,512]{3,2,1,0:T(8,128)(2,1)S(1)}, u32[]{:S(2)}, u32[]{:S(2)}) collective-permute-start(bf16[2,2,256,512]{3,2,1,0:T(8,128)(2,1)} %collective-permute-done.21.site_ref), channel_id=1, source_target_pairs={{0,4},{4,8},{8,12},{12,0},{1,5},{5,9},{9,13},{13,1},{2,6},{6,10},{... | collective-permute-start | bytes 3145736 | tf_op jit(solution)/shard_map/ppermute | solution.py:146
  300.8 1.0 copy-start.13
  301.8 1.2 copy-start.14
  308.0 28.9 %copy-start.7 = (f32[2,2,512,256]{3,2,1,0:T(8,128)}, f32[2,2,512,256]{3,2,1,0:T(8,128)S(1)}, u32[]{:S(2)}) copy-start(f32[2,2,512,256]{3,2,1,0:T(8,128)S(1)} %get-tuple-element.24) | copy-start | bytes 6291460
  308.0 27.3 %collective-permute-start.12 = (bf16[2,2,512,256]{3,2,1,0:T(8,128)(2,1)}, bf16[2,2,512,256]{3,2,1,0:T(8,128)(2,1)}, u32[]{:S(2)}, u32[]{:S(2)}) collective-permute-start(bf16[2,2,512,256]{3,2,1,0:T(8,128)(2,1)} %get-tuple-element.25), channel_id=1, source_target_pairs={{0,1},{2,3},{5,4},{7,6},{8,9},{10,11},{13,12},{15,14},{16,17},{18,... | collective-permute-start | bytes 3145736 | tf_op jit(solution)/shard_map/ppermute | solution.py:230
  314.6 28.6 %copy-start.5 = (f32[2,2,512,256]{3,2,1,0:T(8,128)}, f32[2,2,512,256]{3,2,1,0:T(8,128)S(1)}, u32[]{:S(2)}) copy-start(f32[2,2,512,256]{3,2,1,0:T(8,128)S(1)} %get-tuple-element.35) | copy-start | bytes 6291460
  314.6 24.8 %collective-permute-start.25 = (bf16[2,2,512,256]{3,2,1,0:T(8,128)(2,1)}, bf16[2,2,512,256]{3,2,1,0:T(8,128)(2,1)}, u32[]{:S(2)}, u32[]{:S(2)}) collective-permute-start(bf16[2,2,512,256]{3,2,1,0:T(8,128)(2,1)} %get-tuple-element.36), channel_id=1, source_target_pairs={{1,0},{3,2},{4,5},{6,7},{9,8},{11,10},{12,13},{14,15},{17,16},{19,... | collective-permute-start | bytes 3145736 | tf_op jit(solution)/shard_map/ppermute | solution.py:230
  322.1 1.0 copy-start.15
  323.1 29.8 %collective-permute-start.17 = (bf16[2,2,512,256]{3,2,1,0:T(8,128)(2,1)}, bf16[2,2,512,256]{3,2,1,0:T(8,128)(2,1)}, u32[]{:S(2)}, u32[]{:S(2)}) collective-permute-start(bf16[2,2,512,256]{3,2,1,0:T(8,128)(2,1)} %fusion.10), channel_id=1, source_target_pairs={{1,3},{6,4},{11,9},{12,14},{17,19},{22,20},{27,25},{28,30}} | collective-permute-start | bytes 3145736 | tf_op jit(solution)/shard_map/ppermute | solution.py:242
  326.2 1.2 copy-start.16
  331.7 20.0 %copy-start.8 = (f32[2,2,512,256]{3,2,1,0:T(8,128)}, f32[2,2,512,256]{3,2,1,0:T(8,128)S(1)}, u32[]{:S(2)}) copy-start(f32[2,2,512,256]{3,2,1,0:T(8,128)S(1)} %get-tuple-element.33) | copy-start | bytes 6291460
  331.7 14.0 %collective-permute-start.23 = (bf16[2,2,512,256]{3,2,1,0:T(8,128)(2,1)S(1)}, bf16[2,2,512,256]{3,2,1,0:T(8,128)(2,1)S(1)}, u32[]{:S(2)}, u32[]{:S(2)}) collective-permute-start(bf16[2,2,512,256]{3,2,1,0:T(8,128)(2,1)S(1)} %get-tuple-element.34), channel_id=1, source_target_pairs={{0,1},{2,3},{5,4},{7,6},{8,9},{10,11},{13,12},{15,14},{16,17},{18,... | collective-permute-start | bytes 3145736 | tf_op jit(solution)/shard_map/ppermute | solution.py:230
  333.0 1.6 copy-start.21
  334.6 20.0 %collective-permute-start.19 = (bf16[2,2,512,256]{3,2,1,0:T(8,128)(2,1)S(1)}, bf16[2,2,512,256]{3,2,1,0:T(8,128)(2,1)S(1)}, u32[]{:S(2)}, u32[]{:S(2)}) collective-permute-start(bf16[2,2,512,256]{3,2,1,0:T(8,128)(2,1)S(1)} %copy-done.21), channel_id=1, source_target_pairs={{2,0},{7,5},{8,10},{13,15},{18,16},{23,21},{24,26},{29,31}} | collective-permute-start | bytes 3145736 | tf_op jit(solution)/shard_map/ppermute | solution.py:242
  335.3 20.9 %collective-permute-start.15 = (bf16[2,2,512,256]{3,2,1,0:T(8,128)(2,1)S(1)}, bf16[2,2,512,256]{3,2,1,0:T(8,128)(2,1)}, u32[]{:S(2)}, u32[]{:S(2)}) collective-permute-start(bf16[2,2,512,256]{3,2,1,0:T(8,128)(2,1)S(1)} %fusion.9), channel_id=1, source_target_pairs={{0,2},{5,7},{10,8},{15,13},{16,18},{21,23},{26,24},{31,29}} | collective-permute-start | bytes 3145736 | tf_op jit(solution)/shard_map/ppermute | solution.py:242
  339.4 27.3 %collective-permute-start.13 = (bf16[2,2,512,256]{3,2,1,0:T(8,128)(2,1)}, bf16[2,2,512,256]{3,2,1,0:T(8,128)(2,1)}, u32[]{:S(2)}, u32[]{:S(2)}) collective-permute-start(bf16[2,2,512,256]{3,2,1,0:T(8,128)(2,1)} %fusion.8), channel_id=1, source_target_pairs={{3,1},{4,6},{9,11},{14,12},{19,17},{20,22},{25,27},{30,28}} | collective-permute-start | bytes 3145736 | tf_op jit(solution)/shard_map/ppermute | solution.py:242
  345.7 7.2 %copy-start.18 = (bf16[2,2,512,256]{3,2,1,0:T(8,128)(2,1)}, bf16[2,2,512,256]{3,2,1,0:T(8,128)(2,1)S(1)}, u32[]{:S(2)}) copy-start(bf16[2,2,512,256]{3,2,1,0:T(8,128)(2,1)S(1)} %collective-permute-done.23) | copy-start | bytes 3145732
  345.7 28.2 %collective-permute-start.28 = (bf16[2,2,512,256]{3,2,1,0:T(8,128)(2,1)}, bf16[2,2,512,256]{3,2,1,0:T(8,128)(2,1)}, u32[]{:S(2)}, u32[]{:S(2)}) collective-permute-start(bf16[2,2,512,256]{3,2,1,0:T(8,128)(2,1)} %fusion.14), channel_id=1, source_target_pairs={{1,3},{6,4},{11,9},{12,14},{17,19},{22,20},{27,25},{28,30}} | collective-permute-start | bytes 3145736 | tf_op jit(solution)/shard_map/ppermute | solution.py:242
  352.9 21.0 %collective-permute-start.30 = (bf16[2,2,512,256]{3,2,1,0:T(8,128)(2,1)}, bf16[2,2,512,256]{3,2,1,0:T(8,128)(2,1)}, u32[]{:S(2)}, u32[]{:S(2)}) collective-permute-start(bf16[2,2,512,256]{3,2,1,0:T(8,128)(2,1)} %fusion.15), channel_id=1, source_target_pairs={{2,0},{7,5},{8,10},{13,15},{18,16},{23,21},{24,26},{29,31}} | collective-permute-start | bytes 3145736 | tf_op jit(solution)/shard_map/ppermute | solution.py:242
  354.5 19.3 %collective-permute-start.26 = (bf16[2,2,512,256]{3,2,1,0:T(8,128)(2,1)}, bf16[2,2,512,256]{3,2,1,0:T(8,128)(2,1)}, u32[]{:S(2)}, u32[]{:S(2)}) collective-permute-start(bf16[2,2,512,256]{3,2,1,0:T(8,128)(2,1)} %fusion.13), channel_id=1, source_target_pairs={{0,2},{5,7},{10,8},{15,13},{16,18},{21,23},{26,24},{31,29}} | collective-permute-start | bytes 3145736 | tf_op jit(solution)/shard_map/ppermute | solution.py:242
  356.3 29.3 %collective-permute-start.24 = (bf16[2,2,512,256]{3,2,1,0:T(8,128)(2,1)}, bf16[2,2,512,256]{3,2,1,0:T(8,128)(2,1)}, u32[]{:S(2)}, u32[]{:S(2)}) collective-permute-start(bf16[2,2,512,256]{3,2,1,0:T(8,128)(2,1)} %fusion.12), channel_id=1, source_target_pairs={{3,1},{4,6},{9,11},{14,12},{19,17},{20,22},{25,27},{30,28}} | collective-permute-start | bytes 3145736 | tf_op jit(solution)/shard_map/ppermute | solution.py:242
  357.6 28.0 %copy-start.3 = (f32[2,2,512,256]{3,2,1,0:T(8,128)S(1)}, f32[2,2,512,256]{3,2,1,0:T(8,128)}, u32[]{:S(2)}) copy-start(f32[2,2,512,256]{3,2,1,0:T(8,128)} %copy-done.2) | copy-start | bytes 6291460
  357.6 28.0 %copy-start.6 = (f32[2,2,512,256]{3,2,1,0:T(8,128)S(1)}, f32[2,2,512,256]{3,2,1,0:T(8,128)}, u32[]{:S(2)}) copy-start(f32[2,2,512,256]{3,2,1,0:T(8,128)} %copy-done.5) | copy-start | bytes 6291460
  357.6 28.0 %copy-start.9 = (f32[2,2,512,256]{3,2,1,0:T(8,128)S(1)}, f32[2,2,512,256]{3,2,1,0:T(8,128)}, u32[]{:S(2)}) copy-start(f32[2,2,512,256]{3,2,1,0:T(8,128)} %copy-done.8) | copy-start | bytes 6291460
  357.6 28.0 %copy-start.19 = (bf16[2,2,512,256]{3,2,1,0:T(8,128)(2,1)S(1)}, bf16[2,2,512,256]{3,2,1,0:T(8,128)(2,1)}, u32[]{:S(2)}) copy-start(bf16[2,2,512,256]{3,2,1,0:T(8,128)(2,1)} %copy-done.18) | copy-start | bytes 3145732

commit v2 on v0

v2 whole, which is shorter than its diff:
```python
import jax
import jax.numpy as jnp
from jax import lax
from jax.experimental import pallas as pl
from jax.experimental.pallas import tpu as pltpu
from jax.sharding import PartitionSpec as P

F32 = jnp.float32
BF16 = jnp.bfloat16
VMEM_BYTES = 56 * 1024 * 1024


def params(steps):
    return pltpu.CompilerParams(
        dimension_semantics=("arbitrary",) * steps, vmem_limit_bytes=VMEM_BYTES
    )


def mul(left, right):
    return jnp.dot(left, right, preferred_element_type=F32)


def mul_t(left, right):
    return lax.dot_general(left, right, (((1,), (1,)), ((), ())), preferred_element_type=F32)


def first_kernel(place_ref, mpo_ref, site_ref, *refs):
    g_ref, q_ref = refs[-1], refs[-2]
    env_refs = refs[:-2]
    blocks = len(env_refs) // 2
    w_local = env_refs[0].shape[0]
    mpo_count, phys, _, rows, cols = q_ref.shape
    for which in range(2):
        for w in range(w_local):
            g_real, g_imag = None, None
            for block in range(blocks):
                piece = place_ref[block]
                depth = site_ref.shape[-1]
                real = site_ref[piece, :, 0].reshape(phys * rows, depth)
                imag = site_ref[piece, :, 1].reshape(phys * rows, depth)
                env_real = env_refs[block * 2 + which][w, 0]
                env_imag = env_refs[block * 2 + which][w, 1]
                more_real = mul(real, env_real) + mul(imag, env_imag)
                more_imag = mul(real, env_imag) + mul(imag, -env_real)
                g_real = more_real if g_real is None else g_real + more_real
                g_imag = more_imag if g_imag is None else g_imag + more_imag
            g_ref[which * w_local + w, 0] = g_real
            g_ref[which * w_local + w, 1] = g_imag
    for part in range(2):
        for v in range(mpo_count):
            for t in range(phys):
                total = None
                for w in range(2 * w_local):
                    for s in range(phys):
                        term = mpo_ref[w, v, s, t] * g_ref[w, part, s * rows : (s + 1) * rows]
                        total = term if total is None else total + term
                q_ref[v, t, part] = total.astype(BF16)


def first_product(place, mpo, site, envs, row_tile, col_tile):
    pieces, phys, _, rows, depth = site.shape
    w_local, _, _, cols = envs[0].shape
    mpo_count = mpo.shape[1]
    row_tile, col_tile = min(row_tile, rows), min(col_tile, cols)
    env_spec = pl.BlockSpec((w_local, 2, depth, col_tile), lambda i, j: (0, 0, 0, j))
    smem = pl.BlockSpec(memory_space=pltpu.SMEM)
    return pl.pallas_call(
        first_kernel,
        grid=(rows // row_tile, cols // col_tile),
        in_specs=[
            smem,
            smem,
            pl.BlockSpec((pieces, phys, 2, row_tile, depth), lambda i, j: (0, 0, 0, i, 0)),
        ]
        + [env_spec] * len(envs),
        out_specs=pl.BlockSpec(
            (mpo_count, phys, 2, row_tile, col_tile), lambda i, j: (0, 0, 0, i, j)
        ),
        out_shape=jax.ShapeDtypeStruct((mpo_count, phys, 2, rows, cols), BF16),
        scratch_shapes=[pltpu.VMEM((2 * w_local, 2, phys * row_tile, col_tile), F32)],
        compiler_params=params(2),
        cost_estimate=pl.CostEstimate(
            flops=8 * len(envs) * w_local * phys * rows * depth * cols,
            bytes_accessed=2 * (site.size + len(envs) * envs[0].size) + 4 * mpo_count * phys * rows * cols,
            transcendentals=0,
        ),
        name="first_product",
    )(place, mpo, site, *envs)


def second_kernel(flip_ref, q_one, q_two, site_even, site_odd, *outs):
    def work(site_keep, site_send):
        for q_ref, wide_ref, low_ref in ((q_one, outs[0], outs[2]), (q_two, outs[1], outs[3])):
            for site_ref, out_ref in ((site_keep, wide_ref), (site_send, low_ref)):
                out_real, out_imag = None, None
                for t in range(q_ref.shape[1]):
                    q_real, q_imag = q_ref[0, t, 0], q_ref[0, t, 1]
                    real, imag = site_ref[t, 0], site_ref[t, 1]
                    more_real = mul_t(q_real, real) + mul_t(-q_imag, imag)
                    more_imag = mul_t(q_real, imag) + mul_t(q_imag, real)
                    out_real = more_real if out_real is None else out_real + more_real
                    out_imag = more_imag if out_imag is None else out_imag + more_imag
                out_ref[0, 0] = out_real.astype(out_ref.dtype)
                out_ref[0, 1] = out_imag.astype(out_ref.dtype)

    @pl.when(flip_ref[0] == 0)
    def _():
        work(site_even, site_odd)

    @pl.when(flip_ref[0] != 0)
    def _():
        work(site_odd, site_even)


def second_product(flip, q_one, q_two, site_even, site_odd, row_tile):
    mpo_count, phys, _, rows, cols = q_one.shape
    y_rows = site_even.shape[2]
    row_tile = min(row_tile, rows)
    out_spec = pl.BlockSpec((1, 2, row_tile, y_rows), lambda v, i: (v, 0, i, 0))
    q_spec = pl.BlockSpec((1, phys, 2, row_tile, cols), lambda v, i: (v, 0, 0, i, 0))
    site_spec = pl.BlockSpec((phys, 2, y_rows, cols), lambda v, i: (0, 0, 0, 0))
    shape = (mpo_count, 2, rows, y_rows)
    return pl.pallas_call(
        second_kernel,
        grid=(mpo_count, rows // row_tile),
        in_specs=[pl.BlockSpec(memory_space=pltpu.SMEM), q_spec, q_spec, site_spec, site_spec],
        out_specs=[out_spec] * 4,
        out_shape=[jax.ShapeDtypeStruct(shape, kind) for kind in (F32, F32, BF16, BF16)],
        compiler_params=params(2),
        cost_estimate=pl.CostEstimate(
            flops=32 * mpo_count * phys * rows * y_rows * cols,
            bytes_accessed=q_one.size * 4 + site_even.size * 4 + 24 * mpo_count * rows * y_rows,
            transcendentals=0,
        ),
        name="second_product",
    )(flip, q_one, q_two, site_even, site_odd)


def after(value, *earlier):
    return lax.optimization_barrier((value,) + earlier)[0]


def swap(value):
    return lax.ppermute(value, "depth", [(0, 1), (1, 0)])


def by_depth(depth, mine, sibling):
    return jnp.where(depth == 0, jnp.stack([mine, sibling]), jnp.stack([sibling, mine]))


def split_inputs(environment, site_tensor, mpo):
    depth = lax.axis_index("depth")
    w_local, _, rows, half = environment.shape
    phys = site_tensor.shape[0]
    cols = half // 2
    env_own = lax.dynamic_slice_in_dim(environment, depth * cols, cols, 3)
    env_sib = swap(lax.dynamic_slice_in_dim(environment, (1 - depth) * cols, cols, 3))
    mpo_mine = jnp.concatenate(
        [
            lax.dynamic_slice_in_dim(mpo, depth * w_local, w_local, 0),
            lax.dynamic_slice_in_dim(mpo, (1 - depth) * w_local, w_local, 0),
        ],
        axis=0,
    )
    planar = jnp.transpose(site_tensor.reshape(phys, rows, 2, 2, cols), (3, 0, 2, 1, 4))
    return env_own, env_sib, mpo_mine, planar


def any_line(environment, site_tensor, mpo):
    col_count, depth = lax.axis_size("col"), lax.axis_index("depth")
    env_own, env_sib, mpo_mine, planar = split_inputs(environment, site_tensor, mpo)
    site_own = lax.dynamic_index_in_dim(planar, depth, 0, keepdims=False)
    cols = site_own.shape[3]
    pieces = col_count * 2
    gathered = lax.all_gather(site_own, "col", axis=0)
    site = jnp.moveaxis(by_depth(depth, gathered, swap(gathered)), 0, 1)
    site = site.reshape((pieces,) + site_own.shape)
    env_own = lax.all_gather(env_own, "row", axis=2, tiled=True)
    env_sib = lax.all_gather(env_sib, "row", axis=2, tiled=True)
    envs = []
    for index in range(pieces):
        block = slice(index * cols, (index + 1) * cols)
        envs += [env_own[:, :, block], env_sib[:, :, block]]
    q = first_product(jnp.arange(pieces, dtype=jnp.int32), mpo_mine, site, envs, 256, 256)
    site_all = lax.all_gather(site_own, "row", axis=2, tiled=True)
    total = None
    for t in range(q.shape[1]):
        q_real, q_imag = q[:, t, 0], q[:, t, 1]
        real, imag = site_all[t, 0], site_all[t, 1]
        one = lambda a, b: jnp.einsum("vxc,yc->vxy", a, b, preferred_element_type=F32)
        more = jnp.stack(
            [one(q_real, real) - one(q_imag, imag), one(q_real, imag) + one(q_imag, real)], axis=1
        )
        total = more if total is None else total + more
    return lax.psum_scatter(total, ("col", "depth"), scatter_dimension=3, tiled=True)


def four_rows(environment, site_tensor, mpo):
    row, col, depth = (lax.axis_index(axis) for axis in ("row", "col", "depth"))
    rows = site_tensor.shape[1]
    axes = ("row", "col", "depth")
    place = lambda r, c, d: (r * 2 + c) * 2 + d
    to_host = lambda value: lax.ppermute(value, "row", [(0, 1), (3, 2)])
    to_end = lambda value: lax.ppermute(value, "row", [(1, 0), (2, 3)])
    across = lambda value: lax.ppermute(value, "row", [(1, 2), (2, 1)])
    turn = lambda value: lax.ppermute(value, "col", [(0, 1), (1, 0)])

    def to_col(value, which_rows, far):
        pairs = []
        for r in which_rows:
            goal = r // 2 if not far else 1 - r // 2
            pairs += [(place(r, 1 - goal, d), place(r, goal, d)) for d in range(2)]
        return lax.ppermute(value, axes, pairs)

    env_own, env_sib, mpo_mine, planar = split_inputs(environment, site_tensor, mpo)
    end_own, end_sib = to_host(env_own), to_host(env_sib)
    over_own, over_sib = across(env_own), across(env_sib)
    over_end_own, over_end_sib = across(end_own), across(end_sib)

    planar = after(planar, env_sib)
    site_own = lax.dynamic_index_in_dim(planar, depth, 0, keepdims=False)
    other = turn(site_own)
    here = jnp.concatenate([planar, by_depth(depth, other, swap(other))], axis=0)

    chunks = 2
    y_rows = rows // chunks
    own_chunks = [site_own[:, :, m * y_rows : (m + 1) * y_rows] for m in range(chunks)]
    end_chunks, there = [], []
    gate = end_sib
    for m in range(chunks):
        chunk = to_host(after(own_chunks[m], gate))
        gate = chunk
        other = turn(chunk)
        there.append(
            jnp.concatenate(
                [by_depth(depth, chunk, swap(chunk)), by_depth(depth, other, swap(other))], axis=0
            )
        )
        end_chunks.append(chunk)
    end_site = jnp.concatenate(end_chunks, axis=2)
    there = jnp.concatenate(there, axis=3)

    base = row // 2
    blocks = [row, base * 4 + 1 - row, 3 - row, 3 - (base * 4 + 1 - row)]
    piece = jnp.stack([jnp.where(b // 2 == col, 0, 2) + b % 2 for b in blocks]).astype(jnp.int32)
    envs = [env_own, env_sib, end_own, end_sib, over_own, over_sib, over_end_own, over_end_sib]
    q_here = first_product(piece, mpo_mine, here, envs, 256, 256)
    q_there = first_product(piece, mpo_mine, there, envs, 256, 256)

    is_host = (row == 1) | (row == 2)

    def outputs(site_one, site_two, flip, far):
        keep_here, keep_there, send_here, send_there = second_product(
            flip.astype(jnp.int32).reshape(1), q_here, q_there, site_one, site_two, 256
        )
        low_there = (keep_there + swap(send_there).astype(F32)).astype(BF16)
        sum_here = keep_here + swap(send_here).astype(F32)
        came_here = to_col(sum_here.astype(BF16), (1, 2), far)
        came_there = to_end(low_there)
        turned = to_col(came_there, (0, 3), far)
        total = jnp.where(is_host, sum_here, 0.0)
        for more in (came_here, came_there, turned):
            total = total + more.astype(F32)
        return total

    near = outputs(site_own, end_site, depth != row % 2, False)
    far, gates = [], (over_end_sib, over_end_sib)
    for m in range(chunks):
        over_site = across(after(own_chunks[m], gates[0]))
        over_end_site = across(after(end_chunks[m], gates[1]))
        gates = (over_site, over_end_site)
        far.append(outputs(over_site, over_end_site, depth == row % 2, True))
    far = jnp.concatenate(far, axis=3)
    return jnp.where(col == row // 2, near, far)


def solution(mesh):
    placed = (
        P(("groups", "depth"), None, "row", "col"),
        P("groups", "row", None, "col"),
        P("groups", None, None, None),
    )
    line = mesh.shape["row"] == 4 and mesh.shape["col"] == 2 and mesh.shape["depth"] == 2
    return jax.shard_map(
        four_rows if line else any_line,
        mesh=mesh,
        in_specs=placed,
        out_specs=P("groups", None, "row", ("col", "depth")),
        check_vma=False,
    )
```

time: 742 us -> 450 us (0.61)
  waiting for transfers between devices: 535 us -> 209 us
  matrix products: 115 us -> 0 us
  Pallas kernels: 0 us -> 97.7 us
  starting transfers between devices: 0.16 us -> 60.3 us
  other arithmetic: 10.7 us -> 51.3 us
  local copies, waits for them, and re-layouts: 66.2 us -> 28.9 us
  between operations: 13.2 us -> 0.3 us
    all_gather x3 -> x0, waiting for transfers between devices: 389 us -> none  [the longest x1 144 us: on_device(): lax.all_gather(own_site, 'row', axis=1, tiled=True)]
    ppermute x0 -> x36, waiting for transfers between devices: none -> 209 us  [the longest x3 137 us: four_rows(): to_end = lambda value: lax.ppermute(value, 'row', [(1, 0), (2, 3)])]
    reduce_scatter x2 -> x0, waiting for transfers between devices: 144 us -> none  [the longest x1 124 us: on_device(): lax.psum_scatter(partial_env, ('col', 'depth'), scatter_dimension=3, tile...]
    dot_general x3 -> x0, matrix products: 115 us -> none  [the longest x1 58 us: on_device(): jnp.einsum('wvst,wspxc->vtpxc', mpo_mine, g_local, precision=highest)]
    pallas_call x0 -> x5, Pallas kernels: none -> 97.7 us  [the longest x3 49.7 us: second_product(): pl.pallas_call(second_kernel, grid=(mpo_count, rows // row_tile), in_spec...]
    ppermute x0 -> x36, starting transfers between devices: none -> 60.3 us  [the longest x4 14.7 us: four_rows(): to_host = lambda value: lax.ppermute(value, 'row', [(0, 1), (3, 2)])]
    select_n x0 -> x6, other arithmetic: none -> 22.7 us  [the longest x5 17.7 us: by_depth(): jnp.where(depth == 0, jnp.stack([mine, sibling]), jnp.stack([sibling, min...]
    reshape x2 -> x1, local copies, waits for them, and re-layouts: 28.9 us -> 7.33 us  [split_inputs(): site_tensor.reshape(phys, rows, 2, 2, cols)]
  transfers between devices with their start and end apart: 5 -> 36, of which waited for: 5 -> 9; matrix products, arithmetic and copies ran while one was open for 4% -> 15% of each run, Pallas kernels for 0% -> 22%
where the time goes in v2:
time: 450 us; the launch traced here: 447 us
  waiting for transfers between devices  209 us (46%)
  Pallas kernels  97.7 us (22%)
  starting transfers between devices  60.3 us (13%)
  other arithmetic  51.3 us (11%)
  local copies, waits for them, and re-layouts  28.9 us (6%)
    ppermute x3, waiting for transfers between devices, four_rows(): to_end = lambda value: lax.ppermute(value, 'row', [(1, 0), (2, 3)])  137 us
    pallas_call x3, Pallas kernels, second_product(): pl.pallas_call(second_kernel, grid=(mpo_count, rows // row_tile), in_spec...  49.7 us
    pallas_call x2, Pallas kernels, first_product(): pl.pallas_call(first_kernel, grid=(rows // row_tile, cols // col_tile), i...  47.9 us
    ppermute x3, waiting for transfers between devices, four_rows(): turn = lambda value: lax.ppermute(value, 'col', [(0, 1), (1, 0)])  29.4 us
    ppermute x4, waiting for transfers between devices, four_rows(): to_host = lambda value: lax.ppermute(value, 'row', [(0, 1), (3, 2)])  20.8 us
    ppermute x6, waiting for transfers between devices, to_col(): return lax.ppermute(value, axes, pairs)  18.5 us
    select_n x5, other arithmetic, by_depth(): jnp.where(depth == 0, jnp.stack([mine, sibling]), jnp.stack([sibling, min...  17.7 us
    unnamed x47, local copies, waits for them, and re-layouts  15.9 us
  transfers between devices with their start and end apart: 36, of which 9 were waited for; matrix products, arithmetic and copies ran while one was open for 15% of the time, Pallas kernels for 22%

profile of v2, /device:TPU:1, one launch (start us, length us, event | category | flops | bytes accessed | tf_op | source)
XLA Modules:
  0.0 447.2 jit_solution(13409908712974234679)
XLA Ops:
  0.0 2.7 constant_dynamic-slice_fusion
  2.8 2.7 collective-permute-done.refs_1_
  5.5 5.3 %collective-permute-start.4 = (bf16[1,2,512,512]{3,2,1,0:T(8,128)(2,1)}, bf16[1,2,512,512]{3,2,1,0:T(8,128)(2,1)}, u32[]{:S(2)}, u32[]{:S(2)}) collective-permute-start(bf16[1,2,512,512]{3,2,1,0:T(8,128)(2,1)} %collective-permute-done.refs_1_), channel_id=1, source_target_pairs={{0,4},{12,8},{1,5},{13,9},{2,6},{14,10},{3,7},{15,11},{16,20},{28,... | collective-permute-start | bytes 3145736 | tf_op jit(solution)/shard_map/ppermute | solution.py:203
  10.8 11.1 %copy.4 = bf16[2,512,2,1024]{1,3,2,0:T(8,128)(2,1)} copy(bf16[2,512,2,1024]{3,2,1,0:T(2,128)(2,1)} %param.4) | data formatting | bytes 8388608 | tf_op args[1]
  22.0 7.3 %copy.5 = bf16[2,512,2,2,512]{4,1,2,0,3:T(8,128)(2,1)} copy(bf16[2,512,2,2,512]{1,4,3,2,0:T(8,128)(2,1)} %bitcast.22) | data formatting | bytes 8388608 | tf_op jit(solution)/shard_map/reshape | solution.py:165
  29.3 1.7 dynamic-slice_bitcast_fusion.site_even
  31.0 1.3 collective-permute-start.1
  32.3 1.2 fusion.3
  33.5 3.0 collective-permute-start.9
  36.5 0.7 collective-permute-start.8
  37.2 20.7 %collective-permute-done.9 = bf16[2,2,256,512]{3,2,1,0:T(8,128)(2,1)S(1)} collective-permute-done((bf16[2,2,256,512]{3,2,1,0:T(8,128)(2,1)}, bf16[2,2,256,512]{3,2,1,0:T(8,128)(2,1)S(1)}, u32[]{:S(2)}, u32[]{:S(2)}) %collective-permute-start.9) | collective-permute-done | bytes 1048608 | tf_op jit(solution)/shard_map/ppermute | solution.py:203
  58.0 4.2 collective-permute-start.13
  62.1 1.3 collective-permute-start.11
  63.4 14.3 %collective-permute-done.1 = bf16[2,2,512,512]{3,2,1,0:T(8,128)(2,1)} collective-permute-done((bf16[2,2,512,512]{3,2,1,0:T(8,128)(2,1)S(1)}, bf16[2,2,512,512]{3,2,1,0:T(8,128)(2,1)}, u32[]{:S(2)}, u32[]{:S(2)}) %collective-permute-start.1) | collective-permute-done | bytes 2097184 | tf_op jit(solution)/shard_map/ppermute | solution.py:206
  77.7 2.6 collective-permute-start.2
  80.4 2.3 collective-permute-start.3
  82.7 5.3 %collective-permute-start.14 = (bf16[2,2,256,512]{3,2,1,0:T(8,128)(2,1)S(1)}, bf16[2,2,256,512]{3,2,1,0:T(8,128)(2,1)}, u32[]{:S(2)}, u32[]{:S(2)}) collective-permute-start(bf16[2,2,256,512]{3,2,1,0:T(8,128)(2,1)S(1)} %collective-permute-done.13), channel_id=1, source_target_pairs={{0,1},{1,0},{2,3},{3,2},{4,5},{5,4},{6,7},{7,6},{8,9},{9,8},{10,11... | collective-permute-start | bytes 3145736 | tf_op jit(solution)/shard_map/ppermute | solution.py:144
  88.0 12.2 %collective-permute-done.11 = bf16[2,2,256,512]{3,2,1,0:T(8,128)(2,1)} collective-permute-done((bf16[2,2,256,512]{3,2,1,0:T(8,128)(2,1)S(1)}, bf16[2,2,256,512]{3,2,1,0:T(8,128)(2,1)}, u32[]{:S(2)}, u32[]{:S(2)}) %collective-permute-start.11) | collective-permute-done | bytes 1048608 | tf_op jit(solution)/shard_map/ppermute | solution.py:206
  100.2 1.5 collective-permute-start.12
  103.0 1.5 pad_maximum_fusion.1.site_odd
  104.5 1.7 collective-permute-start.5
  106.2 2.6 maximum_select_fusion.2
  108.8 1.7 collective-permute-start.6
  110.4 1.7 collective-permute-start.7
  112.1 3.2 maximum_select_fusion.4
  115.3 1.2 collective-permute-start.15
  116.6 4.0 maximum_select_fusion.3
  120.6 1.7 collective-permute-start.22
  122.3 5.9 %maximum_select_fusion = bf16[2,2,2,512,512]{4,3,2,1,0:T(8,128)(2,1)} fusion(bf16[1,2,2,512,512]{4,3,2,1,0:T(8,128)(2,1)} %bitcast.9, bf16[1,2,2,512,512]{4,3,2,1,0:T(8,128)(2,1)} %bitcast.8, pred[]{:T(512)S(6)} %eq.47), kind=kLoop, calls=%fused_computation.2 | loop fusion | flops 6291456 | bytes 8388609 | tf_op jit(solution)/shard_map/jit(_where)/select_n | solution.py:148
  128.1 7.5 %pad_maximum_fusion.site_ref = bf16[4,2,2,512,512]{4,3,2,1,0:T(8,128)(2,1)} fusion(bf16[2,2,2,512,512]{4,3,2,1,0:T(8,128)(2,1)} %maximum_select_fusion, bf16[2,2,2,512,512]{4,3,2,1,0:T(8,128)(2,1)} %bitcast.21), kind=kLoop, calls=%fused_computation | loop fusion | flops 4194304 | bytes 16777216 | tf_op jit(solution)/shard_map/concatenate | solution.py:223
  135.6 1.6 collective-permute-start.23
  137.3 2.8 collective-permute-done.15
  140.1 0.9 collective-permute-start.16
  141.0 23.9 %first_product.2.q_one = bf16[2,2,2,512,512]{4,3,2,1,0:T(8,128)(2,1)} custom-call(s32[4]{0:T(128)} %pad_add_fusion.place_ref, f32[2,2,2,2]{3,2,1,0:T(2,128)} %pad_maximum_fusion.2.mpo_ref, bf16[4,2,2,512,512]{4,3,2,1,0:T(8,128)(2,1)} %pad_maximum_fusion.site_ref, bf16[1,2,512,512]{3,2,1,0:T(8,128)(2,1)} %get-tuple-element.45.refs_0_, ...), custom_call_target="tpu_custom_call" | custom-call | flops 17179869184 | bytes 20971520 | tf_op jit(solution)/shard_map/first_product/pallas_call | solution.py:67
  165.0 2.0 maximum_select_fusion.5
  167.8 3.7 maximum_maximum_fusion.site_ref
  171.5 24.0 %first_product.3.q_two = bf16[2,2,2,512,512]{4,3,2,1,0:T(8,128)(2,1)} custom-call(s32[4]{0:T(128)} %pad_add_fusion.place_ref, f32[2,2,2,2]{3,2,1,0:T(2,128)} %pad_maximum_fusion.2.mpo_ref, bf16[4,2,2,512,512]{4,3,2,1,0:T(8,128)(2,1)} %maximum_maximum_fusion.site_ref, bf16[1,2,512,512]{3,2,1,0:T(8,128)(2,1)} %get-tuple-element.45.refs_0_, ...), custom_call_target="tpu_custom_call" | custom-call | flops 17179869184 | bytes 20971520 | tf_op jit(solution)/shard_map/first_product/pallas_call | solution.py:67
  195.5 23.2 %second_product.3 = (f32[2,2,512,512]{3,2,1,0:T(8,128)}, f32[2,2,512,512]{3,2,1,0:T(8,128)}, bf16[2,2,512,512]{3,2,1,0:T(8,128)(2,1)}, bf16[2,2,512,512]{3,2,1,0:T(8,128)(2,1)}) custom-call(s32[1]{0:T(128)} %bitcast.flip_ref, bf16[2,2,2,512,512]{4,3,2,1,0:T(8,128)(2,1)} %first_product.2.q_one, bf16[2,2,2,512,512]{4,3,2,1,0:T(8,128)(2,1)} %first_product.3.q_two, ...), custom_call_target="tpu_custom_call" | custom-call | flops 17179869184 | bytes 25165824 | tf_op jit(solution)/shard_map/second_product/pallas_call | solution.py:123
  219.5 1.7 collective-permute-start.30
  221.1 1.0 copy-done.22
  222.1 13.2 %second_product.5 = (f32[2,2,512,256]{3,2,1,0:T(8,128)}, f32[2,2,512,256]{3,2,1,0:T(8,128)}, bf16[2,2,512,256]{3,2,1,0:T(8,128)(2,1)}, bf16[2,2,512,256]{3,2,1,0:T(8,128)(2,1)}) custom-call(s32[1]{0:T(128)} %bitcast.18.flip_ref, bf16[2,2,2,512,512]{4,3,2,1,0:T(8,128)(2,1)} %first_product.2.q_one, bf16[2,2,2,512,512]{4,3,2,1,0:T(8,128)(2,1)} %first_product.3.q_two, ...), custom_call_target="tpu_custom_call" | custom-call | flops 8589934592 | bytes 16777216 | tf_op jit(solution)/shard_map/second_product/pallas_call | solution.py:123
  236.3 3.6 add_convert_fusion
  239.9 1.4 collective-permute-start.20
  241.3 13.4 %second_product.4 = (f32[2,2,512,256]{3,2,1,0:T(8,128)}, f32[2,2,512,256]{3,2,1,0:T(8,128)}, bf16[2,2,512,256]{3,2,1,0:T(8,128)(2,1)}, bf16[2,2,512,256]{3,2,1,0:T(8,128)(2,1)}) custom-call(s32[1]{0:T(128)} %bitcast.18.flip_ref, bf16[2,2,2,512,512]{4,3,2,1,0:T(8,128)(2,1)} %first_product.2.q_one, bf16[2,2,2,512,512]{4,3,2,1,0:T(8,128)(2,1)} %first_product.3.q_two, ...), custom_call_target="tpu_custom_call" | custom-call | flops 8589934592 | bytes 16777216 | tf_op jit(solution)/shard_map/second_product/pallas_call | solution.py:123
  255.2 1.6 add_convert_fusion.1
  256.8 1.3 collective-permute-start.34
  258.4 0.9 collective-permute-start.32
  260.1 1.6 collective-permute-start.27
  261.7 1.0 copy-done
  262.7 2.2 fusion
  264.9 2.1 collective-permute-start.18
  267.0 101.9 %collective-permute-done.20 = bf16[2,2,512,512]{3,2,1,0:T(8,128)(2,1)} collective-permute-done((bf16[2,2,512,512]{3,2,1,0:T(8,128)(2,1)}, bf16[2,2,512,512]{3,2,1,0:T(8,128)(2,1)}, u32[]{:S(2)}, u32[]{:S(2)}) %collective-permute-start.20) | collective-permute-done | bytes 2097184 | tf_op jit(solution)/shard_map/ppermute | solution.py:204
  368.9 1.3 collective-permute-start.21
  370.2 21.2 %collective-permute-done.34 = bf16[2,2,512,256]{3,2,1,0:T(8,128)(2,1)} collective-permute-done((bf16[2,2,512,256]{3,2,1,0:T(8,128)(2,1)S(1)}, bf16[2,2,512,256]{3,2,1,0:T(8,128)(2,1)}, u32[]{:S(2)}, u32[]{:S(2)}) %collective-permute-start.34) | collective-permute-done | bytes 1048608 | tf_op jit(solution)/shard_map/ppermute | solution.py:204
  391.3 4.1 collective-permute-start.35
  395.4 1.3 fusion.1
  396.7 1.0 copy-done.17
  397.7 1.7 collective-permute-start.25
  399.4 14.4 %collective-permute-done.27 = bf16[2,2,512,256]{3,2,1,0:T(8,128)(2,1)} collective-permute-done((bf16[2,2,512,256]{3,2,1,0:T(8,128)(2,1)S(1)}, bf16[2,2,512,256]{3,2,1,0:T(8,128)(2,1)}, u32[]{:S(2)}, u32[]{:S(2)}) %collective-permute-start.27) | collective-permute-done | bytes 1048608 | tf_op jit(solution)/shard_map/ppermute | solution.py:204
  413.8 4.1 collective-permute-start.28
  417.9 2.6 convert_add_fusion.1
  420.6 18.5 %collective-permute-done.28 = bf16[2,2,512,256]{3,2,1,0:T(8,128)(2,1)} collective-permute-done((bf16[2,2,512,256]{3,2,1,0:T(8,128)(2,1)}, bf16[2,2,512,256]{3,2,1,0:T(8,128)(2,1)}, u32[]{:S(2)}, u32[]{:S(2)}) %collective-permute-start.28) | collective-permute-done | bytes 1048608 | tf_op jit(solution)/shard_map/ppermute | solution.py:213
  439.1 2.6 convert_add_fusion.3
  442.2 5.0 %maximum_select_fusion.1 = f32[2,2,512,512]{3,2,1,0:T(8,128)} fusion(f32[2,2,512,256]{3,2,1,0:T(8,128)S(1)} %convert_add_fusion.1, f32[2,2,512,256]{3,2,1,0:T(8,128)S(1)} %convert_add_fusion.3, bf16[2,2,512,512]{3,2,1,0:T(8,128)(2,1)} %collective-permute-done.21, bf16[2,2,512,512]{3,2,1,0:T(8,128)(2,1)} %collective-permute-done.20, ...), kind=kLoop, calls=%fused_computation.3 | loop fusion | flops 11534336 | bytes 20971522 | tf_op jit(solution)/shard_map/jit(_where)/select_n | solution.py:274
  (84 shorter events, 6.1 us)
Async XLA Ops:
  2.7 2.8 collective-permute-start
  5.5 28.0 %collective-permute-start.4 = (bf16[1,2,512,512]{3,2,1,0:T(8,128)(2,1)}, bf16[1,2,512,512]{3,2,1,0:T(8,128)(2,1)}, u32[]{:S(2)}, u32[]{:S(2)}) collective-permute-start(bf16[1,2,512,512]{3,2,1,0:T(8,128)(2,1)} %collective-permute-done.refs_1_), channel_id=1, source_target_pairs={{0,4},{12,8},{1,5},{13,9},{2,6},{14,10},{3,7},{15,11},{16,20},{28,... | collective-permute-start | bytes 3145736 | tf_op jit(solution)/shard_map/ppermute | solution.py:203
  31.0 2.5 copy-start.2
  31.0 71.4 %copy-start.20 = (f32[2,2,2,2]{3,2,1,0:T(2,128)S(1)}, f32[2,2,2,2]{3,2,1,0:T(2,128)}, u32[]{:S(2)}) copy-start(f32[2,2,2,2]{3,2,1,0:T(2,128)} %param.5) | copy-start | bytes 196
  31.0 46.7 %collective-permute-start.1 = (bf16[2,2,512,512]{3,2,1,0:T(8,128)(2,1)S(1)}, bf16[2,2,512,512]{3,2,1,0:T(8,128)(2,1)}, u32[]{:S(2)}, u32[]{:S(2)}) collective-permute-start(bf16[2,2,512,512]{3,2,1,0:T(8,128)(2,1)S(1)} %dynamic-slice_bitcast_fusion.site_even), channel_id=1, source_target_pairs={{0,2},{2,0},{1,3},{3,1},{4,6},{6,4},{5,7},{7,5},{8,10},{10,8},{9,1... | collective-permute-start | bytes 6291464 | tf_op jit(solution)/shard_map/ppermute | solution.py:206
  33.5 66.7 %copy-start.18 = (bf16[2,2,256,512]{3,2,1,0:T(8,128)(2,1)}, bf16[2,2,256,512]{3,2,1,0:T(8,128)(2,1)S(1)}, u32[]{:S(2)}) copy-start(bf16[2,2,256,512]{3,2,1,0:T(8,128)(2,1)S(1)} %get-tuple-element.37) | copy-start | bytes 3145732
  33.5 24.4 %collective-permute-start.9 = (bf16[2,2,256,512]{3,2,1,0:T(8,128)(2,1)}, bf16[2,2,256,512]{3,2,1,0:T(8,128)(2,1)S(1)}, u32[]{:S(2)}, u32[]{:S(2)}) collective-permute-start(bf16[2,2,256,512]{3,2,1,0:T(8,128)(2,1)} %get-tuple-element.31), channel_id=1, source_target_pairs={{0,4},{12,8},{1,5},{13,9},{2,6},{14,10},{3,7},{15,11},{16,20},{28,... | collective-permute-start | bytes 3145736 | tf_op jit(solution)/shard_map/ppermute | solution.py:203
  36.5 43.9 %collective-permute-start.8 = (bf16[1,2,512,512]{3,2,1,0:T(8,128)(2,1)}, bf16[1,2,512,512]{3,2,1,0:T(8,128)(2,1)S(1)}, u32[]{:S(2)}, u32[]{:S(2)}) collective-permute-start(bf16[1,2,512,512]{3,2,1,0:T(8,128)(2,1)} %collective-permute-done.4.refs_3_), channel_id=1, source_target_pairs={{4,8},{8,4},{5,9},{9,5},{6,10},{10,6},{7,11},{11,7},{20,24},{24,20... | collective-permute-start | bytes 3145736 | tf_op jit(solution)/shard_map/ppermute | solution.py:205
  58.0 46.5 %copy-start.11 = (bf16[2,2,256,512]{3,2,1,0:T(8,128)(2,1)}, bf16[2,2,256,512]{3,2,1,0:T(8,128)(2,1)S(1)}, u32[]{:S(2)}) copy-start(bf16[2,2,256,512]{3,2,1,0:T(8,128)(2,1)S(1)} %collective-permute-done.9) | copy-start | bytes 3145732
  58.0 24.7 %collective-permute-start.13 = (bf16[2,2,256,512]{3,2,1,0:T(8,128)(2,1)S(1)}, bf16[2,2,256,512]{3,2,1,0:T(8,128)(2,1)S(1)}, u32[]{:S(2)}, u32[]{:S(2)}) collective-permute-start(bf16[2,2,256,512]{3,2,1,0:T(8,128)(2,1)S(1)} %get-tuple-element.37), channel_id=1, source_target_pairs={{0,4},{12,8},{1,5},{13,9},{2,6},{14,10},{3,7},{15,11},{16,20},{28,... | collective-permute-start | bytes 3145736 | tf_op jit(solution)/shard_map/ppermute | solution.py:203
  62.1 38.1 %collective-permute-start.11 = (bf16[2,2,256,512]{3,2,1,0:T(8,128)(2,1)S(1)}, bf16[2,2,256,512]{3,2,1,0:T(8,128)(2,1)}, u32[]{:S(2)}, u32[]{:S(2)}) collective-permute-start(bf16[2,2,256,512]{3,2,1,0:T(8,128)(2,1)S(1)} %collective-permute-done.9), channel_id=1, source_target_pairs={{0,2},{2,0},{1,3},{3,1},{4,6},{6,4},{5,7},{7,5},{8,10},{10,8},{9,1... | collective-permute-start | bytes 3145736 | tf_op jit(solution)/shard_map/ppermute | solution.py:206
  77.7 42.8 %collective-permute-start.2 = (bf16[2,2,512,512]{3,2,1,0:T(8,128)(2,1)}, bf16[2,2,512,512]{3,2,1,0:T(8,128)(2,1)}, u32[]{:S(2)}, u32[]{:S(2)}) collective-permute-start(bf16[2,2,512,512]{3,2,1,0:T(8,128)(2,1)} %collective-permute-done.1), channel_id=1, source_target_pairs={{0,1},{1,0},{2,3},{3,2},{4,5},{5,4},{6,7},{7,6},{8,9},{9,8},{10,11... | collective-permute-start | bytes 6291464 | tf_op jit(solution)/shard_map/ppermute | solution.py:144
  80.4 24.1 %collective-permute-start.10 = (bf16[2,2,256,512]{3,2,1,0:T(8,128)(2,1)S(1)}, bf16[2,2,256,512]{3,2,1,0:T(8,128)(2,1)S(1)}, u32[]{:S(2)}, u32[]{:S(2)}) collective-permute-start(bf16[2,2,256,512]{3,2,1,0:T(8,128)(2,1)S(1)} %collective-permute-done.9), channel_id=1, source_target_pairs={{0,1},{1,0},{2,3},{3,2},{4,5},{5,4},{6,7},{7,6},{8,9},{9,8},{10,11... | collective-permute-start | bytes 3145736 | tf_op jit(solution)/shard_map/ppermute | solution.py:144
  80.4 19.8 %copy-start.21 = (bf16[1,2,512,512]{3,2,1,0:T(8,128)(2,1)}, bf16[1,2,512,512]{3,2,1,0:T(8,128)(2,1)S(1)}, u32[]{:S(2)}) copy-start(bf16[1,2,512,512]{3,2,1,0:T(8,128)(2,1)S(1)} %collective-permute-done.8.refs_7_) | copy-start | bytes 3145732
  80.4 28.4 %collective-permute-start.3 = (bf16[1,2,512,512]{3,2,1,0:T(8,128)(2,1)}, bf16[1,2,512,512]{3,2,1,0:T(8,128)(2,1)}, u32[]{:S(2)}, u32[]{:S(2)}) collective-permute-start(bf16[1,2,512,512]{3,2,1,0:T(8,128)(2,1)} %get-tuple-element.45.refs_0_), channel_id=1, source_target_pairs={{0,4},{12,8},{1,5},{13,9},{2,6},{14,10},{3,7},{15,11},{16,20},{28,... | collective-permute-start | bytes 3145736 | tf_op jit(solution)/shard_map/ppermute | solution.py:203
  82.7 27.7 %collective-permute-start.14 = (bf16[2,2,256,512]{3,2,1,0:T(8,128)(2,1)S(1)}, bf16[2,2,256,512]{3,2,1,0:T(8,128)(2,1)}, u32[]{:S(2)}, u32[]{:S(2)}) collective-permute-start(bf16[2,2,256,512]{3,2,1,0:T(8,128)(2,1)S(1)} %collective-permute-done.13), channel_id=1, source_target_pairs={{0,1},{1,0},{2,3},{3,2},{4,5},{5,4},{6,7},{7,6},{8,9},{9,8},{10,11... | collective-permute-start | bytes 3145736 | tf_op jit(solution)/shard_map/ppermute | solution.py:144
  100.2 15.1 %collective-permute-start.12 = (bf16[2,2,256,512]{3,2,1,0:T(8,128)(2,1)}, bf16[2,2,256,512]{3,2,1,0:T(8,128)(2,1)}, u32[]{:S(2)}, u32[]{:S(2)}) collective-permute-start(bf16[2,2,256,512]{3,2,1,0:T(8,128)(2,1)} %collective-permute-done.11), channel_id=1, source_target_pairs={{0,1},{1,0},{2,3},{3,2},{4,5},{5,4},{6,7},{7,6},{8,9},{9,8},{10,11... | collective-permute-start | bytes 3145736 | tf_op jit(solution)/shard_map/ppermute | solution.py:144
  104.5 1.7 copy-start.16
  104.5 31.1 %collective-permute-start.5 = (bf16[1,2,512,512]{3,2,1,0:T(8,128)(2,1)}, bf16[1,2,512,512]{3,2,1,0:T(8,128)(2,1)}, u32[]{:S(2)}, u32[]{:S(2)}) collective-permute-start(bf16[1,2,512,512]{3,2,1,0:T(8,128)(2,1)} %get-tuple-element.45.refs_0_), channel_id=1, source_target_pairs={{4,8},{8,4},{5,9},{9,5},{6,10},{10,6},{7,11},{11,7},{20,24},{24,20... | collective-permute-start | bytes 3145736 | tf_op jit(solution)/shard_map/ppermute | solution.py:205
  108.8 32.3 %collective-permute-start.6 = (bf16[1,2,512,512]{3,2,1,0:T(8,128)(2,1)}, bf16[1,2,512,512]{3,2,1,0:T(8,128)(2,1)}, u32[]{:S(2)}, u32[]{:S(2)}) collective-permute-start(bf16[1,2,512,512]{3,2,1,0:T(8,128)(2,1)} %collective-permute-done.refs_1_), channel_id=1, source_target_pairs={{4,8},{8,4},{5,9},{9,5},{6,10},{10,6},{7,11},{11,7},{20,24},{24,20... | collective-permute-start | bytes 3145736 | tf_op jit(solution)/shard_map/ppermute | solution.py:205
  110.4 30.6 %collective-permute-start.7 = (bf16[1,2,512,512]{3,2,1,0:T(8,128)(2,1)}, bf16[1,2,512,512]{3,2,1,0:T(8,128)(2,1)}, u32[]{:S(2)}, u32[]{:S(2)}) collective-permute-start(bf16[1,2,512,512]{3,2,1,0:T(8,128)(2,1)} %collective-permute-done.3.refs_2_), channel_id=1, source_target_pairs={{4,8},{8,4},{5,9},{9,5},{6,10},{10,6},{7,11},{11,7},{20,24},{24,20... | collective-permute-start | bytes 3145736 | tf_op jit(solution)/shard_map/ppermute | solution.py:205
  115.3 24.7 %collective-permute-start.15 = (bf16[2,2,256,512]{3,2,1,0:T(8,128)(2,1)S(1)}, bf16[2,2,256,512]{3,2,1,0:T(8,128)(2,1)}, u32[]{:S(2)}, u32[]{:S(2)}) collective-permute-start(bf16[2,2,256,512]{3,2,1,0:T(8,128)(2,1)S(1)} %collective-permute-done.13), channel_id=1, source_target_pairs={{0,2},{2,0},{1,3},{3,1},{4,6},{6,4},{5,7},{7,5},{8,10},{10,8},{9,1... | collective-permute-start | bytes 3145736 | tf_op jit(solution)/shard_map/ppermute | solution.py:206
  120.6 98.2 %collective-permute-start.22 = (bf16[2,2,256,512]{3,2,1,0:T(8,128)(2,1)}, bf16[2,2,256,512]{3,2,1,0:T(8,128)(2,1)}, u32[]{:S(2)}, u32[]{:S(2)}) collective-permute-start(bf16[2,2,256,512]{3,2,1,0:T(8,128)(2,1)} %get-tuple-element.31), channel_id=1, source_target_pairs={{4,8},{8,4},{5,9},{9,5},{6,10},{10,6},{7,11},{11,7},{20,24},{24,20... | collective-permute-start | bytes 3145736 | tf_op jit(solution)/shard_map/ppermute | solution.py:205
  135.6 83.8 %collective-permute-start.23 = (bf16[2,2,256,512]{3,2,1,0:T(8,128)(2,1)}, bf16[2,2,256,512]{3,2,1,0:T(8,128)(2,1)}, u32[]{:S(2)}, u32[]{:S(2)}) collective-permute-start(bf16[2,2,256,512]{3,2,1,0:T(8,128)(2,1)} %copy-done.11), channel_id=1, source_target_pairs={{4,8},{8,4},{5,9},{9,5},{6,10},{10,6},{7,11},{11,7},{20,24},{24,20... | collective-permute-start | bytes 3145736 | tf_op jit(solution)/shard_map/ppermute | solution.py:205
  140.1 24.9 %collective-permute-start.16 = (bf16[2,2,256,512]{3,2,1,0:T(8,128)(2,1)}, bf16[2,2,256,512]{3,2,1,0:T(8,128)(2,1)S(1)}, u32[]{:S(2)}, u32[]{:S(2)}) collective-permute-start(bf16[2,2,256,512]{3,2,1,0:T(8,128)(2,1)} %collective-permute-done.15), channel_id=1, source_target_pairs={{0,1},{1,0},{2,3},{3,2},{4,5},{5,4},{6,7},{7,6},{8,9},{9,8},{10,11... | collective-permute-start | bytes 3145736 | tf_op jit(solution)/shard_map/ppermute | solution.py:144
  165.0 2.2 copy-start.6
  165.0 2.8 copy-start.7
  195.5 23.2 %copy-start.19 = (bf16[2,2,256,512]{3,2,1,0:T(8,128)(2,1)S(1)}, bf16[2,2,256,512]{3,2,1,0:T(8,128)(2,1)}, u32[]{:S(2)}) copy-start(bf16[2,2,256,512]{3,2,1,0:T(8,128)(2,1)} %copy-done.18) | copy-start | bytes 3145732
  218.7 17.6 %collective-permute-start.19 = (bf16[2,2,512,512]{3,2,1,0:T(8,128)(2,1)}, bf16[2,2,512,512]{3,2,1,0:T(8,128)(2,1)}, u32[]{:S(2)}, u32[]{:S(2)}) collective-permute-start(bf16[2,2,512,512]{3,2,1,0:T(8,128)(2,1)} %get-tuple-element.30), channel_id=1, source_target_pairs={{0,1},{1,0},{2,3},{3,2},{4,5},{5,4},{6,7},{7,6},{8,9},{9,8},{10,11... | collective-permute-start | bytes 6291464 | tf_op jit(solution)/shard_map/ppermute | solution.py:144
  218.7 2.4 collective-permute-start.29
  219.5 1.7 collective-permute-start.30
  221.1 1.0 copy-start.22
  222.1 14.2 %copy-start.10 = (f32[2,2,512,512]{3,2,1,0:T(8,128)S(1)}, f32[2,2,512,512]{3,2,1,0:T(8,128)}, u32[]{:S(2)}) copy-start(f32[2,2,512,512]{3,2,1,0:T(8,128)} %get-tuple-element.29) | copy-start | bytes 12582916
  235.3 19.5 %collective-permute-start.33 = (bf16[2,2,512,256]{3,2,1,0:T(8,128)(2,1)}, bf16[2,2,512,256]{3,2,1,0:T(8,128)(2,1)}, u32[]{:S(2)}, u32[]{:S(2)}) collective-permute-start(bf16[2,2,512,256]{3,2,1,0:T(8,128)(2,1)} %get-tuple-element.42), channel_id=1, source_target_pairs={{0,1},{1,0},{2,3},{3,2},{4,5},{5,4},{6,7},{7,6},{8,9},{9,8},{10,11... | collective-permute-start | bytes 3145736 | tf_op jit(solution)/shard_map/ppermute | solution.py:144
  235.8 21.1 %collective-permute-start.31 = (bf16[2,2,512,256]{3,2,1,0:T(8,128)(2,1)}, bf16[2,2,512,256]{3,2,1,0:T(8,128)(2,1)S(1)}, u32[]{:S(2)}, u32[]{:S(2)}) collective-permute-start(bf16[2,2,512,256]{3,2,1,0:T(8,128)(2,1)} %get-tuple-element.40), channel_id=1, source_target_pairs={{0,1},{1,0},{2,3},{3,2},{4,5},{5,4},{6,7},{7,6},{8,9},{9,8},{10,11... | collective-permute-start | bytes 3145736 | tf_op jit(solution)/shard_map/ppermute | solution.py:144
  235.8 24.3 %collective-permute-start.17 = (bf16[2,2,512,512]{3,2,1,0:T(8,128)(2,1)}, bf16[2,2,512,512]{3,2,1,0:T(8,128)(2,1)S(1)}, u32[]{:S(2)}, u32[]{:S(2)}) collective-permute-start(bf16[2,2,512,512]{3,2,1,0:T(8,128)(2,1)} %get-tuple-element.28), channel_id=1, source_target_pairs={{0,1},{1,0},{2,3},{3,2},{4,5},{5,4},{6,7},{7,6},{8,9},{9,8},{10,11... | collective-permute-start | bytes 6291464 | tf_op jit(solution)/shard_map/ppermute | solution.py:144
  239.9 15.3 %copy-start.14 = (f32[2,2,512,256]{3,2,1,0:T(8,128)S(1)}, f32[2,2,512,256]{3,2,1,0:T(8,128)}, u32[]{:S(2)}) copy-start(f32[2,2,512,256]{3,2,1,0:T(8,128)} %get-tuple-element.41) | copy-start | bytes 6291460
  239.9 129.0 %collective-permute-start.20 = (bf16[2,2,512,512]{3,2,1,0:T(8,128)(2,1)}, bf16[2,2,512,512]{3,2,1,0:T(8,128)(2,1)}, u32[]{:S(2)}, u32[]{:S(2)}) collective-permute-start(bf16[2,2,512,512]{3,2,1,0:T(8,128)(2,1)} %add_convert_fusion), channel_id=1, source_target_pairs={{4,0},{8,12},{5,1},{9,13},{6,2},{10,14},{7,3},{11,15},{20,16},{24,... | collective-permute-start | bytes 6291464 | tf_op jit(solution)/shard_map/ppermute | solution.py:204
  254.7 3.7 collective-permute-start.26
  254.8 10.2 %collective-permute-start.24 = (bf16[2,2,512,256]{3,2,1,0:T(8,128)(2,1)}, bf16[2,2,512,256]{3,2,1,0:T(8,128)(2,1)S(1)}, u32[]{:S(2)}, u32[]{:S(2)}) collective-permute-start(bf16[2,2,512,256]{3,2,1,0:T(8,128)(2,1)} %get-tuple-element.34), channel_id=1, source_target_pairs={{0,1},{1,0},{2,3},{3,2},{4,5},{5,4},{6,7},{7,6},{8,9},{9,8},{10,11... | collective-permute-start | bytes 3145736 | tf_op jit(solution)/shard_map/ppermute | solution.py:144
  255.2 2.9 copy-start.3
  256.8 134.5 %collective-permute-start.34 = (bf16[2,2,512,256]{3,2,1,0:T(8,128)(2,1)S(1)}, bf16[2,2,512,256]{3,2,1,0:T(8,128)(2,1)}, u32[]{:S(2)}, u32[]{:S(2)}) collective-permute-start(bf16[2,2,512,256]{3,2,1,0:T(8,128)(2,1)S(1)} %add_convert_fusion.1), channel_id=1, source_target_pairs={{4,0},{8,12},{5,1},{9,13},{6,2},{10,14},{7,3},{11,15},{20,16},{24,... | collective-permute-start | bytes 3145736 | tf_op jit(solution)/shard_map/ppermute | solution.py:204
  258.2 1.6 copy-start.15
  258.4 138.3 %collective-permute-start.32 = (bf16[2,2,512,256]{3,2,1,0:T(8,128)(2,1)S(1)}, bf16[2,2,512,256]{3,2,1,0:T(8,128)(2,1)S(1)}, u32[]{:S(2)}, u32[]{:S(2)}) collective-permute-start(bf16[2,2,512,256]{3,2,1,0:T(8,128)(2,1)S(1)} %fusion.2), channel_id=1, source_target_pairs={{4,6},{5,7},{10,8},{11,9},{20,22},{21,23},{26,24},{27,25}} | collective-permute-start | bytes 3145736 | tf_op jit(solution)/shard_map/ppermute | solution.py:213
  259.7 2.9 copy-start
  260.1 4.8 %copy-start.8 = (bf16[2,2,512,512]{3,2,1,0:T(8,128)(2,1)}, bf16[2,2,512,512]{3,2,1,0:T(8,128)(2,1)S(1)}, u32[]{:S(2)}) copy-start(bf16[2,2,512,512]{3,2,1,0:T(8,128)(2,1)S(1)} %collective-permute-done.17) | copy-start | bytes 6291460
  260.1 153.7 %collective-permute-start.27 = (bf16[2,2,512,256]{3,2,1,0:T(8,128)(2,1)S(1)}, bf16[2,2,512,256]{3,2,1,0:T(8,128)(2,1)}, u32[]{:S(2)}, u32[]{:S(2)}) collective-permute-start(bf16[2,2,512,256]{3,2,1,0:T(8,128)(2,1)S(1)} %add_convert_fusion.2), channel_id=1, source_target_pairs={{4,0},{8,12},{5,1},{9,13},{6,2},{10,14},{7,3},{11,15},{20,16},{24,... | collective-permute-start | bytes 3145736 | tf_op jit(solution)/shard_map/ppermute | solution.py:204
  262.7 132.7 %copy-start.4 = (f32[2,2,512,256]{3,2,1,0:T(8,128)S(1)}, f32[2,2,512,256]{3,2,1,0:T(8,128)}, u32[]{:S(2)}) copy-start(f32[2,2,512,256]{3,2,1,0:T(8,128)} %get-tuple-element.33) | copy-start | bytes 6291460
  264.9 131.8 %copy-start.12 = (bf16[2,2,512,256]{3,2,1,0:T(8,128)(2,1)}, bf16[2,2,512,256]{3,2,1,0:T(8,128)(2,1)S(1)}, u32[]{:S(2)}) copy-start(bf16[2,2,512,256]{3,2,1,0:T(8,128)(2,1)S(1)} %collective-permute-done.24) | copy-start | bytes 3145732
  264.9 176.8 %collective-permute-start.18 = (bf16[2,2,512,512]{3,2,1,0:T(8,128)(2,1)}, bf16[2,2,512,512]{3,2,1,0:T(8,128)(2,1)}, u32[]{:S(2)}, u32[]{:S(2)}) collective-permute-start(bf16[2,2,512,512]{3,2,1,0:T(8,128)(2,1)} %fusion), channel_id=1, source_target_pairs={{6,4},{7,5},{8,10},{9,11},{22,20},{23,21},{24,26},{25,27}} | collective-permute-start | bytes 6291464 | tf_op jit(solution)/shard_map/ppermute | solution.py:213
  368.9 72.9 %collective-permute-start.21 = (bf16[2,2,512,512]{3,2,1,0:T(8,128)(2,1)}, bf16[2,2,512,512]{3,2,1,0:T(8,128)(2,1)}, u32[]{:S(2)}, u32[]{:S(2)}) collective-permute-start(bf16[2,2,512,512]{3,2,1,0:T(8,128)(2,1)} %collective-permute-done.20), channel_id=1, source_target_pairs={{2,0},{3,1},{12,14},{13,15},{18,16},{19,17},{28,30},{29,31}} | collective-permute-start | bytes 6291464 | tf_op jit(solution)/shard_map/ppermute | solution.py:213
  391.3 26.6 %collective-permute-start.35 = (bf16[2,2,512,256]{3,2,1,0:T(8,128)(2,1)}, bf16[2,2,512,256]{3,2,1,0:T(8,128)(2,1)}, u32[]{:S(2)}, u32[]{:S(2)}) collective-permute-start(bf16[2,2,512,256]{3,2,1,0:T(8,128)(2,1)} %collective-permute-done.34), channel_id=1, source_target_pairs={{0,2},{1,3},{14,12},{15,13},{16,18},{17,19},{30,28},{31,29}} | collective-permute-start | bytes 3145736 | tf_op jit(solution)/shard_map/ppermute | solution.py:213
  396.7 1.0 copy-start.17
  397.7 22.8 %collective-permute-start.25 = (bf16[2,2,512,256]{3,2,1,0:T(8,128)(2,1)}, bf16[2,2,512,256]{3,2,1,0:T(8,128)(2,1)}, u32[]{:S(2)}, u32[]{:S(2)}) collective-permute-start(bf16[2,2,512,256]{3,2,1,0:T(8,128)(2,1)} %fusion.1), channel_id=1, source_target_pairs={{4,6},{5,7},{10,8},{11,9},{20,22},{21,23},{26,24},{27,25}} | collective-permute-start | bytes 3145736 | tf_op jit(solution)/shard_map/ppermute | solution.py:213
  413.8 25.3 %collective-permute-start.28 = (bf16[2,2,512,256]{3,2,1,0:T(8,128)(2,1)}, bf16[2,2,512,256]{3,2,1,0:T(8,128)(2,1)}, u32[]{:S(2)}, u32[]{:S(2)}) collective-permute-start(bf16[2,2,512,256]{3,2,1,0:T(8,128)(2,1)} %collective-permute-done.27), channel_id=1, source_target_pairs={{0,2},{1,3},{14,12},{15,13},{16,18},{17,19},{30,28},{31,29}} | collective-permute-start | bytes 3145736 | tf_op jit(solution)/shard_map/ppermute | solution.py:213
  417.9 21.2 %copy-start.5 = (f32[2,2,512,256]{3,2,1,0:T(8,128)S(1)}, f32[2,2,512,256]{3,2,1,0:T(8,128)}, u32[]{:S(2)}) copy-start(f32[2,2,512,256]{3,2,1,0:T(8,128)} %get-tuple-element.33) | copy-start | bytes 6291460
  417.9 21.2 %copy-start.13 = (bf16[2,2,512,256]{3,2,1,0:T(8,128)(2,1)S(1)}, bf16[2,2,512,256]{3,2,1,0:T(8,128)(2,1)}, u32[]{:S(2)}) copy-start(bf16[2,2,512,256]{3,2,1,0:T(8,128)(2,1)} %copy-done.12) | copy-start | bytes 3145732
  420.5 21.2 %copy-start.9 = (bf16[2,2,512,512]{3,2,1,0:T(8,128)(2,1)S(1)}, bf16[2,2,512,512]{3,2,1,0:T(8,128)(2,1)}, u32[]{:S(2)}) copy-start(bf16[2,2,512,512]{3,2,1,0:T(8,128)(2,1)} %copy-done.8) | copy-start | bytes 6291460
  439.1 3.1 copy-start.1

commit v3 on v0

v3 whole, which is shorter than its diff:
```python
import functools
import jax
import jax.numpy as jnp
from jax import lax
from jax.experimental import pallas as pl
from jax.experimental.pallas import tpu as pltpu
from jax.sharding import PartitionSpec as P

F32 = jnp.float32
BF16 = jnp.bfloat16
VMEM_BYTES = 56 * 1024 * 1024
LIGHT = pl.CostEstimate(flops=0, bytes_accessed=0, transcendentals=0)


def params(steps):
    return pltpu.CompilerParams(
        dimension_semantics=("arbitrary",) * steps, vmem_limit_bytes=VMEM_BYTES
    )


def mul(left, right):
    return jnp.dot(left, right, preferred_element_type=F32)


def mul_t(left, right):
    return lax.dot_general(left, right, (((1,), (1,)), ((), ())), preferred_element_type=F32)


def first_kernel(w_local, block_ref, mpo_ref, site_ref, *refs):
    q_ref, g_ref = refs[-2:]
    env_refs = refs[:-2]
    mpo_count, phys, _, rows, _ = q_ref.shape
    depth = site_ref.shape[-1]
    for which in range(2):
        for w in range(w_local):
            g_real, g_imag = None, None
            for block in range(len(env_refs) // 2):
                piece = block_ref[block]
                real = site_ref[piece, :, 0].reshape(phys * rows, depth)
                imag = site_ref[piece, :, 1].reshape(phys * rows, depth)
                env_real = env_refs[block * 2 + which][w, 0]
                env_imag = env_refs[block * 2 + which][w, 1]
                more_real = mul(real, env_real) + mul(imag, env_imag)
                more_imag = mul(real, env_imag) + mul(imag, -env_real)
                g_real = more_real if g_real is None else g_real + more_real
                g_imag = more_imag if g_imag is None else g_imag + more_imag
            g_ref[which * w_local + w, 0] = g_real
            g_ref[which * w_local + w, 1] = g_imag
    for part in range(2):
        for v in range(mpo_count):
            for t in range(phys):
                total = None
                for w in range(2 * w_local):
                    for s in range(phys):
                        term = mpo_ref[w, v, s, t] * g_ref[w, part, s * rows : (s + 1) * rows]
                        total = term if total is None else total + term
                q_ref[v, t, part] = total.astype(BF16)


def first_product(blocks, mpo, site, envs, col_tile):
    pieces, phys, _, rows, depth = site.shape
    w_local, _, _, cols = envs[0].shape
    mpo_count = mpo.shape[1]
    col_tile = min(col_tile, cols)
    smem = pl.BlockSpec(memory_space=pltpu.SMEM)
    return pl.pallas_call(
        functools.partial(first_kernel, w_local),
        grid=(cols // col_tile,),
        in_specs=[smem, smem, pl.BlockSpec((pieces, phys, 2, rows, depth), lambda j: (0, 0, 0, 0, 0))]
        + [pl.BlockSpec((w_local, 2, depth, col_tile), lambda j: (0, 0, 0, j))] * len(envs),
        out_specs=pl.BlockSpec((mpo_count, phys, 2, rows, col_tile), lambda j: (0, 0, 0, 0, j)),
        out_shape=jax.ShapeDtypeStruct((mpo_count, phys, 2, rows, cols), BF16),
        scratch_shapes=[pltpu.VMEM((2 * w_local, 2, phys * rows, col_tile), F32)],
        compiler_params=params(1),
        cost_estimate=LIGHT,
        name="first_product",
    )(blocks, mpo, site, *envs)


def second_kernel(tiles, sets, pick_ref, *refs):
    q_refs, out_ref = refs[: 2 * tiles], refs[-1]
    site_refs = refs[2 * tiles : -1]
    per_set = len(site_refs) // sets
    phys, _, rows, _ = q_refs[0].shape[1:]
    mine = pick_ref[0]

    def work(chosen):
        y_first = 0
        for site_ref in chosen:
            y_rows = site_ref.shape[3]
            for tile in range(tiles):
                out_real, out_imag = None, None
                for which in range(2):
                    quarter = mine if which == 0 else 1 - mine
                    q_ref = q_refs[tile * 2 + which]
                    for t in range(phys):
                        q_real, q_imag = q_ref[0, t, 0], q_ref[0, t, 1]
                        real, imag = site_ref[quarter, t, 0], site_ref[quarter, t, 1]
                        more_real = mul_t(q_real, real) + mul_t(-q_imag, imag)
                        more_imag = mul_t(q_real, imag) + mul_t(q_imag, real)
                        out_real = more_real if out_real is None else out_real + more_real
                        out_imag = more_imag if out_imag is None else out_imag + more_imag
                there = (slice(tile * rows, (tile + 1) * rows), slice(y_first, y_first + y_rows))
                out_ref[(0, 0) + there] = out_real.astype(BF16)
                out_ref[(0, 1) + there] = out_imag.astype(BF16)
            y_first += y_rows

    if sets == 1:
        work(site_refs)
    else:
        for number in range(sets):
            pl.when(pick_ref[1] == number)(
                functools.partial(work, site_refs[number * per_set : (number + 1) * per_set])
            )


def second_product(pick, q_tiles, site_sets):
    tiles, sets = len(q_tiles), len(site_sets)
    mpo_count, phys, _, rows, cols = q_tiles[0][0].shape
    sites = [block for chosen in site_sets for block in chosen]
    y_rows = sum(block.shape[3] for block in site_sets[0])
    site_specs = [
        pl.BlockSpec(
            (2,) + block.shape[1:],
            (lambda v, pick: (0, 0, 0, 0, 0)) if block.shape[0] == 2 else (lambda v, pick: (pick[2], 0, 0, 0, 0)),
        )
        for block in sites
    ]
    q_spec = pl.BlockSpec((1, phys, 2, rows, cols), lambda v, pick: (v, 0, 0, 0, 0))
    return pl.pallas_call(
        functools.partial(second_kernel, tiles, sets),
        grid_spec=pltpu.PrefetchScalarGridSpec(
            num_scalar_prefetch=1,
            grid=(mpo_count,),
            in_specs=[q_spec] * (2 * tiles) + site_specs,
            out_specs=pl.BlockSpec((1, 2, tiles * rows, y_rows), lambda v, pick: (v, 0, 0, 0)),
        ),
        out_shape=jax.ShapeDtypeStruct((mpo_count, 2, tiles * rows, y_rows), BF16),
        compiler_params=params(1),
        cost_estimate=LIGHT,
        name="second_product",
    )(pick, *[q for pair in q_tiles for q in pair], *sites)


def finish_kernel(kinds, pick_ref, *refs):
    out_ref = refs[-1]
    pairs = [(refs[2 * i], refs[2 * i + 1]) for i in range(len(refs) // 2)]
    for number, (whole, first, count) in enumerate(kinds):

        @pl.when(pick_ref[0] == number)
        def _(whole=whole, first=first, count=count):
            at = 0
            for one, two in pairs[first : first + count]:
                total = one[0, 0].astype(F32) + two[0, 0].astype(F32)
                if whole == "rows":
                    out_ref[0, 0, at : at + total.shape[0]] = total
                    at += total.shape[0]
                else:
                    out_ref[0, 0, :, at : at + total.shape[1]] = total
                    at += total.shape[1]


def finish(pick, cases):
    kinds, addends = [], []
    for whole, pairs in cases:
        kinds.append((whole, len(addends) // 2, len(pairs)))
        addends += [value for pair in pairs for value in pair]
    mpo_count = addends[0].shape[0]
    rows = sum(pair[0].shape[2] for pair in cases[0][1])
    cols = cases[0][1][0][0].shape[3]
    return pl.pallas_call(
        functools.partial(finish_kernel, kinds),
        grid=(mpo_count, 2),
        in_specs=[pl.BlockSpec(memory_space=pltpu.SMEM)]
        + [pl.BlockSpec((1, 1) + value.shape[2:], lambda v, p: (v, p, 0, 0)) for value in addends],
        out_specs=pl.BlockSpec((1, 1, rows, cols), lambda v, p: (v, p, 0, 0)),
        out_shape=jax.ShapeDtypeStruct((mpo_count, 2, rows, cols), F32),
        compiler_params=params(2),
        name="finish",
    )(pick, *addends)


def after(value, *earlier):
    return lax.optimization_barrier((value,) + earlier)[0]


def swap(value):
    return lax.ppermute(value, "depth", [(0, 1), (1, 0)])


def split_inputs(environment, mpo):
    depth = lax.axis_index("depth")
    w_local, half = environment.shape[0], environment.shape[3]
    cols = half // 2
    env_own = lax.dynamic_slice_in_dim(environment, depth * cols, cols, 3)
    env_sib = swap(lax.dynamic_slice_in_dim(environment, (1 - depth) * cols, cols, 3))
    mpo_mine = jnp.concatenate(
        [
            lax.dynamic_slice_in_dim(mpo, depth * w_local, w_local, 0),
            lax.dynamic_slice_in_dim(mpo, (1 - depth) * w_local, w_local, 0),
        ],
        axis=0,
    )
    return env_own, env_sib, mpo_mine


def one_product(left, right, dims):
    return jnp.einsum(dims, left, right, preferred_element_type=F32)


def any_line(environment, site_tensor, mpo):
    depth = lax.axis_index("depth")
    env_own, env_sib, mpo_mine = split_inputs(environment, mpo)
    env_own = lax.all_gather(env_own, "row", axis=2, tiled=True)
    env_sib = lax.all_gather(env_sib, "row", axis=2, tiled=True)
    env = jnp.concatenate([env_own, env_sib], axis=0)
    cols = env.shape[3]
    planar = jnp.transpose(site_tensor, (0, 2, 1, 3))
    site_own = lax.dynamic_slice_in_dim(planar, depth * cols, cols, 3)
    site = lax.all_gather(planar, "col", axis=3, tiled=True)
    first = functools.partial(one_product, dims="sxa,wac->wsxc")
    g = jnp.stack(
        [
            first(site[:, 0], env[:, 0]) + first(site[:, 1], env[:, 1]),
            first(site[:, 0], env[:, 1]) - first(site[:, 1], env[:, 0]),
        ],
        axis=2,
    )
    q = jnp.einsum("wvst,wspxc->vtpxc", mpo_mine, g, precision=lax.Precision.HIGHEST).astype(BF16)
    site = lax.all_gather(site_own, "row", axis=2, tiled=True)
    second = functools.partial(one_product, dims="vtxc,tyc->vxy")
    total = jnp.stack(
        [
            second(q[:, :, 0], site[:, 0]) - second(q[:, :, 1], site[:, 1]),
            second(q[:, :, 0], site[:, 1]) + second(q[:, :, 1], site[:, 0]),
        ],
        axis=1,
    )
    return lax.psum_scatter(total, ("col", "depth"), scatter_dimension=3, tiled=True)


def four_rows(environment, site_tensor, mpo):
    row, col, depth = (lax.axis_index(axis) for axis in ("row", "col", "depth"))
    rows = site_tensor.shape[1]
    cols = site_tensor.shape[3] // 2
    axes = ("row", "col", "depth")
    place = lambda r, c, d: (r * 2 + c) * 2 + d
    to_host = lambda value: lax.ppermute(value, "row", [(0, 1), (3, 2)])
    to_end = lambda value: lax.ppermute(value, "row", [(1, 0), (2, 3)])
    across = lambda value: lax.ppermute(value, "row", [(1, 2), (2, 1)])

    def to_col(value, which_rows, far):
        pairs = []
        for r in which_rows:
            goal = r // 2 if not far else 1 - r // 2
            pairs += [(place(r, 1 - goal, d), place(r, goal, d)) for d in range(2)]
        return lax.ppermute(value, axes, pairs)

    env_own, env_sib, mpo_mine = split_inputs(environment, mpo)
    over_own, end_own = across(env_own), to_host(env_own)
    over_sib, end_sib = across(env_sib), to_host(env_sib)
    over_end_own = across(after(end_own, over_own))
    over_end_sib = across(after(end_sib, over_sib))
    envs = [env_own, env_sib, end_own, end_sib, over_own, over_sib, over_end_own, over_end_sib]

    quarter = lax.dynamic_slice_in_dim(after(site_tensor, env_sib), depth * cols, cols, 3)
    quarter = jnp.transpose(quarter, (0, 2, 1, 3))
    tiles = 2
    tile_rows = rows // tiles
    gather = lambda value: lax.all_gather(value, ("col", "depth"), axis=0)
    own = [quarter[:, :, m * tile_rows : (m + 1) * tile_rows] for m in range(tiles)]
    here = [gather(after(own[0], over_own, end_own)), gather(after(own[1], over_sib, end_sib))]
    came = [to_host(after(own[0], end_sib))]
    came.append(to_host(after(own[1], came[0])))
    there = [gather(after(came[0], over_end_own, *here)), gather(after(came[1], over_end_sib))]

    side = row // 2
    end = side * 4 + 1 - row
    blocks = jnp.stack([row, end, 3 - row, 3 - end]).astype(jnp.int32)
    pick = jnp.stack([depth, jnp.where(depth == row % 2, 0, 1), col]).astype(jnp.int32)

    def over(part, earlier):
        m, first = part // 2, (part % 2) * (tile_rows // 2)
        chunk = slice(first, first + tile_rows // 2)
        chosen = [
            lax.dynamic_slice_in_dim(whole[m][:, :, :, chunk], col * 2, 2, 0) for whole in (here, there)
        ]
        return across(after(jnp.where(pick[1] == 0, *chosen), earlier))

    def first(site, *earlier):
        return first_product(after(blocks, *earlier), mpo_mine, site, envs, 256)

    def second(q_tiles, sites, *earlier):
        return second_product(after(pick, *earlier), q_tiles, sites)

    near = [here, there]
    over_0 = over(0, over_end_sib)
    q_there_0 = first(there[0])
    pair_there_0 = (q_there_0, swap(q_there_0))
    q_here_0 = first(here[0], q_there_0)
    pair_here_0 = (q_here_0, swap(q_here_0))
    near_there_0 = second([pair_there_0], near, q_here_0, over_0)
    came_there_0 = to_end(near_there_0)
    over_1 = over(1, over_0)
    q_there_1 = first(there[1], near_there_0)
    pair_there_1 = (q_there_1, swap(q_there_1))
    near_there_1 = second([pair_there_1], near, q_there_1, over_1)
    came_there_1 = to_end(near_there_1)
    over_2 = over(2, over_1)
    pairs_there = [pair_there_0, pair_there_1]
    far_there_0 = second(pairs_there, [[over_0, over_1]], near_there_1, came_there_0)
    came_far_0 = to_end(far_there_0)
    turned_there_0 = to_col(came_there_0, (0, 3), False)
    q_here_1 = first(here[1], far_there_0)
    pairs_here = [pair_here_0, (q_here_1, swap(q_here_1))]
    far_there_1 = second(pairs_there, [[over_2]], q_here_1)
    came_far_1 = to_end(far_there_1)
    over_3 = over(3, over_2)
    near_here = second(pairs_here, near, far_there_1, came_there_1, turned_there_0)
    turned_near_here = to_col(near_here, (1, 2), False)
    turned_there_1 = to_col(came_there_1, (0, 3), False)
    far_here_0 = second(pairs_here, [[over_0, over_1]], near_here, over_3)
    turned_far_here_0 = to_col(far_here_0, (1, 2), True)
    far_there_2 = second(pairs_there, [[over_3]], far_here_0)
    came_far_2 = to_end(far_there_2)
    far_here_1 = second(pairs_here, [[over_2, over_3]], far_there_2, came_far_0, turned_there_1)
    turned_far_here_1 = to_col(far_here_1, (1, 2), True)
    near_there = [(came_there_0, turned_there_0), (came_there_1, turned_there_1)]
    near_here = [(near_here, turned_near_here)]
    far_here = [(far_here_0, turned_far_here_0), (far_here_1, turned_far_here_1)]
    far_there = [(came, to_col(came, (0, 3), True)) for came in (came_far_0, came_far_1, came_far_2)]

    is_end = (row == 0) | (row == 3)
    case = jnp.where(is_end, 2, 0) + jnp.where(col == side, 0, 1)
    return finish(
        case.astype(jnp.int32).reshape(1),
        [("cols", near_here), ("cols", far_here), ("rows", near_there), ("cols", far_there)],
    )


def solution(mesh):
    placed = (
        P(("groups", "depth"), None, "row", "col"),
        P("groups", "row", None, "col"),
        P("groups", None, None, None),
    )
    line = mesh.shape["row"] == 4 and mesh.shape["col"] == 2 and mesh.shape["depth"] == 2
    return jax.shard_map(
        four_rows if line else any_line,
        mesh=mesh,
        in_specs=placed,
        out_specs=P("groups", None, "row", ("col", "depth")),
        check_vma=False,
    )
```

time: 742 us -> 452 us (0.61)
  the two profiles are of different devices: /device:TPU:1 before, /device:TPU:10 now
where the time goes in v3:
time: 452 us; the launch traced here: 445 us
  waiting for transfers between devices  184 us (41%)
  Pallas kernels  163 us (36%)
  starting transfers between devices  58.1 us (13%)
  local copies, waits for them, and re-layouts  22.6 us (5%)
  between operations  13.9 us (3%)
    ppermute x8, waiting for transfers between devices, four_rows(): across = lambda value: lax.ppermute(value, 'row', [(1, 2), (2, 1)])  96.3 us
    pallas_call x8, Pallas kernels, second_product(): pl.pallas_call(functools.partial(second_kernel, tiles, sets), grid_spec=p...  95.6 us
    pallas_call x4, Pallas kernels, first_product(): pl.pallas_call(functools.partial(first_kernel, w_local), grid=(cols // co...  59.7 us
    ppermute x4, waiting for transfers between devices, four_rows(): to_host = lambda value: lax.ppermute(value, 'row', [(0, 1), (3, 2)])  47.3 us
    ppermute x8, starting transfers between devices, four_rows(): across = lambda value: lax.ppermute(value, 'row', [(1, 2), (2, 1)])  27.9 us
    ppermute x8, waiting for transfers between devices, to_col(): return lax.ppermute(value, axes, pairs)  24.8 us
    all_gather x4, waiting for transfers between devices, four_rows(): gather = lambda value: lax.all_gather(value, ('col', 'depth'), axis=0)  15.5 us
    ppermute x8, starting transfers between devices, to_col(): return lax.ppermute(value, axes, pairs)  12.5 us
  transfers between devices with their start and end apart: 34, of which 14 were waited for; matrix products, arithmetic and copies ran while one was open for 3% of the time, Pallas kernels for 29%

profile of v3, /device:TPU:10, one launch (start us, length us, event | category | flops | bytes accessed | tf_op | source)
XLA Modules:
  0.0 445.1 jit_solution(15315527030088138211)
XLA Ops:
  6.5 1.9 constant_dynamic-slice_fusion
  8.5 1.3 collective-permute-start.3
  9.8 3.5 collective-permute-start.4
  13.3 1.3 copy.8
  14.9 1.6 fusion.4
  16.5 19.5 %collective-permute-done.3.refs_2_ = bf16[1,2,512,512]{3,2,1,0:T(8,128)(2,1)S(1)} collective-permute-done((bf16[1,2,512,512]{3,2,1,0:T(8,128)(2,1)S(1)}, bf16[1,2,512,512]{3,2,1,0:T(8,128)(2,1)S(1)}, u32[]{:S(2)}, u32[]{:S(2)}) %collective-permute-start.3) | collective-permute-done | bytes 1048608 | tf_op jit(solution)/shard_map/ppermute | solution.py:248
  36.0 1.3 collective-permute-done.4.refs_4_
  37.3 1.0 copy-done.9
  38.3 1.3 collective-permute-start.1
  39.6 3.5 collective-permute-start.6
  43.1 21.9 %collective-permute-done.1.refs_3_ = bf16[1,2,512,512]{3,2,1,0:T(8,128)(2,1)S(1)} collective-permute-done((bf16[1,2,512,512]{3,2,1,0:T(8,128)(2,1)S(1)}, bf16[1,2,512,512]{3,2,1,0:T(8,128)(2,1)S(1)}, u32[]{:S(2)}, u32[]{:S(2)}) %collective-permute-start.1) | collective-permute-done | bytes 1048608 | tf_op jit(solution)/shard_map/ppermute | solution.py:248
  65.0 1.3 collective-permute-done.6.refs_5_
  66.3 1.0 copy-done.11
  67.3 3.5 collective-permute-start.5
  70.8 1.3 collective-permute-start.2
  72.1 21.1 %collective-permute-done.5.refs_6_ = bf16[1,2,512,512]{3,2,1,0:T(8,128)(2,1)S(1)} collective-permute-done((bf16[1,2,512,512]{3,2,1,0:T(8,128)(2,1)S(1)}, bf16[1,2,512,512]{3,2,1,0:T(8,128)(2,1)S(1)}, u32[]{:S(2)}, u32[]{:S(2)}) %collective-permute-start.5) | collective-permute-done | bytes 1048608 | tf_op jit(solution)/shard_map/ppermute | solution.py:250
  93.2 3.5 collective-permute-done.2
  96.7 11.4 %all-gather.11.cloned.1.call-done = bf16[8,2,256,512]{3,2,1,0:T(8,128)(2,1)} async-done(((bf16[2,2,256,512]{3,2,1,0:T(8,128)(2,1)}), bf16[8,2,256,512]{3,2,1,0:T(8,128)(2,1)}) %all-gather.11.cloned.1.call-update) | async-done | bytes 4194320 | tf_op jit(solution)/shard_map/all_gather | solution.py:270
  108.2 3.4 collective-permute-start.7
  111.6 1.3 collective-permute-start.10
  112.9 22.5 %collective-permute-done.7.refs_7_ = bf16[1,2,512,512]{3,2,1,0:T(8,128)(2,1)S(1)} collective-permute-done((bf16[1,2,512,512]{3,2,1,0:T(8,128)(2,1)S(1)}, bf16[1,2,512,512]{3,2,1,0:T(8,128)(2,1)S(1)}, u32[]{:S(2)}, u32[]{:S(2)}) %collective-permute-start.7) | collective-permute-done | bytes 1048608 | tf_op jit(solution)/shard_map/ppermute | solution.py:250
  135.4 1.0 copy-done.13
  136.4 2.4 collective-permute-done.10
  140.2 4.1 all-gather.13.cloned.1.call-done
  144.3 14.8 %first_product.4.refs_0_ = bf16[2,2,2,256,512]{4,3,2,1,0:T(8,128)(2,1)} custom-call(s32[4]{0:T(128)} %pad_add_fusion.1.block_ref, f32[2,2,2,2]{3,2,1,0:T(2,128)} %pad_maximum_fusion.mpo_ref, bf16[4,2,2,256,512]{4,3,2,1,0:T(8,128)(2,1)} %bitcast.24, bf16[1,2,512,512]{3,2,1,0:T(8,128)(2,1)} %copy-done.5, bf16[1,2,512,512]{3,2,1,0:T(8,128)(2,1)} %copy-done.7, ...), custom_call_target="tpu_custom_call" | custom-call | tf_op jit(solution)/shard_map/first_product/pallas_call | solution.py:66
  159.3 4.1 fusion.2
  163.4 1.7 fusion.3
  165.2 3.6 collective-permute-start.8
  169.5 14.8 %first_product.5.refs_0_ = bf16[2,2,2,256,512]{4,3,2,1,0:T(8,128)(2,1)} custom-call(s32[4]{0:T(128)} %pad_add_fusion.1.block_ref, f32[2,2,2,2]{3,2,1,0:T(2,128)} %pad_maximum_fusion.mpo_ref, bf16[4,2,2,256,512]{4,3,2,1,0:T(8,128)(2,1)} %bitcast.15, bf16[1,2,512,512]{3,2,1,0:T(8,128)(2,1)} %copy-done.5, bf16[1,2,512,512]{3,2,1,0:T(8,128)(2,1)} %copy-done.7, ...), custom_call_target="tpu_custom_call" | custom-call | tf_op jit(solution)/shard_map/first_product/pallas_call | solution.py:66
  184.3 8.1 %collective-permute-done.8.refs_4_ = bf16[2,2,2,128,512]{4,3,2,1,0:T(8,128)(2,1)S(1)} collective-permute-done((bf16[2,2,2,128,512]{4,3,2,1,0:T(8,128)(2,1)S(1)}, bf16[2,2,2,128,512]{4,3,2,1,0:T(8,128)(2,1)S(1)}, u32[]{:S(2)}, u32[]{:S(2)}) %collective-permute-start.8) | collective-permute-done | bytes 1048608 | tf_op jit(solution)/shard_map/ppermute | solution.py:250
  192.4 1.4 copy-done.3
  193.8 10.3 %second_product.8 = bf16[2,2,256,512]{3,2,1,0:T(8,128)(2,1)} custom-call(s32[3]{0:T(128)} %pad_add_fusion.pick_ref, bf16[2,2,2,256,512]{4,3,2,1,0:T(8,128)(2,1)} %first_product.4.refs_0_, bf16[2,2,2,256,512]{4,3,2,1,0:T(8,128)(2,1)} %copy-done.3, bf16[4,2,2,256,512]{4,3,2,1,0:T(8,128)(2,1)} %bitcast.16, bf16[4,2,2,256,512]{4,3,2,1,0:T(8,128)(2,1)} %bitcast.19, ...), custom_call_target="tpu_custom_call" | custom-call | tf_op jit(solution)/shard_map/second_product/pallas_call | solution.py:130
  204.2 15.0 %first_product.6.refs_0_.refs_2_ = bf16[2,2,2,256,512]{4,3,2,1,0:T(8,128)(2,1)} custom-call(s32[4]{0:T(128)} %pad_add_fusion.1.block_ref, f32[2,2,2,2]{3,2,1,0:T(2,128)} %pad_maximum_fusion.mpo_ref, bf16[4,2,2,256,512]{4,3,2,1,0:T(8,128)(2,1)} %bitcast.30, bf16[1,2,512,512]{3,2,1,0:T(8,128)(2,1)} %copy-done.5, bf16[1,2,512,512]{3,2,1,0:T(8,128)(2,1)} %copy-done.7, ...), custom_call_target="tpu_custom_call" | custom-call | tf_op jit(solution)/shard_map/first_product/pallas_call | solution.py:66
  219.3 3.4 collective-permute-start.11
  222.7 1.8 collective-permute-start.13
  224.7 22.0 %collective-permute-done.11.refs_5_ = bf16[2,2,2,128,512]{4,3,2,1,0:T(8,128)(2,1)S(1)} collective-permute-done((bf16[2,2,2,128,512]{4,3,2,1,0:T(8,128)(2,1)S(1)}, bf16[2,2,2,128,512]{4,3,2,1,0:T(8,128)(2,1)S(1)}, u32[]{:S(2)}, u32[]{:S(2)}) %collective-permute-start.11) | collective-permute-done | bytes 1048608 | tf_op jit(solution)/shard_map/ppermute | solution.py:250
  246.8 1.3 copy-done.4
  248.1 10.3 %second_product.9 = bf16[2,2,256,512]{3,2,1,0:T(8,128)(2,1)} custom-call(s32[3]{0:T(128)} %pad_add_fusion.pick_ref, bf16[2,2,2,256,512]{4,3,2,1,0:T(8,128)(2,1)} %first_product.6.refs_0_.refs_2_, bf16[2,2,2,256,512]{4,3,2,1,0:T(8,128)(2,1)} %copy-done.4, bf16[4,2,2,256,512]{4,3,2,1,0:T(8,128)(2,1)} %bitcast.17, bf16[4,2,2,256,512]{4,3,2,1,0:T(8,128)(2,1)} %bitcast.20, ...), custom_call_target="tpu_custom_call" | custom-call | tf_op jit(solution)/shard_map/second_product/pallas_call | solution.py:130
  258.5 1.0 copy-done.22
  259.4 13.6 %second_product.10 = bf16[2,2,512,256]{3,2,1,0:T(8,128)(2,1)} custom-call(s32[3]{0:T(128)} %pad_add_fusion.pick_ref, bf16[2,2,2,256,512]{4,3,2,1,0:T(8,128)(2,1)} %first_product.4.refs_0_, bf16[2,2,2,256,512]{4,3,2,1,0:T(8,128)(2,1)} %copy-done.3, bf16[2,2,2,256,512]{4,3,2,1,0:T(8,128)(2,1)} %first_product.6.refs_0_.refs_2_, ...), custom_call_target="tpu_custom_call" | custom-call | tf_op jit(solution)/shard_map/second_product/pallas_call | solution.py:130
  273.0 15.1 %first_product.7.refs_2_ = bf16[2,2,2,256,512]{4,3,2,1,0:T(8,128)(2,1)} custom-call(s32[4]{0:T(128)} %pad_add_fusion.1.block_ref, f32[2,2,2,2]{3,2,1,0:T(2,128)} %pad_maximum_fusion.mpo_ref, bf16[4,2,2,256,512]{4,3,2,1,0:T(8,128)(2,1)} %bitcast.21, bf16[1,2,512,512]{3,2,1,0:T(8,128)(2,1)} %copy-done.5, bf16[1,2,512,512]{3,2,1,0:T(8,128)(2,1)} %copy-done.7, ...), custom_call_target="tpu_custom_call" | custom-call | tf_op jit(solution)/shard_map/first_product/pallas_call | solution.py:66
  288.4 1.9 copy-done.2
  290.9 3.5 collective-permute-start.14
  294.4 1.6 collective-permute-start.16
  296.1 1.3 collective-permute-start.15
  297.4 1.1 dynamic-slice_select_fusion
  298.5 20.0 %collective-permute-done.14.refs_4_ = bf16[2,2,2,128,512]{4,3,2,1,0:T(8,128)(2,1)S(1)} collective-permute-done((bf16[2,2,2,128,512]{4,3,2,1,0:T(8,128)(2,1)S(1)}, bf16[2,2,2,128,512]{4,3,2,1,0:T(8,128)(2,1)S(1)}, u32[]{:S(2)}, u32[]{:S(2)}) %collective-permute-start.14) | collective-permute-done | bytes 1048608 | tf_op jit(solution)/shard_map/ppermute | solution.py:250
  318.5 2.3 collective-permute-start.22
  320.8 3.6 collective-permute-start.20
  324.3 9.2 %second_product.11 = bf16[2,2,512,128]{3,2,1,0:T(8,128)(2,1)} custom-call(s32[3]{0:T(128)} %pad_add_fusion.pick_ref, bf16[2,2,2,256,512]{4,3,2,1,0:T(8,128)(2,1)} %first_product.4.refs_0_, bf16[2,2,2,256,512]{4,3,2,1,0:T(8,128)(2,1)} %copy-done.3, bf16[2,2,2,256,512]{4,3,2,1,0:T(8,128)(2,1)} %first_product.6.refs_0_.refs_2_, ...), custom_call_target="tpu_custom_call" | custom-call | tf_op jit(solution)/shard_map/second_product/pallas_call | solution.py:130
  334.3 1.3 collective-permute-start.26
  335.6 15.8 %second_product.12.refs_0_ = bf16[2,2,512,512]{3,2,1,0:T(8,128)(2,1)} custom-call(s32[3]{0:T(128)} %pad_add_fusion.pick_ref, bf16[2,2,2,256,512]{4,3,2,1,0:T(8,128)(2,1)} %first_product.5.refs_0_, bf16[2,2,2,256,512]{4,3,2,1,0:T(8,128)(2,1)} %copy-done.6, bf16[2,2,2,256,512]{4,3,2,1,0:T(8,128)(2,1)} %first_product.7.refs_2_, ...), custom_call_target="tpu_custom_call" | custom-call | tf_op jit(solution)/shard_map/second_product/pallas_call | solution.py:130
  351.4 3.5 collective-permute-start.19
  355.7 1.7 collective-permute-start.25
  357.4 13.6 %second_product.13.refs_2_ = bf16[2,2,512,256]{3,2,1,0:T(8,128)(2,1)} custom-call(s32[3]{0:T(128)} %pad_add_fusion.pick_ref, bf16[2,2,2,256,512]{4,3,2,1,0:T(8,128)(2,1)} %first_product.5.refs_0_, bf16[2,2,2,256,512]{4,3,2,1,0:T(8,128)(2,1)} %copy-done.6, bf16[2,2,2,256,512]{4,3,2,1,0:T(8,128)(2,1)} %first_product.7.refs_2_, ...), custom_call_target="tpu_custom_call" | custom-call | tf_op jit(solution)/shard_map/second_product/pallas_call | solution.py:130
  371.0 1.5 collective-permute-start.21
  372.5 9.2 %second_product.14 = bf16[2,2,512,128]{3,2,1,0:T(8,128)(2,1)} custom-call(s32[3]{0:T(128)} %pad_add_fusion.pick_ref, bf16[2,2,2,256,512]{4,3,2,1,0:T(8,128)(2,1)} %first_product.4.refs_0_, bf16[2,2,2,256,512]{4,3,2,1,0:T(8,128)(2,1)} %copy-done.3, bf16[2,2,2,256,512]{4,3,2,1,0:T(8,128)(2,1)} %first_product.6.refs_0_.refs_2_, ...), custom_call_target="tpu_custom_call" | custom-call | tf_op jit(solution)/shard_map/second_product/pallas_call | solution.py:130
  381.6 5.2 %collective-permute-start.28 = (bf16[2,2,512,128]{3,2,1,0:T(8,128)(2,1)}, bf16[2,2,512,128]{3,2,1,0:T(8,128)(2,1)}, u32[]{:S(2)}, u32[]{:S(2)}) collective-permute-start(bf16[2,2,512,128]{3,2,1,0:T(8,128)(2,1)} %second_product.14), channel_id=1, source_target_pairs={{4,0},{8,12},{5,1},{9,13},{6,2},{10,14},{7,3},{11,15},{20,16},{24,... | collective-permute-start | bytes 1572872 | tf_op jit(solution)/shard_map/ppermute | solution.py:249
  386.8 13.6 %second_product.15.refs_4_ = bf16[2,2,512,256]{3,2,1,0:T(8,128)(2,1)} custom-call(s32[3]{0:T(128)} %pad_add_fusion.pick_ref, bf16[2,2,2,256,512]{4,3,2,1,0:T(8,128)(2,1)} %first_product.5.refs_0_, bf16[2,2,2,256,512]{4,3,2,1,0:T(8,128)(2,1)} %copy-done.6, bf16[2,2,2,256,512]{4,3,2,1,0:T(8,128)(2,1)} %first_product.7.refs_2_, ...), custom_call_target="tpu_custom_call" | custom-call | tf_op jit(solution)/shard_map/second_product/pallas_call | solution.py:130
  401.2 1.3 collective-permute-start.24
  402.5 1.5 collective-permute-start.29
  404.0 24.8 %collective-permute-done.24.refs_5_ = bf16[2,2,512,256]{3,2,1,0:T(8,128)(2,1)S(1)} collective-permute-done((bf16[2,2,512,256]{3,2,1,0:T(8,128)(2,1)}, bf16[2,2,512,256]{3,2,1,0:T(8,128)(2,1)S(1)}, u32[]{:S(2)}, u32[]{:S(2)}) %collective-permute-start.24) | collective-permute-done | bytes 1048608 | tf_op jit(solution)/shard_map/ppermute | solution.py:257
  428.8 1.0 copy-done.27
  430.5 7.8 %finish.1 = f32[2,2,512,512]{3,2,1,0:T(8,128)} custom-call(s32[1]{0:T(128)} %bitcast.pick_ref, bf16[2,2,512,512]{3,2,1,0:T(8,128)(2,1)} %second_product.12.refs_0_, bf16[2,2,512,512]{3,2,1,0:T(8,128)(2,1)} %copy-done.21, bf16[2,2,512,256]{3,2,1,0:T(8,128)(2,1)} %second_product.13.refs_2_, bf16[2,2,512,256]{3,2,1,0:T(8,128)(2,1)} %collective-permute-done.21.refs_3_, ...), custom_call_target="tpu_custom_call" | custom-call | tf_op jit(solution)/shard_map/finish/pallas_call | solution.py:171
  (99 shorter events, 7.0 us)
Async XLA Ops:
  6.5 90.2 %all-gather.9.cloned.1.call-start = ((), (), s32[]{:S(2)}) async-start(), calls=%async_computation | async-start | bytes 5242880 | tf_op jit(solution)/shard_map/all_gather | solution.py:270
  6.5 6.8 %copy-start.20 = (bf16[2,512,2,1024]{3,2,1,0:T(2,128)(2,1)S(1)}, bf16[2,512,2,1024]{3,2,1,0:T(2,128)(2,1)}, u32[]{:S(2)}) copy-start(bf16[2,512,2,1024]{3,2,1,0:T(2,128)(2,1)} %param.4) | copy-start | bytes 12582916
  8.4 6.2 %copy-start.5 = (bf16[1,2,512,512]{3,2,1,0:T(8,128)(2,1)}, bf16[1,2,512,512]{3,2,1,0:T(8,128)(2,1)S(1)}, u32[]{:S(2)}) copy-start(bf16[1,2,512,512]{3,2,1,0:T(8,128)(2,1)S(1)} %get-tuple-element.63.refs_0_) | copy-start | bytes 3145732
  8.4 4.9 %collective-permute-start = (bf16[1,2,512,512]{3,2,1,0:T(8,128)(2,1)S(1)}, bf16[1,2,512,512]{3,2,1,0:T(8,128)(2,1)S(1)}, u32[]{:S(2)}, u32[]{:S(2)}) collective-permute-start(bf16[1,2,512,512]{3,2,1,0:T(8,128)(2,1)S(1)} %get-tuple-element.64), channel_id=1, source_target_pairs={{0,1},{1,0},{2,3},{3,2},{4,5},{5,4},{6,7},{7,6},{8,9},{9,8},{10,11... | collective-permute-start | bytes 3145736 | tf_op jit(solution)/shard_map/ppermute | solution.py:188
  8.5 27.4 %collective-permute-start.3 = (bf16[1,2,512,512]{3,2,1,0:T(8,128)(2,1)S(1)}, bf16[1,2,512,512]{3,2,1,0:T(8,128)(2,1)S(1)}, u32[]{:S(2)}, u32[]{:S(2)}) collective-permute-start(bf16[1,2,512,512]{3,2,1,0:T(8,128)(2,1)S(1)} %get-tuple-element.63.refs_0_), channel_id=1, source_target_pairs={{0,4},{12,8},{1,5},{13,9},{2,6},{14,10},{3,7},{15,11},{16,20},{28,... | collective-permute-start | bytes 3145736 | tf_op jit(solution)/shard_map/ppermute | solution.py:248
  9.8 27.4 %collective-permute-start.4 = (bf16[1,2,512,512]{3,2,1,0:T(8,128)(2,1)S(1)}, bf16[1,2,512,512]{3,2,1,0:T(8,128)(2,1)S(1)}, u32[]{:S(2)}, u32[]{:S(2)}) collective-permute-start(bf16[1,2,512,512]{3,2,1,0:T(8,128)(2,1)S(1)} %get-tuple-element.63.refs_0_), channel_id=1, source_target_pairs={{4,8},{8,4},{5,9},{9,5},{6,10},{10,6},{7,11},{11,7},{20,24},{24,20... | collective-permute-start | bytes 3145736 | tf_op jit(solution)/shard_map/ppermute | solution.py:250
  13.3 26.3 %copy-start.7 = (bf16[1,2,512,512]{3,2,1,0:T(8,128)(2,1)}, bf16[1,2,512,512]{3,2,1,0:T(8,128)(2,1)S(1)}, u32[]{:S(2)}) copy-start(bf16[1,2,512,512]{3,2,1,0:T(8,128)(2,1)S(1)} %collective-permute-done.refs_1_) | copy-start | bytes 3145732
  36.0 103.0 %copy-start.8 = (bf16[1,2,512,512]{3,2,1,0:T(8,128)(2,1)}, bf16[1,2,512,512]{3,2,1,0:T(8,128)(2,1)S(1)}, u32[]{:S(2)}) copy-start(bf16[1,2,512,512]{3,2,1,0:T(8,128)(2,1)S(1)} %collective-permute-done.3.refs_2_) | copy-start | bytes 3145732
  37.3 1.0 copy-start.9
  38.2 101.4 %copy-start.30 = (f32[2,2,2,2]{3,2,1,0:T(2,128)S(1)}, f32[2,2,2,2]{3,2,1,0:T(2,128)}, u32[]{:S(2)}) copy-start(f32[2,2,2,2]{3,2,1,0:T(2,128)} %param.5) | copy-start | bytes 196
  38.2 69.9 %all-gather.11.cloned.1.call-start = ((), (), s32[]{:S(2)}) async-start(), calls=%async_computation.1 | async-start | bytes 5242880 | tf_op jit(solution)/shard_map/all_gather | solution.py:270
  38.3 26.7 %collective-permute-start.1 = (bf16[1,2,512,512]{3,2,1,0:T(8,128)(2,1)S(1)}, bf16[1,2,512,512]{3,2,1,0:T(8,128)(2,1)S(1)}, u32[]{:S(2)}, u32[]{:S(2)}) collective-permute-start(bf16[1,2,512,512]{3,2,1,0:T(8,128)(2,1)S(1)} %collective-permute-done.refs_1_), channel_id=1, source_target_pairs={{0,4},{12,8},{1,5},{13,9},{2,6},{14,10},{3,7},{15,11},{16,20},{28,... | collective-permute-start | bytes 3145736 | tf_op jit(solution)/shard_map/ppermute | solution.py:248
  39.6 26.7 %collective-permute-start.6 = (bf16[1,2,512,512]{3,2,1,0:T(8,128)(2,1)S(1)}, bf16[1,2,512,512]{3,2,1,0:T(8,128)(2,1)S(1)}, u32[]{:S(2)}, u32[]{:S(2)}) collective-permute-start(bf16[1,2,512,512]{3,2,1,0:T(8,128)(2,1)S(1)} %collective-permute-done.refs_1_), channel_id=1, source_target_pairs={{4,8},{8,4},{5,9},{9,5},{6,10},{10,6},{7,11},{11,7},{20,24},{24,20... | collective-permute-start | bytes 3145736 | tf_op jit(solution)/shard_map/ppermute | solution.py:250
  65.0 79.3 %copy-start.10 = (bf16[1,2,512,512]{3,2,1,0:T(8,128)(2,1)}, bf16[1,2,512,512]{3,2,1,0:T(8,128)(2,1)S(1)}, u32[]{:S(2)}) copy-start(bf16[1,2,512,512]{3,2,1,0:T(8,128)(2,1)S(1)} %collective-permute-done.1.refs_3_) | copy-start | bytes 3145732
  66.3 1.0 copy-start.11
  67.3 77.0 %all-gather.13.cloned.1.call-start = ((), (), s32[]{:S(2)}) async-start(), calls=%async_computation.2 | async-start | bytes 5242880 | tf_op jit(solution)/shard_map/all_gather | solution.py:270
  67.3 25.9 %collective-permute-start.5 = (bf16[1,2,512,512]{3,2,1,0:T(8,128)(2,1)S(1)}, bf16[1,2,512,512]{3,2,1,0:T(8,128)(2,1)S(1)}, u32[]{:S(2)}, u32[]{:S(2)}) collective-permute-start(bf16[1,2,512,512]{3,2,1,0:T(8,128)(2,1)S(1)} %collective-permute-done.3.refs_2_), channel_id=1, source_target_pairs={{4,8},{8,4},{5,9},{9,5},{6,10},{10,6},{7,11},{11,7},{20,24},{24,20... | collective-permute-start | bytes 3145736 | tf_op jit(solution)/shard_map/ppermute | solution.py:250
  70.8 25.9 %collective-permute-start.2 = (bf16[2,2,256,512]{3,2,1,0:T(8,128)(2,1)}, bf16[2,2,256,512]{3,2,1,0:T(8,128)(2,1)}, u32[]{:S(2)}, u32[]{:S(2)}) collective-permute-start(bf16[2,2,256,512]{3,2,1,0:T(8,128)(2,1)} %get-tuple-element.30), channel_id=1, source_target_pairs={{0,4},{12,8},{1,5},{13,9},{2,6},{14,10},{3,7},{15,11},{16,20},{28,... | collective-permute-start | bytes 3145736 | tf_op jit(solution)/shard_map/ppermute | solution.py:248
  93.2 51.1 %copy-start.12 = (bf16[1,2,512,512]{3,2,1,0:T(8,128)(2,1)}, bf16[1,2,512,512]{3,2,1,0:T(8,128)(2,1)S(1)}, u32[]{:S(2)}) copy-start(bf16[1,2,512,512]{3,2,1,0:T(8,128)(2,1)S(1)} %collective-permute-done.5.refs_6_) | copy-start | bytes 3145732
  108.2 84.2 %all-gather.15.cloned.1.call-start = ((), (), s32[]{:S(2)}) async-start(), calls=%async_computation.3 | async-start | bytes 5242880 | tf_op jit(solution)/shard_map/all_gather | solution.py:270
  108.2 27.2 %collective-permute-start.7 = (bf16[1,2,512,512]{3,2,1,0:T(8,128)(2,1)S(1)}, bf16[1,2,512,512]{3,2,1,0:T(8,128)(2,1)S(1)}, u32[]{:S(2)}, u32[]{:S(2)}) collective-permute-start(bf16[1,2,512,512]{3,2,1,0:T(8,128)(2,1)S(1)} %collective-permute-done.1.refs_3_), channel_id=1, source_target_pairs={{4,8},{8,4},{5,9},{9,5},{6,10},{10,6},{7,11},{11,7},{20,24},{24,20... | collective-permute-start | bytes 3145736 | tf_op jit(solution)/shard_map/ppermute | solution.py:250
  111.6 27.2 %collective-permute-start.10 = (bf16[2,2,256,512]{3,2,1,0:T(8,128)(2,1)}, bf16[2,2,256,512]{3,2,1,0:T(8,128)(2,1)}, u32[]{:S(2)}, u32[]{:S(2)}) collective-permute-start(bf16[2,2,256,512]{3,2,1,0:T(8,128)(2,1)} %get-tuple-element.39), channel_id=1, source_target_pairs={{0,4},{12,8},{1,5},{13,9},{2,6},{14,10},{3,7},{15,11},{16,20},{28,... | collective-permute-start | bytes 3145736 | tf_op jit(solution)/shard_map/ppermute | solution.py:248
  135.4 1.0 copy-start.13
  159.1 33.3 %collective-permute-start.9 = (bf16[2,2,2,256,512]{4,3,2,1,0:T(8,128)(2,1)}, bf16[2,2,2,256,512]{4,3,2,1,0:T(8,128)(2,1)S(1)}, u32[]{:S(2)}, u32[]{:S(2)}) collective-permute-start(bf16[2,2,2,256,512]{4,3,2,1,0:T(8,128)(2,1)} %first_product.4.refs_0_), channel_id=1, source_target_pairs={{0,1},{1,0},{2,3},{3,2},{4,5},{5,4},{6,7},{7,6},{8,9},{9,8},{10,11... | collective-permute-start | bytes 6291464 | tf_op jit(solution)/shard_map/ppermute | solution.py:188
  159.3 4.1 copy-start.1
  165.2 27.2 %collective-permute-start.8 = (bf16[2,2,2,128,512]{4,3,2,1,0:T(8,128)(2,1)S(1)}, bf16[2,2,2,128,512]{4,3,2,1,0:T(8,128)(2,1)S(1)}, u32[]{:S(2)}, u32[]{:S(2)}) collective-permute-start(bf16[2,2,2,128,512]{4,3,2,1,0:T(8,128)(2,1)S(1)} %dynamic-slice_select_fusion.3), channel_id=1, source_target_pairs={{4,8},{8,4},{5,9},{9,5},{6,10},{10,6},{7,11},{11,7},{20,24},{24,20... | collective-permute-start | bytes 3145736 | tf_op jit(solution)/shard_map/ppermute | solution.py:250
  192.4 11.7 %copy-start.16 = (bf16[2,2,2,128,512]{4,3,2,1,0:T(8,128)(2,1)}, bf16[2,2,2,128,512]{4,3,2,1,0:T(8,128)(2,1)S(1)}, u32[]{:S(2)}) copy-start(bf16[2,2,2,128,512]{4,3,2,1,0:T(8,128)(2,1)S(1)} %collective-permute-done.8.refs_4_) | copy-start | bytes 3145732
  192.4 1.4 copy-start.3
  204.2 15.0 %copy-start.14 = (bf16[4,2,2,128,512]{4,3,2,1,0:T(8,128)(2,1)S(1)}, bf16[4,2,2,128,512]{4,3,2,1,0:T(8,128)(2,1)}, u32[]{:S(2)}) copy-start(bf16[4,2,2,128,512]{4,3,2,1,0:T(8,128)(2,1)} %get-tuple-element.57) | copy-start | bytes 6291460
  204.2 15.0 %copy-start.15 = (bf16[4,2,2,128,512]{4,3,2,1,0:T(8,128)(2,1)S(1)}, bf16[4,2,2,128,512]{4,3,2,1,0:T(8,128)(2,1)}, u32[]{:S(2)}) copy-start(bf16[4,2,2,128,512]{4,3,2,1,0:T(8,128)(2,1)} %get-tuple-element.59) | copy-start | bytes 6291460
  219.2 27.6 %collective-permute-start.12 = (bf16[2,2,2,256,512]{4,3,2,1,0:T(8,128)(2,1)}, bf16[2,2,2,256,512]{4,3,2,1,0:T(8,128)(2,1)S(1)}, u32[]{:S(2)}, u32[]{:S(2)}) collective-permute-start(bf16[2,2,2,256,512]{4,3,2,1,0:T(8,128)(2,1)} %first_product.6.refs_0_.refs_2_), channel_id=1, source_target_pairs={{0,1},{1,0},{2,3},{3,2},{4,5},{5,4},{6,7},{7,6},{8,9},{9,8},{10,11... | collective-permute-start | bytes 6291464 | tf_op jit(solution)/shard_map/ppermute | solution.py:188
  219.3 27.4 %collective-permute-start.11 = (bf16[2,2,2,128,512]{4,3,2,1,0:T(8,128)(2,1)S(1)}, bf16[2,2,2,128,512]{4,3,2,1,0:T(8,128)(2,1)S(1)}, u32[]{:S(2)}, u32[]{:S(2)}) collective-permute-start(bf16[2,2,2,128,512]{4,3,2,1,0:T(8,128)(2,1)S(1)} %dynamic-slice_select_fusion.2), channel_id=1, source_target_pairs={{4,8},{8,4},{5,9},{9,5},{6,10},{10,6},{7,11},{11,7},{20,24},{24,20... | collective-permute-start | bytes 3145736 | tf_op jit(solution)/shard_map/ppermute | solution.py:250
  222.7 35.7 %collective-permute-start.13 = (bf16[2,2,256,512]{3,2,1,0:T(8,128)(2,1)}, bf16[2,2,256,512]{3,2,1,0:T(8,128)(2,1)S(1)}, u32[]{:S(2)}, u32[]{:S(2)}) collective-permute-start(bf16[2,2,256,512]{3,2,1,0:T(8,128)(2,1)} %second_product.8), channel_id=1, source_target_pairs={{4,0},{8,12},{5,1},{9,13},{6,2},{10,14},{7,3},{11,15},{20,16},{24,... | collective-permute-start | bytes 3145736 | tf_op jit(solution)/shard_map/ppermute | solution.py:249
  224.5 109.8 %collective-permute-start.17 = (bf16[2,2,2,256,512]{4,3,2,1,0:T(8,128)(2,1)}, bf16[2,2,2,256,512]{4,3,2,1,0:T(8,128)(2,1)S(1)}, u32[]{:S(2)}, u32[]{:S(2)}) collective-permute-start(bf16[2,2,2,256,512]{4,3,2,1,0:T(8,128)(2,1)} %first_product.5.refs_0_), channel_id=1, source_target_pairs={{0,1},{1,0},{2,3},{3,2},{4,5},{5,4},{6,7},{7,6},{8,9},{9,8},{10,11... | collective-permute-start | bytes 6291464 | tf_op jit(solution)/shard_map/ppermute | solution.py:188
  246.7 11.7 %copy-start.17 = (bf16[2,2,2,128,512]{4,3,2,1,0:T(8,128)(2,1)}, bf16[2,2,2,128,512]{4,3,2,1,0:T(8,128)(2,1)S(1)}, u32[]{:S(2)}) copy-start(bf16[2,2,2,128,512]{4,3,2,1,0:T(8,128)(2,1)S(1)} %collective-permute-done.11.refs_5_) | copy-start | bytes 3145732
  246.8 1.3 copy-start.4
  258.4 1.0 copy-start.22
  273.0 15.1 %copy-start = (bf16[8,2,256,512]{3,2,1,0:T(8,128)(2,1)S(1)}, bf16[8,2,256,512]{3,2,1,0:T(8,128)(2,1)}, u32[]{:S(2)}) copy-start(bf16[8,2,256,512]{3,2,1,0:T(8,128)(2,1)} %all-gather.11.cloned.1.call-done) | copy-start | bytes 12582916
  288.1 47.5 %collective-permute-start.18 = (bf16[2,2,2,256,512]{4,3,2,1,0:T(8,128)(2,1)}, bf16[2,2,2,256,512]{4,3,2,1,0:T(8,128)(2,1)}, u32[]{:S(2)}, u32[]{:S(2)}) collective-permute-start(bf16[2,2,2,256,512]{4,3,2,1,0:T(8,128)(2,1)} %first_product.7.refs_2_), channel_id=1, source_target_pairs={{0,1},{1,0},{2,3},{3,2},{4,5},{5,4},{6,7},{7,6},{8,9},{9,8},{10,11... | collective-permute-start | bytes 6291464 | tf_op jit(solution)/shard_map/ppermute | solution.py:188
  288.1 2.2 copy-start.2
  290.7 3.7 copy-start.23
  290.9 27.6 %copy-start.26 = (bf16[2,2,512,256]{3,2,1,0:T(8,128)(2,1)S(1)}, bf16[2,2,512,256]{3,2,1,0:T(8,128)(2,1)}, u32[]{:S(2)}) copy-start(bf16[2,2,512,256]{3,2,1,0:T(8,128)(2,1)} %second_product.10) | copy-start | bytes 3145732
  290.9 27.6 %collective-permute-start.14 = (bf16[2,2,2,128,512]{4,3,2,1,0:T(8,128)(2,1)S(1)}, bf16[2,2,2,128,512]{4,3,2,1,0:T(8,128)(2,1)S(1)}, u32[]{:S(2)}, u32[]{:S(2)}) collective-permute-start(bf16[2,2,2,128,512]{4,3,2,1,0:T(8,128)(2,1)S(1)} %dynamic-slice_select_fusion.1), channel_id=1, source_target_pairs={{4,8},{8,4},{5,9},{9,5},{6,10},{10,6},{7,11},{11,7},{20,24},{24,20... | collective-permute-start | bytes 3145736 | tf_op jit(solution)/shard_map/ppermute | solution.py:250
  294.4 26.3 %collective-permute-start.16 = (bf16[2,2,256,512]{3,2,1,0:T(8,128)(2,1)S(1)}, bf16[2,2,256,512]{3,2,1,0:T(8,128)(2,1)}, u32[]{:S(2)}, u32[]{:S(2)}) collective-permute-start(bf16[2,2,256,512]{3,2,1,0:T(8,128)(2,1)S(1)} %copy-done.23), channel_id=1, source_target_pairs={{2,0},{3,1},{12,14},{13,15},{18,16},{19,17},{28,30},{29,31}} | collective-permute-start | bytes 3145736 | tf_op jit(solution)/shard_map/ppermute | solution.py:257
  296.1 37.4 %collective-permute-start.15 = (bf16[2,2,256,512]{3,2,1,0:T(8,128)(2,1)}, bf16[2,2,256,512]{3,2,1,0:T(8,128)(2,1)S(1)}, u32[]{:S(2)}, u32[]{:S(2)}) collective-permute-start(bf16[2,2,256,512]{3,2,1,0:T(8,128)(2,1)} %second_product.9), channel_id=1, source_target_pairs={{4,0},{8,12},{5,1},{9,13},{6,2},{10,14},{7,3},{11,15},{20,16},{24,... | collective-permute-start | bytes 3145736 | tf_op jit(solution)/shard_map/ppermute | solution.py:249
  318.5 5.9 %copy-start.18 = (bf16[2,2,2,128,512]{4,3,2,1,0:T(8,128)(2,1)}, bf16[2,2,2,128,512]{4,3,2,1,0:T(8,128)(2,1)S(1)}, u32[]{:S(2)}) copy-start(bf16[2,2,2,128,512]{4,3,2,1,0:T(8,128)(2,1)S(1)} %collective-permute-done.14.refs_4_) | copy-start | bytes 3145732
  318.5 37.2 %collective-permute-start.22 = (bf16[2,2,512,256]{3,2,1,0:T(8,128)(2,1)S(1)}, bf16[2,2,512,256]{3,2,1,0:T(8,128)(2,1)}, u32[]{:S(2)}, u32[]{:S(2)}) collective-permute-start(bf16[2,2,512,256]{3,2,1,0:T(8,128)(2,1)S(1)} %copy-done.26), channel_id=1, source_target_pairs={{4,0},{8,12},{5,1},{9,13},{6,2},{10,14},{7,3},{11,15},{20,16},{24,... | collective-permute-start | bytes 3145736 | tf_op jit(solution)/shard_map/ppermute | solution.py:249
  320.8 36.6 %collective-permute-start.20 = (bf16[2,2,2,128,512]{4,3,2,1,0:T(8,128)(2,1)}, bf16[2,2,2,128,512]{4,3,2,1,0:T(8,128)(2,1)S(1)}, u32[]{:S(2)}, u32[]{:S(2)}) collective-permute-start(bf16[2,2,2,128,512]{4,3,2,1,0:T(8,128)(2,1)} %dynamic-slice_select_fusion), channel_id=1, source_target_pairs={{4,8},{8,4},{5,9},{9,5},{6,10},{10,6},{7,11},{11,7},{20,24},{24,20... | collective-permute-start | bytes 3145736 | tf_op jit(solution)/shard_map/ppermute | solution.py:250
  333.5 17.9 %copy-start.24 = (bf16[2,2,256,512]{3,2,1,0:T(8,128)(2,1)}, bf16[2,2,256,512]{3,2,1,0:T(8,128)(2,1)S(1)}, u32[]{:S(2)}) copy-start(bf16[2,2,256,512]{3,2,1,0:T(8,128)(2,1)S(1)} %collective-permute-done.15.refs_8_) | copy-start | bytes 3145732
  333.5 48.1 %collective-permute-start.23 = (bf16[2,2,256,512]{3,2,1,0:T(8,128)(2,1)S(1)}, bf16[2,2,256,512]{3,2,1,0:T(8,128)(2,1)S(1)}, u32[]{:S(2)}, u32[]{:S(2)}) collective-permute-start(bf16[2,2,256,512]{3,2,1,0:T(8,128)(2,1)S(1)} %collective-permute-done.15.refs_8_), channel_id=1, source_target_pairs={{2,0},{3,1},{12,14},{13,15},{18,16},{19,17},{28,30},{29,31}} | collective-permute-start | bytes 3145736 | tf_op jit(solution)/shard_map/ppermute | solution.py:257
  334.3 1.4 copy-start.6
  334.3 20.7 %collective-permute-start.26 = (bf16[2,2,512,128]{3,2,1,0:T(8,128)(2,1)}, bf16[2,2,512,128]{3,2,1,0:T(8,128)(2,1)S(1)}, u32[]{:S(2)}, u32[]{:S(2)}) collective-permute-start(bf16[2,2,512,128]{3,2,1,0:T(8,128)(2,1)} %second_product.11), channel_id=1, source_target_pairs={{4,0},{8,12},{5,1},{9,13},{6,2},{10,14},{7,3},{11,15},{20,16},{24,... | collective-permute-start | bytes 1572872 | tf_op jit(solution)/shard_map/ppermute | solution.py:249
  351.4 77.4 %collective-permute-start.19 = (bf16[2,2,512,512]{3,2,1,0:T(8,128)(2,1)}, bf16[2,2,512,512]{3,2,1,0:T(8,128)(2,1)S(1)}, u32[]{:S(2)}, u32[]{:S(2)}) collective-permute-start(bf16[2,2,512,512]{3,2,1,0:T(8,128)(2,1)} %second_product.12.refs_0_), channel_id=1, source_target_pairs={{6,4},{7,5},{8,10},{9,11},{22,20},{23,21},{24,26},{25,27}} | collective-permute-start | bytes 6291464 | tf_op jit(solution)/shard_map/ppermute | solution.py:257
  355.0 16.0 %copy-start.28 = (bf16[2,2,512,128]{3,2,1,0:T(8,128)(2,1)}, bf16[2,2,512,128]{3,2,1,0:T(8,128)(2,1)S(1)}, u32[]{:S(2)}) copy-start(bf16[2,2,512,128]{3,2,1,0:T(8,128)(2,1)S(1)} %collective-permute-done.26.refs_12_) | copy-start | bytes 1572868
  355.0 45.4 %collective-permute-start.27 = (bf16[2,2,512,128]{3,2,1,0:T(8,128)(2,1)S(1)}, bf16[2,2,512,128]{3,2,1,0:T(8,128)(2,1)S(1)}, u32[]{:S(2)}, u32[]{:S(2)}) collective-permute-start(bf16[2,2,512,128]{3,2,1,0:T(8,128)(2,1)S(1)} %collective-permute-done.26.refs_12_), channel_id=1, source_target_pairs={{0,2},{1,3},{14,12},{15,13},{16,18},{17,19},{30,28},{31,29}} | collective-permute-start | bytes 1572872 | tf_op jit(solution)/shard_map/ppermute | solution.py:257
  355.7 48.3 %collective-permute-start.25 = (bf16[2,2,512,256]{3,2,1,0:T(8,128)(2,1)}, bf16[2,2,512,256]{3,2,1,0:T(8,128)(2,1)}, u32[]{:S(2)}, u32[]{:S(2)}) collective-permute-start(bf16[2,2,512,256]{3,2,1,0:T(8,128)(2,1)} %collective-permute-done.22.refs_10_), channel_id=1, source_target_pairs={{0,2},{1,3},{14,12},{15,13},{16,18},{17,19},{30,28},{31,29}} | collective-permute-start | bytes 3145736 | tf_op jit(solution)/shard_map/ppermute | solution.py:257
  357.4 13.6 %copy-start.19 = (bf16[2,2,2,128,512]{4,3,2,1,0:T(8,128)(2,1)}, bf16[2,2,2,128,512]{4,3,2,1,0:T(8,128)(2,1)S(1)}, u32[]{:S(2)}) copy-start(bf16[2,2,2,128,512]{4,3,2,1,0:T(8,128)(2,1)S(1)} %collective-permute-done.20.refs_4_.refs_5_) | copy-start | bytes 3145732
  371.0 33.0 %collective-permute-start.21 = (bf16[2,2,512,256]{3,2,1,0:T(8,128)(2,1)}, bf16[2,2,512,256]{3,2,1,0:T(8,128)(2,1)}, u32[]{:S(2)}, u32[]{:S(2)}) collective-permute-start(bf16[2,2,512,256]{3,2,1,0:T(8,128)(2,1)} %second_product.13.refs_2_), channel_id=1, source_target_pairs={{4,6},{5,7},{10,8},{11,9},{20,22},{21,23},{26,24},{27,25}} | collective-permute-start | bytes 3145736 | tf_op jit(solution)/shard_map/ppermute | solution.py:257
  381.6 18.7 %copy-start.25 = (bf16[2,2,256,512]{3,2,1,0:T(8,128)(2,1)}, bf16[2,2,256,512]{3,2,1,0:T(8,128)(2,1)S(1)}, u32[]{:S(2)}) copy-start(bf16[2,2,256,512]{3,2,1,0:T(8,128)(2,1)S(1)} %collective-permute-done.23.refs_9_) | copy-start | bytes 3145732
  381.6 20.8 %collective-permute-start.28 = (bf16[2,2,512,128]{3,2,1,0:T(8,128)(2,1)}, bf16[2,2,512,128]{3,2,1,0:T(8,128)(2,1)}, u32[]{:S(2)}, u32[]{:S(2)}) collective-permute-start(bf16[2,2,512,128]{3,2,1,0:T(8,128)(2,1)} %second_product.14), channel_id=1, source_target_pairs={{4,0},{8,12},{5,1},{9,13},{6,2},{10,14},{7,3},{11,15},{20,16},{24,... | collective-permute-start | bytes 1572872 | tf_op jit(solution)/shard_map/ppermute | solution.py:249
  401.2 27.6 %collective-permute-start.24 = (bf16[2,2,512,256]{3,2,1,0:T(8,128)(2,1)}, bf16[2,2,512,256]{3,2,1,0:T(8,128)(2,1)S(1)}, u32[]{:S(2)}, u32[]{:S(2)}) collective-permute-start(bf16[2,2,512,256]{3,2,1,0:T(8,128)(2,1)} %second_product.15.refs_4_), channel_id=1, source_target_pairs={{4,6},{5,7},{10,8},{11,9},{20,22},{21,23},{26,24},{27,25}} | collective-permute-start | bytes 3145736 | tf_op jit(solution)/shard_map/ppermute | solution.py:257
  402.5 1.5 collective-permute-start.29
  428.8 1.0 copy-start.27
  428.8 1.7 copy-start.21
  (1 other events, 0.8 us)
Sparse Core Ops, SparseCore 0:
  38.4 33.6 all-gather.8
  73.7 34.4 all-gather.10
  109.7 34.4 all-gather.12
  145.7 34.4 all-gather.14

commit v4 on v0

v4 whole, which is shorter than its diff:
```python
import functools
import jax
import jax.numpy as jnp
from jax import lax
from jax.experimental import pallas as pl
from jax.experimental.pallas import tpu as pltpu
from jax.sharding import PartitionSpec as P

F32 = jnp.float32
BF16 = jnp.bfloat16
VMEM_BYTES = 56 * 1024 * 1024
LIGHT = pl.CostEstimate(flops=0, bytes_accessed=0, transcendentals=0)


def params(steps):
    return pltpu.CompilerParams(
        dimension_semantics=("arbitrary",) * steps, vmem_limit_bytes=VMEM_BYTES
    )


def mul(left, right):
    return jnp.dot(left, right, preferred_element_type=F32)


def mul_t(left, right):
    return lax.dot_general(left, right, (((1,), (1,)), ((), ())), preferred_element_type=F32)


def first_kernel(w_local, block_ref, mpo_ref, site_ref, *refs):
    q_ref, g_ref = refs[-2:]
    env_refs = refs[:-2]
    mpo_count, phys, _, rows, _ = q_ref.shape
    depth = env_refs[0].shape[2]
    per_col = site_ref.shape[-1] // depth
    for which in range(2):
        for w in range(w_local):
            g_real, g_imag = None, None
            for number in range(len(env_refs) // 2):
                block = block_ref[number]
                piece = pl.ds(pl.multiple_of((block % per_col) * depth, depth), depth)
                real = site_ref[block // per_col, :, 0, :, piece].reshape(phys * rows, depth)
                imag = site_ref[block // per_col, :, 1, :, piece].reshape(phys * rows, depth)
                env_real = env_refs[number * 2 + which][w, 0]
                env_imag = env_refs[number * 2 + which][w, 1]
                more_real = mul(real, env_real) + mul(imag, env_imag)
                more_imag = mul(real, env_imag) + mul(imag, -env_real)
                g_real = more_real if g_real is None else g_real + more_real
                g_imag = more_imag if g_imag is None else g_imag + more_imag
            g_ref[which * w_local + w, 0] = g_real
            g_ref[which * w_local + w, 1] = g_imag
    for part in range(2):
        for v in range(mpo_count):
            for t in range(phys):
                total = None
                for w in range(2 * w_local):
                    for s in range(phys):
                        term = mpo_ref[w, v, s, t] * g_ref[w, part, s * rows : (s + 1) * rows]
                        total = term if total is None else total + term
                q_ref[v, t, part] = total.astype(BF16)


def first_product(blocks, mpo, site, envs, row_tile, col_tile):
    col_count, phys, _, rows, wide = site.shape
    w_local, _, depth, cols = envs[0].shape
    mpo_count = mpo.shape[1]
    smem = pl.BlockSpec(memory_space=pltpu.SMEM)
    return pl.pallas_call(
        functools.partial(first_kernel, w_local),
        grid=(rows // row_tile, cols // col_tile),
        in_specs=[
            smem,
            smem,
            pl.BlockSpec((col_count, phys, 2, row_tile, wide), lambda i, j: (0, 0, 0, i, 0)),
        ]
        + [pl.BlockSpec((w_local, 2, depth, col_tile), lambda i, j: (0, 0, 0, j))] * len(envs),
        out_specs=pl.BlockSpec((mpo_count, phys, 2, row_tile, col_tile), lambda i, j: (0, 0, 0, i, j)),
        out_shape=jax.ShapeDtypeStruct((mpo_count, phys, 2, rows, cols), BF16),
        scratch_shapes=[pltpu.VMEM((2 * w_local, 2, phys * row_tile, col_tile), F32)],
        compiler_params=params(2),
        cost_estimate=LIGHT,
        name="first_product",
    )(blocks, mpo, site, *envs)


def second_kernel(pick_ref, q_ref, *refs):
    site_refs, out_ref = refs[:-1], refs[-1]
    join = lambda t, part: jnp.concatenate([site_ref[t, part] for site_ref in site_refs], axis=0)
    out_real, out_imag = None, None
    for t in range(q_ref.shape[1]):
        q_real, q_imag = q_ref[0, t, 0], q_ref[0, t, 1]
        real, imag = join(t, 0), join(t, 1)
        more_real = mul_t(q_real, real) + mul_t(-q_imag, imag)
        more_imag = mul_t(q_real, imag) + mul_t(q_imag, real)
        out_real = more_real if out_real is None else out_real + more_real
        out_imag = more_imag if out_imag is None else out_imag + more_imag
    out_ref[0, 0] = out_real.astype(BF16)
    out_ref[0, 1] = out_imag.astype(BF16)


def second_product(pick, q, sites, row_tile):
    mpo_count, phys, _, rows, cols = q.shape
    y_rows = sum(site.shape[2] for site in sites)
    return pl.pallas_call(
        second_kernel,
        grid=(mpo_count, rows // row_tile),
        in_specs=[
            pl.BlockSpec(memory_space=pltpu.SMEM),
            pl.BlockSpec((1, phys, 2, row_tile, cols), lambda v, i: (v, 0, 0, i, 0)),
        ]
        + [pl.BlockSpec(site.shape, lambda v, i: (0, 0, 0, 0)) for site in sites],
        out_specs=pl.BlockSpec((1, 2, row_tile, y_rows), lambda v, i: (v, 0, i, 0)),
        out_shape=jax.ShapeDtypeStruct((mpo_count, 2, rows, y_rows), BF16),
        compiler_params=params(2),
        cost_estimate=LIGHT,
        name="second_product",
    )(pick, q, *sites)


def finish_kernel(counts, pick_ref, *refs):
    out_ref = refs[-1]
    at = 0
    for step, sizes in enumerate(counts):
        parts = []
        for size in sizes:
            parts.append(refs[at : at + size])
            at += size

        @pl.when(pick_ref[0] == step)
        def _(parts=parts):
            half = sum(part[0].shape[3] for part in parts)
            for other, first in ((False, pick_ref[1]), (True, 1 - pick_ref[1])):
                for number, part in enumerate(parts):
                    width = part[0].shape[3]
                    total = sum(one[0, 0].astype(F32) for one in (part[2:] if other else part[:2]))
                    place = pl.ds(pl.multiple_of(first * half + number * width, width), width)
                    out_ref[0, 0, :, place] = total


def finish(pick, steps):
    parts = [value for step in steps for part in step for value in part]
    owners = [number for number, step in enumerate(steps) for part in step for _ in part]
    mpo_count, _, rows, _ = parts[0].shape
    cols = 2 * sum(part[0].shape[3] for part in steps[0])

    def spec(value, owner):
        def index(v, p, pick):
            mine = (pick[0] == owner).astype(jnp.int32)
            return (v * mine, p * mine, 0, 0)

        return pl.BlockSpec((1, 1) + value.shape[2:], index)

    return pl.pallas_call(
        functools.partial(finish_kernel, [[len(part) for part in step] for step in steps]),
        grid_spec=pltpu.PrefetchScalarGridSpec(
            num_scalar_prefetch=1,
            grid=(mpo_count, 2),
            in_specs=[spec(value, owner) for value, owner in zip(parts, owners)],
            out_specs=pl.BlockSpec((1, 1, rows, cols), lambda v, p, pick: (v, p, 0, 0)),
        ),
        out_shape=jax.ShapeDtypeStruct((mpo_count, 2, rows, cols), F32),
        compiler_params=params(2),
        name="finish",
    )(pick, *parts)


def after(value, *earlier):
    return lax.optimization_barrier((value,) + earlier)[0]


def swap(value):
    return lax.ppermute(value, "depth", [(0, 1), (1, 0)])


def split_inputs(environment, mpo):
    depth = lax.axis_index("depth")
    w_local, half = environment.shape[0], environment.shape[3]
    cols = half // 2
    env_own = lax.dynamic_slice_in_dim(environment, depth * cols, cols, 3)
    env_sib = swap(lax.dynamic_slice_in_dim(environment, (1 - depth) * cols, cols, 3))
    mpo_mine = jnp.concatenate(
        [
            lax.dynamic_slice_in_dim(mpo, depth * w_local, w_local, 0),
            lax.dynamic_slice_in_dim(mpo, (1 - depth) * w_local, w_local, 0),
        ],
        axis=0,
    )
    return env_own, env_sib, mpo_mine


def one_product(left, right, dims):
    return jnp.einsum(dims, left, right, preferred_element_type=F32)


def any_line(environment, site_tensor, mpo):
    depth = lax.axis_index("depth")
    env_own, env_sib, mpo_mine = split_inputs(environment, mpo)
    env_own = lax.all_gather(env_own, "row", axis=2, tiled=True)
    env_sib = lax.all_gather(env_sib, "row", axis=2, tiled=True)
    env = jnp.concatenate([env_own, env_sib], axis=0)
    cols = env.shape[3]
    planar = jnp.transpose(site_tensor, (0, 2, 1, 3))
    site_own = lax.dynamic_slice_in_dim(planar, depth * cols, cols, 3)
    site = lax.all_gather(planar, "col", axis=3, tiled=True)
    first = functools.partial(one_product, dims="sxa,wac->wsxc")
    g = jnp.stack(
        [
            first(site[:, 0], env[:, 0]) + first(site[:, 1], env[:, 1]),
            first(site[:, 0], env[:, 1]) - first(site[:, 1], env[:, 0]),
        ],
        axis=2,
    )
    q = jnp.einsum("wvst,wspxc->vtpxc", mpo_mine, g, precision=lax.Precision.HIGHEST).astype(BF16)
    site = lax.all_gather(site_own, "row", axis=2, tiled=True)
    second = functools.partial(one_product, dims="vtxc,tyc->vxy")
    total = jnp.stack(
        [
            second(q[:, :, 0], site[:, 0]) - second(q[:, :, 1], site[:, 1]),
            second(q[:, :, 0], site[:, 1]) + second(q[:, :, 1], site[:, 0]),
        ],
        axis=1,
    )
    return lax.psum_scatter(total, ("col", "depth"), scatter_dimension=3, tiled=True)


def ring(environment, site_tensor, mpo):
    row_count, col_count = lax.axis_size("row"), lax.axis_size("col")
    row, col, depth = (lax.axis_index(axis) for axis in ("row", "col", "depth"))
    axes = ("row", "col", "depth")
    place = lambda r, c, d: (r * col_count + c) * 2 + d
    shift = lambda value: lax.ppermute(
        value, "row", [(r, (r + 1) % row_count) for r in range(row_count)]
    )
    turn = lambda value: lax.ppermute(value, "col", [(0, 1), (1, 0)])
    in_order = lambda mine, sibling, axis: jnp.where(
        depth == 0,
        jnp.concatenate([mine, sibling], axis=axis),
        jnp.concatenate([sibling, mine], axis=axis),
    )

    env_own, env_sib, mpo_mine = split_inputs(environment, mpo)
    envs = [env_own, env_sib]
    for _ in range(row_count - 1):
        envs += [shift(envs[-2]), shift(envs[-1])]

    planar = jnp.transpose(after(site_tensor, envs[3]), (0, 2, 1, 3))
    rows = planar.shape[2]
    half = rows // 2
    mine = lax.dynamic_slice_in_dim(planar, depth * half, half, 2)
    other = turn(after(mine, envs[4]))
    other = in_order(other, swap(after(other, envs[5])), 2)
    site = jnp.where(col == 0, jnp.stack([planar, other]), jnp.stack([other, planar]))

    parts = [mine[:, :, : half // 2], mine[:, :, half // 2 :]]
    travelling = [[shift(after(part, env)) for part, env in zip(parts, envs[-2:])]]
    for _ in range(row_count - 2):
        travelling.append([shift(part) for part in travelling[-1]])

    blocks = jnp.stack([lax.rem(row - k + row_count, row_count) for k in range(row_count)])
    blocks = after(blocks.astype(jnp.int32), travelling[0][0])
    q = first_product(blocks, mpo_mine, site, envs, half, half)
    q = in_order(q, swap(after(q, travelling[0][1])), 4)

    pick = jnp.stack([lax.rem(row - col * 2 - depth + row_count, row_count), depth]).astype(jnp.int32)
    steps, gate = [], (q,)
    for step in range(row_count):
        goal = [((r - step) % row_count // 2, (r - step) % row_count % 2) for r in range(row_count)]

        def send(value, turned, crossed, cores=(0,)):
            pairs = []
            for r, (c, d) in enumerate(goal):
                for flip in cores:
                    e = d ^ flip
                    source = place(r, 1 - c if turned else c, 1 - e if crossed else e)
                    pairs.append((source, place(r, c, e)))
            return lax.ppermute(value, axes, pairs)

        if step < row_count - 1:
            low = second_product(after(pick, *gate), q, travelling[step - 1] if step else parts, half)
            turned = send(low, True, False, (0, 1))
            total = (low.astype(F32) + turned.astype(F32)).astype(BF16)
            steps.append([(low, turned, send(total, False, True))])
            gate = (low,) + ((travelling[1][0],) if step == 0 else ())
        else:
            done = []
            for number, site in enumerate(travelling[-1]):
                low = second_product(after(pick, *gate), q, [site], half)
                done.append(
                    (low, send(low, True, False), send(low, True, True), send(low, False, True))
                )
                gate = (low,) + steps[number][0][1:]
            steps.append(done)
        if step == row_count - 2:
            gate = gate + steps[0][0][1:2]
    return finish(pick, steps)


def solution(mesh):
    placed = (
        P(("groups", "depth"), None, "row", "col"),
        P("groups", "row", None, "col"),
        P("groups", None, None, None),
    )
    fits = mesh.shape["col"] == 2 and mesh.shape["row"] == 2 * mesh.shape["col"]
    return jax.shard_map(
        ring if fits else any_line,
        mesh=mesh,
        in_specs=placed,
        out_specs=P("groups", None, "row", ("col", "depth")),
        check_vma=False,
    )
```

time: 742 us -> 357 us (0.48)
  waiting for transfers between devices: 535 us -> 217 us
  matrix products: 115 us -> 0 us
  Pallas kernels: 0 us -> 72.7 us
  local copies, waits for them, and re-layouts: 66.2 us -> 10.2 us
  starting transfers between devices: 0.16 us -> 29.6 us
  other arithmetic: 10.7 us -> 25.7 us
  between operations: 13.2 us -> 0.63 us
    all_gather x3 -> x0, waiting for transfers between devices: 389 us -> none  [the longest x1 144 us: on_device(): lax.all_gather(own_site, 'row', axis=1, tiled=True)]
    ppermute x0 -> x28, waiting for transfers between devices: none -> 217 us  [the longest x12 153 us: ring(): lax.ppermute(value, 'row', [(r, (r + 1) % row_count) for r in range(row_c...]
    reduce_scatter x2 -> x0, waiting for transfers between devices: 144 us -> none  [the longest x1 124 us: on_device(): lax.psum_scatter(partial_env, ('col', 'depth'), scatter_dimension=3, tile...]
    dot_general x3 -> x0, matrix products: 115 us -> none  [the longest x1 58 us: on_device(): jnp.einsum('wvst,wspxc->vtpxc', mpo_mine, g_local, precision=highest)]
    pallas_call x0 -> x7, Pallas kernels: none -> 72.7 us  [the longest x5 41.9 us: second_product(): pl.pallas_call(second_kernel, grid=(mpo_count, rows // row_tile), in_spec...]
    ppermute x0 -> x28, starting transfers between devices: none -> 29.6 us  [the longest x12 17.8 us: send(): return lax.ppermute(value, axes, pairs)]
    reshape x2 -> x0, local copies, waits for them, and re-layouts: 28.9 us -> none  [on_device(): g_local = contracted.reshape(w_local, phys_count, row_count, 2, col_count)]
    select_n x0 -> x3, other arithmetic: none -> 21.3 us  [the longest x2 17.2 us: ring(): jnp.where(depth == 0, jnp.concatenate([mine, sibling], axis=axis), jnp.co...]
  transfers between devices with their start and end apart: 5 -> 28, of which waited for: 5 -> 15; matrix products, arithmetic and copies ran while one was open for 4% -> 8% of each run, Pallas kernels for 0% -> 19%
where the time goes in v4:
time: 357 us; the launch traced here: 356 us
  waiting for transfers between devices  217 us (61%)
  Pallas kernels  72.7 us (20%)
  starting transfers between devices  29.6 us (8%)
  other arithmetic  25.7 us (7%)
  local copies, waits for them, and re-layouts  10.2 us (3%)
    ppermute x12, waiting for transfers between devices, ring(): lax.ppermute(value, 'row', [(r, (r + 1) % row_count) for r in range(row_c...  153 us
    pallas_call x5, Pallas kernels, second_product(): pl.pallas_call(second_kernel, grid=(mpo_count, rows // row_tile), in_spec...  41.9 us
    ppermute x12, waiting for transfers between devices, send(): return lax.ppermute(value, axes, pairs)  37.6 us
    pallas_call x1, Pallas kernels, first_product(): pl.pallas_call(functools.partial(first_kernel, w_local), grid=(rows // ro...  24.4 us
    ppermute x1, waiting for transfers between devices, ring(): turn = lambda value: lax.ppermute(value, 'col', [(0, 1), (1, 0)])  19.9 us
    ppermute x12, starting transfers between devices, send(): return lax.ppermute(value, axes, pairs)  17.8 us
    select_n x2, other arithmetic, ring(): jnp.where(depth == 0, jnp.concatenate([mine, sibling], axis=axis), jnp.co...  17.2 us
  transfers between devices with their start and end apart: 28, of which 15 were waited for; matrix products, arithmetic and copies ran while one was open for 8% of the time, Pallas kernels for 19%

profile of v4, /device:TPU:1, one launch (start us, length us, event | category | flops | bytes accessed | tf_op | source)
XLA Modules:
  0.0 356.0 jit_solution(15627027768521899650)
XLA Ops:
  0.0 1.7 constant_dynamic-slice_fusion.2
  1.7 0.1 collective-permute-start
  1.9 2.7 collective-permute-start.2
  4.6 2.3 collective-permute-start.1
  6.9 23.2 %collective-permute-done.2.refs_2_ = bf16[1,2,512,512]{3,2,1,0:T(8,128)(2,1)S(1)} collective-permute-done((bf16[1,2,512,512]{3,2,1,0:T(8,128)(2,1)S(1)}, bf16[1,2,512,512]{3,2,1,0:T(8,128)(2,1)S(1)}, u32[]{:S(2)}, u32[]{:S(2)}) %collective-permute-start.2) | collective-permute-done | bytes 1048608 | tf_op jit(solution)/shard_map/ppermute | solution.py:230
  30.1 22.6 %collective-permute-done.1.refs_3_ = bf16[1,2,512,512]{3,2,1,0:T(8,128)(2,1)} collective-permute-done((bf16[1,2,512,512]{3,2,1,0:T(8,128)(2,1)S(1)}, bf16[1,2,512,512]{3,2,1,0:T(8,128)(2,1)}, u32[]{:S(2)}, u32[]{:S(2)}) %collective-permute-start.1) | collective-permute-done | bytes 1048608 | tf_op jit(solution)/shard_map/ppermute | solution.py:230
  52.7 3.5 copy.8
  56.2 0.0 copy-start
  56.2 0.0 copy-start.25
  56.2 0.2 dynamic-slice_bitcast_fusion
  56.4 18.7 %collective-permute-done.3.refs_4_ = bf16[1,2,512,512]{3,2,1,0:T(8,128)(2,1)} collective-permute-done((bf16[1,2,512,512]{3,2,1,0:T(8,128)(2,1)S(1)}, bf16[1,2,512,512]{3,2,1,0:T(8,128)(2,1)}, u32[]{:S(2)}, u32[]{:S(2)}) %collective-permute-start.3) | collective-permute-done | bytes 1048608 | tf_op jit(solution)/shard_map/ppermute | solution.py:230
  75.2 1.1 collective-permute-start.6
  76.2 0.7 collective-permute-start.4
  76.9 25.0 %collective-permute-done.7.refs_5_ = bf16[1,2,512,512]{3,2,1,0:T(8,128)(2,1)} collective-permute-done((bf16[1,2,512,512]{3,2,1,0:T(8,128)(2,1)}, bf16[1,2,512,512]{3,2,1,0:T(8,128)(2,1)}, u32[]{:S(2)}, u32[]{:S(2)}) %collective-permute-start.7) | collective-permute-done | bytes 1048608 | tf_op jit(solution)/shard_map/ppermute | solution.py:230
  101.9 19.9 %collective-permute-done.6 = bf16[2,2,256,1024]{3,2,1,0:T(8,128)(2,1)} collective-permute-done((bf16[2,2,256,1024]{3,2,1,0:T(8,128)(2,1)S(1)}, bf16[2,2,256,1024]{3,2,1,0:T(8,128)(2,1)}, u32[]{:S(2)}, u32[]{:S(2)}) %collective-permute-start.6) | collective-permute-done | bytes 2097184 | tf_op jit(solution)/shard_map/ppermute | solution.py:233
  121.8 1.5 collective-permute-start.8
  123.3 0.2 fusion
  123.5 0.8 collective-permute-done.4.refs_6_
  124.3 1.0 copy-done.15
  125.3 0.6 pad_add_fusion.1.block_ref
  125.8 0.6 pad_maximum_fusion.mpo_ref
  126.5 23.3 %collective-permute-done.5.refs_0_ = bf16[2,2,128,1024]{3,2,1,0:T(8,128)(2,1)S(1)} collective-permute-done((bf16[2,2,128,1024]{3,2,1,0:T(8,128)(2,1)S(1)}, bf16[2,2,128,1024]{3,2,1,0:T(8,128)(2,1)S(1)}, u32[]{:S(2)}, u32[]{:S(2)}) %collective-permute-start.5) | collective-permute-done | bytes 1048608 | tf_op jit(solution)/shard_map/ppermute | solution.py:230
  149.7 22.6 %collective-permute-done.9.refs_7_ = bf16[1,2,512,512]{3,2,1,0:T(8,128)(2,1)} collective-permute-done((bf16[1,2,512,512]{3,2,1,0:T(8,128)(2,1)}, bf16[1,2,512,512]{3,2,1,0:T(8,128)(2,1)}, u32[]{:S(2)}, u32[]{:S(2)}) %collective-permute-start.9) | collective-permute-done | bytes 1048608 | tf_op jit(solution)/shard_map/ppermute | solution.py:230
  172.3 5.7 %maximum_select_fusion.2 = bf16[1,2,2,512,1024]{4,3,2,1,0:T(8,128)(2,1)S(1)} fusion(bf16[1,2,2,256,1024]{4,3,2,1,0:T(8,128)(2,1)} %bitcast.10, bf16[1,2,2,256,1024]{4,3,2,1,0:T(8,128)(2,1)} %bitcast.9, pred[]{:T(512)S(6)} %eq.7), kind=kLoop, calls=%fused_computation.2 | loop fusion | flops 18874368 | bytes 8388609 | tf_op jit(solution)/shard_map/jit(_where)/select_n | solution.py:234
  178.1 4.0 %maximum_select_fusion.site_ref = bf16[2,2,2,512,1024]{4,3,2,1,0:T(8,128)(2,1)} fusion(bf16[1,2,2,512,1024]{4,3,2,1,0:T(8,128)(2,1)S(1)} %maximum_select_fusion.2, bf16[1,2,2,512,1024]{4,3,2,1,0:T(8,128)(2,1)S(1)} %bitcast.15, pred[]{:T(512)S(6)} %eq.8), kind=kLoop, calls=%fused_computation | loop fusion | flops 12582912 | bytes 16777216 | tf_op jit(solution)/shard_map/jit(_where)/select_n | solution.py:251
  182.1 24.4 %first_product.1 = bf16[2,2,2,512,512]{4,3,2,1,0:T(8,128)(2,1)} custom-call(s32[4]{0:T(128)} %pad_add_fusion.1.block_ref, f32[2,2,2,2]{3,2,1,0:T(2,128)} %pad_maximum_fusion.mpo_ref, bf16[2,2,2,512,1024]{4,3,2,1,0:T(8,128)(2,1)} %maximum_select_fusion.site_ref, bf16[1,2,512,512]{3,2,1,0:T(8,128)(2,1)} %copy-done.5, bf16[1,2,512,512]{3,2,1,0:T(8,128)(2,1)} %copy-done.13, ...), custom_call_target="tpu_custom_call" | custom-call | tf_op jit(solution)/shard_map/first_product/pallas_call | solution.py:67
  206.5 1.0 copy-done.17
  207.5 2.9 collective-permute-start.11
  210.4 0.6 pad_add_fusion.pick_ref
  210.9 0.1 collective-permute-start.17
  211.0 6.5 %collective-permute-done.11 = bf16[2,2,2,512,512]{4,3,2,1,0:T(8,128)(2,1)} collective-permute-done((bf16[2,2,2,512,512]{4,3,2,1,0:T(8,128)(2,1)}, bf16[2,2,2,512,512]{4,3,2,1,0:T(8,128)(2,1)}, u32[]{:S(2)}, u32[]{:S(2)}) %collective-permute-start.11) | collective-permute-done | bytes 4194336 | tf_op jit(solution)/shard_map/ppermute | solution.py:171
  217.5 11.5 %maximum_select_fusion.1.q_ref = bf16[2,2,2,512,1024]{4,3,2,1,0:T(8,128)(2,1)} fusion(bf16[2,2,2,512,512]{4,3,2,1,0:T(8,128)(2,1)} %collective-permute-done.11, bf16[2,2,2,512,512]{4,3,2,1,0:T(8,128)(2,1)} %first_product.1, pred[]{:T(512)S(6)} %eq.7), kind=kLoop, calls=%fused_computation.1 | loop fusion | flops 37748736 | bytes 16777216 | tf_op jit(solution)/shard_map/jit(_where)/select_n | solution.py:234
  229.0 8.6 %second_product.5.refs_0_ = bf16[2,2,512,256]{3,2,1,0:T(8,128)(2,1)} custom-call(s32[2]{0:T(128)} %pad_add_fusion.pick_ref, bf16[2,2,2,512,1024]{4,3,2,1,0:T(8,128)(2,1)} %maximum_select_fusion.1.q_ref, bf16[2,2,128,1024]{3,2,1,0:T(8,128)(2,1)} %copy-done.10, bf16[2,2,128,1024]{3,2,1,0:T(8,128)(2,1)} %copy-done.9), custom_call_target="tpu_custom_call" | custom-call | tf_op jit(solution)/shard_map/second_product/pallas_call | solution.py:103
  237.6 1.3 collective-permute-start.12
  238.9 0.2 collective-permute-start.20
  239.1 8.6 %second_product.6.refs_3_ = bf16[2,2,512,256]{3,2,1,0:T(8,128)(2,1)} custom-call(s32[2]{0:T(128)} %pad_add_fusion.pick_ref, bf16[2,2,2,512,1024]{4,3,2,1,0:T(8,128)(2,1)} %maximum_select_fusion.1.q_ref, bf16[2,2,128,1024]{3,2,1,0:T(8,128)(2,1)} %copy-done.12, bf16[2,2,128,1024]{3,2,1,0:T(8,128)(2,1)} %copy-done.17), custom_call_target="tpu_custom_call" | custom-call | tf_op jit(solution)/shard_map/second_product/pallas_call | solution.py:103
  247.7 12.7 %collective-permute-done.17.refs_1_ = bf16[2,2,128,1024]{3,2,1,0:T(8,128)(2,1)S(1)} collective-permute-done((bf16[2,2,128,1024]{3,2,1,0:T(8,128)(2,1)}, bf16[2,2,128,1024]{3,2,1,0:T(8,128)(2,1)S(1)}, u32[]{:S(2)}, u32[]{:S(2)}) %collective-permute-start.17) | collective-permute-done | bytes 1048608 | tf_op jit(solution)/shard_map/ppermute | solution.py:230
  260.5 1.0 copy-done.18
  261.5 8.6 %second_product.7.refs_6_ = bf16[2,2,512,256]{3,2,1,0:T(8,128)(2,1)} custom-call(s32[2]{0:T(128)} %pad_add_fusion.pick_ref, bf16[2,2,2,512,1024]{4,3,2,1,0:T(8,128)(2,1)} %maximum_select_fusion.1.q_ref, bf16[2,2,128,1024]{3,2,1,0:T(8,128)(2,1)} %collective-permute-done.14.refs_0_, bf16[2,2,128,1024]{3,2,1,0:T(8,128)(2,1)} %copy-done.18), custom_call_target="tpu_custom_call" | custom-call | tf_op jit(solution)/shard_map/second_product/pallas_call | solution.py:103
  270.1 2.8 collective-permute-start.18
  272.8 1.4 collective-permute-start.15
  274.2 0.1 collective-permute-start.24
  274.3 1.3 add_convert_fusion.2
  275.6 3.1 collective-permute-start.13
  278.8 4.3 %collective-permute-done.20.refs_0_ = bf16[2,2,128,1024]{3,2,1,0:T(8,128)(2,1)} collective-permute-done((bf16[2,2,128,1024]{3,2,1,0:T(8,128)(2,1)}, bf16[2,2,128,1024]{3,2,1,0:T(8,128)(2,1)}, u32[]{:S(2)}, u32[]{:S(2)}) %collective-permute-start.20) | collective-permute-done | bytes 1048608 | tf_op jit(solution)/shard_map/ppermute | solution.py:230
  283.1 8.0 %second_product.8.refs_9_ = bf16[2,2,512,128]{3,2,1,0:T(8,128)(2,1)} custom-call(s32[2]{0:T(128)} %pad_add_fusion.pick_ref, bf16[2,2,2,512,1024]{4,3,2,1,0:T(8,128)(2,1)} %maximum_select_fusion.1.q_ref, bf16[2,2,128,1024]{3,2,1,0:T(8,128)(2,1)} %collective-permute-done.20.refs_0_), custom_call_target="tpu_custom_call" | custom-call | tf_op jit(solution)/shard_map/second_product/pallas_call | solution.py:103
  291.1 1.4 collective-permute-start.21
  292.5 2.3 collective-permute-done.18.refs_7_
  294.8 1.3 collective-permute-start.22
  296.1 1.2 add_convert_fusion
  297.3 19.8 %collective-permute-done.15.refs_4_ = bf16[2,2,512,256]{3,2,1,0:T(8,128)(2,1)S(1)} collective-permute-done((bf16[2,2,512,256]{3,2,1,0:T(8,128)(2,1)S(1)}, bf16[2,2,512,256]{3,2,1,0:T(8,128)(2,1)S(1)}, u32[]{:S(2)}, u32[]{:S(2)}) %collective-permute-start.15) | collective-permute-done | bytes 1048608 | tf_op jit(solution)/shard_map/ppermute | solution.py:275
  317.2 0.7 collective-permute-start.19
  317.9 0.2 add_convert_fusion.1
  318.2 0.7 collective-permute-start.16
  318.9 1.3 collective-permute-start.23
  320.2 8.1 %second_product.9.refs_13_ = bf16[2,2,512,128]{3,2,1,0:T(8,128)(2,1)} custom-call(s32[2]{0:T(128)} %pad_add_fusion.pick_ref, bf16[2,2,2,512,1024]{4,3,2,1,0:T(8,128)(2,1)} %maximum_select_fusion.1.q_ref, bf16[2,2,128,1024]{3,2,1,0:T(8,128)(2,1)} %copy-done.21), custom_call_target="tpu_custom_call" | custom-call | tf_op jit(solution)/shard_map/second_product/pallas_call | solution.py:103
  328.3 1.3 collective-permute-start.25
  329.6 1.3 collective-permute-start.26
  330.9 1.3 collective-permute-start.27
  332.3 13.3 %collective-permute-done.25.refs_14_ = bf16[2,2,512,128]{3,2,1,0:T(8,128)(2,1)S(1)} collective-permute-done((bf16[2,2,512,128]{3,2,1,0:T(8,128)(2,1)}, bf16[2,2,512,128]{3,2,1,0:T(8,128)(2,1)S(1)}, u32[]{:S(2)}, u32[]{:S(2)}) %collective-permute-start.25) | collective-permute-done | bytes 524320 | tf_op jit(solution)/shard_map/ppermute | solution.py:275
  345.6 2.1 collective-permute-done.26.refs_15_
  347.8 0.8 copy-done.23
  348.6 0.8 copy-done.24
  349.4 6.5 %finish.1 = f32[2,2,512,512]{3,2,1,0:T(8,128)} custom-call(s32[2]{0:T(128)} %pad_add_fusion.pick_ref, bf16[2,2,512,256]{3,2,1,0:T(8,128)(2,1)} %second_product.5.refs_0_, bf16[2,2,512,256]{3,2,1,0:T(8,128)(2,1)} %copy-done.6, bf16[2,2,512,256]{3,2,1,0:T(8,128)(2,1)} %copy-done.16, bf16[2,2,512,256]{3,2,1,0:T(8,128)(2,1)} %second_product.6.refs_3_, ...), custom_call_target="tpu_custom_call" | custom-call | tf_op jit(solution)/shard_map/finish/pallas_call | solution.py:152
  (65 shorter events, 0.1 us)
Async XLA Ops:
  1.7 54.4 %copy-start.5 = (bf16[1,2,512,512]{3,2,1,0:T(8,128)(2,1)}, bf16[1,2,512,512]{3,2,1,0:T(8,128)(2,1)S(1)}, u32[]{:S(2)}) copy-start(bf16[1,2,512,512]{3,2,1,0:T(8,128)(2,1)S(1)} %get-tuple-element.33.refs_0_) | copy-start | bytes 3145732
  1.7 2.9 collective-permute-start
  1.9 28.2 %collective-permute-start.2 = (bf16[1,2,512,512]{3,2,1,0:T(8,128)(2,1)S(1)}, bf16[1,2,512,512]{3,2,1,0:T(8,128)(2,1)S(1)}, u32[]{:S(2)}, u32[]{:S(2)}) collective-permute-start(bf16[1,2,512,512]{3,2,1,0:T(8,128)(2,1)S(1)} %get-tuple-element.33.refs_0_), channel_id=1, source_target_pairs={{0,4},{4,8},{8,12},{12,0},{1,5},{5,9},{9,13},{13,1},{2,6},{6,10},{... | collective-permute-start | bytes 3145736 | tf_op jit(solution)/shard_map/ppermute | solution.py:230
  4.6 51.6 %copy-start.13 = (bf16[1,2,512,512]{3,2,1,0:T(8,128)(2,1)}, bf16[1,2,512,512]{3,2,1,0:T(8,128)(2,1)S(1)}, u32[]{:S(2)}) copy-start(bf16[1,2,512,512]{3,2,1,0:T(8,128)(2,1)S(1)} %collective-permute-done.refs_1_) | copy-start | bytes 3145732
  4.6 48.1 %collective-permute-start.1 = (bf16[1,2,512,512]{3,2,1,0:T(8,128)(2,1)S(1)}, bf16[1,2,512,512]{3,2,1,0:T(8,128)(2,1)}, u32[]{:S(2)}, u32[]{:S(2)}) collective-permute-start(bf16[1,2,512,512]{3,2,1,0:T(8,128)(2,1)S(1)} %collective-permute-done.refs_1_), channel_id=1, source_target_pairs={{0,4},{4,8},{8,12},{12,0},{1,5},{5,9},{9,13},{13,1},{2,6},{6,10},{... | collective-permute-start | bytes 3145736 | tf_op jit(solution)/shard_map/ppermute | solution.py:230
  30.1 26.1 %copy-start.14 = (bf16[1,2,512,512]{3,2,1,0:T(8,128)(2,1)}, bf16[1,2,512,512]{3,2,1,0:T(8,128)(2,1)S(1)}, u32[]{:S(2)}) copy-start(bf16[1,2,512,512]{3,2,1,0:T(8,128)(2,1)S(1)} %collective-permute-done.2.refs_2_) | copy-start | bytes 3145732
  30.1 45.0 %collective-permute-start.3 = (bf16[1,2,512,512]{3,2,1,0:T(8,128)(2,1)S(1)}, bf16[1,2,512,512]{3,2,1,0:T(8,128)(2,1)}, u32[]{:S(2)}, u32[]{:S(2)}) collective-permute-start(bf16[1,2,512,512]{3,2,1,0:T(8,128)(2,1)S(1)} %collective-permute-done.2.refs_2_), channel_id=1, source_target_pairs={{0,4},{4,8},{8,12},{12,0},{1,5},{5,9},{9,13},{13,1},{2,6},{6,10},{... | collective-permute-start | bytes 3145736 | tf_op jit(solution)/shard_map/ppermute | solution.py:230
  56.2 67.3 %copy-start = (bf16[2,512,2,1024]{3,1,2,0:T(8,128)(2,1)}, bf16[2,512,2,1024]{3,1,2,0:T(8,128)(2,1)S(1)}, u32[]{:S(2)}) copy-start(bf16[2,512,2,1024]{3,1,2,0:T(8,128)(2,1)S(1)} %copy.8) | copy-start | bytes 12582916
  56.2 69.6 %copy-start.25 = (f32[2,2,2,2]{3,2,1,0:T(2,128)S(1)}, f32[2,2,2,2]{3,2,1,0:T(2,128)}, u32[]{:S(2)}) copy-start(f32[2,2,2,2]{3,2,1,0:T(2,128)} %param.5) | copy-start | bytes 196
  75.2 46.6 %collective-permute-start.6 = (bf16[2,2,256,1024]{3,2,1,0:T(8,128)(2,1)S(1)}, bf16[2,2,256,1024]{3,2,1,0:T(8,128)(2,1)}, u32[]{:S(2)}, u32[]{:S(2)}) collective-permute-start(bf16[2,2,256,1024]{3,2,1,0:T(8,128)(2,1)S(1)} %dynamic-slice_bitcast_fusion), channel_id=1, source_target_pairs={{0,2},{2,0},{1,3},{3,1},{4,6},{6,4},{5,7},{7,5},{8,10},{10,8},{9,1... | collective-permute-start | bytes 6291464 | tf_op jit(solution)/shard_map/ppermute | solution.py:233
  76.2 25.7 %collective-permute-start.7 = (bf16[1,2,512,512]{3,2,1,0:T(8,128)(2,1)}, bf16[1,2,512,512]{3,2,1,0:T(8,128)(2,1)}, u32[]{:S(2)}, u32[]{:S(2)}) collective-permute-start(bf16[1,2,512,512]{3,2,1,0:T(8,128)(2,1)} %collective-permute-done.1.refs_3_), channel_id=1, source_target_pairs={{0,4},{4,8},{8,12},{12,0},{1,5},{5,9},{9,13},{13,1},{2,6},{6,10},{... | collective-permute-start | bytes 3145736 | tf_op jit(solution)/shard_map/ppermute | solution.py:230
  76.2 48.1 %collective-permute-start.4 = (bf16[1,2,512,512]{3,2,1,0:T(8,128)(2,1)}, bf16[1,2,512,512]{3,2,1,0:T(8,128)(2,1)S(1)}, u32[]{:S(2)}, u32[]{:S(2)}) collective-permute-start(bf16[1,2,512,512]{3,2,1,0:T(8,128)(2,1)} %collective-permute-done.3.refs_4_), channel_id=1, source_target_pairs={{0,4},{4,8},{8,12},{12,0},{1,5},{5,9},{9,13},{13,1},{2,6},{6,10},{... | collective-permute-start | bytes 3145736 | tf_op jit(solution)/shard_map/ppermute | solution.py:230
  121.8 50.5 %collective-permute-start.8 = (bf16[2,2,256,1024]{3,2,1,0:T(8,128)(2,1)}, bf16[2,2,256,1024]{3,2,1,0:T(8,128)(2,1)}, u32[]{:S(2)}, u32[]{:S(2)}) collective-permute-start(bf16[2,2,256,1024]{3,2,1,0:T(8,128)(2,1)} %collective-permute-done.6), channel_id=1, source_target_pairs={{0,1},{1,0},{2,3},{3,2},{4,5},{5,4},{6,7},{7,6},{8,9},{9,8},{10,11... | collective-permute-start | bytes 6291464 | tf_op jit(solution)/shard_map/ppermute | solution.py:171
  123.5 54.6 %copy-start.9 = (bf16[2,2,128,1024]{3,2,1,0:T(8,128)(2,1)}, bf16[2,2,128,1024]{3,2,1,0:T(8,128)(2,1)S(1)}, u32[]{:S(2)}) copy-start(bf16[2,2,128,1024]{3,2,1,0:T(8,128)(2,1)S(1)} %get-tuple-element.22.refs_1_) | copy-start | bytes 3145732
  123.5 54.6 %copy-start.10 = (bf16[2,2,128,1024]{3,2,1,0:T(8,128)(2,1)}, bf16[2,2,128,1024]{3,2,1,0:T(8,128)(2,1)S(1)}, u32[]{:S(2)}) copy-start(bf16[2,2,128,1024]{3,2,1,0:T(8,128)(2,1)S(1)} %get-tuple-element.18.refs_0_) | copy-start | bytes 3145732
  124.3 1.0 copy-start.15
  125.3 24.5 %collective-permute-start.5 = (bf16[2,2,128,1024]{3,2,1,0:T(8,128)(2,1)S(1)}, bf16[2,2,128,1024]{3,2,1,0:T(8,128)(2,1)S(1)}, u32[]{:S(2)}, u32[]{:S(2)}) collective-permute-start(bf16[2,2,128,1024]{3,2,1,0:T(8,128)(2,1)S(1)} %get-tuple-element.18.refs_0_), channel_id=1, source_target_pairs={{0,4},{4,8},{8,12},{12,0},{1,5},{5,9},{9,13},{13,1},{2,6},{6,10},{... | collective-permute-start | bytes 3145736 | tf_op jit(solution)/shard_map/ppermute | solution.py:230
  125.3 47.0 %collective-permute-start.9 = (bf16[1,2,512,512]{3,2,1,0:T(8,128)(2,1)}, bf16[1,2,512,512]{3,2,1,0:T(8,128)(2,1)}, u32[]{:S(2)}, u32[]{:S(2)}) collective-permute-start(bf16[1,2,512,512]{3,2,1,0:T(8,128)(2,1)} %collective-permute-done.7.refs_5_), channel_id=1, source_target_pairs={{0,4},{4,8},{8,12},{12,0},{1,5},{5,9},{9,13},{13,1},{2,6},{6,10},{... | collective-permute-start | bytes 3145736 | tf_op jit(solution)/shard_map/ppermute | solution.py:230
  149.7 61.2 %copy-start.12 = (bf16[2,2,128,1024]{3,2,1,0:T(8,128)(2,1)}, bf16[2,2,128,1024]{3,2,1,0:T(8,128)(2,1)S(1)}, u32[]{:S(2)}) copy-start(bf16[2,2,128,1024]{3,2,1,0:T(8,128)(2,1)S(1)} %collective-permute-done.5.refs_0_) | copy-start | bytes 3145732
  172.3 34.2 %collective-permute-start.10 = (bf16[2,2,128,1024]{3,2,1,0:T(8,128)(2,1)S(1)}, bf16[2,2,128,1024]{3,2,1,0:T(8,128)(2,1)S(1)}, u32[]{:S(2)}, u32[]{:S(2)}) collective-permute-start(bf16[2,2,128,1024]{3,2,1,0:T(8,128)(2,1)S(1)} %get-tuple-element.22.refs_1_), channel_id=1, source_target_pairs={{0,4},{4,8},{8,12},{12,0},{1,5},{5,9},{9,13},{13,1},{2,6},{6,10},{... | collective-permute-start | bytes 3145736 | tf_op jit(solution)/shard_map/ppermute | solution.py:230
  172.3 5.8 %copy-start.1 = (bf16[2,512,2,1024]{3,1,2,0:T(8,128)(2,1)S(1)}, bf16[2,512,2,1024]{3,1,2,0:T(8,128)(2,1)}, u32[]{:S(2)}) copy-start(bf16[2,512,2,1024]{3,1,2,0:T(8,128)(2,1)} %copy-done) | copy-start | bytes 12582916
  206.5 1.0 copy-start.17
  207.5 10.0 %collective-permute-start.11 = (bf16[2,2,2,512,512]{4,3,2,1,0:T(8,128)(2,1)}, bf16[2,2,2,512,512]{4,3,2,1,0:T(8,128)(2,1)}, u32[]{:S(2)}, u32[]{:S(2)}) collective-permute-start(bf16[2,2,2,512,512]{4,3,2,1,0:T(8,128)(2,1)} %first_product.1), channel_id=1, source_target_pairs={{0,1},{1,0},{2,3},{3,2},{4,5},{5,4},{6,7},{7,6},{8,9},{9,8},{10,11... | collective-permute-start | bytes 12582920 | tf_op jit(solution)/shard_map/ppermute | solution.py:171
  210.9 28.0 %collective-permute-start.14 = (bf16[2,2,128,1024]{3,2,1,0:T(8,128)(2,1)S(1)}, bf16[2,2,128,1024]{3,2,1,0:T(8,128)(2,1)}, u32[]{:S(2)}, u32[]{:S(2)}) collective-permute-start(bf16[2,2,128,1024]{3,2,1,0:T(8,128)(2,1)S(1)} %collective-permute-done.5.refs_0_), channel_id=1, source_target_pairs={{0,4},{4,8},{8,12},{12,0},{1,5},{5,9},{9,13},{13,1},{2,6},{6,10},{... | collective-permute-start | bytes 3145736 | tf_op jit(solution)/shard_map/ppermute | solution.py:230
  210.9 49.6 %collective-permute-start.17 = (bf16[2,2,128,1024]{3,2,1,0:T(8,128)(2,1)}, bf16[2,2,128,1024]{3,2,1,0:T(8,128)(2,1)S(1)}, u32[]{:S(2)}, u32[]{:S(2)}) collective-permute-start(bf16[2,2,128,1024]{3,2,1,0:T(8,128)(2,1)} %copy-done.17), channel_id=1, source_target_pairs={{0,4},{4,8},{8,12},{12,0},{1,5},{5,9},{9,13},{13,1},{2,6},{6,10},{... | collective-permute-start | bytes 3145736 | tf_op jit(solution)/shard_map/ppermute | solution.py:230
  237.6 36.7 %collective-permute-start.12 = (bf16[2,2,512,256]{3,2,1,0:T(8,128)(2,1)}, bf16[2,2,512,256]{3,2,1,0:T(8,128)(2,1)S(1)}, u32[]{:S(2)}, u32[]{:S(2)}) collective-permute-start(bf16[2,2,512,256]{3,2,1,0:T(8,128)(2,1)} %second_product.5.refs_0_), channel_id=1, source_target_pairs={{2,0},{3,1},{7,5},{6,4},{8,10},{9,11},{13,15},{12,14},{18,16},{19,... | collective-permute-start | bytes 3145736 | tf_op jit(solution)/shard_map/ppermute | solution.py:275
  238.9 44.2 %collective-permute-start.20 = (bf16[2,2,128,1024]{3,2,1,0:T(8,128)(2,1)}, bf16[2,2,128,1024]{3,2,1,0:T(8,128)(2,1)}, u32[]{:S(2)}, u32[]{:S(2)}) collective-permute-start(bf16[2,2,128,1024]{3,2,1,0:T(8,128)(2,1)} %collective-permute-done.14.refs_0_), channel_id=1, source_target_pairs={{0,4},{4,8},{8,12},{12,0},{1,5},{5,9},{9,13},{13,1},{2,6},{6,10},{... | collective-permute-start | bytes 3145736 | tf_op jit(solution)/shard_map/ppermute | solution.py:230
  247.7 25.1 %copy-start.3 = (bf16[2,2,512,256]{3,2,1,0:T(8,128)(2,1)S(1)}, bf16[2,2,512,256]{3,2,1,0:T(8,128)(2,1)}, u32[]{:S(2)}) copy-start(bf16[2,2,512,256]{3,2,1,0:T(8,128)(2,1)} %second_product.6.refs_3_) | copy-start | bytes 3145732
  247.7 26.5 %copy-start.2 = (bf16[2,2,512,256]{3,2,1,0:T(8,128)(2,1)S(1)}, bf16[2,2,512,256]{3,2,1,0:T(8,128)(2,1)}, u32[]{:S(2)}) copy-start(bf16[2,2,512,256]{3,2,1,0:T(8,128)(2,1)} %second_product.5.refs_0_) | copy-start | bytes 3145732
  260.5 1.0 copy-start.18
  270.1 24.7 %collective-permute-start.18 = (bf16[2,2,512,256]{3,2,1,0:T(8,128)(2,1)}, bf16[2,2,512,256]{3,2,1,0:T(8,128)(2,1)S(1)}, u32[]{:S(2)}, u32[]{:S(2)}) collective-permute-start(bf16[2,2,512,256]{3,2,1,0:T(8,128)(2,1)} %second_product.7.refs_6_), channel_id=1, source_target_pairs={{0,2},{1,3},{5,7},{4,6},{10,8},{11,9},{15,13},{14,12},{16,18},{17,... | collective-permute-start | bytes 3145736 | tf_op jit(solution)/shard_map/ppermute | solution.py:275
  272.8 44.3 %collective-permute-start.15 = (bf16[2,2,512,256]{3,2,1,0:T(8,128)(2,1)S(1)}, bf16[2,2,512,256]{3,2,1,0:T(8,128)(2,1)S(1)}, u32[]{:S(2)}, u32[]{:S(2)}) collective-permute-start(bf16[2,2,512,256]{3,2,1,0:T(8,128)(2,1)S(1)} %copy-done.3), channel_id=1, source_target_pairs={{1,3},{0,2},{6,4},{7,5},{11,9},{10,8},{12,14},{13,15},{17,19},{16,... | collective-permute-start | bytes 3145736 | tf_op jit(solution)/shard_map/ppermute | solution.py:275
  274.2 43.9 %collective-permute-start.24 = (bf16[2,2,128,1024]{3,2,1,0:T(8,128)(2,1)}, bf16[2,2,128,1024]{3,2,1,0:T(8,128)(2,1)S(1)}, u32[]{:S(2)}, u32[]{:S(2)}) collective-permute-start(bf16[2,2,128,1024]{3,2,1,0:T(8,128)(2,1)} %copy-done.18), channel_id=1, source_target_pairs={{0,4},{4,8},{8,12},{12,0},{1,5},{5,9},{9,13},{13,1},{2,6},{6,10},{... | collective-permute-start | bytes 3145736 | tf_op jit(solution)/shard_map/ppermute | solution.py:230
  274.3 16.8 %copy-start.6 = (bf16[2,2,512,256]{3,2,1,0:T(8,128)(2,1)}, bf16[2,2,512,256]{3,2,1,0:T(8,128)(2,1)S(1)}, u32[]{:S(2)}) copy-start(bf16[2,2,512,256]{3,2,1,0:T(8,128)(2,1)S(1)} %collective-permute-done.12.refs_1_) | copy-start | bytes 3145732
  275.6 20.5 %copy-start.4 = (bf16[2,2,512,256]{3,2,1,0:T(8,128)(2,1)S(1)}, bf16[2,2,512,256]{3,2,1,0:T(8,128)(2,1)}, u32[]{:S(2)}) copy-start(bf16[2,2,512,256]{3,2,1,0:T(8,128)(2,1)} %second_product.7.refs_6_) | copy-start | bytes 3145732
  275.6 43.3 %collective-permute-start.13 = (bf16[2,2,512,256]{3,2,1,0:T(8,128)(2,1)}, bf16[2,2,512,256]{3,2,1,0:T(8,128)(2,1)S(1)}, u32[]{:S(2)}, u32[]{:S(2)}) collective-permute-start(bf16[2,2,512,256]{3,2,1,0:T(8,128)(2,1)} %add_convert_fusion.2), channel_id=1, source_target_pairs={{1,0},{4,5},{11,10},{14,15},{17,16},{20,21},{27,26},{30,31}} | collective-permute-start | bytes 3145736 | tf_op jit(solution)/shard_map/ppermute | solution.py:275
  291.1 27.8 %copy-start.11 = (bf16[2,2,512,128]{3,2,1,0:T(8,128)(2,1)S(1)}, bf16[2,2,512,128]{3,2,1,0:T(8,128)(2,1)}, u32[]{:S(2)}) copy-start(bf16[2,2,512,128]{3,2,1,0:T(8,128)(2,1)} %second_product.8.refs_9_) | copy-start | bytes 1572868
  291.1 37.2 %collective-permute-start.21 = (bf16[2,2,512,128]{3,2,1,0:T(8,128)(2,1)}, bf16[2,2,512,128]{3,2,1,0:T(8,128)(2,1)}, u32[]{:S(2)}, u32[]{:S(2)}) collective-permute-start(bf16[2,2,512,128]{3,2,1,0:T(8,128)(2,1)} %second_product.8.refs_9_), channel_id=1, source_target_pairs={{3,1},{4,6},{9,11},{14,12},{19,17},{20,22},{25,27},{30,28}} | collective-permute-start | bytes 1572872 | tf_op jit(solution)/shard_map/ppermute | solution.py:275
  294.8 33.5 %copy-start.7 = (bf16[2,2,512,256]{3,2,1,0:T(8,128)(2,1)}, bf16[2,2,512,256]{3,2,1,0:T(8,128)(2,1)S(1)}, u32[]{:S(2)}) copy-start(bf16[2,2,512,256]{3,2,1,0:T(8,128)(2,1)S(1)} %collective-permute-done.18.refs_7_) | copy-start | bytes 3145732
  294.8 34.8 %collective-permute-start.22 = (bf16[2,2,512,128]{3,2,1,0:T(8,128)(2,1)}, bf16[2,2,512,128]{3,2,1,0:T(8,128)(2,1)}, u32[]{:S(2)}, u32[]{:S(2)}) collective-permute-start(bf16[2,2,512,128]{3,2,1,0:T(8,128)(2,1)} %second_product.8.refs_9_), channel_id=1, source_target_pairs={{2,1},{5,6},{8,11},{15,12},{18,17},{21,22},{24,27},{31,28}} | collective-permute-start | bytes 1572872 | tf_op jit(solution)/shard_map/ppermute | solution.py:275
  317.2 11.2 %copy-start.8 = (bf16[2,2,512,256]{3,2,1,0:T(8,128)(2,1)}, bf16[2,2,512,256]{3,2,1,0:T(8,128)(2,1)S(1)}, u32[]{:S(2)}) copy-start(bf16[2,2,512,256]{3,2,1,0:T(8,128)(2,1)S(1)} %collective-permute-done.15.refs_4_) | copy-start | bytes 3145732
  317.2 15.1 %collective-permute-start.19 = (bf16[2,2,512,256]{3,2,1,0:T(8,128)(2,1)}, bf16[2,2,512,256]{3,2,1,0:T(8,128)(2,1)S(1)}, u32[]{:S(2)}, u32[]{:S(2)}) collective-permute-start(bf16[2,2,512,256]{3,2,1,0:T(8,128)(2,1)} %add_convert_fusion), channel_id=1, source_target_pairs={{3,2},{6,7},{9,8},{12,13},{19,18},{22,23},{25,24},{28,29}} | collective-permute-start | bytes 3145736 | tf_op jit(solution)/shard_map/ppermute | solution.py:275
  318.1 2.1 copy-start.21
  318.2 14.1 %collective-permute-start.16 = (bf16[2,2,512,256]{3,2,1,0:T(8,128)(2,1)S(1)}, bf16[2,2,512,256]{3,2,1,0:T(8,128)(2,1)S(1)}, u32[]{:S(2)}, u32[]{:S(2)}) collective-permute-start(bf16[2,2,512,256]{3,2,1,0:T(8,128)(2,1)S(1)} %add_convert_fusion.1), channel_id=1, source_target_pairs={{2,3},{5,4},{8,9},{15,14},{18,19},{21,20},{24,25},{31,30}} | collective-permute-start | bytes 3145736 | tf_op jit(solution)/shard_map/ppermute | solution.py:275
  318.9 9.4 %copy-start.16 = (bf16[2,2,512,256]{3,2,1,0:T(8,128)(2,1)}, bf16[2,2,512,256]{3,2,1,0:T(8,128)(2,1)S(1)}, u32[]{:S(2)}) copy-start(bf16[2,2,512,256]{3,2,1,0:T(8,128)(2,1)S(1)} %collective-permute-done.13.refs_2_) | copy-start | bytes 3145732
  318.9 12.0 %collective-permute-start.23 = (bf16[2,2,512,128]{3,2,1,0:T(8,128)(2,1)S(1)}, bf16[2,2,512,128]{3,2,1,0:T(8,128)(2,1)}, u32[]{:S(2)}, u32[]{:S(2)}) collective-permute-start(bf16[2,2,512,128]{3,2,1,0:T(8,128)(2,1)S(1)} %copy-done.11), channel_id=1, source_target_pairs={{0,1},{7,6},{10,11},{13,12},{16,17},{23,22},{26,27},{29,28}} | collective-permute-start | bytes 1572872 | tf_op jit(solution)/shard_map/ppermute | solution.py:275
  328.3 17.3 %collective-permute-start.25 = (bf16[2,2,512,128]{3,2,1,0:T(8,128)(2,1)}, bf16[2,2,512,128]{3,2,1,0:T(8,128)(2,1)S(1)}, u32[]{:S(2)}, u32[]{:S(2)}) collective-permute-start(bf16[2,2,512,128]{3,2,1,0:T(8,128)(2,1)} %second_product.9.refs_13_), channel_id=1, source_target_pairs={{3,1},{4,6},{9,11},{14,12},{19,17},{20,22},{25,27},{30,28}} | collective-permute-start | bytes 1572872 | tf_op jit(solution)/shard_map/ppermute | solution.py:275
  329.6 18.1 %collective-permute-start.26 = (bf16[2,2,512,128]{3,2,1,0:T(8,128)(2,1)}, bf16[2,2,512,128]{3,2,1,0:T(8,128)(2,1)S(1)}, u32[]{:S(2)}, u32[]{:S(2)}) collective-permute-start(bf16[2,2,512,128]{3,2,1,0:T(8,128)(2,1)} %second_product.9.refs_13_), channel_id=1, source_target_pairs={{2,1},{5,6},{8,11},{15,12},{18,17},{21,22},{24,27},{31,28}} | collective-permute-start | bytes 1572872 | tf_op jit(solution)/shard_map/ppermute | solution.py:275
  330.9 16.8 %collective-permute-start.27 = (bf16[2,2,512,128]{3,2,1,0:T(8,128)(2,1)}, bf16[2,2,512,128]{3,2,1,0:T(8,128)(2,1)S(1)}, u32[]{:S(2)}, u32[]{:S(2)}) collective-permute-start(bf16[2,2,512,128]{3,2,1,0:T(8,128)(2,1)} %second_product.9.refs_13_), channel_id=1, source_target_pairs={{0,1},{7,6},{10,11},{13,12},{16,17},{23,22},{26,27},{29,28}} | collective-permute-start | bytes 1572872 | tf_op jit(solution)/shard_map/ppermute | solution.py:275
  332.3 15.5 %copy-start.19 = (bf16[2,2,512,256]{3,2,1,0:T(8,128)(2,1)}, bf16[2,2,512,256]{3,2,1,0:T(8,128)(2,1)S(1)}, u32[]{:S(2)}) copy-start(bf16[2,2,512,256]{3,2,1,0:T(8,128)(2,1)S(1)} %collective-permute-done.19.refs_8_) | copy-start | bytes 3145732
  332.3 15.5 %copy-start.20 = (bf16[2,2,512,256]{3,2,1,0:T(8,128)(2,1)}, bf16[2,2,512,256]{3,2,1,0:T(8,128)(2,1)S(1)}, u32[]{:S(2)}) copy-start(bf16[2,2,512,256]{3,2,1,0:T(8,128)(2,1)S(1)} %collective-permute-done.16.refs_5_) | copy-start | bytes 3145732
  345.6 2.2 copy-start.22
  347.8 0.8 copy-start.23
  348.6 0.8 copy-start.24

commit v5 on v4

--- a/solution.py
+++ b/solution.py
@@ -251,14 +251,14 @@
     site = jnp.where(col == 0, jnp.stack([planar, other]), jnp.stack([other, planar]))
 
     parts = [mine[:, :, : half // 2], mine[:, :, half // 2 :]]
-    travelling = [[shift(after(part, env)) for part, env in zip(parts, envs[-2:])]]
+    travelling = [[shift(after(part, env, site)) for part, env in zip(parts, envs[-2:])]]
     for _ in range(row_count - 2):
         travelling.append([shift(part) for part in travelling[-1]])
 
     blocks = jnp.stack([lax.rem(row - k + row_count, row_count) for k in range(row_count)])
-    blocks = after(blocks.astype(jnp.int32), travelling[0][0])
+    blocks = after(blocks.astype(jnp.int32), *travelling[0])
     q = first_product(blocks, mpo_mine, site, envs, half, half)
-    q = in_order(q, swap(after(q, travelling[0][1])), 4)
+    q = in_order(q, swap(after(q, travelling[1][0])), 4)
 
     pick = jnp.stack([lax.rem(row - col * 2 - depth + row_count, row_count), depth]).astype(jnp.int32)
     steps, gate = [], (q,)

time: 357 us -> 378 us (1.059)
  waiting for transfers between devices: 217 us -> 238 us
    ppermute x12, waiting for transfers between devices: 153 us -> 165 us  [ring(): lax.ppermute(value, 'row', [(r, (r + 1) % row_count) for r in range(row_c...]
    ppermute x12, waiting for transfers between devices: 37.6 us -> 42.8 us  [send(): return lax.ppermute(value, axes, pairs)]
  transfers between devices with their start and end apart: 28 -> 28, of which waited for: 15 -> 16; matrix products, arithmetic and copies ran while one was open for 8% -> 8% of each run, Pallas kernels for 19% -> 18%
where the time goes in v5:
time: 378 us
  waiting for transfers between devices  238 us (63%)
  Pallas kernels  72.7 us (19%)
  starting transfers between devices  29.1 us (8%)
  other arithmetic  24.9 us (7%)
  local copies, waits for them, and re-layouts  12.3 us (3%)
    ppermute x12, waiting for transfers between devices, ring(): lax.ppermute(value, 'row', [(r, (r + 1) % row_count) for r in range(row_c...  165 us
    ppermute x12, waiting for transfers between devices, send(): return lax.ppermute(value, axes, pairs)  42.8 us
    pallas_call x5, Pallas kernels, second_product(): pl.pallas_call(second_kernel, grid=(mpo_count, rows // row_tile), in_spec...  41.9 us
    pallas_call x1, Pallas kernels, first_product(): pl.pallas_call(functools.partial(first_kernel, w_local), grid=(rows // ro...  24.4 us
    ppermute x1, waiting for transfers between devices, ring(): turn = lambda value: lax.ppermute(value, 'col', [(0, 1), (1, 0)])  20.2 us
    ppermute x12, starting transfers between devices, send(): return lax.ppermute(value, axes, pairs)  19.2 us
    select_n x2, other arithmetic, ring(): jnp.where(depth == 0, jnp.concatenate([mine, sibling], axis=axis), jnp.co...  17.2 us
    ppermute x3, waiting for transfers between devices, swap(): return lax.ppermute(value, 'depth', [(0, 1), (1, 0)])  9.89 us
  transfers between devices with their start and end apart: 28, of which 16 were waited for; matrix products, arithmetic and copies ran while one was open for 8% of the time, Pallas kernels for 18%

profile of v5, /device:TPU:1, one launch (start us, length us, event | category | flops | bytes accessed | tf_op | source)
XLA Modules:
  0.0 377.5 jit_solution(4870479059631995132)
XLA Ops:
  0.0 1.7 constant_dynamic-slice_fusion.2
  1.7 0.1 collective-permute-start
  1.9 2.7 collective-permute-start.2
  4.6 2.3 collective-permute-start.1
  6.9 23.3 %collective-permute-done.2.refs_2_ = bf16[1,2,512,512]{3,2,1,0:T(8,128)(2,1)} collective-permute-done((bf16[1,2,512,512]{3,2,1,0:T(8,128)(2,1)S(1)}, bf16[1,2,512,512]{3,2,1,0:T(8,128)(2,1)}, u32[]{:S(2)}, u32[]{:S(2)}) %collective-permute-start.2) | collective-permute-done | bytes 1048608 | tf_op jit(solution)/shard_map/ppermute | solution.py:230
  30.2 22.4 %collective-permute-done.1.refs_3_ = bf16[1,2,512,512]{3,2,1,0:T(8,128)(2,1)S(1)} collective-permute-done((bf16[1,2,512,512]{3,2,1,0:T(8,128)(2,1)S(1)}, bf16[1,2,512,512]{3,2,1,0:T(8,128)(2,1)S(1)}, u32[]{:S(2)}, u32[]{:S(2)}) %collective-permute-start.1) | collective-permute-done | bytes 1048608 | tf_op jit(solution)/shard_map/ppermute | solution.py:230
  52.6 1.0 copy-done.13
  53.6 3.5 copy.8
  57.1 0.0 copy-start
  57.1 2.0 copy-done
  59.1 0.2 dynamic-slice_bitcast_fusion
  59.3 15.8 %collective-permute-done.3.refs_4_ = bf16[1,2,512,512]{3,2,1,0:T(8,128)(2,1)} collective-permute-done((bf16[1,2,512,512]{3,2,1,0:T(8,128)(2,1)}, bf16[1,2,512,512]{3,2,1,0:T(8,128)(2,1)}, u32[]{:S(2)}, u32[]{:S(2)}) %collective-permute-start.3) | collective-permute-done | bytes 1048608 | tf_op jit(solution)/shard_map/ppermute | solution.py:230
  75.2 1.1 collective-permute-start.5
  76.2 25.4 %collective-permute-done.6.refs_5_ = bf16[1,2,512,512]{3,2,1,0:T(8,128)(2,1)S(1)} collective-permute-done((bf16[1,2,512,512]{3,2,1,0:T(8,128)(2,1)S(1)}, bf16[1,2,512,512]{3,2,1,0:T(8,128)(2,1)S(1)}, u32[]{:S(2)}, u32[]{:S(2)}) %collective-permute-start.6) | collective-permute-done | bytes 1048608 | tf_op jit(solution)/shard_map/ppermute | solution.py:230
  101.6 20.2 %collective-permute-done.5 = bf16[2,2,256,1024]{3,2,1,0:T(8,128)(2,1)} collective-permute-done((bf16[2,2,256,1024]{3,2,1,0:T(8,128)(2,1)S(1)}, bf16[2,2,256,1024]{3,2,1,0:T(8,128)(2,1)}, u32[]{:S(2)}, u32[]{:S(2)}) %collective-permute-start.5) | collective-permute-done | bytes 2097184 | tf_op jit(solution)/shard_map/ppermute | solution.py:233
  121.8 1.5 collective-permute-start.7
  123.3 0.2 fusion
  123.5 0.6 collective-permute-start.9
  124.1 3.3 collective-permute-done.7
  127.4 5.6 %maximum_select_fusion.2 = bf16[1,2,2,512,1024]{4,3,2,1,0:T(8,128)(2,1)S(1)} fusion(bf16[1,2,2,256,1024]{4,3,2,1,0:T(8,128)(2,1)} %bitcast.10, bf16[1,2,2,256,1024]{4,3,2,1,0:T(8,128)(2,1)} %bitcast.9, pred[]{:T(512)S(6)} %eq.7), kind=kLoop, calls=%fused_computation.2 | loop fusion | flops 18874368 | bytes 8388609 | tf_op jit(solution)/shard_map/jit(_where)/select_n | solution.py:234
  133.1 4.0 %maximum_select_fusion.site_ref = bf16[2,2,2,512,1024]{4,3,2,1,0:T(8,128)(2,1)} fusion(bf16[1,2,2,512,1024]{4,3,2,1,0:T(8,128)(2,1)S(1)} %maximum_select_fusion.2, bf16[1,2,2,512,1024]{4,3,2,1,0:T(8,128)(2,1)S(1)} %bitcast.15, pred[]{:T(512)S(6)} %eq.8), kind=kLoop, calls=%fused_computation | loop fusion | flops 12582912 | bytes 16777216 | tf_op jit(solution)/shard_map/jit(_where)/select_n | solution.py:251
  137.1 13.0 %collective-permute-done.4.refs_6_ = bf16[1,2,512,512]{3,2,1,0:T(8,128)(2,1)S(1)} collective-permute-done((bf16[1,2,512,512]{3,2,1,0:T(8,128)(2,1)}, bf16[1,2,512,512]{3,2,1,0:T(8,128)(2,1)S(1)}, u32[]{:S(2)}, u32[]{:S(2)}) %collective-permute-start.4) | collective-permute-done | bytes 1048608 | tf_op jit(solution)/shard_map/ppermute | solution.py:230
  150.1 22.5 %collective-permute-done.9.refs_7_ = bf16[1,2,512,512]{3,2,1,0:T(8,128)(2,1)S(1)} collective-permute-done((bf16[1,2,512,512]{3,2,1,0:T(8,128)(2,1)}, bf16[1,2,512,512]{3,2,1,0:T(8,128)(2,1)S(1)}, u32[]{:S(2)}, u32[]{:S(2)}) %collective-permute-start.9) | collective-permute-done | bytes 1048608 | tf_op jit(solution)/shard_map/ppermute | solution.py:230
  172.6 1.0 copy-done.19
  173.6 21.5 %collective-permute-done.8.refs_0_ = bf16[2,2,128,1024]{3,2,1,0:T(8,128)(2,1)S(1)} collective-permute-done((bf16[2,2,128,1024]{3,2,1,0:T(8,128)(2,1)S(1)}, bf16[2,2,128,1024]{3,2,1,0:T(8,128)(2,1)S(1)}, u32[]{:S(2)}, u32[]{:S(2)}) %collective-permute-start.8) | collective-permute-done | bytes 1048608 | tf_op jit(solution)/shard_map/ppermute | solution.py:230
  195.1 0.7 pad_add_fusion.1.block_ref
  195.8 0.6 pad_maximum_fusion.mpo_ref
  196.4 21.2 %collective-permute-done.10.refs_1_ = bf16[2,2,128,1024]{3,2,1,0:T(8,128)(2,1)} collective-permute-done((bf16[2,2,128,1024]{3,2,1,0:T(8,128)(2,1)S(1)}, bf16[2,2,128,1024]{3,2,1,0:T(8,128)(2,1)}, u32[]{:S(2)}, u32[]{:S(2)}) %collective-permute-start.10) | collective-permute-done | bytes 1048608 | tf_op jit(solution)/shard_map/ppermute | solution.py:230
  217.6 24.4 %first_product.1 = bf16[2,2,2,512,512]{4,3,2,1,0:T(8,128)(2,1)} custom-call(s32[4]{0:T(128)} %pad_add_fusion.1.block_ref, f32[2,2,2,2]{3,2,1,0:T(2,128)} %pad_maximum_fusion.mpo_ref, bf16[2,2,2,512,1024]{4,3,2,1,0:T(8,128)(2,1)} %maximum_select_fusion.site_ref, bf16[1,2,512,512]{3,2,1,0:T(8,128)(2,1)} %copy-done.5, bf16[1,2,512,512]{3,2,1,0:T(8,128)(2,1)} %copy-done.12, ...), custom_call_target="tpu_custom_call" | custom-call | tf_op jit(solution)/shard_map/first_product/pallas_call | solution.py:67
  242.0 1.2 collective-permute-start.12
  243.2 0.6 pad_add_fusion.pick_ref
  243.8 6.6 %collective-permute-done.12 = bf16[2,2,2,512,512]{4,3,2,1,0:T(8,128)(2,1)} collective-permute-done((bf16[2,2,2,512,512]{4,3,2,1,0:T(8,128)(2,1)}, bf16[2,2,2,512,512]{4,3,2,1,0:T(8,128)(2,1)}, u32[]{:S(2)}, u32[]{:S(2)}) %collective-permute-start.12) | collective-permute-done | bytes 4194336 | tf_op jit(solution)/shard_map/ppermute | solution.py:171
  250.4 11.5 %maximum_select_fusion.1.q_ref = bf16[2,2,2,512,1024]{4,3,2,1,0:T(8,128)(2,1)} fusion(bf16[2,2,2,512,512]{4,3,2,1,0:T(8,128)(2,1)} %collective-permute-done.12, bf16[2,2,2,512,512]{4,3,2,1,0:T(8,128)(2,1)} %first_product.1, pred[]{:T(512)S(6)} %eq.7), kind=kLoop, calls=%fused_computation.1 | loop fusion | flops 37748736 | bytes 16777216 | tf_op jit(solution)/shard_map/jit(_where)/select_n | solution.py:234
  261.9 8.6 %second_product.5.refs_0_ = bf16[2,2,512,256]{3,2,1,0:T(8,128)(2,1)} custom-call(s32[2]{0:T(128)} %pad_add_fusion.pick_ref, bf16[2,2,2,512,1024]{4,3,2,1,0:T(8,128)(2,1)} %maximum_select_fusion.1.q_ref, bf16[2,2,128,1024]{3,2,1,0:T(8,128)(2,1)} %copy-done.10, bf16[2,2,128,1024]{3,2,1,0:T(8,128)(2,1)} %copy-done.9), custom_call_target="tpu_custom_call" | custom-call | tf_op jit(solution)/shard_map/second_product/pallas_call | solution.py:103
  270.5 1.3 collective-permute-start.13
  271.8 0.2 collective-permute-start.20
  272.0 8.6 %second_product.6.refs_3_ = bf16[2,2,512,256]{3,2,1,0:T(8,128)(2,1)} custom-call(s32[2]{0:T(128)} %pad_add_fusion.pick_ref, bf16[2,2,2,512,1024]{4,3,2,1,0:T(8,128)(2,1)} %maximum_select_fusion.1.q_ref, bf16[2,2,128,1024]{3,2,1,0:T(8,128)(2,1)} %copy-done.16, bf16[2,2,128,1024]{3,2,1,0:T(8,128)(2,1)} %collective-permute-done.10.refs_1_), custom_call_target="tpu_custom_call" | custom-call | tf_op jit(solution)/shard_map/second_product/pallas_call | solution.py:103
  280.7 1.0 copy-done.21
  281.7 8.6 %second_product.7.refs_6_ = bf16[2,2,512,256]{3,2,1,0:T(8,128)(2,1)} custom-call(s32[2]{0:T(128)} %pad_add_fusion.pick_ref, bf16[2,2,2,512,1024]{4,3,2,1,0:T(8,128)(2,1)} %maximum_select_fusion.1.q_ref, bf16[2,2,128,1024]{3,2,1,0:T(8,128)(2,1)} %copy-done.15, bf16[2,2,128,1024]{3,2,1,0:T(8,128)(2,1)} %copy-done.21), custom_call_target="tpu_custom_call" | custom-call | tf_op jit(solution)/shard_map/second_product/pallas_call | solution.py:103
  290.2 4.1 %collective-permute-start.18 = (bf16[2,2,512,256]{3,2,1,0:T(8,128)(2,1)}, bf16[2,2,512,256]{3,2,1,0:T(8,128)(2,1)S(1)}, u32[]{:S(2)}, u32[]{:S(2)}) collective-permute-start(bf16[2,2,512,256]{3,2,1,0:T(8,128)(2,1)} %second_product.7.refs_6_), channel_id=1, source_target_pairs={{0,2},{1,3},{5,7},{4,6},{10,8},{11,9},{15,13},{14,12},{16,18},{17,... | collective-permute-start | bytes 3145736 | tf_op jit(solution)/shard_map/ppermute | solution.py:275
  294.4 1.4 collective-permute-start.15
  295.7 0.1 collective-permute-start.24
  295.8 1.3 collective-permute-done.13.refs_1_
  297.0 1.3 add_convert_fusion.2
  298.4 3.2 collective-permute-start.14
  301.6 8.1 %second_product.8.refs_9_ = bf16[2,2,512,128]{3,2,1,0:T(8,128)(2,1)} custom-call(s32[2]{0:T(128)} %pad_add_fusion.pick_ref, bf16[2,2,2,512,1024]{4,3,2,1,0:T(8,128)(2,1)} %maximum_select_fusion.1.q_ref, bf16[2,2,128,1024]{3,2,1,0:T(8,128)(2,1)} %collective-permute-done.20.refs_0_), custom_call_target="tpu_custom_call" | custom-call | tf_op jit(solution)/shard_map/second_product/pallas_call | solution.py:103
  309.7 1.4 collective-permute-start.21
  311.1 5.3 %collective-permute-done.18.refs_7_ = bf16[2,2,512,256]{3,2,1,0:T(8,128)(2,1)S(1)} collective-permute-done((bf16[2,2,512,256]{3,2,1,0:T(8,128)(2,1)}, bf16[2,2,512,256]{3,2,1,0:T(8,128)(2,1)S(1)}, u32[]{:S(2)}, u32[]{:S(2)}) %collective-permute-start.18) | collective-permute-done | bytes 1048608 | tf_op jit(solution)/shard_map/ppermute | solution.py:275
  316.4 1.3 collective-permute-start.22
  317.7 0.2 add_convert_fusion
  318.0 20.8 %collective-permute-done.15.refs_4_ = bf16[2,2,512,256]{3,2,1,0:T(8,128)(2,1)S(1)} collective-permute-done((bf16[2,2,512,256]{3,2,1,0:T(8,128)(2,1)S(1)}, bf16[2,2,512,256]{3,2,1,0:T(8,128)(2,1)S(1)}, u32[]{:S(2)}, u32[]{:S(2)}) %collective-permute-start.15) | collective-permute-done | bytes 1048608 | tf_op jit(solution)/shard_map/ppermute | solution.py:275
  338.8 0.7 collective-permute-start.19
  339.5 0.2 add_convert_fusion.1
  339.8 0.7 collective-permute-start.16
  340.5 1.3 collective-permute-start.23
  341.8 8.1 %second_product.9.refs_13_ = bf16[2,2,512,128]{3,2,1,0:T(8,128)(2,1)} custom-call(s32[2]{0:T(128)} %pad_add_fusion.pick_ref, bf16[2,2,2,512,1024]{4,3,2,1,0:T(8,128)(2,1)} %maximum_select_fusion.1.q_ref, bf16[2,2,128,1024]{3,2,1,0:T(8,128)(2,1)} %collective-permute-done.24.refs_0_), custom_call_target="tpu_custom_call" | custom-call | tf_op jit(solution)/shard_map/second_product/pallas_call | solution.py:103
  349.9 1.3 collective-permute-start.25
  351.3 1.3 collective-permute-start.26
  352.6 1.3 collective-permute-start.27
  353.9 13.2 %collective-permute-done.25.refs_14_ = bf16[2,2,512,128]{3,2,1,0:T(8,128)(2,1)S(1)} collective-permute-done((bf16[2,2,512,128]{3,2,1,0:T(8,128)(2,1)}, bf16[2,2,512,128]{3,2,1,0:T(8,128)(2,1)S(1)}, u32[]{:S(2)}, u32[]{:S(2)}) %collective-permute-start.25) | collective-permute-done | bytes 524320 | tf_op jit(solution)/shard_map/ppermute | solution.py:275
  367.2 2.1 collective-permute-done.26.refs_15_
  369.3 0.8 copy-done.25
  370.1 0.8 copy-done.26
  370.9 6.5 %finish.1 = f32[2,2,512,512]{3,2,1,0:T(8,128)} custom-call(s32[2]{0:T(128)} %pad_add_fusion.pick_ref, bf16[2,2,512,256]{3,2,1,0:T(8,128)(2,1)} %second_product.5.refs_0_, bf16[2,2,512,256]{3,2,1,0:T(8,128)(2,1)} %copy-done.6, bf16[2,2,512,256]{3,2,1,0:T(8,128)(2,1)} %copy-done.20, bf16[2,2,512,256]{3,2,1,0:T(8,128)(2,1)} %second_product.6.refs_3_, ...), custom_call_target="tpu_custom_call" | custom-call | tf_op jit(solution)/shard_map/finish/pallas_call | solution.py:152
  (69 shorter events, 0.1 us)
Async XLA Ops:
  1.7 55.4 %copy-start.5 = (bf16[1,2,512,512]{3,2,1,0:T(8,128)(2,1)}, bf16[1,2,512,512]{3,2,1,0:T(8,128)(2,1)S(1)}, u32[]{:S(2)}) copy-start(bf16[1,2,512,512]{3,2,1,0:T(8,128)(2,1)S(1)} %get-tuple-element.33.refs_0_) | copy-start | bytes 3145732
  1.7 2.9 collective-permute-start
  1.9 28.3 %collective-permute-start.2 = (bf16[1,2,512,512]{3,2,1,0:T(8,128)(2,1)S(1)}, bf16[1,2,512,512]{3,2,1,0:T(8,128)(2,1)}, u32[]{:S(2)}, u32[]{:S(2)}) collective-permute-start(bf16[1,2,512,512]{3,2,1,0:T(8,128)(2,1)S(1)} %get-tuple-element.33.refs_0_), channel_id=1, source_target_pairs={{0,4},{4,8},{8,12},{12,0},{1,5},{5,9},{9,13},{13,1},{2,6},{6,10},{... | collective-permute-start | bytes 3145736 | tf_op jit(solution)/shard_map/ppermute | solution.py:230
  4.6 48.0 %copy-start.12 = (bf16[1,2,512,512]{3,2,1,0:T(8,128)(2,1)}, bf16[1,2,512,512]{3,2,1,0:T(8,128)(2,1)S(1)}, u32[]{:S(2)}) copy-start(bf16[1,2,512,512]{3,2,1,0:T(8,128)(2,1)S(1)} %collective-permute-done.refs_1_) | copy-start | bytes 3145732
  4.6 48.0 %collective-permute-start.1 = (bf16[1,2,512,512]{3,2,1,0:T(8,128)(2,1)S(1)}, bf16[1,2,512,512]{3,2,1,0:T(8,128)(2,1)S(1)}, u32[]{:S(2)}, u32[]{:S(2)}) collective-permute-start(bf16[1,2,512,512]{3,2,1,0:T(8,128)(2,1)S(1)} %collective-permute-done.refs_1_), channel_id=1, source_target_pairs={{0,4},{4,8},{8,12},{12,0},{1,5},{5,9},{9,13},{13,1},{2,6},{6,10},{... | collective-permute-start | bytes 3145736 | tf_op jit(solution)/shard_map/ppermute | solution.py:230
  30.2 44.9 %collective-permute-start.3 = (bf16[1,2,512,512]{3,2,1,0:T(8,128)(2,1)}, bf16[1,2,512,512]{3,2,1,0:T(8,128)(2,1)}, u32[]{:S(2)}, u32[]{:S(2)}) collective-permute-start(bf16[1,2,512,512]{3,2,1,0:T(8,128)(2,1)} %collective-permute-done.2.refs_2_), channel_id=1, source_target_pairs={{0,4},{4,8},{8,12},{12,0},{1,5},{5,9},{9,13},{13,1},{2,6},{6,10},{... | collective-permute-start | bytes 3145736 | tf_op jit(solution)/shard_map/ppermute | solution.py:230
  52.6 1.0 copy-start.13
  57.1 2.0 copy-start
  59.1 17.1 %copy-start.14 = (bf16[1,2,512,512]{3,2,1,0:T(8,128)(2,1)S(1)}, bf16[1,2,512,512]{3,2,1,0:T(8,128)(2,1)}, u32[]{:S(2)}) copy-start(bf16[1,2,512,512]{3,2,1,0:T(8,128)(2,1)} %copy-done.13) | copy-start | bytes 3145732
  75.2 46.6 %collective-permute-start.5 = (bf16[2,2,256,1024]{3,2,1,0:T(8,128)(2,1)S(1)}, bf16[2,2,256,1024]{3,2,1,0:T(8,128)(2,1)}, u32[]{:S(2)}, u32[]{:S(2)}) collective-permute-start(bf16[2,2,256,1024]{3,2,1,0:T(8,128)(2,1)S(1)} %dynamic-slice_bitcast_fusion), channel_id=1, source_target_pairs={{0,2},{2,0},{1,3},{3,1},{4,6},{6,4},{5,7},{7,5},{8,10},{10,8},{9,1... | collective-permute-start | bytes 6291464 | tf_op jit(solution)/shard_map/ppermute | solution.py:233
  76.2 25.4 %collective-permute-start.6 = (bf16[1,2,512,512]{3,2,1,0:T(8,128)(2,1)S(1)}, bf16[1,2,512,512]{3,2,1,0:T(8,128)(2,1)S(1)}, u32[]{:S(2)}, u32[]{:S(2)}) collective-permute-start(bf16[1,2,512,512]{3,2,1,0:T(8,128)(2,1)S(1)} %copy-done.14), channel_id=1, source_target_pairs={{0,4},{4,8},{8,12},{12,0},{1,5},{5,9},{9,13},{13,1},{2,6},{6,10},{... | collective-permute-start | bytes 3145736 | tf_op jit(solution)/shard_map/ppermute | solution.py:230
  101.6 20.2 %copy-start.17 = (bf16[1,2,512,512]{3,2,1,0:T(8,128)(2,1)}, bf16[1,2,512,512]{3,2,1,0:T(8,128)(2,1)S(1)}, u32[]{:S(2)}) copy-start(bf16[1,2,512,512]{3,2,1,0:T(8,128)(2,1)S(1)} %collective-permute-done.6.refs_5_) | copy-start | bytes 3145732
  121.8 5.6 %collective-permute-start.7 = (bf16[2,2,256,1024]{3,2,1,0:T(8,128)(2,1)}, bf16[2,2,256,1024]{3,2,1,0:T(8,128)(2,1)}, u32[]{:S(2)}, u32[]{:S(2)}) collective-permute-start(bf16[2,2,256,1024]{3,2,1,0:T(8,128)(2,1)} %collective-permute-done.5), channel_id=1, source_target_pairs={{0,1},{1,0},{2,3},{3,2},{4,5},{5,4},{6,7},{7,6},{8,9},{9,8},{10,11... | collective-permute-start | bytes 6291464 | tf_op jit(solution)/shard_map/ppermute | solution.py:171
  123.3 26.8 %collective-permute-start.4 = (bf16[1,2,512,512]{3,2,1,0:T(8,128)(2,1)}, bf16[1,2,512,512]{3,2,1,0:T(8,128)(2,1)S(1)}, u32[]{:S(2)}, u32[]{:S(2)}) collective-permute-start(bf16[1,2,512,512]{3,2,1,0:T(8,128)(2,1)} %collective-permute-done.3.refs_4_), channel_id=1, source_target_pairs={{0,4},{4,8},{8,12},{12,0},{1,5},{5,9},{9,13},{13,1},{2,6},{6,10},{... | collective-permute-start | bytes 3145736 | tf_op jit(solution)/shard_map/ppermute | solution.py:230
  123.5 26.6 %copy-start.10 = (bf16[2,2,128,1024]{3,2,1,0:T(8,128)(2,1)}, bf16[2,2,128,1024]{3,2,1,0:T(8,128)(2,1)S(1)}, u32[]{:S(2)}) copy-start(bf16[2,2,128,1024]{3,2,1,0:T(8,128)(2,1)S(1)} %get-tuple-element.20.refs_0_) | copy-start | bytes 3145732
  123.5 49.1 %copy-start.9 = (bf16[2,2,128,1024]{3,2,1,0:T(8,128)(2,1)}, bf16[2,2,128,1024]{3,2,1,0:T(8,128)(2,1)S(1)}, u32[]{:S(2)}) copy-start(bf16[2,2,128,1024]{3,2,1,0:T(8,128)(2,1)S(1)} %get-tuple-element.21.refs_1_) | copy-start | bytes 3145732
  123.5 49.0 %collective-permute-start.9 = (bf16[1,2,512,512]{3,2,1,0:T(8,128)(2,1)}, bf16[1,2,512,512]{3,2,1,0:T(8,128)(2,1)S(1)}, u32[]{:S(2)}, u32[]{:S(2)}) collective-permute-start(bf16[1,2,512,512]{3,2,1,0:T(8,128)(2,1)} %copy-done.17), channel_id=1, source_target_pairs={{0,4},{4,8},{8,12},{12,0},{1,5},{5,9},{9,13},{13,1},{2,6},{6,10},{... | collective-permute-start | bytes 3145736 | tf_op jit(solution)/shard_map/ppermute | solution.py:230
  127.4 5.6 %copy-start.1 = (bf16[2,512,2,1024]{3,1,2,0:T(8,128)(2,1)S(1)}, bf16[2,512,2,1024]{3,1,2,0:T(8,128)(2,1)}, u32[]{:S(2)}) copy-start(bf16[2,512,2,1024]{3,1,2,0:T(8,128)(2,1)} %copy-done) | copy-start | bytes 12582916
  133.1 62.7 %copy-start.27 = (f32[2,2,2,2]{3,2,1,0:T(2,128)S(1)}, f32[2,2,2,2]{3,2,1,0:T(2,128)}, u32[]{:S(2)}) copy-start(f32[2,2,2,2]{3,2,1,0:T(2,128)} %param.5) | copy-start | bytes 196
  150.1 44.9 %copy-start.18 = (bf16[1,2,512,512]{3,2,1,0:T(8,128)(2,1)}, bf16[1,2,512,512]{3,2,1,0:T(8,128)(2,1)S(1)}, u32[]{:S(2)}) copy-start(bf16[1,2,512,512]{3,2,1,0:T(8,128)(2,1)S(1)} %collective-permute-done.4.refs_6_) | copy-start | bytes 3145732
  150.1 44.9 %collective-permute-start.8 = (bf16[2,2,128,1024]{3,2,1,0:T(8,128)(2,1)S(1)}, bf16[2,2,128,1024]{3,2,1,0:T(8,128)(2,1)S(1)}, u32[]{:S(2)}, u32[]{:S(2)}) collective-permute-start(bf16[2,2,128,1024]{3,2,1,0:T(8,128)(2,1)S(1)} %get-tuple-element.20.refs_0_), channel_id=1, source_target_pairs={{0,4},{4,8},{8,12},{12,0},{1,5},{5,9},{9,13},{13,1},{2,6},{6,10},{... | collective-permute-start | bytes 3145736 | tf_op jit(solution)/shard_map/ppermute | solution.py:230
  172.6 1.0 copy-start.19
  172.6 45.0 %collective-permute-start.10 = (bf16[2,2,128,1024]{3,2,1,0:T(8,128)(2,1)S(1)}, bf16[2,2,128,1024]{3,2,1,0:T(8,128)(2,1)}, u32[]{:S(2)}, u32[]{:S(2)}) collective-permute-start(bf16[2,2,128,1024]{3,2,1,0:T(8,128)(2,1)S(1)} %get-tuple-element.21.refs_1_), channel_id=1, source_target_pairs={{0,4},{4,8},{8,12},{12,0},{1,5},{5,9},{9,13},{13,1},{2,6},{6,10},{... | collective-permute-start | bytes 3145736 | tf_op jit(solution)/shard_map/ppermute | solution.py:230
  195.0 46.9 %copy-start.16 = (bf16[2,2,128,1024]{3,2,1,0:T(8,128)(2,1)}, bf16[2,2,128,1024]{3,2,1,0:T(8,128)(2,1)S(1)}, u32[]{:S(2)}) copy-start(bf16[2,2,128,1024]{3,2,1,0:T(8,128)(2,1)S(1)} %collective-permute-done.8.refs_0_) | copy-start | bytes 3145732
  195.0 46.9 %collective-permute-start.11 = (bf16[2,2,128,1024]{3,2,1,0:T(8,128)(2,1)S(1)}, bf16[2,2,128,1024]{3,2,1,0:T(8,128)(2,1)S(1)}, u32[]{:S(2)}, u32[]{:S(2)}) collective-permute-start(bf16[2,2,128,1024]{3,2,1,0:T(8,128)(2,1)S(1)} %collective-permute-done.8.refs_0_), channel_id=1, source_target_pairs={{0,4},{4,8},{8,12},{12,0},{1,5},{5,9},{9,13},{13,1},{2,6},{6,10},{... | collective-permute-start | bytes 3145736 | tf_op jit(solution)/shard_map/ppermute | solution.py:230
  242.0 29.8 %copy-start.15 = (bf16[2,2,128,1024]{3,2,1,0:T(8,128)(2,1)}, bf16[2,2,128,1024]{3,2,1,0:T(8,128)(2,1)S(1)}, u32[]{:S(2)}) copy-start(bf16[2,2,128,1024]{3,2,1,0:T(8,128)(2,1)S(1)} %collective-permute-done.11.refs_0_) | copy-start | bytes 3145732
  242.0 8.4 %collective-permute-start.12 = (bf16[2,2,2,512,512]{4,3,2,1,0:T(8,128)(2,1)}, bf16[2,2,2,512,512]{4,3,2,1,0:T(8,128)(2,1)}, u32[]{:S(2)}, u32[]{:S(2)}) collective-permute-start(bf16[2,2,2,512,512]{4,3,2,1,0:T(8,128)(2,1)} %first_product.1), channel_id=1, source_target_pairs={{0,1},{1,0},{2,3},{3,2},{4,5},{5,4},{6,7},{7,6},{8,9},{9,8},{10,11... | collective-permute-start | bytes 12582920 | tf_op jit(solution)/shard_map/ppermute | solution.py:171
  243.8 36.8 %collective-permute-start.17 = (bf16[2,2,128,1024]{3,2,1,0:T(8,128)(2,1)}, bf16[2,2,128,1024]{3,2,1,0:T(8,128)(2,1)S(1)}, u32[]{:S(2)}, u32[]{:S(2)}) collective-permute-start(bf16[2,2,128,1024]{3,2,1,0:T(8,128)(2,1)} %collective-permute-done.10.refs_1_), channel_id=1, source_target_pairs={{0,4},{4,8},{8,12},{12,0},{1,5},{5,9},{9,13},{13,1},{2,6},{6,10},{... | collective-permute-start | bytes 3145736 | tf_op jit(solution)/shard_map/ppermute | solution.py:230
  270.5 26.6 %collective-permute-start.13 = (bf16[2,2,512,256]{3,2,1,0:T(8,128)(2,1)}, bf16[2,2,512,256]{3,2,1,0:T(8,128)(2,1)S(1)}, u32[]{:S(2)}, u32[]{:S(2)}) collective-permute-start(bf16[2,2,512,256]{3,2,1,0:T(8,128)(2,1)} %second_product.5.refs_0_), channel_id=1, source_target_pairs={{2,0},{3,1},{7,5},{6,4},{8,10},{9,11},{13,15},{12,14},{18,16},{19,... | collective-permute-start | bytes 3145736 | tf_op jit(solution)/shard_map/ppermute | solution.py:275
  271.8 29.8 %collective-permute-start.20 = (bf16[2,2,128,1024]{3,2,1,0:T(8,128)(2,1)S(1)}, bf16[2,2,128,1024]{3,2,1,0:T(8,128)(2,1)}, u32[]{:S(2)}, u32[]{:S(2)}) collective-permute-start(bf16[2,2,128,1024]{3,2,1,0:T(8,128)(2,1)S(1)} %collective-permute-done.11.refs_0_), channel_id=1, source_target_pairs={{0,4},{4,8},{8,12},{12,0},{1,5},{5,9},{9,13},{13,1},{2,6},{6,10},{... | collective-permute-start | bytes 3145736 | tf_op jit(solution)/shard_map/ppermute | solution.py:230
  280.6 13.7 %copy-start.3 = (bf16[2,2,512,256]{3,2,1,0:T(8,128)(2,1)S(1)}, bf16[2,2,512,256]{3,2,1,0:T(8,128)(2,1)}, u32[]{:S(2)}) copy-start(bf16[2,2,512,256]{3,2,1,0:T(8,128)(2,1)} %second_product.6.refs_3_) | copy-start | bytes 3145732
  280.6 16.4 %copy-start.2 = (bf16[2,2,512,256]{3,2,1,0:T(8,128)(2,1)S(1)}, bf16[2,2,512,256]{3,2,1,0:T(8,128)(2,1)}, u32[]{:S(2)}) copy-start(bf16[2,2,512,256]{3,2,1,0:T(8,128)(2,1)} %second_product.5.refs_0_) | copy-start | bytes 3145732
  280.6 1.0 copy-start.21
  290.2 26.2 %collective-permute-start.18 = (bf16[2,2,512,256]{3,2,1,0:T(8,128)(2,1)}, bf16[2,2,512,256]{3,2,1,0:T(8,128)(2,1)S(1)}, u32[]{:S(2)}, u32[]{:S(2)}) collective-permute-start(bf16[2,2,512,256]{3,2,1,0:T(8,128)(2,1)} %second_product.7.refs_6_), channel_id=1, source_target_pairs={{0,2},{1,3},{5,7},{4,6},{10,8},{11,9},{15,13},{14,12},{16,18},{17,... | collective-permute-start | bytes 3145736 | tf_op jit(solution)/shard_map/ppermute | solution.py:275
  294.4 44.4 %collective-permute-start.15 = (bf16[2,2,512,256]{3,2,1,0:T(8,128)(2,1)S(1)}, bf16[2,2,512,256]{3,2,1,0:T(8,128)(2,1)S(1)}, u32[]{:S(2)}, u32[]{:S(2)}) collective-permute-start(bf16[2,2,512,256]{3,2,1,0:T(8,128)(2,1)S(1)} %copy-done.3), channel_id=1, source_target_pairs={{1,3},{0,2},{6,4},{7,5},{11,9},{10,8},{12,14},{13,15},{17,19},{16,... | collective-permute-start | bytes 3145736 | tf_op jit(solution)/shard_map/ppermute | solution.py:275
  295.7 44.1 %collective-permute-start.24 = (bf16[2,2,128,1024]{3,2,1,0:T(8,128)(2,1)}, bf16[2,2,128,1024]{3,2,1,0:T(8,128)(2,1)}, u32[]{:S(2)}, u32[]{:S(2)}) collective-permute-start(bf16[2,2,128,1024]{3,2,1,0:T(8,128)(2,1)} %copy-done.21), channel_id=1, source_target_pairs={{0,4},{4,8},{8,12},{12,0},{1,5},{5,9},{9,13},{13,1},{2,6},{6,10},{... | collective-permute-start | bytes 3145736 | tf_op jit(solution)/shard_map/ppermute | solution.py:230
  297.0 12.6 %copy-start.6 = (bf16[2,2,512,256]{3,2,1,0:T(8,128)(2,1)}, bf16[2,2,512,256]{3,2,1,0:T(8,128)(2,1)S(1)}, u32[]{:S(2)}) copy-start(bf16[2,2,512,256]{3,2,1,0:T(8,128)(2,1)S(1)} %collective-permute-done.13.refs_1_) | copy-start | bytes 3145732
  298.4 19.4 %copy-start.4 = (bf16[2,2,512,256]{3,2,1,0:T(8,128)(2,1)S(1)}, bf16[2,2,512,256]{3,2,1,0:T(8,128)(2,1)}, u32[]{:S(2)}) copy-start(bf16[2,2,512,256]{3,2,1,0:T(8,128)(2,1)} %second_product.7.refs_6_) | copy-start | bytes 3145732
  298.4 42.2 %collective-permute-start.14 = (bf16[2,2,512,256]{3,2,1,0:T(8,128)(2,1)}, bf16[2,2,512,256]{3,2,1,0:T(8,128)(2,1)S(1)}, u32[]{:S(2)}, u32[]{:S(2)}) collective-permute-start(bf16[2,2,512,256]{3,2,1,0:T(8,128)(2,1)} %add_convert_fusion.2), channel_id=1, source_target_pairs={{1,0},{4,5},{11,10},{14,15},{17,16},{20,21},{27,26},{30,31}} | collective-permute-start | bytes 3145736 | tf_op jit(solution)/shard_map/ppermute | solution.py:275
  309.7 30.9 %copy-start.11 = (bf16[2,2,512,128]{3,2,1,0:T(8,128)(2,1)S(1)}, bf16[2,2,512,128]{3,2,1,0:T(8,128)(2,1)}, u32[]{:S(2)}) copy-start(bf16[2,2,512,128]{3,2,1,0:T(8,128)(2,1)} %second_product.8.refs_9_) | copy-start | bytes 1572868
  309.7 40.3 %collective-permute-start.21 = (bf16[2,2,512,128]{3,2,1,0:T(8,128)(2,1)}, bf16[2,2,512,128]{3,2,1,0:T(8,128)(2,1)}, u32[]{:S(2)}, u32[]{:S(2)}) collective-permute-start(bf16[2,2,512,128]{3,2,1,0:T(8,128)(2,1)} %second_product.8.refs_9_), channel_id=1, source_target_pairs={{3,1},{4,6},{9,11},{14,12},{19,17},{20,22},{25,27},{30,28}} | collective-permute-start | bytes 1572872 | tf_op jit(solution)/shard_map/ppermute | solution.py:275
  316.4 33.5 %copy-start.7 = (bf16[2,2,512,256]{3,2,1,0:T(8,128)(2,1)}, bf16[2,2,512,256]{3,2,1,0:T(8,128)(2,1)S(1)}, u32[]{:S(2)}) copy-start(bf16[2,2,512,256]{3,2,1,0:T(8,128)(2,1)S(1)} %collective-permute-done.18.refs_7_) | copy-start | bytes 3145732
  316.4 34.8 %collective-permute-start.22 = (bf16[2,2,512,128]{3,2,1,0:T(8,128)(2,1)}, bf16[2,2,512,128]{3,2,1,0:T(8,128)(2,1)}, u32[]{:S(2)}, u32[]{:S(2)}) collective-permute-start(bf16[2,2,512,128]{3,2,1,0:T(8,128)(2,1)} %second_product.8.refs_9_), channel_id=1, source_target_pairs={{2,1},{5,6},{8,11},{15,12},{18,17},{21,22},{24,27},{31,28}} | collective-permute-start | bytes 1572872 | tf_op jit(solution)/shard_map/ppermute | solution.py:275
  338.8 11.1 %copy-start.8 = (bf16[2,2,512,256]{3,2,1,0:T(8,128)(2,1)}, bf16[2,2,512,256]{3,2,1,0:T(8,128)(2,1)S(1)}, u32[]{:S(2)}) copy-start(bf16[2,2,512,256]{3,2,1,0:T(8,128)(2,1)S(1)} %collective-permute-done.15.refs_4_) | copy-start | bytes 3145732
  338.8 15.1 %collective-permute-start.19 = (bf16[2,2,512,256]{3,2,1,0:T(8,128)(2,1)S(1)}, bf16[2,2,512,256]{3,2,1,0:T(8,128)(2,1)S(1)}, u32[]{:S(2)}, u32[]{:S(2)}) collective-permute-start(bf16[2,2,512,256]{3,2,1,0:T(8,128)(2,1)S(1)} %add_convert_fusion), channel_id=1, source_target_pairs={{3,2},{6,7},{9,8},{12,13},{19,18},{22,23},{25,24},{28,29}} | collective-permute-start | bytes 3145736 | tf_op jit(solution)/shard_map/ppermute | solution.py:275
  339.8 14.1 %collective-permute-start.16 = (bf16[2,2,512,256]{3,2,1,0:T(8,128)(2,1)S(1)}, bf16[2,2,512,256]{3,2,1,0:T(8,128)(2,1)S(1)}, u32[]{:S(2)}, u32[]{:S(2)}) collective-permute-start(bf16[2,2,512,256]{3,2,1,0:T(8,128)(2,1)S(1)} %add_convert_fusion.1), channel_id=1, source_target_pairs={{2,3},{5,4},{8,9},{15,14},{18,19},{21,20},{24,25},{31,30}} | collective-permute-start | bytes 3145736 | tf_op jit(solution)/shard_map/ppermute | solution.py:275
  340.5 9.4 %copy-start.20 = (bf16[2,2,512,256]{3,2,1,0:T(8,128)(2,1)}, bf16[2,2,512,256]{3,2,1,0:T(8,128)(2,1)S(1)}, u32[]{:S(2)}) copy-start(bf16[2,2,512,256]{3,2,1,0:T(8,128)(2,1)S(1)} %collective-permute-done.14.refs_2_) | copy-start | bytes 3145732
  340.5 12.0 %collective-permute-start.23 = (bf16[2,2,512,128]{3,2,1,0:T(8,128)(2,1)S(1)}, bf16[2,2,512,128]{3,2,1,0:T(8,128)(2,1)}, u32[]{:S(2)}, u32[]{:S(2)}) collective-permute-start(bf16[2,2,512,128]{3,2,1,0:T(8,128)(2,1)S(1)} %copy-done.11), channel_id=1, source_target_pairs={{0,1},{7,6},{10,11},{13,12},{16,17},{23,22},{26,27},{29,28}} | collective-permute-start | bytes 1572872 | tf_op jit(solution)/shard_map/ppermute | solution.py:275
  349.9 17.2 %collective-permute-start.25 = (bf16[2,2,512,128]{3,2,1,0:T(8,128)(2,1)}, bf16[2,2,512,128]{3,2,1,0:T(8,128)(2,1)S(1)}, u32[]{:S(2)}, u32[]{:S(2)}) collective-permute-start(bf16[2,2,512,128]{3,2,1,0:T(8,128)(2,1)} %second_product.9.refs_13_), channel_id=1, source_target_pairs={{3,1},{4,6},{9,11},{14,12},{19,17},{20,22},{25,27},{30,28}} | collective-permute-start | bytes 1572872 | tf_op jit(solution)/shard_map/ppermute | solution.py:275
  351.3 18.1 %collective-permute-start.26 = (bf16[2,2,512,128]{3,2,1,0:T(8,128)(2,1)}, bf16[2,2,512,128]{3,2,1,0:T(8,128)(2,1)S(1)}, u32[]{:S(2)}, u32[]{:S(2)}) collective-permute-start(bf16[2,2,512,128]{3,2,1,0:T(8,128)(2,1)} %second_product.9.refs_13_), channel_id=1, source_target_pairs={{2,1},{5,6},{8,11},{15,12},{18,17},{21,22},{24,27},{31,28}} | collective-permute-start | bytes 1572872 | tf_op jit(solution)/shard_map/ppermute | solution.py:275
  352.6 16.7 %collective-permute-start.27 = (bf16[2,2,512,128]{3,2,1,0:T(8,128)(2,1)}, bf16[2,2,512,128]{3,2,1,0:T(8,128)(2,1)S(1)}, u32[]{:S(2)}, u32[]{:S(2)}) collective-permute-start(bf16[2,2,512,128]{3,2,1,0:T(8,128)(2,1)} %second_product.9.refs_13_), channel_id=1, source_target_pairs={{0,1},{7,6},{10,11},{13,12},{16,17},{23,22},{26,27},{29,28}} | collective-permute-start | bytes 1572872 | tf_op jit(solution)/shard_map/ppermute | solution.py:275
  353.9 15.4 %copy-start.22 = (bf16[2,2,512,256]{3,2,1,0:T(8,128)(2,1)}, bf16[2,2,512,256]{3,2,1,0:T(8,128)(2,1)S(1)}, u32[]{:S(2)}) copy-start(bf16[2,2,512,256]{3,2,1,0:T(8,128)(2,1)S(1)} %collective-permute-done.19.refs_8_) | copy-start | bytes 3145732
  353.9 15.4 %copy-start.23 = (bf16[2,2,512,256]{3,2,1,0:T(8,128)(2,1)}, bf16[2,2,512,256]{3,2,1,0:T(8,128)(2,1)S(1)}, u32[]{:S(2)}) copy-start(bf16[2,2,512,256]{3,2,1,0:T(8,128)(2,1)S(1)} %collective-permute-done.16.refs_5_) | copy-start | bytes 3145732
  367.2 2.2 copy-start.24
  369.3 0.8 copy-start.25
  370.1 0.8 copy-start.26

commit v6 on v5

--- a/solution.py
+++ b/solution.py
@@ -242,12 +242,12 @@
     for _ in range(row_count - 1):
         envs += [shift(envs[-2]), shift(envs[-1])]
 
-    planar = jnp.transpose(after(site_tensor, envs[3]), (0, 2, 1, 3))
+    planar = jnp.transpose(after(site_tensor, env_sib), (0, 2, 1, 3))
     rows = planar.shape[2]
     half = rows // 2
     mine = lax.dynamic_slice_in_dim(planar, depth * half, half, 2)
-    other = turn(after(mine, envs[4]))
-    other = in_order(other, swap(after(other, envs[5])), 2)
+    other = turn(mine)
+    other = in_order(other, swap(after(other, envs[4], envs[5])), 2)
     site = jnp.where(col == 0, jnp.stack([planar, other]), jnp.stack([other, planar]))
 
     parts = [mine[:, :, : half // 2], mine[:, :, half // 2 :]]

time: 378 us -> 354 us (0.937)
  waiting for transfers between devices: 238 us -> 213 us
    ppermute x1, waiting for transfers between devices: 20.2 us -> 0.01 us  [ring(): turn = lambda value: lax.ppermute(value, 'col', [(0, 1), (1, 0)])]
    ppermute x12, waiting for transfers between devices: 165 us -> 161 us  [ring(): lax.ppermute(value, 'row', [(r, (r + 1) % row_count) for r in range(row_c...]
    unnamed x56 -> x60, local copies, waits for them, and re-layouts: 6.69 us -> 7.66 us
  transfers between devices with their start and end apart: 28 -> 28, of which waited for: 16 -> 15; matrix products, arithmetic and copies ran while one was open for 8% -> 8% of each run, Pallas kernels for 18% -> 19%
where the time goes in v6:
time: 354 us
  waiting for transfers between devices  213 us (60%)
  Pallas kernels  72.7 us (21%)
  starting transfers between devices  28.6 us (8%)
  other arithmetic  25.9 us (7%)
  local copies, waits for them, and re-layouts  13.2 us (4%)
    ppermute x12, waiting for transfers between devices, ring(): lax.ppermute(value, 'row', [(r, (r + 1) % row_count) for r in range(row_c...  161 us
    pallas_call x5, Pallas kernels, second_product(): pl.pallas_call(second_kernel, grid=(mpo_count, rows // row_tile), in_spec...  41.9 us
    ppermute x12, waiting for transfers between devices, send(): return lax.ppermute(value, axes, pairs)  41.9 us
    pallas_call x1, Pallas kernels, first_product(): pl.pallas_call(functools.partial(first_kernel, w_local), grid=(rows // ro...  24.4 us
    ppermute x12, starting transfers between devices, send(): return lax.ppermute(value, axes, pairs)  19.2 us
    select_n x2, other arithmetic, ring(): jnp.where(depth == 0, jnp.concatenate([mine, sibling], axis=axis), jnp.co...  17.1 us
    ppermute x3, waiting for transfers between devices, swap(): return lax.ppermute(value, 'depth', [(0, 1), (1, 0)])  9.64 us
    unnamed x60, local copies, waits for them, and re-layouts  7.66 us
  transfers between devices with their start and end apart: 28, of which 15 were waited for; matrix products, arithmetic and copies ran while one was open for 8% of the time, Pallas kernels for 19%

profile of v6, /device:TPU:1, one launch (start us, length us, event | category | flops | bytes accessed | tf_op | source)
XLA Modules:
  0.0 353.6 jit_solution(17493063729997896244)
XLA Ops:
  0.0 1.7 constant_dynamic-slice_fusion.2
  1.7 0.1 collective-permute-start
  1.8 2.7 collective-permute-start.1
  4.6 1.0 copy-done.12
  5.5 3.5 copy.8
  9.1 2.0 copy-done
  11.1 0.2 dynamic-slice_bitcast_fusion
  11.3 1.0 copy-done.13
  12.3 2.3 collective-permute-start.5
  14.6 1.2 collective-permute-start.4
  15.8 14.4 %collective-permute-done.1.refs_2_ = bf16[1,2,512,512]{3,2,1,0:T(8,128)(2,1)} collective-permute-done((bf16[1,2,512,512]{3,2,1,0:T(8,128)(2,1)S(1)}, bf16[1,2,512,512]{3,2,1,0:T(8,128)(2,1)}, u32[]{:S(2)}, u32[]{:S(2)}) %collective-permute-start.1) | collective-permute-done | bytes 1048608 | tf_op jit(solution)/shard_map/ppermute | solution.py:230
  30.2 22.4 %collective-permute-done.5.refs_3_ = bf16[1,2,512,512]{3,2,1,0:T(8,128)(2,1)S(1)} collective-permute-done((bf16[1,2,512,512]{3,2,1,0:T(8,128)(2,1)S(1)}, bf16[1,2,512,512]{3,2,1,0:T(8,128)(2,1)S(1)}, u32[]{:S(2)}, u32[]{:S(2)}) %collective-permute-start.5) | collective-permute-done | bytes 1048608 | tf_op jit(solution)/shard_map/ppermute | solution.py:230
  52.5 22.5 %collective-permute-done.2.refs_4_ = bf16[1,2,512,512]{3,2,1,0:T(8,128)(2,1)S(1)} collective-permute-done((bf16[1,2,512,512]{3,2,1,0:T(8,128)(2,1)}, bf16[1,2,512,512]{3,2,1,0:T(8,128)(2,1)S(1)}, u32[]{:S(2)}, u32[]{:S(2)}) %collective-permute-start.2) | collective-permute-done | bytes 1048608 | tf_op jit(solution)/shard_map/ppermute | solution.py:230
  75.0 22.5 %collective-permute-done.6.refs_5_ = bf16[1,2,512,512]{3,2,1,0:T(8,128)(2,1)S(1)} collective-permute-done((bf16[1,2,512,512]{3,2,1,0:T(8,128)(2,1)S(1)}, bf16[1,2,512,512]{3,2,1,0:T(8,128)(2,1)S(1)}, u32[]{:S(2)}, u32[]{:S(2)}) %collective-permute-start.6) | collective-permute-done | bytes 1048608 | tf_op jit(solution)/shard_map/ppermute | solution.py:230
  97.5 1.0 copy-done.17
  98.4 0.6 collective-permute-start.7
  99.1 0.2 fusion
  99.3 0.1 collective-permute-start.3
  99.4 0.7 collective-permute-start.9
  100.1 3.1 collective-permute-done.7
  103.2 5.6 %maximum_select_fusion.2 = bf16[1,2,2,512,1024]{4,3,2,1,0:T(8,128)(2,1)S(1)} fusion(bf16[1,2,2,256,1024]{4,3,2,1,0:T(8,128)(2,1)} %bitcast.10, bf16[1,2,2,256,1024]{4,3,2,1,0:T(8,128)(2,1)} %bitcast.9, pred[]{:T(512)S(6)} %eq.7), kind=kLoop, calls=%fused_computation.2 | loop fusion | flops 18874368 | bytes 8388609 | tf_op jit(solution)/shard_map/jit(_where)/select_n | solution.py:234
  108.9 4.1 %maximum_select_fusion.site_ref = bf16[2,2,2,512,1024]{4,3,2,1,0:T(8,128)(2,1)} fusion(bf16[1,2,2,512,1024]{4,3,2,1,0:T(8,128)(2,1)S(1)} %maximum_select_fusion.2, bf16[1,2,2,512,1024]{4,3,2,1,0:T(8,128)(2,1)S(1)} %bitcast.15, pred[]{:T(512)S(6)} %eq.8), kind=kLoop, calls=%fused_computation | loop fusion | flops 12582912 | bytes 16777216 | tf_op jit(solution)/shard_map/jit(_where)/select_n | solution.py:251
  113.0 13.2 %collective-permute-done.3.refs_6_ = bf16[1,2,512,512]{3,2,1,0:T(8,128)(2,1)S(1)} collective-permute-done((bf16[1,2,512,512]{3,2,1,0:T(8,128)(2,1)}, bf16[1,2,512,512]{3,2,1,0:T(8,128)(2,1)S(1)}, u32[]{:S(2)}, u32[]{:S(2)}) %collective-permute-start.3) | collective-permute-done | bytes 1048608 | tf_op jit(solution)/shard_map/ppermute | solution.py:230
  126.2 22.5 %collective-permute-done.9.refs_7_ = bf16[1,2,512,512]{3,2,1,0:T(8,128)(2,1)S(1)} collective-permute-done((bf16[1,2,512,512]{3,2,1,0:T(8,128)(2,1)}, bf16[1,2,512,512]{3,2,1,0:T(8,128)(2,1)S(1)}, u32[]{:S(2)}, u32[]{:S(2)}) %collective-permute-start.9) | collective-permute-done | bytes 1048608 | tf_op jit(solution)/shard_map/ppermute | solution.py:230
  148.6 22.6 %collective-permute-done.8.refs_0_ = bf16[2,2,128,1024]{3,2,1,0:T(8,128)(2,1)} collective-permute-done((bf16[2,2,128,1024]{3,2,1,0:T(8,128)(2,1)S(1)}, bf16[2,2,128,1024]{3,2,1,0:T(8,128)(2,1)}, u32[]{:S(2)}, u32[]{:S(2)}) %collective-permute-start.8) | collective-permute-done | bytes 1048608 | tf_op jit(solution)/shard_map/ppermute | solution.py:230
  171.2 0.6 pad_add_fusion.1.block_ref
  171.9 0.6 pad_maximum_fusion.mpo_ref
  172.5 21.2 %collective-permute-done.10.refs_1_ = bf16[2,2,128,1024]{3,2,1,0:T(8,128)(2,1)} collective-permute-done((bf16[2,2,128,1024]{3,2,1,0:T(8,128)(2,1)S(1)}, bf16[2,2,128,1024]{3,2,1,0:T(8,128)(2,1)}, u32[]{:S(2)}, u32[]{:S(2)}) %collective-permute-start.10) | collective-permute-done | bytes 1048608 | tf_op jit(solution)/shard_map/ppermute | solution.py:230
  193.7 24.4 %first_product.1 = bf16[2,2,2,512,512]{4,3,2,1,0:T(8,128)(2,1)} custom-call(s32[4]{0:T(128)} %pad_add_fusion.1.block_ref, f32[2,2,2,2]{3,2,1,0:T(2,128)} %pad_maximum_fusion.mpo_ref, bf16[2,2,2,512,1024]{4,3,2,1,0:T(8,128)(2,1)} %maximum_select_fusion.site_ref, bf16[1,2,512,512]{3,2,1,0:T(8,128)(2,1)} %copy-done.5, bf16[1,2,512,512]{3,2,1,0:T(8,128)(2,1)} %copy-done.12, ...), custom_call_target="tpu_custom_call" | custom-call | tf_op jit(solution)/shard_map/first_product/pallas_call | solution.py:67
  218.1 1.2 collective-permute-start.12
  219.3 0.6 pad_add_fusion.pick_ref
  219.9 6.5 %collective-permute-done.12 = bf16[2,2,2,512,512]{4,3,2,1,0:T(8,128)(2,1)} collective-permute-done((bf16[2,2,2,512,512]{4,3,2,1,0:T(8,128)(2,1)}, bf16[2,2,2,512,512]{4,3,2,1,0:T(8,128)(2,1)}, u32[]{:S(2)}, u32[]{:S(2)}) %collective-permute-start.12) | collective-permute-done | bytes 4194336 | tf_op jit(solution)/shard_map/ppermute | solution.py:171
  226.4 11.5 %maximum_select_fusion.1.q_ref = bf16[2,2,2,512,1024]{4,3,2,1,0:T(8,128)(2,1)} fusion(bf16[2,2,2,512,512]{4,3,2,1,0:T(8,128)(2,1)} %collective-permute-done.12, bf16[2,2,2,512,512]{4,3,2,1,0:T(8,128)(2,1)} %first_product.1, pred[]{:T(512)S(6)} %eq.7), kind=kLoop, calls=%fused_computation.1 | loop fusion | flops 37748736 | bytes 16777216 | tf_op jit(solution)/shard_map/jit(_where)/select_n | solution.py:234
  237.9 8.6 %second_product.5.refs_0_ = bf16[2,2,512,256]{3,2,1,0:T(8,128)(2,1)} custom-call(s32[2]{0:T(128)} %pad_add_fusion.pick_ref, bf16[2,2,2,512,1024]{4,3,2,1,0:T(8,128)(2,1)} %maximum_select_fusion.1.q_ref, bf16[2,2,128,1024]{3,2,1,0:T(8,128)(2,1)} %copy-done.10, bf16[2,2,128,1024]{3,2,1,0:T(8,128)(2,1)} %copy-done.9), custom_call_target="tpu_custom_call" | custom-call | tf_op jit(solution)/shard_map/second_product/pallas_call | solution.py:103
  246.5 1.3 collective-permute-start.13
  247.8 0.2 collective-permute-start.20
  248.0 8.6 %second_product.6.refs_3_ = bf16[2,2,512,256]{3,2,1,0:T(8,128)(2,1)} custom-call(s32[2]{0:T(128)} %pad_add_fusion.pick_ref, bf16[2,2,2,512,1024]{4,3,2,1,0:T(8,128)(2,1)} %maximum_select_fusion.1.q_ref, bf16[2,2,128,1024]{3,2,1,0:T(8,128)(2,1)} %collective-permute-done.8.refs_0_, bf16[2,2,128,1024]{3,2,1,0:T(8,128)(2,1)} %collective-permute-done.10.refs_1_), custom_call_target="tpu_custom_call" | custom-call | tf_op jit(solution)/shard_map/second_product/pallas_call | solution.py:103
  256.7 1.0 copy-done.21
  257.7 8.6 %second_product.7.refs_6_ = bf16[2,2,512,256]{3,2,1,0:T(8,128)(2,1)} custom-call(s32[2]{0:T(128)} %pad_add_fusion.pick_ref, bf16[2,2,2,512,1024]{4,3,2,1,0:T(8,128)(2,1)} %maximum_select_fusion.1.q_ref, bf16[2,2,128,1024]{3,2,1,0:T(8,128)(2,1)} %copy-done.14, bf16[2,2,128,1024]{3,2,1,0:T(8,128)(2,1)} %copy-done.21), custom_call_target="tpu_custom_call" | custom-call | tf_op jit(solution)/shard_map/second_product/pallas_call | solution.py:103
  266.3 4.1 %collective-permute-start.18 = (bf16[2,2,512,256]{3,2,1,0:T(8,128)(2,1)}, bf16[2,2,512,256]{3,2,1,0:T(8,128)(2,1)S(1)}, u32[]{:S(2)}, u32[]{:S(2)}) collective-permute-start(bf16[2,2,512,256]{3,2,1,0:T(8,128)(2,1)} %second_product.7.refs_6_), channel_id=1, source_target_pairs={{0,2},{1,3},{5,7},{4,6},{10,8},{11,9},{15,13},{14,12},{16,18},{17,... | collective-permute-start | bytes 3145736 | tf_op jit(solution)/shard_map/ppermute | solution.py:275
  270.4 1.4 collective-permute-start.15
  271.7 0.1 collective-permute-start.24
  271.8 1.3 collective-permute-done.13.refs_1_
  273.1 1.3 add_convert_fusion.2
  274.4 3.2 collective-permute-start.14
  277.6 8.1 %second_product.8.refs_9_ = bf16[2,2,512,128]{3,2,1,0:T(8,128)(2,1)} custom-call(s32[2]{0:T(128)} %pad_add_fusion.pick_ref, bf16[2,2,2,512,1024]{4,3,2,1,0:T(8,128)(2,1)} %maximum_select_fusion.1.q_ref, bf16[2,2,128,1024]{3,2,1,0:T(8,128)(2,1)} %collective-permute-done.20.refs_0_), custom_call_target="tpu_custom_call" | custom-call | tf_op jit(solution)/shard_map/second_product/pallas_call | solution.py:103
  285.7 1.4 collective-permute-start.21
  287.1 5.4 %collective-permute-done.18.refs_7_ = bf16[2,2,512,256]{3,2,1,0:T(8,128)(2,1)S(1)} collective-permute-done((bf16[2,2,512,256]{3,2,1,0:T(8,128)(2,1)}, bf16[2,2,512,256]{3,2,1,0:T(8,128)(2,1)S(1)}, u32[]{:S(2)}, u32[]{:S(2)}) %collective-permute-start.18) | collective-permute-done | bytes 1048608 | tf_op jit(solution)/shard_map/ppermute | solution.py:275
  292.5 1.3 collective-permute-start.22
  293.8 1.3 add_convert_fusion
  295.0 19.8 %collective-permute-done.15.refs_4_ = bf16[2,2,512,256]{3,2,1,0:T(8,128)(2,1)S(1)} collective-permute-done((bf16[2,2,512,256]{3,2,1,0:T(8,128)(2,1)S(1)}, bf16[2,2,512,256]{3,2,1,0:T(8,128)(2,1)S(1)}, u32[]{:S(2)}, u32[]{:S(2)}) %collective-permute-start.15) | collective-permute-done | bytes 1048608 | tf_op jit(solution)/shard_map/ppermute | solution.py:275
  314.8 0.7 collective-permute-start.19
  315.5 0.2 add_convert_fusion.1
  315.8 0.7 collective-permute-start.16
  316.6 1.3 collective-permute-start.23
  317.9 8.1 %second_product.9.refs_13_ = bf16[2,2,512,128]{3,2,1,0:T(8,128)(2,1)} custom-call(s32[2]{0:T(128)} %pad_add_fusion.pick_ref, bf16[2,2,2,512,1024]{4,3,2,1,0:T(8,128)(2,1)} %maximum_select_fusion.1.q_ref, bf16[2,2,128,1024]{3,2,1,0:T(8,128)(2,1)} %collective-permute-done.24.refs_0_), custom_call_target="tpu_custom_call" | custom-call | tf_op jit(solution)/shard_map/second_product/pallas_call | solution.py:103
  326.0 1.3 collective-permute-start.25
  327.3 1.3 collective-permute-start.26
  328.6 1.3 collective-permute-start.27
  329.9 13.2 %collective-permute-done.25.refs_14_ = bf16[2,2,512,128]{3,2,1,0:T(8,128)(2,1)S(1)} collective-permute-done((bf16[2,2,512,128]{3,2,1,0:T(8,128)(2,1)}, bf16[2,2,512,128]{3,2,1,0:T(8,128)(2,1)S(1)}, u32[]{:S(2)}, u32[]{:S(2)}) %collective-permute-start.25) | collective-permute-done | bytes 524320 | tf_op jit(solution)/shard_map/ppermute | solution.py:275
  343.2 2.2 collective-permute-done.26.refs_15_
  345.4 0.8 copy-done.27
  346.1 0.8 copy-done.28
  346.9 6.5 %finish.1 = f32[2,2,512,512]{3,2,1,0:T(8,128)} custom-call(s32[2]{0:T(128)} %pad_add_fusion.pick_ref, bf16[2,2,512,256]{3,2,1,0:T(8,128)(2,1)} %second_product.5.refs_0_, bf16[2,2,512,256]{3,2,1,0:T(8,128)(2,1)} %copy-done.6, bf16[2,2,512,256]{3,2,1,0:T(8,128)(2,1)} %copy-done.20, bf16[2,2,512,256]{3,2,1,0:T(8,128)(2,1)} %second_product.6.refs_3_, ...), custom_call_target="tpu_custom_call" | custom-call | tf_op jit(solution)/shard_map/finish/pallas_call | solution.py:152
  (73 shorter events, 0.2 us)
Async XLA Ops:
  1.7 7.4 %copy-start.5 = (bf16[1,2,512,512]{3,2,1,0:T(8,128)(2,1)}, bf16[1,2,512,512]{3,2,1,0:T(8,128)(2,1)S(1)}, u32[]{:S(2)}) copy-start(bf16[1,2,512,512]{3,2,1,0:T(8,128)(2,1)S(1)} %get-tuple-element.31.refs_0_) | copy-start | bytes 3145732
  1.7 2.9 collective-permute-start
  1.8 28.3 %collective-permute-start.1 = (bf16[1,2,512,512]{3,2,1,0:T(8,128)(2,1)S(1)}, bf16[1,2,512,512]{3,2,1,0:T(8,128)(2,1)}, u32[]{:S(2)}, u32[]{:S(2)}) collective-permute-start(bf16[1,2,512,512]{3,2,1,0:T(8,128)(2,1)S(1)} %get-tuple-element.31.refs_0_), channel_id=1, source_target_pairs={{0,4},{4,8},{8,12},{12,0},{1,5},{5,9},{9,13},{13,1},{2,6},{6,10},{... | collective-permute-start | bytes 3145736 | tf_op jit(solution)/shard_map/ppermute | solution.py:230
  4.6 1.0 copy-start.12
  9.1 2.0 copy-start
  11.1 1.2 copy-start.13
  12.3 40.2 %collective-permute-start.5 = (bf16[1,2,512,512]{3,2,1,0:T(8,128)(2,1)S(1)}, bf16[1,2,512,512]{3,2,1,0:T(8,128)(2,1)S(1)}, u32[]{:S(2)}, u32[]{:S(2)}) collective-permute-start(bf16[1,2,512,512]{3,2,1,0:T(8,128)(2,1)S(1)} %copy-done.13), channel_id=1, source_target_pairs={{0,4},{4,8},{8,12},{12,0},{1,5},{5,9},{9,13},{13,1},{2,6},{6,10},{... | collective-permute-start | bytes 3145736 | tf_op jit(solution)/shard_map/ppermute | solution.py:230
  14.6 60.4 %collective-permute-start.4 = (bf16[2,2,256,1024]{3,2,1,0:T(8,128)(2,1)S(1)}, bf16[2,2,256,1024]{3,2,1,0:T(8,128)(2,1)}, u32[]{:S(2)}, u32[]{:S(2)}) collective-permute-start(bf16[2,2,256,1024]{3,2,1,0:T(8,128)(2,1)S(1)} %dynamic-slice_bitcast_fusion), channel_id=1, source_target_pairs={{0,2},{2,0},{1,3},{3,1},{4,6},{6,4},{5,7},{7,5},{8,10},{10,8},{9,1... | collective-permute-start | bytes 6291464 | tf_op jit(solution)/shard_map/ppermute | solution.py:233
  30.2 44.8 %collective-permute-start.2 = (bf16[1,2,512,512]{3,2,1,0:T(8,128)(2,1)}, bf16[1,2,512,512]{3,2,1,0:T(8,128)(2,1)S(1)}, u32[]{:S(2)}, u32[]{:S(2)}) collective-permute-start(bf16[1,2,512,512]{3,2,1,0:T(8,128)(2,1)} %collective-permute-done.1.refs_2_), channel_id=1, source_target_pairs={{0,4},{4,8},{8,12},{12,0},{1,5},{5,9},{9,13},{13,1},{2,6},{6,10},{... | collective-permute-start | bytes 3145736 | tf_op jit(solution)/shard_map/ppermute | solution.py:230
  52.5 22.5 %copy-start.15 = (bf16[1,2,512,512]{3,2,1,0:T(8,128)(2,1)}, bf16[1,2,512,512]{3,2,1,0:T(8,128)(2,1)S(1)}, u32[]{:S(2)}) copy-start(bf16[1,2,512,512]{3,2,1,0:T(8,128)(2,1)S(1)} %collective-permute-done.5.refs_3_) | copy-start | bytes 3145732
  52.5 44.9 %collective-permute-start.6 = (bf16[1,2,512,512]{3,2,1,0:T(8,128)(2,1)S(1)}, bf16[1,2,512,512]{3,2,1,0:T(8,128)(2,1)S(1)}, u32[]{:S(2)}, u32[]{:S(2)}) collective-permute-start(bf16[1,2,512,512]{3,2,1,0:T(8,128)(2,1)S(1)} %collective-permute-done.5.refs_3_), channel_id=1, source_target_pairs={{0,4},{4,8},{8,12},{12,0},{1,5},{5,9},{9,13},{13,1},{2,6},{6,10},{... | collective-permute-start | bytes 3145736 | tf_op jit(solution)/shard_map/ppermute | solution.py:230
  75.0 22.5 %copy-start.16 = (bf16[1,2,512,512]{3,2,1,0:T(8,128)(2,1)}, bf16[1,2,512,512]{3,2,1,0:T(8,128)(2,1)S(1)}, u32[]{:S(2)}) copy-start(bf16[1,2,512,512]{3,2,1,0:T(8,128)(2,1)S(1)} %collective-permute-done.2.refs_4_) | copy-start | bytes 3145732
  97.5 1.0 copy-start.17
  98.4 4.8 %collective-permute-start.7 = (bf16[2,2,256,1024]{3,2,1,0:T(8,128)(2,1)}, bf16[2,2,256,1024]{3,2,1,0:T(8,128)(2,1)}, u32[]{:S(2)}, u32[]{:S(2)}) collective-permute-start(bf16[2,2,256,1024]{3,2,1,0:T(8,128)(2,1)} %collective-permute-done.4), channel_id=1, source_target_pairs={{0,1},{1,0},{2,3},{3,2},{4,5},{5,4},{6,7},{7,6},{8,9},{9,8},{10,11... | collective-permute-start | bytes 6291464 | tf_op jit(solution)/shard_map/ppermute | solution.py:171
  99.3 26.9 %copy-start.10 = (bf16[2,2,128,1024]{3,2,1,0:T(8,128)(2,1)}, bf16[2,2,128,1024]{3,2,1,0:T(8,128)(2,1)S(1)}, u32[]{:S(2)}) copy-start(bf16[2,2,128,1024]{3,2,1,0:T(8,128)(2,1)S(1)} %get-tuple-element.18.refs_0_) | copy-start | bytes 3145732
  99.3 49.3 %copy-start.9 = (bf16[2,2,128,1024]{3,2,1,0:T(8,128)(2,1)}, bf16[2,2,128,1024]{3,2,1,0:T(8,128)(2,1)S(1)}, u32[]{:S(2)}) copy-start(bf16[2,2,128,1024]{3,2,1,0:T(8,128)(2,1)S(1)} %get-tuple-element.19.refs_1_) | copy-start | bytes 3145732
  99.3 26.9 %collective-permute-start.3 = (bf16[1,2,512,512]{3,2,1,0:T(8,128)(2,1)}, bf16[1,2,512,512]{3,2,1,0:T(8,128)(2,1)S(1)}, u32[]{:S(2)}, u32[]{:S(2)}) collective-permute-start(bf16[1,2,512,512]{3,2,1,0:T(8,128)(2,1)} %copy-done.16), channel_id=1, source_target_pairs={{0,4},{4,8},{8,12},{12,0},{1,5},{5,9},{9,13},{13,1},{2,6},{6,10},{... | collective-permute-start | bytes 3145736 | tf_op jit(solution)/shard_map/ppermute | solution.py:230
  99.4 49.3 %collective-permute-start.9 = (bf16[1,2,512,512]{3,2,1,0:T(8,128)(2,1)}, bf16[1,2,512,512]{3,2,1,0:T(8,128)(2,1)S(1)}, u32[]{:S(2)}, u32[]{:S(2)}) collective-permute-start(bf16[1,2,512,512]{3,2,1,0:T(8,128)(2,1)} %copy-done.17), channel_id=1, source_target_pairs={{0,4},{4,8},{8,12},{12,0},{1,5},{5,9},{9,13},{13,1},{2,6},{6,10},{... | collective-permute-start | bytes 3145736 | tf_op jit(solution)/shard_map/ppermute | solution.py:230
  103.2 5.7 %copy-start.1 = (bf16[2,512,2,1024]{3,1,2,0:T(8,128)(2,1)S(1)}, bf16[2,512,2,1024]{3,1,2,0:T(8,128)(2,1)}, u32[]{:S(2)}) copy-start(bf16[2,512,2,1024]{3,1,2,0:T(8,128)(2,1)} %copy-done) | copy-start | bytes 12582916
  108.9 63.0 %copy-start.29 = (f32[2,2,2,2]{3,2,1,0:T(2,128)S(1)}, f32[2,2,2,2]{3,2,1,0:T(2,128)}, u32[]{:S(2)}) copy-start(f32[2,2,2,2]{3,2,1,0:T(2,128)} %param.5) | copy-start | bytes 196
  126.2 45.0 %copy-start.18 = (bf16[1,2,512,512]{3,2,1,0:T(8,128)(2,1)}, bf16[1,2,512,512]{3,2,1,0:T(8,128)(2,1)S(1)}, u32[]{:S(2)}) copy-start(bf16[1,2,512,512]{3,2,1,0:T(8,128)(2,1)S(1)} %collective-permute-done.3.refs_6_) | copy-start | bytes 3145732
  126.2 45.0 %collective-permute-start.8 = (bf16[2,2,128,1024]{3,2,1,0:T(8,128)(2,1)S(1)}, bf16[2,2,128,1024]{3,2,1,0:T(8,128)(2,1)}, u32[]{:S(2)}, u32[]{:S(2)}) collective-permute-start(bf16[2,2,128,1024]{3,2,1,0:T(8,128)(2,1)S(1)} %get-tuple-element.18.refs_0_), channel_id=1, source_target_pairs={{0,4},{4,8},{8,12},{12,0},{1,5},{5,9},{9,13},{13,1},{2,6},{6,10},{... | collective-permute-start | bytes 3145736 | tf_op jit(solution)/shard_map/ppermute | solution.py:230
  148.6 22.6 %copy-start.19 = (bf16[1,2,512,512]{3,2,1,0:T(8,128)(2,1)}, bf16[1,2,512,512]{3,2,1,0:T(8,128)(2,1)S(1)}, u32[]{:S(2)}) copy-start(bf16[1,2,512,512]{3,2,1,0:T(8,128)(2,1)S(1)} %collective-permute-done.9.refs_7_) | copy-start | bytes 3145732
  148.6 45.0 %collective-permute-start.10 = (bf16[2,2,128,1024]{3,2,1,0:T(8,128)(2,1)S(1)}, bf16[2,2,128,1024]{3,2,1,0:T(8,128)(2,1)}, u32[]{:S(2)}, u32[]{:S(2)}) collective-permute-start(bf16[2,2,128,1024]{3,2,1,0:T(8,128)(2,1)S(1)} %get-tuple-element.19.refs_1_), channel_id=1, source_target_pairs={{0,4},{4,8},{8,12},{12,0},{1,5},{5,9},{9,13},{13,1},{2,6},{6,10},{... | collective-permute-start | bytes 3145736 | tf_op jit(solution)/shard_map/ppermute | solution.py:230
  171.2 46.8 %collective-permute-start.11 = (bf16[2,2,128,1024]{3,2,1,0:T(8,128)(2,1)}, bf16[2,2,128,1024]{3,2,1,0:T(8,128)(2,1)S(1)}, u32[]{:S(2)}, u32[]{:S(2)}) collective-permute-start(bf16[2,2,128,1024]{3,2,1,0:T(8,128)(2,1)} %collective-permute-done.8.refs_0_), channel_id=1, source_target_pairs={{0,4},{4,8},{8,12},{12,0},{1,5},{5,9},{9,13},{13,1},{2,6},{6,10},{... | collective-permute-start | bytes 3145736 | tf_op jit(solution)/shard_map/ppermute | solution.py:230
  218.1 29.7 %copy-start.14 = (bf16[2,2,128,1024]{3,2,1,0:T(8,128)(2,1)}, bf16[2,2,128,1024]{3,2,1,0:T(8,128)(2,1)S(1)}, u32[]{:S(2)}) copy-start(bf16[2,2,128,1024]{3,2,1,0:T(8,128)(2,1)S(1)} %collective-permute-done.11.refs_0_) | copy-start | bytes 3145732
  218.1 8.4 %collective-permute-start.12 = (bf16[2,2,2,512,512]{4,3,2,1,0:T(8,128)(2,1)}, bf16[2,2,2,512,512]{4,3,2,1,0:T(8,128)(2,1)}, u32[]{:S(2)}, u32[]{:S(2)}) collective-permute-start(bf16[2,2,2,512,512]{4,3,2,1,0:T(8,128)(2,1)} %first_product.1), channel_id=1, source_target_pairs={{0,1},{1,0},{2,3},{3,2},{4,5},{5,4},{6,7},{7,6},{8,9},{9,8},{10,11... | collective-permute-start | bytes 12582920 | tf_op jit(solution)/shard_map/ppermute | solution.py:171
  219.9 36.8 %collective-permute-start.17 = (bf16[2,2,128,1024]{3,2,1,0:T(8,128)(2,1)}, bf16[2,2,128,1024]{3,2,1,0:T(8,128)(2,1)S(1)}, u32[]{:S(2)}, u32[]{:S(2)}) collective-permute-start(bf16[2,2,128,1024]{3,2,1,0:T(8,128)(2,1)} %collective-permute-done.10.refs_1_), channel_id=1, source_target_pairs={{0,4},{4,8},{8,12},{12,0},{1,5},{5,9},{9,13},{13,1},{2,6},{6,10},{... | collective-permute-start | bytes 3145736 | tf_op jit(solution)/shard_map/ppermute | solution.py:230
  246.5 26.6 %collective-permute-start.13 = (bf16[2,2,512,256]{3,2,1,0:T(8,128)(2,1)}, bf16[2,2,512,256]{3,2,1,0:T(8,128)(2,1)S(1)}, u32[]{:S(2)}, u32[]{:S(2)}) collective-permute-start(bf16[2,2,512,256]{3,2,1,0:T(8,128)(2,1)} %second_product.5.refs_0_), channel_id=1, source_target_pairs={{2,0},{3,1},{7,5},{6,4},{8,10},{9,11},{13,15},{12,14},{18,16},{19,... | collective-permute-start | bytes 3145736 | tf_op jit(solution)/shard_map/ppermute | solution.py:275
  247.8 29.8 %collective-permute-start.20 = (bf16[2,2,128,1024]{3,2,1,0:T(8,128)(2,1)S(1)}, bf16[2,2,128,1024]{3,2,1,0:T(8,128)(2,1)}, u32[]{:S(2)}, u32[]{:S(2)}) collective-permute-start(bf16[2,2,128,1024]{3,2,1,0:T(8,128)(2,1)S(1)} %collective-permute-done.11.refs_0_), channel_id=1, source_target_pairs={{0,4},{4,8},{8,12},{12,0},{1,5},{5,9},{9,13},{13,1},{2,6},{6,10},{... | collective-permute-start | bytes 3145736 | tf_op jit(solution)/shard_map/ppermute | solution.py:230
  256.7 13.7 %copy-start.3 = (bf16[2,2,512,256]{3,2,1,0:T(8,128)(2,1)S(1)}, bf16[2,2,512,256]{3,2,1,0:T(8,128)(2,1)}, u32[]{:S(2)}) copy-start(bf16[2,2,512,256]{3,2,1,0:T(8,128)(2,1)} %second_product.6.refs_3_) | copy-start | bytes 3145732
  256.7 16.4 %copy-start.2 = (bf16[2,2,512,256]{3,2,1,0:T(8,128)(2,1)S(1)}, bf16[2,2,512,256]{3,2,1,0:T(8,128)(2,1)}, u32[]{:S(2)}) copy-start(bf16[2,2,512,256]{3,2,1,0:T(8,128)(2,1)} %second_product.5.refs_0_) | copy-start | bytes 3145732
  256.7 1.0 copy-start.21
  266.3 26.2 %collective-permute-start.18 = (bf16[2,2,512,256]{3,2,1,0:T(8,128)(2,1)}, bf16[2,2,512,256]{3,2,1,0:T(8,128)(2,1)S(1)}, u32[]{:S(2)}, u32[]{:S(2)}) collective-permute-start(bf16[2,2,512,256]{3,2,1,0:T(8,128)(2,1)} %second_product.7.refs_6_), channel_id=1, source_target_pairs={{0,2},{1,3},{5,7},{4,6},{10,8},{11,9},{15,13},{14,12},{16,18},{17,... | collective-permute-start | bytes 3145736 | tf_op jit(solution)/shard_map/ppermute | solution.py:275
  270.4 44.4 %collective-permute-start.15 = (bf16[2,2,512,256]{3,2,1,0:T(8,128)(2,1)S(1)}, bf16[2,2,512,256]{3,2,1,0:T(8,128)(2,1)S(1)}, u32[]{:S(2)}, u32[]{:S(2)}) collective-permute-start(bf16[2,2,512,256]{3,2,1,0:T(8,128)(2,1)S(1)} %copy-done.3), channel_id=1, source_target_pairs={{1,3},{0,2},{6,4},{7,5},{11,9},{10,8},{12,14},{13,15},{17,19},{16,... | collective-permute-start | bytes 3145736 | tf_op jit(solution)/shard_map/ppermute | solution.py:275
  271.7 44.1 %collective-permute-start.24 = (bf16[2,2,128,1024]{3,2,1,0:T(8,128)(2,1)}, bf16[2,2,128,1024]{3,2,1,0:T(8,128)(2,1)}, u32[]{:S(2)}, u32[]{:S(2)}) collective-permute-start(bf16[2,2,128,1024]{3,2,1,0:T(8,128)(2,1)} %copy-done.21), channel_id=1, source_target_pairs={{0,4},{4,8},{8,12},{12,0},{1,5},{5,9},{9,13},{13,1},{2,6},{6,10},{... | collective-permute-start | bytes 3145736 | tf_op jit(solution)/shard_map/ppermute | solution.py:230
  273.1 12.6 %copy-start.6 = (bf16[2,2,512,256]{3,2,1,0:T(8,128)(2,1)}, bf16[2,2,512,256]{3,2,1,0:T(8,128)(2,1)S(1)}, u32[]{:S(2)}) copy-start(bf16[2,2,512,256]{3,2,1,0:T(8,128)(2,1)S(1)} %collective-permute-done.13.refs_1_) | copy-start | bytes 3145732
  274.4 19.4 %copy-start.4 = (bf16[2,2,512,256]{3,2,1,0:T(8,128)(2,1)S(1)}, bf16[2,2,512,256]{3,2,1,0:T(8,128)(2,1)}, u32[]{:S(2)}) copy-start(bf16[2,2,512,256]{3,2,1,0:T(8,128)(2,1)} %second_product.7.refs_6_) | copy-start | bytes 3145732
  274.4 42.2 %collective-permute-start.14 = (bf16[2,2,512,256]{3,2,1,0:T(8,128)(2,1)}, bf16[2,2,512,256]{3,2,1,0:T(8,128)(2,1)S(1)}, u32[]{:S(2)}, u32[]{:S(2)}) collective-permute-start(bf16[2,2,512,256]{3,2,1,0:T(8,128)(2,1)} %add_convert_fusion.2), channel_id=1, source_target_pairs={{1,0},{4,5},{11,10},{14,15},{17,16},{20,21},{27,26},{30,31}} | collective-permute-start | bytes 3145736 | tf_op jit(solution)/shard_map/ppermute | solution.py:275
  285.7 30.9 %copy-start.11 = (bf16[2,2,512,128]{3,2,1,0:T(8,128)(2,1)S(1)}, bf16[2,2,512,128]{3,2,1,0:T(8,128)(2,1)}, u32[]{:S(2)}) copy-start(bf16[2,2,512,128]{3,2,1,0:T(8,128)(2,1)} %second_product.8.refs_9_) | copy-start | bytes 1572868
  285.7 40.3 %collective-permute-start.21 = (bf16[2,2,512,128]{3,2,1,0:T(8,128)(2,1)}, bf16[2,2,512,128]{3,2,1,0:T(8,128)(2,1)S(1)}, u32[]{:S(2)}, u32[]{:S(2)}) collective-permute-start(bf16[2,2,512,128]{3,2,1,0:T(8,128)(2,1)} %second_product.8.refs_9_), channel_id=1, source_target_pairs={{3,1},{4,6},{9,11},{14,12},{19,17},{20,22},{25,27},{30,28}} | collective-permute-start | bytes 1572872 | tf_op jit(solution)/shard_map/ppermute | solution.py:275
  292.5 33.5 %copy-start.7 = (bf16[2,2,512,256]{3,2,1,0:T(8,128)(2,1)}, bf16[2,2,512,256]{3,2,1,0:T(8,128)(2,1)S(1)}, u32[]{:S(2)}) copy-start(bf16[2,2,512,256]{3,2,1,0:T(8,128)(2,1)S(1)} %collective-permute-done.18.refs_7_) | copy-start | bytes 3145732
  292.5 34.8 %collective-permute-start.22 = (bf16[2,2,512,128]{3,2,1,0:T(8,128)(2,1)}, bf16[2,2,512,128]{3,2,1,0:T(8,128)(2,1)S(1)}, u32[]{:S(2)}, u32[]{:S(2)}) collective-permute-start(bf16[2,2,512,128]{3,2,1,0:T(8,128)(2,1)} %second_product.8.refs_9_), channel_id=1, source_target_pairs={{2,1},{5,6},{8,11},{15,12},{18,17},{21,22},{24,27},{31,28}} | collective-permute-start | bytes 1572872 | tf_op jit(solution)/shard_map/ppermute | solution.py:275
  314.8 11.1 %copy-start.8 = (bf16[2,2,512,256]{3,2,1,0:T(8,128)(2,1)}, bf16[2,2,512,256]{3,2,1,0:T(8,128)(2,1)S(1)}, u32[]{:S(2)}) copy-start(bf16[2,2,512,256]{3,2,1,0:T(8,128)(2,1)S(1)} %collective-permute-done.15.refs_4_) | copy-start | bytes 3145732
  314.8 15.1 %collective-permute-start.19 = (bf16[2,2,512,256]{3,2,1,0:T(8,128)(2,1)}, bf16[2,2,512,256]{3,2,1,0:T(8,128)(2,1)S(1)}, u32[]{:S(2)}, u32[]{:S(2)}) collective-permute-start(bf16[2,2,512,256]{3,2,1,0:T(8,128)(2,1)} %add_convert_fusion), channel_id=1, source_target_pairs={{3,2},{6,7},{9,8},{12,13},{19,18},{22,23},{25,24},{28,29}} | collective-permute-start | bytes 3145736 | tf_op jit(solution)/shard_map/ppermute | solution.py:275
  315.8 14.1 %collective-permute-start.16 = (bf16[2,2,512,256]{3,2,1,0:T(8,128)(2,1)S(1)}, bf16[2,2,512,256]{3,2,1,0:T(8,128)(2,1)S(1)}, u32[]{:S(2)}, u32[]{:S(2)}) collective-permute-start(bf16[2,2,512,256]{3,2,1,0:T(8,128)(2,1)S(1)} %add_convert_fusion.1), channel_id=1, source_target_pairs={{2,3},{5,4},{8,9},{15,14},{18,19},{21,20},{24,25},{31,30}} | collective-permute-start | bytes 3145736 | tf_op jit(solution)/shard_map/ppermute | solution.py:275
  316.6 9.4 %copy-start.20 = (bf16[2,2,512,256]{3,2,1,0:T(8,128)(2,1)}, bf16[2,2,512,256]{3,2,1,0:T(8,128)(2,1)S(1)}, u32[]{:S(2)}) copy-start(bf16[2,2,512,256]{3,2,1,0:T(8,128)(2,1)S(1)} %collective-permute-done.14.refs_2_) | copy-start | bytes 3145732
  316.6 12.0 %collective-permute-start.23 = (bf16[2,2,512,128]{3,2,1,0:T(8,128)(2,1)S(1)}, bf16[2,2,512,128]{3,2,1,0:T(8,128)(2,1)}, u32[]{:S(2)}, u32[]{:S(2)}) collective-permute-start(bf16[2,2,512,128]{3,2,1,0:T(8,128)(2,1)S(1)} %copy-done.11), channel_id=1, source_target_pairs={{0,1},{7,6},{10,11},{13,12},{16,17},{23,22},{26,27},{29,28}} | collective-permute-start | bytes 1572872 | tf_op jit(solution)/shard_map/ppermute | solution.py:275
  326.0 19.4 %copy-start.24 = (bf16[2,2,512,128]{3,2,1,0:T(8,128)(2,1)}, bf16[2,2,512,128]{3,2,1,0:T(8,128)(2,1)S(1)}, u32[]{:S(2)}) copy-start(bf16[2,2,512,128]{3,2,1,0:T(8,128)(2,1)S(1)} %collective-permute-done.21.refs_10_) | copy-start | bytes 1572868
  326.0 17.2 %collective-permute-start.25 = (bf16[2,2,512,128]{3,2,1,0:T(8,128)(2,1)}, bf16[2,2,512,128]{3,2,1,0:T(8,128)(2,1)S(1)}, u32[]{:S(2)}, u32[]{:S(2)}) collective-permute-start(bf16[2,2,512,128]{3,2,1,0:T(8,128)(2,1)} %second_product.9.refs_13_), channel_id=1, source_target_pairs={{3,1},{4,6},{9,11},{14,12},{19,17},{20,22},{25,27},{30,28}} | collective-permute-start | bytes 1572872 | tf_op jit(solution)/shard_map/ppermute | solution.py:275
  327.3 18.1 %copy-start.25 = (bf16[2,2,512,128]{3,2,1,0:T(8,128)(2,1)}, bf16[2,2,512,128]{3,2,1,0:T(8,128)(2,1)S(1)}, u32[]{:S(2)}) copy-start(bf16[2,2,512,128]{3,2,1,0:T(8,128)(2,1)S(1)} %collective-permute-done.22.refs_11_) | copy-start | bytes 1572868
  327.3 18.0 %collective-permute-start.26 = (bf16[2,2,512,128]{3,2,1,0:T(8,128)(2,1)}, bf16[2,2,512,128]{3,2,1,0:T(8,128)(2,1)S(1)}, u32[]{:S(2)}, u32[]{:S(2)}) collective-permute-start(bf16[2,2,512,128]{3,2,1,0:T(8,128)(2,1)} %second_product.9.refs_13_), channel_id=1, source_target_pairs={{2,1},{5,6},{8,11},{15,12},{18,17},{21,22},{24,27},{31,28}} | collective-permute-start | bytes 1572872 | tf_op jit(solution)/shard_map/ppermute | solution.py:275
  328.6 16.7 %collective-permute-start.27 = (bf16[2,2,512,128]{3,2,1,0:T(8,128)(2,1)}, bf16[2,2,512,128]{3,2,1,0:T(8,128)(2,1)S(1)}, u32[]{:S(2)}, u32[]{:S(2)}) collective-permute-start(bf16[2,2,512,128]{3,2,1,0:T(8,128)(2,1)} %second_product.9.refs_13_), channel_id=1, source_target_pairs={{0,1},{7,6},{10,11},{13,12},{16,17},{23,22},{26,27},{29,28}} | collective-permute-start | bytes 1572872 | tf_op jit(solution)/shard_map/ppermute | solution.py:275
  329.9 15.4 %copy-start.22 = (bf16[2,2,512,256]{3,2,1,0:T(8,128)(2,1)}, bf16[2,2,512,256]{3,2,1,0:T(8,128)(2,1)S(1)}, u32[]{:S(2)}) copy-start(bf16[2,2,512,256]{3,2,1,0:T(8,128)(2,1)S(1)} %collective-permute-done.19.refs_8_) | copy-start | bytes 3145732
  329.9 15.4 %copy-start.23 = (bf16[2,2,512,256]{3,2,1,0:T(8,128)(2,1)}, bf16[2,2,512,256]{3,2,1,0:T(8,128)(2,1)S(1)}, u32[]{:S(2)}) copy-start(bf16[2,2,512,256]{3,2,1,0:T(8,128)(2,1)S(1)} %collective-permute-done.16.refs_5_) | copy-start | bytes 3145732
  343.2 2.2 copy-start.26
  345.3 0.8 copy-start.27
  346.1 0.8 copy-start.28

commit v7 on v6

--- a/solution.py
+++ b/solution.py
@@ -34,20 +34,20 @@
     per_col = site_ref.shape[-1] // depth
     for which in range(2):
         for w in range(w_local):
-            g_real, g_imag = None, None
+            with_real, with_imag = None, None
             for number in range(len(env_refs) // 2):
                 block = block_ref[number]
                 piece = pl.ds(pl.multiple_of((block % per_col) * depth, depth), depth)
-                real = site_ref[block // per_col, :, 0, :, piece].reshape(phys * rows, depth)
-                imag = site_ref[block // per_col, :, 1, :, piece].reshape(phys * rows, depth)
-                env_real = env_refs[number * 2 + which][w, 0]
-                env_imag = env_refs[number * 2 + which][w, 1]
-                more_real = mul(real, env_real) + mul(imag, env_imag)
-                more_imag = mul(real, env_imag) + mul(imag, -env_real)
-                g_real = more_real if g_real is None else g_real + more_real
-                g_imag = more_imag if g_imag is None else g_imag + more_imag
-            g_ref[which * w_local + w, 0] = g_real
-            g_ref[which * w_local + w, 1] = g_imag
+                left = site_ref[block // per_col, :, :, :, piece].reshape(phys * 2 * rows, depth)
+                env_ref = env_refs[number * 2 + which]
+                more_real, more_imag = mul(left, env_ref[w, 0]), mul(left, env_ref[w, 1])
+                with_real = more_real if with_real is None else with_real + more_real
+                with_imag = more_imag if with_imag is None else with_imag + more_imag
+            for s in range(phys):
+                real, imag = (slice((2 * s + part) * rows, (2 * s + part + 1) * rows) for part in range(2))
+                there = slice(s * rows, (s + 1) * rows)
+                g_ref[which * w_local + w, 0, there] = with_real[real] + with_imag[imag]
+                g_ref[which * w_local + w, 1, there] = with_imag[real] - with_real[imag]
     for part in range(2):
         for v in range(mpo_count):
             for t in range(phys):
@@ -82,85 +82,82 @@
     )(blocks, mpo, site, *envs)
 
 
-def second_kernel(pick_ref, q_ref, *refs):
+def second_kernel(pick_ref, own_ref, sib_ref, *refs):
     site_refs, out_ref = refs[:-1], refs[-1]
-    join = lambda t, part: jnp.concatenate([site_ref[t, part] for site_ref in site_refs], axis=0)
-    out_real, out_imag = None, None
-    for t in range(q_ref.shape[1]):
-        q_real, q_imag = q_ref[0, t, 0], q_ref[0, t, 1]
-        real, imag = join(t, 0), join(t, 1)
-        more_real = mul_t(q_real, real) + mul_t(-q_imag, imag)
-        more_imag = mul_t(q_real, imag) + mul_t(q_imag, real)
-        out_real = more_real if out_real is None else out_real + more_real
-        out_imag = more_imag if out_imag is None else out_imag + more_imag
-    out_ref[0, 0] = out_real.astype(BF16)
-    out_ref[0, 1] = out_imag.astype(BF16)
-
-
-def second_product(pick, q, sites, row_tile):
-    mpo_count, phys, _, rows, cols = q.shape
+    phys, _, rows, cols = own_ref.shape[1:]
+    with_real, with_imag = None, None
+    for q_ref, quarter in ((own_ref, pick_ref[0]), (sib_ref, 1 - pick_ref[0])):
+        piece = pl.ds(pl.multiple_of(quarter * cols, cols), cols)
+        join = lambda t, part: jnp.concatenate([site_ref[t, part, :, piece] for site_ref in site_refs], axis=0)
+        for t in range(phys):
+            left = q_ref[0, t].reshape(2 * rows, cols)
+            more_real, more_imag = mul_t(left, join(t, 0)), mul_t(left, join(t, 1))
+            with_real = more_real if with_real is None else with_real + more_real
+            with_imag = more_imag if with_imag is None else with_imag + more_imag
+    out_ref[0, 0] = (with_real[:rows] - with_imag[rows:]).astype(BF16)
+    out_ref[0, 1] = (with_imag[:rows] + with_real[rows:]).astype(BF16)
+
+
+def second_product(pick, own, sib, sites):
+    mpo_count, phys, _, rows, cols = own.shape
     y_rows = sum(site.shape[2] for site in sites)
+    q_spec = pl.BlockSpec((1, phys, 2, rows, cols), lambda v: (v, 0, 0, 0, 0))
     return pl.pallas_call(
         second_kernel,
-        grid=(mpo_count, rows // row_tile),
-        in_specs=[
-            pl.BlockSpec(memory_space=pltpu.SMEM),
-            pl.BlockSpec((1, phys, 2, row_tile, cols), lambda v, i: (v, 0, 0, i, 0)),
-        ]
-        + [pl.BlockSpec(site.shape, lambda v, i: (0, 0, 0, 0)) for site in sites],
-        out_specs=pl.BlockSpec((1, 2, row_tile, y_rows), lambda v, i: (v, 0, i, 0)),
+        grid=(mpo_count,),
+        in_specs=[pl.BlockSpec(memory_space=pltpu.SMEM), q_spec, q_spec]
+        + [pl.BlockSpec(site.shape, lambda v: (0, 0, 0, 0)) for site in sites],
+        out_specs=pl.BlockSpec((1, 2, rows, y_rows), lambda v: (v, 0, 0, 0)),
         out_shape=jax.ShapeDtypeStruct((mpo_count, 2, rows, y_rows), BF16),
-        compiler_params=params(2),
+        compiler_params=params(1),
         cost_estimate=LIGHT,
         name="second_product",
-    )(pick, q, *sites)
-
-
-def finish_kernel(counts, pick_ref, *refs):
+    )(pick, own, sib, *sites)
+
+
+def finish_kernel(pick_ref, base_ref, *refs):
     out_ref = refs[-1]
-    at = 0
-    for step, sizes in enumerate(counts):
-        parts = []
-        for size in sizes:
-            parts.append(refs[at : at + size])
-            at += size
-
-        @pl.when(pick_ref[0] == step)
-        def _(parts=parts):
-            half = sum(part[0].shape[3] for part in parts)
-            for other, first in ((False, pick_ref[1]), (True, 1 - pick_ref[1])):
-                for number, part in enumerate(parts):
-                    width = part[0].shape[3]
-                    total = sum(one[0, 0].astype(F32) for one in (part[2:] if other else part[:2]))
-                    place = pl.ds(pl.multiple_of(first * half + number * width, width), width)
-                    out_ref[0, 0, :, place] = total
-
-
-def finish(pick, steps):
-    parts = [value for step in steps for part in step for value in part]
-    owners = [number for number, step in enumerate(steps) for part in step for _ in part]
-    mpo_count, _, rows, _ = parts[0].shape
-    cols = 2 * sum(part[0].shape[3] for part in steps[0])
-
-    def spec(value, owner):
+    parts = [refs[at : at + 4] for at in range(0, len(refs) - 1, 4)]
+
+    @pl.when(pick_ref[0] == 0)
+    def _():
+        out_ref[0, 0] = base_ref[0, 0].astype(F32)
+
+    @pl.when(pick_ref[0] != 0)
+    def _():
+        half = sum(part[0].shape[3] for part in parts)
+        for side, first in ((0, pick_ref[1]), (1, 1 - pick_ref[1])):
+            for number, part in enumerate(parts):
+                one, two = part[2 * side : 2 * side + 2]
+                width = one.shape[3]
+                place = pl.ds(pl.multiple_of(first * half + number * width, width), width)
+                out_ref[0, 0, :, place] = one[0, 0].astype(F32) + two[0, 0].astype(F32)
+
+
+def finish(pick, base, parts):
+    addends = [value for part in parts for value in part]
+    mpo_count, _, rows, cols = base.shape
+
+    def spec(value, used):
         def index(v, p, pick):
-            mine = (pick[0] == owner).astype(jnp.int32)
+            mine = (pick[0] == used).astype(jnp.int32)
             return (v * mine, p * mine, 0, 0)
 
         return pl.BlockSpec((1, 1) + value.shape[2:], index)
 
     return pl.pallas_call(
-        functools.partial(finish_kernel, [[len(part) for part in step] for step in steps]),
+        finish_kernel,
         grid_spec=pltpu.PrefetchScalarGridSpec(
             num_scalar_prefetch=1,
             grid=(mpo_count, 2),
-            in_specs=[spec(value, owner) for value, owner in zip(parts, owners)],
+            in_specs=[spec(base, 0)] + [spec(value, 1) for value in addends],
             out_specs=pl.BlockSpec((1, 1, rows, cols), lambda v, p, pick: (v, p, 0, 0)),
         ),
         out_shape=jax.ShapeDtypeStruct((mpo_count, 2, rows, cols), F32),
         compiler_params=params(2),
+        cost_estimate=LIGHT,
         name="finish",
-    )(pick, *parts)
+    )(pick, base, *addends)
 
 
 def after(value, *earlier):
@@ -258,40 +255,57 @@
     blocks = jnp.stack([lax.rem(row - k + row_count, row_count) for k in range(row_count)])
     blocks = after(blocks.astype(jnp.int32), *travelling[0])
     q = first_product(blocks, mpo_mine, site, envs, half, half)
-    q = in_order(q, swap(after(q, travelling[1][0])), 4)
-
-    pick = jnp.stack([lax.rem(row - col * 2 - depth + row_count, row_count), depth]).astype(jnp.int32)
-    steps, gate = [], (q,)
-    for step in range(row_count):
-        goal = [((r - step) % row_count // 2, (r - step) % row_count % 2) for r in range(row_count)]
-
-        def send(value, turned, crossed, cores=(0,)):
-            pairs = []
-            for r, (c, d) in enumerate(goal):
-                for flip in cores:
-                    e = d ^ flip
-                    source = place(r, 1 - c if turned else c, 1 - e if crossed else e)
-                    pairs.append((source, place(r, c, e)))
-            return lax.ppermute(value, axes, pairs)
-
-        if step < row_count - 1:
-            low = second_product(after(pick, *gate), q, travelling[step - 1] if step else parts, half)
-            turned = send(low, True, False, (0, 1))
-            total = (low.astype(F32) + turned.astype(F32)).astype(BF16)
-            steps.append([(low, turned, send(total, False, True))])
-            gate = (low,) + ((travelling[1][0],) if step == 0 else ())
-        else:
-            done = []
-            for number, site in enumerate(travelling[-1]):
-                low = second_product(after(pick, *gate), q, [site], half)
-                done.append(
-                    (low, send(low, True, False), send(low, True, True), send(low, False, True))
-                )
-                gate = (low,) + steps[number][0][1:]
-            steps.append(done)
-        if step == row_count - 2:
-            gate = gate + steps[0][0][1:2]
-    return finish(pick, steps)
+    q_sib = swap(after(q, travelling[1][0]))
+
+    goals = [
+        [((r - step) % row_count // 2, (r - step) % row_count % 2) for r in range(row_count)]
+        for step in range(row_count)
+    ]
+    pick = depth.astype(jnp.int32).reshape(1)
+
+    def second(sites, *earlier):
+        return second_product(after(pick, *earlier), q, q_sib, sites)
+
+    def turn_to_goal(value, goal):
+        return lax.ppermute(
+            value,
+            axes,
+            [(place(r, 1 - c, d), place(r, c, d)) for r, (c, _) in enumerate(goal) for d in range(2)],
+        )
+
+    def send(value, goal, turned, crossed):
+        return lax.ppermute(
+            value,
+            axes,
+            [
+                (place(r, 1 - c if turned else c, 1 - d if crossed else d), place(r, c, d))
+                for r, (c, d) in enumerate(goal)
+            ],
+        )
+
+    step_of = lambda d: lax.rem(row - col * 2 - d + row_count, row_count)
+    lows = [second(parts)]
+    turned = [turn_to_goal(lows[0], goals[0])]
+    lows.append(second(travelling[0], lows[0], travelling[1][1]))
+    turned.append(turn_to_goal(lows[1], goals[1]))
+    lows.append(second(travelling[1], lows[1], turned[0]))
+    turned.append(turn_to_goal(lows[2], goals[2]))
+    totals = [(low.astype(F32) + came.astype(F32)).astype(BF16) for low, came in zip(lows, turned)]
+
+    def total_at(step):
+        return jnp.where(step == 0, totals[0], jnp.where(step == 1, totals[1], totals[2]))
+
+    def last_part(number, *earlier):
+        low = second([travelling[2][number]], *earlier)
+        ways = ((True, False), (True, True), (False, True))
+        return [low] + [send(low, goals[3], *way) for way in ways]
+
+    last = [last_part(0, lows[2])]
+    mine, siblings = total_at(step_of(depth)), total_at(step_of(1 - depth))
+    last.append(last_part(1, *last[0], mine, siblings))
+    base = in_order(mine, swap(after(siblings, last[1][0])), 3)
+    came_last = (step_of(depth) == row_count - 1).astype(jnp.int32)
+    return finish(jnp.stack([came_last, depth.astype(jnp.int32)]), base, last)
 
 
 def solution(mesh):

time: 354 us -> 339 us (0.958)
  other arithmetic: 25.9 us -> 17.6 us
  waiting for transfers between devices: 213 us -> 206 us
    ppermute x12 -> x9, waiting for transfers between devices: 41.9 us -> 28.1 us  [the longest x3 18.5 us: turn_to_goal(): lax.ppermute(value, axes, [(place(r, 1 - c, d), place(r, c, d)) for r, (c...]
    select_n x2, other arithmetic: 17.1 us -> 7.47 us  [ring(): jnp.where(depth == 0, jnp.concatenate([mine, sibling], axis=axis), jnp.co...]
    ppermute x12, waiting for transfers between devices: 161 us -> 168 us  [ring(): lax.ppermute(value, 'row', [(r, (r + 1) % row_count) for r in range(row_c...]
    select_n x0 -> x1, other arithmetic: none -> 4.16 us  [total_at(): jnp.where(step == 0, totals[0], jnp.where(step == 1, totals[1], totals[2]))]
    ppermute x12 -> x9, starting transfers between devices: 19.2 us -> 15.9 us  [the longest x3 8.16 us: turn_to_goal(): lax.ppermute(value, axes, [(place(r, 1 - c, d), place(r, c, d)) for r, (c...]
    unnamed x60 -> x50, local copies, waits for them, and re-layouts: 7.66 us -> 9.77 us
    ppermute x3 -> x4, waiting for transfers between devices: 9.64 us -> 10.1 us  [swap(): return lax.ppermute(value, 'depth', [(0, 1), (1, 0)])]
  transfers between devices with their start and end apart: 28 -> 26, of which waited for: 15 -> 15; matrix products, arithmetic and copies ran while one was open for 8% -> 6% of each run, Pallas kernels for 19% -> 17%
where the time goes in v7:
time: 339 us
  waiting for transfers between devices  206 us (61%)
  Pallas kernels  72.6 us (21%)
  starting transfers between devices  27.4 us (8%)
  other arithmetic  17.6 us (5%)
  local copies, waits for them, and re-layouts  15.3 us (5%)
    ppermute x12, waiting for transfers between devices, ring(): lax.ppermute(value, 'row', [(r, (r + 1) % row_count) for r in range(row_c...  168 us
    pallas_call x5, Pallas kernels, second_product(): pl.pallas_call(second_kernel, grid=(mpo_count,), in_specs=[pl.BlockSpec(m...  41.8 us
    pallas_call x1, Pallas kernels, first_product(): pl.pallas_call(functools.partial(first_kernel, w_local), grid=(rows // ro...  25 us
    ppermute x3, waiting for transfers between devices, turn_to_goal(): lax.ppermute(value, axes, [(place(r, 1 - c, d), place(r, c, d)) for r, (c...  18.5 us
    ppermute x4, waiting for transfers between devices, swap(): return lax.ppermute(value, 'depth', [(0, 1), (1, 0)])  10.1 us
    unnamed x50, local copies, waits for them, and re-layouts  9.77 us
    ppermute x6, waiting for transfers between devices, send(): lax.ppermute(value, axes, [(place(r, 1 - c if turned else c, 1 - d if cro...  9.54 us
    ppermute x3, starting transfers between devices, turn_to_goal(): lax.ppermute(value, axes, [(place(r, 1 - c, d), place(r, c, d)) for r, (c...  8.16 us
  transfers between devices with their start and end apart: 26, of which 15 were waited for; matrix products, arithmetic and copies ran while one was open for 6% of the time, Pallas kernels for 17%

profile of v7, /device:TPU:1, one launch (start us, length us, event | category | flops | bytes accessed | tf_op | source)
XLA Modules:
  0.0 339.0 jit_solution(1189769004207425360)
XLA Ops:
  0.0 1.7 constant_dynamic-slice_fusion.2
  1.7 0.1 collective-permute-start
  1.8 2.7 collective-permute-start.1
  4.6 1.0 copy-done.10
  5.5 3.5 %copy.8 = bf16[2,512,2,1024]{3,1,2,0:T(8,128)(2,1)S(1)} copy(bf16[2,512,2,1024]{3,2,1,0:T(2,128)(2,1)} %param.4) | data formatting | bytes 8388608 | tf_op jit(solution)/shard_map/optimization_barrier | solution.py:164
  9.1 0.0 copy-start.1
  9.1 2.0 copy-done.1
  11.1 0.2 dynamic-slice_bitcast_fusion
  11.3 1.0 copy-done.11
  12.3 2.3 collective-permute-start.5
  14.6 1.2 collective-permute-start.4
  15.8 14.4 %collective-permute-done.1.refs_2_ = bf16[1,2,512,512]{3,2,1,0:T(8,128)(2,1)} collective-permute-done((bf16[1,2,512,512]{3,2,1,0:T(8,128)(2,1)S(1)}, bf16[1,2,512,512]{3,2,1,0:T(8,128)(2,1)}, u32[]{:S(2)}, u32[]{:S(2)}) %collective-permute-start.1) | collective-permute-done | bytes 1048608 | tf_op jit(solution)/shard_map/ppermute | solution.py:227
  30.2 0.0 collective-permute-start.2
  30.2 22.4 %collective-permute-done.5.refs_3_ = bf16[1,2,512,512]{3,2,1,0:T(8,128)(2,1)S(1)} collective-permute-done((bf16[1,2,512,512]{3,2,1,0:T(8,128)(2,1)S(1)}, bf16[1,2,512,512]{3,2,1,0:T(8,128)(2,1)S(1)}, u32[]{:S(2)}, u32[]{:S(2)}) %collective-permute-start.5) | collective-permute-done | bytes 1048608 | tf_op jit(solution)/shard_map/ppermute | solution.py:227
  52.5 22.5 %collective-permute-done.2.refs_4_ = bf16[1,2,512,512]{3,2,1,0:T(8,128)(2,1)S(1)} collective-permute-done((bf16[1,2,512,512]{3,2,1,0:T(8,128)(2,1)}, bf16[1,2,512,512]{3,2,1,0:T(8,128)(2,1)S(1)}, u32[]{:S(2)}, u32[]{:S(2)}) %collective-permute-start.2) | collective-permute-done | bytes 1048608 | tf_op jit(solution)/shard_map/ppermute | solution.py:227
  75.0 0.0 collective-permute-done.4
  75.0 22.5 %collective-permute-done.6.refs_5_ = bf16[1,2,512,512]{3,2,1,0:T(8,128)(2,1)S(1)} collective-permute-done((bf16[1,2,512,512]{3,2,1,0:T(8,128)(2,1)S(1)}, bf16[1,2,512,512]{3,2,1,0:T(8,128)(2,1)S(1)}, u32[]{:S(2)}, u32[]{:S(2)}) %collective-permute-start.6) | collective-permute-done | bytes 1048608 | tf_op jit(solution)/shard_map/ppermute | solution.py:227
  97.5 1.0 copy-done.14
  98.4 0.6 collective-permute-start.7
  99.1 0.2 fusion
  99.3 0.1 collective-permute-start.3
  99.4 0.7 collective-permute-start.9
  100.1 3.1 collective-permute-done.7
  103.2 5.6 %maximum_select_fusion.1 = bf16[1,2,2,512,1024]{4,3,2,1,0:T(8,128)(2,1)S(1)} fusion(bf16[1,2,2,256,1024]{4,3,2,1,0:T(8,128)(2,1)} %bitcast.10, bf16[1,2,2,256,1024]{4,3,2,1,0:T(8,128)(2,1)} %bitcast.9, pred[]{:T(512)S(6)} %eq.23), kind=kLoop, calls=%fused_computation.1 | loop fusion | flops 18874368 | bytes 8388609 | tf_op jit(solution)/shard_map/jit(_where)/select_n | solution.py:231
  108.9 0.0 copy-start.24
  108.9 4.0 %maximum_select_fusion.site_ref = bf16[2,2,2,512,1024]{4,3,2,1,0:T(8,128)(2,1)} fusion(bf16[1,2,2,512,1024]{4,3,2,1,0:T(8,128)(2,1)S(1)} %maximum_select_fusion.1, bf16[1,2,2,512,1024]{4,3,2,1,0:T(8,128)(2,1)S(1)} %bitcast.15, pred[]{:T(512)S(6)} %eq.25), kind=kLoop, calls=%fused_computation | loop fusion | flops 12582912 | bytes 16777216 | tf_op jit(solution)/shard_map/jit(_where)/select_n | solution.py:248
  112.9 13.2 %collective-permute-done.3.refs_6_ = bf16[1,2,512,512]{3,2,1,0:T(8,128)(2,1)S(1)} collective-permute-done((bf16[1,2,512,512]{3,2,1,0:T(8,128)(2,1)}, bf16[1,2,512,512]{3,2,1,0:T(8,128)(2,1)S(1)}, u32[]{:S(2)}, u32[]{:S(2)}) %collective-permute-start.3) | collective-permute-done | bytes 1048608 | tf_op jit(solution)/shard_map/ppermute | solution.py:227
  126.2 22.5 %collective-permute-done.9.refs_7_ = bf16[1,2,512,512]{3,2,1,0:T(8,128)(2,1)S(1)} collective-permute-done((bf16[1,2,512,512]{3,2,1,0:T(8,128)(2,1)}, bf16[1,2,512,512]{3,2,1,0:T(8,128)(2,1)S(1)}, u32[]{:S(2)}, u32[]{:S(2)}) %collective-permute-start.9) | collective-permute-done | bytes 1048608 | tf_op jit(solution)/shard_map/ppermute | solution.py:227
  148.6 1.0 copy-done.19
  149.6 21.5 %collective-permute-done.8.refs_0_ = bf16[2,2,128,1024]{3,2,1,0:T(8,128)(2,1)S(1)} collective-permute-done((bf16[2,2,128,1024]{3,2,1,0:T(8,128)(2,1)S(1)}, bf16[2,2,128,1024]{3,2,1,0:T(8,128)(2,1)S(1)}, u32[]{:S(2)}, u32[]{:S(2)}) %collective-permute-start.8) | collective-permute-done | bytes 1048608 | tf_op jit(solution)/shard_map/ppermute | solution.py:227
  171.1 0.8 pad_add_fusion.1.block_ref
  171.9 0.6 pad_maximum_fusion.mpo_ref
  172.5 21.1 %collective-permute-done.10.refs_1_ = bf16[2,2,128,1024]{3,2,1,0:T(8,128)(2,1)S(1)} collective-permute-done((bf16[2,2,128,1024]{3,2,1,0:T(8,128)(2,1)S(1)}, bf16[2,2,128,1024]{3,2,1,0:T(8,128)(2,1)S(1)}, u32[]{:S(2)}, u32[]{:S(2)}) %collective-permute-start.10) | collective-permute-done | bytes 1048608 | tf_op jit(solution)/shard_map/ppermute | solution.py:227
  193.6 25.0 %first_product.1.own_ref = bf16[2,2,2,512,512]{4,3,2,1,0:T(8,128)(2,1)} custom-call(s32[4]{0:T(128)} %pad_add_fusion.1.block_ref, f32[2,2,2,2]{3,2,1,0:T(2,128)} %pad_maximum_fusion.mpo_ref, bf16[2,2,2,512,1024]{4,3,2,1,0:T(8,128)(2,1)} %maximum_select_fusion.site_ref, bf16[1,2,512,512]{3,2,1,0:T(8,128)(2,1)} %copy-done.3, ...), custom_call_target="tpu_custom_call" | custom-call | tf_op jit(solution)/shard_map/first_product/pallas_call | solution.py:67
  218.6 1.2 collective-permute-start.12
  219.8 7.0 %collective-permute-done.12.sib_ref = bf16[2,2,2,512,512]{4,3,2,1,0:T(8,128)(2,1)S(1)} collective-permute-done((bf16[2,2,2,512,512]{4,3,2,1,0:T(8,128)(2,1)}, bf16[2,2,2,512,512]{4,3,2,1,0:T(8,128)(2,1)S(1)}, u32[]{:S(2)}, u32[]{:S(2)}) %collective-permute-start.12) | collective-permute-done | bytes 4194336 | tf_op jit(solution)/shard_map/ppermute | solution.py:168
  226.8 2.0 copy-done
  228.8 8.4 %second_product.5 = bf16[2,2,512,256]{3,2,1,0:T(8,128)(2,1)} custom-call(s32[1]{0:T(128)} %bitcast.1.pick_ref, bf16[2,2,2,512,512]{4,3,2,1,0:T(8,128)(2,1)} %first_product.1.own_ref, bf16[2,2,2,512,512]{4,3,2,1,0:T(8,128)(2,1)} %copy-done, bf16[2,2,128,1024]{3,2,1,0:T(8,128)(2,1)} %copy-done.9, bf16[2,2,128,1024]{3,2,1,0:T(8,128)(2,1)} %copy-done.8), custom_call_target="tpu_custom_call" | custom-call | tf_op jit(solution)/shard_map/second_product/pallas_call | solution.py:105
  237.2 1.3 collective-permute-start.13
  238.5 0.2 collective-permute-start.17
  238.7 7.6 %collective-permute-done.14.refs_1_ = bf16[2,2,128,1024]{3,2,1,0:T(8,128)(2,1)S(1)} collective-permute-done((bf16[2,2,128,1024]{3,2,1,0:T(8,128)(2,1)S(1)}, bf16[2,2,128,1024]{3,2,1,0:T(8,128)(2,1)S(1)}, u32[]{:S(2)}, u32[]{:S(2)}) %collective-permute-start.14) | collective-permute-done | bytes 1048608 | tf_op jit(solution)/shard_map/ppermute | solution.py:227
  246.3 8.8 %second_product.6 = bf16[2,2,512,256]{3,2,1,0:T(8,128)(2,1)} custom-call(s32[1]{0:T(128)} %bitcast.1.pick_ref, bf16[2,2,2,512,512]{4,3,2,1,0:T(8,128)(2,1)} %first_product.1.own_ref, bf16[2,2,2,512,512]{4,3,2,1,0:T(8,128)(2,1)} %copy-done, bf16[2,2,128,1024]{3,2,1,0:T(8,128)(2,1)} %copy-done.15, bf16[2,2,128,1024]{3,2,1,0:T(8,128)(2,1)} %copy-done.16), custom_call_target="tpu_custom_call" | custom-call | tf_op jit(solution)/shard_map/second_product/pallas_call | solution.py:105
  255.1 4.1 %collective-permute-start.15 = (bf16[2,2,512,256]{3,2,1,0:T(8,128)(2,1)}, bf16[2,2,512,256]{3,2,1,0:T(8,128)(2,1)}, u32[]{:S(2)}, u32[]{:S(2)}) collective-permute-start(bf16[2,2,512,256]{3,2,1,0:T(8,128)(2,1)} %second_product.6), channel_id=1, source_target_pairs={{0,2},{1,3},{6,4},{7,5},{10,8},{11,9},{12,14},{13,15},{16,18},{17,... | collective-permute-start | bytes 3145736 | tf_op jit(solution)/shard_map/ppermute | solution.py:270
  259.2 4.4 %collective-permute-done.13 = bf16[2,2,512,256]{3,2,1,0:T(8,128)(2,1)S(1)} collective-permute-done((bf16[2,2,512,256]{3,2,1,0:T(8,128)(2,1)}, bf16[2,2,512,256]{3,2,1,0:T(8,128)(2,1)S(1)}, u32[]{:S(2)}, u32[]{:S(2)}) %collective-permute-start.13) | collective-permute-done | bytes 1048608 | tf_op jit(solution)/shard_map/ppermute | solution.py:270
  263.6 8.8 %second_product.7 = bf16[2,2,512,256]{3,2,1,0:T(8,128)(2,1)} custom-call(s32[1]{0:T(128)} %bitcast.1.pick_ref, bf16[2,2,2,512,512]{4,3,2,1,0:T(8,128)(2,1)} %first_product.1.own_ref, bf16[2,2,2,512,512]{4,3,2,1,0:T(8,128)(2,1)} %copy-done, bf16[2,2,128,1024]{3,2,1,0:T(8,128)(2,1)} %collective-permute-done.11.refs_0_, bf16[2,2,128,1024]{3,2,1,0:T(8,128)(2,1)} %copy-done.18), custom_call_target="tpu_custom_call" | custom-call | tf_op jit(solution)/shard_map/second_product/pallas_call | solution.py:105
  272.4 2.7 collective-permute-start.16
  275.2 1.0 copy-done.21
  276.1 7.9 %second_product.8.refs_0_ = bf16[2,2,512,128]{3,2,1,0:T(8,128)(2,1)} custom-call(s32[1]{0:T(128)} %bitcast.1.pick_ref, bf16[2,2,2,512,512]{4,3,2,1,0:T(8,128)(2,1)} %first_product.1.own_ref, bf16[2,2,2,512,512]{4,3,2,1,0:T(8,128)(2,1)} %copy-done, bf16[2,2,128,1024]{3,2,1,0:T(8,128)(2,1)} %copy-done.21), custom_call_target="tpu_custom_call" | custom-call | tf_op jit(solution)/shard_map/second_product/pallas_call | solution.py:105
  284.1 1.3 collective-permute-start.18
  285.3 1.3 collective-permute-start.19
  286.6 1.3 collective-permute-start.20
  288.0 14.1 %collective-permute-done.16 = bf16[2,2,512,256]{3,2,1,0:T(8,128)(2,1)} collective-permute-done((bf16[2,2,512,256]{3,2,1,0:T(8,128)(2,1)}, bf16[2,2,512,256]{3,2,1,0:T(8,128)(2,1)}, u32[]{:S(2)}, u32[]{:S(2)}) %collective-permute-start.16) | collective-permute-done | bytes 1048608 | tf_op jit(solution)/shard_map/ppermute | solution.py:270
  302.1 4.2 %select_select_fusion.1 = (bf16[2,2,512,256]{3,2,1,0:T(8,128)(2,1)}, bf16[2,2,512,256]{3,2,1,0:T(8,128)(2,1)}) fusion(pred[]{:T(512)S(6)} %eq.26, pred[]{:T(512)S(6)} %eq.24, bf16[2,2,512,256]{3,2,1,0:T(8,128)(2,1)} %copy-done.20, bf16[2,2,512,256]{3,2,1,0:T(8,128)(2,1)S(1)} %copy-done.4, bf16[2,2,512,256]{3,2,1,0:T(8,128)(2,1)} %collective-permute-done.15, ...), kind=kLoop, calls=%fused_computation.8 | loop fusion | flops 8388608 | bytes 8388612 | tf_op jit(solution)/shard_map/jit(_where)/select_n | solution.py:296
  306.3 8.0 %second_product.9.refs_4_ = bf16[2,2,512,128]{3,2,1,0:T(8,128)(2,1)} custom-call(s32[1]{0:T(128)} %bitcast.1.pick_ref, bf16[2,2,2,512,512]{4,3,2,1,0:T(8,128)(2,1)} %first_product.1.own_ref, bf16[2,2,2,512,512]{4,3,2,1,0:T(8,128)(2,1)} %copy-done, bf16[2,2,128,1024]{3,2,1,0:T(8,128)(2,1)} %collective-permute-done.21.refs_0_), custom_call_target="tpu_custom_call" | custom-call | tf_op jit(solution)/shard_map/second_product/pallas_call | solution.py:105
  314.3 2.2 collective-permute-start.22
  316.5 1.3 collective-permute-start.23
  317.8 1.3 collective-permute-start.24
  319.1 1.3 collective-permute-start.25
  320.4 0.6 pad_add_fusion.pick_ref
  321.0 1.8 maximum_select_fusion.2.base_ref
  322.8 7.7 %collective-permute-done.23.refs_5_ = bf16[2,2,512,128]{3,2,1,0:T(8,128)(2,1)S(1)} collective-permute-done((bf16[2,2,512,128]{3,2,1,0:T(8,128)(2,1)}, bf16[2,2,512,128]{3,2,1,0:T(8,128)(2,1)S(1)}, u32[]{:S(2)}, u32[]{:S(2)}) %collective-permute-start.23) | collective-permute-done | bytes 524320 | tf_op jit(solution)/shard_map/ppermute | solution.py:277
  330.6 1.8 collective-permute-done.24.refs_6_
  332.4 0.8 copy-done.23
  333.2 5.8 %finish.1 = f32[2,2,512,512]{3,2,1,0:T(8,128)} custom-call(s32[2]{0:T(128)} %pad_add_fusion.pick_ref, bf16[2,2,512,512]{3,2,1,0:T(8,128)(2,1)} %maximum_select_fusion.2.base_ref, bf16[2,2,512,128]{3,2,1,0:T(8,128)(2,1)} %second_product.8.refs_0_, bf16[2,2,512,128]{3,2,1,0:T(8,128)(2,1)} %collective-permute-done.18.refs_1_, ...), custom_call_target="tpu_custom_call" | custom-call | tf_op jit(solution)/shard_map/finish/pallas_call | solution.py:148
  (57 shorter events, 0.1 us)
Async XLA Ops:
  1.7 7.4 %copy-start.3 = (bf16[1,2,512,512]{3,2,1,0:T(8,128)(2,1)}, bf16[1,2,512,512]{3,2,1,0:T(8,128)(2,1)S(1)}, u32[]{:S(2)}) copy-start(bf16[1,2,512,512]{3,2,1,0:T(8,128)(2,1)S(1)} %get-tuple-element.33.refs_0_) | copy-start | bytes 3145732
  1.7 2.9 collective-permute-start
  1.8 28.3 %collective-permute-start.1 = (bf16[1,2,512,512]{3,2,1,0:T(8,128)(2,1)S(1)}, bf16[1,2,512,512]{3,2,1,0:T(8,128)(2,1)}, u32[]{:S(2)}, u32[]{:S(2)}) collective-permute-start(bf16[1,2,512,512]{3,2,1,0:T(8,128)(2,1)S(1)} %get-tuple-element.33.refs_0_), channel_id=1, source_target_pairs={{0,4},{4,8},{8,12},{12,0},{1,5},{5,9},{9,13},{13,1},{2,6},{6,10},{... | collective-permute-start | bytes 3145736 | tf_op jit(solution)/shard_map/ppermute | solution.py:227
  4.6 1.0 copy-start.10
  9.1 2.0 copy-start.1
  11.1 1.2 copy-start.11
  12.3 40.2 %collective-permute-start.5 = (bf16[1,2,512,512]{3,2,1,0:T(8,128)(2,1)S(1)}, bf16[1,2,512,512]{3,2,1,0:T(8,128)(2,1)S(1)}, u32[]{:S(2)}, u32[]{:S(2)}) collective-permute-start(bf16[1,2,512,512]{3,2,1,0:T(8,128)(2,1)S(1)} %copy-done.11), channel_id=1, source_target_pairs={{0,4},{4,8},{8,12},{12,0},{1,5},{5,9},{9,13},{13,1},{2,6},{6,10},{... | collective-permute-start | bytes 3145736 | tf_op jit(solution)/shard_map/ppermute | solution.py:227
  14.6 60.4 %collective-permute-start.4 = (bf16[2,2,256,1024]{3,2,1,0:T(8,128)(2,1)S(1)}, bf16[2,2,256,1024]{3,2,1,0:T(8,128)(2,1)}, u32[]{:S(2)}, u32[]{:S(2)}) collective-permute-start(bf16[2,2,256,1024]{3,2,1,0:T(8,128)(2,1)S(1)} %dynamic-slice_bitcast_fusion), channel_id=1, source_target_pairs={{0,2},{2,0},{1,3},{3,1},{4,6},{6,4},{5,7},{7,5},{8,10},{10,8},{9,1... | collective-permute-start | bytes 6291464 | tf_op jit(solution)/shard_map/ppermute | solution.py:230
  30.2 44.8 %collective-permute-start.2 = (bf16[1,2,512,512]{3,2,1,0:T(8,128)(2,1)}, bf16[1,2,512,512]{3,2,1,0:T(8,128)(2,1)S(1)}, u32[]{:S(2)}, u32[]{:S(2)}) collective-permute-start(bf16[1,2,512,512]{3,2,1,0:T(8,128)(2,1)} %collective-permute-done.1.refs_2_), channel_id=1, source_target_pairs={{0,4},{4,8},{8,12},{12,0},{1,5},{5,9},{9,13},{13,1},{2,6},{6,10},{... | collective-permute-start | bytes 3145736 | tf_op jit(solution)/shard_map/ppermute | solution.py:227
  52.5 22.5 %copy-start.12 = (bf16[1,2,512,512]{3,2,1,0:T(8,128)(2,1)}, bf16[1,2,512,512]{3,2,1,0:T(8,128)(2,1)S(1)}, u32[]{:S(2)}) copy-start(bf16[1,2,512,512]{3,2,1,0:T(8,128)(2,1)S(1)} %collective-permute-done.5.refs_3_) | copy-start | bytes 3145732
  52.5 44.9 %collective-permute-start.6 = (bf16[1,2,512,512]{3,2,1,0:T(8,128)(2,1)S(1)}, bf16[1,2,512,512]{3,2,1,0:T(8,128)(2,1)S(1)}, u32[]{:S(2)}, u32[]{:S(2)}) collective-permute-start(bf16[1,2,512,512]{3,2,1,0:T(8,128)(2,1)S(1)} %collective-permute-done.5.refs_3_), channel_id=1, source_target_pairs={{0,4},{4,8},{8,12},{12,0},{1,5},{5,9},{9,13},{13,1},{2,6},{6,10},{... | collective-permute-start | bytes 3145736 | tf_op jit(solution)/shard_map/ppermute | solution.py:227
  75.0 22.5 %copy-start.13 = (bf16[1,2,512,512]{3,2,1,0:T(8,128)(2,1)}, bf16[1,2,512,512]{3,2,1,0:T(8,128)(2,1)S(1)}, u32[]{:S(2)}) copy-start(bf16[1,2,512,512]{3,2,1,0:T(8,128)(2,1)S(1)} %collective-permute-done.2.refs_4_) | copy-start | bytes 3145732
  97.5 1.0 copy-start.14
  98.4 4.8 %collective-permute-start.7 = (bf16[2,2,256,1024]{3,2,1,0:T(8,128)(2,1)}, bf16[2,2,256,1024]{3,2,1,0:T(8,128)(2,1)}, u32[]{:S(2)}, u32[]{:S(2)}) collective-permute-start(bf16[2,2,256,1024]{3,2,1,0:T(8,128)(2,1)} %collective-permute-done.4), channel_id=1, source_target_pairs={{0,1},{1,0},{2,3},{3,2},{4,5},{5,4},{6,7},{7,6},{8,9},{9,8},{10,11... | collective-permute-start | bytes 6291464 | tf_op jit(solution)/shard_map/ppermute | solution.py:168
  99.3 26.9 %copy-start.9 = (bf16[2,2,128,1024]{3,2,1,0:T(8,128)(2,1)}, bf16[2,2,128,1024]{3,2,1,0:T(8,128)(2,1)S(1)}, u32[]{:S(2)}) copy-start(bf16[2,2,128,1024]{3,2,1,0:T(8,128)(2,1)S(1)} %get-tuple-element.18.refs_0_) | copy-start | bytes 3145732
  99.3 50.3 %copy-start.8 = (bf16[2,2,128,1024]{3,2,1,0:T(8,128)(2,1)}, bf16[2,2,128,1024]{3,2,1,0:T(8,128)(2,1)S(1)}, u32[]{:S(2)}) copy-start(bf16[2,2,128,1024]{3,2,1,0:T(8,128)(2,1)S(1)} %get-tuple-element.19.refs_1_) | copy-start | bytes 3145732
  99.3 26.9 %collective-permute-start.3 = (bf16[1,2,512,512]{3,2,1,0:T(8,128)(2,1)}, bf16[1,2,512,512]{3,2,1,0:T(8,128)(2,1)S(1)}, u32[]{:S(2)}, u32[]{:S(2)}) collective-permute-start(bf16[1,2,512,512]{3,2,1,0:T(8,128)(2,1)} %copy-done.13), channel_id=1, source_target_pairs={{0,4},{4,8},{8,12},{12,0},{1,5},{5,9},{9,13},{13,1},{2,6},{6,10},{... | collective-permute-start | bytes 3145736 | tf_op jit(solution)/shard_map/ppermute | solution.py:227
  99.4 49.3 %collective-permute-start.9 = (bf16[1,2,512,512]{3,2,1,0:T(8,128)(2,1)}, bf16[1,2,512,512]{3,2,1,0:T(8,128)(2,1)S(1)}, u32[]{:S(2)}, u32[]{:S(2)}) collective-permute-start(bf16[1,2,512,512]{3,2,1,0:T(8,128)(2,1)} %copy-done.14), channel_id=1, source_target_pairs={{0,4},{4,8},{8,12},{12,0},{1,5},{5,9},{9,13},{13,1},{2,6},{6,10},{... | collective-permute-start | bytes 3145736 | tf_op jit(solution)/shard_map/ppermute | solution.py:227
  103.2 5.7 %copy-start.2 = (bf16[2,512,2,1024]{3,1,2,0:T(8,128)(2,1)S(1)}, bf16[2,512,2,1024]{3,1,2,0:T(8,128)(2,1)}, u32[]{:S(2)}) copy-start(bf16[2,512,2,1024]{3,1,2,0:T(8,128)(2,1)} %copy-done.1) | copy-start | bytes 12582916
  108.9 63.0 %copy-start.24 = (f32[2,2,2,2]{3,2,1,0:T(2,128)S(1)}, f32[2,2,2,2]{3,2,1,0:T(2,128)}, u32[]{:S(2)}) copy-start(f32[2,2,2,2]{3,2,1,0:T(2,128)} %param.5) | copy-start | bytes 196
  126.2 44.9 %copy-start.17 = (bf16[1,2,512,512]{3,2,1,0:T(8,128)(2,1)}, bf16[1,2,512,512]{3,2,1,0:T(8,128)(2,1)S(1)}, u32[]{:S(2)}) copy-start(bf16[1,2,512,512]{3,2,1,0:T(8,128)(2,1)S(1)} %collective-permute-done.3.refs_6_) | copy-start | bytes 3145732
  126.2 44.9 %collective-permute-start.8 = (bf16[2,2,128,1024]{3,2,1,0:T(8,128)(2,1)S(1)}, bf16[2,2,128,1024]{3,2,1,0:T(8,128)(2,1)S(1)}, u32[]{:S(2)}, u32[]{:S(2)}) collective-permute-start(bf16[2,2,128,1024]{3,2,1,0:T(8,128)(2,1)S(1)} %get-tuple-element.18.refs_0_), channel_id=1, source_target_pairs={{0,4},{4,8},{8,12},{12,0},{1,5},{5,9},{9,13},{13,1},{2,6},{6,10},{... | collective-permute-start | bytes 3145736 | tf_op jit(solution)/shard_map/ppermute | solution.py:227
  148.6 1.0 copy-start.19
  149.6 44.0 %collective-permute-start.10 = (bf16[2,2,128,1024]{3,2,1,0:T(8,128)(2,1)S(1)}, bf16[2,2,128,1024]{3,2,1,0:T(8,128)(2,1)S(1)}, u32[]{:S(2)}, u32[]{:S(2)}) collective-permute-start(bf16[2,2,128,1024]{3,2,1,0:T(8,128)(2,1)S(1)} %get-tuple-element.19.refs_1_), channel_id=1, source_target_pairs={{0,4},{4,8},{8,12},{12,0},{1,5},{5,9},{9,13},{13,1},{2,6},{6,10},{... | collective-permute-start | bytes 3145736 | tf_op jit(solution)/shard_map/ppermute | solution.py:227
  171.1 47.4 %copy-start.15 = (bf16[2,2,128,1024]{3,2,1,0:T(8,128)(2,1)}, bf16[2,2,128,1024]{3,2,1,0:T(8,128)(2,1)S(1)}, u32[]{:S(2)}) copy-start(bf16[2,2,128,1024]{3,2,1,0:T(8,128)(2,1)S(1)} %collective-permute-done.8.refs_0_) | copy-start | bytes 3145732
  171.1 47.4 %collective-permute-start.11 = (bf16[2,2,128,1024]{3,2,1,0:T(8,128)(2,1)S(1)}, bf16[2,2,128,1024]{3,2,1,0:T(8,128)(2,1)}, u32[]{:S(2)}, u32[]{:S(2)}) collective-permute-start(bf16[2,2,128,1024]{3,2,1,0:T(8,128)(2,1)S(1)} %collective-permute-done.8.refs_0_), channel_id=1, source_target_pairs={{0,4},{4,8},{8,12},{12,0},{1,5},{5,9},{9,13},{13,1},{2,6},{6,10},{... | collective-permute-start | bytes 3145736 | tf_op jit(solution)/shard_map/ppermute | solution.py:227
  193.6 26.2 %copy-start.16 = (bf16[2,2,128,1024]{3,2,1,0:T(8,128)(2,1)}, bf16[2,2,128,1024]{3,2,1,0:T(8,128)(2,1)S(1)}, u32[]{:S(2)}) copy-start(bf16[2,2,128,1024]{3,2,1,0:T(8,128)(2,1)S(1)} %collective-permute-done.10.refs_1_) | copy-start | bytes 3145732
  218.6 8.2 %collective-permute-start.12 = (bf16[2,2,2,512,512]{4,3,2,1,0:T(8,128)(2,1)}, bf16[2,2,2,512,512]{4,3,2,1,0:T(8,128)(2,1)S(1)}, u32[]{:S(2)}, u32[]{:S(2)}) collective-permute-start(bf16[2,2,2,512,512]{4,3,2,1,0:T(8,128)(2,1)} %first_product.1.own_ref), channel_id=1, source_target_pairs={{0,1},{1,0},{2,3},{3,2},{4,5},{5,4},{6,7},{7,6},{8,9},{9,8},{10,11... | collective-permute-start | bytes 12582920 | tf_op jit(solution)/shard_map/ppermute | solution.py:168
  219.8 26.5 %collective-permute-start.14 = (bf16[2,2,128,1024]{3,2,1,0:T(8,128)(2,1)S(1)}, bf16[2,2,128,1024]{3,2,1,0:T(8,128)(2,1)S(1)}, u32[]{:S(2)}, u32[]{:S(2)}) collective-permute-start(bf16[2,2,128,1024]{3,2,1,0:T(8,128)(2,1)S(1)} %collective-permute-done.10.refs_1_), channel_id=1, source_target_pairs={{0,4},{4,8},{8,12},{12,0},{1,5},{5,9},{9,13},{13,1},{2,6},{6,10},{... | collective-permute-start | bytes 3145736 | tf_op jit(solution)/shard_map/ppermute | solution.py:227
  226.8 2.0 copy-start
  237.2 26.5 %collective-permute-start.13 = (bf16[2,2,512,256]{3,2,1,0:T(8,128)(2,1)}, bf16[2,2,512,256]{3,2,1,0:T(8,128)(2,1)S(1)}, u32[]{:S(2)}, u32[]{:S(2)}) collective-permute-start(bf16[2,2,512,256]{3,2,1,0:T(8,128)(2,1)} %second_product.5), channel_id=1, source_target_pairs={{2,0},{3,1},{6,4},{7,5},{8,10},{9,11},{12,14},{13,15},{18,16},{19,... | collective-permute-start | bytes 3145736 | tf_op jit(solution)/shard_map/ppermute | solution.py:270
  238.5 36.7 %collective-permute-start.17 = (bf16[2,2,128,1024]{3,2,1,0:T(8,128)(2,1)}, bf16[2,2,128,1024]{3,2,1,0:T(8,128)(2,1)S(1)}, u32[]{:S(2)}, u32[]{:S(2)}) collective-permute-start(bf16[2,2,128,1024]{3,2,1,0:T(8,128)(2,1)} %collective-permute-done.11.refs_0_), channel_id=1, source_target_pairs={{0,4},{4,8},{8,12},{12,0},{1,5},{5,9},{9,13},{13,1},{2,6},{6,10},{... | collective-permute-start | bytes 3145736 | tf_op jit(solution)/shard_map/ppermute | solution.py:227
  246.3 17.3 %copy-start.18 = (bf16[2,2,128,1024]{3,2,1,0:T(8,128)(2,1)}, bf16[2,2,128,1024]{3,2,1,0:T(8,128)(2,1)S(1)}, u32[]{:S(2)}) copy-start(bf16[2,2,128,1024]{3,2,1,0:T(8,128)(2,1)S(1)} %collective-permute-done.14.refs_1_) | copy-start | bytes 3145732
  255.1 31.6 %collective-permute-start.15 = (bf16[2,2,512,256]{3,2,1,0:T(8,128)(2,1)}, bf16[2,2,512,256]{3,2,1,0:T(8,128)(2,1)}, u32[]{:S(2)}, u32[]{:S(2)}) collective-permute-start(bf16[2,2,512,256]{3,2,1,0:T(8,128)(2,1)} %second_product.6), channel_id=1, source_target_pairs={{0,2},{1,3},{6,4},{7,5},{10,8},{11,9},{12,14},{13,15},{16,18},{17,... | collective-permute-start | bytes 3145736 | tf_op jit(solution)/shard_map/ppermute | solution.py:270
  263.6 8.8 %copy-start.20 = (bf16[2,2,512,256]{3,2,1,0:T(8,128)(2,1)}, bf16[2,2,512,256]{3,2,1,0:T(8,128)(2,1)S(1)}, u32[]{:S(2)}) copy-start(bf16[2,2,512,256]{3,2,1,0:T(8,128)(2,1)S(1)} %collective-permute-done.13) | copy-start | bytes 3145732
  272.4 29.7 %copy-start.4 = (bf16[2,2,512,256]{3,2,1,0:T(8,128)(2,1)S(1)}, bf16[2,2,512,256]{3,2,1,0:T(8,128)(2,1)}, u32[]{:S(2)}) copy-start(bf16[2,2,512,256]{3,2,1,0:T(8,128)(2,1)} %second_product.5) | copy-start | bytes 3145732
  272.4 29.7 %copy-start.5 = (bf16[2,2,512,256]{3,2,1,0:T(8,128)(2,1)S(1)}, bf16[2,2,512,256]{3,2,1,0:T(8,128)(2,1)}, u32[]{:S(2)}) copy-start(bf16[2,2,512,256]{3,2,1,0:T(8,128)(2,1)} %second_product.6) | copy-start | bytes 3145732
  272.4 29.6 %copy-start.6 = (bf16[2,2,512,256]{3,2,1,0:T(8,128)(2,1)S(1)}, bf16[2,2,512,256]{3,2,1,0:T(8,128)(2,1)}, u32[]{:S(2)}) copy-start(bf16[2,2,512,256]{3,2,1,0:T(8,128)(2,1)} %second_product.7) | copy-start | bytes 3145732
  272.4 29.6 %collective-permute-start.16 = (bf16[2,2,512,256]{3,2,1,0:T(8,128)(2,1)}, bf16[2,2,512,256]{3,2,1,0:T(8,128)(2,1)}, u32[]{:S(2)}, u32[]{:S(2)}) collective-permute-start(bf16[2,2,512,256]{3,2,1,0:T(8,128)(2,1)} %second_product.7), channel_id=1, source_target_pairs={{0,2},{1,3},{4,6},{5,7},{10,8},{11,9},{14,12},{15,13},{16,18},{17,... | collective-permute-start | bytes 3145736 | tf_op jit(solution)/shard_map/ppermute | solution.py:270
  275.2 31.1 %collective-permute-start.21 = (bf16[2,2,128,1024]{3,2,1,0:T(8,128)(2,1)}, bf16[2,2,128,1024]{3,2,1,0:T(8,128)(2,1)}, u32[]{:S(2)}, u32[]{:S(2)}) collective-permute-start(bf16[2,2,128,1024]{3,2,1,0:T(8,128)(2,1)} %copy-done.18), channel_id=1, source_target_pairs={{0,4},{4,8},{8,12},{12,0},{1,5},{5,9},{9,13},{13,1},{2,6},{6,10},{... | collective-permute-start | bytes 3145736 | tf_op jit(solution)/shard_map/ppermute | solution.py:227
  275.2 1.0 copy-start.21
  284.1 22.2 %collective-permute-start.18 = (bf16[2,2,512,128]{3,2,1,0:T(8,128)(2,1)}, bf16[2,2,512,128]{3,2,1,0:T(8,128)(2,1)}, u32[]{:S(2)}, u32[]{:S(2)}) collective-permute-start(bf16[2,2,512,128]{3,2,1,0:T(8,128)(2,1)} %second_product.8.refs_0_), channel_id=1, source_target_pairs={{3,1},{4,6},{9,11},{14,12},{19,17},{20,22},{25,27},{30,28}} | collective-permute-start | bytes 1572872 | tf_op jit(solution)/shard_map/ppermute | solution.py:277
  285.3 20.9 %collective-permute-start.19 = (bf16[2,2,512,128]{3,2,1,0:T(8,128)(2,1)}, bf16[2,2,512,128]{3,2,1,0:T(8,128)(2,1)}, u32[]{:S(2)}, u32[]{:S(2)}) collective-permute-start(bf16[2,2,512,128]{3,2,1,0:T(8,128)(2,1)} %second_product.8.refs_0_), channel_id=1, source_target_pairs={{2,1},{5,6},{8,11},{15,12},{18,17},{21,22},{24,27},{31,28}} | collective-permute-start | bytes 1572872 | tf_op jit(solution)/shard_map/ppermute | solution.py:277
  286.6 19.6 %collective-permute-start.20 = (bf16[2,2,512,128]{3,2,1,0:T(8,128)(2,1)}, bf16[2,2,512,128]{3,2,1,0:T(8,128)(2,1)}, u32[]{:S(2)}, u32[]{:S(2)}) collective-permute-start(bf16[2,2,512,128]{3,2,1,0:T(8,128)(2,1)} %second_product.8.refs_0_), channel_id=1, source_target_pairs={{0,1},{7,6},{10,11},{13,12},{16,17},{23,22},{26,27},{29,28}} | collective-permute-start | bytes 1572872 | tf_op jit(solution)/shard_map/ppermute | solution.py:277
  306.3 14.8 %copy-start.7 = (bf16[2,2,512,256]{3,2,1,0:T(8,128)(2,1)S(1)}, bf16[2,2,512,256]{3,2,1,0:T(8,128)(2,1)}, u32[]{:S(2)}) copy-start(bf16[2,2,512,256]{3,2,1,0:T(8,128)(2,1)} %get-tuple-element.27) | copy-start | bytes 3145732
  314.3 6.7 %collective-permute-start.22 = (bf16[2,2,512,256]{3,2,1,0:T(8,128)(2,1)}, bf16[2,2,512,256]{3,2,1,0:T(8,128)(2,1)S(1)}, u32[]{:S(2)}, u32[]{:S(2)}) collective-permute-start(bf16[2,2,512,256]{3,2,1,0:T(8,128)(2,1)} %get-tuple-element.26), channel_id=1, source_target_pairs={{0,1},{1,0},{2,3},{3,2},{4,5},{5,4},{6,7},{7,6},{8,9},{9,8},{10,11... | collective-permute-start | bytes 3145736 | tf_op jit(solution)/shard_map/ppermute | solution.py:168
  316.5 14.1 %collective-permute-start.23 = (bf16[2,2,512,128]{3,2,1,0:T(8,128)(2,1)}, bf16[2,2,512,128]{3,2,1,0:T(8,128)(2,1)S(1)}, u32[]{:S(2)}, u32[]{:S(2)}) collective-permute-start(bf16[2,2,512,128]{3,2,1,0:T(8,128)(2,1)} %second_product.9.refs_4_), channel_id=1, source_target_pairs={{3,1},{4,6},{9,11},{14,12},{19,17},{20,22},{25,27},{30,28}} | collective-permute-start | bytes 1572872 | tf_op jit(solution)/shard_map/ppermute | solution.py:277
  317.8 14.6 %collective-permute-start.24 = (bf16[2,2,512,128]{3,2,1,0:T(8,128)(2,1)}, bf16[2,2,512,128]{3,2,1,0:T(8,128)(2,1)S(1)}, u32[]{:S(2)}, u32[]{:S(2)}) collective-permute-start(bf16[2,2,512,128]{3,2,1,0:T(8,128)(2,1)} %second_product.9.refs_4_), channel_id=1, source_target_pairs={{2,1},{5,6},{8,11},{15,12},{18,17},{21,22},{24,27},{31,28}} | collective-permute-start | bytes 1572872 | tf_op jit(solution)/shard_map/ppermute | solution.py:277
  319.1 13.3 %collective-permute-start.25 = (bf16[2,2,512,128]{3,2,1,0:T(8,128)(2,1)}, bf16[2,2,512,128]{3,2,1,0:T(8,128)(2,1)}, u32[]{:S(2)}, u32[]{:S(2)}) collective-permute-start(bf16[2,2,512,128]{3,2,1,0:T(8,128)(2,1)} %second_product.9.refs_4_), channel_id=1, source_target_pairs={{0,1},{7,6},{10,11},{13,12},{16,17},{23,22},{26,27},{29,28}} | collective-permute-start | bytes 1572872 | tf_op jit(solution)/shard_map/ppermute | solution.py:277
  330.6 1.8 copy-start.22
  332.4 0.8 copy-start.23

commit v8 on v7

--- a/solution.py
+++ b/solution.py
@@ -115,33 +115,35 @@
     )(pick, own, sib, *sites)
 
 
-def finish_kernel(pick_ref, base_ref, *refs):
+def finish_kernel(pick_ref, mine_ref, siblings_ref, *refs):
     out_ref = refs[-1]
     parts = [refs[at : at + 4] for at in range(0, len(refs) - 1, 4)]
+    half = mine_ref.shape[3]
+    halves = [pl.multiple_of(core * half, half) for core in (pick_ref[1], 1 - pick_ref[1])]
 
     @pl.when(pick_ref[0] == 0)
     def _():
-        out_ref[0, 0] = base_ref[0, 0].astype(F32)
+        for ref, first in zip((mine_ref, siblings_ref), halves):
+            out_ref[0, 0, :, pl.ds(first, half)] = ref[0, 0].astype(F32)
 
     @pl.when(pick_ref[0] != 0)
     def _():
-        half = sum(part[0].shape[3] for part in parts)
-        for side, first in ((0, pick_ref[1]), (1, 1 - pick_ref[1])):
+        for side, first in enumerate(halves):
             for number, part in enumerate(parts):
                 one, two = part[2 * side : 2 * side + 2]
                 width = one.shape[3]
-                place = pl.ds(pl.multiple_of(first * half + number * width, width), width)
+                place = pl.ds(pl.multiple_of(first + number * width, width), width)
                 out_ref[0, 0, :, place] = one[0, 0].astype(F32) + two[0, 0].astype(F32)
 
 
-def finish(pick, base, parts):
+def finish(pick, mine, siblings, parts):
     addends = [value for part in parts for value in part]
-    mpo_count, _, rows, cols = base.shape
+    mpo_count, _, rows, half = mine.shape
 
     def spec(value, used):
         def index(v, p, pick):
-            mine = (pick[0] == used).astype(jnp.int32)
-            return (v * mine, p * mine, 0, 0)
+            wanted = (pick[0] == used).astype(jnp.int32)
+            return (v * wanted, p * wanted, 0, 0)
 
         return pl.BlockSpec((1, 1) + value.shape[2:], index)
 
@@ -150,14 +152,14 @@
         grid_spec=pltpu.PrefetchScalarGridSpec(
             num_scalar_prefetch=1,
             grid=(mpo_count, 2),
-            in_specs=[spec(base, 0)] + [spec(value, 1) for value in addends],
-            out_specs=pl.BlockSpec((1, 1, rows, cols), lambda v, p, pick: (v, p, 0, 0)),
+            in_specs=[spec(mine, 0), spec(siblings, 0)] + [spec(value, 1) for value in addends],
+            out_specs=pl.BlockSpec((1, 1, rows, 2 * half), lambda v, p, pick: (v, p, 0, 0)),
         ),
-        out_shape=jax.ShapeDtypeStruct((mpo_count, 2, rows, cols), F32),
+        out_shape=jax.ShapeDtypeStruct((mpo_count, 2, rows, 2 * half), F32),
         compiler_params=params(2),
         cost_estimate=LIGHT,
         name="finish",
-    )(pick, base, *addends)
+    )(pick, mine, siblings, *addends)
 
 
 def after(value, *earlier):
@@ -253,9 +255,9 @@
         travelling.append([shift(part) for part in travelling[-1]])
 
     blocks = jnp.stack([lax.rem(row - k + row_count, row_count) for k in range(row_count)])
-    blocks = after(blocks.astype(jnp.int32), *travelling[0])
+    blocks = after(blocks.astype(jnp.int32), travelling[0][0])
     q = first_product(blocks, mpo_mine, site, envs, half, half)
-    q_sib = swap(after(q, travelling[1][0]))
+    q_sib = swap(after(q, travelling[0][1]))
 
     goals = [
         [((r - step) % row_count // 2, (r - step) % row_count % 2) for r in range(row_count)]
@@ -286,11 +288,11 @@
     step_of = lambda d: lax.rem(row - col * 2 - d + row_count, row_count)
     lows = [second(parts)]
     turned = [turn_to_goal(lows[0], goals[0])]
-    lows.append(second(travelling[0], lows[0], travelling[1][1]))
+    lows.append(second(travelling[0], lows[0], travelling[1][0]))
     turned.append(turn_to_goal(lows[1], goals[1]))
     lows.append(second(travelling[1], lows[1], turned[0]))
     turned.append(turn_to_goal(lows[2], goals[2]))
-    totals = [(low.astype(F32) + came.astype(F32)).astype(BF16) for low, came in zip(lows, turned)]
+    totals = [low.astype(F32) + came.astype(F32) for low, came in zip(lows, turned)]
 
     def total_at(step):
         return jnp.where(step == 0, totals[0], jnp.where(step == 1, totals[1], totals[2]))
@@ -301,11 +303,11 @@
         return [low] + [send(low, goals[3], *way) for way in ways]
 
     last = [last_part(0, lows[2])]
-    mine, siblings = total_at(step_of(depth)), total_at(step_of(1 - depth))
+    mine, siblings = total_at(step_of(depth)), total_at(step_of(1 - depth)).astype(BF16)
     last.append(last_part(1, *last[0], mine, siblings))
-    base = in_order(mine, swap(after(siblings, last[1][0])), 3)
+    siblings = swap(siblings)
     came_last = (step_of(depth) == row_count - 1).astype(jnp.int32)
-    return finish(jnp.stack([came_last, depth.astype(jnp.int32)]), base, last)
+    return finish(jnp.stack([came_last, depth.astype(jnp.int32)]), mine, siblings, last)
 
 
 def solution(mesh):

time: 339 us -> 328 us (0.968)
  waiting for transfers between devices: 206 us -> 193 us
  local copies, waits for them, and re-layouts: 15.3 us -> 20.1 us
    ppermute x3, waiting for transfers between devices: 18.5 us -> 4.68 us  [turn_to_goal(): lax.ppermute(value, axes, [(place(r, 1 - c, d), place(r, c, d)) for r, (c...]
    ppermute x6, waiting for transfers between devices: 9.54 us -> 17.7 us  [send(): lax.ppermute(value, axes, [(place(r, 1 - c if turned else c, 1 - d if cro...]
    ppermute x12, waiting for transfers between devices: 168 us -> 161 us  [ring(): lax.ppermute(value, 'row', [(r, (r + 1) % row_count) for r in range(row_c...]
    select_n x1 -> x0, other arithmetic: 4.16 us -> none  [total_at(): jnp.where(step == 0, totals[0], jnp.where(step == 1, totals[1], totals[2]))]
    unnamed x50 -> x56, local copies, waits for them, and re-layouts: 9.77 us -> 13.5 us
    convert_element_type x0 -> x1, other arithmetic: none -> 3.55 us  [ring(): total_at(step_of(1 - depth)).astype(BF16)]
    select_n x2 -> x1, other arithmetic: 7.47 us -> 5.69 us  [ring(): jnp.where(depth == 0, jnp.concatenate([mine, sibling], axis=axis), jnp.co...]
  transfers between devices with their start and end apart: 26 -> 26, of which waited for: 15 -> 17; matrix products, arithmetic and copies ran while one was open for 6% -> 6% of each run, Pallas kernels for 17% -> 20%
where the time goes in v8:
time: 328 us; the launch traced here: 327 us
  waiting for transfers between devices  193 us (59%)
  Pallas kernels  71.8 us (22%)
  starting transfers between devices  27.2 us (8%)
  local copies, waits for them, and re-layouts  20.1 us (6%)
  other arithmetic  15.1 us (5%)
    ppermute x12, waiting for transfers between devices, ring(): lax.ppermute(value, 'row', [(r, (r + 1) % row_count) for r in range(row_c...  161 us
    pallas_call x5, Pallas kernels, second_product(): pl.pallas_call(second_kernel, grid=(mpo_count,), in_specs=[pl.BlockSpec(m...  41 us
    pallas_call x1, Pallas kernels, first_product(): pl.pallas_call(functools.partial(first_kernel, w_local), grid=(rows // ro...  25 us
    ppermute x6, waiting for transfers between devices, send(): lax.ppermute(value, axes, [(place(r, 1 - c if turned else c, 1 - d if cro...  17.7 us
    unnamed x56, local copies, waits for them, and re-layouts  13.5 us
    ppermute x4, waiting for transfers between devices, swap(): return lax.ppermute(value, 'depth', [(0, 1), (1, 0)])  9.19 us
    ppermute x3, starting transfers between devices, turn_to_goal(): lax.ppermute(value, axes, [(place(r, 1 - c, d), place(r, c, d)) for r, (c...  8.59 us
    ppermute x6, starting transfers between devices, send(): lax.ppermute(value, axes, [(place(r, 1 - c if turned else c, 1 - d if cro...  7.73 us
  transfers between devices with their start and end apart: 26, of which 17 were waited for; matrix products, arithmetic and copies ran while one was open for 6% of the time, Pallas kernels for 20%

profile of v8, /device:TPU:1, one launch (start us, length us, event | category | flops | bytes accessed | tf_op | source)
XLA Modules:
  0.0 327.4 jit_solution(6555495616457153440)
XLA Ops:
  0.0 1.7 constant_dynamic-slice_fusion.2
  1.7 0.1 collective-permute-start
  1.8 2.7 collective-permute-start.1
  4.6 1.0 copy-done.8
  5.6 3.5 %copy.8 = bf16[2,512,2,1024]{3,1,2,0:T(8,128)(2,1)S(1)} copy(bf16[2,512,2,1024]{3,2,1,0:T(2,128)(2,1)} %param.4) | data formatting | bytes 8388608 | tf_op jit(solution)/shard_map/optimization_barrier | solution.py:166
  9.1 2.0 copy-done.1
  11.2 0.2 dynamic-slice_bitcast_fusion
  11.3 1.0 copy-done.9
  12.4 2.3 collective-permute-start.5
  14.7 1.2 collective-permute-start.4
  15.9 14.3 %collective-permute-done.1.refs_2_ = bf16[1,2,512,512]{3,2,1,0:T(8,128)(2,1)} collective-permute-done((bf16[1,2,512,512]{3,2,1,0:T(8,128)(2,1)S(1)}, bf16[1,2,512,512]{3,2,1,0:T(8,128)(2,1)}, u32[]{:S(2)}, u32[]{:S(2)}) %collective-permute-start.1) | collective-permute-done | bytes 1048608 | tf_op jit(solution)/shard_map/ppermute | solution.py:229
  30.2 22.4 %collective-permute-done.5.refs_3_ = bf16[1,2,512,512]{3,2,1,0:T(8,128)(2,1)S(1)} collective-permute-done((bf16[1,2,512,512]{3,2,1,0:T(8,128)(2,1)S(1)}, bf16[1,2,512,512]{3,2,1,0:T(8,128)(2,1)S(1)}, u32[]{:S(2)}, u32[]{:S(2)}) %collective-permute-start.5) | collective-permute-done | bytes 1048608 | tf_op jit(solution)/shard_map/ppermute | solution.py:229
  52.5 22.5 %collective-permute-done.2.refs_4_ = bf16[1,2,512,512]{3,2,1,0:T(8,128)(2,1)S(1)} collective-permute-done((bf16[1,2,512,512]{3,2,1,0:T(8,128)(2,1)}, bf16[1,2,512,512]{3,2,1,0:T(8,128)(2,1)S(1)}, u32[]{:S(2)}, u32[]{:S(2)}) %collective-permute-start.2) | collective-permute-done | bytes 1048608 | tf_op jit(solution)/shard_map/ppermute | solution.py:229
  75.0 22.5 %collective-permute-done.6.refs_5_ = bf16[1,2,512,512]{3,2,1,0:T(8,128)(2,1)S(1)} collective-permute-done((bf16[1,2,512,512]{3,2,1,0:T(8,128)(2,1)S(1)}, bf16[1,2,512,512]{3,2,1,0:T(8,128)(2,1)S(1)}, u32[]{:S(2)}, u32[]{:S(2)}) %collective-permute-start.6) | collective-permute-done | bytes 1048608 | tf_op jit(solution)/shard_map/ppermute | solution.py:229
  97.5 1.0 copy-done.12
  98.4 0.6 collective-permute-start.7
  99.1 1.2 fusion
  100.3 0.7 collective-permute-start.9
  101.0 2.2 collective-permute-done.7
  103.2 5.7 %maximum_select_fusion.1 = bf16[1,2,2,512,1024]{4,3,2,1,0:T(8,128)(2,1)S(1)} fusion(bf16[1,2,2,256,1024]{4,3,2,1,0:T(8,128)(2,1)} %bitcast.10, bf16[1,2,2,256,1024]{4,3,2,1,0:T(8,128)(2,1)} %bitcast.9, pred[]{:T(512)S(6)} %eq.24), kind=kLoop, calls=%fused_computation.1 | loop fusion | flops 18874368 | bytes 8388609 | tf_op jit(solution)/shard_map/jit(_where)/select_n | solution.py:233
  108.9 4.0 %maximum_select_fusion.site_ref = bf16[2,2,2,512,1024]{4,3,2,1,0:T(8,128)(2,1)} fusion(bf16[1,2,2,512,1024]{4,3,2,1,0:T(8,128)(2,1)S(1)} %maximum_select_fusion.1, bf16[1,2,2,512,1024]{4,3,2,1,0:T(8,128)(2,1)S(1)} %bitcast.15, pred[]{:T(512)S(6)} %eq.23), kind=kLoop, calls=%fused_computation | loop fusion | flops 12582912 | bytes 16777216 | tf_op jit(solution)/shard_map/jit(_where)/select_n | solution.py:250
  112.9 14.1 %collective-permute-done.3.refs_6_ = bf16[1,2,512,512]{3,2,1,0:T(8,128)(2,1)S(1)} collective-permute-done((bf16[1,2,512,512]{3,2,1,0:T(8,128)(2,1)}, bf16[1,2,512,512]{3,2,1,0:T(8,128)(2,1)S(1)}, u32[]{:S(2)}, u32[]{:S(2)}) %collective-permute-start.3) | collective-permute-done | bytes 1048608 | tf_op jit(solution)/shard_map/ppermute | solution.py:229
  127.1 22.5 %collective-permute-done.9.refs_7_ = bf16[1,2,512,512]{3,2,1,0:T(8,128)(2,1)S(1)} collective-permute-done((bf16[1,2,512,512]{3,2,1,0:T(8,128)(2,1)}, bf16[1,2,512,512]{3,2,1,0:T(8,128)(2,1)S(1)}, u32[]{:S(2)}, u32[]{:S(2)}) %collective-permute-start.9) | collective-permute-done | bytes 1048608 | tf_op jit(solution)/shard_map/ppermute | solution.py:229
  149.6 1.0 copy-done.17
  150.5 0.6 pad_add_fusion.1.block_ref
  151.2 0.6 pad_maximum_fusion.mpo_ref
  151.8 20.2 %collective-permute-done.8.refs_0_ = bf16[2,2,128,1024]{3,2,1,0:T(8,128)(2,1)S(1)} collective-permute-done((bf16[2,2,128,1024]{3,2,1,0:T(8,128)(2,1)}, bf16[2,2,128,1024]{3,2,1,0:T(8,128)(2,1)S(1)}, u32[]{:S(2)}, u32[]{:S(2)}) %collective-permute-start.8) | collective-permute-done | bytes 1048608 | tf_op jit(solution)/shard_map/ppermute | solution.py:229
  172.0 25.0 %first_product.1.own_ref = bf16[2,2,2,512,512]{4,3,2,1,0:T(8,128)(2,1)} custom-call(s32[4]{0:T(128)} %pad_add_fusion.1.block_ref, f32[2,2,2,2]{3,2,1,0:T(2,128)} %pad_maximum_fusion.mpo_ref, bf16[2,2,2,512,1024]{4,3,2,1,0:T(8,128)(2,1)} %maximum_select_fusion.site_ref, bf16[1,2,512,512]{3,2,1,0:T(8,128)(2,1)} %copy-done.3, ...), custom_call_target="tpu_custom_call" | custom-call | tf_op jit(solution)/shard_map/first_product/pallas_call | solution.py:67
  197.0 1.2 collective-permute-start.11
  198.3 7.0 %collective-permute-done.11.sib_ref = bf16[2,2,2,512,512]{4,3,2,1,0:T(8,128)(2,1)S(1)} collective-permute-done((bf16[2,2,2,512,512]{4,3,2,1,0:T(8,128)(2,1)}, bf16[2,2,2,512,512]{4,3,2,1,0:T(8,128)(2,1)S(1)}, u32[]{:S(2)}, u32[]{:S(2)}) %collective-permute-start.11) | collective-permute-done | bytes 4194336 | tf_op jit(solution)/shard_map/ppermute | solution.py:170
  205.3 2.0 copy-done
  207.2 8.4 %second_product.5 = bf16[2,2,512,256]{3,2,1,0:T(8,128)(2,1)} custom-call(s32[1]{0:T(128)} %bitcast.1.pick_ref, bf16[2,2,2,512,512]{4,3,2,1,0:T(8,128)(2,1)} %first_product.1.own_ref, bf16[2,2,2,512,512]{4,3,2,1,0:T(8,128)(2,1)} %copy-done, bf16[2,2,128,1024]{3,2,1,0:T(8,128)(2,1)} %get-tuple-element.17.refs_0_, bf16[2,2,128,1024]{3,2,1,0:T(8,128)(2,1)} %copy-done.7), custom_call_target="tpu_custom_call" | custom-call | tf_op jit(solution)/shard_map/second_product/pallas_call | solution.py:105
  215.6 1.3 collective-permute-start.12
  216.9 0.1 collective-permute-start.15
  217.0 7.9 %collective-permute-done.13.refs_0_ = bf16[2,2,128,1024]{3,2,1,0:T(8,128)(2,1)} collective-permute-done((bf16[2,2,128,1024]{3,2,1,0:T(8,128)(2,1)S(1)}, bf16[2,2,128,1024]{3,2,1,0:T(8,128)(2,1)}, u32[]{:S(2)}, u32[]{:S(2)}) %collective-permute-start.13) | collective-permute-done | bytes 1048608 | tf_op jit(solution)/shard_map/ppermute | solution.py:229
  224.9 8.4 %second_product.6 = bf16[2,2,512,256]{3,2,1,0:T(8,128)(2,1)} custom-call(s32[1]{0:T(128)} %bitcast.1.pick_ref, bf16[2,2,2,512,512]{4,3,2,1,0:T(8,128)(2,1)} %first_product.1.own_ref, bf16[2,2,2,512,512]{4,3,2,1,0:T(8,128)(2,1)} %copy-done, bf16[2,2,128,1024]{3,2,1,0:T(8,128)(2,1)} %copy-done.13, bf16[2,2,128,1024]{3,2,1,0:T(8,128)(2,1)} %copy-done.14), custom_call_target="tpu_custom_call" | custom-call | tf_op jit(solution)/shard_map/second_product/pallas_call | solution.py:105
  233.3 4.2 %collective-permute-start.14 = (bf16[2,2,512,256]{3,2,1,0:T(8,128)(2,1)}, bf16[2,2,512,256]{3,2,1,0:T(8,128)(2,1)}, u32[]{:S(2)}, u32[]{:S(2)}) collective-permute-start(bf16[2,2,512,256]{3,2,1,0:T(8,128)(2,1)} %second_product.6), channel_id=1, source_target_pairs={{0,2},{1,3},{6,4},{7,5},{10,8},{11,9},{12,14},{13,15},{16,18},{17,... | collective-permute-start | bytes 3145736 | tf_op jit(solution)/shard_map/ppermute | solution.py:272
  237.4 4.7 %collective-permute-done.12 = bf16[2,2,512,256]{3,2,1,0:T(8,128)(2,1)S(1)} collective-permute-done((bf16[2,2,512,256]{3,2,1,0:T(8,128)(2,1)}, bf16[2,2,512,256]{3,2,1,0:T(8,128)(2,1)S(1)}, u32[]{:S(2)}, u32[]{:S(2)}) %collective-permute-start.12) | collective-permute-done | bytes 1048608 | tf_op jit(solution)/shard_map/ppermute | solution.py:272
  242.1 5.1 %collective-permute-done.15.refs_1_ = bf16[2,2,128,1024]{3,2,1,0:T(8,128)(2,1)S(1)} collective-permute-done((bf16[2,2,128,1024]{3,2,1,0:T(8,128)(2,1)S(1)}, bf16[2,2,128,1024]{3,2,1,0:T(8,128)(2,1)S(1)}, u32[]{:S(2)}, u32[]{:S(2)}) %collective-permute-start.15) | collective-permute-done | bytes 1048608 | tf_op jit(solution)/shard_map/ppermute | solution.py:229
  247.2 1.0 copy-done.15
  248.2 8.4 %second_product.7 = bf16[2,2,512,256]{3,2,1,0:T(8,128)(2,1)} custom-call(s32[1]{0:T(128)} %bitcast.1.pick_ref, bf16[2,2,2,512,512]{4,3,2,1,0:T(8,128)(2,1)} %first_product.1.own_ref, bf16[2,2,2,512,512]{4,3,2,1,0:T(8,128)(2,1)} %copy-done, bf16[2,2,128,1024]{3,2,1,0:T(8,128)(2,1)} %collective-permute-done.13.refs_0_, bf16[2,2,128,1024]{3,2,1,0:T(8,128)(2,1)} %copy-done.15), custom_call_target="tpu_custom_call" | custom-call | tf_op jit(solution)/shard_map/second_product/pallas_call | solution.py:105
  256.7 3.2 collective-permute-start.16
  260.0 9.9 %collective-permute-done.18.refs_0_ = bf16[2,2,128,1024]{3,2,1,0:T(8,128)(2,1)} collective-permute-done((bf16[2,2,128,1024]{3,2,1,0:T(8,128)(2,1)}, bf16[2,2,128,1024]{3,2,1,0:T(8,128)(2,1)}, u32[]{:S(2)}, u32[]{:S(2)}) %collective-permute-start.18) | collective-permute-done | bytes 1048608 | tf_op jit(solution)/shard_map/ppermute | solution.py:229
  269.8 7.9 %second_product.8.refs_0_ = bf16[2,2,512,128]{3,2,1,0:T(8,128)(2,1)} custom-call(s32[1]{0:T(128)} %bitcast.1.pick_ref, bf16[2,2,2,512,512]{4,3,2,1,0:T(8,128)(2,1)} %first_product.1.own_ref, bf16[2,2,2,512,512]{4,3,2,1,0:T(8,128)(2,1)} %copy-done, bf16[2,2,128,1024]{3,2,1,0:T(8,128)(2,1)} %collective-permute-done.18.refs_0_), custom_call_target="tpu_custom_call" | custom-call | tf_op jit(solution)/shard_map/second_product/pallas_call | solution.py:105
  277.7 1.3 collective-permute-start.19
  279.0 1.3 collective-permute-start.20
  280.3 1.3 collective-permute-start.21
  281.7 3.5 %select_convert_fusion = (bf16[2,2,512,256]{3,2,1,0:T(8,128)(2,1)S(1)}, f32[2,2,512,256]{3,2,1,0:T(8,128)}) fusion(bf16[2,2,512,256]{3,2,1,0:T(8,128)(2,1)S(1)} %copy-done.19, bf16[2,2,512,256]{3,2,1,0:T(8,128)(2,1)S(1)} %copy-done.4, bf16[2,2,512,256]{3,2,1,0:T(8,128)(2,1)} %collective-permute-done.14, bf16[2,2,512,256]{3,2,1,0:T(8,128)(2,1)S(1)} %copy-done.5, ...), kind=kLoop, calls=%fused_computation.2 | loop fusion | flops 7340032 | bytes 9437188 | tf_op jit(solution)/shard_map/convert_element_type | solution.py:306
  285.2 1.8 collective-permute-start.17
  287.0 4.8 %collective-permute-done.19.refs_1_ = bf16[2,2,512,128]{3,2,1,0:T(8,128)(2,1)S(1)} collective-permute-done((bf16[2,2,512,128]{3,2,1,0:T(8,128)(2,1)}, bf16[2,2,512,128]{3,2,1,0:T(8,128)(2,1)S(1)}, u32[]{:S(2)}, u32[]{:S(2)}) %collective-permute-start.19) | collective-permute-done | bytes 524320 | tf_op jit(solution)/shard_map/ppermute | solution.py:279
  291.8 1.6 collective-permute-done.20.refs_2_
  293.5 0.9 copy-done.23
  294.3 0.8 copy-done.24
  295.1 1.0 copy-done.20
  296.1 7.9 %second_product.9.refs_4_ = bf16[2,2,512,128]{3,2,1,0:T(8,128)(2,1)} custom-call(s32[1]{0:T(128)} %bitcast.1.pick_ref, bf16[2,2,2,512,512]{4,3,2,1,0:T(8,128)(2,1)} %first_product.1.own_ref, bf16[2,2,2,512,512]{4,3,2,1,0:T(8,128)(2,1)} %copy-done, bf16[2,2,128,1024]{3,2,1,0:T(8,128)(2,1)} %copy-done.20), custom_call_target="tpu_custom_call" | custom-call | tf_op jit(solution)/shard_map/second_product/pallas_call | solution.py:105
  304.0 1.3 collective-permute-start.23
  305.3 1.3 collective-permute-start.24
  306.6 1.3 collective-permute-start.25
  307.9 0.6 pad_add_fusion.pick_ref
  308.5 9.3 %collective-permute-done.23.refs_5_ = bf16[2,2,512,128]{3,2,1,0:T(8,128)(2,1)S(1)} collective-permute-done((bf16[2,2,512,128]{3,2,1,0:T(8,128)(2,1)}, bf16[2,2,512,128]{3,2,1,0:T(8,128)(2,1)S(1)}, u32[]{:S(2)}, u32[]{:S(2)}) %collective-permute-start.23) | collective-permute-done | bytes 524320 | tf_op jit(solution)/shard_map/ppermute | solution.py:279
  317.8 1.9 collective-permute-done.24.refs_6_
  319.8 0.8 copy-done.26
  320.5 1.0 copy-done.21
  321.5 5.8 %finish.1 = f32[2,2,512,512]{3,2,1,0:T(8,128)} custom-call(s32[2]{0:T(128)} %pad_add_fusion.pick_ref, f32[2,2,512,256]{3,2,1,0:T(8,128)} %get-tuple-element.26.mine_ref, bf16[2,2,512,256]{3,2,1,0:T(8,128)(2,1)} %copy-done.21, bf16[2,2,512,128]{3,2,1,0:T(8,128)(2,1)} %second_product.8.refs_0_, bf16[2,2,512,128]{3,2,1,0:T(8,128)(2,1)} %copy-done.22, ...), custom_call_target="tpu_custom_call" | custom-call | tf_op jit(solution)/shard_map/finish/pallas_call | solution.py:150
  (62 shorter events, 0.2 us)
Async XLA Ops:
  1.7 7.4 %copy-start.3 = (bf16[1,2,512,512]{3,2,1,0:T(8,128)(2,1)}, bf16[1,2,512,512]{3,2,1,0:T(8,128)(2,1)S(1)}, u32[]{:S(2)}) copy-start(bf16[1,2,512,512]{3,2,1,0:T(8,128)(2,1)S(1)} %get-tuple-element.31.refs_0_) | copy-start | bytes 3145732
  1.7 2.9 collective-permute-start
  1.8 28.3 %collective-permute-start.1 = (bf16[1,2,512,512]{3,2,1,0:T(8,128)(2,1)S(1)}, bf16[1,2,512,512]{3,2,1,0:T(8,128)(2,1)}, u32[]{:S(2)}, u32[]{:S(2)}) collective-permute-start(bf16[1,2,512,512]{3,2,1,0:T(8,128)(2,1)S(1)} %get-tuple-element.31.refs_0_), channel_id=1, source_target_pairs={{0,4},{4,8},{8,12},{12,0},{1,5},{5,9},{9,13},{13,1},{2,6},{6,10},{... | collective-permute-start | bytes 3145736 | tf_op jit(solution)/shard_map/ppermute | solution.py:229
  4.6 1.0 copy-start.8
  9.1 2.0 copy-start.1
  11.1 1.2 copy-start.9
  12.4 40.1 %collective-permute-start.5 = (bf16[1,2,512,512]{3,2,1,0:T(8,128)(2,1)S(1)}, bf16[1,2,512,512]{3,2,1,0:T(8,128)(2,1)S(1)}, u32[]{:S(2)}, u32[]{:S(2)}) collective-permute-start(bf16[1,2,512,512]{3,2,1,0:T(8,128)(2,1)S(1)} %copy-done.9), channel_id=1, source_target_pairs={{0,4},{4,8},{8,12},{12,0},{1,5},{5,9},{9,13},{13,1},{2,6},{6,10},{... | collective-permute-start | bytes 3145736 | tf_op jit(solution)/shard_map/ppermute | solution.py:229
  14.7 60.3 %collective-permute-start.4 = (bf16[2,2,256,1024]{3,2,1,0:T(8,128)(2,1)S(1)}, bf16[2,2,256,1024]{3,2,1,0:T(8,128)(2,1)}, u32[]{:S(2)}, u32[]{:S(2)}) collective-permute-start(bf16[2,2,256,1024]{3,2,1,0:T(8,128)(2,1)S(1)} %dynamic-slice_bitcast_fusion), channel_id=1, source_target_pairs={{0,2},{2,0},{1,3},{3,1},{4,6},{6,4},{5,7},{7,5},{8,10},{10,8},{9,1... | collective-permute-start | bytes 6291464 | tf_op jit(solution)/shard_map/ppermute | solution.py:232
  30.2 44.8 %collective-permute-start.2 = (bf16[1,2,512,512]{3,2,1,0:T(8,128)(2,1)}, bf16[1,2,512,512]{3,2,1,0:T(8,128)(2,1)S(1)}, u32[]{:S(2)}, u32[]{:S(2)}) collective-permute-start(bf16[1,2,512,512]{3,2,1,0:T(8,128)(2,1)} %collective-permute-done.1.refs_2_), channel_id=1, source_target_pairs={{0,4},{4,8},{8,12},{12,0},{1,5},{5,9},{9,13},{13,1},{2,6},{6,10},{... | collective-permute-start | bytes 3145736 | tf_op jit(solution)/shard_map/ppermute | solution.py:229
  52.5 22.5 %copy-start.10 = (bf16[1,2,512,512]{3,2,1,0:T(8,128)(2,1)}, bf16[1,2,512,512]{3,2,1,0:T(8,128)(2,1)S(1)}, u32[]{:S(2)}) copy-start(bf16[1,2,512,512]{3,2,1,0:T(8,128)(2,1)S(1)} %collective-permute-done.5.refs_3_) | copy-start | bytes 3145732
  52.5 44.9 %collective-permute-start.6 = (bf16[1,2,512,512]{3,2,1,0:T(8,128)(2,1)S(1)}, bf16[1,2,512,512]{3,2,1,0:T(8,128)(2,1)S(1)}, u32[]{:S(2)}, u32[]{:S(2)}) collective-permute-start(bf16[1,2,512,512]{3,2,1,0:T(8,128)(2,1)S(1)} %collective-permute-done.5.refs_3_), channel_id=1, source_target_pairs={{0,4},{4,8},{8,12},{12,0},{1,5},{5,9},{9,13},{13,1},{2,6},{6,10},{... | collective-permute-start | bytes 3145736 | tf_op jit(solution)/shard_map/ppermute | solution.py:229
  75.0 22.5 %copy-start.11 = (bf16[1,2,512,512]{3,2,1,0:T(8,128)(2,1)}, bf16[1,2,512,512]{3,2,1,0:T(8,128)(2,1)S(1)}, u32[]{:S(2)}) copy-start(bf16[1,2,512,512]{3,2,1,0:T(8,128)(2,1)S(1)} %collective-permute-done.2.refs_4_) | copy-start | bytes 3145732
  97.5 1.0 copy-start.12
  98.4 4.8 %collective-permute-start.7 = (bf16[2,2,256,1024]{3,2,1,0:T(8,128)(2,1)}, bf16[2,2,256,1024]{3,2,1,0:T(8,128)(2,1)}, u32[]{:S(2)}, u32[]{:S(2)}) collective-permute-start(bf16[2,2,256,1024]{3,2,1,0:T(8,128)(2,1)} %collective-permute-done.4), channel_id=1, source_target_pairs={{0,1},{1,0},{2,3},{3,2},{4,5},{5,4},{6,7},{7,6},{8,9},{9,8},{10,11... | collective-permute-start | bytes 6291464 | tf_op jit(solution)/shard_map/ppermute | solution.py:170
  100.3 50.3 %copy-start.7 = (bf16[2,2,128,1024]{3,2,1,0:T(8,128)(2,1)}, bf16[2,2,128,1024]{3,2,1,0:T(8,128)(2,1)S(1)}, u32[]{:S(2)}) copy-start(bf16[2,2,128,1024]{3,2,1,0:T(8,128)(2,1)S(1)} %get-tuple-element.19.refs_1_) | copy-start | bytes 3145732
  100.3 26.8 %collective-permute-start.3 = (bf16[1,2,512,512]{3,2,1,0:T(8,128)(2,1)}, bf16[1,2,512,512]{3,2,1,0:T(8,128)(2,1)S(1)}, u32[]{:S(2)}, u32[]{:S(2)}) collective-permute-start(bf16[1,2,512,512]{3,2,1,0:T(8,128)(2,1)} %copy-done.11), channel_id=1, source_target_pairs={{0,4},{4,8},{8,12},{12,0},{1,5},{5,9},{9,13},{13,1},{2,6},{6,10},{... | collective-permute-start | bytes 3145736 | tf_op jit(solution)/shard_map/ppermute | solution.py:229
  100.3 49.3 %collective-permute-start.9 = (bf16[1,2,512,512]{3,2,1,0:T(8,128)(2,1)}, bf16[1,2,512,512]{3,2,1,0:T(8,128)(2,1)S(1)}, u32[]{:S(2)}, u32[]{:S(2)}) collective-permute-start(bf16[1,2,512,512]{3,2,1,0:T(8,128)(2,1)} %copy-done.12), channel_id=1, source_target_pairs={{0,4},{4,8},{8,12},{12,0},{1,5},{5,9},{9,13},{13,1},{2,6},{6,10},{... | collective-permute-start | bytes 3145736 | tf_op jit(solution)/shard_map/ppermute | solution.py:229
  103.2 5.7 %copy-start.2 = (bf16[2,512,2,1024]{3,1,2,0:T(8,128)(2,1)S(1)}, bf16[2,512,2,1024]{3,1,2,0:T(8,128)(2,1)}, u32[]{:S(2)}) copy-start(bf16[2,512,2,1024]{3,1,2,0:T(8,128)(2,1)} %copy-done.1) | copy-start | bytes 12582916
  108.9 42.3 %copy-start.27 = (f32[2,2,2,2]{3,2,1,0:T(2,128)S(1)}, f32[2,2,2,2]{3,2,1,0:T(2,128)}, u32[]{:S(2)}) copy-start(f32[2,2,2,2]{3,2,1,0:T(2,128)} %param.5) | copy-start | bytes 196
  127.1 22.5 %copy-start.16 = (bf16[1,2,512,512]{3,2,1,0:T(8,128)(2,1)}, bf16[1,2,512,512]{3,2,1,0:T(8,128)(2,1)S(1)}, u32[]{:S(2)}) copy-start(bf16[1,2,512,512]{3,2,1,0:T(8,128)(2,1)S(1)} %collective-permute-done.3.refs_6_) | copy-start | bytes 3145732
  127.1 44.9 %collective-permute-start.8 = (bf16[2,2,128,1024]{3,2,1,0:T(8,128)(2,1)}, bf16[2,2,128,1024]{3,2,1,0:T(8,128)(2,1)S(1)}, u32[]{:S(2)}, u32[]{:S(2)}) collective-permute-start(bf16[2,2,128,1024]{3,2,1,0:T(8,128)(2,1)} %get-tuple-element.17.refs_0_), channel_id=1, source_target_pairs={{0,4},{4,8},{8,12},{12,0},{1,5},{5,9},{9,13},{13,1},{2,6},{6,10},{... | collective-permute-start | bytes 3145736 | tf_op jit(solution)/shard_map/ppermute | solution.py:229
  149.6 1.0 copy-start.17
  150.5 46.5 %collective-permute-start.10 = (bf16[2,2,128,1024]{3,2,1,0:T(8,128)(2,1)S(1)}, bf16[2,2,128,1024]{3,2,1,0:T(8,128)(2,1)S(1)}, u32[]{:S(2)}, u32[]{:S(2)}) collective-permute-start(bf16[2,2,128,1024]{3,2,1,0:T(8,128)(2,1)S(1)} %get-tuple-element.19.refs_1_), channel_id=1, source_target_pairs={{0,4},{4,8},{8,12},{12,0},{1,5},{5,9},{9,13},{13,1},{2,6},{6,10},{... | collective-permute-start | bytes 3145736 | tf_op jit(solution)/shard_map/ppermute | solution.py:229
  172.0 26.2 %copy-start.13 = (bf16[2,2,128,1024]{3,2,1,0:T(8,128)(2,1)}, bf16[2,2,128,1024]{3,2,1,0:T(8,128)(2,1)S(1)}, u32[]{:S(2)}) copy-start(bf16[2,2,128,1024]{3,2,1,0:T(8,128)(2,1)S(1)} %collective-permute-done.8.refs_0_) | copy-start | bytes 3145732
  197.0 27.9 %copy-start.14 = (bf16[2,2,128,1024]{3,2,1,0:T(8,128)(2,1)}, bf16[2,2,128,1024]{3,2,1,0:T(8,128)(2,1)S(1)}, u32[]{:S(2)}) copy-start(bf16[2,2,128,1024]{3,2,1,0:T(8,128)(2,1)S(1)} %collective-permute-done.10.refs_1_) | copy-start | bytes 3145732
  197.0 8.2 %collective-permute-start.11 = (bf16[2,2,2,512,512]{4,3,2,1,0:T(8,128)(2,1)}, bf16[2,2,2,512,512]{4,3,2,1,0:T(8,128)(2,1)S(1)}, u32[]{:S(2)}, u32[]{:S(2)}) collective-permute-start(bf16[2,2,2,512,512]{4,3,2,1,0:T(8,128)(2,1)} %first_product.1.own_ref), channel_id=1, source_target_pairs={{0,1},{1,0},{2,3},{3,2},{4,5},{5,4},{6,7},{7,6},{8,9},{9,8},{10,11... | collective-permute-start | bytes 12582920 | tf_op jit(solution)/shard_map/ppermute | solution.py:170
  198.3 26.6 %collective-permute-start.13 = (bf16[2,2,128,1024]{3,2,1,0:T(8,128)(2,1)S(1)}, bf16[2,2,128,1024]{3,2,1,0:T(8,128)(2,1)}, u32[]{:S(2)}, u32[]{:S(2)}) collective-permute-start(bf16[2,2,128,1024]{3,2,1,0:T(8,128)(2,1)S(1)} %collective-permute-done.8.refs_0_), channel_id=1, source_target_pairs={{0,4},{4,8},{8,12},{12,0},{1,5},{5,9},{9,13},{13,1},{2,6},{6,10},{... | collective-permute-start | bytes 3145736 | tf_op jit(solution)/shard_map/ppermute | solution.py:229
  205.2 2.0 copy-start
  215.6 26.5 %collective-permute-start.12 = (bf16[2,2,512,256]{3,2,1,0:T(8,128)(2,1)}, bf16[2,2,512,256]{3,2,1,0:T(8,128)(2,1)S(1)}, u32[]{:S(2)}, u32[]{:S(2)}) collective-permute-start(bf16[2,2,512,256]{3,2,1,0:T(8,128)(2,1)} %second_product.5), channel_id=1, source_target_pairs={{2,0},{3,1},{6,4},{7,5},{8,10},{9,11},{12,14},{13,15},{18,16},{19,... | collective-permute-start | bytes 3145736 | tf_op jit(solution)/shard_map/ppermute | solution.py:272
  216.9 30.3 %collective-permute-start.15 = (bf16[2,2,128,1024]{3,2,1,0:T(8,128)(2,1)S(1)}, bf16[2,2,128,1024]{3,2,1,0:T(8,128)(2,1)S(1)}, u32[]{:S(2)}, u32[]{:S(2)}) collective-permute-start(bf16[2,2,128,1024]{3,2,1,0:T(8,128)(2,1)S(1)} %collective-permute-done.10.refs_1_), channel_id=1, source_target_pairs={{0,4},{4,8},{8,12},{12,0},{1,5},{5,9},{9,13},{13,1},{2,6},{6,10},{... | collective-permute-start | bytes 3145736 | tf_op jit(solution)/shard_map/ppermute | solution.py:229
  224.9 44.9 %collective-permute-start.18 = (bf16[2,2,128,1024]{3,2,1,0:T(8,128)(2,1)}, bf16[2,2,128,1024]{3,2,1,0:T(8,128)(2,1)}, u32[]{:S(2)}, u32[]{:S(2)}) collective-permute-start(bf16[2,2,128,1024]{3,2,1,0:T(8,128)(2,1)} %collective-permute-done.13.refs_0_), channel_id=1, source_target_pairs={{0,4},{4,8},{8,12},{12,0},{1,5},{5,9},{9,13},{13,1},{2,6},{6,10},{... | collective-permute-start | bytes 3145736 | tf_op jit(solution)/shard_map/ppermute | solution.py:229
  233.3 47.0 %collective-permute-start.14 = (bf16[2,2,512,256]{3,2,1,0:T(8,128)(2,1)}, bf16[2,2,512,256]{3,2,1,0:T(8,128)(2,1)}, u32[]{:S(2)}, u32[]{:S(2)}) collective-permute-start(bf16[2,2,512,256]{3,2,1,0:T(8,128)(2,1)} %second_product.6), channel_id=1, source_target_pairs={{0,2},{1,3},{6,4},{7,5},{10,8},{11,9},{12,14},{13,15},{16,18},{17,... | collective-permute-start | bytes 3145736 | tf_op jit(solution)/shard_map/ppermute | solution.py:272
  242.1 14.6 %copy-start.18 = (bf16[2,2,512,256]{3,2,1,0:T(8,128)(2,1)}, bf16[2,2,512,256]{3,2,1,0:T(8,128)(2,1)S(1)}, u32[]{:S(2)}) copy-start(bf16[2,2,512,256]{3,2,1,0:T(8,128)(2,1)S(1)} %collective-permute-done.12) | copy-start | bytes 3145732
  247.2 1.0 copy-start.15
  256.7 25.0 %collective-permute-start.16 = (bf16[2,2,512,256]{3,2,1,0:T(8,128)(2,1)}, bf16[2,2,512,256]{3,2,1,0:T(8,128)(2,1)S(1)}, u32[]{:S(2)}, u32[]{:S(2)}) collective-permute-start(bf16[2,2,512,256]{3,2,1,0:T(8,128)(2,1)} %second_product.7), channel_id=1, source_target_pairs={{0,2},{1,3},{4,6},{5,7},{10,8},{11,9},{14,12},{15,13},{16,18},{17,... | collective-permute-start | bytes 3145736 | tf_op jit(solution)/shard_map/ppermute | solution.py:272
  259.8 35.3 %collective-permute-start.22 = (bf16[2,2,128,1024]{3,2,1,0:T(8,128)(2,1)}, bf16[2,2,128,1024]{3,2,1,0:T(8,128)(2,1)S(1)}, u32[]{:S(2)}, u32[]{:S(2)}) collective-permute-start(bf16[2,2,128,1024]{3,2,1,0:T(8,128)(2,1)} %copy-done.15), channel_id=1, source_target_pairs={{0,4},{4,8},{8,12},{12,0},{1,5},{5,9},{9,13},{13,1},{2,6},{6,10},{... | collective-permute-start | bytes 3145736 | tf_op jit(solution)/shard_map/ppermute | solution.py:229
  259.9 21.7 %copy-start.4 = (bf16[2,2,512,256]{3,2,1,0:T(8,128)(2,1)S(1)}, bf16[2,2,512,256]{3,2,1,0:T(8,128)(2,1)}, u32[]{:S(2)}) copy-start(bf16[2,2,512,256]{3,2,1,0:T(8,128)(2,1)} %second_product.5) | copy-start | bytes 3145732
  259.9 21.7 %copy-start.5 = (bf16[2,2,512,256]{3,2,1,0:T(8,128)(2,1)S(1)}, bf16[2,2,512,256]{3,2,1,0:T(8,128)(2,1)}, u32[]{:S(2)}) copy-start(bf16[2,2,512,256]{3,2,1,0:T(8,128)(2,1)} %second_product.6) | copy-start | bytes 3145732
  259.9 21.7 %copy-start.6 = (bf16[2,2,512,256]{3,2,1,0:T(8,128)(2,1)S(1)}, bf16[2,2,512,256]{3,2,1,0:T(8,128)(2,1)}, u32[]{:S(2)}) copy-start(bf16[2,2,512,256]{3,2,1,0:T(8,128)(2,1)} %second_product.7) | copy-start | bytes 3145732
  259.9 21.7 %copy-start.19 = (bf16[2,2,512,256]{3,2,1,0:T(8,128)(2,1)S(1)}, bf16[2,2,512,256]{3,2,1,0:T(8,128)(2,1)}, u32[]{:S(2)}) copy-start(bf16[2,2,512,256]{3,2,1,0:T(8,128)(2,1)} %copy-done.18) | copy-start | bytes 3145732
  277.7 14.1 %collective-permute-start.19 = (bf16[2,2,512,128]{3,2,1,0:T(8,128)(2,1)}, bf16[2,2,512,128]{3,2,1,0:T(8,128)(2,1)S(1)}, u32[]{:S(2)}, u32[]{:S(2)}) collective-permute-start(bf16[2,2,512,128]{3,2,1,0:T(8,128)(2,1)} %second_product.8.refs_0_), channel_id=1, source_target_pairs={{3,1},{4,6},{9,11},{14,12},{19,17},{20,22},{25,27},{30,28}} | collective-permute-start | bytes 1572872 | tf_op jit(solution)/shard_map/ppermute | solution.py:279
  279.0 14.5 %collective-permute-start.20 = (bf16[2,2,512,128]{3,2,1,0:T(8,128)(2,1)}, bf16[2,2,512,128]{3,2,1,0:T(8,128)(2,1)S(1)}, u32[]{:S(2)}, u32[]{:S(2)}) collective-permute-start(bf16[2,2,512,128]{3,2,1,0:T(8,128)(2,1)} %second_product.8.refs_0_), channel_id=1, source_target_pairs={{2,1},{5,6},{8,11},{15,12},{18,17},{21,22},{24,27},{31,28}} | collective-permute-start | bytes 1572872 | tf_op jit(solution)/shard_map/ppermute | solution.py:279
  280.3 13.1 %collective-permute-start.21 = (bf16[2,2,512,128]{3,2,1,0:T(8,128)(2,1)}, bf16[2,2,512,128]{3,2,1,0:T(8,128)(2,1)S(1)}, u32[]{:S(2)}, u32[]{:S(2)}) collective-permute-start(bf16[2,2,512,128]{3,2,1,0:T(8,128)(2,1)} %second_product.8.refs_0_), channel_id=1, source_target_pairs={{0,1},{7,6},{10,11},{13,12},{16,17},{23,22},{26,27},{29,28}} | collective-permute-start | bytes 1572872 | tf_op jit(solution)/shard_map/ppermute | solution.py:279
  285.2 34.5 %collective-permute-start.17 = (bf16[2,2,512,256]{3,2,1,0:T(8,128)(2,1)S(1)}, bf16[2,2,512,256]{3,2,1,0:T(8,128)(2,1)S(1)}, u32[]{:S(2)}, u32[]{:S(2)}) collective-permute-start(bf16[2,2,512,256]{3,2,1,0:T(8,128)(2,1)S(1)} %get-tuple-element.25), channel_id=1, source_target_pairs={{0,1},{1,0},{2,3},{3,2},{4,5},{5,4},{6,7},{7,6},{8,9},{9,8},{10,11... | collective-permute-start | bytes 3145736 | tf_op jit(solution)/shard_map/ppermute | solution.py:170
  291.8 12.2 %copy-start.22 = (bf16[2,2,512,128]{3,2,1,0:T(8,128)(2,1)}, bf16[2,2,512,128]{3,2,1,0:T(8,128)(2,1)S(1)}, u32[]{:S(2)}) copy-start(bf16[2,2,512,128]{3,2,1,0:T(8,128)(2,1)S(1)} %collective-permute-done.19.refs_1_) | copy-start | bytes 1572868
  293.5 0.9 copy-start.23
  294.3 0.8 copy-start.24
  295.1 1.0 copy-start.20
  304.0 13.8 %collective-permute-start.23 = (bf16[2,2,512,128]{3,2,1,0:T(8,128)(2,1)}, bf16[2,2,512,128]{3,2,1,0:T(8,128)(2,1)S(1)}, u32[]{:S(2)}, u32[]{:S(2)}) collective-permute-start(bf16[2,2,512,128]{3,2,1,0:T(8,128)(2,1)} %second_product.9.refs_4_), channel_id=1, source_target_pairs={{3,1},{4,6},{9,11},{14,12},{19,17},{20,22},{25,27},{30,28}} | collective-permute-start | bytes 1572872 | tf_op jit(solution)/shard_map/ppermute | solution.py:279
  305.3 14.5 %collective-permute-start.24 = (bf16[2,2,512,128]{3,2,1,0:T(8,128)(2,1)}, bf16[2,2,512,128]{3,2,1,0:T(8,128)(2,1)S(1)}, u32[]{:S(2)}, u32[]{:S(2)}) collective-permute-start(bf16[2,2,512,128]{3,2,1,0:T(8,128)(2,1)} %second_product.9.refs_4_), channel_id=1, source_target_pairs={{2,1},{5,6},{8,11},{15,12},{18,17},{21,22},{24,27},{31,28}} | collective-permute-start | bytes 1572872 | tf_op jit(solution)/shard_map/ppermute | solution.py:279
  306.6 13.2 %collective-permute-start.25 = (bf16[2,2,512,128]{3,2,1,0:T(8,128)(2,1)}, bf16[2,2,512,128]{3,2,1,0:T(8,128)(2,1)}, u32[]{:S(2)}, u32[]{:S(2)}) collective-permute-start(bf16[2,2,512,128]{3,2,1,0:T(8,128)(2,1)} %second_product.9.refs_4_), channel_id=1, source_target_pairs={{0,1},{7,6},{10,11},{13,12},{16,17},{23,22},{26,27},{29,28}} | collective-permute-start | bytes 1572872 | tf_op jit(solution)/shard_map/ppermute | solution.py:279
  317.8 2.0 copy-start.25
  319.7 0.8 copy-start.26
  320.5 1.0 copy-start.21

commit v9 on v8

v9 whole, which is shorter than its diff:
```python
import functools
import jax
import jax.numpy as jnp
from jax import lax
from jax.experimental import pallas as pl
from jax.experimental.pallas import tpu as pltpu
from jax.sharding import PartitionSpec as P

F32 = jnp.float32
BF16 = jnp.bfloat16
VMEM_BYTES = 56 * 1024 * 1024
LIGHT = pl.CostEstimate(flops=0, bytes_accessed=0, transcendentals=0)


def params(steps):
    return pltpu.CompilerParams(
        dimension_semantics=("arbitrary",) * steps, vmem_limit_bytes=VMEM_BYTES
    )


def mul(left, right):
    return jnp.dot(left, right, preferred_element_type=F32)


def mul_t(left, right):
    return lax.dot_general(left, right, (((1,), (1,)), ((), ())), preferred_element_type=F32)


def first_kernel(block_ref, mpo_ref, site_ref, *refs):
    q_ref, g_ref = refs[-2:]
    env_refs = refs[:-2]
    mpo_count, phys, _, rows, _ = q_ref.shape
    depth = env_refs[0].shape[2]
    per_col = site_ref.shape[-1] // depth
    w_local = mpo_count // 2
    for w in range(mpo_count):
        with_real, with_imag = None, None
        for number in range(len(env_refs) // 2):
            env_ref = env_refs[number * 2 + w // w_local]
            block = block_ref[number]
            piece = pl.ds(pl.multiple_of((block % per_col) * depth, depth), depth)
            left = site_ref[block // per_col, :, :, :, piece].reshape(phys * 2 * rows, depth)
            more_real, more_imag = mul(left, env_ref[w % w_local, 0]), mul(left, env_ref[w % w_local, 1])
            with_real = more_real if with_real is None else with_real + more_real
            with_imag = more_imag if with_imag is None else with_imag + more_imag
        for s in range(phys):
            real, imag = (slice((2 * s + part) * rows, (2 * s + part + 1) * rows) for part in range(2))
            there = slice(s * rows, (s + 1) * rows)
            g_ref[w, 0, there] = with_real[real] + with_imag[imag]
            g_ref[w, 1, there] = with_imag[real] - with_real[imag]
    for part in range(2):
        for v in range(mpo_count):
            for t in range(phys):
                total = None
                for w in range(mpo_count):
                    for s in range(phys):
                        term = mpo_ref[w, v, s, t] * g_ref[w, part, s * rows : (s + 1) * rows]
                        total = term if total is None else total + term
                q_ref[v, t, part] = total.astype(BF16)


def first_product(blocks, mpo, site, envs, row_tile, col_tile):
    col_count, phys, _, rows, wide = site.shape
    w_local, _, depth, cols = envs[0].shape
    mpo_count = mpo.shape[1]
    smem = pl.BlockSpec(memory_space=pltpu.SMEM)
    return pl.pallas_call(
        first_kernel,
        grid=(rows // row_tile, cols // col_tile),
        in_specs=[
            smem,
            smem,
            pl.BlockSpec((col_count, phys, 2, row_tile, wide), lambda i, j: (0, 0, 0, i, 0)),
        ]
        + [pl.BlockSpec((w_local, 2, depth, col_tile), lambda i, j: (0, 0, 0, j))] * len(envs),
        out_specs=pl.BlockSpec((mpo_count, phys, 2, row_tile, col_tile), lambda i, j: (0, 0, 0, i, j)),
        out_shape=jax.ShapeDtypeStruct((mpo_count, phys, 2, rows, cols), BF16),
        scratch_shapes=[pltpu.VMEM((mpo_count, 2, phys * row_tile, col_tile), F32)],
        compiler_params=params(2),
        cost_estimate=LIGHT,
        name="first_product",
    )(blocks, mpo, site, *envs)


def second_kernel(pick_ref, own_ref, sib_ref, *refs):
    site_refs, out_ref = refs[:-1], refs[-1]
    phys, _, rows, cols = own_ref.shape[1:]
    total = None
    for q_ref, quarter in ((own_ref, pick_ref[0]), (sib_ref, 1 - pick_ref[0])):
        piece = pl.ds(pl.multiple_of(quarter * cols, cols), cols)
        for t in range(phys):
            right = [site_ref[t, part, :, piece] for part in range(2) for site_ref in site_refs]
            more = mul_t(q_ref[0, t].reshape(2 * rows, cols), jnp.concatenate(right, axis=0))
            total = more if total is None else total + more
    width = total.shape[1] // 2
    out_ref[0, 0] = (total[:rows, :width] - total[rows:, width:]).astype(BF16)
    out_ref[0, 1] = (total[:rows, width:] + total[rows:, :width]).astype(BF16)


def second_product(pick, own, sib, sites):
    mpo_count, phys, _, rows, cols = own.shape
    y_rows = sum(site.shape[2] for site in sites)
    q_spec = pl.BlockSpec((1, phys, 2, rows, cols), lambda v: (v, 0, 0, 0, 0))
    return pl.pallas_call(
        second_kernel,
        grid=(mpo_count,),
        in_specs=[pl.BlockSpec(memory_space=pltpu.SMEM), q_spec, q_spec]
        + [pl.BlockSpec(site.shape, lambda v: (0, 0, 0, 0)) for site in sites],
        out_specs=pl.BlockSpec((1, 2, rows, y_rows), lambda v: (v, 0, 0, 0)),
        out_shape=jax.ShapeDtypeStruct((mpo_count, 2, rows, y_rows), BF16),
        compiler_params=params(1),
        cost_estimate=LIGHT,
        name="second_product",
    )(pick, own, sib, *sites)


def finish_kernel(pick_ref, mine_ref, siblings_ref, out_ref):
    half = mine_ref.shape[3]
    for ref, core in ((mine_ref, pick_ref[0]), (siblings_ref, 1 - pick_ref[0])):
        out_ref[0, 0, :, pl.ds(pl.multiple_of(core * half, half), half)] = ref[0, 0].astype(F32)


def finish(pick, mine, siblings):
    mpo_count, _, rows, half = mine.shape
    half_spec = pl.BlockSpec((1, 1, rows, half), lambda v, p: (v, p, 0, 0))
    return pl.pallas_call(
        finish_kernel,
        grid=(mpo_count, 2),
        in_specs=[pl.BlockSpec(memory_space=pltpu.SMEM), half_spec, half_spec],
        out_specs=pl.BlockSpec((1, 1, rows, 2 * half), lambda v, p: (v, p, 0, 0)),
        out_shape=jax.ShapeDtypeStruct((mpo_count, 2, rows, 2 * half), F32),
        compiler_params=params(2),
        cost_estimate=LIGHT,
        name="finish",
    )(pick, mine, siblings)


def after(value, *earlier):
    return lax.optimization_barrier((value,) + earlier)[0]


def swap(value):
    return lax.ppermute(value, "depth", [(0, 1), (1, 0)])


def split_inputs(environment, mpo):
    depth = lax.axis_index("depth")
    w_local, half = environment.shape[0], environment.shape[3]
    cols = half // 2
    env_own = lax.dynamic_slice_in_dim(environment, depth * cols, cols, 3)
    env_sib = swap(lax.dynamic_slice_in_dim(environment, (1 - depth) * cols, cols, 3))
    mpo_mine = jnp.concatenate(
        [
            lax.dynamic_slice_in_dim(mpo, depth * w_local, w_local, 0),
            lax.dynamic_slice_in_dim(mpo, (1 - depth) * w_local, w_local, 0),
        ],
        axis=0,
    )
    return env_own, env_sib, mpo_mine


def one_product(left, right, dims):
    return jnp.einsum(dims, left, right, preferred_element_type=F32)


def any_line(environment, site_tensor, mpo):
    depth = lax.axis_index("depth")
    env_own, env_sib, mpo_mine = split_inputs(environment, mpo)
    env_own = lax.all_gather(env_own, "row", axis=2, tiled=True)
    env_sib = lax.all_gather(env_sib, "row", axis=2, tiled=True)
    env = jnp.concatenate([env_own, env_sib], axis=0)
    cols = env.shape[3]
    planar = jnp.transpose(site_tensor, (0, 2, 1, 3))
    site_own = lax.dynamic_slice_in_dim(planar, depth * cols, cols, 3)
    site = lax.all_gather(planar, "col", axis=3, tiled=True)
    first = functools.partial(one_product, dims="sxa,wac->wsxc")
    g = jnp.stack(
        [
            first(site[:, 0], env[:, 0]) + first(site[:, 1], env[:, 1]),
            first(site[:, 0], env[:, 1]) - first(site[:, 1], env[:, 0]),
        ],
        axis=2,
    )
    q = jnp.einsum("wvst,wspxc->vtpxc", mpo_mine, g, precision=lax.Precision.HIGHEST).astype(BF16)
    site = lax.all_gather(site_own, "row", axis=2, tiled=True)
    second = functools.partial(one_product, dims="vtxc,tyc->vxy")
    total = jnp.stack(
        [
            second(q[:, :, 0], site[:, 0]) - second(q[:, :, 1], site[:, 1]),
            second(q[:, :, 0], site[:, 1]) + second(q[:, :, 1], site[:, 0]),
        ],
        axis=1,
    )
    return lax.psum_scatter(total, ("col", "depth"), scatter_dimension=3, tiled=True)


def four_rows(environment, site_tensor, mpo):
    row, col, depth = (lax.axis_index(axis) for axis in ("row", "col", "depth"))
    axes = ("row", "col", "depth")
    place = lambda r, c, d: (r * 2 + c) * 2 + d
    both = lambda value: lax.ppermute(value, "row", [(0, 1), (1, 0), (2, 3), (3, 2)])
    to_host = lambda value: lax.ppermute(value, "row", [(0, 1), (3, 2)])
    to_end = lambda value: lax.ppermute(value, "row", [(1, 0), (2, 3)])
    across = lambda value: lax.ppermute(value, "row", [(1, 2), (2, 1)])
    turn = lambda value: lax.ppermute(value, "col", [(0, 1), (1, 0)])

    def to_col(value, which_rows, far):
        pairs = []
        for r in which_rows:
            goal = 1 - r // 2 if far else r // 2
            pairs += [(place(r, 1 - goal, d), place(r, goal, d)) for d in range(2)]
        return lax.ppermute(value, axes, pairs)

    in_order = lambda mine, sibling, axis: jnp.where(
        depth == 0,
        jnp.concatenate([mine, sibling], axis=axis),
        jnp.concatenate([sibling, mine], axis=axis),
    )
    is_host = (row == 1) | (row == 2)
    hosts_or = lambda at_host, at_end: jnp.where(is_host, at_host, at_end)

    env_own, env_sib, mpo_mine = split_inputs(environment, mpo)
    env = [env_own, env_sib]
    planar = jnp.transpose(after(site_tensor, env_sib), (0, 2, 1, 3))
    rows = planar.shape[2]
    half = rows // 2
    mine = lax.dynamic_slice_in_dim(planar, depth * half, half, 2)

    def rows_of(own, turned, own_swapped, turned_swapped):
        near = in_order(own, own_swapped, 2)
        other = in_order(turned, turned_swapped, 2)
        return jnp.where(col == 0, jnp.stack([near, other]), jnp.stack([other, near]))

    parts = [mine[:, :, : half // 2], mine[:, :, half // 2 :]]
    side_env, over_env = [both(one) for one in env], [across(one) for one in env]
    turned = turn(mine)
    swapped = [swap(after(value, *side_env)) for value in (mine, turned)]
    far_env, over_side_env, side_parts, there_parts, turned_parts = [], [], [], [], []
    gates = (*side_env, *over_env)
    for m in range(2):
        far_env.append(to_end(after(over_env[m], *gates)))
        over_side_env.append(across(after(side_env[m], *gates)))
        side_parts.append(to_host(after(parts[m], *gates)))
        there_parts.append(hosts_or(side_parts[m], parts[m]))
        gates = (far_env[m], over_side_env[m], side_parts[m], *swapped)
    site_here = rows_of(mine, turned, *swapped)
    turned_parts = [turn(part) for part in there_parts]
    gates = (*gates, turned_parts[0])
    over_site = across(after(mine, *gates))
    over_side_env_both = jnp.concatenate(over_side_env, axis=0)
    far_side_env = to_end(after(over_side_env_both, *gates))
    gates = (over_site, far_side_env)
    over_side_parts, host_parts = [], []
    for m in range(2):
        over_side_parts.append(across(after(side_parts[m], *gates)))
        host_parts.append(to_end(after(parts[m], *gates)))
        gates = (over_side_parts[m], host_parts[m])

    side = row ^ 1
    at_host = jnp.stack([row, side, 3 - row, 3 - side]).astype(jnp.int32)
    at_end = jnp.stack([row, side, 3 - side, 3 - row]).astype(jnp.int32)
    pick = depth.astype(jnp.int32).reshape(1)

    def first(blocks, site, envs, *earlier):
        q = first_product(blocks, mpo_mine, site, envs, half, half)
        return q, swap(after(q, *earlier))

    def second(q, sites, *earlier):
        return second_product(after(pick, *earlier), q[0], q[1], sites)

    q_here = first(at_host, site_here, env + side_env + over_env + over_side_env)
    there, turned = (
        jnp.concatenate([after(part, q_here[0]) for part in pair], axis=2)
        for pair in (there_parts, turned_parts)
    )
    site_there = rows_of(there, turned, swap(there), swap(turned))
    last_env = hosts_or(over_side_env_both, far_side_env)
    w_local = environment.shape[0]
    q_there = first(
        hosts_or(at_host, at_end),
        site_there,
        env
        + side_env
        + [hosts_or(*pair) for pair in zip(over_env, far_env)]
        + [last_env[:w_local], last_env[w_local:]],
        over_side_parts[0],
        host_parts[0],
    )
    here_over = second(q_here, [over_site], q_there[0])
    here_own = second(q_here, [mine], here_over)
    there_own = second(q_there, [hosts_or(over_site, after(mine, q_there[0]))], here_own)
    there_side = second(
        q_there, [hosts_or(*part) for part in zip(over_side_parts, host_parts)], there_own
    )
    came_here_over = to_col(here_over, (1, 2), True)
    far_there_own = to_end(there_own)
    near_own = hosts_or(here_own, there_own)
    came_near_own = to_col(near_own, range(4), False)
    far_there_side = to_end(there_side)
    here_side = second(q_here, side_parts, there_side, came_here_over)
    near_side = hosts_or(here_side, there_side)
    came_near_side = to_col(near_side, range(4), False)
    came_far_own = to_col(far_there_own, (0, 3), True)
    here_over_side = second(q_here, over_side_parts, here_side, far_there_own, came_near_own)
    came_here_over_side = to_col(here_over_side, (1, 2), True)
    came_far_side = to_col(after(far_there_side, came_far_own), (0, 3), True)

    is_near = col == row // 2
    wide = lambda value: value.astype(F32)
    one = jnp.where(
        is_near,
        wide(near_own) + wide(came_near_own),
        hosts_or(wide(here_over) + wide(came_here_over), wide(far_there_own) + wide(came_far_own)),
    )
    two = jnp.where(
        is_near,
        wide(near_side) + wide(came_near_side),
        hosts_or(wide(here_over_side) + wide(came_here_over_side), wide(far_there_side)),
    )
    one, two = lax.optimization_barrier((one, two))
    two = two + wide(came_far_side)
    one_is_mine = (depth == row % 2) ^ (is_host & ~is_near)
    kept = jnp.where(one_is_mine, one, two)
    given = jnp.where(one_is_mine, two, one).astype(BF16)
    return finish(pick, kept, swap(given))


def solution(mesh):
    placed = (
        P(("groups", "depth"), None, "row", "col"),
        P("groups", "row", None, "col"),
        P("groups", None, None, None),
    )
    fits = mesh.shape["col"] == 2 and mesh.shape["row"] == 4
    return jax.shard_map(
        four_rows if fits else any_line,
        mesh=mesh,
        in_specs=placed,
        out_specs=P("groups", None, "row", ("col", "depth")),
        check_vma=False,
    )
```

time: 328 us -> 345 us (1.052)
  waiting for transfers between devices: 193 us -> 110 us
  other arithmetic: 15.1 us -> 54.9 us
  Pallas kernels: 71.8 us -> 105 us
  starting transfers between devices: 27.2 us -> 57.3 us
  local copies, waits for them, and re-layouts: 20.1 us -> 16.4 us
    ppermute x22 -> x27, waiting for transfers between devices: 184 us -> 107 us  [the longest x2 41.9 us: four_rows(): lax.ppermute(value, 'row', [(0, 1), (1, 0), (2, 3), (3, 2)])]
    select_n x2 -> x20, other arithmetic: 9.71 us -> 49.2 us  [the longest x4 18.9 us: four_rows(): jnp.where(depth == 0, jnp.concatenate([mine, sibling], axis=axis), jnp.co...]
    pallas_call x2 -> x3, Pallas kernels: 30.8 us -> 53.8 us  [the longest x2 49.3 us: first_product(): pl.pallas_call(first_kernel, grid=(rows // row_tile, cols // col_tile), i...]
    ppermute x22 -> x27, starting transfers between devices: 23.4 us -> 41.4 us  [the longest x6 12 us: to_col(): return lax.ppermute(value, axes, pairs)]
    ppermute x4 -> x8, starting transfers between devices: 3.79 us -> 15.9 us  [swap(): return lax.ppermute(value, 'depth', [(0, 1), (1, 0)])]
    pallas_call x5 -> x6, Pallas kernels: 41 us -> 51.1 us  [second_product(): pl.pallas_call(second_kernel, grid=(mpo_count,), in_specs=[pl.BlockSpec(m...]
    unnamed x56 -> x51, local copies, waits for them, and re-layouts: 13.5 us -> 5.49 us
    ppermute x4 -> x8, waiting for transfers between devices: 9.19 us -> 2.62 us  [swap(): return lax.ppermute(value, 'depth', [(0, 1), (1, 0)])]
  transfers between devices with their start and end apart: 26 -> 35, of which waited for: 17 -> 13; matrix products, arithmetic and copies ran while one was open for 6% -> 17% of each run, Pallas kernels for 20% -> 29%
where the time goes in v9:
time: 345 us; the launch traced here: 344 us
  waiting for transfers between devices  110 us (32%)
  Pallas kernels  105 us (30%)
  starting transfers between devices  57.3 us (17%)
  other arithmetic  54.9 us (16%)
  local copies, waits for them, and re-layouts  16.4 us (5%)
    pallas_call x6, Pallas kernels, second_product(): pl.pallas_call(second_kernel, grid=(mpo_count,), in_specs=[pl.BlockSpec(m...  51.1 us
    pallas_call x2, Pallas kernels, first_product(): pl.pallas_call(first_kernel, grid=(rows // row_tile, cols // col_tile), i...  49.3 us
    ppermute x2, waiting for transfers between devices, four_rows(): lax.ppermute(value, 'row', [(0, 1), (1, 0), (2, 3), (3, 2)])  41.9 us
    ppermute x7, waiting for transfers between devices, four_rows(): to_end = lambda value: lax.ppermute(value, 'row', [(1, 0), (2, 3)])  26.7 us
    ppermute x2, waiting for transfers between devices, four_rows(): to_host = lambda value: lax.ppermute(value, 'row', [(0, 1), (3, 2)])  20.1 us
    select_n x4, other arithmetic, four_rows(): jnp.where(depth == 0, jnp.concatenate([mine, sibling], axis=axis), jnp.co...  18.9 us
    ppermute x8, starting transfers between devices, swap(): return lax.ppermute(value, 'depth', [(0, 1), (1, 0)])  15.9 us
    select_n x11, other arithmetic, four_rows(): hosts_or = lambda at_host, at_end: jnp.where(is_host, at_host, at_end)  15.5 us
  transfers between devices with their start and end apart: 35, of which 13 were waited for; matrix products, arithmetic and copies ran while one was open for 17% of the time, Pallas kernels for 29%

profile of v9, /device:TPU:1, one launch (start us, length us, event | category | flops | bytes accessed | tf_op | source)
XLA Modules:
  0.0 343.6 jit_solution(10514056948141077157)
XLA Ops:
  0.0 1.7 constant_dynamic-slice_fusion
  1.9 2.6 collective-permute-done.refs_1_
  5.5 3.5 %copy.4 = bf16[2,512,2,1024]{3,1,2,0:T(8,128)(2,1)S(1)} copy(bf16[2,512,2,1024]{3,2,1,0:T(2,128)(2,1)} %param.4) | data formatting | bytes 8388608 | tf_op jit(solution)/shard_map/optimization_barrier | solution.py:139
  9.0 1.9 dynamic-slice_bitcast_fusion
  10.9 2.3 collective-permute-start.7
  13.2 1.3 collective-permute-start.1
  14.7 1.6 collective-permute-start.3
  16.3 1.7 collective-permute-start.4
  18.0 19.4 %collective-permute-done.1.refs_2_ = bf16[1,2,512,512]{3,2,1,0:T(8,128)(2,1)} collective-permute-done((bf16[1,2,512,512]{3,2,1,0:T(8,128)(2,1)S(1)}, bf16[1,2,512,512]{3,2,1,0:T(8,128)(2,1)}, u32[]{:S(2)}, u32[]{:S(2)}) %collective-permute-start.1) | collective-permute-done | bytes 1048608 | tf_op jit(solution)/shard_map/ppermute | solution.py:201
  37.3 22.5 %collective-permute-done.2.refs_3_ = bf16[1,2,512,512]{3,2,1,0:T(8,128)(2,1)} collective-permute-done((bf16[1,2,512,512]{3,2,1,0:T(8,128)(2,1)S(1)}, bf16[1,2,512,512]{3,2,1,0:T(8,128)(2,1)}, u32[]{:S(2)}, u32[]{:S(2)}) %collective-permute-start.2) | collective-permute-done | bytes 1048608 | tf_op jit(solution)/shard_map/ppermute | solution.py:201
  59.8 1.5 collective-permute-start.6
  62.5 4.3 %collective-permute-start.5 = (bf16[2,2,128,1024]{3,2,1,0:T(8,128)(2,1)}, bf16[2,2,128,1024]{3,2,1,0:T(8,128)(2,1)}, u32[]{:S(2)}, u32[]{:S(2)}) collective-permute-start(bf16[2,2,128,1024]{3,2,1,0:T(8,128)(2,1)} %slice.16), channel_id=1, source_target_pairs={{0,4},{12,8},{1,5},{13,9},{2,6},{14,10},{3,7},{15,11},{16,20},{28,... | collective-permute-start | bytes 3145736 | tf_op jit(solution)/shard_map/ppermute | solution.py:202
  67.5 1.3 collective-permute-start.10
  69.4 17.0 %collective-permute-done.5.refs_0_ = bf16[2,2,128,1024]{3,2,1,0:T(8,128)(2,1)} collective-permute-done((bf16[2,2,128,1024]{3,2,1,0:T(8,128)(2,1)}, bf16[2,2,128,1024]{3,2,1,0:T(8,128)(2,1)}, u32[]{:S(2)}, u32[]{:S(2)}) %collective-permute-start.5) | collective-permute-done | bytes 1048608 | tf_op jit(solution)/shard_map/ppermute | solution.py:202
  86.4 1.5 broadcast_select_fusion.7
  87.9 4.0 %collective-permute-done.10 = bf16[1,2,512,512]{3,2,1,0:T(8,128)(2,1)} collective-permute-done((bf16[1,2,512,512]{3,2,1,0:T(8,128)(2,1)}, bf16[1,2,512,512]{3,2,1,0:T(8,128)(2,1)}, u32[]{:S(2)}, u32[]{:S(2)}) %collective-permute-start.10) | collective-permute-done | bytes 1048608 | tf_op jit(solution)/shard_map/ppermute | solution.py:203
  91.9 2.3 collective-permute-start.12
  96.9 1.3 collective-permute-start.17
  98.2 5.8 %maximum_select_fusion.2 = bf16[1,2,2,512,1024]{4,3,2,1,0:T(8,128)(2,1)S(1)} fusion(bf16[1,2,2,256,1024]{4,3,2,1,0:T(8,128)(2,1)} %bitcast.7, bf16[1,2,2,256,1024]{4,3,2,1,0:T(8,128)(2,1)} %get-tuple-element.65, pred[]{:T(512)S(6)} %eq.29), kind=kLoop, calls=%fused_computation.2 | loop fusion | flops 18874368 | bytes 8388609 | tf_op jit(solution)/shard_map/jit(_where)/select_n | solution.py:214
  104.0 5.6 %maximum_select_fusion.3 = bf16[1,2,2,512,1024]{4,3,2,1,0:T(8,128)(2,1)S(1)} fusion(bf16[1,2,2,256,1024]{4,3,2,1,0:T(8,128)(2,1)} %bitcast.10, bf16[1,2,2,256,1024]{4,3,2,1,0:T(8,128)(2,1)} %bitcast.9, pred[]{:T(512)S(6)} %eq.29), kind=kLoop, calls=%fused_computation.3 | loop fusion | flops 18874368 | bytes 8388609 | tf_op jit(solution)/shard_map/jit(_where)/select_n | solution.py:214
  109.6 3.2 collective-permute-done.12.refs_1_
  113.2 3.0 collective-permute-done.14
  116.3 3.6 %collective-permute-done.17 = bf16[1,2,512,512]{3,2,1,0:T(8,128)(2,1)S(1)} collective-permute-done((bf16[1,2,512,512]{3,2,1,0:T(8,128)(2,1)}, bf16[1,2,512,512]{3,2,1,0:T(8,128)(2,1)S(1)}, u32[]{:S(2)}, u32[]{:S(2)}) %collective-permute-start.17) | collective-permute-done | bytes 1048608 | tf_op jit(solution)/shard_map/ppermute | solution.py:203
  122.4 2.0 collective-permute-start.20
  124.5 4.1 %maximum_select_fusion.site_ref = bf16[2,2,2,512,1024]{4,3,2,1,0:T(8,128)(2,1)} fusion(bf16[1,2,2,512,1024]{4,3,2,1,0:T(8,128)(2,1)S(1)} %maximum_select_fusion.3, bf16[1,2,2,512,1024]{4,3,2,1,0:T(8,128)(2,1)S(1)} %maximum_select_fusion.2, pred[]{:T(512)S(6)} %eq.28), kind=kLoop, calls=%fused_computation | loop fusion | flops 12582912 | bytes 16777216 | tf_op jit(solution)/shard_map/jit(_where)/select_n | solution.py:232
  128.5 24.7 %first_product.2.own_ref = bf16[2,2,2,512,512]{4,3,2,1,0:T(8,128)(2,1)} custom-call(s32[4]{0:T(128)} %pad_add_fusion.block_ref, f32[2,2,2,2]{3,2,1,0:T(2,128)} %pad_maximum_fusion.2.mpo_ref, bf16[2,2,2,512,1024]{4,3,2,1,0:T(8,128)(2,1)} %maximum_select_fusion.site_ref, bf16[1,2,512,512]{3,2,1,0:T(8,128)(2,1)} %copy-done.2, ...), custom_call_target="tpu_custom_call" | custom-call | tf_op jit(solution)/shard_map/first_product/pallas_call | solution.py:67
  153.3 1.5 pad_maximum_fusion
  154.8 4.8 %collective-permute-start.13 = (bf16[2,2,256,1024]{3,2,1,0:T(8,128)(2,1)S(1)}, bf16[2,2,256,1024]{3,2,1,0:T(8,128)(2,1)S(1)}, u32[]{:S(2)}, u32[]{:S(2)}) collective-permute-start(bf16[2,2,256,1024]{3,2,1,0:T(8,128)(2,1)S(1)} %pad_maximum_fusion), channel_id=1, source_target_pairs={{0,1},{1,0},{2,3},{3,2},{4,5},{5,4},{6,7},{7,6},{8,9},{9,8},{10,11... | collective-permute-start | bytes 6291464 | tf_op jit(solution)/shard_map/ppermute | solution.py:143
  159.6 1.4 pad_maximum_fusion.1
  161.8 2.3 broadcast_select_fusion.3.refs_4_
  165.7 1.7 collective-permute-start.21
  167.4 1.5 collective-permute-start.22
  168.9 1.8 broadcast_select_fusion.1
  170.7 1.5 fusion.1
  172.2 3.8 %maximum_select_fusion.4 = bf16[1,2,2,512,1024]{4,3,2,1,0:T(8,128)(2,1)S(1)} fusion(bf16[1,2,2,256,1024]{4,3,2,1,0:T(8,128)(2,1)S(1)} %bitcast.22, bf16[1,2,2,128,1024]{4,3,2,1,0:T(8,128)(2,1)S(1)} %bitcast.19, bf16[1,2,2,128,1024]{4,3,2,1,0:T(8,128)(2,1)} %bitcast.11, pred[]{:T(512)S(6)} %eq.29), kind=kLoop, calls=%fused_computation.4 | loop fusion | flops 27262976 | bytes 8388609 | tf_op jit(solution)/shard_map/jit(_where)/select_n | solution.py:214
  176.0 3.7 %maximum_select_fusion.5 = bf16[1,2,2,512,1024]{4,3,2,1,0:T(8,128)(2,1)S(1)} fusion(bf16[1,2,2,256,1024]{4,3,2,1,0:T(8,128)(2,1)S(1)} %bitcast.21, bf16[1,2,2,128,1024]{4,3,2,1,0:T(8,128)(2,1)} %bitcast.15, bf16[1,2,2,128,1024]{4,3,2,1,0:T(8,128)(2,1)S(1)} %bitcast.20, pred[]{:T(512)S(6)} %eq.29), kind=kLoop, calls=%fused_computation.5 | loop fusion | flops 27262976 | bytes 8388609 | tf_op jit(solution)/shard_map/jit(_where)/select_n | solution.py:214
  179.7 4.1 %maximum_select_fusion.1.site_ref = bf16[2,2,2,512,1024]{4,3,2,1,0:T(8,128)(2,1)} fusion(bf16[1,2,2,512,1024]{4,3,2,1,0:T(8,128)(2,1)S(1)} %maximum_select_fusion.5, bf16[1,2,2,512,1024]{4,3,2,1,0:T(8,128)(2,1)S(1)} %maximum_select_fusion.4, pred[]{:T(512)S(6)} %eq.28), kind=kLoop, calls=%fused_computation.1 | loop fusion | flops 12582912 | bytes 16777216 | tf_op jit(solution)/shard_map/jit(_where)/select_n | solution.py:232
  183.8 24.6 %first_product.3.own_ref = bf16[2,2,2,512,512]{4,3,2,1,0:T(8,128)(2,1)} custom-call(s32[4]{0:T(128)} %broadcast_select_fusion.10.block_ref, f32[2,2,2,2]{3,2,1,0:T(2,128)} %pad_maximum_fusion.2.mpo_ref, bf16[2,2,2,512,1024]{4,3,2,1,0:T(8,128)(2,1)} %maximum_select_fusion.1.site_ref, bf16[1,2,512,512]{3,2,1,0:T(8,128)(2,1)} %copy-done.2, ...), custom_call_target="tpu_custom_call" | custom-call | tf_op jit(solution)/shard_map/first_product/pallas_call | solution.py:67
  208.4 5.7 %collective-permute-start.23 = (bf16[2,2,2,512,512]{4,3,2,1,0:T(8,128)(2,1)}, bf16[2,2,2,512,512]{4,3,2,1,0:T(8,128)(2,1)}, u32[]{:S(2)}, u32[]{:S(2)}) collective-permute-start(bf16[2,2,2,512,512]{4,3,2,1,0:T(8,128)(2,1)} %first_product.3.own_ref), channel_id=1, source_target_pairs={{0,1},{1,0},{2,3},{3,2},{4,5},{5,4},{6,7},{7,6},{8,9},{9,8},{10,11... | collective-permute-start | bytes 12582920 | tf_op jit(solution)/shard_map/ppermute | solution.py:143
  214.8 1.3 collective-permute-start.29
  216.1 1.6 broadcast_select_fusion.refs_0_
  217.7 8.5 %second_product.6 = bf16[2,2,512,256]{3,2,1,0:T(8,128)(2,1)} custom-call(s32[1]{0:T(128)} %bitcast.pick_ref, bf16[2,2,2,512,512]{4,3,2,1,0:T(8,128)(2,1)} %first_product.2.own_ref, bf16[2,2,2,512,512]{4,3,2,1,0:T(8,128)(2,1)} %collective-permute-done.19.sib_ref, bf16[2,2,256,1024]{3,2,1,0:T(8,128)(2,1)} %collective-permute-done.20.refs_0_), custom_call_target="tpu_custom_call" | custom-call | tf_op jit(solution)/shard_map/second_product/pallas_call | solution.py:104
  227.1 8.5 %second_product.7 = bf16[2,2,512,256]{3,2,1,0:T(8,128)(2,1)} custom-call(s32[1]{0:T(128)} %bitcast.pick_ref, bf16[2,2,2,512,512]{4,3,2,1,0:T(8,128)(2,1)} %first_product.2.own_ref, bf16[2,2,2,512,512]{4,3,2,1,0:T(8,128)(2,1)} %collective-permute-done.19.sib_ref, bf16[2,2,256,1024]{3,2,1,0:T(8,128)(2,1)} %copy-done.1), custom_call_target="tpu_custom_call" | custom-call | tf_op jit(solution)/shard_map/second_product/pallas_call | solution.py:104
  235.6 8.5 %second_product.8 = bf16[2,2,512,256]{3,2,1,0:T(8,128)(2,1)} custom-call(s32[1]{0:T(128)} %bitcast.pick_ref, bf16[2,2,2,512,512]{4,3,2,1,0:T(8,128)(2,1)} %first_product.3.own_ref, bf16[2,2,2,512,512]{4,3,2,1,0:T(8,128)(2,1)} %collective-permute-done.23.sib_ref, bf16[2,2,256,1024]{3,2,1,0:T(8,128)(2,1)} %broadcast_select_fusion.refs_0_), custom_call_target="tpu_custom_call" | custom-call | tf_op jit(solution)/shard_map/second_product/pallas_call | solution.py:104
  245.5 1.3 broadcast_select_fusion.9
  246.8 1.3 collective-permute-start.24
  248.1 2.4 broadcast_select_fusion.5.refs_0_
  250.5 2.7 broadcast_select_fusion.4.refs_1_
  253.2 8.4 %second_product.9 = bf16[2,2,512,256]{3,2,1,0:T(8,128)(2,1)} custom-call(s32[1]{0:T(128)} %bitcast.pick_ref, bf16[2,2,2,512,512]{4,3,2,1,0:T(8,128)(2,1)} %first_product.3.own_ref, bf16[2,2,2,512,512]{4,3,2,1,0:T(8,128)(2,1)} %collective-permute-done.23.sib_ref, bf16[2,2,128,1024]{3,2,1,0:T(8,128)(2,1)} %broadcast_select_fusion.5.refs_0_, ...), custom_call_target="tpu_custom_call" | custom-call | tf_op jit(solution)/shard_map/second_product/pallas_call | solution.py:104
  261.6 1.4 collective-permute-start.32
  263.1 8.8 %second_product.10 = bf16[2,2,512,256]{3,2,1,0:T(8,128)(2,1)} custom-call(s32[1]{0:T(128)} %bitcast.pick_ref, bf16[2,2,2,512,512]{4,3,2,1,0:T(8,128)(2,1)} %first_product.2.own_ref, bf16[2,2,2,512,512]{4,3,2,1,0:T(8,128)(2,1)} %collective-permute-done.19.sib_ref, bf16[2,2,128,1024]{3,2,1,0:T(8,128)(2,1)} %collective-permute-done.5.refs_0_, ...), custom_call_target="tpu_custom_call" | custom-call | tf_op jit(solution)/shard_map/second_product/pallas_call | solution.py:104
  271.8 10.4 %collective-permute-done.26 = bf16[2,2,512,256]{3,2,1,0:T(8,128)(2,1)S(1)} collective-permute-done((bf16[2,2,512,256]{3,2,1,0:T(8,128)(2,1)}, bf16[2,2,512,256]{3,2,1,0:T(8,128)(2,1)S(1)}, u32[]{:S(2)}, u32[]{:S(2)}) %collective-permute-start.26) | collective-permute-done | bytes 1048608 | tf_op jit(solution)/shard_map/ppermute | solution.py:203
  282.3 1.6 collective-permute-start.27
  284.0 1.3 collective-permute-start.30
  286.3 8.4 %second_product.11 = bf16[2,2,512,256]{3,2,1,0:T(8,128)(2,1)} custom-call(s32[1]{0:T(128)} %bitcast.pick_ref, bf16[2,2,2,512,512]{4,3,2,1,0:T(8,128)(2,1)} %first_product.2.own_ref, bf16[2,2,2,512,512]{4,3,2,1,0:T(8,128)(2,1)} %collective-permute-done.19.sib_ref, bf16[2,2,128,1024]{3,2,1,0:T(8,128)(2,1)} %collective-permute-done.21.refs_0_, ...), custom_call_target="tpu_custom_call" | custom-call | tf_op jit(solution)/shard_map/second_product/pallas_call | solution.py:104
  294.7 1.8 collective-permute-start.31
  296.4 8.4 %collective-permute-done.32 = bf16[2,2,512,256]{3,2,1,0:T(8,128)(2,1)} collective-permute-done((bf16[2,2,512,256]{3,2,1,0:T(8,128)(2,1)}, bf16[2,2,512,256]{3,2,1,0:T(8,128)(2,1)}, u32[]{:S(2)}, u32[]{:S(2)}) %collective-permute-start.32) | collective-permute-done | bytes 1048608 | tf_op jit(solution)/shard_map/ppermute | solution.py:203
  305.8 5.1 %collective-permute-start.33 = (bf16[2,2,512,256]{3,2,1,0:T(8,128)(2,1)}, bf16[2,2,512,256]{3,2,1,0:T(8,128)(2,1)}, u32[]{:S(2)}, u32[]{:S(2)}) collective-permute-start(bf16[2,2,512,256]{3,2,1,0:T(8,128)(2,1)} %collective-permute-done.32), channel_id=1, source_target_pairs={{0,2},{1,3},{14,12},{15,13},{16,18},{17,19},{30,28},{31,29}} | collective-permute-start | bytes 3145736 | tf_op jit(solution)/shard_map/ppermute | solution.py:212
  311.0 2.9 select_select_fusion
  315.1 15.3 %collective-permute-done.33 = bf16[2,2,512,256]{3,2,1,0:T(8,128)(2,1)} collective-permute-done((bf16[2,2,512,256]{3,2,1,0:T(8,128)(2,1)}, bf16[2,2,512,256]{3,2,1,0:T(8,128)(2,1)}, u32[]{:S(2)}, u32[]{:S(2)}) %collective-permute-start.33) | collective-permute-done | bytes 1048608 | tf_op jit(solution)/shard_map/ppermute | solution.py:212
  330.5 1.6 select_convert_fusion
  332.1 3.2 collective-permute-start.34
  335.3 2.9 fusion.mine_ref
  339.2 4.4 %finish.1 = f32[2,2,512,512]{3,2,1,0:T(8,128)} custom-call(s32[1]{0:T(128)} %bitcast.pick_ref, f32[2,2,512,256]{3,2,1,0:T(8,128)} %fusion.mine_ref, bf16[2,2,512,256]{3,2,1,0:T(8,128)(2,1)} %copy-done.23), custom_call_target="tpu_custom_call" | custom-call | tf_op jit(solution)/shard_map/finish/pallas_call | solution.py:126
  (98 shorter events, 19.2 us)
Async XLA Ops:
  1.7 12.9 %copy-start.2 = (bf16[1,2,512,512]{3,2,1,0:T(8,128)(2,1)}, bf16[1,2,512,512]{3,2,1,0:T(8,128)(2,1)S(1)}, u32[]{:S(2)}) copy-start(bf16[1,2,512,512]{3,2,1,0:T(8,128)(2,1)S(1)} %get-tuple-element.71.refs_0_) | copy-start | bytes 3145732
  1.7 2.7 collective-permute-start
  4.5 1.0 copy-start.3
  9.0 5.5 %copy-start.4 = (bf16[1,2,512,512]{3,2,1,0:T(8,128)(2,1)S(1)}, bf16[1,2,512,512]{3,2,1,0:T(8,128)(2,1)}, u32[]{:S(2)}) copy-start(bf16[1,2,512,512]{3,2,1,0:T(8,128)(2,1)} %copy-done.3) | copy-start | bytes 3145732
  9.0 59.8 %copy-start.24 = (f32[2,2,2,2]{3,2,1,0:T(2,128)S(1)}, f32[2,2,2,2]{3,2,1,0:T(2,128)}, u32[]{:S(2)}) copy-start(f32[2,2,2,2]{3,2,1,0:T(2,128)} %param.5) | copy-start | bytes 196
  10.8 205.3 %copy-start.1 = (bf16[2,2,256,1024]{3,2,1,0:T(8,128)(2,1)}, bf16[2,2,256,1024]{3,2,1,0:T(8,128)(2,1)S(1)}, u32[]{:S(2)}) copy-start(bf16[2,2,256,1024]{3,2,1,0:T(8,128)(2,1)S(1)} %get-tuple-element.56.refs_0_) | copy-start | bytes 6291460
  10.9 50.5 %collective-permute-start.7 = (bf16[2,2,256,1024]{3,2,1,0:T(8,128)(2,1)S(1)}, bf16[2,2,256,1024]{3,2,1,0:T(8,128)(2,1)}, u32[]{:S(2)}, u32[]{:S(2)}) collective-permute-start(bf16[2,2,256,1024]{3,2,1,0:T(8,128)(2,1)S(1)} %get-tuple-element.56.refs_0_), channel_id=1, source_target_pairs={{0,2},{2,0},{1,3},{3,1},{4,6},{6,4},{5,7},{7,5},{8,10},{10,8},{9,1... | collective-permute-start | bytes 6291464 | tf_op jit(solution)/shard_map/ppermute | solution.py:205
  13.2 24.2 %collective-permute-start.1 = (bf16[1,2,512,512]{3,2,1,0:T(8,128)(2,1)S(1)}, bf16[1,2,512,512]{3,2,1,0:T(8,128)(2,1)}, u32[]{:S(2)}, u32[]{:S(2)}) collective-permute-start(bf16[1,2,512,512]{3,2,1,0:T(8,128)(2,1)S(1)} %get-tuple-element.71.refs_0_), channel_id=1, source_target_pairs={{0,4},{4,0},{8,12},{12,8},{1,5},{5,1},{9,13},{13,9},{2,6},{6,2},{1... | collective-permute-start | bytes 3145736 | tf_op jit(solution)/shard_map/ppermute | solution.py:201
  14.5 45.3 %collective-permute-start.2 = (bf16[1,2,512,512]{3,2,1,0:T(8,128)(2,1)S(1)}, bf16[1,2,512,512]{3,2,1,0:T(8,128)(2,1)}, u32[]{:S(2)}, u32[]{:S(2)}) collective-permute-start(bf16[1,2,512,512]{3,2,1,0:T(8,128)(2,1)S(1)} %copy-done.4), channel_id=1, source_target_pairs={{0,4},{4,0},{8,12},{12,8},{1,5},{5,1},{9,13},{13,9},{2,6},{6,2},{1... | collective-permute-start | bytes 3145736 | tf_op jit(solution)/shard_map/ppermute | solution.py:201
  14.7 47.8 %collective-permute-start.3 = (bf16[1,2,512,512]{3,2,1,0:T(8,128)(2,1)S(1)}, bf16[1,2,512,512]{3,2,1,0:T(8,128)(2,1)}, u32[]{:S(2)}, u32[]{:S(2)}) collective-permute-start(bf16[1,2,512,512]{3,2,1,0:T(8,128)(2,1)S(1)} %get-tuple-element.71.refs_0_), channel_id=1, source_target_pairs={{4,8},{8,4},{5,9},{9,5},{6,10},{10,6},{7,11},{11,7},{20,24},{24,20... | collective-permute-start | bytes 3145736 | tf_op jit(solution)/shard_map/ppermute | solution.py:204
  16.3 46.2 %collective-permute-start.4 = (bf16[1,2,512,512]{3,2,1,0:T(8,128)(2,1)S(1)}, bf16[1,2,512,512]{3,2,1,0:T(8,128)(2,1)}, u32[]{:S(2)}, u32[]{:S(2)}) collective-permute-start(bf16[1,2,512,512]{3,2,1,0:T(8,128)(2,1)S(1)} %copy-done.4), channel_id=1, source_target_pairs={{4,8},{8,4},{5,9},{9,5},{6,10},{10,6},{7,11},{11,7},{20,24},{24,20... | collective-permute-start | bytes 3145736 | tf_op jit(solution)/shard_map/ppermute | solution.py:204
  59.8 32.1 %collective-permute-start.6 = (bf16[2,2,256,1024]{3,2,1,0:T(8,128)(2,1)S(1)}, bf16[2,2,256,1024]{3,2,1,0:T(8,128)(2,1)}, u32[]{:S(2)}, u32[]{:S(2)}) collective-permute-start(bf16[2,2,256,1024]{3,2,1,0:T(8,128)(2,1)S(1)} %get-tuple-element.56.refs_0_), channel_id=1, source_target_pairs={{0,1},{1,0},{2,3},{3,2},{4,5},{5,4},{6,7},{7,6},{8,9},{9,8},{10,11... | collective-permute-start | bytes 6291464 | tf_op jit(solution)/shard_map/ppermute | solution.py:143
  61.3 30.6 %collective-permute-start.8 = (bf16[2,2,256,1024]{3,2,1,0:T(8,128)(2,1)}, bf16[2,2,256,1024]{3,2,1,0:T(8,128)(2,1)}, u32[]{:S(2)}, u32[]{:S(2)}) collective-permute-start(bf16[2,2,256,1024]{3,2,1,0:T(8,128)(2,1)} %collective-permute-done.7), channel_id=1, source_target_pairs={{0,1},{1,0},{2,3},{3,2},{4,5},{5,4},{6,7},{7,6},{8,9},{9,8},{10,11... | collective-permute-start | bytes 6291464 | tf_op jit(solution)/shard_map/ppermute | solution.py:143
  62.5 23.9 %collective-permute-start.5 = (bf16[2,2,128,1024]{3,2,1,0:T(8,128)(2,1)}, bf16[2,2,128,1024]{3,2,1,0:T(8,128)(2,1)}, u32[]{:S(2)}, u32[]{:S(2)}) collective-permute-start(bf16[2,2,128,1024]{3,2,1,0:T(8,128)(2,1)} %slice.16), channel_id=1, source_target_pairs={{0,4},{12,8},{1,5},{13,9},{2,6},{14,10},{3,7},{15,11},{16,20},{28,... | collective-permute-start | bytes 3145736 | tf_op jit(solution)/shard_map/ppermute | solution.py:202
  66.7 21.1 %collective-permute-start.9 = (bf16[1,2,512,512]{3,2,1,0:T(8,128)(2,1)}, bf16[1,2,512,512]{3,2,1,0:T(8,128)(2,1)S(1)}, u32[]{:S(2)}, u32[]{:S(2)}) collective-permute-start(bf16[1,2,512,512]{3,2,1,0:T(8,128)(2,1)} %collective-permute-done.1.refs_2_), channel_id=1, source_target_pairs={{4,8},{8,4},{5,9},{9,5},{6,10},{10,6},{7,11},{11,7},{20,24},{24,20... | collective-permute-start | bytes 3145736 | tf_op jit(solution)/shard_map/ppermute | solution.py:204
  67.5 24.4 %collective-permute-start.10 = (bf16[1,2,512,512]{3,2,1,0:T(8,128)(2,1)}, bf16[1,2,512,512]{3,2,1,0:T(8,128)(2,1)}, u32[]{:S(2)}, u32[]{:S(2)}) collective-permute-start(bf16[1,2,512,512]{3,2,1,0:T(8,128)(2,1)} %collective-permute-done.3.refs_4_), channel_id=1, source_target_pairs={{4,0},{8,12},{5,1},{9,13},{6,2},{10,14},{7,3},{11,15},{20,16},{24,... | collective-permute-start | bytes 3145736 | tf_op jit(solution)/shard_map/ppermute | solution.py:203
  87.9 16.1 %copy-start.6 = (bf16[1,2,512,512]{3,2,1,0:T(8,128)(2,1)}, bf16[1,2,512,512]{3,2,1,0:T(8,128)(2,1)S(1)}, u32[]{:S(2)}) copy-start(bf16[1,2,512,512]{3,2,1,0:T(8,128)(2,1)S(1)} %collective-permute-done.9.refs_6_) | copy-start | bytes 3145732
  91.9 20.9 %collective-permute-start.12 = (bf16[2,2,128,1024]{3,2,1,0:T(8,128)(2,1)}, bf16[2,2,128,1024]{3,2,1,0:T(8,128)(2,1)}, u32[]{:S(2)}, u32[]{:S(2)}) collective-permute-start(bf16[2,2,128,1024]{3,2,1,0:T(8,128)(2,1)} %get-tuple-element.59), channel_id=1, source_target_pairs={{0,4},{12,8},{1,5},{13,9},{2,6},{14,10},{3,7},{15,11},{16,20},{28,... | collective-permute-start | bytes 3145736 | tf_op jit(solution)/shard_map/ppermute | solution.py:202
  94.8 21.4 %collective-permute-start.14 = (bf16[2,2,128,1024]{3,2,1,0:T(8,128)(2,1)}, bf16[2,2,128,1024]{3,2,1,0:T(8,128)(2,1)S(1)}, u32[]{:S(2)}, u32[]{:S(2)}) collective-permute-start(bf16[2,2,128,1024]{3,2,1,0:T(8,128)(2,1)} %get-tuple-element.42), channel_id=1, source_target_pairs={{0,2},{2,0},{1,3},{3,1},{4,6},{6,4},{5,7},{7,5},{8,10},{10,8},{9,1... | collective-permute-start | bytes 3145736 | tf_op jit(solution)/shard_map/ppermute | solution.py:205
  96.2 20.1 %collective-permute-start.11 = (bf16[1,2,512,512]{3,2,1,0:T(8,128)(2,1)}, bf16[1,2,512,512]{3,2,1,0:T(8,128)(2,1)S(1)}, u32[]{:S(2)}, u32[]{:S(2)}) collective-permute-start(bf16[1,2,512,512]{3,2,1,0:T(8,128)(2,1)} %collective-permute-done.2.refs_3_), channel_id=1, source_target_pairs={{4,8},{8,4},{5,9},{9,5},{6,10},{10,6},{7,11},{11,7},{20,24},{24,20... | collective-permute-start | bytes 3145736 | tf_op jit(solution)/shard_map/ppermute | solution.py:204
  96.9 23.0 %collective-permute-start.17 = (bf16[1,2,512,512]{3,2,1,0:T(8,128)(2,1)}, bf16[1,2,512,512]{3,2,1,0:T(8,128)(2,1)S(1)}, u32[]{:S(2)}, u32[]{:S(2)}) collective-permute-start(bf16[1,2,512,512]{3,2,1,0:T(8,128)(2,1)} %collective-permute-done.4.refs_5_), channel_id=1, source_target_pairs={{4,0},{8,12},{5,1},{9,13},{6,2},{10,14},{7,3},{11,15},{20,16},{24,... | collective-permute-start | bytes 3145736 | tf_op jit(solution)/shard_map/ppermute | solution.py:203
  112.9 46.7 %collective-permute-start.15 = (bf16[2,2,128,1024]{3,2,1,0:T(8,128)(2,1)S(1)}, bf16[2,2,128,1024]{3,2,1,0:T(8,128)(2,1)}, u32[]{:S(2)}, u32[]{:S(2)}) collective-permute-start(bf16[2,2,128,1024]{3,2,1,0:T(8,128)(2,1)S(1)} %broadcast_select_fusion.6), channel_id=1, source_target_pairs={{0,2},{2,0},{1,3},{3,1},{4,6},{6,4},{5,7},{7,5},{8,10},{10,8},{9,1... | collective-permute-start | bytes 3145736 | tf_op jit(solution)/shard_map/ppermute | solution.py:205
  116.2 12.3 %copy-start.11 = (bf16[2,2,128,1024]{3,2,1,0:T(8,128)(2,1)}, bf16[2,2,128,1024]{3,2,1,0:T(8,128)(2,1)S(1)}, u32[]{:S(2)}) copy-start(bf16[2,2,128,1024]{3,2,1,0:T(8,128)(2,1)S(1)} %collective-permute-done.14) | copy-start | bytes 3145732
  116.3 12.3 %copy-start.8 = (bf16[1,2,512,512]{3,2,1,0:T(8,128)(2,1)}, bf16[1,2,512,512]{3,2,1,0:T(8,128)(2,1)S(1)}, u32[]{:S(2)}) copy-start(bf16[1,2,512,512]{3,2,1,0:T(8,128)(2,1)S(1)} %collective-permute-done.11.refs_7_) | copy-start | bytes 3145732
  119.9 8.6 %copy-start.21 = (bf16[1,2,512,512]{3,2,1,0:T(8,128)(2,1)}, bf16[1,2,512,512]{3,2,1,0:T(8,128)(2,1)S(1)}, u32[]{:S(2)}) copy-start(bf16[1,2,512,512]{3,2,1,0:T(8,128)(2,1)S(1)} %collective-permute-done.17) | copy-start | bytes 3145732
  121.1 44.6 %collective-permute-start.18 = (bf16[2,2,512,512]{3,2,1,0:T(8,128)(2,1)}, bf16[2,2,512,512]{3,2,1,0:T(8,128)(2,1)}, u32[]{:S(2)}, u32[]{:S(2)}) collective-permute-start(bf16[2,2,512,512]{3,2,1,0:T(8,128)(2,1)} %constant_dynamic-update-slice_fusion), channel_id=1, source_target_pairs={{4,0},{8,12},{5,1},{9,13},{6,2},{10,14},{7,3},{11,15},{20,16},{24,... | collective-permute-start | bytes 6291464 | tf_op jit(solution)/shard_map/ppermute | solution.py:203
  122.4 43.3 %collective-permute-start.20 = (bf16[2,2,256,1024]{3,2,1,0:T(8,128)(2,1)S(1)}, bf16[2,2,256,1024]{3,2,1,0:T(8,128)(2,1)}, u32[]{:S(2)}, u32[]{:S(2)}) collective-permute-start(bf16[2,2,256,1024]{3,2,1,0:T(8,128)(2,1)S(1)} %get-tuple-element.56.refs_0_), channel_id=1, source_target_pairs={{4,8},{8,4},{5,9},{9,5},{6,10},{10,6},{7,11},{11,7},{20,24},{24,20... | collective-permute-start | bytes 6291464 | tf_op jit(solution)/shard_map/ppermute | solution.py:204
  153.3 6.3 %copy-start.12 = (bf16[2,2,128,1024]{3,2,1,0:T(8,128)(2,1)S(1)}, bf16[2,2,128,1024]{3,2,1,0:T(8,128)(2,1)}, u32[]{:S(2)}) copy-start(bf16[2,2,128,1024]{3,2,1,0:T(8,128)(2,1)} %copy-done.11) | copy-start | bytes 3145732
  154.8 9.3 %copy-start = (bf16[2,2,2,512,512]{4,3,2,1,0:T(8,128)(2,1)S(1)}, bf16[2,2,2,512,512]{4,3,2,1,0:T(8,128)(2,1)}, u32[]{:S(2)}) copy-start(bf16[2,2,2,512,512]{4,3,2,1,0:T(8,128)(2,1)} %first_product.2.own_ref) | copy-start | bytes 12582916
  154.8 9.6 %copy-start.22 = (bf16[1,2,512,512]{3,2,1,0:T(8,128)(2,1)S(1)}, bf16[1,2,512,512]{3,2,1,0:T(8,128)(2,1)}, u32[]{:S(2)}) copy-start(bf16[1,2,512,512]{3,2,1,0:T(8,128)(2,1)} %copy-done.21) | copy-start | bytes 3145732
  154.8 17.4 %collective-permute-start.13 = (bf16[2,2,256,1024]{3,2,1,0:T(8,128)(2,1)S(1)}, bf16[2,2,256,1024]{3,2,1,0:T(8,128)(2,1)S(1)}, u32[]{:S(2)}, u32[]{:S(2)}) collective-permute-start(bf16[2,2,256,1024]{3,2,1,0:T(8,128)(2,1)S(1)} %pad_maximum_fusion), channel_id=1, source_target_pairs={{0,1},{1,0},{2,3},{3,2},{4,5},{5,4},{6,7},{7,6},{8,9},{9,8},{10,11... | collective-permute-start | bytes 6291464 | tf_op jit(solution)/shard_map/ppermute | solution.py:143
  161.0 15.0 %collective-permute-start.16 = (bf16[2,2,256,1024]{3,2,1,0:T(8,128)(2,1)S(1)}, bf16[2,2,256,1024]{3,2,1,0:T(8,128)(2,1)S(1)}, u32[]{:S(2)}, u32[]{:S(2)}) collective-permute-start(bf16[2,2,256,1024]{3,2,1,0:T(8,128)(2,1)S(1)} %pad_maximum_fusion.1), channel_id=1, source_target_pairs={{0,1},{1,0},{2,3},{3,2},{4,5},{5,4},{6,7},{7,6},{8,9},{9,8},{10,11... | collective-permute-start | bytes 6291464 | tf_op jit(solution)/shard_map/ppermute | solution.py:143
  164.1 53.7 %collective-permute-start.19 = (bf16[2,2,2,512,512]{4,3,2,1,0:T(8,128)(2,1)S(1)}, bf16[2,2,2,512,512]{4,3,2,1,0:T(8,128)(2,1)}, u32[]{:S(2)}, u32[]{:S(2)}) collective-permute-start(bf16[2,2,2,512,512]{4,3,2,1,0:T(8,128)(2,1)S(1)} %copy-done), channel_id=1, source_target_pairs={{0,1},{1,0},{2,3},{3,2},{4,5},{5,4},{6,7},{7,6},{8,9},{9,8},{10,11... | collective-permute-start | bytes 12582920 | tf_op jit(solution)/shard_map/ppermute | solution.py:143
  165.7 42.6 %collective-permute-start.21 = (bf16[2,2,128,1024]{3,2,1,0:T(8,128)(2,1)}, bf16[2,2,128,1024]{3,2,1,0:T(8,128)(2,1)}, u32[]{:S(2)}, u32[]{:S(2)}) collective-permute-start(bf16[2,2,128,1024]{3,2,1,0:T(8,128)(2,1)} %collective-permute-done.5.refs_0_), channel_id=1, source_target_pairs={{4,8},{8,4},{5,9},{9,5},{6,10},{10,6},{7,11},{11,7},{20,24},{24,20... | collective-permute-start | bytes 3145736 | tf_op jit(solution)/shard_map/ppermute | solution.py:204
  167.4 41.0 %collective-permute-start.22 = (bf16[2,2,128,1024]{3,2,1,0:T(8,128)(2,1)}, bf16[2,2,128,1024]{3,2,1,0:T(8,128)(2,1)}, u32[]{:S(2)}, u32[]{:S(2)}) collective-permute-start(bf16[2,2,128,1024]{3,2,1,0:T(8,128)(2,1)} %slice.16), channel_id=1, source_target_pairs={{4,0},{8,12},{5,1},{9,13},{6,2},{10,14},{7,3},{11,15},{20,16},{24,... | collective-permute-start | bytes 3145736 | tf_op jit(solution)/shard_map/ppermute | solution.py:203
  208.4 27.2 %collective-permute-start.23 = (bf16[2,2,2,512,512]{4,3,2,1,0:T(8,128)(2,1)}, bf16[2,2,2,512,512]{4,3,2,1,0:T(8,128)(2,1)}, u32[]{:S(2)}, u32[]{:S(2)}) collective-permute-start(bf16[2,2,2,512,512]{4,3,2,1,0:T(8,128)(2,1)} %first_product.3.own_ref), channel_id=1, source_target_pairs={{0,1},{1,0},{2,3},{3,2},{4,5},{5,4},{6,7},{7,6},{8,9},{9,8},{10,11... | collective-permute-start | bytes 12582920 | tf_op jit(solution)/shard_map/ppermute | solution.py:143
  214.1 36.4 %collective-permute-start.28 = (bf16[2,2,128,1024]{3,2,1,0:T(8,128)(2,1)}, bf16[2,2,128,1024]{3,2,1,0:T(8,128)(2,1)S(1)}, u32[]{:S(2)}, u32[]{:S(2)}) collective-permute-start(bf16[2,2,128,1024]{3,2,1,0:T(8,128)(2,1)} %collective-permute-done.12.refs_1_), channel_id=1, source_target_pairs={{4,8},{8,4},{5,9},{9,5},{6,10},{10,6},{7,11},{11,7},{20,24},{24,20... | collective-permute-start | bytes 3145736 | tf_op jit(solution)/shard_map/ppermute | solution.py:204
  214.8 35.7 %collective-permute-start.29 = (bf16[2,2,128,1024]{3,2,1,0:T(8,128)(2,1)}, bf16[2,2,128,1024]{3,2,1,0:T(8,128)(2,1)}, u32[]{:S(2)}, u32[]{:S(2)}) collective-permute-start(bf16[2,2,128,1024]{3,2,1,0:T(8,128)(2,1)} %get-tuple-element.59), channel_id=1, source_target_pairs={{4,0},{8,12},{5,1},{9,13},{6,2},{10,14},{7,3},{11,15},{20,16},{24,... | collective-permute-start | bytes 3145736 | tf_op jit(solution)/shard_map/ppermute | solution.py:203
  226.2 36.9 %collective-permute-start.25 = (bf16[2,2,512,256]{3,2,1,0:T(8,128)(2,1)}, bf16[2,2,512,256]{3,2,1,0:T(8,128)(2,1)S(1)}, u32[]{:S(2)}, u32[]{:S(2)}) collective-permute-start(bf16[2,2,512,256]{3,2,1,0:T(8,128)(2,1)} %second_product.6), channel_id=1, source_target_pairs={{4,6},{5,7},{10,8},{11,9},{20,22},{21,23},{26,24},{27,25}} | collective-permute-start | bytes 3145736 | tf_op jit(solution)/shard_map/ppermute | solution.py:212
  235.6 9.8 %copy-start.10 = (bf16[2,2,512,256]{3,2,1,0:T(8,128)(2,1)S(1)}, bf16[2,2,512,256]{3,2,1,0:T(8,128)(2,1)}, u32[]{:S(2)}) copy-start(bf16[2,2,512,256]{3,2,1,0:T(8,128)(2,1)} %second_product.7) | copy-start | bytes 3145732
  244.2 38.1 %collective-permute-start.26 = (bf16[2,2,512,256]{3,2,1,0:T(8,128)(2,1)}, bf16[2,2,512,256]{3,2,1,0:T(8,128)(2,1)S(1)}, u32[]{:S(2)}, u32[]{:S(2)}) collective-permute-start(bf16[2,2,512,256]{3,2,1,0:T(8,128)(2,1)} %second_product.8), channel_id=1, source_target_pairs={{4,0},{8,12},{5,1},{9,13},{6,2},{10,14},{7,3},{11,15},{20,16},{24,... | collective-permute-start | bytes 3145736 | tf_op jit(solution)/shard_map/ppermute | solution.py:203
  246.8 38.4 %collective-permute-start.24 = (bf16[2,2,512,256]{3,2,1,0:T(8,128)(2,1)S(1)}, bf16[2,2,512,256]{3,2,1,0:T(8,128)(2,1)S(1)}, u32[]{:S(2)}, u32[]{:S(2)}) collective-permute-start(bf16[2,2,512,256]{3,2,1,0:T(8,128)(2,1)S(1)} %broadcast_select_fusion.9), channel_id=1, source_target_pairs={{2,0},{3,1},{6,4},{7,5},{8,10},{9,11},{12,14},{13,15},{18,16},{19,... | collective-permute-start | bytes 3145736 | tf_op jit(solution)/shard_map/ppermute | solution.py:212
  250.5 11.1 %copy-start.7 = (bf16[2,2,128,1024]{3,2,1,0:T(8,128)(2,1)}, bf16[2,2,128,1024]{3,2,1,0:T(8,128)(2,1)S(1)}, u32[]{:S(2)}) copy-start(bf16[2,2,128,1024]{3,2,1,0:T(8,128)(2,1)S(1)} %collective-permute-done.28.refs_1_) | copy-start | bytes 3145732
  261.6 22.2 %copy-start.9 = (bf16[2,2,512,256]{3,2,1,0:T(8,128)(2,1)S(1)}, bf16[2,2,512,256]{3,2,1,0:T(8,128)(2,1)}, u32[]{:S(2)}) copy-start(bf16[2,2,512,256]{3,2,1,0:T(8,128)(2,1)} %second_product.9) | copy-start | bytes 3145732
  261.6 43.2 %collective-permute-start.32 = (bf16[2,2,512,256]{3,2,1,0:T(8,128)(2,1)}, bf16[2,2,512,256]{3,2,1,0:T(8,128)(2,1)}, u32[]{:S(2)}, u32[]{:S(2)}) collective-permute-start(bf16[2,2,512,256]{3,2,1,0:T(8,128)(2,1)} %second_product.9), channel_id=1, source_target_pairs={{4,0},{8,12},{5,1},{9,13},{6,2},{10,14},{7,3},{11,15},{20,16},{24,... | collective-permute-start | bytes 3145736 | tf_op jit(solution)/shard_map/ppermute | solution.py:203
  263.1 8.8 %copy-start.13 = (bf16[2,2,512,256]{3,2,1,0:T(8,128)(2,1)}, bf16[2,2,512,256]{3,2,1,0:T(8,128)(2,1)S(1)}, u32[]{:S(2)}) copy-start(bf16[2,2,512,256]{3,2,1,0:T(8,128)(2,1)S(1)} %collective-permute-done.25) | copy-start | bytes 3145732
  282.2 12.4 %copy-start.15 = (bf16[2,2,512,256]{3,2,1,0:T(8,128)(2,1)}, bf16[2,2,512,256]{3,2,1,0:T(8,128)(2,1)S(1)}, u32[]{:S(2)}) copy-start(bf16[2,2,512,256]{3,2,1,0:T(8,128)(2,1)S(1)} %collective-permute-done.26) | copy-start | bytes 3145732
  282.3 22.6 %collective-permute-start.27 = (bf16[2,2,512,256]{3,2,1,0:T(8,128)(2,1)S(1)}, bf16[2,2,512,256]{3,2,1,0:T(8,128)(2,1)S(1)}, u32[]{:S(2)}, u32[]{:S(2)}) collective-permute-start(bf16[2,2,512,256]{3,2,1,0:T(8,128)(2,1)S(1)} %collective-permute-done.26), channel_id=1, source_target_pairs={{0,2},{1,3},{14,12},{15,13},{16,18},{17,19},{30,28},{31,29}} | collective-permute-start | bytes 3145736 | tf_op jit(solution)/shard_map/ppermute | solution.py:212
  284.0 27.0 %collective-permute-start.30 = (bf16[2,2,512,256]{3,2,1,0:T(8,128)(2,1)S(1)}, bf16[2,2,512,256]{3,2,1,0:T(8,128)(2,1)}, u32[]{:S(2)}, u32[]{:S(2)}) collective-permute-start(bf16[2,2,512,256]{3,2,1,0:T(8,128)(2,1)S(1)} %broadcast_select_fusion.8), channel_id=1, source_target_pairs={{2,0},{3,1},{6,4},{7,5},{8,10},{9,11},{12,14},{13,15},{18,16},{19,... | collective-permute-start | bytes 3145736 | tf_op jit(solution)/shard_map/ppermute | solution.py:212
  285.3 1.0 copy-start.17
  294.7 19.3 %copy-start.5 = (bf16[2,2,512,256]{3,2,1,0:T(8,128)(2,1)S(1)}, bf16[2,2,512,256]{3,2,1,0:T(8,128)(2,1)}, u32[]{:S(2)}) copy-start(bf16[2,2,512,256]{3,2,1,0:T(8,128)(2,1)} %second_product.6) | copy-start | bytes 3145732
  294.7 16.3 %collective-permute-start.31 = (bf16[2,2,512,256]{3,2,1,0:T(8,128)(2,1)}, bf16[2,2,512,256]{3,2,1,0:T(8,128)(2,1)}, u32[]{:S(2)}, u32[]{:S(2)}) collective-permute-start(bf16[2,2,512,256]{3,2,1,0:T(8,128)(2,1)} %second_product.11), channel_id=1, source_target_pairs={{4,6},{5,7},{10,8},{11,9},{20,22},{21,23},{26,24},{27,25}} | collective-permute-start | bytes 3145736 | tf_op jit(solution)/shard_map/ppermute | solution.py:212
  304.9 1.0 copy-start.19
  305.8 24.6 %collective-permute-start.33 = (bf16[2,2,512,256]{3,2,1,0:T(8,128)(2,1)}, bf16[2,2,512,256]{3,2,1,0:T(8,128)(2,1)}, u32[]{:S(2)}, u32[]{:S(2)}) collective-permute-start(bf16[2,2,512,256]{3,2,1,0:T(8,128)(2,1)} %collective-permute-done.32), channel_id=1, source_target_pairs={{0,2},{1,3},{14,12},{15,13},{16,18},{17,19},{30,28},{31,29}} | collective-permute-start | bytes 3145736 | tf_op jit(solution)/shard_map/ppermute | solution.py:212
  311.0 3.0 copy-start.14
  311.0 3.0 copy-start.16
  311.0 3.1 copy-start.18
  311.0 3.4 copy-start.20
  332.1 6.1 %collective-permute-start.34 = (bf16[2,2,512,256]{3,2,1,0:T(8,128)(2,1)S(1)}, bf16[2,2,512,256]{3,2,1,0:T(8,128)(2,1)S(1)}, u32[]{:S(2)}, u32[]{:S(2)}) collective-permute-start(bf16[2,2,512,256]{3,2,1,0:T(8,128)(2,1)S(1)} %select_convert_fusion), channel_id=1, source_target_pairs={{0,1},{1,0},{2,3},{3,2},{4,5},{5,4},{6,7},{7,6},{8,9},{9,8},{10,11... | collective-permute-start | bytes 3145736 | tf_op jit(solution)/shard_map/ppermute | solution.py:143
  338.2 1.0 copy-start.23

commit v10 on v9

--- a/solution.py
+++ b/solution.py
@@ -26,21 +26,58 @@
     return lax.dot_general(left, right, (((1,), (1,)), ((), ())), preferred_element_type=F32)
 
 
-def first_kernel(block_ref, mpo_ref, site_ref, *refs):
-    q_ref, g_ref = refs[-2:]
-    env_refs = refs[:-2]
-    mpo_count, phys, _, rows, _ = q_ref.shape
-    depth = env_refs[0].shape[2]
+def first_kernel(sources, pick_ref, mpo_ref, *refs):
+    q_ref, site_ref, env_ref, g_ref, site_sems, env_sems = refs[-6:]
+    site_refs, env_refs = refs[:4], refs[4:-6]
+    mpo_count, phys, _, rows, cols = q_ref.shape
+    w_local, _, depth, _ = env_ref.shape[1:]
     per_col = site_ref.shape[-1] // depth
-    w_local = mpo_count // 2
+    tile, col_tile = pl.program_id(0), pl.program_id(1)
+
+    def site_copy(which, other):
+        there = 1 - pick_ref[1] if other else pick_ref[1]
+        return pltpu.make_async_copy(
+            site_refs[other * 2 + which], site_ref.at[which, there], site_sems.at[which, other]
+        )
+
+    def env_copy(number, at_end):
+        source, first = sources[number][1 if at_end and len(sources[number]) > 1 else 0]
+        return pltpu.make_async_copy(
+            env_refs[source].at[pl.ds(first, w_local)], env_ref.at[number], env_sems.at[number]
+        )
+
+    def start_envs(at_end):
+        for number in range(len(sources)):
+            env_copy(number, at_end).start()
+
+    @pl.when((tile == 0) & (col_tile == 0))
+    def _():
+        for other in range(2):
+            site_copy(0, other).start()
+        pl.when(pick_ref[2] == 0)(functools.partial(start_envs, False))
+        pl.when(pick_ref[2] != 0)(functools.partial(start_envs, True))
+        for other in range(2):
+            site_copy(1, other).start()
+        for other in range(2):
+            site_copy(0, other).wait()
+        for number in range(len(sources)):
+            env_copy(number, False).wait()
+
+    @pl.when((tile == 1) & (col_tile == 0))
+    def _():
+        for other in range(2):
+            site_copy(1, other).wait()
+
+    columns = pl.ds(pl.multiple_of(col_tile * cols, cols), cols)
     for w in range(mpo_count):
         with_real, with_imag = None, None
-        for number in range(len(env_refs) // 2):
-            env_ref = env_refs[number * 2 + w // w_local]
-            block = block_ref[number]
+        for number in range(len(sources) // 2):
+            block = pick_ref[3 + number]
             piece = pl.ds(pl.multiple_of((block % per_col) * depth, depth), depth)
-            left = site_ref[block // per_col, :, :, :, piece].reshape(phys * 2 * rows, depth)
-            more_real, more_imag = mul(left, env_ref[w % w_local, 0]), mul(left, env_ref[w % w_local, 1])
+            left = site_ref[tile, block // per_col, :, :, :, piece].reshape(phys * 2 * rows, depth)
+            env = number * 2 + w // w_local
+            more_real = mul(left, env_ref[env, w % w_local, 0, :, columns])
+            more_imag = mul(left, env_ref[env, w % w_local, 1, :, columns])
             with_real = more_real if with_real is None else with_real + more_real
             with_imag = more_imag if with_imag is None else with_imag + more_imag
         for s in range(phys):
@@ -59,59 +96,114 @@
                 q_ref[v, t, part] = total.astype(BF16)
 
 
-def first_product(blocks, mpo, site, envs, row_tile, col_tile):
-    col_count, phys, _, rows, wide = site.shape
-    w_local, _, depth, cols = envs[0].shape
+def first_product(pick, mpo, site, envs, col_tile):
+    phys, _, half, wide = site[0].shape
+    arrays, sources = [], []
+    for choices in envs:
+        sources.append([])
+        for array, start in choices:
+            known = [number for number, one in enumerate(arrays) if one is array]
+            if not known:
+                arrays.append(array)
+            sources[-1].append((known[0] if known else len(arrays) - 1, start))
+    _, _, depth, cols = arrays[0].shape
     mpo_count = mpo.shape[1]
-    smem = pl.BlockSpec(memory_space=pltpu.SMEM)
+    w_local = mpo_count // 2
+    anywhere = pl.BlockSpec(memory_space=pl.ANY)
     return pl.pallas_call(
-        first_kernel,
-        grid=(rows // row_tile, cols // col_tile),
-        in_specs=[
-            smem,
-            smem,
-            pl.BlockSpec((col_count, phys, 2, row_tile, wide), lambda i, j: (0, 0, 0, i, 0)),
-        ]
-        + [pl.BlockSpec((w_local, 2, depth, col_tile), lambda i, j: (0, 0, 0, j))] * len(envs),
-        out_specs=pl.BlockSpec((mpo_count, phys, 2, row_tile, col_tile), lambda i, j: (0, 0, 0, i, j)),
-        out_shape=jax.ShapeDtypeStruct((mpo_count, phys, 2, rows, cols), BF16),
-        scratch_shapes=[pltpu.VMEM((mpo_count, 2, phys * row_tile, col_tile), F32)],
+        functools.partial(first_kernel, sources),
+        grid_spec=pltpu.PrefetchScalarGridSpec(
+            num_scalar_prefetch=1,
+            grid=(2, cols // col_tile),
+            in_specs=[pl.BlockSpec(memory_space=pltpu.SMEM)] + [anywhere] * (4 + len(arrays)),
+            out_specs=pl.BlockSpec(
+                (mpo_count, phys, 2, half, col_tile),
+                lambda i, j, pick: (0, 0, 0, jnp.where(i == 0, pick[0], 1 - pick[0]), j),
+            ),
+            scratch_shapes=[
+                pltpu.VMEM((2, 2, phys, 2, half, wide), BF16),
+                pltpu.VMEM((len(sources), w_local, 2, depth, cols), BF16),
+                pltpu.VMEM((mpo_count, 2, phys * half, col_tile), F32),
+                pltpu.SemaphoreType.DMA((2, 2)),
+                pltpu.SemaphoreType.DMA((len(sources),)),
+            ],
+        ),
+        out_shape=jax.ShapeDtypeStruct((mpo_count, phys, 2, 2 * half, cols), BF16),
         compiler_params=params(2),
         cost_estimate=LIGHT,
         name="first_product",
-    )(blocks, mpo, site, *envs)
-
-
-def second_kernel(pick_ref, own_ref, sib_ref, *refs):
-    site_refs, out_ref = refs[:-1], refs[-1]
+    )(pick, mpo, *site, *arrays)
+
+
+def second_kernel(groups, pick_ref, own_ref, sib_ref, *refs):
+    count = len(groups)
+    sems, scratch = refs[-1], refs[-1 - count : -1]
+    out_refs = refs[-1 - 2 * count : -1 - count]
+    site_refs = refs[: -1 - 2 * count]
     phys, _, rows, cols = own_ref.shape[1:]
-    total = None
-    for q_ref, quarter in ((own_ref, pick_ref[0]), (sib_ref, 1 - pick_ref[0])):
-        piece = pl.ds(pl.multiple_of(quarter * cols, cols), cols)
-        for t in range(phys):
-            right = [site_ref[t, part, :, piece] for part in range(2) for site_ref in site_refs]
-            more = mul_t(q_ref[0, t].reshape(2 * rows, cols), jnp.concatenate(right, axis=0))
-            total = more if total is None else total + more
-    width = total.shape[1] // 2
-    out_ref[0, 0] = (total[:rows, :width] - total[rows:, width:]).astype(BF16)
-    out_ref[0, 1] = (total[:rows, width:] + total[rows:, :width]).astype(BF16)
-
-
-def second_product(pick, own, sib, sites):
+
+    def copies(at_end):
+        sem = 0
+        for group, (parts, y_rows) in enumerate(groups):
+            first = 0
+            for choices, extent in parts:
+                source = site_refs[choices[-1] if at_end else choices[0]]
+                for part in range(2):
+                    there = scratch[group].at[:, pl.ds(part * y_rows + first, extent)]
+                    yield pltpu.make_async_copy(source.at[:, part], there, sems.at[sem])
+                    sem += 1
+                first += extent
+
+    def start(at_end):
+        for copy in copies(at_end):
+            copy.start()
+
+    @pl.when(pl.program_id(0) == 0)
+    def _():
+        pl.when(pick_ref[2] == 0)(functools.partial(start, False))
+        pl.when(pick_ref[2] != 0)(functools.partial(start, True))
+        for copy in copies(False):
+            copy.wait()
+
+    for (_, width), site_ref, out_ref in zip(groups, scratch, out_refs):
+        total = None
+        for q_ref, quarter in ((own_ref, pick_ref[0]), (sib_ref, 1 - pick_ref[0])):
+            piece = pl.ds(pl.multiple_of(quarter * cols, cols), cols)
+            for t in range(phys):
+                more = mul_t(q_ref[0, t].reshape(2 * rows, cols), site_ref[t, :, piece])
+                total = more if total is None else total + more
+        out_ref[0, 0] = (total[:rows, :width] - total[rows:, width:]).astype(BF16)
+        out_ref[0, 1] = (total[:rows, width:] + total[rows:, :width]).astype(BF16)
+
+
+def second_product(pick, own, sib, site_groups):
     mpo_count, phys, _, rows, cols = own.shape
-    y_rows = sum(site.shape[2] for site in sites)
-    q_spec = pl.BlockSpec((1, phys, 2, rows, cols), lambda v: (v, 0, 0, 0, 0))
+    arrays, groups = [], []
+    for group in site_groups:
+        parts = []
+        for choices in group:
+            choices = choices if isinstance(choices, tuple) else (choices,)
+            parts.append((list(range(len(arrays), len(arrays) + len(choices))), choices[0].shape[2]))
+            arrays += choices
+        groups.append((parts, sum(extent for _, extent in parts)))
+    wide = arrays[0].shape[3]
+    q_spec = pl.BlockSpec((1, phys, 2, rows, cols), lambda v, pick: (v, 0, 0, 0, 0))
+    widths = [width for _, width in groups]
     return pl.pallas_call(
-        second_kernel,
-        grid=(mpo_count,),
-        in_specs=[pl.BlockSpec(memory_space=pltpu.SMEM), q_spec, q_spec]
-        + [pl.BlockSpec(site.shape, lambda v: (0, 0, 0, 0)) for site in sites],
-        out_specs=pl.BlockSpec((1, 2, rows, y_rows), lambda v: (v, 0, 0, 0)),
-        out_shape=jax.ShapeDtypeStruct((mpo_count, 2, rows, y_rows), BF16),
+        functools.partial(second_kernel, groups),
+        grid_spec=pltpu.PrefetchScalarGridSpec(
+            num_scalar_prefetch=1,
+            grid=(mpo_count,),
+            in_specs=[q_spec, q_spec] + [pl.BlockSpec(memory_space=pl.ANY)] * len(arrays),
+            out_specs=[pl.BlockSpec((1, 2, rows, width), lambda v, pick: (v, 0, 0, 0)) for width in widths],
+            scratch_shapes=[pltpu.VMEM((phys, 2 * width, wide), BF16) for width in widths]
+            + [pltpu.SemaphoreType.DMA((2 * sum(len(parts) for parts, _ in groups),))],
+        ),
+        out_shape=[jax.ShapeDtypeStruct((mpo_count, 2, rows, width), BF16) for width in widths],
         compiler_params=params(1),
         cost_estimate=LIGHT,
         name="second_product",
-    )(pick, own, sib, *sites)
+    )(pick, own, sib, *arrays)
 
 
 def finish_kernel(pick_ref, mine_ref, siblings_ref, out_ref):
@@ -211,44 +303,37 @@
             pairs += [(place(r, 1 - goal, d), place(r, goal, d)) for d in range(2)]
         return lax.ppermute(value, axes, pairs)
 
-    in_order = lambda mine, sibling, axis: jnp.where(
-        depth == 0,
-        jnp.concatenate([mine, sibling], axis=axis),
-        jnp.concatenate([sibling, mine], axis=axis),
-    )
     is_host = (row == 1) | (row == 2)
     hosts_or = lambda at_host, at_end: jnp.where(is_host, at_host, at_end)
 
     env_own, env_sib, mpo_mine = split_inputs(environment, mpo)
+    w_local = environment.shape[0]
     env = [env_own, env_sib]
+    side_env, over_env = [both(env_own)], [across(env_own)]
+    second_part = after(env_sib, side_env[0], over_env[0])
+    side_env.append(both(second_part))
+    over_env.append(across(second_part))
+
     planar = jnp.transpose(after(site_tensor, env_sib), (0, 2, 1, 3))
-    rows = planar.shape[2]
-    half = rows // 2
+    half = planar.shape[2] // 2
     mine = lax.dynamic_slice_in_dim(planar, depth * half, half, 2)
-
-    def rows_of(own, turned, own_swapped, turned_swapped):
-        near = in_order(own, own_swapped, 2)
-        other = in_order(turned, turned_swapped, 2)
-        return jnp.where(col == 0, jnp.stack([near, other]), jnp.stack([other, near]))
-
     parts = [mine[:, :, : half // 2], mine[:, :, half // 2 :]]
-    side_env, over_env = [both(one) for one in env], [across(one) for one in env]
     turned = turn(mine)
-    swapped = [swap(after(value, *side_env)) for value in (mine, turned)]
-    far_env, over_side_env, side_parts, there_parts, turned_parts = [], [], [], [], []
+    site_here = [mine, swap(after(mine, *side_env)), turned, swap(after(turned, *side_env))]
+    far_env, over_side_env, side_parts = [], [], []
     gates = (*side_env, *over_env)
     for m in range(2):
         far_env.append(to_end(after(over_env[m], *gates)))
         over_side_env.append(across(after(side_env[m], *gates)))
         side_parts.append(to_host(after(parts[m], *gates)))
-        there_parts.append(hosts_or(side_parts[m], parts[m]))
-        gates = (far_env[m], over_side_env[m], side_parts[m], *swapped)
-    site_here = rows_of(mine, turned, *swapped)
-    turned_parts = [turn(part) for part in there_parts]
+        gates = (far_env[m], over_side_env[m], side_parts[m], *site_here[1::2])
+    there_parts = [hosts_or(side_parts[0], parts[0])]
+    turned_parts = [turn(there_parts[0])]
+    there_parts.append(hosts_or(side_parts[1], after(parts[1], turned_parts[0])))
+    turned_parts.append(turn(there_parts[1]))
     gates = (*gates, turned_parts[0])
     over_site = across(after(mine, *gates))
-    over_side_env_both = jnp.concatenate(over_side_env, axis=0)
-    far_side_env = to_end(after(over_side_env_both, *gates))
+    far_side_env = to_end(after(jnp.concatenate(over_side_env, axis=0), *gates))
     gates = (over_site, far_side_env)
     over_side_parts, host_parts = [], []
     for m in range(2):
@@ -257,51 +342,50 @@
         gates = (over_side_parts[m], host_parts[m])
 
     side = row ^ 1
-    at_host = jnp.stack([row, side, 3 - row, 3 - side]).astype(jnp.int32)
-    at_end = jnp.stack([row, side, 3 - side, 3 - row]).astype(jnp.int32)
-    pick = depth.astype(jnp.int32).reshape(1)
-
-    def first(blocks, site, envs, *earlier):
-        q = first_product(blocks, mpo_mine, site, envs, half, half)
-        return q, swap(after(q, *earlier))
-
-    def second(q, sites, *earlier):
-        return second_product(after(pick, *earlier), q[0], q[1], sites)
-
-    q_here = first(at_host, site_here, env + side_env + over_env + over_side_env)
+    at_host, at_end = (row, side, 3 - row, 3 - side), (row, side, 3 - side, 3 - row)
+    pick_here = jnp.stack([depth, col, 0 * row, *at_host]).astype(jnp.int32)
+    pick_there = jnp.stack(
+        [depth, col, hosts_or(0, 1), *[hosts_or(*pair) for pair in zip(at_host, at_end)]]
+    ).astype(jnp.int32)
+    pick = pick_there[:3]
+
+    def second(q, site_groups, *earlier):
+        outs = second_product(after(pick, *earlier), q[0], q[1], site_groups)
+        return outs if len(outs) > 1 else outs[0]
+
+    whole = lambda arrays: [[(one, 0)] for one in arrays]
+    q_here = first_product(
+        pick_here, mpo_mine, site_here, whole(env + side_env + over_env + over_side_env), half
+    )
     there, turned = (
-        jnp.concatenate([after(part, q_here[0]) for part in pair], axis=2)
+        jnp.concatenate([after(part, q_here) for part in pair], axis=2)
         for pair in (there_parts, turned_parts)
     )
-    site_there = rows_of(there, turned, swap(there), swap(turned))
-    last_env = hosts_or(over_side_env_both, far_side_env)
-    w_local = environment.shape[0]
-    q_there = first(
-        hosts_or(at_host, at_end),
-        site_there,
-        env
-        + side_env
-        + [hosts_or(*pair) for pair in zip(over_env, far_env)]
-        + [last_env[:w_local], last_env[w_local:]],
-        over_side_parts[0],
-        host_parts[0],
-    )
-    here_over = second(q_here, [over_site], q_there[0])
-    here_own = second(q_here, [mine], here_over)
-    there_own = second(q_there, [hosts_or(over_site, after(mine, q_there[0]))], here_own)
-    there_side = second(
-        q_there, [hosts_or(*part) for part in zip(over_side_parts, host_parts)], there_own
-    )
+    q_there = first_product(
+        pick_there,
+        mpo_mine,
+        [there, swap(there), turned, swap(turned)],
+        whole(env + side_env)
+        + [[(at_host, 0), (at_end, 0)] for at_host, at_end in zip(over_env, far_env)]
+        + [[(over_side_env[m], 0), (far_side_env, m * w_local)] for m in range(2)],
+        half,
+    )
+    q_here = (q_here, swap(q_here))
+    q_there = (q_there, swap(after(q_there, over_side_parts[0], host_parts[0])))
+    here_over, here_own = second(q_here, [[over_site], [mine]], q_there[0])
+    there_own = second(q_there, [[(over_site, mine)]], here_own)
+    there_side = second(q_there, [list(zip(over_side_parts, host_parts))], there_own)
     came_here_over = to_col(here_over, (1, 2), True)
     far_there_own = to_end(there_own)
     near_own = hosts_or(here_own, there_own)
     came_near_own = to_col(near_own, range(4), False)
     far_there_side = to_end(there_side)
-    here_side = second(q_here, side_parts, there_side, came_here_over)
+    here_side, here_over_side = second(
+        q_here, [side_parts, over_side_parts], there_side, came_here_over, far_there_own, came_near_own
+    )
     near_side = hosts_or(here_side, there_side)
     came_near_side = to_col(near_side, range(4), False)
     came_far_own = to_col(far_there_own, (0, 3), True)
-    here_over_side = second(q_here, over_side_parts, here_side, far_there_own, came_near_own)
     came_here_over_side = to_col(here_over_side, (1, 2), True)
     came_far_side = to_col(after(far_there_side, came_far_own), (0, 3), True)
 

time: 345 us -> 338 us (0.980)
  other arithmetic: 54.9 us -> 15.3 us
  waiting for transfers between devices: 110 us -> 129 us
  Pallas kernels: 105 us -> 112 us
    select_n x6 -> x0, other arithmetic: 27 us -> none  [the longest x4 18.9 us: four_rows(): jnp.where(depth == 0, jnp.concatenate([mine, sibling], axis=axis), jnp.co...]
    ppermute x3, waiting for transfers between devices: 3.02 us -> 17.8 us  [four_rows(): turn = lambda value: lax.ppermute(value, 'col', [(0, 1), (1, 0)])]
    select_n x11 -> x3, other arithmetic: 15.5 us -> 2.73 us  [four_rows(): hosts_or = lambda at_host, at_end: jnp.where(is_host, at_host, at_end)]
    ppermute x6, waiting for transfers between devices: 15.4 us -> 25.9 us  [to_col(): return lax.ppermute(value, axes, pairs)]
    pallas_call x8 -> x6, Pallas kernels: 100 us -> 107 us  [the longest x2 55.1 us: first_product(): pl.pallas_call(functools.partial(first_kernel, sources), grid_spec=pltpu....]
    ppermute x7, waiting for transfers between devices: 26.7 us -> 21.9 us  [four_rows(): to_end = lambda value: lax.ppermute(value, 'row', [(1, 0), (2, 3)])]
    ppermute x2, starting transfers between devices: 1.47 us -> 5.51 us  [four_rows(): lax.ppermute(value, 'row', [(0, 1), (1, 0), (2, 3), (3, 2)])]
    ppermute x6, starting transfers between devices: 12 us -> 15.8 us  [to_col(): return lax.ppermute(value, axes, pairs)]
  transfers between devices with their start and end apart: 35 -> 35, of which waited for: 13 -> 12; matrix products, arithmetic and copies ran while one was open for 17% -> 8% of each run, Pallas kernels for 29% -> 32%
where the time goes in v10:
time: 338 us; the launch traced here: 337 us
  waiting for transfers between devices  129 us (38%)
  Pallas kernels  112 us (33%)
  starting transfers between devices  60.7 us (18%)
  local copies, waits for them, and re-layouts  19.4 us (6%)
  other arithmetic  15.3 us (5%)
    pallas_call x2, Pallas kernels, first_product(): pl.pallas_call(functools.partial(first_kernel, sources), grid_spec=pltpu....  55.1 us
    pallas_call x4, Pallas kernels, second_product(): pl.pallas_call(functools.partial(second_kernel, groups), grid_spec=pltpu....  52.2 us
    ppermute x2, waiting for transfers between devices, four_rows(): lax.ppermute(value, 'row', [(0, 1), (1, 0), (2, 3), (3, 2)])  39.5 us
    ppermute x6, waiting for transfers between devices, to_col(): return lax.ppermute(value, axes, pairs)  25.9 us
    ppermute x2, waiting for transfers between devices, four_rows(): to_host = lambda value: lax.ppermute(value, 'row', [(0, 1), (3, 2)])  23.7 us
    ppermute x7, waiting for transfers between devices, four_rows(): to_end = lambda value: lax.ppermute(value, 'row', [(1, 0), (2, 3)])  21.9 us
    ppermute x3, waiting for transfers between devices, four_rows(): turn = lambda value: lax.ppermute(value, 'col', [(0, 1), (1, 0)])  17.8 us
    ppermute x6, starting transfers between devices, to_col(): return lax.ppermute(value, axes, pairs)  15.8 us
  transfers between devices with their start and end apart: 35, of which 12 were waited for; matrix products, arithmetic and copies ran while one was open for 8% of the time, Pallas kernels for 32%

profile of v10, /device:TPU:1, one launch (start us, length us, event | category | flops | bytes accessed | tf_op | source)
XLA Modules:
  0.0 336.5 jit_solution(15080391615806010351)
XLA Ops:
  0.0 1.7 constant_dynamic-slice_fusion
  1.8 1.6 collective-permute-start.2
  3.4 4.4 %collective-permute-start.1 = (bf16[1,2,512,512]{3,2,1,0:T(8,128)(2,1)S(1)}, bf16[1,2,512,512]{3,2,1,0:T(8,128)(2,1)}, u32[]{:S(2)}, u32[]{:S(2)}) collective-permute-start(bf16[1,2,512,512]{3,2,1,0:T(8,128)(2,1)S(1)} %get-tuple-element.73.refs_4_), channel_id=1, source_target_pairs={{0,4},{4,0},{8,12},{12,8},{1,5},{5,1},{9,13},{13,9},{2,6},{6,2},{1... | collective-permute-start | bytes 3145736 | tf_op jit(solution)/shard_map/ppermute | solution.py:293
  7.8 1.0 copy-done.5
  8.8 3.5 %copy.4 = bf16[2,512,2,1024]{3,1,2,0:T(8,128)(2,1)S(1)} copy(bf16[2,512,2,1024]{3,2,1,0:T(2,128)(2,1)} %param.4) | data formatting | bytes 8388608 | tf_op jit(solution)/shard_map/optimization_barrier | solution.py:231
  12.6 1.3 collective-permute-start.7
  13.8 17.4 %collective-permute-done.1.refs_6_ = bf16[1,2,512,512]{3,2,1,0:T(8,128)(2,1)} collective-permute-done((bf16[1,2,512,512]{3,2,1,0:T(8,128)(2,1)S(1)}, bf16[1,2,512,512]{3,2,1,0:T(8,128)(2,1)}, u32[]{:S(2)}, u32[]{:S(2)}) %collective-permute-start.1) | collective-permute-done | bytes 1048608 | tf_op jit(solution)/shard_map/ppermute | solution.py:293
  31.2 1.1 collective-permute-start.3
  33.1 22.1 %collective-permute-done.3.refs_7_ = bf16[1,2,512,512]{3,2,1,0:T(8,128)(2,1)S(1)} collective-permute-done((bf16[1,2,512,512]{3,2,1,0:T(8,128)(2,1)S(1)}, bf16[1,2,512,512]{3,2,1,0:T(8,128)(2,1)S(1)}, u32[]{:S(2)}, u32[]{:S(2)}) %collective-permute-start.3) | collective-permute-done | bytes 1048608 | tf_op jit(solution)/shard_map/ppermute | solution.py:293
  55.2 1.6 collective-permute-start.6
  56.8 2.5 collective-permute-done.7.refs_2_
  59.3 1.4 collective-permute-start.8
  60.8 1.0 slice.10
  61.8 1.0 copy-done.9
  62.8 3.0 collective-permute-start.5
  66.5 1.3 collective-permute-start.10
  67.8 19.8 %collective-permute-done.5.refs_0_ = bf16[2,2,128,1024]{3,2,1,0:T(8,128)(2,1)} collective-permute-done((bf16[2,2,128,1024]{3,2,1,0:T(8,128)(2,1)}, bf16[2,2,128,1024]{3,2,1,0:T(8,128)(2,1)}, u32[]{:S(2)}, u32[]{:S(2)}) %collective-permute-start.5) | collective-permute-done | bytes 1048608 | tf_op jit(solution)/shard_map/ppermute | solution.py:294
  87.8 1.3 collective-permute-start.13
  89.1 4.1 %collective-permute-done.10.refs_9_ = bf16[1,2,512,512]{3,2,1,0:T(8,128)(2,1)} collective-permute-done((bf16[1,2,512,512]{3,2,1,0:T(8,128)(2,1)}, bf16[1,2,512,512]{3,2,1,0:T(8,128)(2,1)}, u32[]{:S(2)}, u32[]{:S(2)}) %collective-permute-start.10) | collective-permute-done | bytes 1048608 | tf_op jit(solution)/shard_map/ppermute | solution.py:295
  93.2 1.3 collective-permute-start.12
  95.3 1.3 collective-permute-start.17
  96.6 15.3 %collective-permute-done.13 = bf16[2,2,128,1024]{3,2,1,0:T(8,128)(2,1)S(1)} collective-permute-done((bf16[2,2,128,1024]{3,2,1,0:T(8,128)(2,1)S(1)}, bf16[2,2,128,1024]{3,2,1,0:T(8,128)(2,1)S(1)}, u32[]{:S(2)}, u32[]{:S(2)}) %collective-permute-start.13) | collective-permute-done | bytes 1048608 | tf_op jit(solution)/shard_map/ppermute | solution.py:297
  111.9 3.9 %collective-permute-done.12.refs_1_ = bf16[2,2,128,1024]{3,2,1,0:T(8,128)(2,1)S(1)} collective-permute-done((bf16[2,2,128,1024]{3,2,1,0:T(8,128)(2,1)S(1)}, bf16[2,2,128,1024]{3,2,1,0:T(8,128)(2,1)S(1)}, u32[]{:S(2)}, u32[]{:S(2)}) %collective-permute-start.12) | collective-permute-done | bytes 1048608 | tf_op jit(solution)/shard_map/ppermute | solution.py:294
  115.8 1.2 broadcast_select_fusion
  117.0 1.3 collective-permute-start.15
  118.3 2.3 collective-permute-done.17.refs_11_
  120.6 1.5 pad_maximum_fusion
  122.1 1.3 collective-permute-start.18
  123.4 2.1 collective-permute-start.20
  126.7 27.7 %first_product.2.own_ref = bf16[2,2,2,512,512]{4,3,2,1,0:T(8,128)(2,1)} custom-call(s32[7]{0:T(128)} %stack.50.pick_ref, f32[2,2,2,2]{3,2,1,0:T(2,128)} %pad_maximum_fusion.1.mpo_ref, bf16[2,2,256,1024]{3,2,1,0:T(8,128)(2,1)} %copy-done, bf16[2,2,256,1024]{3,2,1,0:T(8,128)(2,1)} %collective-permute-done.6.refs_1_, ...), custom_call_target="tpu_custom_call" | custom-call | tf_op jit(solution)/shard_map/first_product/pallas_call | solution.py:113
  154.4 1.0 constant_dynamic-update-slice_fusion.1
  155.5 2.3 constant_dynamic-update-slice_fusion.refs_0_
  157.7 2.4 collective-permute-start.14
  160.1 1.1 constant_dynamic-update-slice_fusion.3
  161.2 2.3 constant_dynamic-update-slice_fusion.2.refs_2_
  163.4 5.7 %collective-permute-done.18.refs_13_ = bf16[2,2,512,512]{3,2,1,0:T(8,128)(2,1)} collective-permute-done((bf16[2,2,512,512]{3,2,1,0:T(8,128)(2,1)}, bf16[2,2,512,512]{3,2,1,0:T(8,128)(2,1)}, u32[]{:S(2)}, u32[]{:S(2)}) %collective-permute-start.18) | collective-permute-done | bytes 2097184 | tf_op jit(solution)/shard_map/ppermute | solution.py:295
  169.9 1.5 collective-permute-start.22
  172.1 3.2 collective-permute-start.19
  175.2 27.4 %first_product.3.own_ref = bf16[2,2,2,512,512]{4,3,2,1,0:T(8,128)(2,1)} custom-call(s32[7]{0:T(128)} %stack.47.pick_ref, f32[2,2,2,2]{3,2,1,0:T(2,128)} %pad_maximum_fusion.1.mpo_ref, bf16[2,2,256,1024]{3,2,1,0:T(8,128)(2,1)} %constant_dynamic-update-slice_fusion.refs_0_, bf16[2,2,256,1024]{3,2,1,0:T(8,128)(2,1)} %collective-permute-done.14.refs_1_, ...), custom_call_target="tpu_custom_call" | custom-call | tf_op jit(solution)/shard_map/first_product/pallas_call | solution.py:113
  203.6 1.6 collective-permute-start.28
  205.3 1.3 collective-permute-start.29
  206.6 1.9 copy-done.1
  208.5 15.6 %second_product.4 = (bf16[2,2,512,256]{3,2,1,0:T(8,128)(2,1)}, bf16[2,2,512,256]{3,2,1,0:T(8,128)(2,1)}) custom-call(s32[3]{0:T(128)} %pad_add_fusion.pick_ref, bf16[2,2,2,512,512]{4,3,2,1,0:T(8,128)(2,1)} %first_product.2.own_ref, bf16[2,2,2,512,512]{4,3,2,1,0:T(8,128)(2,1)} %copy-done.1, bf16[2,2,256,1024]{3,2,1,0:T(8,128)(2,1)} %collective-permute-done.20.refs_0_, ...), custom_call_target="tpu_custom_call" | custom-call | tf_op jit(solution)/shard_map/second_product/pallas_call | solution.py:192
  225.0 10.5 %second_product.5 = bf16[2,2,512,256]{3,2,1,0:T(8,128)(2,1)} custom-call(s32[3]{0:T(128)} %pad_add_fusion.pick_ref, bf16[2,2,2,512,512]{4,3,2,1,0:T(8,128)(2,1)} %first_product.3.own_ref, bf16[2,2,2,512,512]{4,3,2,1,0:T(8,128)(2,1)} %collective-permute-done.23.sib_ref, bf16[2,2,256,1024]{3,2,1,0:T(8,128)(2,1)} %collective-permute-done.20.refs_0_, ...), custom_call_target="tpu_custom_call" | custom-call | tf_op jit(solution)/shard_map/second_product/pallas_call | solution.py:192
  235.5 1.4 broadcast_select_fusion.3
  237.0 1.3 collective-permute-start.24
  238.3 1.3 collective-permute-start.26
  239.6 10.5 %second_product.6 = bf16[2,2,512,256]{3,2,1,0:T(8,128)(2,1)} custom-call(s32[3]{0:T(128)} %pad_add_fusion.pick_ref, bf16[2,2,2,512,512]{4,3,2,1,0:T(8,128)(2,1)} %first_product.3.own_ref, bf16[2,2,2,512,512]{4,3,2,1,0:T(8,128)(2,1)} %collective-permute-done.23.sib_ref, bf16[2,2,128,1024]{3,2,1,0:T(8,128)(2,1)} %copy-done.17, ...), custom_call_target="tpu_custom_call" | custom-call | tf_op jit(solution)/shard_map/second_product/pallas_call | solution.py:192
  250.1 1.6 collective-permute-start.32
  251.8 11.6 %collective-permute-done.24 = bf16[2,2,512,256]{3,2,1,0:T(8,128)(2,1)S(1)} collective-permute-done((bf16[2,2,512,256]{3,2,1,0:T(8,128)(2,1)S(1)}, bf16[2,2,512,256]{3,2,1,0:T(8,128)(2,1)S(1)}, u32[]{:S(2)}, u32[]{:S(2)}) %collective-permute-start.24) | collective-permute-done | bytes 1048608 | tf_op jit(solution)/shard_map/ppermute | solution.py:304
  263.4 9.9 %collective-permute-done.26 = bf16[2,2,512,256]{3,2,1,0:T(8,128)(2,1)} collective-permute-done((bf16[2,2,512,256]{3,2,1,0:T(8,128)(2,1)S(1)}, bf16[2,2,512,256]{3,2,1,0:T(8,128)(2,1)}, u32[]{:S(2)}, u32[]{:S(2)}) %collective-permute-start.26) | collective-permute-done | bytes 1048608 | tf_op jit(solution)/shard_map/ppermute | solution.py:295
  273.3 4.7 %collective-permute-start.27 = (bf16[2,2,512,256]{3,2,1,0:T(8,128)(2,1)}, bf16[2,2,512,256]{3,2,1,0:T(8,128)(2,1)}, u32[]{:S(2)}, u32[]{:S(2)}) collective-permute-start(bf16[2,2,512,256]{3,2,1,0:T(8,128)(2,1)} %collective-permute-done.26), channel_id=1, source_target_pairs={{0,2},{1,3},{14,12},{15,13},{16,18},{17,19},{30,28},{31,29}} | collective-permute-start | bytes 3145736 | tf_op jit(solution)/shard_map/ppermute | solution.py:304
  278.0 15.6 %second_product.7 = (bf16[2,2,512,256]{3,2,1,0:T(8,128)(2,1)}, bf16[2,2,512,256]{3,2,1,0:T(8,128)(2,1)}) custom-call(s32[3]{0:T(128)} %pad_add_fusion.pick_ref, bf16[2,2,2,512,512]{4,3,2,1,0:T(8,128)(2,1)} %first_product.2.own_ref, bf16[2,2,2,512,512]{4,3,2,1,0:T(8,128)(2,1)} %copy-done.1, bf16[2,2,128,1024]{3,2,1,0:T(8,128)(2,1)} %collective-permute-done.5.refs_0_, ...), custom_call_target="tpu_custom_call" | custom-call | tf_op jit(solution)/shard_map/second_product/pallas_call | solution.py:192
  293.8 1.3 collective-permute-start.30
  295.1 1.6 collective-permute-start.31
  296.8 6.0 %collective-permute-start.33 = (bf16[2,2,512,256]{3,2,1,0:T(8,128)(2,1)}, bf16[2,2,512,256]{3,2,1,0:T(8,128)(2,1)}, u32[]{:S(2)}, u32[]{:S(2)}) collective-permute-start(bf16[2,2,512,256]{3,2,1,0:T(8,128)(2,1)} %collective-permute-done.32), channel_id=1, source_target_pairs={{0,2},{1,3},{14,12},{15,13},{16,18},{17,19},{30,28},{31,29}} | collective-permute-start | bytes 3145736 | tf_op jit(solution)/shard_map/ppermute | solution.py:304
  302.8 14.2 %collective-permute-done.30 = bf16[2,2,512,256]{3,2,1,0:T(8,128)(2,1)} collective-permute-done((bf16[2,2,512,256]{3,2,1,0:T(8,128)(2,1)S(1)}, bf16[2,2,512,256]{3,2,1,0:T(8,128)(2,1)}, u32[]{:S(2)}, u32[]{:S(2)}) %collective-permute-start.30) | collective-permute-done | bytes 1048608 | tf_op jit(solution)/shard_map/ppermute | solution.py:304
  317.0 2.8 select_select_fusion
  319.8 2.3 select_select_fusion.1
  322.1 1.6 select_convert_fusion
  323.7 4.5 %collective-permute-start.34 = (bf16[2,2,512,256]{3,2,1,0:T(8,128)(2,1)S(1)}, bf16[2,2,512,256]{3,2,1,0:T(8,128)(2,1)S(1)}, u32[]{:S(2)}, u32[]{:S(2)}) collective-permute-start(bf16[2,2,512,256]{3,2,1,0:T(8,128)(2,1)S(1)} %select_convert_fusion), channel_id=1, source_target_pairs={{0,1},{1,0},{2,3},{3,2},{4,5},{5,4},{6,7},{7,6},{8,9},{9,8},{10,11... | collective-permute-start | bytes 3145736 | tf_op jit(solution)/shard_map/ppermute | solution.py:235
  328.2 2.9 fusion.mine_ref
  331.1 1.0 copy-done.28
  332.1 4.4 %finish.1 = f32[2,2,512,512]{3,2,1,0:T(8,128)} custom-call(s32[3]{0:T(128)} %pad_add_fusion.pick_ref, f32[2,2,512,256]{3,2,1,0:T(8,128)} %fusion.mine_ref, bf16[2,2,512,256]{3,2,1,0:T(8,128)(2,1)} %copy-done.28), custom_call_target="tpu_custom_call" | custom-call | tf_op jit(solution)/shard_map/finish/pallas_call | solution.py:218
  (95 shorter events, 7.3 us)
Async XLA Ops:
  1.7 10.7 %copy-start.2 = (bf16[1,2,512,512]{3,2,1,0:T(8,128)(2,1)}, bf16[1,2,512,512]{3,2,1,0:T(8,128)(2,1)S(1)}, u32[]{:S(2)}) copy-start(bf16[1,2,512,512]{3,2,1,0:T(8,128)(2,1)S(1)} %get-tuple-element.73.refs_4_) | copy-start | bytes 3145732
  1.7 6.1 %collective-permute-start = (bf16[1,2,512,512]{3,2,1,0:T(8,128)(2,1)S(1)}, bf16[1,2,512,512]{3,2,1,0:T(8,128)(2,1)S(1)}, u32[]{:S(2)}, u32[]{:S(2)}) collective-permute-start(bf16[1,2,512,512]{3,2,1,0:T(8,128)(2,1)S(1)} %get-tuple-element.74), channel_id=1, source_target_pairs={{0,1},{1,0},{2,3},{3,2},{4,5},{5,4},{6,7},{7,6},{8,9},{9,8},{10,11... | collective-permute-start | bytes 3145736 | tf_op jit(solution)/shard_map/ppermute | solution.py:235
  1.8 12.0 %collective-permute-start.2 = (bf16[1,2,512,512]{3,2,1,0:T(8,128)(2,1)S(1)}, bf16[1,2,512,512]{3,2,1,0:T(8,128)(2,1)}, u32[]{:S(2)}, u32[]{:S(2)}) collective-permute-start(bf16[1,2,512,512]{3,2,1,0:T(8,128)(2,1)S(1)} %get-tuple-element.73.refs_4_), channel_id=1, source_target_pairs={{4,8},{8,4},{5,9},{9,5},{6,10},{10,6},{7,11},{11,7},{20,24},{24,20... | collective-permute-start | bytes 3145736 | tf_op jit(solution)/shard_map/ppermute | solution.py:296
  3.4 27.8 %collective-permute-start.1 = (bf16[1,2,512,512]{3,2,1,0:T(8,128)(2,1)S(1)}, bf16[1,2,512,512]{3,2,1,0:T(8,128)(2,1)}, u32[]{:S(2)}, u32[]{:S(2)}) collective-permute-start(bf16[1,2,512,512]{3,2,1,0:T(8,128)(2,1)S(1)} %get-tuple-element.73.refs_4_), channel_id=1, source_target_pairs={{0,4},{4,0},{8,12},{12,8},{1,5},{5,1},{9,13},{13,9},{2,6},{6,2},{1... | collective-permute-start | bytes 3145736 | tf_op jit(solution)/shard_map/ppermute | solution.py:293
  7.8 1.0 copy-start.5
  12.3 18.9 %copy-start.6 = (bf16[1,2,512,512]{3,2,1,0:T(8,128)(2,1)S(1)}, bf16[1,2,512,512]{3,2,1,0:T(8,128)(2,1)}, u32[]{:S(2)}) copy-start(bf16[1,2,512,512]{3,2,1,0:T(8,128)(2,1)} %copy-done.5) | copy-start | bytes 3145732
  12.5 110.8 %copy-start = (bf16[2,2,256,1024]{3,2,1,0:T(8,128)(2,1)}, bf16[2,2,256,1024]{3,2,1,0:T(8,128)(2,1)S(1)}, u32[]{:S(2)}) copy-start(bf16[2,2,256,1024]{3,2,1,0:T(8,128)(2,1)S(1)} %dynamic-slice_bitcast_fusion.refs_0_.refs_1_) | copy-start | bytes 6291460
  12.6 46.8 %collective-permute-start.7 = (bf16[2,2,256,1024]{3,2,1,0:T(8,128)(2,1)S(1)}, bf16[2,2,256,1024]{3,2,1,0:T(8,128)(2,1)}, u32[]{:S(2)}, u32[]{:S(2)}) collective-permute-start(bf16[2,2,256,1024]{3,2,1,0:T(8,128)(2,1)S(1)} %dynamic-slice_bitcast_fusion.refs_0_.refs_1_), channel_id=1, source_target_pairs={{0,2},{2,0},{1,3},{3,1},{4,6},{6,4},{5,7},{7,5},{8,10},{10,8},{9,1... | collective-permute-start | bytes 6291464 | tf_op jit(solution)/shard_map/ppermute | solution.py:297
  31.2 24.0 %collective-permute-start.3 = (bf16[1,2,512,512]{3,2,1,0:T(8,128)(2,1)S(1)}, bf16[1,2,512,512]{3,2,1,0:T(8,128)(2,1)S(1)}, u32[]{:S(2)}, u32[]{:S(2)}) collective-permute-start(bf16[1,2,512,512]{3,2,1,0:T(8,128)(2,1)S(1)} %copy-done.6), channel_id=1, source_target_pairs={{0,4},{4,0},{8,12},{12,8},{1,5},{5,1},{9,13},{13,9},{2,6},{6,2},{1... | collective-permute-start | bytes 3145736 | tf_op jit(solution)/shard_map/ppermute | solution.py:293
  32.4 29.4 %collective-permute-start.4 = (bf16[1,2,512,512]{3,2,1,0:T(8,128)(2,1)S(1)}, bf16[1,2,512,512]{3,2,1,0:T(8,128)(2,1)S(1)}, u32[]{:S(2)}, u32[]{:S(2)}) collective-permute-start(bf16[1,2,512,512]{3,2,1,0:T(8,128)(2,1)S(1)} %copy-done.6), channel_id=1, source_target_pairs={{4,8},{8,4},{5,9},{9,5},{6,10},{10,6},{7,11},{11,7},{20,24},{24,20... | collective-permute-start | bytes 3145736 | tf_op jit(solution)/shard_map/ppermute | solution.py:296
  55.2 4.1 %copy-start.7 = (bf16[1,2,512,512]{3,2,1,0:T(8,128)(2,1)}, bf16[1,2,512,512]{3,2,1,0:T(8,128)(2,1)S(1)}, u32[]{:S(2)}) copy-start(bf16[1,2,512,512]{3,2,1,0:T(8,128)(2,1)S(1)} %collective-permute-done.3.refs_7_) | copy-start | bytes 3145732
  55.2 37.9 %collective-permute-start.6 = (bf16[2,2,256,1024]{3,2,1,0:T(8,128)(2,1)S(1)}, bf16[2,2,256,1024]{3,2,1,0:T(8,128)(2,1)}, u32[]{:S(2)}, u32[]{:S(2)}) collective-permute-start(bf16[2,2,256,1024]{3,2,1,0:T(8,128)(2,1)S(1)} %dynamic-slice_bitcast_fusion.refs_0_.refs_1_), channel_id=1, source_target_pairs={{0,1},{1,0},{2,3},{3,2},{4,5},{5,4},{6,7},{7,6},{8,9},{9,8},{10,11... | collective-permute-start | bytes 6291464 | tf_op jit(solution)/shard_map/ppermute | solution.py:235
  59.3 33.8 %collective-permute-start.8 = (bf16[2,2,256,1024]{3,2,1,0:T(8,128)(2,1)}, bf16[2,2,256,1024]{3,2,1,0:T(8,128)(2,1)}, u32[]{:S(2)}, u32[]{:S(2)}) collective-permute-start(bf16[2,2,256,1024]{3,2,1,0:T(8,128)(2,1)} %collective-permute-done.7.refs_2_), channel_id=1, source_target_pairs={{0,1},{1,0},{2,3},{3,2},{4,5},{5,4},{6,7},{7,6},{8,9},{9,8},{10,11... | collective-permute-start | bytes 6291464 | tf_op jit(solution)/shard_map/ppermute | solution.py:235
  62.8 24.8 %collective-permute-start.5 = (bf16[2,2,128,1024]{3,2,1,0:T(8,128)(2,1)}, bf16[2,2,128,1024]{3,2,1,0:T(8,128)(2,1)}, u32[]{:S(2)}, u32[]{:S(2)}) collective-permute-start(bf16[2,2,128,1024]{3,2,1,0:T(8,128)(2,1)} %slice.10), channel_id=1, source_target_pairs={{0,4},{12,8},{1,5},{13,9},{2,6},{14,10},{3,7},{15,11},{16,20},{28,... | collective-permute-start | bytes 3145736 | tf_op jit(solution)/shard_map/ppermute | solution.py:294
  65.7 23.3 %collective-permute-start.9 = (bf16[1,2,512,512]{3,2,1,0:T(8,128)(2,1)}, bf16[1,2,512,512]{3,2,1,0:T(8,128)(2,1)S(1)}, u32[]{:S(2)}, u32[]{:S(2)}) collective-permute-start(bf16[1,2,512,512]{3,2,1,0:T(8,128)(2,1)} %collective-permute-done.1.refs_6_), channel_id=1, source_target_pairs={{4,8},{8,4},{5,9},{9,5},{6,10},{10,6},{7,11},{11,7},{20,24},{24,20... | collective-permute-start | bytes 3145736 | tf_op jit(solution)/shard_map/ppermute | solution.py:296
  66.5 26.7 %collective-permute-start.10 = (bf16[1,2,512,512]{3,2,1,0:T(8,128)(2,1)}, bf16[1,2,512,512]{3,2,1,0:T(8,128)(2,1)}, u32[]{:S(2)}, u32[]{:S(2)}) collective-permute-start(bf16[1,2,512,512]{3,2,1,0:T(8,128)(2,1)} %collective-permute-done.2.refs_8_), channel_id=1, source_target_pairs={{4,0},{8,12},{5,1},{9,13},{6,2},{10,14},{7,3},{11,15},{20,16},{24,... | collective-permute-start | bytes 3145736 | tf_op jit(solution)/shard_map/ppermute | solution.py:295
  67.8 26.7 %copy-start.8 = (bf16[1,2,512,512]{3,2,1,0:T(8,128)(2,1)S(1)}, bf16[1,2,512,512]{3,2,1,0:T(8,128)(2,1)}, u32[]{:S(2)}) copy-start(bf16[1,2,512,512]{3,2,1,0:T(8,128)(2,1)} %copy-done.7) | copy-start | bytes 3145732
  67.8 27.5 %copy-start.10 = (bf16[1,2,512,512]{3,2,1,0:T(8,128)(2,1)S(1)}, bf16[1,2,512,512]{3,2,1,0:T(8,128)(2,1)}, u32[]{:S(2)}) copy-start(bf16[1,2,512,512]{3,2,1,0:T(8,128)(2,1)} %copy-done.9) | copy-start | bytes 3145732
  87.8 34.3 %copy-start.13 = (bf16[2,2,128,1024]{3,2,1,0:T(8,128)(2,1)}, bf16[2,2,128,1024]{3,2,1,0:T(8,128)(2,1)S(1)}, u32[]{:S(2)}) copy-start(bf16[2,2,128,1024]{3,2,1,0:T(8,128)(2,1)S(1)} %get-tuple-element.64) | copy-start | bytes 3145732
  87.8 35.6 %copy-start.15 = (bf16[2,2,128,1024]{3,2,1,0:T(8,128)(2,1)}, bf16[2,2,128,1024]{3,2,1,0:T(8,128)(2,1)S(1)}, u32[]{:S(2)}) copy-start(bf16[2,2,128,1024]{3,2,1,0:T(8,128)(2,1)S(1)} %get-tuple-element.46) | copy-start | bytes 3145732
  87.8 24.1 %collective-permute-start.13 = (bf16[2,2,128,1024]{3,2,1,0:T(8,128)(2,1)S(1)}, bf16[2,2,128,1024]{3,2,1,0:T(8,128)(2,1)S(1)}, u32[]{:S(2)}, u32[]{:S(2)}) collective-permute-start(bf16[2,2,128,1024]{3,2,1,0:T(8,128)(2,1)S(1)} %get-tuple-element.46), channel_id=1, source_target_pairs={{0,2},{2,0},{1,3},{3,1},{4,6},{6,4},{5,7},{7,5},{8,10},{10,8},{9,1... | collective-permute-start | bytes 3145736 | tf_op jit(solution)/shard_map/ppermute | solution.py:297
  89.1 33.0 %copy-start.3 = (bf16[1,2,512,512]{3,2,1,0:T(8,128)(2,1)}, bf16[1,2,512,512]{3,2,1,0:T(8,128)(2,1)S(1)}, u32[]{:S(2)}) copy-start(bf16[1,2,512,512]{3,2,1,0:T(8,128)(2,1)S(1)} %collective-permute-done.9.refs_10_.refs_12_) | copy-start | bytes 3145732
  93.2 22.7 %collective-permute-start.12 = (bf16[2,2,128,1024]{3,2,1,0:T(8,128)(2,1)S(1)}, bf16[2,2,128,1024]{3,2,1,0:T(8,128)(2,1)S(1)}, u32[]{:S(2)}, u32[]{:S(2)}) collective-permute-start(bf16[2,2,128,1024]{3,2,1,0:T(8,128)(2,1)S(1)} %get-tuple-element.64), channel_id=1, source_target_pairs={{0,4},{12,8},{1,5},{13,9},{2,6},{14,10},{3,7},{15,11},{16,20},{28,... | collective-permute-start | bytes 3145736 | tf_op jit(solution)/shard_map/ppermute | solution.py:294
  94.5 23.8 %collective-permute-start.11 = (bf16[1,2,512,512]{3,2,1,0:T(8,128)(2,1)S(1)}, bf16[1,2,512,512]{3,2,1,0:T(8,128)(2,1)S(1)}, u32[]{:S(2)}, u32[]{:S(2)}) collective-permute-start(bf16[1,2,512,512]{3,2,1,0:T(8,128)(2,1)S(1)} %copy-done.8), channel_id=1, source_target_pairs={{4,8},{8,4},{5,9},{9,5},{6,10},{10,6},{7,11},{11,7},{20,24},{24,20... | collective-permute-start | bytes 3145736 | tf_op jit(solution)/shard_map/ppermute | solution.py:296
  95.3 25.3 %collective-permute-start.17 = (bf16[1,2,512,512]{3,2,1,0:T(8,128)(2,1)S(1)}, bf16[1,2,512,512]{3,2,1,0:T(8,128)(2,1)}, u32[]{:S(2)}, u32[]{:S(2)}) collective-permute-start(bf16[1,2,512,512]{3,2,1,0:T(8,128)(2,1)S(1)} %copy-done.10), channel_id=1, source_target_pairs={{4,0},{8,12},{5,1},{9,13},{6,2},{10,14},{7,3},{11,15},{20,16},{24,... | collective-permute-start | bytes 3145736 | tf_op jit(solution)/shard_map/ppermute | solution.py:295
  111.9 6.4 %copy-start.25 = (bf16[2,2,128,1024]{3,2,1,0:T(8,128)(2,1)}, bf16[2,2,128,1024]{3,2,1,0:T(8,128)(2,1)S(1)}, u32[]{:S(2)}) copy-start(bf16[2,2,128,1024]{3,2,1,0:T(8,128)(2,1)S(1)} %collective-permute-done.13) | copy-start | bytes 3145732
  115.8 2.5 copy-start.11
  117.0 9.1 %copy-start.29 = (f32[2,2,2,2]{3,2,1,0:T(2,128)S(1)}, f32[2,2,2,2]{3,2,1,0:T(2,128)}, u32[]{:S(2)}) copy-start(f32[2,2,2,2]{3,2,1,0:T(2,128)} %param.5) | copy-start | bytes 196
  117.0 44.2 %collective-permute-start.15 = (bf16[2,2,128,1024]{3,2,1,0:T(8,128)(2,1)}, bf16[2,2,128,1024]{3,2,1,0:T(8,128)(2,1)}, u32[]{:S(2)}, u32[]{:S(2)}) collective-permute-start(bf16[2,2,128,1024]{3,2,1,0:T(8,128)(2,1)} %broadcast_select_fusion), channel_id=1, source_target_pairs={{0,2},{2,0},{1,3},{3,1},{4,6},{6,4},{5,7},{7,5},{8,10},{10,8},{9,1... | collective-permute-start | bytes 3145736 | tf_op jit(solution)/shard_map/ppermute | solution.py:297
  118.3 5.1 %copy-start.4 = (bf16[1,2,512,512]{3,2,1,0:T(8,128)(2,1)}, bf16[1,2,512,512]{3,2,1,0:T(8,128)(2,1)S(1)}, u32[]{:S(2)}) copy-start(bf16[1,2,512,512]{3,2,1,0:T(8,128)(2,1)S(1)} %collective-permute-done.11.refs_11_.refs_14_) | copy-start | bytes 3145732
  122.1 47.1 %collective-permute-start.18 = (bf16[2,2,512,512]{3,2,1,0:T(8,128)(2,1)}, bf16[2,2,512,512]{3,2,1,0:T(8,128)(2,1)}, u32[]{:S(2)}, u32[]{:S(2)}) collective-permute-start(bf16[2,2,512,512]{3,2,1,0:T(8,128)(2,1)} %pad_maximum_fusion), channel_id=1, source_target_pairs={{4,0},{8,12},{5,1},{9,13},{6,2},{10,14},{7,3},{11,15},{20,16},{24,... | collective-permute-start | bytes 6291464 | tf_op jit(solution)/shard_map/ppermute | solution.py:295
  123.4 45.7 %collective-permute-start.20 = (bf16[2,2,256,1024]{3,2,1,0:T(8,128)(2,1)S(1)}, bf16[2,2,256,1024]{3,2,1,0:T(8,128)(2,1)}, u32[]{:S(2)}, u32[]{:S(2)}) collective-permute-start(bf16[2,2,256,1024]{3,2,1,0:T(8,128)(2,1)S(1)} %dynamic-slice_bitcast_fusion.refs_0_.refs_1_), channel_id=1, source_target_pairs={{4,8},{8,4},{5,9},{9,5},{6,10},{10,6},{7,11},{11,7},{20,24},{24,20... | collective-permute-start | bytes 6291464 | tf_op jit(solution)/shard_map/ppermute | solution.py:296
  126.7 27.7 %copy-start.16 = (bf16[2,2,128,1024]{3,2,1,0:T(8,128)(2,1)S(1)}, bf16[2,2,128,1024]{3,2,1,0:T(8,128)(2,1)}, u32[]{:S(2)}) copy-start(bf16[2,2,128,1024]{3,2,1,0:T(8,128)(2,1)} %copy-done.15) | copy-start | bytes 3145732
  154.4 5.7 %copy-start.26 = (bf16[2,2,128,1024]{3,2,1,0:T(8,128)(2,1)S(1)}, bf16[2,2,128,1024]{3,2,1,0:T(8,128)(2,1)}, u32[]{:S(2)}) copy-start(bf16[2,2,128,1024]{3,2,1,0:T(8,128)(2,1)} %copy-done.25) | copy-start | bytes 3145732
  157.7 17.5 %collective-permute-start.14 = (bf16[2,2,256,1024]{3,2,1,0:T(8,128)(2,1)}, bf16[2,2,256,1024]{3,2,1,0:T(8,128)(2,1)}, u32[]{:S(2)}, u32[]{:S(2)}) collective-permute-start(bf16[2,2,256,1024]{3,2,1,0:T(8,128)(2,1)} %constant_dynamic-update-slice_fusion.refs_0_), channel_id=1, source_target_pairs={{0,1},{1,0},{2,3},{3,2},{4,5},{5,4},{6,7},{7,6},{8,9},{9,8},{10,11... | collective-permute-start | bytes 6291464 | tf_op jit(solution)/shard_map/ppermute | solution.py:235
  163.4 11.8 %collective-permute-start.16 = (bf16[2,2,256,1024]{3,2,1,0:T(8,128)(2,1)}, bf16[2,2,256,1024]{3,2,1,0:T(8,128)(2,1)}, u32[]{:S(2)}, u32[]{:S(2)}) collective-permute-start(bf16[2,2,256,1024]{3,2,1,0:T(8,128)(2,1)} %constant_dynamic-update-slice_fusion.2.refs_2_), channel_id=1, source_target_pairs={{0,1},{1,0},{2,3},{3,2},{4,5},{5,4},{6,7},{7,6},{8,9},{9,8},{10,11... | collective-permute-start | bytes 6291464 | tf_op jit(solution)/shard_map/ppermute | solution.py:235
  169.1 33.5 %collective-permute-start.21 = (bf16[2,2,128,1024]{3,2,1,0:T(8,128)(2,1)}, bf16[2,2,128,1024]{3,2,1,0:T(8,128)(2,1)S(1)}, u32[]{:S(2)}, u32[]{:S(2)}) collective-permute-start(bf16[2,2,128,1024]{3,2,1,0:T(8,128)(2,1)} %collective-permute-done.5.refs_0_), channel_id=1, source_target_pairs={{4,8},{8,4},{5,9},{9,5},{6,10},{10,6},{7,11},{11,7},{20,24},{24,20... | collective-permute-start | bytes 3145736 | tf_op jit(solution)/shard_map/ppermute | solution.py:296
  169.9 32.8 %collective-permute-start.22 = (bf16[2,2,128,1024]{3,2,1,0:T(8,128)(2,1)}, bf16[2,2,128,1024]{3,2,1,0:T(8,128)(2,1)}, u32[]{:S(2)}, u32[]{:S(2)}) collective-permute-start(bf16[2,2,128,1024]{3,2,1,0:T(8,128)(2,1)} %slice.10), channel_id=1, source_target_pairs={{4,0},{8,12},{5,1},{9,13},{6,2},{10,14},{7,3},{11,15},{20,16},{24,... | collective-permute-start | bytes 3145736 | tf_op jit(solution)/shard_map/ppermute | solution.py:295
  172.0 31.6 %copy-start.12 = (bf16[2,2,128,1024]{3,2,1,0:T(8,128)(2,1)S(1)}, bf16[2,2,128,1024]{3,2,1,0:T(8,128)(2,1)}, u32[]{:S(2)}) copy-start(bf16[2,2,128,1024]{3,2,1,0:T(8,128)(2,1)} %copy-done.11) | copy-start | bytes 3145732
  172.0 33.2 %copy-start.14 = (bf16[2,2,128,1024]{3,2,1,0:T(8,128)(2,1)S(1)}, bf16[2,2,128,1024]{3,2,1,0:T(8,128)(2,1)}, u32[]{:S(2)}) copy-start(bf16[2,2,128,1024]{3,2,1,0:T(8,128)(2,1)} %copy-done.13) | copy-start | bytes 3145732
  172.1 34.5 %collective-permute-start.19 = (bf16[2,2,2,512,512]{4,3,2,1,0:T(8,128)(2,1)}, bf16[2,2,2,512,512]{4,3,2,1,0:T(8,128)(2,1)S(1)}, u32[]{:S(2)}, u32[]{:S(2)}) collective-permute-start(bf16[2,2,2,512,512]{4,3,2,1,0:T(8,128)(2,1)} %first_product.2.own_ref), channel_id=1, source_target_pairs={{0,1},{1,0},{2,3},{3,2},{4,5},{5,4},{6,7},{7,6},{8,9},{9,8},{10,11... | collective-permute-start | bytes 12582920 | tf_op jit(solution)/shard_map/ppermute | solution.py:235
  202.7 21.5 %copy-start.17 = (bf16[2,2,128,1024]{3,2,1,0:T(8,128)(2,1)}, bf16[2,2,128,1024]{3,2,1,0:T(8,128)(2,1)S(1)}, u32[]{:S(2)}) copy-start(bf16[2,2,128,1024]{3,2,1,0:T(8,128)(2,1)S(1)} %collective-permute-done.21.refs_0_.refs_2_) | copy-start | bytes 3145732
  202.7 22.3 %collective-permute-start.23 = (bf16[2,2,2,512,512]{4,3,2,1,0:T(8,128)(2,1)}, bf16[2,2,2,512,512]{4,3,2,1,0:T(8,128)(2,1)}, u32[]{:S(2)}, u32[]{:S(2)}) collective-permute-start(bf16[2,2,2,512,512]{4,3,2,1,0:T(8,128)(2,1)} %first_product.3.own_ref), channel_id=1, source_target_pairs={{0,1},{1,0},{2,3},{3,2},{4,5},{5,4},{6,7},{7,6},{8,9},{9,8},{10,11... | collective-permute-start | bytes 12582920 | tf_op jit(solution)/shard_map/ppermute | solution.py:235
  203.6 36.0 %collective-permute-start.28 = (bf16[2,2,128,1024]{3,2,1,0:T(8,128)(2,1)S(1)}, bf16[2,2,128,1024]{3,2,1,0:T(8,128)(2,1)}, u32[]{:S(2)}, u32[]{:S(2)}) collective-permute-start(bf16[2,2,128,1024]{3,2,1,0:T(8,128)(2,1)S(1)} %copy-done.12), channel_id=1, source_target_pairs={{4,8},{8,4},{5,9},{9,5},{6,10},{10,6},{7,11},{11,7},{20,24},{24,20... | collective-permute-start | bytes 3145736 | tf_op jit(solution)/shard_map/ppermute | solution.py:296
  205.3 34.3 %collective-permute-start.29 = (bf16[2,2,128,1024]{3,2,1,0:T(8,128)(2,1)S(1)}, bf16[2,2,128,1024]{3,2,1,0:T(8,128)(2,1)}, u32[]{:S(2)}, u32[]{:S(2)}) collective-permute-start(bf16[2,2,128,1024]{3,2,1,0:T(8,128)(2,1)S(1)} %copy-done.14), channel_id=1, source_target_pairs={{4,0},{8,12},{5,1},{9,13},{6,2},{10,14},{7,3},{11,15},{20,16},{24,... | collective-permute-start | bytes 3145736 | tf_op jit(solution)/shard_map/ppermute | solution.py:295
  206.6 2.0 copy-start.1
  224.1 11.4 %copy-start.27 = (bf16[2,2,512,256]{3,2,1,0:T(8,128)(2,1)S(1)}, bf16[2,2,512,256]{3,2,1,0:T(8,128)(2,1)}, u32[]{:S(2)}) copy-start(bf16[2,2,512,256]{3,2,1,0:T(8,128)(2,1)} %get-tuple-element.56) | copy-start | bytes 3145732
  224.1 27.6 %collective-permute-start.25 = (bf16[2,2,512,256]{3,2,1,0:T(8,128)(2,1)}, bf16[2,2,512,256]{3,2,1,0:T(8,128)(2,1)S(1)}, u32[]{:S(2)}, u32[]{:S(2)}) collective-permute-start(bf16[2,2,512,256]{3,2,1,0:T(8,128)(2,1)} %get-tuple-element.61), channel_id=1, source_target_pairs={{4,6},{5,7},{10,8},{11,9},{20,22},{21,23},{26,24},{27,25}} | collective-permute-start | bytes 3145736 | tf_op jit(solution)/shard_map/ppermute | solution.py:304
  235.5 2.7 copy-start.19
  237.0 26.4 %collective-permute-start.24 = (bf16[2,2,512,256]{3,2,1,0:T(8,128)(2,1)S(1)}, bf16[2,2,512,256]{3,2,1,0:T(8,128)(2,1)S(1)}, u32[]{:S(2)}, u32[]{:S(2)}) collective-permute-start(bf16[2,2,512,256]{3,2,1,0:T(8,128)(2,1)S(1)} %broadcast_select_fusion.3), channel_id=1, source_target_pairs={{2,0},{3,1},{6,4},{7,5},{8,10},{9,11},{12,14},{13,15},{18,16},{19,... | collective-permute-start | bytes 3145736 | tf_op jit(solution)/shard_map/ppermute | solution.py:304
  238.3 35.0 %collective-permute-start.26 = (bf16[2,2,512,256]{3,2,1,0:T(8,128)(2,1)S(1)}, bf16[2,2,512,256]{3,2,1,0:T(8,128)(2,1)}, u32[]{:S(2)}, u32[]{:S(2)}) collective-permute-start(bf16[2,2,512,256]{3,2,1,0:T(8,128)(2,1)S(1)} %copy-done.19), channel_id=1, source_target_pairs={{4,0},{8,12},{5,1},{9,13},{6,2},{10,14},{7,3},{11,15},{20,16},{24,... | collective-permute-start | bytes 3145736 | tf_op jit(solution)/shard_map/ppermute | solution.py:295
  250.1 43.6 %copy-start.18 = (bf16[2,2,512,256]{3,2,1,0:T(8,128)(2,1)S(1)}, bf16[2,2,512,256]{3,2,1,0:T(8,128)(2,1)}, u32[]{:S(2)}) copy-start(bf16[2,2,512,256]{3,2,1,0:T(8,128)(2,1)} %second_product.6) | copy-start | bytes 3145732
  250.1 46.6 %collective-permute-start.32 = (bf16[2,2,512,256]{3,2,1,0:T(8,128)(2,1)}, bf16[2,2,512,256]{3,2,1,0:T(8,128)(2,1)}, u32[]{:S(2)}, u32[]{:S(2)}) collective-permute-start(bf16[2,2,512,256]{3,2,1,0:T(8,128)(2,1)} %second_product.6), channel_id=1, source_target_pairs={{4,0},{8,12},{5,1},{9,13},{6,2},{10,14},{7,3},{11,15},{20,16},{24,... | collective-permute-start | bytes 3145736 | tf_op jit(solution)/shard_map/ppermute | solution.py:295
  251.8 41.9 %copy-start.21 = (bf16[2,2,512,256]{3,2,1,0:T(8,128)(2,1)}, bf16[2,2,512,256]{3,2,1,0:T(8,128)(2,1)S(1)}, u32[]{:S(2)}) copy-start(bf16[2,2,512,256]{3,2,1,0:T(8,128)(2,1)S(1)} %collective-permute-done.25) | copy-start | bytes 3145732
  263.4 30.3 %copy-start.23 = (bf16[2,2,512,256]{3,2,1,0:T(8,128)(2,1)}, bf16[2,2,512,256]{3,2,1,0:T(8,128)(2,1)S(1)}, u32[]{:S(2)}) copy-start(bf16[2,2,512,256]{3,2,1,0:T(8,128)(2,1)S(1)} %collective-permute-done.24) | copy-start | bytes 3145732
  273.3 23.4 %collective-permute-start.27 = (bf16[2,2,512,256]{3,2,1,0:T(8,128)(2,1)}, bf16[2,2,512,256]{3,2,1,0:T(8,128)(2,1)}, u32[]{:S(2)}, u32[]{:S(2)}) collective-permute-start(bf16[2,2,512,256]{3,2,1,0:T(8,128)(2,1)} %collective-permute-done.26), channel_id=1, source_target_pairs={{0,2},{1,3},{14,12},{15,13},{16,18},{17,19},{30,28},{31,29}} | collective-permute-start | bytes 3145736 | tf_op jit(solution)/shard_map/ppermute | solution.py:304
  293.8 23.2 %collective-permute-start.30 = (bf16[2,2,512,256]{3,2,1,0:T(8,128)(2,1)S(1)}, bf16[2,2,512,256]{3,2,1,0:T(8,128)(2,1)}, u32[]{:S(2)}, u32[]{:S(2)}) collective-permute-start(bf16[2,2,512,256]{3,2,1,0:T(8,128)(2,1)S(1)} %broadcast_select_fusion.2), channel_id=1, source_target_pairs={{2,0},{3,1},{6,4},{7,5},{8,10},{9,11},{12,14},{13,15},{18,16},{19,... | collective-permute-start | bytes 3145736 | tf_op jit(solution)/shard_map/ppermute | solution.py:304
  295.1 21.9 %collective-permute-start.31 = (bf16[2,2,512,256]{3,2,1,0:T(8,128)(2,1)}, bf16[2,2,512,256]{3,2,1,0:T(8,128)(2,1)}, u32[]{:S(2)}, u32[]{:S(2)}) collective-permute-start(bf16[2,2,512,256]{3,2,1,0:T(8,128)(2,1)} %get-tuple-element.67), channel_id=1, source_target_pairs={{4,6},{5,7},{10,8},{11,9},{20,22},{21,23},{26,24},{27,25}} | collective-permute-start | bytes 3145736 | tf_op jit(solution)/shard_map/ppermute | solution.py:304
  296.8 25.4 %collective-permute-start.33 = (bf16[2,2,512,256]{3,2,1,0:T(8,128)(2,1)}, bf16[2,2,512,256]{3,2,1,0:T(8,128)(2,1)}, u32[]{:S(2)}, u32[]{:S(2)}) collective-permute-start(bf16[2,2,512,256]{3,2,1,0:T(8,128)(2,1)} %collective-permute-done.32), channel_id=1, source_target_pairs={{0,2},{1,3},{14,12},{15,13},{16,18},{17,19},{30,28},{31,29}} | collective-permute-start | bytes 3145736 | tf_op jit(solution)/shard_map/ppermute | solution.py:304
  302.8 17.0 %copy-start.20 = (bf16[2,2,512,256]{3,2,1,0:T(8,128)(2,1)S(1)}, bf16[2,2,512,256]{3,2,1,0:T(8,128)(2,1)}, u32[]{:S(2)}) copy-start(bf16[2,2,512,256]{3,2,1,0:T(8,128)(2,1)} %get-tuple-element.61) | copy-start | bytes 3145732
  302.8 17.0 %copy-start.22 = (bf16[2,2,512,256]{3,2,1,0:T(8,128)(2,1)S(1)}, bf16[2,2,512,256]{3,2,1,0:T(8,128)(2,1)}, u32[]{:S(2)}) copy-start(bf16[2,2,512,256]{3,2,1,0:T(8,128)(2,1)} %copy-done.21) | copy-start | bytes 3145732
  302.8 17.0 %copy-start.24 = (bf16[2,2,512,256]{3,2,1,0:T(8,128)(2,1)S(1)}, bf16[2,2,512,256]{3,2,1,0:T(8,128)(2,1)}, u32[]{:S(2)}) copy-start(bf16[2,2,512,256]{3,2,1,0:T(8,128)(2,1)} %copy-done.23) | copy-start | bytes 3145732
  323.7 7.3 %collective-permute-start.34 = (bf16[2,2,512,256]{3,2,1,0:T(8,128)(2,1)S(1)}, bf16[2,2,512,256]{3,2,1,0:T(8,128)(2,1)S(1)}, u32[]{:S(2)}, u32[]{:S(2)}) collective-permute-start(bf16[2,2,512,256]{3,2,1,0:T(8,128)(2,1)S(1)} %select_convert_fusion), channel_id=1, source_target_pairs={{0,1},{1,0},{2,3},{3,2},{4,5},{5,4},{6,7},{7,6},{8,9},{9,8},{10,11... | collective-permute-start | bytes 3145736 | tf_op jit(solution)/shard_map/ppermute | solution.py:235
  331.1 1.0 copy-start.28
  (1 other events, 1.0 us)

commit v11 on v10

--- a/solution.py
+++ b/solution.py
@@ -26,53 +26,60 @@
     return lax.dot_general(left, right, (((1,), (1,)), ((), ())), preferred_element_type=F32)
 
 
-def first_kernel(sources, pick_ref, mpo_ref, *refs):
+def first_kernel(site_sources, sources, pick_ref, mpo_ref, *refs):
     q_ref, site_ref, env_ref, g_ref, site_sems, env_sems = refs[-6:]
-    site_refs, env_refs = refs[:4], refs[4:-6]
+    source_refs = refs[:-6]
     mpo_count, phys, _, rows, cols = q_ref.shape
     w_local, _, depth, _ = env_ref.shape[1:]
     per_col = site_ref.shape[-1] // depth
     tile, col_tile = pl.program_id(0), pl.program_id(1)
 
-    def site_copy(which, other):
-        there = 1 - pick_ref[1] if other else pick_ref[1]
+    def start_site(which, at_end):
+        for col in range(site_ref.shape[1]):
+            first = 0
+            for source in site_sources[-1 if at_end else 0]:
+                extent = source_refs[source].shape[3]
+                pltpu.make_async_copy(
+                    source_refs[source].at[col * 2 + which],
+                    site_ref.at[which, col, :, :, pl.ds(first, extent)],
+                    site_sems.at[which, col],
+                ).start()
+                first += extent
+
+    def wait_site(which):
+        for col in range(site_ref.shape[1]):
+            there = site_ref.at[which, col]
+            pltpu.make_async_copy(there, there, site_sems.at[which, col]).wait()
+
+    def env_copy(number, at_end):
+        source, first = sources[number][-1 if at_end else 0]
         return pltpu.make_async_copy(
-            site_refs[other * 2 + which], site_ref.at[which, there], site_sems.at[which, other]
+            source_refs[source].at[pl.ds(first, w_local)], env_ref.at[number], env_sems.at[number]
         )
 
-    def env_copy(number, at_end):
-        source, first = sources[number][1 if at_end and len(sources[number]) > 1 else 0]
-        return pltpu.make_async_copy(
-            env_refs[source].at[pl.ds(first, w_local)], env_ref.at[number], env_sems.at[number]
-        )
-
-    def start_envs(at_end):
+    def start(at_end):
+        start_site(0, at_end)
         for number in range(len(sources)):
             env_copy(number, at_end).start()
+        start_site(1, at_end)
 
     @pl.when((tile == 0) & (col_tile == 0))
     def _():
-        for other in range(2):
-            site_copy(0, other).start()
-        pl.when(pick_ref[2] == 0)(functools.partial(start_envs, False))
-        pl.when(pick_ref[2] != 0)(functools.partial(start_envs, True))
-        for other in range(2):
-            site_copy(1, other).start()
-        for other in range(2):
-            site_copy(0, other).wait()
+        pl.when(pick_ref[1] == 0)(functools.partial(start, False))
+        pl.when(pick_ref[1] != 0)(functools.partial(start, True))
+        wait_site(0)
         for number in range(len(sources)):
             env_copy(number, False).wait()
 
     @pl.when((tile == 1) & (col_tile == 0))
     def _():
-        for other in range(2):
-            site_copy(1, other).wait()
+        wait_site(1)
 
     columns = pl.ds(pl.multiple_of(col_tile * cols, cols), cols)
     for w in range(mpo_count):
         with_real, with_imag = None, None
         for number in range(len(sources) // 2):
-            block = pick_ref[3 + number]
+            block = pick_ref[2 + number]
             piece = pl.ds(pl.multiple_of((block % per_col) * depth, depth), depth)
             left = site_ref[tile, block // per_col, :, :, :, piece].reshape(phys * 2 * rows, depth)
             env = number * 2 + w // w_local
@@ -96,35 +103,38 @@
                 q_ref[v, t, part] = total.astype(BF16)
 
 
-def first_product(pick, mpo, site, envs, col_tile):
-    phys, _, half, wide = site[0].shape
-    arrays, sources = [], []
-    for choices in envs:
-        sources.append([])
-        for array, start in choices:
-            known = [number for number, one in enumerate(arrays) if one is array]
-            if not known:
-                arrays.append(array)
-            sources[-1].append((known[0] if known else len(arrays) - 1, start))
-    _, _, depth, cols = arrays[0].shape
+def first_product(pick, mpo, sites, envs, col_tile):
+    arrays = []
+
+    def number_of(array):
+        for number, one in enumerate(arrays):
+            if one is array:
+                return number
+        arrays.append(array)
+        return len(arrays) - 1
+
+    site_sources = [[number_of(one) for one in choice] for choice in sites]
+    sources = [[(number_of(one), start) for one, start in choices] for choices in envs]
+    pieces, phys, _, _, wide = sites[0][0].shape
+    half = sum(one.shape[3] for one in sites[0])
+    _, _, depth, cols = envs[0][0][0].shape
     mpo_count = mpo.shape[1]
     w_local = mpo_count // 2
-    anywhere = pl.BlockSpec(memory_space=pl.ANY)
     return pl.pallas_call(
-        functools.partial(first_kernel, sources),
+        functools.partial(first_kernel, site_sources, sources),
         grid_spec=pltpu.PrefetchScalarGridSpec(
             num_scalar_prefetch=1,
             grid=(2, cols // col_tile),
-            in_specs=[pl.BlockSpec(memory_space=pltpu.SMEM)] + [anywhere] * (4 + len(arrays)),
+            in_specs=[pl.BlockSpec(memory_space=pltpu.SMEM)]
+            + [pl.BlockSpec(memory_space=pl.ANY)] * len(arrays),
             out_specs=pl.BlockSpec(
-                (mpo_count, phys, 2, half, col_tile),
-                lambda i, j, pick: (0, 0, 0, jnp.where(i == 0, pick[0], 1 - pick[0]), j),
+                (mpo_count, phys, 2, half, col_tile), lambda i, j, pick: (0, 0, 0, i, j)
             ),
             scratch_shapes=[
-                pltpu.VMEM((2, 2, phys, 2, half, wide), BF16),
+                pltpu.VMEM((2, pieces // 2, phys, 2, half, wide), BF16),
                 pltpu.VMEM((len(sources), w_local, 2, depth, cols), BF16),
                 pltpu.VMEM((mpo_count, 2, phys * half, col_tile), F32),
-                pltpu.SemaphoreType.DMA((2, 2)),
+                pltpu.SemaphoreType.DMA((2, pieces // 2)),
                 pltpu.SemaphoreType.DMA((len(sources),)),
             ],
         ),
@@ -132,7 +142,7 @@
         compiler_params=params(2),
         cost_estimate=LIGHT,
         name="first_product",
-    )(pick, mpo, *site, *arrays)
+    )(pick, mpo, *arrays)
 
 
 def second_kernel(groups, pick_ref, own_ref, sib_ref, *refs):
@@ -160,8 +170,8 @@
 
     @pl.when(pl.program_id(0) == 0)
     def _():
-        pl.when(pick_ref[2] == 0)(functools.partial(start, False))
-        pl.when(pick_ref[2] != 0)(functools.partial(start, True))
+        pl.when(pick_ref[1] == 0)(functools.partial(start, False))
+        pl.when(pick_ref[1] != 0)(functools.partial(start, True))
         for copy in copies(False):
             copy.wait()
 
@@ -309,74 +319,64 @@
     env_own, env_sib, mpo_mine = split_inputs(environment, mpo)
     w_local = environment.shape[0]
     env = [env_own, env_sib]
-    side_env, over_env = [both(env_own)], [across(env_own)]
-    second_part = after(env_sib, side_env[0], over_env[0])
-    side_env.append(both(second_part))
-    over_env.append(across(second_part))
-
     planar = jnp.transpose(after(site_tensor, env_sib), (0, 2, 1, 3))
     half = planar.shape[2] // 2
     mine = lax.dynamic_slice_in_dim(planar, depth * half, half, 2)
     parts = [mine[:, :, : half // 2], mine[:, :, half // 2 :]]
-    turned = turn(mine)
-    site_here = [mine, swap(after(mine, *side_env)), turned, swap(after(turned, *side_env))]
+    gather = lambda value: lax.all_gather(value, ("col", "depth"), axis=0)
+    site_here = gather(mine)
+
+    side_env, over_env = [both(one) for one in env], [across(one) for one in env]
     far_env, over_side_env, side_parts = [], [], []
-    gates = (*side_env, *over_env)
     for m in range(2):
-        far_env.append(to_end(after(over_env[m], *gates)))
-        over_side_env.append(across(after(side_env[m], *gates)))
+        far_env.append(to_end(after(over_env[m], side_env[m])))
+        over_side_env.append(across(after(side_env[m], over_env[m])))
+        gates = (side_env[1], over_env[1]) if m == 0 else (side_parts[0], far_env[0], over_side_env[0])
         side_parts.append(to_host(after(parts[m], *gates)))
-        gates = (far_env[m], over_side_env[m], side_parts[m], *site_here[1::2])
-    there_parts = [hosts_or(side_parts[0], parts[0])]
-    turned_parts = [turn(there_parts[0])]
-    there_parts.append(hosts_or(side_parts[1], after(parts[1], turned_parts[0])))
-    turned_parts.append(turn(there_parts[1]))
-    gates = (*gates, turned_parts[0])
-    over_site = across(after(mine, *gates))
-    far_side_env = to_end(after(jnp.concatenate(over_side_env, axis=0), *gates))
-    gates = (over_site, far_side_env)
+    over_site = [across(after(parts[m], over_side_env[m])) for m in range(2)]
+    far_side_env = [to_end(after(over_side_env[m], far_env[m])) for m in range(2)]
+    site_there = [gather(after(side_parts[m], far_env[m], over_side_env[m])) for m in range(2)]
+
+    side = row ^ 1
+    at_host, at_end = (row, side, 3 - row, 3 - side), (row, side, 3 - side, 3 - row)
+    pick_here = jnp.stack([depth, 0 * row, *at_host]).astype(jnp.int32)
+    pick_there = jnp.stack(
+        [depth, hosts_or(0, 1), *[hosts_or(*pair) for pair in zip(at_host, at_end)]]
+    ).astype(jnp.int32)
+    pick = pick_there[:2]
+
+    def second(q, site_groups, *earlier):
+        outs = second_product(after(pick, *earlier), q[0], q[1], site_groups)
+        return outs if len(outs) > 1 else outs[0]
+
+    q_here = first_product(
+        pick_here,
+        mpo_mine,
+        [[site_here]],
+        [[(one, 0)] for one in env + side_env + over_env + over_side_env],
+        half,
+    )
     over_side_parts, host_parts = [], []
+    gates = (*over_site, *far_side_env, q_here)
     for m in range(2):
         over_side_parts.append(across(after(side_parts[m], *gates)))
         host_parts.append(to_end(after(parts[m], *gates)))
-        gates = (over_side_parts[m], host_parts[m])
-
-    side = row ^ 1
-    at_host, at_end = (row, side, 3 - row, 3 - side), (row, side, 3 - side, 3 - row)
-    pick_here = jnp.stack([depth, col, 0 * row, *at_host]).astype(jnp.int32)
-    pick_there = jnp.stack(
-        [depth, col, hosts_or(0, 1), *[hosts_or(*pair) for pair in zip(at_host, at_end)]]
-    ).astype(jnp.int32)
-    pick = pick_there[:3]
-
-    def second(q, site_groups, *earlier):
-        outs = second_product(after(pick, *earlier), q[0], q[1], site_groups)
-        return outs if len(outs) > 1 else outs[0]
-
-    whole = lambda arrays: [[(one, 0)] for one in arrays]
-    q_here = first_product(
-        pick_here, mpo_mine, site_here, whole(env + side_env + over_env + over_side_env), half
-    )
-    there, turned = (
-        jnp.concatenate([after(part, q_here) for part in pair], axis=2)
-        for pair in (there_parts, turned_parts)
-    )
+        gates = (over_side_parts[0], host_parts[0])
     q_there = first_product(
-        pick_there,
+        after(pick_there, q_here),
         mpo_mine,
-        [there, swap(there), turned, swap(turned)],
-        whole(env + side_env)
-        + [[(at_host, 0), (at_end, 0)] for at_host, at_end in zip(over_env, far_env)]
-        + [[(over_side_env[m], 0), (far_side_env, m * w_local)] for m in range(2)],
+        [site_there, [site_here]],
+        [[(one, 0)] for one in env + side_env]
+        + [[(at_host, 0), (at_end, 0)] for at_host, at_end in zip(over_env + over_side_env, far_env + far_side_env)],
         half,
     )
     q_here = (q_here, swap(q_here))
     q_there = (q_there, swap(after(q_there, over_side_parts[0], host_parts[0])))
-    here_over, here_own = second(q_here, [[over_site], [mine]], q_there[0])
-    there_own = second(q_there, [[(over_site, mine)]], here_own)
-    there_side = second(q_there, [list(zip(over_side_parts, host_parts))], there_own)
+    there_own = second(q_there, [list(zip(over_site, parts))])
+    here_over, here_own = second(q_here, [over_site, parts], there_own)
+    there_side = second(q_there, [list(zip(over_side_parts, host_parts))], here_own)
+    far_there_own = to_end(there_own)
     came_here_over = to_col(here_over, (1, 2), True)
-    far_there_own = to_end(there_own)
     near_own = hosts_or(here_own, there_own)
     came_near_own = to_col(near_own, range(4), False)
     far_there_side = to_end(there_side)
@@ -384,8 +384,8 @@
         q_here, [side_parts, over_side_parts], there_side, came_here_over, far_there_own, came_near_own
     )
     near_side = hosts_or(here_side, there_side)
-    came_near_side = to_col(near_side, range(4), False)
     came_far_own = to_col(far_there_own, (0, 3), True)
+    came_near_side = to_col(after(near_side, came_far_own), range(4), False)
     came_here_over_side = to_col(here_over_side, (1, 2), True)
     came_far_side = to_col(after(far_there_side, came_far_own), (0, 3), True)
 

time: 338 us -> 360 us (1.065)
  waiting for transfers between devices: 129 us -> 146 us
  between operations: 0.59 us -> 13.6 us
  local copies, waits for them, and re-layouts: 19.4 us -> 10.6 us
  other arithmetic: 15.3 us -> 11.7 us
    ppermute x7 -> x8, waiting for transfers between devices: 21.9 us -> 76 us  [four_rows(): to_end = lambda value: lax.ppermute(value, 'row', [(1, 0), (2, 3)])]
    ppermute x2, waiting for transfers between devices: 23.7 us -> 4.75 us  [four_rows(): to_host = lambda value: lax.ppermute(value, 'row', [(0, 1), (3, 2)])]
    ppermute x3 -> x0, waiting for transfers between devices: 17.8 us -> none  [four_rows(): turn = lambda value: lax.ppermute(value, 'col', [(0, 1), (1, 0)])]
    ppermute x8 -> x4, waiting for transfers between devices: 0.02 us -> 14.2 us  [swap(): return lax.ppermute(value, 'depth', [(0, 1), (1, 0)])]
    ppermute x6, waiting for transfers between devices: 25.9 us -> 14.2 us  [to_col(): return lax.ppermute(value, axes, pairs)]
    ppermute x2, starting transfers between devices: 4.3 us -> 14.5 us  [four_rows(): to_host = lambda value: lax.ppermute(value, 'row', [(0, 1), (3, 2)])]
    ppermute x8 -> x4, starting transfers between devices: 13.4 us -> 8.11 us  [swap(): return lax.ppermute(value, 'depth', [(0, 1), (1, 0)])]
    unnamed x62 -> x42, local copies, waits for them, and re-layouts: 7.14 us -> 2.05 us
  transfers between devices with their start and end apart: 35 -> 33, of which waited for: 12 -> 14; matrix products, arithmetic and copies ran while one was open for 8% -> 3% of each run, Pallas kernels for 32% -> 30%
where the time goes in v11:
time: 360 us; the launch traced here: 358 us
  waiting for transfers between devices  146 us (41%)
  Pallas kernels  113 us (31%)
  starting transfers between devices  62.3 us (17%)
  between operations  13.6 us (4%)
  other arithmetic  11.7 us (3%)
  local copies, waits for them, and re-layouts  10.6 us (3%)
    ppermute x8, waiting for transfers between devices, four_rows(): to_end = lambda value: lax.ppermute(value, 'row', [(1, 0), (2, 3)])  76 us
    pallas_call x2, Pallas kernels, first_product(): pl.pallas_call(functools.partial(first_kernel, site_sources, sources), gr...  56.5 us
    pallas_call x4, Pallas kernels, second_product(): pl.pallas_call(functools.partial(second_kernel, groups), grid_spec=pltpu....  52.6 us
    ppermute x2, waiting for transfers between devices, four_rows(): lax.ppermute(value, 'row', [(0, 1), (1, 0), (2, 3), (3, 2)])  37.3 us
    ppermute x2, starting transfers between devices, four_rows(): to_host = lambda value: lax.ppermute(value, 'row', [(0, 1), (3, 2)])  14.5 us
    ppermute x4, waiting for transfers between devices, swap(): return lax.ppermute(value, 'depth', [(0, 1), (1, 0)])  14.2 us
    ppermute x6, waiting for transfers between devices, to_col(): return lax.ppermute(value, axes, pairs)  14.2 us
    ppermute x6, starting transfers between devices, to_col(): return lax.ppermute(value, axes, pairs)  13.2 us
  transfers between devices with their start and end apart: 33, of which 14 were waited for; matrix products, arithmetic and copies ran while one was open for 3% of the time, Pallas kernels for 30%

profile of v11, /device:TPU:1, one launch (start us, length us, event | category | flops | bytes accessed | tf_op | source)
XLA Modules:
  0.0 358.2 jit_solution(15119688246873419367)
XLA Ops:
  6.5 1.7 constant_dynamic-slice_fusion
  8.2 0.1 collective-permute-start
  8.3 2.6 collective-permute-done.refs_2_.refs_4_
  11.0 3.9 %copy.5 = bf16[2,512,2,1024]{3,1,2,0:T(8,128)(2,1)S(1)} copy(bf16[2,512,2,1024]{3,2,1,0:T(2,128)(2,1)} %param.4) | data formatting | bytes 8388608 | tf_op jit(solution)/shard_map/optimization_barrier | solution.py:241
  14.8 1.5 dynamic-slice_bitcast_fusion
  16.4 2.5 collective-permute-start.1
  18.9 0.7 collective-permute-start.3
  19.6 3.8 %collective-permute-start.2 = (bf16[1,2,512,512]{3,2,1,0:T(8,128)(2,1)}, bf16[1,2,512,512]{3,2,1,0:T(8,128)(2,1)}, u32[]{:S(2)}, u32[]{:S(2)}) collective-permute-start(bf16[1,2,512,512]{3,2,1,0:T(8,128)(2,1)} %copy-done.7), channel_id=1, source_target_pairs={{0,4},{4,0},{8,12},{12,8},{1,5},{5,1},{9,13},{13,9},{2,6},{6,2},{1... | collective-permute-start | bytes 3145736 | tf_op jit(solution)/shard_map/ppermute | solution.py:303
  23.5 1.7 collective-permute-start.4
  25.1 17.1 %collective-permute-done.1.refs_3_.refs_5_ = bf16[1,2,512,512]{3,2,1,0:T(8,128)(2,1)S(1)} collective-permute-done((bf16[1,2,512,512]{3,2,1,0:T(8,128)(2,1)S(1)}, bf16[1,2,512,512]{3,2,1,0:T(8,128)(2,1)S(1)}, u32[]{:S(2)}, u32[]{:S(2)}) %collective-permute-start.1) | collective-permute-done | bytes 1048608 | tf_op jit(solution)/shard_map/ppermute | solution.py:303
  42.3 0.7 collective-permute-start.5
  43.0 1.3 collective-permute-start.8
  44.3 0.2 fusion.1
  44.5 20.2 %collective-permute-done.2.refs_4_.refs_6_ = bf16[1,2,512,512]{3,2,1,0:T(8,128)(2,1)} collective-permute-done((bf16[1,2,512,512]{3,2,1,0:T(8,128)(2,1)}, bf16[1,2,512,512]{3,2,1,0:T(8,128)(2,1)}, u32[]{:S(2)}, u32[]{:S(2)}) %collective-permute-start.2) | collective-permute-done | bytes 1048608 | tf_op jit(solution)/shard_map/ppermute | solution.py:303
  64.7 7.1 %collective-permute-start.7 = (bf16[2,2,128,1024]{3,2,1,0:T(8,128)(2,1)S(1)}, bf16[2,2,128,1024]{3,2,1,0:T(8,128)(2,1)}, u32[]{:S(2)}, u32[]{:S(2)}) collective-permute-start(bf16[2,2,128,1024]{3,2,1,0:T(8,128)(2,1)S(1)} %get-tuple-element.50.refs_1_.refs_2_), channel_id=1, source_target_pairs={{0,4},{12,8},{1,5},{13,9},{2,6},{14,10},{3,7},{15,11},{16,20},{28,... | collective-permute-start | bytes 3145736 | tf_op jit(solution)/shard_map/ppermute | solution.py:304
  71.8 15.3 %collective-permute-done.8.refs_8_ = bf16[1,2,512,512]{3,2,1,0:T(8,128)(2,1)S(1)} collective-permute-done((bf16[1,2,512,512]{3,2,1,0:T(8,128)(2,1)S(1)}, bf16[1,2,512,512]{3,2,1,0:T(8,128)(2,1)S(1)}, u32[]{:S(2)}, u32[]{:S(2)}) %collective-permute-start.8) | collective-permute-done | bytes 1048608 | tf_op jit(solution)/shard_map/ppermute | solution.py:305
  87.1 1.0 copy-done.15
  88.1 3.2 collective-permute-done.7.refs_0_
  91.3 1.6 collective-permute-start.6
  92.9 1.3 collective-permute-start.10
  94.2 7.4 %collective-permute-start.9 = (bf16[2,2,128,1024]{3,2,1,0:T(8,128)(2,1)S(1)}, bf16[2,2,128,1024]{3,2,1,0:T(8,128)(2,1)}, u32[]{:S(2)}, u32[]{:S(2)}) collective-permute-start(bf16[2,2,128,1024]{3,2,1,0:T(8,128)(2,1)S(1)} %get-tuple-element.57.refs_3_), channel_id=1, source_target_pairs={{0,4},{12,8},{1,5},{13,9},{2,6},{14,10},{3,7},{15,11},{16,20},{28,... | collective-permute-start | bytes 3145736 | tf_op jit(solution)/shard_map/ppermute | solution.py:304
  101.6 16.4 %collective-permute-done.10.refs_10_ = bf16[1,2,512,512]{3,2,1,0:T(8,128)(2,1)} collective-permute-done((bf16[1,2,512,512]{3,2,1,0:T(8,128)(2,1)}, bf16[1,2,512,512]{3,2,1,0:T(8,128)(2,1)}, u32[]{:S(2)}, u32[]{:S(2)}) %collective-permute-start.10) | collective-permute-done | bytes 1048608 | tf_op jit(solution)/shard_map/ppermute | solution.py:305
  118.1 1.6 collective-permute-done.9.refs_1_
  119.7 1.3 collective-permute-start.11
  121.0 1.6 collective-permute-start.13
  122.6 1.3 collective-permute-start.12
  123.9 1.6 collective-permute-start.14
  125.5 0.7 stack.45.pick_ref
  126.2 0.6 pad_maximum_fusion.mpo_ref
  126.8 27.6 %first_product.2.own_ref = bf16[2,2,2,512,512]{4,3,2,1,0:T(8,128)(2,1)} custom-call(s32[6]{0:T(128)} %stack.45.pick_ref, f32[2,2,2,2]{3,2,1,0:T(2,128)} %pad_maximum_fusion.mpo_ref, bf16[4,2,2,256,1024]{4,3,2,1,0:T(8,128)(2,1)} %bitcast.13, bf16[1,2,512,512]{3,2,1,0:T(8,128)(2,1)} %copy-done.2, bf16[1,2,512,512]{3,2,1,0:T(8,128)(2,1)} %copy-done.7, ...), custom_call_target="tpu_custom_call" | custom-call | tf_op jit(solution)/shard_map/first_product/pallas_call | solution.py:123
  154.5 10.6 %collective-permute-done.12.refs_14_ = bf16[1,2,512,512]{3,2,1,0:T(8,128)(2,1)} collective-permute-done((bf16[1,2,512,512]{3,2,1,0:T(8,128)(2,1)}, bf16[1,2,512,512]{3,2,1,0:T(8,128)(2,1)}, u32[]{:S(2)}, u32[]{:S(2)}) %collective-permute-start.12) | collective-permute-done | bytes 1048608 | tf_op jit(solution)/shard_map/ppermute | solution.py:305
  165.1 0.7 collective-permute-start.15
  165.8 1.5 collective-permute-start.16
  167.3 0.7 stack.42.pick_ref
  168.0 28.9 %first_product.3.own_ref = bf16[2,2,2,512,512]{4,3,2,1,0:T(8,128)(2,1)} custom-call(s32[6]{0:T(128)} %stack.42.pick_ref, f32[2,2,2,2]{3,2,1,0:T(2,128)} %pad_maximum_fusion.mpo_ref, bf16[4,2,2,128,1024]{4,3,2,1,0:T(8,128)(2,1)} %bitcast.15, bf16[4,2,2,128,1024]{4,3,2,1,0:T(8,128)(2,1)} %bitcast.16, bf16[4,2,2,256,1024]{4,3,2,1,0:T(8,128)(2,1)} %bitcast.14, ...), custom_call_target="tpu_custom_call" | custom-call | tf_op jit(solution)/shard_map/first_product/pallas_call | solution.py:123
  196.9 5.1 %collective-permute-start.17 = (bf16[2,2,2,512,512]{4,3,2,1,0:T(8,128)(2,1)}, bf16[2,2,2,512,512]{4,3,2,1,0:T(8,128)(2,1)}, u32[]{:S(2)}, u32[]{:S(2)}) collective-permute-start(bf16[2,2,2,512,512]{4,3,2,1,0:T(8,128)(2,1)} %first_product.3.own_ref), channel_id=1, source_target_pairs={{0,1},{1,0},{2,3},{3,2},{4,5},{5,4},{6,7},{7,6},{8,9},{9,8},{10,11... | collective-permute-start | bytes 12582920 | tf_op jit(solution)/shard_map/ppermute | solution.py:245
  202.2 0.6 pad_add_fusion.pick_ref
  202.7 11.6 %collective-permute-done.17.sib_ref = bf16[2,2,2,512,512]{4,3,2,1,0:T(8,128)(2,1)} collective-permute-done((bf16[2,2,2,512,512]{4,3,2,1,0:T(8,128)(2,1)}, bf16[2,2,2,512,512]{4,3,2,1,0:T(8,128)(2,1)}, u32[]{:S(2)}, u32[]{:S(2)}) %collective-permute-start.17) | collective-permute-done | bytes 4194336 | tf_op jit(solution)/shard_map/ppermute | solution.py:245
  214.3 10.5 %second_product.4 = bf16[2,2,512,256]{3,2,1,0:T(8,128)(2,1)} custom-call(s32[2]{0:T(128)} %pad_add_fusion.pick_ref, bf16[2,2,2,512,512]{4,3,2,1,0:T(8,128)(2,1)} %first_product.3.own_ref, bf16[2,2,2,512,512]{4,3,2,1,0:T(8,128)(2,1)} %collective-permute-done.17.sib_ref, bf16[2,2,128,1024]{3,2,1,0:T(8,128)(2,1)} %collective-permute-done.13.refs_0_, ...), custom_call_target="tpu_custom_call" | custom-call | tf_op jit(solution)/shard_map/second_product/pallas_call | solution.py:202
  224.8 1.3 collective-permute-start.21
  226.1 0.7 collective-permute-start.23
  226.9 1.3 collective-permute-start.24
  228.2 15.8 %second_product.5 = (bf16[2,2,512,256]{3,2,1,0:T(8,128)(2,1)}, bf16[2,2,512,256]{3,2,1,0:T(8,128)(2,1)}) custom-call(s32[2]{0:T(128)} %pad_add_fusion.pick_ref, bf16[2,2,2,512,512]{4,3,2,1,0:T(8,128)(2,1)} %first_product.2.own_ref, bf16[2,2,2,512,512]{4,3,2,1,0:T(8,128)(2,1)} %collective-permute-done.18.sib_ref, ...), custom_call_target="tpu_custom_call" | custom-call | tf_op jit(solution)/shard_map/second_product/pallas_call | solution.py:202
  244.0 0.7 collective-permute-start.20
  244.9 1.3 collective-permute-start.19
  246.2 9.5 %collective-permute-done.21 = bf16[2,2,512,256]{3,2,1,0:T(8,128)(2,1)} collective-permute-done((bf16[2,2,512,256]{3,2,1,0:T(8,128)(2,1)}, bf16[2,2,512,256]{3,2,1,0:T(8,128)(2,1)}, u32[]{:S(2)}, u32[]{:S(2)}) %collective-permute-start.21) | collective-permute-done | bytes 1048608 | tf_op jit(solution)/shard_map/ppermute | solution.py:305
  255.7 4.1 %collective-permute-start.22 = (bf16[2,2,512,256]{3,2,1,0:T(8,128)(2,1)}, bf16[2,2,512,256]{3,2,1,0:T(8,128)(2,1)}, u32[]{:S(2)}, u32[]{:S(2)}) collective-permute-start(bf16[2,2,512,256]{3,2,1,0:T(8,128)(2,1)} %collective-permute-done.21), channel_id=1, source_target_pairs={{0,2},{1,3},{14,12},{15,13},{16,18},{17,19},{30,28},{31,29}} | collective-permute-start | bytes 3145736 | tf_op jit(solution)/shard_map/ppermute | solution.py:314
  259.8 18.4 %collective-permute-done.24.refs_3_ = bf16[2,2,128,1024]{3,2,1,0:T(8,128)(2,1)} collective-permute-done((bf16[2,2,128,1024]{3,2,1,0:T(8,128)(2,1)S(1)}, bf16[2,2,128,1024]{3,2,1,0:T(8,128)(2,1)}, u32[]{:S(2)}, u32[]{:S(2)}) %collective-permute-start.24) | collective-permute-done | bytes 1048608 | tf_op jit(solution)/shard_map/ppermute | solution.py:305
  278.2 10.5 %second_product.6 = bf16[2,2,512,256]{3,2,1,0:T(8,128)(2,1)} custom-call(s32[2]{0:T(128)} %pad_add_fusion.pick_ref, bf16[2,2,2,512,512]{4,3,2,1,0:T(8,128)(2,1)} %first_product.3.own_ref, bf16[2,2,2,512,512]{4,3,2,1,0:T(8,128)(2,1)} %collective-permute-done.17.sib_ref, bf16[2,2,128,1024]{3,2,1,0:T(8,128)(2,1)} %copy-done.11, ...), custom_call_target="tpu_custom_call" | custom-call | tf_op jit(solution)/shard_map/second_product/pallas_call | solution.py:202
  288.7 1.4 collective-permute-start.27
  290.2 15.7 %second_product.7 = (bf16[2,2,512,256]{3,2,1,0:T(8,128)(2,1)}, bf16[2,2,512,256]{3,2,1,0:T(8,128)(2,1)}) custom-call(s32[2]{0:T(128)} %pad_add_fusion.pick_ref, bf16[2,2,2,512,512]{4,3,2,1,0:T(8,128)(2,1)} %first_product.2.own_ref, bf16[2,2,2,512,512]{4,3,2,1,0:T(8,128)(2,1)} %collective-permute-done.18.sib_ref, ...), custom_call_target="tpu_custom_call" | custom-call | tf_op jit(solution)/shard_map/second_product/pallas_call | solution.py:202
  305.9 1.7 collective-permute-start.26
  307.7 1.3 collective-permute-start.25
  309.0 5.8 %collective-permute-done.27 = bf16[2,2,512,256]{3,2,1,0:T(8,128)(2,1)} collective-permute-done((bf16[2,2,512,256]{3,2,1,0:T(8,128)(2,1)}, bf16[2,2,512,256]{3,2,1,0:T(8,128)(2,1)}, u32[]{:S(2)}, u32[]{:S(2)}) %collective-permute-start.27) | collective-permute-done | bytes 1048608 | tf_op jit(solution)/shard_map/ppermute | solution.py:305
  314.9 4.1 %collective-permute-start.28 = (bf16[2,2,512,256]{3,2,1,0:T(8,128)(2,1)}, bf16[2,2,512,256]{3,2,1,0:T(8,128)(2,1)}, u32[]{:S(2)}, u32[]{:S(2)}) collective-permute-start(bf16[2,2,512,256]{3,2,1,0:T(8,128)(2,1)} %collective-permute-done.27), channel_id=1, source_target_pairs={{0,2},{1,3},{14,12},{15,13},{16,18},{17,19},{30,28},{31,29}} | collective-permute-start | bytes 3145736 | tf_op jit(solution)/shard_map/ppermute | solution.py:314
  319.0 3.3 select_select_fusion.1
  322.3 11.2 %collective-permute-done.25 = bf16[2,2,512,256]{3,2,1,0:T(8,128)(2,1)} collective-permute-done((bf16[2,2,512,256]{3,2,1,0:T(8,128)(2,1)S(1)}, bf16[2,2,512,256]{3,2,1,0:T(8,128)(2,1)}, u32[]{:S(2)}, u32[]{:S(2)}) %collective-permute-start.25) | collective-permute-done | bytes 1048608 | tf_op jit(solution)/shard_map/ppermute | solution.py:314
  333.5 2.5 select_select_fusion
  336.0 3.0 collective-permute-done.28
  338.9 1.6 select_convert_fusion
  340.5 2.8 collective-permute-start.29
  343.3 2.9 fusion.mine_ref
  346.2 1.0 copy-done.19
  347.2 4.4 %finish.1 = f32[2,2,512,512]{3,2,1,0:T(8,128)} custom-call(s32[2]{0:T(128)} %pad_add_fusion.pick_ref, f32[2,2,512,256]{3,2,1,0:T(8,128)} %fusion.mine_ref, bf16[2,2,512,256]{3,2,1,0:T(8,128)(2,1)} %copy-done.19), custom_call_target="tpu_custom_call" | custom-call | tf_op jit(solution)/shard_map/finish/pallas_call | solution.py:228
  (69 shorter events, 0.6 us)
Async XLA Ops:
  6.5 120.3 %all-gather.7.cloned.1.call-start = ((), (), s32[]{:S(2)}) async-start(), calls=%async_computation | async-start | bytes 10485760 | tf_op jit(solution)/shard_map/all_gather | solution.py:326
  8.2 10.7 %copy-start.2 = (bf16[1,2,512,512]{3,2,1,0:T(8,128)(2,1)}, bf16[1,2,512,512]{3,2,1,0:T(8,128)(2,1)S(1)}, u32[]{:S(2)}) copy-start(bf16[1,2,512,512]{3,2,1,0:T(8,128)(2,1)S(1)} %get-tuple-element.67.refs_1_.refs_3_) | copy-start | bytes 3145732
  8.2 2.7 collective-permute-start
  11.0 3.9 %copy-start.7 = (bf16[1,2,512,512]{3,2,1,0:T(8,128)(2,1)}, bf16[1,2,512,512]{3,2,1,0:T(8,128)(2,1)S(1)}, u32[]{:S(2)}) copy-start(bf16[1,2,512,512]{3,2,1,0:T(8,128)(2,1)S(1)} %collective-permute-done.refs_2_.refs_4_) | copy-start | bytes 3145732
  16.3 27.9 %copy-start.1 = (bf16[2,2,256,1024]{3,2,1,0:T(8,128)(2,1)S(1)}, bf16[2,2,256,1024]{3,2,1,0:T(8,128)(2,1)}, u32[]{:S(2)}) copy-start(bf16[2,2,256,1024]{3,2,1,0:T(8,128)(2,1)} %dynamic-slice_bitcast_fusion) | copy-start | bytes 6291460
  16.4 151.6 %all-gather.9.cloned.1.call-start = ((), (), s32[]{:S(2)}) async-start(), calls=%async_computation.1 | async-start | bytes 5242880 | tf_op jit(solution)/shard_map/all_gather | solution.py:326
  16.4 25.8 %collective-permute-start.1 = (bf16[1,2,512,512]{3,2,1,0:T(8,128)(2,1)S(1)}, bf16[1,2,512,512]{3,2,1,0:T(8,128)(2,1)S(1)}, u32[]{:S(2)}, u32[]{:S(2)}) collective-permute-start(bf16[1,2,512,512]{3,2,1,0:T(8,128)(2,1)S(1)} %get-tuple-element.67.refs_1_.refs_3_), channel_id=1, source_target_pairs={{0,4},{4,0},{8,12},{12,8},{1,5},{5,1},{9,13},{13,9},{2,6},{6,2},{1... | collective-permute-start | bytes 3145736 | tf_op jit(solution)/shard_map/ppermute | solution.py:303
  18.9 23.3 %collective-permute-start.3 = (bf16[1,2,512,512]{3,2,1,0:T(8,128)(2,1)S(1)}, bf16[1,2,512,512]{3,2,1,0:T(8,128)(2,1)S(1)}, u32[]{:S(2)}, u32[]{:S(2)}) collective-permute-start(bf16[1,2,512,512]{3,2,1,0:T(8,128)(2,1)S(1)} %get-tuple-element.67.refs_1_.refs_3_), channel_id=1, source_target_pairs={{4,8},{8,4},{5,9},{9,5},{6,10},{10,6},{7,11},{11,7},{20,24},{24,20... | collective-permute-start | bytes 3145736 | tf_op jit(solution)/shard_map/ppermute | solution.py:306
  19.6 45.1 %collective-permute-start.2 = (bf16[1,2,512,512]{3,2,1,0:T(8,128)(2,1)}, bf16[1,2,512,512]{3,2,1,0:T(8,128)(2,1)}, u32[]{:S(2)}, u32[]{:S(2)}) collective-permute-start(bf16[1,2,512,512]{3,2,1,0:T(8,128)(2,1)} %copy-done.7), channel_id=1, source_target_pairs={{0,4},{4,0},{8,12},{12,8},{1,5},{5,1},{9,13},{13,9},{2,6},{6,2},{1... | collective-permute-start | bytes 3145736 | tf_op jit(solution)/shard_map/ppermute | solution.py:303
  23.5 41.2 %collective-permute-start.4 = (bf16[1,2,512,512]{3,2,1,0:T(8,128)(2,1)}, bf16[1,2,512,512]{3,2,1,0:T(8,128)(2,1)}, u32[]{:S(2)}, u32[]{:S(2)}) collective-permute-start(bf16[1,2,512,512]{3,2,1,0:T(8,128)(2,1)} %copy-done.7), channel_id=1, source_target_pairs={{4,8},{8,4},{5,9},{9,5},{6,10},{10,6},{7,11},{11,7},{20,24},{24,20... | collective-permute-start | bytes 3145736 | tf_op jit(solution)/shard_map/ppermute | solution.py:306
  42.2 22.5 %copy-start.8 = (bf16[1,2,512,512]{3,2,1,0:T(8,128)(2,1)}, bf16[1,2,512,512]{3,2,1,0:T(8,128)(2,1)S(1)}, u32[]{:S(2)}) copy-start(bf16[1,2,512,512]{3,2,1,0:T(8,128)(2,1)S(1)} %collective-permute-done.1.refs_3_.refs_5_) | copy-start | bytes 3145732
  42.3 22.5 %copy-start.9 = (bf16[1,2,512,512]{3,2,1,0:T(8,128)(2,1)}, bf16[1,2,512,512]{3,2,1,0:T(8,128)(2,1)S(1)}, u32[]{:S(2)}) copy-start(bf16[1,2,512,512]{3,2,1,0:T(8,128)(2,1)S(1)} %collective-permute-done.3.refs_5_.refs_7_) | copy-start | bytes 3145732
  42.3 29.6 %collective-permute-start.5 = (bf16[1,2,512,512]{3,2,1,0:T(8,128)(2,1)S(1)}, bf16[1,2,512,512]{3,2,1,0:T(8,128)(2,1)S(1)}, u32[]{:S(2)}, u32[]{:S(2)}) collective-permute-start(bf16[1,2,512,512]{3,2,1,0:T(8,128)(2,1)S(1)} %collective-permute-done.1.refs_3_.refs_5_), channel_id=1, source_target_pairs={{4,8},{8,4},{5,9},{9,5},{6,10},{10,6},{7,11},{11,7},{20,24},{24,20... | collective-permute-start | bytes 3145736 | tf_op jit(solution)/shard_map/ppermute | solution.py:306
  43.0 44.1 %collective-permute-start.8 = (bf16[1,2,512,512]{3,2,1,0:T(8,128)(2,1)S(1)}, bf16[1,2,512,512]{3,2,1,0:T(8,128)(2,1)S(1)}, u32[]{:S(2)}, u32[]{:S(2)}) collective-permute-start(bf16[1,2,512,512]{3,2,1,0:T(8,128)(2,1)S(1)} %collective-permute-done.3.refs_5_.refs_7_), channel_id=1, source_target_pairs={{4,0},{8,12},{5,1},{9,13},{6,2},{10,14},{7,3},{11,15},{20,16},{24,... | collective-permute-start | bytes 3145736 | tf_op jit(solution)/shard_map/ppermute | solution.py:305
  44.5 20.3 %copy-start.5 = (bf16[2,2,128,1024]{3,2,1,0:T(8,128)(2,1)}, bf16[2,2,128,1024]{3,2,1,0:T(8,128)(2,1)S(1)}, u32[]{:S(2)}) copy-start(bf16[2,2,128,1024]{3,2,1,0:T(8,128)(2,1)S(1)} %get-tuple-element.50.refs_1_.refs_2_) | copy-start | bytes 3145732
  44.5 109.9 %copy-start.3 = (bf16[2,2,128,1024]{3,2,1,0:T(8,128)(2,1)}, bf16[2,2,128,1024]{3,2,1,0:T(8,128)(2,1)S(1)}, u32[]{:S(2)}) copy-start(bf16[2,2,128,1024]{3,2,1,0:T(8,128)(2,1)S(1)} %get-tuple-element.57.refs_3_) | copy-start | bytes 3145732
  44.5 81.7 %copy-start.20 = (f32[2,2,2,2]{3,2,1,0:T(2,128)S(1)}, f32[2,2,2,2]{3,2,1,0:T(2,128)}, u32[]{:S(2)}) copy-start(f32[2,2,2,2]{3,2,1,0:T(2,128)} %param.5) | copy-start | bytes 196
  64.7 26.5 %collective-permute-start.7 = (bf16[2,2,128,1024]{3,2,1,0:T(8,128)(2,1)S(1)}, bf16[2,2,128,1024]{3,2,1,0:T(8,128)(2,1)}, u32[]{:S(2)}, u32[]{:S(2)}) collective-permute-start(bf16[2,2,128,1024]{3,2,1,0:T(8,128)(2,1)S(1)} %get-tuple-element.50.refs_1_.refs_2_), channel_id=1, source_target_pairs={{0,4},{12,8},{1,5},{13,9},{2,6},{14,10},{3,7},{15,11},{16,20},{28,... | collective-permute-start | bytes 3145736 | tf_op jit(solution)/shard_map/ppermute | solution.py:304
  71.8 49.1 %copy-start.6 = (bf16[2,2,128,1024]{3,2,1,0:T(8,128)(2,1)S(1)}, bf16[2,2,128,1024]{3,2,1,0:T(8,128)(2,1)}, u32[]{:S(2)}) copy-start(bf16[2,2,128,1024]{3,2,1,0:T(8,128)(2,1)} %copy-done.5) | copy-start | bytes 3145732
  71.8 15.3 %copy-start.10 = (bf16[1,2,512,512]{3,2,1,0:T(8,128)(2,1)}, bf16[1,2,512,512]{3,2,1,0:T(8,128)(2,1)S(1)}, u32[]{:S(2)}) copy-start(bf16[1,2,512,512]{3,2,1,0:T(8,128)(2,1)S(1)} %collective-permute-done.5.refs_7_.refs_11_) | copy-start | bytes 3145732
  87.1 1.0 copy-start.15
  91.3 76.7 %all-gather.11.cloned.1.call-start = ((), (), s32[]{:S(2)}) async-start(), calls=%async_computation.2 | async-start | bytes 5242880 | tf_op jit(solution)/shard_map/all_gather | solution.py:326
  91.3 10.3 %collective-permute-start.6 = (bf16[1,2,512,512]{3,2,1,0:T(8,128)(2,1)}, bf16[1,2,512,512]{3,2,1,0:T(8,128)(2,1)}, u32[]{:S(2)}, u32[]{:S(2)}) collective-permute-start(bf16[1,2,512,512]{3,2,1,0:T(8,128)(2,1)} %collective-permute-done.2.refs_4_.refs_6_), channel_id=1, source_target_pairs={{4,8},{8,4},{5,9},{9,5},{6,10},{10,6},{7,11},{11,7},{20,24},{24,20... | collective-permute-start | bytes 3145736 | tf_op jit(solution)/shard_map/ppermute | solution.py:306
  92.9 25.1 %collective-permute-start.10 = (bf16[1,2,512,512]{3,2,1,0:T(8,128)(2,1)}, bf16[1,2,512,512]{3,2,1,0:T(8,128)(2,1)}, u32[]{:S(2)}, u32[]{:S(2)}) collective-permute-start(bf16[1,2,512,512]{3,2,1,0:T(8,128)(2,1)} %collective-permute-done.4.refs_6_.refs_9_), channel_id=1, source_target_pairs={{4,0},{8,12},{5,1},{9,13},{6,2},{10,14},{7,3},{11,15},{20,16},{24,... | collective-permute-start | bytes 3145736 | tf_op jit(solution)/shard_map/ppermute | solution.py:305
  94.2 25.4 %collective-permute-start.9 = (bf16[2,2,128,1024]{3,2,1,0:T(8,128)(2,1)S(1)}, bf16[2,2,128,1024]{3,2,1,0:T(8,128)(2,1)}, u32[]{:S(2)}, u32[]{:S(2)}) collective-permute-start(bf16[2,2,128,1024]{3,2,1,0:T(8,128)(2,1)S(1)} %get-tuple-element.57.refs_3_), channel_id=1, source_target_pairs={{0,4},{12,8},{1,5},{13,9},{2,6},{14,10},{3,7},{15,11},{16,20},{28,... | collective-permute-start | bytes 3145736 | tf_op jit(solution)/shard_map/ppermute | solution.py:304
  119.7 34.8 %collective-permute-start.11 = (bf16[1,2,512,512]{3,2,1,0:T(8,128)(2,1)}, bf16[1,2,512,512]{3,2,1,0:T(8,128)(2,1)}, u32[]{:S(2)}, u32[]{:S(2)}) collective-permute-start(bf16[1,2,512,512]{3,2,1,0:T(8,128)(2,1)} %copy-done.10), channel_id=1, source_target_pairs={{4,0},{8,12},{5,1},{9,13},{6,2},{10,14},{7,3},{11,15},{20,16},{24,... | collective-permute-start | bytes 3145736 | tf_op jit(solution)/shard_map/ppermute | solution.py:305
  121.0 33.5 %collective-permute-start.13 = (bf16[2,2,128,1024]{3,2,1,0:T(8,128)(2,1)S(1)}, bf16[2,2,128,1024]{3,2,1,0:T(8,128)(2,1)}, u32[]{:S(2)}, u32[]{:S(2)}) collective-permute-start(bf16[2,2,128,1024]{3,2,1,0:T(8,128)(2,1)S(1)} %copy-done.6), channel_id=1, source_target_pairs={{4,8},{8,4},{5,9},{9,5},{6,10},{10,6},{7,11},{11,7},{20,24},{24,20... | collective-permute-start | bytes 3145736 | tf_op jit(solution)/shard_map/ppermute | solution.py:306
  122.6 42.5 %collective-permute-start.12 = (bf16[1,2,512,512]{3,2,1,0:T(8,128)(2,1)}, bf16[1,2,512,512]{3,2,1,0:T(8,128)(2,1)}, u32[]{:S(2)}, u32[]{:S(2)}) collective-permute-start(bf16[1,2,512,512]{3,2,1,0:T(8,128)(2,1)} %collective-permute-done.6.refs_8_.refs_13_), channel_id=1, source_target_pairs={{4,0},{8,12},{5,1},{9,13},{6,2},{10,14},{7,3},{11,15},{20,16},{24,... | collective-permute-start | bytes 3145736 | tf_op jit(solution)/shard_map/ppermute | solution.py:305
  123.9 41.2 %collective-permute-start.14 = (bf16[2,2,128,1024]{3,2,1,0:T(8,128)(2,1)S(1)}, bf16[2,2,128,1024]{3,2,1,0:T(8,128)(2,1)}, u32[]{:S(2)}, u32[]{:S(2)}) collective-permute-start(bf16[2,2,128,1024]{3,2,1,0:T(8,128)(2,1)S(1)} %get-tuple-element.57.refs_3_), channel_id=1, source_target_pairs={{4,8},{8,4},{5,9},{9,5},{6,10},{10,6},{7,11},{11,7},{20,24},{24,20... | collective-permute-start | bytes 3145736 | tf_op jit(solution)/shard_map/ppermute | solution.py:306
  165.1 31.8 %collective-permute-start.15 = (bf16[2,2,128,1024]{3,2,1,0:T(8,128)(2,1)}, bf16[2,2,128,1024]{3,2,1,0:T(8,128)(2,1)S(1)}, u32[]{:S(2)}, u32[]{:S(2)}) collective-permute-start(bf16[2,2,128,1024]{3,2,1,0:T(8,128)(2,1)} %collective-permute-done.7.refs_0_), channel_id=1, source_target_pairs={{4,8},{8,4},{5,9},{9,5},{6,10},{10,6},{7,11},{11,7},{20,24},{24,20... | collective-permute-start | bytes 3145736 | tf_op jit(solution)/shard_map/ppermute | solution.py:306
  165.8 31.1 %collective-permute-start.16 = (bf16[2,2,128,1024]{3,2,1,0:T(8,128)(2,1)S(1)}, bf16[2,2,128,1024]{3,2,1,0:T(8,128)(2,1)}, u32[]{:S(2)}, u32[]{:S(2)}) collective-permute-start(bf16[2,2,128,1024]{3,2,1,0:T(8,128)(2,1)S(1)} %copy-done.6), channel_id=1, source_target_pairs={{4,0},{8,12},{5,1},{9,13},{6,2},{10,14},{7,3},{11,15},{20,16},{24,... | collective-permute-start | bytes 3145736 | tf_op jit(solution)/shard_map/ppermute | solution.py:305
  168.0 34.1 %copy-start = (bf16[2,2,2,512,512]{4,3,2,1,0:T(8,128)(2,1)S(1)}, bf16[2,2,2,512,512]{4,3,2,1,0:T(8,128)(2,1)}, u32[]{:S(2)}) copy-start(bf16[2,2,2,512,512]{4,3,2,1,0:T(8,128)(2,1)} %first_product.2.own_ref) | copy-start | bytes 12582916
  196.9 27.9 %copy-start.11 = (bf16[2,2,128,1024]{3,2,1,0:T(8,128)(2,1)}, bf16[2,2,128,1024]{3,2,1,0:T(8,128)(2,1)S(1)}, u32[]{:S(2)}) copy-start(bf16[2,2,128,1024]{3,2,1,0:T(8,128)(2,1)S(1)} %collective-permute-done.15.refs_0_.refs_2_) | copy-start | bytes 3145732
  196.9 17.3 %collective-permute-start.17 = (bf16[2,2,2,512,512]{4,3,2,1,0:T(8,128)(2,1)}, bf16[2,2,2,512,512]{4,3,2,1,0:T(8,128)(2,1)}, u32[]{:S(2)}, u32[]{:S(2)}) collective-permute-start(bf16[2,2,2,512,512]{4,3,2,1,0:T(8,128)(2,1)} %first_product.3.own_ref), channel_id=1, source_target_pairs={{0,1},{1,0},{2,3},{3,2},{4,5},{5,4},{6,7},{7,6},{8,9},{9,8},{10,11... | collective-permute-start | bytes 12582920 | tf_op jit(solution)/shard_map/ppermute | solution.py:245
  202.1 26.1 %collective-permute-start.18 = (bf16[2,2,2,512,512]{4,3,2,1,0:T(8,128)(2,1)S(1)}, bf16[2,2,2,512,512]{4,3,2,1,0:T(8,128)(2,1)}, u32[]{:S(2)}, u32[]{:S(2)}) collective-permute-start(bf16[2,2,2,512,512]{4,3,2,1,0:T(8,128)(2,1)S(1)} %copy-done), channel_id=1, source_target_pairs={{0,1},{1,0},{2,3},{3,2},{4,5},{5,4},{6,7},{7,6},{8,9},{9,8},{10,11... | collective-permute-start | bytes 12582920 | tf_op jit(solution)/shard_map/ppermute | solution.py:245
  202.7 24.1 %copy-start.4 = (bf16[2,2,128,1024]{3,2,1,0:T(8,128)(2,1)S(1)}, bf16[2,2,128,1024]{3,2,1,0:T(8,128)(2,1)}, u32[]{:S(2)}) copy-start(bf16[2,2,128,1024]{3,2,1,0:T(8,128)(2,1)} %copy-done.3) | copy-start | bytes 3145732
  224.8 30.9 %collective-permute-start.21 = (bf16[2,2,512,256]{3,2,1,0:T(8,128)(2,1)}, bf16[2,2,512,256]{3,2,1,0:T(8,128)(2,1)}, u32[]{:S(2)}, u32[]{:S(2)}) collective-permute-start(bf16[2,2,512,256]{3,2,1,0:T(8,128)(2,1)} %second_product.4), channel_id=1, source_target_pairs={{4,0},{8,12},{5,1},{9,13},{6,2},{10,14},{7,3},{11,15},{20,16},{24,... | collective-permute-start | bytes 3145736 | tf_op jit(solution)/shard_map/ppermute | solution.py:305
  226.1 33.7 %collective-permute-start.23 = (bf16[2,2,128,1024]{3,2,1,0:T(8,128)(2,1)}, bf16[2,2,128,1024]{3,2,1,0:T(8,128)(2,1)S(1)}, u32[]{:S(2)}, u32[]{:S(2)}) collective-permute-start(bf16[2,2,128,1024]{3,2,1,0:T(8,128)(2,1)} %collective-permute-done.9.refs_1_), channel_id=1, source_target_pairs={{4,8},{8,4},{5,9},{9,5},{6,10},{10,6},{7,11},{11,7},{20,24},{24,20... | collective-permute-start | bytes 3145736 | tf_op jit(solution)/shard_map/ppermute | solution.py:306
  226.9 51.3 %collective-permute-start.24 = (bf16[2,2,128,1024]{3,2,1,0:T(8,128)(2,1)S(1)}, bf16[2,2,128,1024]{3,2,1,0:T(8,128)(2,1)}, u32[]{:S(2)}, u32[]{:S(2)}) collective-permute-start(bf16[2,2,128,1024]{3,2,1,0:T(8,128)(2,1)S(1)} %copy-done.4), channel_id=1, source_target_pairs={{4,0},{8,12},{5,1},{9,13},{6,2},{10,14},{7,3},{11,15},{20,16},{24,... | collective-permute-start | bytes 3145736 | tf_op jit(solution)/shard_map/ppermute | solution.py:305
  228.2 16.6 %copy-start.14 = (bf16[2,2,512,256]{3,2,1,0:T(8,128)(2,1)S(1)}, bf16[2,2,512,256]{3,2,1,0:T(8,128)(2,1)}, u32[]{:S(2)}) copy-start(bf16[2,2,512,256]{3,2,1,0:T(8,128)(2,1)} %second_product.4) | copy-start | bytes 3145732
  244.0 46.1 %collective-permute-start.20 = (bf16[2,2,512,256]{3,2,1,0:T(8,128)(2,1)}, bf16[2,2,512,256]{3,2,1,0:T(8,128)(2,1)S(1)}, u32[]{:S(2)}, u32[]{:S(2)}) collective-permute-start(bf16[2,2,512,256]{3,2,1,0:T(8,128)(2,1)} %get-tuple-element.54), channel_id=1, source_target_pairs={{4,6},{5,7},{10,8},{11,9},{20,22},{21,23},{26,24},{27,25}} | collective-permute-start | bytes 3145736 | tf_op jit(solution)/shard_map/ppermute | solution.py:314
  244.9 45.3 %collective-permute-start.19 = (bf16[2,2,512,256]{3,2,1,0:T(8,128)(2,1)S(1)}, bf16[2,2,512,256]{3,2,1,0:T(8,128)(2,1)S(1)}, u32[]{:S(2)}, u32[]{:S(2)}) collective-permute-start(bf16[2,2,512,256]{3,2,1,0:T(8,128)(2,1)S(1)} %broadcast_select_fusion.1), channel_id=1, source_target_pairs={{2,0},{3,1},{6,4},{7,5},{8,10},{9,11},{12,14},{13,15},{18,16},{19,... | collective-permute-start | bytes 3145736 | tf_op jit(solution)/shard_map/ppermute | solution.py:314
  255.7 52.0 %collective-permute-start.22 = (bf16[2,2,512,256]{3,2,1,0:T(8,128)(2,1)}, bf16[2,2,512,256]{3,2,1,0:T(8,128)(2,1)}, u32[]{:S(2)}, u32[]{:S(2)}) collective-permute-start(bf16[2,2,512,256]{3,2,1,0:T(8,128)(2,1)} %collective-permute-done.21), channel_id=1, source_target_pairs={{0,2},{1,3},{14,12},{15,13},{16,18},{17,19},{30,28},{31,29}} | collective-permute-start | bytes 3145736 | tf_op jit(solution)/shard_map/ppermute | solution.py:314
  259.8 18.4 %copy-start.12 = (bf16[2,2,128,1024]{3,2,1,0:T(8,128)(2,1)}, bf16[2,2,128,1024]{3,2,1,0:T(8,128)(2,1)S(1)}, u32[]{:S(2)}) copy-start(bf16[2,2,128,1024]{3,2,1,0:T(8,128)(2,1)S(1)} %collective-permute-done.23.refs_2_.refs_3_) | copy-start | bytes 3145732
  288.7 18.9 %copy-start.13 = (bf16[2,2,512,256]{3,2,1,0:T(8,128)(2,1)S(1)}, bf16[2,2,512,256]{3,2,1,0:T(8,128)(2,1)}, u32[]{:S(2)}) copy-start(bf16[2,2,512,256]{3,2,1,0:T(8,128)(2,1)} %second_product.6) | copy-start | bytes 3145732
  288.7 26.1 %collective-permute-start.27 = (bf16[2,2,512,256]{3,2,1,0:T(8,128)(2,1)}, bf16[2,2,512,256]{3,2,1,0:T(8,128)(2,1)}, u32[]{:S(2)}, u32[]{:S(2)}) collective-permute-start(bf16[2,2,512,256]{3,2,1,0:T(8,128)(2,1)} %second_product.6), channel_id=1, source_target_pairs={{4,0},{8,12},{5,1},{9,13},{6,2},{10,14},{7,3},{11,15},{20,16},{24,... | collective-permute-start | bytes 3145736 | tf_op jit(solution)/shard_map/ppermute | solution.py:305
  290.2 15.7 %copy-start.16 = (bf16[2,2,512,256]{3,2,1,0:T(8,128)(2,1)}, bf16[2,2,512,256]{3,2,1,0:T(8,128)(2,1)S(1)}, u32[]{:S(2)}) copy-start(bf16[2,2,512,256]{3,2,1,0:T(8,128)(2,1)S(1)} %collective-permute-done.20) | copy-start | bytes 3145732
  290.2 15.7 %copy-start.17 = (bf16[2,2,512,256]{3,2,1,0:T(8,128)(2,1)}, bf16[2,2,512,256]{3,2,1,0:T(8,128)(2,1)S(1)}, u32[]{:S(2)}) copy-start(bf16[2,2,512,256]{3,2,1,0:T(8,128)(2,1)S(1)} %collective-permute-done.19) | copy-start | bytes 3145732
  305.9 16.4 %collective-permute-start.26 = (bf16[2,2,512,256]{3,2,1,0:T(8,128)(2,1)}, bf16[2,2,512,256]{3,2,1,0:T(8,128)(2,1)}, u32[]{:S(2)}, u32[]{:S(2)}) collective-permute-start(bf16[2,2,512,256]{3,2,1,0:T(8,128)(2,1)} %get-tuple-element.61), channel_id=1, source_target_pairs={{4,6},{5,7},{10,8},{11,9},{20,22},{21,23},{26,24},{27,25}} | collective-permute-start | bytes 3145736 | tf_op jit(solution)/shard_map/ppermute | solution.py:314
  307.7 25.8 %collective-permute-start.25 = (bf16[2,2,512,256]{3,2,1,0:T(8,128)(2,1)S(1)}, bf16[2,2,512,256]{3,2,1,0:T(8,128)(2,1)}, u32[]{:S(2)}, u32[]{:S(2)}) collective-permute-start(bf16[2,2,512,256]{3,2,1,0:T(8,128)(2,1)S(1)} %broadcast_select_fusion), channel_id=1, source_target_pairs={{2,0},{3,1},{6,4},{7,5},{8,10},{9,11},{12,14},{13,15},{18,16},{19,... | collective-permute-start | bytes 3145736 | tf_op jit(solution)/shard_map/ppermute | solution.py:314
  314.9 24.1 %collective-permute-start.28 = (bf16[2,2,512,256]{3,2,1,0:T(8,128)(2,1)}, bf16[2,2,512,256]{3,2,1,0:T(8,128)(2,1)}, u32[]{:S(2)}, u32[]{:S(2)}) collective-permute-start(bf16[2,2,512,256]{3,2,1,0:T(8,128)(2,1)} %collective-permute-done.27), channel_id=1, source_target_pairs={{0,2},{1,3},{14,12},{15,13},{16,18},{17,19},{30,28},{31,29}} | collective-permute-start | bytes 3145736 | tf_op jit(solution)/shard_map/ppermute | solution.py:314
  319.0 14.5 %copy-start.18 = (bf16[2,2,512,256]{3,2,1,0:T(8,128)(2,1)S(1)}, bf16[2,2,512,256]{3,2,1,0:T(8,128)(2,1)}, u32[]{:S(2)}) copy-start(bf16[2,2,512,256]{3,2,1,0:T(8,128)(2,1)} %get-tuple-element.61) | copy-start | bytes 3145732
  340.5 5.7 %collective-permute-start.29 = (bf16[2,2,512,256]{3,2,1,0:T(8,128)(2,1)S(1)}, bf16[2,2,512,256]{3,2,1,0:T(8,128)(2,1)S(1)}, u32[]{:S(2)}, u32[]{:S(2)}) collective-permute-start(bf16[2,2,512,256]{3,2,1,0:T(8,128)(2,1)S(1)} %select_convert_fusion), channel_id=1, source_target_pairs={{0,1},{1,0},{2,3},{3,2},{4,5},{5,4},{6,7},{7,6},{8,9},{9,8},{10,11... | collective-permute-start | bytes 3145736 | tf_op jit(solution)/shard_map/ppermute | solution.py:245
  346.2 1.0 copy-start.19
Sparse Core Ops, SparseCore 0:
  16.5 60.7 all-gather.6
  91.4 38.2 all-gather.8
  131.2 34.4 all-gather.10

commit v12 on v8

--- a/solution.py
+++ b/solution.py
@@ -85,17 +85,16 @@
 def second_kernel(pick_ref, own_ref, sib_ref, *refs):
     site_refs, out_ref = refs[:-1], refs[-1]
     phys, _, rows, cols = own_ref.shape[1:]
-    with_real, with_imag = None, None
+    total = None
     for q_ref, quarter in ((own_ref, pick_ref[0]), (sib_ref, 1 - pick_ref[0])):
         piece = pl.ds(pl.multiple_of(quarter * cols, cols), cols)
-        join = lambda t, part: jnp.concatenate([site_ref[t, part, :, piece] for site_ref in site_refs], axis=0)
         for t in range(phys):
-            left = q_ref[0, t].reshape(2 * rows, cols)
-            more_real, more_imag = mul_t(left, join(t, 0)), mul_t(left, join(t, 1))
-            with_real = more_real if with_real is None else with_real + more_real
-            with_imag = more_imag if with_imag is None else with_imag + more_imag
-    out_ref[0, 0] = (with_real[:rows] - with_imag[rows:]).astype(BF16)
-    out_ref[0, 1] = (with_imag[:rows] + with_real[rows:]).astype(BF16)
+            right = [site_ref[t, part, :, piece] for part in range(2) for site_ref in site_refs]
+            more = mul_t(q_ref[0, t].reshape(2 * rows, cols), jnp.concatenate(right, axis=0))
+            total = more if total is None else total + more
+    width = total.shape[1] // 2
+    out_ref[0, 0] = (total[:rows, :width] - total[rows:, width:]).astype(BF16)
+    out_ref[0, 1] = (total[:rows, width:] + total[rows:, :width]).astype(BF16)
 
 
 def second_product(pick, own, sib, sites):
@@ -246,7 +245,7 @@
     half = rows // 2
     mine = lax.dynamic_slice_in_dim(planar, depth * half, half, 2)
     other = turn(mine)
-    other = in_order(other, swap(after(other, envs[4], envs[5])), 2)
+    other = in_order(other, swap(after(other, envs[4])), 2)
     site = jnp.where(col == 0, jnp.stack([planar, other]), jnp.stack([other, planar]))
 
     parts = [mine[:, :, : half // 2], mine[:, :, half // 2 :]]
@@ -255,9 +254,9 @@
         travelling.append([shift(part) for part in travelling[-1]])
 
     blocks = jnp.stack([lax.rem(row - k + row_count, row_count) for k in range(row_count)])
-    blocks = after(blocks.astype(jnp.int32), travelling[0][0])
+    blocks = blocks.astype(jnp.int32)
     q = first_product(blocks, mpo_mine, site, envs, half, half)
-    q_sib = swap(after(q, travelling[0][1]))
+    q_sib = swap(after(q, *travelling[0]))
 
     goals = [
         [((r - step) % row_count // 2, (r - step) % row_count % 2) for r in range(row_count)]

time: 328 us -> 322 us (0.982)
  Pallas kernels: 71.8 us -> 67.2 us
    pallas_call x5, Pallas kernels: 41 us -> 36.8 us  [second_product(): pl.pallas_call(second_kernel, grid=(mpo_count,), in_specs=[pl.BlockSpec(m...]
    unnamed x56 -> x52, local copies, waits for them, and re-layouts: 13.5 us -> 11.4 us
  transfers between devices with their start and end apart: 26 -> 26, of which waited for: 17 -> 18; matrix products, arithmetic and copies ran while one was open for 6% -> 6% of each run, Pallas kernels for 20% -> 19%
where the time goes in v12:
time: 322 us
  waiting for transfers between devices  194 us (60%)
  Pallas kernels  67.2 us (21%)
  starting transfers between devices  26.9 us (8%)
  local copies, waits for them, and re-layouts  18 us (6%)
  other arithmetic  15.1 us (5%)
    ppermute x12, waiting for transfers between devices, ring(): lax.ppermute(value, 'row', [(r, (r + 1) % row_count) for r in range(row_c...  161 us
    pallas_call x5, Pallas kernels, second_product(): pl.pallas_call(second_kernel, grid=(mpo_count,), in_specs=[pl.BlockSpec(m...  36.8 us
    pallas_call x1, Pallas kernels, first_product(): pl.pallas_call(functools.partial(first_kernel, w_local), grid=(rows // ro...  24.6 us
    ppermute x6, waiting for transfers between devices, send(): lax.ppermute(value, axes, [(place(r, 1 - c if turned else c, 1 - d if cro...  16.2 us
    unnamed x52, local copies, waits for them, and re-layouts  11.4 us
    ppermute x3, starting transfers between devices, turn_to_goal(): lax.ppermute(value, axes, [(place(r, 1 - c, d), place(r, c, d)) for r, (c...  8.01 us
    ppermute x6, starting transfers between devices, send(): lax.ppermute(value, axes, [(place(r, 1 - c if turned else c, 1 - d if cro...  7.73 us
    ppermute x4, waiting for transfers between devices, swap(): return lax.ppermute(value, 'depth', [(0, 1), (1, 0)])  7 us
  transfers between devices with their start and end apart: 26, of which 18 were waited for; matrix products, arithmetic and copies ran while one was open for 6% of the time, Pallas kernels for 19%

profile of v12, /device:TPU:1, one launch (start us, length us, event | category | flops | bytes accessed | tf_op | source)
XLA Modules:
  0.0 321.6 jit_solution(14485247130189013205)
XLA Ops:
  0.0 1.7 constant_dynamic-slice_fusion
  1.7 0.1 collective-permute-start
  1.8 2.7 collective-permute-start.2
  4.6 1.0 copy-done.8
  5.6 3.5 %copy.8 = bf16[2,512,2,1024]{3,1,2,0:T(8,128)(2,1)S(1)} copy(bf16[2,512,2,1024]{3,2,1,0:T(2,128)(2,1)} %param.4) | data formatting | bytes 8388608 | tf_op jit(solution)/shard_map/optimization_barrier | solution.py:165
  9.1 0.0 copy-start.1
  9.1 2.0 copy-done.1
  11.2 0.2 dynamic-slice_bitcast_fusion
  11.3 2.3 collective-permute-start.1
  13.6 16.6 %collective-permute-done.2.refs_2_ = bf16[1,2,512,512]{3,2,1,0:T(8,128)(2,1)} collective-permute-done((bf16[1,2,512,512]{3,2,1,0:T(8,128)(2,1)S(1)}, bf16[1,2,512,512]{3,2,1,0:T(8,128)(2,1)}, u32[]{:S(2)}, u32[]{:S(2)}) %collective-permute-start.2) | collective-permute-done | bytes 1048608 | tf_op jit(solution)/shard_map/ppermute | solution.py:228
  30.2 0.5 collective-permute-start.5
  30.7 25.5 %collective-permute-done.3.refs_4_ = bf16[1,2,512,512]{3,2,1,0:T(8,128)(2,1)S(1)} collective-permute-done((bf16[1,2,512,512]{3,2,1,0:T(8,128)(2,1)}, bf16[1,2,512,512]{3,2,1,0:T(8,128)(2,1)S(1)}, u32[]{:S(2)}, u32[]{:S(2)}) %collective-permute-start.3) | collective-permute-done | bytes 1048608 | tf_op jit(solution)/shard_map/ppermute | solution.py:228
  56.2 3.2 collective-permute-done.1
  59.4 0.9 collective-permute-start.4
  60.3 18.5 %collective-permute-done.5.refs_3_ = bf16[1,2,512,512]{3,2,1,0:T(8,128)(2,1)} collective-permute-done((bf16[1,2,512,512]{3,2,1,0:T(8,128)(2,1)S(1)}, bf16[1,2,512,512]{3,2,1,0:T(8,128)(2,1)}, u32[]{:S(2)}, u32[]{:S(2)}) %collective-permute-start.5) | collective-permute-done | bytes 1048608 | tf_op jit(solution)/shard_map/ppermute | solution.py:228
  78.8 1.2 fusion
  80.0 24.0 %collective-permute-done.6.refs_5_ = bf16[1,2,512,512]{3,2,1,0:T(8,128)(2,1)} collective-permute-done((bf16[1,2,512,512]{3,2,1,0:T(8,128)(2,1)}, bf16[1,2,512,512]{3,2,1,0:T(8,128)(2,1)}, u32[]{:S(2)}, u32[]{:S(2)}) %collective-permute-start.6) | collective-permute-done | bytes 1048608 | tf_op jit(solution)/shard_map/ppermute | solution.py:228
  104.1 5.7 %maximum_select_fusion.1 = bf16[1,2,2,512,1024]{4,3,2,1,0:T(8,128)(2,1)S(1)} fusion(bf16[1,2,2,256,1024]{4,3,2,1,0:T(8,128)(2,1)} %bitcast.10, bf16[1,2,2,256,1024]{4,3,2,1,0:T(8,128)(2,1)} %bitcast.9, pred[]{:T(512)S(6)} %eq.24), kind=kLoop, calls=%fused_computation.1 | loop fusion | flops 18874368 | bytes 8388609 | tf_op jit(solution)/shard_map/jit(_where)/select_n | solution.py:232
  109.8 4.0 %maximum_select_fusion.site_ref = bf16[2,2,2,512,1024]{4,3,2,1,0:T(8,128)(2,1)} fusion(bf16[1,2,2,512,1024]{4,3,2,1,0:T(8,128)(2,1)S(1)} %maximum_select_fusion.1, bf16[1,2,2,512,1024]{4,3,2,1,0:T(8,128)(2,1)S(1)} %bitcast.15, pred[]{:T(512)S(6)} %eq.23), kind=kLoop, calls=%fused_computation | loop fusion | flops 12582912 | bytes 16777216 | tf_op jit(solution)/shard_map/jit(_where)/select_n | solution.py:249
  113.8 12.6 %collective-permute-done.7.refs_6_ = bf16[1,2,512,512]{3,2,1,0:T(8,128)(2,1)S(1)} collective-permute-done((bf16[1,2,512,512]{3,2,1,0:T(8,128)(2,1)}, bf16[1,2,512,512]{3,2,1,0:T(8,128)(2,1)S(1)}, u32[]{:S(2)}, u32[]{:S(2)}) %collective-permute-start.7) | collective-permute-done | bytes 1048608 | tf_op jit(solution)/shard_map/ppermute | solution.py:228
  126.4 22.5 %collective-permute-done.8.refs_7_ = bf16[1,2,512,512]{3,2,1,0:T(8,128)(2,1)S(1)} collective-permute-done((bf16[1,2,512,512]{3,2,1,0:T(8,128)(2,1)}, bf16[1,2,512,512]{3,2,1,0:T(8,128)(2,1)S(1)}, u32[]{:S(2)}, u32[]{:S(2)}) %collective-permute-start.8) | collective-permute-done | bytes 1048608 | tf_op jit(solution)/shard_map/ppermute | solution.py:228
  148.9 1.0 copy-done.15
  149.9 0.7 pad_add_fusion.1.block_ref
  150.5 0.6 pad_maximum_fusion.mpo_ref
  151.1 24.6 %first_product.1.own_ref = bf16[2,2,2,512,512]{4,3,2,1,0:T(8,128)(2,1)} custom-call(s32[4]{0:T(128)} %pad_add_fusion.1.block_ref, f32[2,2,2,2]{3,2,1,0:T(2,128)} %pad_maximum_fusion.mpo_ref, bf16[2,2,2,512,1024]{4,3,2,1,0:T(8,128)(2,1)} %maximum_select_fusion.site_ref, bf16[1,2,512,512]{3,2,1,0:T(8,128)(2,1)} %copy-done.3, ...), custom_call_target="tpu_custom_call" | custom-call | tf_op jit(solution)/shard_map/first_product/pallas_call | solution.py:67
  175.7 18.1 %collective-permute-done.10.refs_1_ = bf16[2,2,128,1024]{3,2,1,0:T(8,128)(2,1)S(1)} collective-permute-done((bf16[2,2,128,1024]{3,2,1,0:T(8,128)(2,1)S(1)}, bf16[2,2,128,1024]{3,2,1,0:T(8,128)(2,1)S(1)}, u32[]{:S(2)}, u32[]{:S(2)}) %collective-permute-start.10) | collective-permute-done | bytes 1048608 | tf_op jit(solution)/shard_map/ppermute | solution.py:228
  193.8 2.4 collective-permute-start.11
  196.3 7.0 %collective-permute-done.11.sib_ref = bf16[2,2,2,512,512]{4,3,2,1,0:T(8,128)(2,1)S(1)} collective-permute-done((bf16[2,2,2,512,512]{4,3,2,1,0:T(8,128)(2,1)}, bf16[2,2,2,512,512]{4,3,2,1,0:T(8,128)(2,1)S(1)}, u32[]{:S(2)}, u32[]{:S(2)}) %collective-permute-start.11) | collective-permute-done | bytes 4194336 | tf_op jit(solution)/shard_map/ppermute | solution.py:169
  203.3 2.0 copy-done
  205.2 8.4 %second_product.5 = bf16[2,2,512,256]{3,2,1,0:T(8,128)(2,1)} custom-call(s32[1]{0:T(128)} %bitcast.1.pick_ref, bf16[2,2,2,512,512]{4,3,2,1,0:T(8,128)(2,1)} %first_product.1.own_ref, bf16[2,2,2,512,512]{4,3,2,1,0:T(8,128)(2,1)} %copy-done, bf16[2,2,128,1024]{3,2,1,0:T(8,128)(2,1)} %get-tuple-element.16.refs_0_, bf16[2,2,128,1024]{3,2,1,0:T(8,128)(2,1)} %copy-done.7), custom_call_target="tpu_custom_call" | custom-call | tf_op jit(solution)/shard_map/second_product/pallas_call | solution.py:104
  213.6 1.3 collective-permute-start.12
  214.9 0.1 collective-permute-start.15
  215.0 8.0 %collective-permute-done.13.refs_0_ = bf16[2,2,128,1024]{3,2,1,0:T(8,128)(2,1)} collective-permute-done((bf16[2,2,128,1024]{3,2,1,0:T(8,128)(2,1)S(1)}, bf16[2,2,128,1024]{3,2,1,0:T(8,128)(2,1)}, u32[]{:S(2)}, u32[]{:S(2)}) %collective-permute-start.13) | collective-permute-done | bytes 1048608 | tf_op jit(solution)/shard_map/ppermute | solution.py:228
  223.0 8.4 %second_product.6 = bf16[2,2,512,256]{3,2,1,0:T(8,128)(2,1)} custom-call(s32[1]{0:T(128)} %bitcast.1.pick_ref, bf16[2,2,2,512,512]{4,3,2,1,0:T(8,128)(2,1)} %first_product.1.own_ref, bf16[2,2,2,512,512]{4,3,2,1,0:T(8,128)(2,1)} %copy-done, bf16[2,2,128,1024]{3,2,1,0:T(8,128)(2,1)} %copy-done.11, bf16[2,2,128,1024]{3,2,1,0:T(8,128)(2,1)} %copy-done.12), custom_call_target="tpu_custom_call" | custom-call | tf_op jit(solution)/shard_map/second_product/pallas_call | solution.py:104
  231.4 3.9 %collective-permute-start.14 = (bf16[2,2,512,256]{3,2,1,0:T(8,128)(2,1)}, bf16[2,2,512,256]{3,2,1,0:T(8,128)(2,1)}, u32[]{:S(2)}, u32[]{:S(2)}) collective-permute-start(bf16[2,2,512,256]{3,2,1,0:T(8,128)(2,1)} %second_product.6), channel_id=1, source_target_pairs={{0,2},{1,3},{6,4},{7,5},{10,8},{11,9},{12,14},{13,15},{16,18},{17,... | collective-permute-start | bytes 3145736 | tf_op jit(solution)/shard_map/ppermute | solution.py:271
  235.2 4.9 %collective-permute-done.12 = bf16[2,2,512,256]{3,2,1,0:T(8,128)(2,1)S(1)} collective-permute-done((bf16[2,2,512,256]{3,2,1,0:T(8,128)(2,1)}, bf16[2,2,512,256]{3,2,1,0:T(8,128)(2,1)S(1)}, u32[]{:S(2)}, u32[]{:S(2)}) %collective-permute-start.12) | collective-permute-done | bytes 1048608 | tf_op jit(solution)/shard_map/ppermute | solution.py:271
  240.1 5.2 %collective-permute-done.15.refs_1_ = bf16[2,2,128,1024]{3,2,1,0:T(8,128)(2,1)S(1)} collective-permute-done((bf16[2,2,128,1024]{3,2,1,0:T(8,128)(2,1)S(1)}, bf16[2,2,128,1024]{3,2,1,0:T(8,128)(2,1)S(1)}, u32[]{:S(2)}, u32[]{:S(2)}) %collective-permute-start.15) | collective-permute-done | bytes 1048608 | tf_op jit(solution)/shard_map/ppermute | solution.py:228
  245.3 1.0 copy-done.13
  246.3 8.4 %second_product.7 = bf16[2,2,512,256]{3,2,1,0:T(8,128)(2,1)} custom-call(s32[1]{0:T(128)} %bitcast.1.pick_ref, bf16[2,2,2,512,512]{4,3,2,1,0:T(8,128)(2,1)} %first_product.1.own_ref, bf16[2,2,2,512,512]{4,3,2,1,0:T(8,128)(2,1)} %copy-done, bf16[2,2,128,1024]{3,2,1,0:T(8,128)(2,1)} %collective-permute-done.13.refs_0_, bf16[2,2,128,1024]{3,2,1,0:T(8,128)(2,1)} %copy-done.13), custom_call_target="tpu_custom_call" | custom-call | tf_op jit(solution)/shard_map/second_product/pallas_call | solution.py:104
  254.7 2.9 collective-permute-start.16
  257.6 0.1 collective-permute-start.22
  257.7 10.2 %collective-permute-done.18.refs_0_ = bf16[2,2,128,1024]{3,2,1,0:T(8,128)(2,1)} collective-permute-done((bf16[2,2,128,1024]{3,2,1,0:T(8,128)(2,1)}, bf16[2,2,128,1024]{3,2,1,0:T(8,128)(2,1)}, u32[]{:S(2)}, u32[]{:S(2)}) %collective-permute-start.18) | collective-permute-done | bytes 1048608 | tf_op jit(solution)/shard_map/ppermute | solution.py:228
  267.9 5.8 %second_product.8.refs_0_ = bf16[2,2,512,128]{3,2,1,0:T(8,128)(2,1)} custom-call(s32[1]{0:T(128)} %bitcast.1.pick_ref, bf16[2,2,2,512,512]{4,3,2,1,0:T(8,128)(2,1)} %first_product.1.own_ref, bf16[2,2,2,512,512]{4,3,2,1,0:T(8,128)(2,1)} %copy-done, bf16[2,2,128,1024]{3,2,1,0:T(8,128)(2,1)} %collective-permute-done.18.refs_0_), custom_call_target="tpu_custom_call" | custom-call | tf_op jit(solution)/shard_map/second_product/pallas_call | solution.py:104
  273.7 1.3 collective-permute-start.19
  275.0 1.3 collective-permute-start.20
  276.3 1.3 collective-permute-start.21
  277.6 1.5 collective-permute-done.16
  279.1 3.6 %select_convert_fusion = (bf16[2,2,512,256]{3,2,1,0:T(8,128)(2,1)S(1)}, f32[2,2,512,256]{3,2,1,0:T(8,128)}) fusion(bf16[2,2,512,256]{3,2,1,0:T(8,128)(2,1)S(1)} %copy-done.17, bf16[2,2,512,256]{3,2,1,0:T(8,128)(2,1)S(1)} %copy-done.4, bf16[2,2,512,256]{3,2,1,0:T(8,128)(2,1)} %collective-permute-done.14, bf16[2,2,512,256]{3,2,1,0:T(8,128)(2,1)S(1)} %copy-done.5, ...), kind=kLoop, calls=%fused_computation.2 | loop fusion | flops 7340032 | bytes 9437188 | tf_op jit(solution)/shard_map/convert_element_type | solution.py:305
  282.7 2.1 collective-permute-start.17
  284.8 3.0 collective-permute-done.19.refs_1_
  287.8 1.9 collective-permute-done.20.refs_2_
  289.7 0.8 copy-done.21
  290.6 0.8 copy-done.22
  291.4 1.0 copy-done.18
  292.4 5.8 %second_product.9.refs_4_ = bf16[2,2,512,128]{3,2,1,0:T(8,128)(2,1)} custom-call(s32[1]{0:T(128)} %bitcast.1.pick_ref, bf16[2,2,2,512,512]{4,3,2,1,0:T(8,128)(2,1)} %first_product.1.own_ref, bf16[2,2,2,512,512]{4,3,2,1,0:T(8,128)(2,1)} %copy-done, bf16[2,2,128,1024]{3,2,1,0:T(8,128)(2,1)} %copy-done.18), custom_call_target="tpu_custom_call" | custom-call | tf_op jit(solution)/shard_map/second_product/pallas_call | solution.py:104
  298.1 1.3 collective-permute-start.23
  299.4 1.3 collective-permute-start.24
  300.7 1.3 collective-permute-start.25
  302.0 0.6 pad_add_fusion.pick_ref
  302.7 9.3 %collective-permute-done.23.refs_5_ = bf16[2,2,512,128]{3,2,1,0:T(8,128)(2,1)S(1)} collective-permute-done((bf16[2,2,512,128]{3,2,1,0:T(8,128)(2,1)}, bf16[2,2,512,128]{3,2,1,0:T(8,128)(2,1)S(1)}, u32[]{:S(2)}, u32[]{:S(2)}) %collective-permute-start.23) | collective-permute-done | bytes 524320 | tf_op jit(solution)/shard_map/ppermute | solution.py:278
  311.9 1.9 collective-permute-done.24.refs_6_
  313.9 0.8 copy-done.24
  314.7 1.0 copy-done.19
  315.7 5.8 %finish.1 = f32[2,2,512,512]{3,2,1,0:T(8,128)} custom-call(s32[2]{0:T(128)} %pad_add_fusion.pick_ref, f32[2,2,512,256]{3,2,1,0:T(8,128)} %get-tuple-element.24.mine_ref, bf16[2,2,512,256]{3,2,1,0:T(8,128)(2,1)} %copy-done.19, bf16[2,2,512,128]{3,2,1,0:T(8,128)(2,1)} %second_product.8.refs_0_, bf16[2,2,512,128]{3,2,1,0:T(8,128)(2,1)} %copy-done.20, ...), custom_call_target="tpu_custom_call" | custom-call | tf_op jit(solution)/shard_map/finish/pallas_call | solution.py:149
  (58 shorter events, 0.1 us)
Async XLA Ops:
  1.7 7.4 %copy-start.3 = (bf16[1,2,512,512]{3,2,1,0:T(8,128)(2,1)}, bf16[1,2,512,512]{3,2,1,0:T(8,128)(2,1)S(1)}, u32[]{:S(2)}) copy-start(bf16[1,2,512,512]{3,2,1,0:T(8,128)(2,1)S(1)} %get-tuple-element.29.refs_0_) | copy-start | bytes 3145732
  1.7 2.9 collective-permute-start
  1.8 28.3 %collective-permute-start.2 = (bf16[1,2,512,512]{3,2,1,0:T(8,128)(2,1)S(1)}, bf16[1,2,512,512]{3,2,1,0:T(8,128)(2,1)}, u32[]{:S(2)}, u32[]{:S(2)}) collective-permute-start(bf16[1,2,512,512]{3,2,1,0:T(8,128)(2,1)S(1)} %get-tuple-element.29.refs_0_), channel_id=1, source_target_pairs={{0,4},{4,8},{8,12},{12,0},{1,5},{5,9},{9,13},{13,1},{2,6},{6,10},{... | collective-permute-start | bytes 3145736 | tf_op jit(solution)/shard_map/ppermute | solution.py:228
  4.6 1.0 copy-start.8
  9.1 2.0 copy-start.1
  11.1 19.0 %copy-start.9 = (bf16[1,2,512,512]{3,2,1,0:T(8,128)(2,1)S(1)}, bf16[1,2,512,512]{3,2,1,0:T(8,128)(2,1)}, u32[]{:S(2)}) copy-start(bf16[1,2,512,512]{3,2,1,0:T(8,128)(2,1)} %copy-done.8) | copy-start | bytes 3145732
  11.3 48.1 %collective-permute-start.1 = (bf16[2,2,256,1024]{3,2,1,0:T(8,128)(2,1)S(1)}, bf16[2,2,256,1024]{3,2,1,0:T(8,128)(2,1)}, u32[]{:S(2)}, u32[]{:S(2)}) collective-permute-start(bf16[2,2,256,1024]{3,2,1,0:T(8,128)(2,1)S(1)} %dynamic-slice_bitcast_fusion), channel_id=1, source_target_pairs={{0,2},{2,0},{1,3},{3,1},{4,6},{6,4},{5,7},{7,5},{8,10},{10,8},{9,1... | collective-permute-start | bytes 6291464 | tf_op jit(solution)/shard_map/ppermute | solution.py:231
  30.2 26.1 %collective-permute-start.3 = (bf16[1,2,512,512]{3,2,1,0:T(8,128)(2,1)}, bf16[1,2,512,512]{3,2,1,0:T(8,128)(2,1)S(1)}, u32[]{:S(2)}, u32[]{:S(2)}) collective-permute-start(bf16[1,2,512,512]{3,2,1,0:T(8,128)(2,1)} %collective-permute-done.2.refs_2_), channel_id=1, source_target_pairs={{0,4},{4,8},{8,12},{12,0},{1,5},{5,9},{9,13},{13,1},{2,6},{6,10},{... | collective-permute-start | bytes 3145736 | tf_op jit(solution)/shard_map/ppermute | solution.py:228
  30.2 48.6 %collective-permute-start.5 = (bf16[1,2,512,512]{3,2,1,0:T(8,128)(2,1)S(1)}, bf16[1,2,512,512]{3,2,1,0:T(8,128)(2,1)}, u32[]{:S(2)}, u32[]{:S(2)}) collective-permute-start(bf16[1,2,512,512]{3,2,1,0:T(8,128)(2,1)S(1)} %copy-done.9), channel_id=1, source_target_pairs={{0,4},{4,8},{8,12},{12,0},{1,5},{5,9},{9,13},{13,1},{2,6},{6,10},{... | collective-permute-start | bytes 3145736 | tf_op jit(solution)/shard_map/ppermute | solution.py:228
  56.2 22.6 %copy-start.10 = (bf16[1,2,512,512]{3,2,1,0:T(8,128)(2,1)}, bf16[1,2,512,512]{3,2,1,0:T(8,128)(2,1)S(1)}, u32[]{:S(2)}) copy-start(bf16[1,2,512,512]{3,2,1,0:T(8,128)(2,1)S(1)} %collective-permute-done.3.refs_4_) | copy-start | bytes 3145732
  59.4 44.7 %collective-permute-start.4 = (bf16[2,2,256,1024]{3,2,1,0:T(8,128)(2,1)}, bf16[2,2,256,1024]{3,2,1,0:T(8,128)(2,1)}, u32[]{:S(2)}, u32[]{:S(2)}) collective-permute-start(bf16[2,2,256,1024]{3,2,1,0:T(8,128)(2,1)} %collective-permute-done.1), channel_id=1, source_target_pairs={{0,1},{1,0},{2,3},{3,2},{4,5},{5,4},{6,7},{7,6},{8,9},{9,8},{10,11... | collective-permute-start | bytes 6291464 | tf_op jit(solution)/shard_map/ppermute | solution.py:169
  78.8 25.3 %collective-permute-start.6 = (bf16[1,2,512,512]{3,2,1,0:T(8,128)(2,1)}, bf16[1,2,512,512]{3,2,1,0:T(8,128)(2,1)}, u32[]{:S(2)}, u32[]{:S(2)}) collective-permute-start(bf16[1,2,512,512]{3,2,1,0:T(8,128)(2,1)} %collective-permute-done.5.refs_3_), channel_id=1, source_target_pairs={{0,4},{4,8},{8,12},{12,0},{1,5},{5,9},{9,13},{13,1},{2,6},{6,10},{... | collective-permute-start | bytes 3145736 | tf_op jit(solution)/shard_map/ppermute | solution.py:228
  80.0 69.9 %copy-start.7 = (bf16[2,2,128,1024]{3,2,1,0:T(8,128)(2,1)}, bf16[2,2,128,1024]{3,2,1,0:T(8,128)(2,1)S(1)}, u32[]{:S(2)}) copy-start(bf16[2,2,128,1024]{3,2,1,0:T(8,128)(2,1)S(1)} %get-tuple-element.17.refs_1_) | copy-start | bytes 3145732
  80.0 46.4 %collective-permute-start.7 = (bf16[1,2,512,512]{3,2,1,0:T(8,128)(2,1)}, bf16[1,2,512,512]{3,2,1,0:T(8,128)(2,1)S(1)}, u32[]{:S(2)}, u32[]{:S(2)}) collective-permute-start(bf16[1,2,512,512]{3,2,1,0:T(8,128)(2,1)} %copy-done.10), channel_id=1, source_target_pairs={{0,4},{4,8},{8,12},{12,0},{1,5},{5,9},{9,13},{13,1},{2,6},{6,10},{... | collective-permute-start | bytes 3145736 | tf_op jit(solution)/shard_map/ppermute | solution.py:228
  104.1 44.8 %collective-permute-start.8 = (bf16[1,2,512,512]{3,2,1,0:T(8,128)(2,1)}, bf16[1,2,512,512]{3,2,1,0:T(8,128)(2,1)S(1)}, u32[]{:S(2)}, u32[]{:S(2)}) collective-permute-start(bf16[1,2,512,512]{3,2,1,0:T(8,128)(2,1)} %collective-permute-done.6.refs_5_), channel_id=1, source_target_pairs={{0,4},{4,8},{8,12},{12,0},{1,5},{5,9},{9,13},{13,1},{2,6},{6,10},{... | collective-permute-start | bytes 3145736 | tf_op jit(solution)/shard_map/ppermute | solution.py:228
  104.1 5.7 %copy-start.2 = (bf16[2,512,2,1024]{3,1,2,0:T(8,128)(2,1)S(1)}, bf16[2,512,2,1024]{3,1,2,0:T(8,128)(2,1)}, u32[]{:S(2)}) copy-start(bf16[2,512,2,1024]{3,1,2,0:T(8,128)(2,1)} %copy-done.1) | copy-start | bytes 12582916
  109.7 40.8 %copy-start.25 = (f32[2,2,2,2]{3,2,1,0:T(2,128)S(1)}, f32[2,2,2,2]{3,2,1,0:T(2,128)}, u32[]{:S(2)}) copy-start(f32[2,2,2,2]{3,2,1,0:T(2,128)} %param.5) | copy-start | bytes 196
  126.4 22.5 %copy-start.14 = (bf16[1,2,512,512]{3,2,1,0:T(8,128)(2,1)}, bf16[1,2,512,512]{3,2,1,0:T(8,128)(2,1)S(1)}, u32[]{:S(2)}) copy-start(bf16[1,2,512,512]{3,2,1,0:T(8,128)(2,1)S(1)} %collective-permute-done.7.refs_6_) | copy-start | bytes 3145732
  126.4 49.3 %collective-permute-start.9 = (bf16[2,2,128,1024]{3,2,1,0:T(8,128)(2,1)}, bf16[2,2,128,1024]{3,2,1,0:T(8,128)(2,1)S(1)}, u32[]{:S(2)}, u32[]{:S(2)}) collective-permute-start(bf16[2,2,128,1024]{3,2,1,0:T(8,128)(2,1)} %get-tuple-element.16.refs_0_), channel_id=1, source_target_pairs={{0,4},{4,8},{8,12},{12,0},{1,5},{5,9},{9,13},{13,1},{2,6},{6,10},{... | collective-permute-start | bytes 3145736 | tf_op jit(solution)/shard_map/ppermute | solution.py:228
  148.9 1.0 copy-start.15
  149.9 44.0 %collective-permute-start.10 = (bf16[2,2,128,1024]{3,2,1,0:T(8,128)(2,1)S(1)}, bf16[2,2,128,1024]{3,2,1,0:T(8,128)(2,1)S(1)}, u32[]{:S(2)}, u32[]{:S(2)}) collective-permute-start(bf16[2,2,128,1024]{3,2,1,0:T(8,128)(2,1)S(1)} %get-tuple-element.17.refs_1_), channel_id=1, source_target_pairs={{0,4},{4,8},{8,12},{12,0},{1,5},{5,9},{9,13},{13,1},{2,6},{6,10},{... | collective-permute-start | bytes 3145736 | tf_op jit(solution)/shard_map/ppermute | solution.py:228
  175.7 47.2 %copy-start.11 = (bf16[2,2,128,1024]{3,2,1,0:T(8,128)(2,1)}, bf16[2,2,128,1024]{3,2,1,0:T(8,128)(2,1)S(1)}, u32[]{:S(2)}) copy-start(bf16[2,2,128,1024]{3,2,1,0:T(8,128)(2,1)S(1)} %collective-permute-done.9.refs_0_) | copy-start | bytes 3145732
  193.8 29.1 %copy-start.12 = (bf16[2,2,128,1024]{3,2,1,0:T(8,128)(2,1)}, bf16[2,2,128,1024]{3,2,1,0:T(8,128)(2,1)S(1)}, u32[]{:S(2)}) copy-start(bf16[2,2,128,1024]{3,2,1,0:T(8,128)(2,1)S(1)} %collective-permute-done.10.refs_1_) | copy-start | bytes 3145732
  193.8 9.4 %collective-permute-start.11 = (bf16[2,2,2,512,512]{4,3,2,1,0:T(8,128)(2,1)}, bf16[2,2,2,512,512]{4,3,2,1,0:T(8,128)(2,1)S(1)}, u32[]{:S(2)}, u32[]{:S(2)}) collective-permute-start(bf16[2,2,2,512,512]{4,3,2,1,0:T(8,128)(2,1)} %first_product.1.own_ref), channel_id=1, source_target_pairs={{0,1},{1,0},{2,3},{3,2},{4,5},{5,4},{6,7},{7,6},{8,9},{9,8},{10,11... | collective-permute-start | bytes 12582920 | tf_op jit(solution)/shard_map/ppermute | solution.py:169
  196.3 26.7 %collective-permute-start.13 = (bf16[2,2,128,1024]{3,2,1,0:T(8,128)(2,1)S(1)}, bf16[2,2,128,1024]{3,2,1,0:T(8,128)(2,1)}, u32[]{:S(2)}, u32[]{:S(2)}) collective-permute-start(bf16[2,2,128,1024]{3,2,1,0:T(8,128)(2,1)S(1)} %collective-permute-done.9.refs_0_), channel_id=1, source_target_pairs={{0,4},{4,8},{8,12},{12,0},{1,5},{5,9},{9,13},{13,1},{2,6},{6,10},{... | collective-permute-start | bytes 3145736 | tf_op jit(solution)/shard_map/ppermute | solution.py:228
  203.3 2.0 copy-start
  213.6 26.5 %collective-permute-start.12 = (bf16[2,2,512,256]{3,2,1,0:T(8,128)(2,1)}, bf16[2,2,512,256]{3,2,1,0:T(8,128)(2,1)S(1)}, u32[]{:S(2)}, u32[]{:S(2)}) collective-permute-start(bf16[2,2,512,256]{3,2,1,0:T(8,128)(2,1)} %second_product.5), channel_id=1, source_target_pairs={{2,0},{3,1},{6,4},{7,5},{8,10},{9,11},{12,14},{13,15},{18,16},{19,... | collective-permute-start | bytes 3145736 | tf_op jit(solution)/shard_map/ppermute | solution.py:271
  214.9 30.4 %collective-permute-start.15 = (bf16[2,2,128,1024]{3,2,1,0:T(8,128)(2,1)S(1)}, bf16[2,2,128,1024]{3,2,1,0:T(8,128)(2,1)S(1)}, u32[]{:S(2)}, u32[]{:S(2)}) collective-permute-start(bf16[2,2,128,1024]{3,2,1,0:T(8,128)(2,1)S(1)} %collective-permute-done.10.refs_1_), channel_id=1, source_target_pairs={{0,4},{4,8},{8,12},{12,0},{1,5},{5,9},{9,13},{13,1},{2,6},{6,10},{... | collective-permute-start | bytes 3145736 | tf_op jit(solution)/shard_map/ppermute | solution.py:228
  223.0 44.9 %collective-permute-start.18 = (bf16[2,2,128,1024]{3,2,1,0:T(8,128)(2,1)}, bf16[2,2,128,1024]{3,2,1,0:T(8,128)(2,1)}, u32[]{:S(2)}, u32[]{:S(2)}) collective-permute-start(bf16[2,2,128,1024]{3,2,1,0:T(8,128)(2,1)} %collective-permute-done.13.refs_0_), channel_id=1, source_target_pairs={{0,4},{4,8},{8,12},{12,0},{1,5},{5,9},{9,13},{13,1},{2,6},{6,10},{... | collective-permute-start | bytes 3145736 | tf_op jit(solution)/shard_map/ppermute | solution.py:228
  231.4 44.9 %collective-permute-start.14 = (bf16[2,2,512,256]{3,2,1,0:T(8,128)(2,1)}, bf16[2,2,512,256]{3,2,1,0:T(8,128)(2,1)}, u32[]{:S(2)}, u32[]{:S(2)}) collective-permute-start(bf16[2,2,512,256]{3,2,1,0:T(8,128)(2,1)} %second_product.6), channel_id=1, source_target_pairs={{0,2},{1,3},{6,4},{7,5},{10,8},{11,9},{12,14},{13,15},{16,18},{17,... | collective-permute-start | bytes 3145736 | tf_op jit(solution)/shard_map/ppermute | solution.py:271
  240.1 14.6 %copy-start.16 = (bf16[2,2,512,256]{3,2,1,0:T(8,128)(2,1)}, bf16[2,2,512,256]{3,2,1,0:T(8,128)(2,1)S(1)}, u32[]{:S(2)}) copy-start(bf16[2,2,512,256]{3,2,1,0:T(8,128)(2,1)S(1)} %collective-permute-done.12) | copy-start | bytes 3145732
  245.3 1.0 copy-start.13
  254.7 24.4 %collective-permute-start.16 = (bf16[2,2,512,256]{3,2,1,0:T(8,128)(2,1)}, bf16[2,2,512,256]{3,2,1,0:T(8,128)(2,1)S(1)}, u32[]{:S(2)}, u32[]{:S(2)}) collective-permute-start(bf16[2,2,512,256]{3,2,1,0:T(8,128)(2,1)} %second_product.7), channel_id=1, source_target_pairs={{0,2},{1,3},{4,6},{5,7},{10,8},{11,9},{14,12},{15,13},{16,18},{17,... | collective-permute-start | bytes 3145736 | tf_op jit(solution)/shard_map/ppermute | solution.py:271
  257.6 33.8 %collective-permute-start.22 = (bf16[2,2,128,1024]{3,2,1,0:T(8,128)(2,1)}, bf16[2,2,128,1024]{3,2,1,0:T(8,128)(2,1)S(1)}, u32[]{:S(2)}, u32[]{:S(2)}) collective-permute-start(bf16[2,2,128,1024]{3,2,1,0:T(8,128)(2,1)} %copy-done.13), channel_id=1, source_target_pairs={{0,4},{4,8},{8,12},{12,0},{1,5},{5,9},{9,13},{13,1},{2,6},{6,10},{... | collective-permute-start | bytes 3145736 | tf_op jit(solution)/shard_map/ppermute | solution.py:228
  257.7 21.4 %copy-start.4 = (bf16[2,2,512,256]{3,2,1,0:T(8,128)(2,1)S(1)}, bf16[2,2,512,256]{3,2,1,0:T(8,128)(2,1)}, u32[]{:S(2)}) copy-start(bf16[2,2,512,256]{3,2,1,0:T(8,128)(2,1)} %second_product.5) | copy-start | bytes 3145732
  257.7 21.4 %copy-start.5 = (bf16[2,2,512,256]{3,2,1,0:T(8,128)(2,1)S(1)}, bf16[2,2,512,256]{3,2,1,0:T(8,128)(2,1)}, u32[]{:S(2)}) copy-start(bf16[2,2,512,256]{3,2,1,0:T(8,128)(2,1)} %second_product.6) | copy-start | bytes 3145732
  257.7 21.4 %copy-start.6 = (bf16[2,2,512,256]{3,2,1,0:T(8,128)(2,1)S(1)}, bf16[2,2,512,256]{3,2,1,0:T(8,128)(2,1)}, u32[]{:S(2)}) copy-start(bf16[2,2,512,256]{3,2,1,0:T(8,128)(2,1)} %second_product.7) | copy-start | bytes 3145732
  257.7 21.4 %copy-start.17 = (bf16[2,2,512,256]{3,2,1,0:T(8,128)(2,1)S(1)}, bf16[2,2,512,256]{3,2,1,0:T(8,128)(2,1)}, u32[]{:S(2)}) copy-start(bf16[2,2,512,256]{3,2,1,0:T(8,128)(2,1)} %copy-done.16) | copy-start | bytes 3145732
  273.7 14.1 %collective-permute-start.19 = (bf16[2,2,512,128]{3,2,1,0:T(8,128)(2,1)}, bf16[2,2,512,128]{3,2,1,0:T(8,128)(2,1)S(1)}, u32[]{:S(2)}, u32[]{:S(2)}) collective-permute-start(bf16[2,2,512,128]{3,2,1,0:T(8,128)(2,1)} %second_product.8.refs_0_), channel_id=1, source_target_pairs={{3,1},{4,6},{9,11},{14,12},{19,17},{20,22},{25,27},{30,28}} | collective-permute-start | bytes 1572872 | tf_op jit(solution)/shard_map/ppermute | solution.py:278
  275.0 14.7 %collective-permute-start.20 = (bf16[2,2,512,128]{3,2,1,0:T(8,128)(2,1)}, bf16[2,2,512,128]{3,2,1,0:T(8,128)(2,1)S(1)}, u32[]{:S(2)}, u32[]{:S(2)}) collective-permute-start(bf16[2,2,512,128]{3,2,1,0:T(8,128)(2,1)} %second_product.8.refs_0_), channel_id=1, source_target_pairs={{2,1},{5,6},{8,11},{15,12},{18,17},{21,22},{24,27},{31,28}} | collective-permute-start | bytes 1572872 | tf_op jit(solution)/shard_map/ppermute | solution.py:278
  276.3 13.4 %collective-permute-start.21 = (bf16[2,2,512,128]{3,2,1,0:T(8,128)(2,1)}, bf16[2,2,512,128]{3,2,1,0:T(8,128)(2,1)S(1)}, u32[]{:S(2)}, u32[]{:S(2)}) collective-permute-start(bf16[2,2,512,128]{3,2,1,0:T(8,128)(2,1)} %second_product.8.refs_0_), channel_id=1, source_target_pairs={{0,1},{7,6},{10,11},{13,12},{16,17},{23,22},{26,27},{29,28}} | collective-permute-start | bytes 1572872 | tf_op jit(solution)/shard_map/ppermute | solution.py:278
  282.7 31.2 %collective-permute-start.17 = (bf16[2,2,512,256]{3,2,1,0:T(8,128)(2,1)S(1)}, bf16[2,2,512,256]{3,2,1,0:T(8,128)(2,1)S(1)}, u32[]{:S(2)}, u32[]{:S(2)}) collective-permute-start(bf16[2,2,512,256]{3,2,1,0:T(8,128)(2,1)S(1)} %get-tuple-element.23), channel_id=1, source_target_pairs={{0,1},{1,0},{2,3},{3,2},{4,5},{5,4},{6,7},{7,6},{8,9},{9,8},{10,11... | collective-permute-start | bytes 3145736 | tf_op jit(solution)/shard_map/ppermute | solution.py:169
  287.8 10.4 %copy-start.20 = (bf16[2,2,512,128]{3,2,1,0:T(8,128)(2,1)}, bf16[2,2,512,128]{3,2,1,0:T(8,128)(2,1)S(1)}, u32[]{:S(2)}) copy-start(bf16[2,2,512,128]{3,2,1,0:T(8,128)(2,1)S(1)} %collective-permute-done.19.refs_1_) | copy-start | bytes 1572868
  289.7 0.9 copy-start.21
  290.6 0.8 copy-start.22
  291.4 1.0 copy-start.18
  298.1 13.8 %collective-permute-start.23 = (bf16[2,2,512,128]{3,2,1,0:T(8,128)(2,1)}, bf16[2,2,512,128]{3,2,1,0:T(8,128)(2,1)S(1)}, u32[]{:S(2)}, u32[]{:S(2)}) collective-permute-start(bf16[2,2,512,128]{3,2,1,0:T(8,128)(2,1)} %second_product.9.refs_4_), channel_id=1, source_target_pairs={{3,1},{4,6},{9,11},{14,12},{19,17},{20,22},{25,27},{30,28}} | collective-permute-start | bytes 1572872 | tf_op jit(solution)/shard_map/ppermute | solution.py:278
  299.4 14.5 %collective-permute-start.24 = (bf16[2,2,512,128]{3,2,1,0:T(8,128)(2,1)}, bf16[2,2,512,128]{3,2,1,0:T(8,128)(2,1)S(1)}, u32[]{:S(2)}, u32[]{:S(2)}) collective-permute-start(bf16[2,2,512,128]{3,2,1,0:T(8,128)(2,1)} %second_product.9.refs_4_), channel_id=1, source_target_pairs={{2,1},{5,6},{8,11},{15,12},{18,17},{21,22},{24,27},{31,28}} | collective-permute-start | bytes 1572872 | tf_op jit(solution)/shard_map/ppermute | solution.py:278
  300.7 13.2 %collective-permute-start.25 = (bf16[2,2,512,128]{3,2,1,0:T(8,128)(2,1)}, bf16[2,2,512,128]{3,2,1,0:T(8,128)(2,1)}, u32[]{:S(2)}, u32[]{:S(2)}) collective-permute-start(bf16[2,2,512,128]{3,2,1,0:T(8,128)(2,1)} %second_product.9.refs_4_), channel_id=1, source_target_pairs={{0,1},{7,6},{10,11},{13,12},{16,17},{23,22},{26,27},{29,28}} | collective-permute-start | bytes 1572872 | tf_op jit(solution)/shard_map/ppermute | solution.py:278
  311.9 2.0 copy-start.23
  313.9 0.8 copy-start.24
  314.7 1.0 copy-start.19

commit v13 on v12

--- a/solution.py
+++ b/solution.py
@@ -8,7 +8,7 @@
 
 F32 = jnp.float32
 BF16 = jnp.bfloat16
-VMEM_BYTES = 56 * 1024 * 1024
+VMEM_BYTES = 64 * 1024 * 1024
 LIGHT = pl.CostEstimate(flops=0, bytes_accessed=0, transcendentals=0)
 
 
@@ -116,7 +116,6 @@
 
 def finish_kernel(pick_ref, mine_ref, siblings_ref, *refs):
     out_ref = refs[-1]
-    parts = [refs[at : at + 4] for at in range(0, len(refs) - 1, 4)]
     half = mine_ref.shape[3]
     halves = [pl.multiple_of(core * half, half) for core in (pick_ref[1], 1 - pick_ref[1])]
 
@@ -128,15 +127,12 @@
     @pl.when(pick_ref[0] != 0)
     def _():
         for side, first in enumerate(halves):
-            for number, part in enumerate(parts):
-                one, two = part[2 * side : 2 * side + 2]
-                width = one.shape[3]
-                place = pl.ds(pl.multiple_of(first + number * width, width), width)
-                out_ref[0, 0, :, place] = one[0, 0].astype(F32) + two[0, 0].astype(F32)
-
-
-def finish(pick, mine, siblings, parts):
-    addends = [value for part in parts for value in part]
+            one, two = refs[2 * side : 2 * side + 2]
+            place = pl.ds(first, one.shape[3])
+            out_ref[0, 0, :, place] = one[0, 0].astype(F32) + two[0, 0].astype(F32)
+
+
+def finish(pick, mine, siblings, part):
     mpo_count, _, rows, half = mine.shape
 
     def spec(value, used):
@@ -151,14 +147,59 @@
         grid_spec=pltpu.PrefetchScalarGridSpec(
             num_scalar_prefetch=1,
             grid=(mpo_count, 2),
-            in_specs=[spec(mine, 0), spec(siblings, 0)] + [spec(value, 1) for value in addends],
+            in_specs=[spec(mine, 0), spec(siblings, 0)] + [spec(value, 1) for value in part],
             out_specs=pl.BlockSpec((1, 1, rows, 2 * half), lambda v, p, pick: (v, p, 0, 0)),
         ),
         out_shape=jax.ShapeDtypeStruct((mpo_count, 2, rows, 2 * half), F32),
         compiler_params=params(2),
         cost_estimate=LIGHT,
         name="finish",
-    )(pick, mine, siblings, *addends)
+    )(pick, mine, siblings, *part)
+
+
+def finish_last_kernel(pick_ref, *refs):
+    part, (_, out_ref, sum_ref, sems) = refs[:4], refs[4:]
+    mpo_count, _, _, width = part[0].shape
+    half = out_ref.shape[3] // 2
+
+    @pl.when(pick_ref[0] != 0)
+    def _():
+        copies = []
+        for v in range(mpo_count):
+            for p in range(2):
+                for side, core in enumerate((pick_ref[1], 1 - pick_ref[1])):
+                    one, two = part[2 * side : 2 * side + 2]
+                    sum_ref[side, v, p] = one[v, p].astype(F32) + two[v, p].astype(F32)
+                    place = pl.ds(pl.multiple_of(core * half + half - width, width), width)
+                    copies.append(
+                        pltpu.make_async_copy(
+                            sum_ref.at[side, v, p], out_ref.at[v, p, :, place], sems.at[side, v, p]
+                        )
+                    )
+                    copies[-1].start()
+        for copy in copies:
+            copy.wait()
+
+
+def finish_last(pick, out, part):
+    mpo_count, _, rows, width = part[0].shape
+    anywhere = pl.BlockSpec(memory_space=pl.ANY)
+    return pl.pallas_call(
+        finish_last_kernel,
+        in_specs=[pl.BlockSpec(memory_space=pltpu.SMEM)]
+        + [pl.BlockSpec(memory_space=pltpu.VMEM)] * 4
+        + [anywhere],
+        out_specs=anywhere,
+        out_shape=jax.ShapeDtypeStruct(out.shape, F32),
+        input_output_aliases={5: 0},
+        scratch_shapes=[
+            pltpu.VMEM((2, mpo_count, 2, rows, width), F32),
+            pltpu.SemaphoreType.DMA((2, mpo_count, 2)),
+        ],
+        compiler_params=pltpu.CompilerParams(vmem_limit_bytes=VMEM_BYTES),
+        cost_estimate=LIGHT,
+        name="finish_last",
+    )(pick, *part, out)
 
 
 def after(value, *earlier):
@@ -306,7 +347,9 @@
     last.append(last_part(1, *last[0], mine, siblings))
     siblings = swap(siblings)
     came_last = (step_of(depth) == row_count - 1).astype(jnp.int32)
-    return finish(jnp.stack([came_last, depth.astype(jnp.int32)]), mine, siblings, last)
+    pick = jnp.stack([came_last, depth.astype(jnp.int32)])
+    out = finish(after(pick, last[1][0]), mine, siblings, last[0])
+    return finish_last(pick, out, last[1])
 
 
 def solution(mesh):

time: 322 us -> 316 us (0.981)
  local copies, waits for them, and re-layouts: 18 us -> 11 us
  waiting for transfers between devices: 194 us -> 190 us
    unnamed x52 -> x16, local copies, waits for them, and re-layouts: 11.4 us -> 4 us
    ppermute x6, waiting for transfers between devices: 16.2 us -> 10.2 us  [send(): lax.ppermute(value, axes, [(place(r, 1 - c if turned else c, 1 - d if cro...]
    ppermute x12, waiting for transfers between devices: 161 us -> 166 us  [ring(): lax.ppermute(value, 'row', [(r, (r + 1) % row_count) for r in range(row_c...]
  transfers between devices with their start and end apart: 26 -> 26, of which waited for: 18 -> 19; matrix products, arithmetic and copies ran while one was open for 6% -> 7% of each run, Pallas kernels for 19% -> 21%
where the time goes in v13:
time: 316 us; the launch traced here: 315 us
  waiting for transfers between devices  190 us (60%)
  Pallas kernels  69.5 us (22%)
  starting transfers between devices  27.7 us (9%)
  other arithmetic  17.1 us (5%)
  local copies, waits for them, and re-layouts  11 us (3%)
    ppermute x12, waiting for transfers between devices, ring(): lax.ppermute(value, 'row', [(r, (r + 1) % row_count) for r in range(row_c...  166 us
    pallas_call x5, Pallas kernels, second_product(): pl.pallas_call(second_kernel, grid=(mpo_count,), in_specs=[pl.BlockSpec(m...  36.8 us
    pallas_call x1, Pallas kernels, first_product(): pl.pallas_call(functools.partial(first_kernel, w_local), grid=(rows // ro...  24.6 us
    ppermute x6, waiting for transfers between devices, send(): lax.ppermute(value, axes, [(place(r, 1 - c if turned else c, 1 - d if cro...  10.2 us
    ppermute x3, starting transfers between devices, turn_to_goal(): lax.ppermute(value, axes, [(place(r, 1 - c, d), place(r, c, d)) for r, (c...  8.92 us
    ppermute x6, starting transfers between devices, send(): lax.ppermute(value, axes, [(place(r, 1 - c if turned else c, 1 - d if cro...  7.73 us
    ppermute x4, waiting for transfers between devices, swap(): return lax.ppermute(value, 'depth', [(0, 1), (1, 0)])  7.13 us
  transfers between devices with their start and end apart: 26, of which 19 were waited for; matrix products, arithmetic and copies ran while one was open for 7% of the time, Pallas kernels for 21%

profile of v13, /device:TPU:1, one launch (start us, length us, event | category | flops | bytes accessed | tf_op | source)
XLA Modules:
  0.0 315.4 jit_solution(8542805816142371238)
XLA Ops:
  0.0 1.7 constant_dynamic-slice_fusion
  1.7 0.1 collective-permute-start
  1.8 2.7 collective-permute-start.2
  4.6 1.0 copy-done.3
  5.5 3.5 %copy.9 = bf16[2,512,2,1024]{3,1,2,0:T(8,128)(2,1)S(1)} copy(bf16[2,512,2,1024]{3,2,1,0:T(2,128)(2,1)} %param.4) | data formatting | bytes 8388608 | tf_op jit(solution)/shard_map/optimization_barrier | solution.py:206
  9.1 0.0 copy-start
  9.1 2.0 copy-done
  11.1 0.2 dynamic-slice_bitcast_fusion
  11.3 2.3 collective-permute-start.1
  13.5 16.6 %collective-permute-done.2.refs_2_ = bf16[1,2,512,512]{3,2,1,0:T(8,128)(2,1)} collective-permute-done((bf16[1,2,512,512]{3,2,1,0:T(8,128)(2,1)S(1)}, bf16[1,2,512,512]{3,2,1,0:T(8,128)(2,1)}, u32[]{:S(2)}, u32[]{:S(2)}) %collective-permute-start.2) | collective-permute-done | bytes 1048608 | tf_op jit(solution)/shard_map/ppermute | solution.py:269
  30.2 0.0 collective-permute-start.3
  30.2 0.5 collective-permute-start.5
  30.7 25.5 %collective-permute-done.3.refs_4_ = bf16[1,2,512,512]{3,2,1,0:T(8,128)(2,1)S(1)} collective-permute-done((bf16[1,2,512,512]{3,2,1,0:T(8,128)(2,1)}, bf16[1,2,512,512]{3,2,1,0:T(8,128)(2,1)S(1)}, u32[]{:S(2)}, u32[]{:S(2)}) %collective-permute-start.3) | collective-permute-done | bytes 1048608 | tf_op jit(solution)/shard_map/ppermute | solution.py:269
  56.2 3.1 collective-permute-done.1
  59.3 0.9 collective-permute-start.4
  60.2 18.6 %collective-permute-done.5.refs_3_ = bf16[1,2,512,512]{3,2,1,0:T(8,128)(2,1)} collective-permute-done((bf16[1,2,512,512]{3,2,1,0:T(8,128)(2,1)S(1)}, bf16[1,2,512,512]{3,2,1,0:T(8,128)(2,1)}, u32[]{:S(2)}, u32[]{:S(2)}) %collective-permute-start.5) | collective-permute-done | bytes 1048608 | tf_op jit(solution)/shard_map/ppermute | solution.py:269
  78.8 0.0 collective-permute-start.6
  78.8 1.7 fusion
  80.5 0.0 collective-permute-start.7
  80.5 23.6 %collective-permute-done.6.refs_5_ = bf16[1,2,512,512]{3,2,1,0:T(8,128)(2,1)} collective-permute-done((bf16[1,2,512,512]{3,2,1,0:T(8,128)(2,1)}, bf16[1,2,512,512]{3,2,1,0:T(8,128)(2,1)}, u32[]{:S(2)}, u32[]{:S(2)}) %collective-permute-start.6) | collective-permute-done | bytes 1048608 | tf_op jit(solution)/shard_map/ppermute | solution.py:269
  104.0 0.0 collective-permute-start.8
  104.1 5.6 %maximum_select_fusion.1 = bf16[1,2,2,512,1024]{4,3,2,1,0:T(8,128)(2,1)S(1)} fusion(bf16[1,2,2,256,1024]{4,3,2,1,0:T(8,128)(2,1)} %bitcast.10, bf16[1,2,2,256,1024]{4,3,2,1,0:T(8,128)(2,1)} %bitcast.9, pred[]{:T(512)S(6)} %eq.23), kind=kLoop, calls=%fused_computation.1 | loop fusion | flops 18874368 | bytes 8388609 | tf_op jit(solution)/shard_map/jit(_where)/select_n | solution.py:273
  109.7 0.0 copy-start.7
  109.7 4.1 %maximum_select_fusion.site_ref = bf16[2,2,2,512,1024]{4,3,2,1,0:T(8,128)(2,1)} fusion(bf16[1,2,2,512,1024]{4,3,2,1,0:T(8,128)(2,1)S(1)} %maximum_select_fusion.1, bf16[1,2,2,512,1024]{4,3,2,1,0:T(8,128)(2,1)S(1)} %bitcast.15, pred[]{:T(512)S(6)} %eq.22), kind=kLoop, calls=%fused_computation | loop fusion | flops 12582912 | bytes 16777216 | tf_op jit(solution)/shard_map/jit(_where)/select_n | solution.py:290
  113.8 12.6 %collective-permute-done.7.refs_6_ = bf16[1,2,512,512]{3,2,1,0:T(8,128)(2,1)S(1)} collective-permute-done((bf16[1,2,512,512]{3,2,1,0:T(8,128)(2,1)S(1)}, bf16[1,2,512,512]{3,2,1,0:T(8,128)(2,1)S(1)}, u32[]{:S(2)}, u32[]{:S(2)}) %collective-permute-start.7) | collective-permute-done | bytes 1048608 | tf_op jit(solution)/shard_map/ppermute | solution.py:269
  126.4 1.0 copy-done.6
  127.4 21.6 %collective-permute-done.8.refs_7_ = bf16[1,2,512,512]{3,2,1,0:T(8,128)(2,1)} collective-permute-done((bf16[1,2,512,512]{3,2,1,0:T(8,128)(2,1)}, bf16[1,2,512,512]{3,2,1,0:T(8,128)(2,1)}, u32[]{:S(2)}, u32[]{:S(2)}) %collective-permute-start.8) | collective-permute-done | bytes 1048608 | tf_op jit(solution)/shard_map/ppermute | solution.py:269
  149.0 0.7 pad_add_fusion.1.block_ref
  149.7 0.6 pad_maximum_fusion.mpo_ref
  150.3 24.6 %first_product.1.own_ref = bf16[2,2,2,512,512]{4,3,2,1,0:T(8,128)(2,1)} custom-call(s32[4]{0:T(128)} %pad_add_fusion.1.block_ref, f32[2,2,2,2]{3,2,1,0:T(2,128)} %pad_maximum_fusion.mpo_ref, bf16[2,2,2,512,1024]{4,3,2,1,0:T(8,128)(2,1)} %maximum_select_fusion.site_ref, bf16[1,2,512,512]{3,2,1,0:T(8,128)(2,1)} %copy-done.2, ...), custom_call_target="tpu_custom_call" | custom-call | tf_op jit(solution)/shard_map/first_product/pallas_call | solution.py:67
  174.9 19.1 %collective-permute-done.10.refs_1_ = bf16[2,2,128,1024]{3,2,1,0:T(8,128)(2,1)} collective-permute-done((bf16[2,2,128,1024]{3,2,1,0:T(8,128)(2,1)}, bf16[2,2,128,1024]{3,2,1,0:T(8,128)(2,1)}, u32[]{:S(2)}, u32[]{:S(2)}) %collective-permute-start.10) | collective-permute-done | bytes 1048608 | tf_op jit(solution)/shard_map/ppermute | solution.py:269
  193.9 2.4 collective-permute-start.11
  196.4 7.1 %collective-permute-done.11.sib_ref = bf16[2,2,2,512,512]{4,3,2,1,0:T(8,128)(2,1)} collective-permute-done((bf16[2,2,2,512,512]{4,3,2,1,0:T(8,128)(2,1)}, bf16[2,2,2,512,512]{4,3,2,1,0:T(8,128)(2,1)}, u32[]{:S(2)}, u32[]{:S(2)}) %collective-permute-start.11) | collective-permute-done | bytes 4194336 | tf_op jit(solution)/shard_map/ppermute | solution.py:210
  203.5 8.4 %second_product.5 = bf16[2,2,512,256]{3,2,1,0:T(8,128)(2,1)} custom-call(s32[1]{0:T(128)} %bitcast.1.pick_ref, bf16[2,2,2,512,512]{4,3,2,1,0:T(8,128)(2,1)} %first_product.1.own_ref, bf16[2,2,2,512,512]{4,3,2,1,0:T(8,128)(2,1)} %collective-permute-done.11.sib_ref, bf16[2,2,128,1024]{3,2,1,0:T(8,128)(2,1)} %get-tuple-element.17.refs_0_, ...), custom_call_target="tpu_custom_call" | custom-call | tf_op jit(solution)/shard_map/second_product/pallas_call | solution.py:104
  211.9 1.3 collective-permute-start.13
  213.2 0.1 collective-permute-start.14
  213.2 10.1 %collective-permute-done.12.refs_0_ = bf16[2,2,128,1024]{3,2,1,0:T(8,128)(2,1)} collective-permute-done((bf16[2,2,128,1024]{3,2,1,0:T(8,128)(2,1)}, bf16[2,2,128,1024]{3,2,1,0:T(8,128)(2,1)}, u32[]{:S(2)}, u32[]{:S(2)}) %collective-permute-start.12) | collective-permute-done | bytes 1048608 | tf_op jit(solution)/shard_map/ppermute | solution.py:269
  223.3 0.0 collective-permute-start.15
  223.3 8.4 %second_product.6 = bf16[2,2,512,256]{3,2,1,0:T(8,128)(2,1)} custom-call(s32[1]{0:T(128)} %bitcast.1.pick_ref, bf16[2,2,2,512,512]{4,3,2,1,0:T(8,128)(2,1)} %first_product.1.own_ref, bf16[2,2,2,512,512]{4,3,2,1,0:T(8,128)(2,1)} %collective-permute-done.11.sib_ref, bf16[2,2,128,1024]{3,2,1,0:T(8,128)(2,1)} %collective-permute-done.9.refs_0_, ...), custom_call_target="tpu_custom_call" | custom-call | tf_op jit(solution)/shard_map/second_product/pallas_call | solution.py:104
  231.7 3.8 %collective-permute-start.19 = (bf16[2,2,512,256]{3,2,1,0:T(8,128)(2,1)}, bf16[2,2,512,256]{3,2,1,0:T(8,128)(2,1)}, u32[]{:S(2)}, u32[]{:S(2)}) collective-permute-start(bf16[2,2,512,256]{3,2,1,0:T(8,128)(2,1)} %second_product.6), channel_id=1, source_target_pairs={{0,2},{1,3},{6,4},{7,5},{10,8},{11,9},{12,14},{13,15},{16,18},{17,... | collective-permute-start | bytes 3145736 | tf_op jit(solution)/shard_map/ppermute | solution.py:312
  235.5 2.9 collective-permute-done.13
  238.4 7.3 %collective-permute-done.14.refs_1_ = bf16[2,2,128,1024]{3,2,1,0:T(8,128)(2,1)} collective-permute-done((bf16[2,2,128,1024]{3,2,1,0:T(8,128)(2,1)}, bf16[2,2,128,1024]{3,2,1,0:T(8,128)(2,1)}, u32[]{:S(2)}, u32[]{:S(2)}) %collective-permute-start.14) | collective-permute-done | bytes 1048608 | tf_op jit(solution)/shard_map/ppermute | solution.py:269
  245.7 8.4 %second_product.7 = bf16[2,2,512,256]{3,2,1,0:T(8,128)(2,1)} custom-call(s32[1]{0:T(128)} %bitcast.1.pick_ref, bf16[2,2,2,512,512]{4,3,2,1,0:T(8,128)(2,1)} %first_product.1.own_ref, bf16[2,2,2,512,512]{4,3,2,1,0:T(8,128)(2,1)} %collective-permute-done.11.sib_ref, bf16[2,2,128,1024]{3,2,1,0:T(8,128)(2,1)} %collective-permute-done.12.refs_0_, ...), custom_call_target="tpu_custom_call" | custom-call | tf_op jit(solution)/shard_map/second_product/pallas_call | solution.py:104
  254.1 3.8 %collective-permute-start.20 = (bf16[2,2,512,256]{3,2,1,0:T(8,128)(2,1)}, bf16[2,2,512,256]{3,2,1,0:T(8,128)(2,1)}, u32[]{:S(2)}, u32[]{:S(2)}) collective-permute-start(bf16[2,2,512,256]{3,2,1,0:T(8,128)(2,1)} %second_product.7), channel_id=1, source_target_pairs={{0,2},{1,3},{4,6},{5,7},{10,8},{11,9},{14,12},{15,13},{16,18},{17,... | collective-permute-start | bytes 3145736 | tf_op jit(solution)/shard_map/ppermute | solution.py:312
  257.9 10.3 %collective-permute-done.15.refs_0_ = bf16[2,2,128,1024]{3,2,1,0:T(8,128)(2,1)} collective-permute-done((bf16[2,2,128,1024]{3,2,1,0:T(8,128)(2,1)}, bf16[2,2,128,1024]{3,2,1,0:T(8,128)(2,1)}, u32[]{:S(2)}, u32[]{:S(2)}) %collective-permute-start.15) | collective-permute-done | bytes 1048608 | tf_op jit(solution)/shard_map/ppermute | solution.py:269
  268.2 5.8 %second_product.8.refs_0_ = bf16[2,2,512,128]{3,2,1,0:T(8,128)(2,1)} custom-call(s32[1]{0:T(128)} %bitcast.1.pick_ref, bf16[2,2,2,512,512]{4,3,2,1,0:T(8,128)(2,1)} %first_product.1.own_ref, bf16[2,2,2,512,512]{4,3,2,1,0:T(8,128)(2,1)} %collective-permute-done.11.sib_ref, bf16[2,2,128,1024]{3,2,1,0:T(8,128)(2,1)} %collective-permute-done.15.refs_0_), custom_call_target="tpu_custom_call" | custom-call | tf_op jit(solution)/shard_map/second_product/pallas_call | solution.py:104
  274.0 1.3 collective-permute-start.16
  275.3 1.3 collective-permute-start.17
  276.6 1.3 collective-permute-start.18
  277.9 0.7 collective-permute-done.20
  278.6 5.5 %select_convert_fusion = (bf16[2,2,512,256]{3,2,1,0:T(8,128)(2,1)}, f32[2,2,512,256]{3,2,1,0:T(8,128)}) fusion(bf16[2,2,512,256]{3,2,1,0:T(8,128)(2,1)} %collective-permute-done.13, bf16[2,2,512,256]{3,2,1,0:T(8,128)(2,1)} %second_product.5, bf16[2,2,512,256]{3,2,1,0:T(8,128)(2,1)} %collective-permute-done.19, bf16[2,2,512,256]{3,2,1,0:T(8,128)(2,1)} %second_product.6, ...), kind=kLoop, calls=%fused_computation.2 | loop fusion | flops 7340032 | bytes 9437188 | tf_op jit(solution)/shard_map/convert_element_type | solution.py:346
  284.1 2.0 collective-permute-start.25
  286.1 2.1 collective-permute-done.16.refs_1_
  288.2 1.9 collective-permute-done.17.refs_2_
  290.2 0.5 collective-permute-done.21.refs_0_
  290.7 5.8 %second_product.9.refs_0_ = bf16[2,2,512,128]{3,2,1,0:T(8,128)(2,1)} custom-call(s32[1]{0:T(128)} %bitcast.1.pick_ref, bf16[2,2,2,512,512]{4,3,2,1,0:T(8,128)(2,1)} %first_product.1.own_ref, bf16[2,2,2,512,512]{4,3,2,1,0:T(8,128)(2,1)} %collective-permute-done.11.sib_ref, bf16[2,2,128,1024]{3,2,1,0:T(8,128)(2,1)} %collective-permute-done.21.refs_0_), custom_call_target="tpu_custom_call" | custom-call | tf_op jit(solution)/shard_map/second_product/pallas_call | solution.py:104
  296.5 1.3 collective-permute-start.22
  297.8 1.3 collective-permute-start.23
  299.1 1.3 collective-permute-start.24
  300.4 0.7 pad_add_fusion.pick_ref
  301.1 5.2 %finish.1.refs_4_ = f32[2,2,512,512]{3,2,1,0:T(8,128)} custom-call(s32[2]{0:T(128)} %pad_add_fusion.pick_ref, f32[2,2,512,256]{3,2,1,0:T(8,128)} %get-tuple-element.26.mine_ref, bf16[2,2,512,256]{3,2,1,0:T(8,128)(2,1)} %collective-permute-done.25.siblings_ref, bf16[2,2,512,128]{3,2,1,0:T(8,128)(2,1)} %second_product.8.refs_0_, ...), custom_call_target="tpu_custom_call" | custom-call | tf_op jit(solution)/shard_map/finish/pallas_call | solution.py:145
  306.2 4.2 %collective-permute-done.22.refs_1_ = bf16[2,2,512,128]{3,2,1,0:T(8,128)(2,1)} collective-permute-done((bf16[2,2,512,128]{3,2,1,0:T(8,128)(2,1)}, bf16[2,2,512,128]{3,2,1,0:T(8,128)(2,1)}, u32[]{:S(2)}, u32[]{:S(2)}) %collective-permute-start.22) | collective-permute-done | bytes 524320 | tf_op jit(solution)/shard_map/ppermute | solution.py:319
  310.4 1.9 collective-permute-done.23.refs_2_
  312.3 2.9 finish_last.1
  (23 shorter events, 0.1 us)
Async XLA Ops:
  1.7 7.4 %copy-start.2 = (bf16[1,2,512,512]{3,2,1,0:T(8,128)(2,1)}, bf16[1,2,512,512]{3,2,1,0:T(8,128)(2,1)S(1)}, u32[]{:S(2)}) copy-start(bf16[1,2,512,512]{3,2,1,0:T(8,128)(2,1)S(1)} %get-tuple-element.31.refs_0_) | copy-start | bytes 3145732
  1.7 2.9 collective-permute-start
  1.8 28.3 %collective-permute-start.2 = (bf16[1,2,512,512]{3,2,1,0:T(8,128)(2,1)S(1)}, bf16[1,2,512,512]{3,2,1,0:T(8,128)(2,1)}, u32[]{:S(2)}, u32[]{:S(2)}) collective-permute-start(bf16[1,2,512,512]{3,2,1,0:T(8,128)(2,1)S(1)} %get-tuple-element.31.refs_0_), channel_id=1, source_target_pairs={{0,4},{4,8},{8,12},{12,0},{1,5},{5,9},{9,13},{13,1},{2,6},{6,10},{... | collective-permute-start | bytes 3145736 | tf_op jit(solution)/shard_map/ppermute | solution.py:269
  4.6 1.0 copy-start.3
  9.1 2.0 copy-start
  11.1 19.1 %copy-start.4 = (bf16[1,2,512,512]{3,2,1,0:T(8,128)(2,1)S(1)}, bf16[1,2,512,512]{3,2,1,0:T(8,128)(2,1)}, u32[]{:S(2)}) copy-start(bf16[1,2,512,512]{3,2,1,0:T(8,128)(2,1)} %copy-done.3) | copy-start | bytes 3145732
  11.3 48.1 %collective-permute-start.1 = (bf16[2,2,256,1024]{3,2,1,0:T(8,128)(2,1)S(1)}, bf16[2,2,256,1024]{3,2,1,0:T(8,128)(2,1)}, u32[]{:S(2)}, u32[]{:S(2)}) collective-permute-start(bf16[2,2,256,1024]{3,2,1,0:T(8,128)(2,1)S(1)} %dynamic-slice_bitcast_fusion), channel_id=1, source_target_pairs={{0,2},{2,0},{1,3},{3,1},{4,6},{6,4},{5,7},{7,5},{8,10},{10,8},{9,1... | collective-permute-start | bytes 6291464 | tf_op jit(solution)/shard_map/ppermute | solution.py:272
  30.2 26.1 %collective-permute-start.3 = (bf16[1,2,512,512]{3,2,1,0:T(8,128)(2,1)}, bf16[1,2,512,512]{3,2,1,0:T(8,128)(2,1)S(1)}, u32[]{:S(2)}, u32[]{:S(2)}) collective-permute-start(bf16[1,2,512,512]{3,2,1,0:T(8,128)(2,1)} %collective-permute-done.2.refs_2_), channel_id=1, source_target_pairs={{0,4},{4,8},{8,12},{12,0},{1,5},{5,9},{9,13},{13,1},{2,6},{6,10},{... | collective-permute-start | bytes 3145736 | tf_op jit(solution)/shard_map/ppermute | solution.py:269
  30.2 48.6 %collective-permute-start.5 = (bf16[1,2,512,512]{3,2,1,0:T(8,128)(2,1)S(1)}, bf16[1,2,512,512]{3,2,1,0:T(8,128)(2,1)}, u32[]{:S(2)}, u32[]{:S(2)}) collective-permute-start(bf16[1,2,512,512]{3,2,1,0:T(8,128)(2,1)S(1)} %copy-done.4), channel_id=1, source_target_pairs={{0,4},{4,8},{8,12},{12,0},{1,5},{5,9},{9,13},{13,1},{2,6},{6,10},{... | collective-permute-start | bytes 3145736 | tf_op jit(solution)/shard_map/ppermute | solution.py:269
  56.2 53.5 %copy-start.5 = (bf16[1,2,512,512]{3,2,1,0:T(8,128)(2,1)}, bf16[1,2,512,512]{3,2,1,0:T(8,128)(2,1)S(1)}, u32[]{:S(2)}) copy-start(bf16[1,2,512,512]{3,2,1,0:T(8,128)(2,1)S(1)} %collective-permute-done.3.refs_4_) | copy-start | bytes 3145732
  59.3 44.7 %collective-permute-start.4 = (bf16[2,2,256,1024]{3,2,1,0:T(8,128)(2,1)}, bf16[2,2,256,1024]{3,2,1,0:T(8,128)(2,1)}, u32[]{:S(2)}, u32[]{:S(2)}) collective-permute-start(bf16[2,2,256,1024]{3,2,1,0:T(8,128)(2,1)} %collective-permute-done.1), channel_id=1, source_target_pairs={{0,1},{1,0},{2,3},{3,2},{4,5},{5,4},{6,7},{7,6},{8,9},{9,8},{10,11... | collective-permute-start | bytes 6291464 | tf_op jit(solution)/shard_map/ppermute | solution.py:210
  78.8 25.3 %collective-permute-start.6 = (bf16[1,2,512,512]{3,2,1,0:T(8,128)(2,1)}, bf16[1,2,512,512]{3,2,1,0:T(8,128)(2,1)}, u32[]{:S(2)}, u32[]{:S(2)}) collective-permute-start(bf16[1,2,512,512]{3,2,1,0:T(8,128)(2,1)} %collective-permute-done.5.refs_3_), channel_id=1, source_target_pairs={{0,4},{4,8},{8,12},{12,0},{1,5},{5,9},{9,13},{13,1},{2,6},{6,10},{... | collective-permute-start | bytes 3145736 | tf_op jit(solution)/shard_map/ppermute | solution.py:269
  80.5 46.0 %collective-permute-start.7 = (bf16[1,2,512,512]{3,2,1,0:T(8,128)(2,1)S(1)}, bf16[1,2,512,512]{3,2,1,0:T(8,128)(2,1)S(1)}, u32[]{:S(2)}, u32[]{:S(2)}) collective-permute-start(bf16[1,2,512,512]{3,2,1,0:T(8,128)(2,1)S(1)} %collective-permute-done.3.refs_4_), channel_id=1, source_target_pairs={{0,4},{4,8},{8,12},{12,0},{1,5},{5,9},{9,13},{13,1},{2,6},{6,10},{... | collective-permute-start | bytes 3145736 | tf_op jit(solution)/shard_map/ppermute | solution.py:269
  104.0 44.9 %collective-permute-start.8 = (bf16[1,2,512,512]{3,2,1,0:T(8,128)(2,1)}, bf16[1,2,512,512]{3,2,1,0:T(8,128)(2,1)}, u32[]{:S(2)}, u32[]{:S(2)}) collective-permute-start(bf16[1,2,512,512]{3,2,1,0:T(8,128)(2,1)} %collective-permute-done.6.refs_5_), channel_id=1, source_target_pairs={{0,4},{4,8},{8,12},{12,0},{1,5},{5,9},{9,13},{13,1},{2,6},{6,10},{... | collective-permute-start | bytes 3145736 | tf_op jit(solution)/shard_map/ppermute | solution.py:269
  104.1 5.6 %copy-start.1 = (bf16[2,512,2,1024]{3,1,2,0:T(8,128)(2,1)S(1)}, bf16[2,512,2,1024]{3,1,2,0:T(8,128)(2,1)}, u32[]{:S(2)}) copy-start(bf16[2,512,2,1024]{3,1,2,0:T(8,128)(2,1)} %copy-done) | copy-start | bytes 12582916
  109.7 40.0 %copy-start.7 = (f32[2,2,2,2]{3,2,1,0:T(2,128)S(1)}, f32[2,2,2,2]{3,2,1,0:T(2,128)}, u32[]{:S(2)}) copy-start(f32[2,2,2,2]{3,2,1,0:T(2,128)} %param.5) | copy-start | bytes 196
  126.4 1.0 copy-start.6
  127.4 47.5 %collective-permute-start.9 = (bf16[2,2,128,1024]{3,2,1,0:T(8,128)(2,1)}, bf16[2,2,128,1024]{3,2,1,0:T(8,128)(2,1)}, u32[]{:S(2)}, u32[]{:S(2)}) collective-permute-start(bf16[2,2,128,1024]{3,2,1,0:T(8,128)(2,1)} %get-tuple-element.17.refs_0_), channel_id=1, source_target_pairs={{0,4},{4,8},{8,12},{12,0},{1,5},{5,9},{9,13},{13,1},{2,6},{6,10},{... | collective-permute-start | bytes 3145736 | tf_op jit(solution)/shard_map/ppermute | solution.py:269
  149.0 44.9 %collective-permute-start.10 = (bf16[2,2,128,1024]{3,2,1,0:T(8,128)(2,1)}, bf16[2,2,128,1024]{3,2,1,0:T(8,128)(2,1)}, u32[]{:S(2)}, u32[]{:S(2)}) collective-permute-start(bf16[2,2,128,1024]{3,2,1,0:T(8,128)(2,1)} %get-tuple-element.18.refs_1_), channel_id=1, source_target_pairs={{0,4},{4,8},{8,12},{12,0},{1,5},{5,9},{9,13},{13,1},{2,6},{6,10},{... | collective-permute-start | bytes 3145736 | tf_op jit(solution)/shard_map/ppermute | solution.py:269
  193.9 9.6 %collective-permute-start.11 = (bf16[2,2,2,512,512]{4,3,2,1,0:T(8,128)(2,1)}, bf16[2,2,2,512,512]{4,3,2,1,0:T(8,128)(2,1)}, u32[]{:S(2)}, u32[]{:S(2)}) collective-permute-start(bf16[2,2,2,512,512]{4,3,2,1,0:T(8,128)(2,1)} %first_product.1.own_ref), channel_id=1, source_target_pairs={{0,1},{1,0},{2,3},{3,2},{4,5},{5,4},{6,7},{7,6},{8,9},{9,8},{10,11... | collective-permute-start | bytes 12582920 | tf_op jit(solution)/shard_map/ppermute | solution.py:210
  196.4 26.9 %collective-permute-start.12 = (bf16[2,2,128,1024]{3,2,1,0:T(8,128)(2,1)}, bf16[2,2,128,1024]{3,2,1,0:T(8,128)(2,1)}, u32[]{:S(2)}, u32[]{:S(2)}) collective-permute-start(bf16[2,2,128,1024]{3,2,1,0:T(8,128)(2,1)} %collective-permute-done.9.refs_0_), channel_id=1, source_target_pairs={{0,4},{4,8},{8,12},{12,0},{1,5},{5,9},{9,13},{13,1},{2,6},{6,10},{... | collective-permute-start | bytes 3145736 | tf_op jit(solution)/shard_map/ppermute | solution.py:269
  211.9 26.6 %collective-permute-start.13 = (bf16[2,2,512,256]{3,2,1,0:T(8,128)(2,1)}, bf16[2,2,512,256]{3,2,1,0:T(8,128)(2,1)}, u32[]{:S(2)}, u32[]{:S(2)}) collective-permute-start(bf16[2,2,512,256]{3,2,1,0:T(8,128)(2,1)} %second_product.5), channel_id=1, source_target_pairs={{2,0},{3,1},{6,4},{7,5},{8,10},{9,11},{12,14},{13,15},{18,16},{19,... | collective-permute-start | bytes 3145736 | tf_op jit(solution)/shard_map/ppermute | solution.py:312
  213.2 32.6 %collective-permute-start.14 = (bf16[2,2,128,1024]{3,2,1,0:T(8,128)(2,1)}, bf16[2,2,128,1024]{3,2,1,0:T(8,128)(2,1)}, u32[]{:S(2)}, u32[]{:S(2)}) collective-permute-start(bf16[2,2,128,1024]{3,2,1,0:T(8,128)(2,1)} %collective-permute-done.10.refs_1_), channel_id=1, source_target_pairs={{0,4},{4,8},{8,12},{12,0},{1,5},{5,9},{9,13},{13,1},{2,6},{6,10},{... | collective-permute-start | bytes 3145736 | tf_op jit(solution)/shard_map/ppermute | solution.py:269
  223.3 44.9 %collective-permute-start.15 = (bf16[2,2,128,1024]{3,2,1,0:T(8,128)(2,1)}, bf16[2,2,128,1024]{3,2,1,0:T(8,128)(2,1)}, u32[]{:S(2)}, u32[]{:S(2)}) collective-permute-start(bf16[2,2,128,1024]{3,2,1,0:T(8,128)(2,1)} %collective-permute-done.12.refs_0_), channel_id=1, source_target_pairs={{0,4},{4,8},{8,12},{12,0},{1,5},{5,9},{9,13},{13,1},{2,6},{6,10},{... | collective-permute-start | bytes 3145736 | tf_op jit(solution)/shard_map/ppermute | solution.py:269
  231.7 44.9 %collective-permute-start.19 = (bf16[2,2,512,256]{3,2,1,0:T(8,128)(2,1)}, bf16[2,2,512,256]{3,2,1,0:T(8,128)(2,1)}, u32[]{:S(2)}, u32[]{:S(2)}) collective-permute-start(bf16[2,2,512,256]{3,2,1,0:T(8,128)(2,1)} %second_product.6), channel_id=1, source_target_pairs={{0,2},{1,3},{6,4},{7,5},{10,8},{11,9},{12,14},{13,15},{16,18},{17,... | collective-permute-start | bytes 3145736 | tf_op jit(solution)/shard_map/ppermute | solution.py:312
  254.1 24.5 %collective-permute-start.20 = (bf16[2,2,512,256]{3,2,1,0:T(8,128)(2,1)}, bf16[2,2,512,256]{3,2,1,0:T(8,128)(2,1)}, u32[]{:S(2)}, u32[]{:S(2)}) collective-permute-start(bf16[2,2,512,256]{3,2,1,0:T(8,128)(2,1)} %second_product.7), channel_id=1, source_target_pairs={{0,2},{1,3},{4,6},{5,7},{10,8},{11,9},{14,12},{15,13},{16,18},{17,... | collective-permute-start | bytes 3145736 | tf_op jit(solution)/shard_map/ppermute | solution.py:312
  257.9 32.8 %collective-permute-start.21 = (bf16[2,2,128,1024]{3,2,1,0:T(8,128)(2,1)}, bf16[2,2,128,1024]{3,2,1,0:T(8,128)(2,1)}, u32[]{:S(2)}, u32[]{:S(2)}) collective-permute-start(bf16[2,2,128,1024]{3,2,1,0:T(8,128)(2,1)} %collective-permute-done.14.refs_1_), channel_id=1, source_target_pairs={{0,4},{4,8},{8,12},{12,0},{1,5},{5,9},{9,13},{13,1},{2,6},{6,10},{... | collective-permute-start | bytes 3145736 | tf_op jit(solution)/shard_map/ppermute | solution.py:269
  274.0 14.2 %collective-permute-start.16 = (bf16[2,2,512,128]{3,2,1,0:T(8,128)(2,1)}, bf16[2,2,512,128]{3,2,1,0:T(8,128)(2,1)}, u32[]{:S(2)}, u32[]{:S(2)}) collective-permute-start(bf16[2,2,512,128]{3,2,1,0:T(8,128)(2,1)} %second_product.8.refs_0_), channel_id=1, source_target_pairs={{3,1},{4,6},{9,11},{14,12},{19,17},{20,22},{25,27},{30,28}} | collective-permute-start | bytes 1572872 | tf_op jit(solution)/shard_map/ppermute | solution.py:319
  275.3 14.9 %collective-permute-start.17 = (bf16[2,2,512,128]{3,2,1,0:T(8,128)(2,1)}, bf16[2,2,512,128]{3,2,1,0:T(8,128)(2,1)}, u32[]{:S(2)}, u32[]{:S(2)}) collective-permute-start(bf16[2,2,512,128]{3,2,1,0:T(8,128)(2,1)} %second_product.8.refs_0_), channel_id=1, source_target_pairs={{2,1},{5,6},{8,11},{15,12},{18,17},{21,22},{24,27},{31,28}} | collective-permute-start | bytes 1572872 | tf_op jit(solution)/shard_map/ppermute | solution.py:319
  276.6 13.5 %collective-permute-start.18 = (bf16[2,2,512,128]{3,2,1,0:T(8,128)(2,1)}, bf16[2,2,512,128]{3,2,1,0:T(8,128)(2,1)}, u32[]{:S(2)}, u32[]{:S(2)}) collective-permute-start(bf16[2,2,512,128]{3,2,1,0:T(8,128)(2,1)} %second_product.8.refs_0_), channel_id=1, source_target_pairs={{0,1},{7,6},{10,11},{13,12},{16,17},{23,22},{26,27},{29,28}} | collective-permute-start | bytes 1572872 | tf_op jit(solution)/shard_map/ppermute | solution.py:319
  284.1 17.0 %collective-permute-start.25 = (bf16[2,2,512,256]{3,2,1,0:T(8,128)(2,1)}, bf16[2,2,512,256]{3,2,1,0:T(8,128)(2,1)}, u32[]{:S(2)}, u32[]{:S(2)}) collective-permute-start(bf16[2,2,512,256]{3,2,1,0:T(8,128)(2,1)} %get-tuple-element.25), channel_id=1, source_target_pairs={{0,1},{1,0},{2,3},{3,2},{4,5},{5,4},{6,7},{7,6},{8,9},{9,8},{10,11... | collective-permute-start | bytes 3145736 | tf_op jit(solution)/shard_map/ppermute | solution.py:210
  296.5 13.9 %collective-permute-start.22 = (bf16[2,2,512,128]{3,2,1,0:T(8,128)(2,1)}, bf16[2,2,512,128]{3,2,1,0:T(8,128)(2,1)}, u32[]{:S(2)}, u32[]{:S(2)}) collective-permute-start(bf16[2,2,512,128]{3,2,1,0:T(8,128)(2,1)} %second_product.9.refs_0_), channel_id=1, source_target_pairs={{3,1},{4,6},{9,11},{14,12},{19,17},{20,22},{25,27},{30,28}} | collective-permute-start | bytes 1572872 | tf_op jit(solution)/shard_map/ppermute | solution.py:319
  297.8 14.6 %collective-permute-start.23 = (bf16[2,2,512,128]{3,2,1,0:T(8,128)(2,1)}, bf16[2,2,512,128]{3,2,1,0:T(8,128)(2,1)}, u32[]{:S(2)}, u32[]{:S(2)}) collective-permute-start(bf16[2,2,512,128]{3,2,1,0:T(8,128)(2,1)} %second_product.9.refs_0_), channel_id=1, source_target_pairs={{2,1},{5,6},{8,11},{15,12},{18,17},{21,22},{24,27},{31,28}} | collective-permute-start | bytes 1572872 | tf_op jit(solution)/shard_map/ppermute | solution.py:319
  299.1 13.3 %collective-permute-start.24 = (bf16[2,2,512,128]{3,2,1,0:T(8,128)(2,1)}, bf16[2,2,512,128]{3,2,1,0:T(8,128)(2,1)}, u32[]{:S(2)}, u32[]{:S(2)}) collective-permute-start(bf16[2,2,512,128]{3,2,1,0:T(8,128)(2,1)} %second_product.9.refs_0_), channel_id=1, source_target_pairs={{0,1},{7,6},{10,11},{13,12},{16,17},{23,22},{26,27},{29,28}} | collective-permute-start | bytes 1572872 | tf_op jit(solution)/shard_map/ppermute | solution.py:319

commit v14 on v13

--- a/solution.py
+++ b/solution.py
@@ -8,7 +8,7 @@
 
 F32 = jnp.float32
 BF16 = jnp.bfloat16
-VMEM_BYTES = 64 * 1024 * 1024
+VMEM_BYTES = 40 * 1024 * 1024
 LIGHT = pl.CostEstimate(flops=0, bytes_accessed=0, transcendentals=0)
 
 
@@ -286,7 +286,7 @@
     half = rows // 2
     mine = lax.dynamic_slice_in_dim(planar, depth * half, half, 2)
     other = turn(mine)
-    other = in_order(other, swap(after(other, envs[4])), 2)
+    other = in_order(other, swap(after(other, envs[3], envs[4])), 2)
     site = jnp.where(col == 0, jnp.stack([planar, other]), jnp.stack([other, planar]))
 
     parts = [mine[:, :, : half // 2], mine[:, :, half // 2 :]]

time: 316 us -> 315 us (level)
  local copies, waits for them, and re-layouts: 11 us -> 26.2 us
  Pallas kernels: 69.5 us -> 55.8 us
  other arithmetic: 17.1 us -> 13.4 us
    unnamed x16 -> x62, local copies, waits for them, and re-layouts: 4 us -> 17.6 us
    pallas_call x5, Pallas kernels: 36.8 us -> 25.6 us  [second_product(): pl.pallas_call(second_kernel, grid=(mpo_count,), in_specs=[pl.BlockSpec(m...]
    ppermute x12, waiting for transfers between devices: 166 us -> 172 us  [ring(): lax.ppermute(value, 'row', [(r, (r + 1) % row_count) for r in range(row_c...]
  transfers between devices with their start and end apart: 26 -> 26, of which waited for: 19 -> 17; matrix products, arithmetic and copies ran while one was open for 7% -> 6% of each run, Pallas kernels for 21% -> 17%
where the time goes in v14:
time: 315 us; the launch traced here: 314 us
  waiting for transfers between devices  191 us (61%)
  Pallas kernels  55.8 us (18%)
  starting transfers between devices  27.2 us (9%)
  local copies, waits for them, and re-layouts  26.2 us (8%)
  other arithmetic  13.4 us (4%)
    ppermute x12, waiting for transfers between devices, ring(): lax.ppermute(value, 'row', [(r, (r + 1) % row_count) for r in range(row_c...  172 us
    pallas_call x5, Pallas kernels, second_product(): pl.pallas_call(second_kernel, grid=(mpo_count,), in_specs=[pl.BlockSpec(m...  25.6 us
    pallas_call x1, Pallas kernels, first_product(): pl.pallas_call(functools.partial(first_kernel, w_local), grid=(rows // ro...  23.4 us
    unnamed x62, local copies, waits for them, and re-layouts  17.6 us
    ppermute x6, waiting for transfers between devices, send(): lax.ppermute(value, axes, [(place(r, 1 - c if turned else c, 1 - d if cro...  11.2 us
    ppermute x3, starting transfers between devices, turn_to_goal(): lax.ppermute(value, axes, [(place(r, 1 - c, d), place(r, c, d)) for r, (c...  9.49 us
    ppermute x6, starting transfers between devices, send(): lax.ppermute(value, axes, [(place(r, 1 - c if turned else c, 1 - d if cro...  7.75 us
    ppermute x4, waiting for transfers between devices, swap(): return lax.ppermute(value, 'depth', [(0, 1), (1, 0)])  6.86 us
  transfers between devices with their start and end apart: 26, of which 17 were waited for; matrix products, arithmetic and copies ran while one was open for 6% of the time, Pallas kernels for 17%

profile of v14, /device:TPU:1, one launch (start us, length us, event | category | flops | bytes accessed | tf_op | source)
XLA Modules:
  0.0 313.9 jit_solution(18118328989470805753)
XLA Ops:
  0.0 2.7 constant_dynamic-slice_fusion
  2.8 2.7 collective-permute-start.3
  5.5 0.1 collective-permute-done.refs_1_
  5.6 3.9 %copy.9 = bf16[2,512,2,1024]{3,1,2,0:T(8,128)(2,1)S(1)} copy(bf16[2,512,2,1024]{3,2,1,0:T(2,128)(2,1)} %param.4) | data formatting | bytes 8388608 | tf_op jit(solution)/shard_map/optimization_barrier | solution.py:206
  9.5 0.2 dynamic-slice_bitcast_fusion
  9.7 2.4 collective-permute-start.1
  12.1 1.3 collective-permute-start.2
  13.4 17.7 %collective-permute-done.3.refs_2_ = bf16[1,2,512,512]{3,2,1,0:T(8,128)(2,1)S(1)} collective-permute-done((bf16[1,2,512,512]{3,2,1,0:T(8,128)(2,1)S(1)}, bf16[1,2,512,512]{3,2,1,0:T(8,128)(2,1)S(1)}, u32[]{:S(2)}, u32[]{:S(2)}) %collective-permute-start.3) | collective-permute-done | bytes 1048608 | tf_op jit(solution)/shard_map/ppermute | solution.py:269
  31.1 1.0 copy-done.11
  32.0 21.6 %collective-permute-done.2.refs_3_ = bf16[1,2,512,512]{3,2,1,0:T(8,128)(2,1)} collective-permute-done((bf16[1,2,512,512]{3,2,1,0:T(8,128)(2,1)S(1)}, bf16[1,2,512,512]{3,2,1,0:T(8,128)(2,1)}, u32[]{:S(2)}, u32[]{:S(2)}) %collective-permute-start.2) | collective-permute-done | bytes 1048608 | tf_op jit(solution)/shard_map/ppermute | solution.py:269
  53.6 22.4 %collective-permute-done.4.refs_4_ = bf16[1,2,512,512]{3,2,1,0:T(8,128)(2,1)S(1)} collective-permute-done((bf16[1,2,512,512]{3,2,1,0:T(8,128)(2,1)S(1)}, bf16[1,2,512,512]{3,2,1,0:T(8,128)(2,1)S(1)}, u32[]{:S(2)}, u32[]{:S(2)}) %collective-permute-start.4) | collective-permute-done | bytes 1048608 | tf_op jit(solution)/shard_map/ppermute | solution.py:269
  76.0 1.0 copy-done.13
  77.0 0.6 collective-permute-start.5
  77.6 1.8 fusion
  79.4 0.8 collective-permute-start.7
  80.2 24.2 %collective-permute-done.6.refs_5_ = bf16[1,2,512,512]{3,2,1,0:T(8,128)(2,1)} collective-permute-done((bf16[1,2,512,512]{3,2,1,0:T(8,128)(2,1)}, bf16[1,2,512,512]{3,2,1,0:T(8,128)(2,1)}, u32[]{:S(2)}, u32[]{:S(2)}) %collective-permute-start.6) | collective-permute-done | bytes 1048608 | tf_op jit(solution)/shard_map/ppermute | solution.py:269
  104.5 5.3 %maximum_select_fusion.1 = bf16[1,2,2,512,1024]{4,3,2,1,0:T(8,128)(2,1)S(1)} fusion(bf16[1,2,2,256,1024]{4,3,2,1,0:T(8,128)(2,1)} %bitcast.10, bf16[1,2,2,256,1024]{4,3,2,1,0:T(8,128)(2,1)} %bitcast.9, pred[]{:T(512)S(6)} %eq.23), kind=kLoop, calls=%fused_computation.1 | loop fusion | flops 18874368 | bytes 8388609 | tf_op jit(solution)/shard_map/jit(_where)/select_n | solution.py:273
  109.8 4.1 %maximum_select_fusion.site_ref = bf16[2,2,2,512,1024]{4,3,2,1,0:T(8,128)(2,1)} fusion(bf16[1,2,2,512,1024]{4,3,2,1,0:T(8,128)(2,1)S(1)} %maximum_select_fusion.1, bf16[1,2,2,512,1024]{4,3,2,1,0:T(8,128)(2,1)S(1)} %bitcast.15, pred[]{:T(512)S(6)} %eq.22), kind=kLoop, calls=%fused_computation | loop fusion | flops 12582912 | bytes 16777216 | tf_op jit(solution)/shard_map/jit(_where)/select_n | solution.py:290
  113.9 12.9 %collective-permute-done.7.refs_6_ = bf16[1,2,512,512]{3,2,1,0:T(8,128)(2,1)S(1)} collective-permute-done((bf16[1,2,512,512]{3,2,1,0:T(8,128)(2,1)}, bf16[1,2,512,512]{3,2,1,0:T(8,128)(2,1)S(1)}, u32[]{:S(2)}, u32[]{:S(2)}) %collective-permute-start.7) | collective-permute-done | bytes 1048608 | tf_op jit(solution)/shard_map/ppermute | solution.py:269
  126.8 1.0 copy-done.15
  127.8 21.5 %collective-permute-done.8.refs_7_ = bf16[1,2,512,512]{3,2,1,0:T(8,128)(2,1)S(1)} collective-permute-done((bf16[1,2,512,512]{3,2,1,0:T(8,128)(2,1)}, bf16[1,2,512,512]{3,2,1,0:T(8,128)(2,1)S(1)}, u32[]{:S(2)}, u32[]{:S(2)}) %collective-permute-start.8) | collective-permute-done | bytes 1048608 | tf_op jit(solution)/shard_map/ppermute | solution.py:269
  149.3 1.0 copy-done.17
  150.3 0.1 pad_add_fusion.1.block_ref
  150.4 1.2 copy-done.10
  151.6 1.2 copy-done.12
  152.8 1.2 copy-done.14
  154.0 1.2 copy-done.16
  155.3 1.2 copy-done.18
  156.5 23.4 %first_product.1.own_ref = bf16[2,2,2,512,512]{4,3,2,1,0:T(8,128)(2,1)S(1)} custom-call(s32[4]{0:T(128)S(1)} %pad_add_fusion.1.block_ref, f32[2,2,2,2]{3,2,1,0:T(2,128)S(1)} %pad_maximum_fusion.mpo_ref, bf16[2,2,2,512,1024]{4,3,2,1,0:T(8,128)(2,1)} %maximum_select_fusion.site_ref, bf16[1,2,512,512]{3,2,1,0:T(8,128)(2,1)S(1)} %get-tuple-element.31.refs_0_, ...), custom_call_target="tpu_custom_call" | custom-call | tf_op jit(solution)/shard_map/first_product/pallas_call | solution.py:67
  179.9 14.4 %collective-permute-done.10.refs_1_ = bf16[2,2,128,1024]{3,2,1,0:T(8,128)(2,1)} collective-permute-done((bf16[2,2,128,1024]{3,2,1,0:T(8,128)(2,1)S(1)}, bf16[2,2,128,1024]{3,2,1,0:T(8,128)(2,1)}, u32[]{:S(2)}, u32[]{:S(2)}) %collective-permute-start.10) | collective-permute-done | bytes 1048608 | tf_op jit(solution)/shard_map/ppermute | solution.py:269
  194.3 0.8 collective-permute-start.11
  195.2 6.8 %collective-permute-done.11.sib_ref = bf16[2,2,2,512,512]{4,3,2,1,0:T(8,128)(2,1)S(1)} collective-permute-done((bf16[2,2,2,512,512]{4,3,2,1,0:T(8,128)(2,1)S(1)}, bf16[2,2,2,512,512]{4,3,2,1,0:T(8,128)(2,1)S(1)}, u32[]{:S(2)}, u32[]{:S(2)}) %collective-permute-start.11) | collective-permute-done | bytes 4194336 | tf_op jit(solution)/shard_map/ppermute | solution.py:210
  202.0 4.8 %second_product.5 = bf16[2,2,512,256]{3,2,1,0:T(8,128)(2,1)S(1)} custom-call(s32[1]{0:T(128)} %bitcast.1.pick_ref, bf16[2,2,2,512,512]{4,3,2,1,0:T(8,128)(2,1)S(1)} %first_product.1.own_ref, bf16[2,2,2,512,512]{4,3,2,1,0:T(8,128)(2,1)S(1)} %collective-permute-done.11.sib_ref, bf16[2,2,128,1024]{3,2,1,0:T(8,128)(2,1)S(1)} %get-tuple-element.17.refs_0_, ...), custom_call_target="tpu_custom_call" | custom-call | tf_op jit(solution)/shard_map/second_product/pallas_call | solution.py:104
  206.8 1.3 collective-permute-start.13
  208.1 14.0 %collective-permute-done.12.refs_0_ = bf16[2,2,128,1024]{3,2,1,0:T(8,128)(2,1)} collective-permute-done((bf16[2,2,128,1024]{3,2,1,0:T(8,128)(2,1)}, bf16[2,2,128,1024]{3,2,1,0:T(8,128)(2,1)}, u32[]{:S(2)}, u32[]{:S(2)}) %collective-permute-start.12) | collective-permute-done | bytes 1048608 | tf_op jit(solution)/shard_map/ppermute | solution.py:269
  222.1 6.3 %second_product.6 = bf16[2,2,512,256]{3,2,1,0:T(8,128)(2,1)S(1)} custom-call(s32[1]{0:T(128)} %bitcast.1.pick_ref, bf16[2,2,2,512,512]{4,3,2,1,0:T(8,128)(2,1)S(1)} %first_product.1.own_ref, bf16[2,2,2,512,512]{4,3,2,1,0:T(8,128)(2,1)S(1)} %collective-permute-done.11.sib_ref, bf16[2,2,128,1024]{3,2,1,0:T(8,128)(2,1)} %collective-permute-done.9.refs_0_, ...), custom_call_target="tpu_custom_call" | custom-call | tf_op jit(solution)/shard_map/second_product/pallas_call | solution.py:104
  228.4 4.1 %collective-permute-start.19 = (bf16[2,2,512,256]{3,2,1,0:T(8,128)(2,1)S(1)}, bf16[2,2,512,256]{3,2,1,0:T(8,128)(2,1)}, u32[]{:S(2)}, u32[]{:S(2)}) collective-permute-start(bf16[2,2,512,256]{3,2,1,0:T(8,128)(2,1)S(1)} %second_product.6), channel_id=1, source_target_pairs={{0,2},{1,3},{6,4},{7,5},{10,8},{11,9},{12,14},{13,15},{16,18},{17,... | collective-permute-start | bytes 3145736 | tf_op jit(solution)/shard_map/ppermute | solution.py:312
  232.5 0.6 collective-permute-done.13
  233.1 11.4 %collective-permute-done.14.refs_1_ = bf16[2,2,128,1024]{3,2,1,0:T(8,128)(2,1)} collective-permute-done((bf16[2,2,128,1024]{3,2,1,0:T(8,128)(2,1)}, bf16[2,2,128,1024]{3,2,1,0:T(8,128)(2,1)}, u32[]{:S(2)}, u32[]{:S(2)}) %collective-permute-start.14) | collective-permute-done | bytes 1048608 | tf_op jit(solution)/shard_map/ppermute | solution.py:269
  244.6 6.3 %second_product.7 = bf16[2,2,512,256]{3,2,1,0:T(8,128)(2,1)S(1)} custom-call(s32[1]{0:T(128)} %bitcast.1.pick_ref, bf16[2,2,2,512,512]{4,3,2,1,0:T(8,128)(2,1)S(1)} %first_product.1.own_ref, bf16[2,2,2,512,512]{4,3,2,1,0:T(8,128)(2,1)S(1)} %collective-permute-done.11.sib_ref, bf16[2,2,128,1024]{3,2,1,0:T(8,128)(2,1)} %collective-permute-done.12.refs_0_, ...), custom_call_target="tpu_custom_call" | custom-call | tf_op jit(solution)/shard_map/second_product/pallas_call | solution.py:104
  250.9 4.1 %collective-permute-start.20 = (bf16[2,2,512,256]{3,2,1,0:T(8,128)(2,1)S(1)}, bf16[2,2,512,256]{3,2,1,0:T(8,128)(2,1)}, u32[]{:S(2)}, u32[]{:S(2)}) collective-permute-start(bf16[2,2,512,256]{3,2,1,0:T(8,128)(2,1)S(1)} %second_product.7), channel_id=1, source_target_pairs={{0,2},{1,3},{4,6},{5,7},{10,8},{11,9},{14,12},{15,13},{16,18},{17,... | collective-permute-start | bytes 3145736 | tf_op jit(solution)/shard_map/ppermute | solution.py:312
  255.0 12.0 %collective-permute-done.15.refs_0_ = bf16[2,2,128,1024]{3,2,1,0:T(8,128)(2,1)} collective-permute-done((bf16[2,2,128,1024]{3,2,1,0:T(8,128)(2,1)}, bf16[2,2,128,1024]{3,2,1,0:T(8,128)(2,1)}, u32[]{:S(2)}, u32[]{:S(2)}) %collective-permute-start.15) | collective-permute-done | bytes 1048608 | tf_op jit(solution)/shard_map/ppermute | solution.py:269
  267.0 2.2 copy-done.1
  269.2 2.2 copy-done.3
  271.4 4.0 %second_product.8.refs_0_ = bf16[2,2,512,128]{3,2,1,0:T(8,128)(2,1)S(1)} custom-call(s32[1]{0:T(128)} %bitcast.1.pick_ref, bf16[2,2,2,512,512]{4,3,2,1,0:T(8,128)(2,1)S(1)} %copy-done.1, bf16[2,2,2,512,512]{4,3,2,1,0:T(8,128)(2,1)S(1)} %copy-done.3, bf16[2,2,128,1024]{3,2,1,0:T(8,128)(2,1)} %collective-permute-done.15.refs_0_), custom_call_target="tpu_custom_call" | custom-call | tf_op jit(solution)/shard_map/second_product/pallas_call | solution.py:104
  275.4 1.3 collective-permute-start.16
  276.7 1.3 collective-permute-start.17
  278.0 1.3 collective-permute-start.18
  279.4 3.8 %select_convert_fusion = (bf16[2,2,512,256]{3,2,1,0:T(8,128)(2,1)}, f32[2,2,512,256]{3,2,1,0:T(8,128)S(1)}) fusion(bf16[2,2,512,256]{3,2,1,0:T(8,128)(2,1)S(1)} %copy-done.29, bf16[2,2,512,256]{3,2,1,0:T(8,128)(2,1)S(1)} %second_product.5, bf16[2,2,512,256]{3,2,1,0:T(8,128)(2,1)} %collective-permute-done.19, bf16[2,2,512,256]{3,2,1,0:T(8,128)(2,1)S(1)} %copy-done.5, ...), kind=kLoop, calls=%fused_computation.2 | loop fusion | flops 7340032 | bytes 9437188 | tf_op jit(solution)/shard_map/convert_element_type | solution.py:346
  283.2 1.2 collective-permute-start.25
  284.3 5.1 %collective-permute-done.16.refs_1_ = bf16[2,2,512,128]{3,2,1,0:T(8,128)(2,1)S(1)} collective-permute-done((bf16[2,2,512,128]{3,2,1,0:T(8,128)(2,1)S(1)}, bf16[2,2,512,128]{3,2,1,0:T(8,128)(2,1)S(1)}, u32[]{:S(2)}, u32[]{:S(2)}) %collective-permute-start.16) | collective-permute-done | bytes 524320 | tf_op jit(solution)/shard_map/ppermute | solution.py:319
  289.4 1.5 collective-permute-done.17.refs_2_
  291.0 4.2 %second_product.9.refs_0_ = bf16[2,2,512,128]{3,2,1,0:T(8,128)(2,1)S(1)} custom-call(s32[1]{0:T(128)} %bitcast.1.pick_ref, bf16[2,2,2,512,512]{4,3,2,1,0:T(8,128)(2,1)S(1)} %copy-done.1, bf16[2,2,2,512,512]{4,3,2,1,0:T(8,128)(2,1)S(1)} %copy-done.3, bf16[2,2,128,1024]{3,2,1,0:T(8,128)(2,1)} %collective-permute-done.21.refs_0_), custom_call_target="tpu_custom_call" | custom-call | tf_op jit(solution)/shard_map/second_product/pallas_call | solution.py:104
  295.3 1.3 collective-permute-start.22
  296.6 1.3 collective-permute-start.23
  297.9 1.3 collective-permute-start.24
  299.2 0.1 pad_add_fusion.pick_ref
  299.3 1.0 copy-done.20
  300.3 1.0 copy-done.22
  301.3 1.0 copy-done.24
  302.4 4.0 %finish.1.refs_4_ = f32[2,2,512,512]{3,2,1,0:T(8,128)} custom-call(s32[2]{0:T(128)S(1)} %pad_add_fusion.pick_ref, f32[2,2,512,256]{3,2,1,0:T(8,128)S(1)} %get-tuple-element.26.mine_ref, bf16[2,2,512,256]{3,2,1,0:T(8,128)(2,1)} %collective-permute-done.25.siblings_ref, bf16[2,2,512,128]{3,2,1,0:T(8,128)(2,1)S(1)} %copy-done.8, ...), custom_call_target="tpu_custom_call" | custom-call | tf_op jit(solution)/shard_map/finish/pallas_call | solution.py:145
  306.3 2.6 collective-permute-done.22.refs_1_
  309.0 1.9 collective-permute-done.23.refs_2_
  310.9 2.8 finish_last.1
  (69 shorter events, 0.3 us)
Async XLA Ops:
  2.7 2.9 collective-permute-start
  2.8 28.3 %collective-permute-start.3 = (bf16[1,2,512,512]{3,2,1,0:T(8,128)(2,1)S(1)}, bf16[1,2,512,512]{3,2,1,0:T(8,128)(2,1)S(1)}, u32[]{:S(2)}, u32[]{:S(2)}) collective-permute-start(bf16[1,2,512,512]{3,2,1,0:T(8,128)(2,1)S(1)} %get-tuple-element.31.refs_0_), channel_id=1, source_target_pairs={{0,4},{4,8},{8,12},{12,0},{1,5},{5,9},{9,13},{13,1},{2,6},{6,10},{... | collective-permute-start | bytes 3145736 | tf_op jit(solution)/shard_map/ppermute | solution.py:269
  5.6 6.5 %copy-start.9 = (bf16[1,2,512,512]{3,2,1,0:T(8,128)(2,1)}, bf16[1,2,512,512]{3,2,1,0:T(8,128)(2,1)S(1)}, u32[]{:S(2)}) copy-start(bf16[1,2,512,512]{3,2,1,0:T(8,128)(2,1)S(1)} %collective-permute-done.refs_1_) | copy-start | bytes 3145732
  9.5 67.6 %copy-start.25 = (bf16[2,512,2,1024]{3,1,2,0:T(8,128)(2,1)}, bf16[2,512,2,1024]{3,1,2,0:T(8,128)(2,1)S(1)}, u32[]{:S(2)}) copy-start(bf16[2,512,2,1024]{3,1,2,0:T(8,128)(2,1)S(1)} %copy.9) | copy-start | bytes 12582916
  9.7 67.9 %copy-start.27 = (bf16[2,2,256,1024]{3,2,1,0:T(8,128)(2,1)}, bf16[2,2,256,1024]{3,2,1,0:T(8,128)(2,1)S(1)}, u32[]{:S(2)}) copy-start(bf16[2,2,256,1024]{3,2,1,0:T(8,128)(2,1)S(1)} %dynamic-slice_bitcast_fusion) | copy-start | bytes 6291460
  9.7 67.3 %collective-permute-start.1 = (bf16[2,2,256,1024]{3,2,1,0:T(8,128)(2,1)S(1)}, bf16[2,2,256,1024]{3,2,1,0:T(8,128)(2,1)}, u32[]{:S(2)}, u32[]{:S(2)}) collective-permute-start(bf16[2,2,256,1024]{3,2,1,0:T(8,128)(2,1)S(1)} %dynamic-slice_bitcast_fusion), channel_id=1, source_target_pairs={{0,2},{2,0},{1,3},{3,1},{4,6},{6,4},{5,7},{7,5},{8,10},{10,8},{9,1... | collective-permute-start | bytes 6291464 | tf_op jit(solution)/shard_map/ppermute | solution.py:272
  12.1 41.5 %collective-permute-start.2 = (bf16[1,2,512,512]{3,2,1,0:T(8,128)(2,1)S(1)}, bf16[1,2,512,512]{3,2,1,0:T(8,128)(2,1)}, u32[]{:S(2)}, u32[]{:S(2)}) collective-permute-start(bf16[1,2,512,512]{3,2,1,0:T(8,128)(2,1)S(1)} %collective-permute-done.refs_1_), channel_id=1, source_target_pairs={{0,4},{4,8},{8,12},{12,0},{1,5},{5,9},{9,13},{13,1},{2,6},{6,10},{... | collective-permute-start | bytes 3145736 | tf_op jit(solution)/shard_map/ppermute | solution.py:269
  31.1 44.9 %collective-permute-start.4 = (bf16[1,2,512,512]{3,2,1,0:T(8,128)(2,1)S(1)}, bf16[1,2,512,512]{3,2,1,0:T(8,128)(2,1)S(1)}, u32[]{:S(2)}, u32[]{:S(2)}) collective-permute-start(bf16[1,2,512,512]{3,2,1,0:T(8,128)(2,1)S(1)} %collective-permute-done.3.refs_2_), channel_id=1, source_target_pairs={{0,4},{4,8},{8,12},{12,0},{1,5},{5,9},{9,13},{13,1},{2,6},{6,10},{... | collective-permute-start | bytes 3145736 | tf_op jit(solution)/shard_map/ppermute | solution.py:269
  31.1 1.0 copy-start.11
  76.0 1.0 copy-start.13
  77.0 27.4 %collective-permute-start.5 = (bf16[2,2,256,1024]{3,2,1,0:T(8,128)(2,1)}, bf16[2,2,256,1024]{3,2,1,0:T(8,128)(2,1)}, u32[]{:S(2)}, u32[]{:S(2)}) collective-permute-start(bf16[2,2,256,1024]{3,2,1,0:T(8,128)(2,1)} %collective-permute-done.1), channel_id=1, source_target_pairs={{0,1},{1,0},{2,3},{3,2},{4,5},{5,4},{6,7},{7,6},{8,9},{9,8},{10,11... | collective-permute-start | bytes 6291464 | tf_op jit(solution)/shard_map/ppermute | solution.py:210
  77.6 26.8 %collective-permute-start.6 = (bf16[1,2,512,512]{3,2,1,0:T(8,128)(2,1)}, bf16[1,2,512,512]{3,2,1,0:T(8,128)(2,1)}, u32[]{:S(2)}, u32[]{:S(2)}) collective-permute-start(bf16[1,2,512,512]{3,2,1,0:T(8,128)(2,1)} %collective-permute-done.2.refs_3_), channel_id=1, source_target_pairs={{0,4},{4,8},{8,12},{12,0},{1,5},{5,9},{9,13},{13,1},{2,6},{6,10},{... | collective-permute-start | bytes 3145736 | tf_op jit(solution)/shard_map/ppermute | solution.py:269
  79.4 47.4 %collective-permute-start.7 = (bf16[1,2,512,512]{3,2,1,0:T(8,128)(2,1)}, bf16[1,2,512,512]{3,2,1,0:T(8,128)(2,1)S(1)}, u32[]{:S(2)}, u32[]{:S(2)}) collective-permute-start(bf16[1,2,512,512]{3,2,1,0:T(8,128)(2,1)} %copy-done.13), channel_id=1, source_target_pairs={{0,4},{4,8},{8,12},{12,0},{1,5},{5,9},{9,13},{13,1},{2,6},{6,10},{... | collective-permute-start | bytes 3145736 | tf_op jit(solution)/shard_map/ppermute | solution.py:269
  104.4 44.8 %collective-permute-start.8 = (bf16[1,2,512,512]{3,2,1,0:T(8,128)(2,1)}, bf16[1,2,512,512]{3,2,1,0:T(8,128)(2,1)S(1)}, u32[]{:S(2)}, u32[]{:S(2)}) collective-permute-start(bf16[1,2,512,512]{3,2,1,0:T(8,128)(2,1)} %collective-permute-done.6.refs_5_), channel_id=1, source_target_pairs={{0,4},{4,8},{8,12},{12,0},{1,5},{5,9},{9,13},{13,1},{2,6},{6,10},{... | collective-permute-start | bytes 3145736 | tf_op jit(solution)/shard_map/ppermute | solution.py:269
  104.5 5.3 %copy-start.26 = (bf16[2,512,2,1024]{3,1,2,0:T(8,128)(2,1)S(1)}, bf16[2,512,2,1024]{3,1,2,0:T(8,128)(2,1)}, u32[]{:S(2)}) copy-start(bf16[2,512,2,1024]{3,1,2,0:T(8,128)(2,1)} %copy-done.25) | copy-start | bytes 12582916
  109.8 40.5 %copy-start.30 = (f32[2,2,2,2]{3,2,1,0:T(2,128)S(1)}, f32[2,2,2,2]{3,2,1,0:T(2,128)}, u32[]{:S(2)}) copy-start(f32[2,2,2,2]{3,2,1,0:T(2,128)} %param.5) | copy-start | bytes 196
  126.8 1.0 copy-start.15
  127.8 52.1 %collective-permute-start.9 = (bf16[2,2,128,1024]{3,2,1,0:T(8,128)(2,1)S(1)}, bf16[2,2,128,1024]{3,2,1,0:T(8,128)(2,1)}, u32[]{:S(2)}, u32[]{:S(2)}) collective-permute-start(bf16[2,2,128,1024]{3,2,1,0:T(8,128)(2,1)S(1)} %get-tuple-element.17.refs_0_), channel_id=1, source_target_pairs={{0,4},{4,8},{8,12},{12,0},{1,5},{5,9},{9,13},{13,1},{2,6},{6,10},{... | collective-permute-start | bytes 3145736 | tf_op jit(solution)/shard_map/ppermute | solution.py:269
  149.3 1.0 copy-start.17
  150.3 44.1 %collective-permute-start.10 = (bf16[2,2,128,1024]{3,2,1,0:T(8,128)(2,1)S(1)}, bf16[2,2,128,1024]{3,2,1,0:T(8,128)(2,1)}, u32[]{:S(2)}, u32[]{:S(2)}) collective-permute-start(bf16[2,2,128,1024]{3,2,1,0:T(8,128)(2,1)S(1)} %get-tuple-element.18.refs_1_), channel_id=1, source_target_pairs={{0,4},{4,8},{8,12},{12,0},{1,5},{5,9},{9,13},{13,1},{2,6},{6,10},{... | collective-permute-start | bytes 3145736 | tf_op jit(solution)/shard_map/ppermute | solution.py:269
  150.4 1.2 copy-start.10
  151.6 1.2 copy-start.12
  152.8 1.2 copy-start.14
  154.0 1.2 copy-start.16
  155.3 1.2 copy-start.18
  179.9 64.7 %copy-start = (bf16[2,2,2,512,512]{4,3,2,1,0:T(8,128)(2,1)}, bf16[2,2,2,512,512]{4,3,2,1,0:T(8,128)(2,1)S(1)}, u32[]{:S(2)}) copy-start(bf16[2,2,2,512,512]{4,3,2,1,0:T(8,128)(2,1)S(1)} %first_product.1.own_ref) | copy-start | bytes 12582916
  194.3 7.6 %collective-permute-start.11 = (bf16[2,2,2,512,512]{4,3,2,1,0:T(8,128)(2,1)S(1)}, bf16[2,2,2,512,512]{4,3,2,1,0:T(8,128)(2,1)S(1)}, u32[]{:S(2)}, u32[]{:S(2)}) collective-permute-start(bf16[2,2,2,512,512]{4,3,2,1,0:T(8,128)(2,1)S(1)} %first_product.1.own_ref), channel_id=1, source_target_pairs={{0,1},{1,0},{2,3},{3,2},{4,5},{5,4},{6,7},{7,6},{8,9},{9,8},{10,11... | collective-permute-start | bytes 12582920 | tf_op jit(solution)/shard_map/ppermute | solution.py:210
  195.2 26.9 %collective-permute-start.12 = (bf16[2,2,128,1024]{3,2,1,0:T(8,128)(2,1)}, bf16[2,2,128,1024]{3,2,1,0:T(8,128)(2,1)}, u32[]{:S(2)}, u32[]{:S(2)}) collective-permute-start(bf16[2,2,128,1024]{3,2,1,0:T(8,128)(2,1)} %collective-permute-done.9.refs_0_), channel_id=1, source_target_pairs={{0,4},{4,8},{8,12},{12,0},{1,5},{5,9},{9,13},{13,1},{2,6},{6,10},{... | collective-permute-start | bytes 3145736 | tf_op jit(solution)/shard_map/ppermute | solution.py:269
  202.0 42.6 %copy-start.2 = (bf16[2,2,2,512,512]{4,3,2,1,0:T(8,128)(2,1)}, bf16[2,2,2,512,512]{4,3,2,1,0:T(8,128)(2,1)S(1)}, u32[]{:S(2)}) copy-start(bf16[2,2,2,512,512]{4,3,2,1,0:T(8,128)(2,1)S(1)} %collective-permute-done.11.sib_ref) | copy-start | bytes 12582916
  206.8 26.4 %collective-permute-start.13 = (bf16[2,2,512,256]{3,2,1,0:T(8,128)(2,1)S(1)}, bf16[2,2,512,256]{3,2,1,0:T(8,128)(2,1)S(1)}, u32[]{:S(2)}, u32[]{:S(2)}) collective-permute-start(bf16[2,2,512,256]{3,2,1,0:T(8,128)(2,1)S(1)} %second_product.5), channel_id=1, source_target_pairs={{2,0},{3,1},{6,4},{7,5},{8,10},{9,11},{12,14},{13,15},{18,16},{19,... | collective-permute-start | bytes 3145736 | tf_op jit(solution)/shard_map/ppermute | solution.py:312
  208.1 36.5 %collective-permute-start.14 = (bf16[2,2,128,1024]{3,2,1,0:T(8,128)(2,1)}, bf16[2,2,128,1024]{3,2,1,0:T(8,128)(2,1)}, u32[]{:S(2)}, u32[]{:S(2)}) collective-permute-start(bf16[2,2,128,1024]{3,2,1,0:T(8,128)(2,1)} %collective-permute-done.10.refs_1_), channel_id=1, source_target_pairs={{0,4},{4,8},{8,12},{12,0},{1,5},{5,9},{9,13},{13,1},{2,6},{6,10},{... | collective-permute-start | bytes 3145736 | tf_op jit(solution)/shard_map/ppermute | solution.py:269
  222.1 44.9 %collective-permute-start.15 = (bf16[2,2,128,1024]{3,2,1,0:T(8,128)(2,1)}, bf16[2,2,128,1024]{3,2,1,0:T(8,128)(2,1)}, u32[]{:S(2)}, u32[]{:S(2)}) collective-permute-start(bf16[2,2,128,1024]{3,2,1,0:T(8,128)(2,1)} %collective-permute-done.12.refs_0_), channel_id=1, source_target_pairs={{0,4},{4,8},{8,12},{12,0},{1,5},{5,9},{9,13},{13,1},{2,6},{6,10},{... | collective-permute-start | bytes 3145736 | tf_op jit(solution)/shard_map/ppermute | solution.py:269
  228.4 22.5 %copy-start.4 = (bf16[2,2,512,256]{3,2,1,0:T(8,128)(2,1)}, bf16[2,2,512,256]{3,2,1,0:T(8,128)(2,1)S(1)}, u32[]{:S(2)}) copy-start(bf16[2,2,512,256]{3,2,1,0:T(8,128)(2,1)S(1)} %second_product.6) | copy-start | bytes 3145732
  228.4 49.6 %collective-permute-start.19 = (bf16[2,2,512,256]{3,2,1,0:T(8,128)(2,1)S(1)}, bf16[2,2,512,256]{3,2,1,0:T(8,128)(2,1)}, u32[]{:S(2)}, u32[]{:S(2)}) collective-permute-start(bf16[2,2,512,256]{3,2,1,0:T(8,128)(2,1)S(1)} %second_product.6), channel_id=1, source_target_pairs={{0,2},{1,3},{6,4},{7,5},{10,8},{11,9},{12,14},{13,15},{16,18},{17,... | collective-permute-start | bytes 3145736 | tf_op jit(solution)/shard_map/ppermute | solution.py:312
  233.1 17.8 %copy-start.28 = (bf16[2,2,512,256]{3,2,1,0:T(8,128)(2,1)}, bf16[2,2,512,256]{3,2,1,0:T(8,128)(2,1)S(1)}, u32[]{:S(2)}) copy-start(bf16[2,2,512,256]{3,2,1,0:T(8,128)(2,1)S(1)} %collective-permute-done.13) | copy-start | bytes 3145732
  250.9 24.5 %copy-start.6 = (bf16[2,2,512,256]{3,2,1,0:T(8,128)(2,1)}, bf16[2,2,512,256]{3,2,1,0:T(8,128)(2,1)S(1)}, u32[]{:S(2)}) copy-start(bf16[2,2,512,256]{3,2,1,0:T(8,128)(2,1)S(1)} %second_product.7) | copy-start | bytes 3145732
  250.9 28.4 %collective-permute-start.20 = (bf16[2,2,512,256]{3,2,1,0:T(8,128)(2,1)S(1)}, bf16[2,2,512,256]{3,2,1,0:T(8,128)(2,1)}, u32[]{:S(2)}, u32[]{:S(2)}) collective-permute-start(bf16[2,2,512,256]{3,2,1,0:T(8,128)(2,1)S(1)} %second_product.7), channel_id=1, source_target_pairs={{0,2},{1,3},{4,6},{5,7},{10,8},{11,9},{14,12},{15,13},{16,18},{17,... | collective-permute-start | bytes 3145736 | tf_op jit(solution)/shard_map/ppermute | solution.py:312
  255.0 36.0 %collective-permute-start.21 = (bf16[2,2,128,1024]{3,2,1,0:T(8,128)(2,1)}, bf16[2,2,128,1024]{3,2,1,0:T(8,128)(2,1)}, u32[]{:S(2)}, u32[]{:S(2)}) collective-permute-start(bf16[2,2,128,1024]{3,2,1,0:T(8,128)(2,1)} %collective-permute-done.14.refs_1_), channel_id=1, source_target_pairs={{0,4},{4,8},{8,12},{12,0},{1,5},{5,9},{9,13},{13,1},{2,6},{6,10},{... | collective-permute-start | bytes 3145736 | tf_op jit(solution)/shard_map/ppermute | solution.py:269
  267.0 2.2 copy-start.1
  269.2 2.2 copy-start.3
  271.4 7.9 %copy-start.5 = (bf16[2,2,512,256]{3,2,1,0:T(8,128)(2,1)S(1)}, bf16[2,2,512,256]{3,2,1,0:T(8,128)(2,1)}, u32[]{:S(2)}) copy-start(bf16[2,2,512,256]{3,2,1,0:T(8,128)(2,1)} %copy-done.4) | copy-start | bytes 3145732
  271.4 7.9 %copy-start.29 = (bf16[2,2,512,256]{3,2,1,0:T(8,128)(2,1)S(1)}, bf16[2,2,512,256]{3,2,1,0:T(8,128)(2,1)}, u32[]{:S(2)}) copy-start(bf16[2,2,512,256]{3,2,1,0:T(8,128)(2,1)} %copy-done.28) | copy-start | bytes 3145732
  275.4 7.7 %copy-start.7 = (bf16[2,2,512,128]{3,2,1,0:T(8,128)(2,1)}, bf16[2,2,512,128]{3,2,1,0:T(8,128)(2,1)S(1)}, u32[]{:S(2)}) copy-start(bf16[2,2,512,128]{3,2,1,0:T(8,128)(2,1)S(1)} %second_product.8.refs_0_) | copy-start | bytes 1572868
  275.4 14.0 %collective-permute-start.16 = (bf16[2,2,512,128]{3,2,1,0:T(8,128)(2,1)S(1)}, bf16[2,2,512,128]{3,2,1,0:T(8,128)(2,1)S(1)}, u32[]{:S(2)}, u32[]{:S(2)}) collective-permute-start(bf16[2,2,512,128]{3,2,1,0:T(8,128)(2,1)S(1)} %second_product.8.refs_0_), channel_id=1, source_target_pairs={{3,1},{4,6},{9,11},{14,12},{19,17},{20,22},{25,27},{30,28}} | collective-permute-start | bytes 1572872 | tf_op jit(solution)/shard_map/ppermute | solution.py:319
  276.7 14.2 %collective-permute-start.17 = (bf16[2,2,512,128]{3,2,1,0:T(8,128)(2,1)S(1)}, bf16[2,2,512,128]{3,2,1,0:T(8,128)(2,1)S(1)}, u32[]{:S(2)}, u32[]{:S(2)}) collective-permute-start(bf16[2,2,512,128]{3,2,1,0:T(8,128)(2,1)S(1)} %second_product.8.refs_0_), channel_id=1, source_target_pairs={{2,1},{5,6},{8,11},{15,12},{18,17},{21,22},{24,27},{31,28}} | collective-permute-start | bytes 1572872 | tf_op jit(solution)/shard_map/ppermute | solution.py:319
  278.0 12.9 %collective-permute-start.18 = (bf16[2,2,512,128]{3,2,1,0:T(8,128)(2,1)S(1)}, bf16[2,2,512,128]{3,2,1,0:T(8,128)(2,1)S(1)}, u32[]{:S(2)}, u32[]{:S(2)}) collective-permute-start(bf16[2,2,512,128]{3,2,1,0:T(8,128)(2,1)S(1)} %second_product.8.refs_0_), channel_id=1, source_target_pairs={{0,1},{7,6},{10,11},{13,12},{16,17},{23,22},{26,27},{29,28}} | collective-permute-start | bytes 1572872 | tf_op jit(solution)/shard_map/ppermute | solution.py:319
  283.2 16.1 %collective-permute-start.25 = (bf16[2,2,512,256]{3,2,1,0:T(8,128)(2,1)}, bf16[2,2,512,256]{3,2,1,0:T(8,128)(2,1)}, u32[]{:S(2)}, u32[]{:S(2)}) collective-permute-start(bf16[2,2,512,256]{3,2,1,0:T(8,128)(2,1)} %get-tuple-element.25), channel_id=1, source_target_pairs={{0,1},{1,0},{2,3},{3,2},{4,5},{5,4},{6,7},{7,6},{8,9},{9,8},{10,11... | collective-permute-start | bytes 3145736 | tf_op jit(solution)/shard_map/ppermute | solution.py:210
  289.4 5.8 %copy-start.19 = (bf16[2,2,512,128]{3,2,1,0:T(8,128)(2,1)}, bf16[2,2,512,128]{3,2,1,0:T(8,128)(2,1)S(1)}, u32[]{:S(2)}) copy-start(bf16[2,2,512,128]{3,2,1,0:T(8,128)(2,1)S(1)} %collective-permute-done.16.refs_1_) | copy-start | bytes 1572868
  291.0 4.3 %copy-start.21 = (bf16[2,2,512,128]{3,2,1,0:T(8,128)(2,1)}, bf16[2,2,512,128]{3,2,1,0:T(8,128)(2,1)S(1)}, u32[]{:S(2)}) copy-start(bf16[2,2,512,128]{3,2,1,0:T(8,128)(2,1)S(1)} %collective-permute-done.17.refs_2_) | copy-start | bytes 1572868
  291.0 4.3 %copy-start.23 = (bf16[2,2,512,128]{3,2,1,0:T(8,128)(2,1)}, bf16[2,2,512,128]{3,2,1,0:T(8,128)(2,1)S(1)}, u32[]{:S(2)}) copy-start(bf16[2,2,512,128]{3,2,1,0:T(8,128)(2,1)S(1)} %collective-permute-done.18.refs_3_) | copy-start | bytes 1572868
  291.0 8.3 %copy-start.8 = (bf16[2,2,512,128]{3,2,1,0:T(8,128)(2,1)S(1)}, bf16[2,2,512,128]{3,2,1,0:T(8,128)(2,1)}, u32[]{:S(2)}) copy-start(bf16[2,2,512,128]{3,2,1,0:T(8,128)(2,1)} %copy-done.7) | copy-start | bytes 1572868
  295.3 13.7 %collective-permute-start.22 = (bf16[2,2,512,128]{3,2,1,0:T(8,128)(2,1)S(1)}, bf16[2,2,512,128]{3,2,1,0:T(8,128)(2,1)}, u32[]{:S(2)}, u32[]{:S(2)}) collective-permute-start(bf16[2,2,512,128]{3,2,1,0:T(8,128)(2,1)S(1)} %second_product.9.refs_0_), channel_id=1, source_target_pairs={{3,1},{4,6},{9,11},{14,12},{19,17},{20,22},{25,27},{30,28}} | collective-permute-start | bytes 1572872 | tf_op jit(solution)/shard_map/ppermute | solution.py:319
  296.6 14.3 %collective-permute-start.23 = (bf16[2,2,512,128]{3,2,1,0:T(8,128)(2,1)S(1)}, bf16[2,2,512,128]{3,2,1,0:T(8,128)(2,1)}, u32[]{:S(2)}, u32[]{:S(2)}) collective-permute-start(bf16[2,2,512,128]{3,2,1,0:T(8,128)(2,1)S(1)} %second_product.9.refs_0_), channel_id=1, source_target_pairs={{2,1},{5,6},{8,11},{15,12},{18,17},{21,22},{24,27},{31,28}} | collective-permute-start | bytes 1572872 | tf_op jit(solution)/shard_map/ppermute | solution.py:319
  297.9 13.1 %collective-permute-start.24 = (bf16[2,2,512,128]{3,2,1,0:T(8,128)(2,1)S(1)}, bf16[2,2,512,128]{3,2,1,0:T(8,128)(2,1)}, u32[]{:S(2)}, u32[]{:S(2)}) collective-permute-start(bf16[2,2,512,128]{3,2,1,0:T(8,128)(2,1)S(1)} %second_product.9.refs_0_), channel_id=1, source_target_pairs={{0,1},{7,6},{10,11},{13,12},{16,17},{23,22},{26,27},{29,28}} | collective-permute-start | bytes 1572872 | tf_op jit(solution)/shard_map/ppermute | solution.py:319
  299.3 1.0 copy-start.20
  300.3 1.0 copy-start.22
  301.3 1.0 copy-start.24

commit v15 on v14

--- a/solution.py
+++ b/solution.py
@@ -8,7 +8,7 @@
 
 F32 = jnp.float32
 BF16 = jnp.bfloat16
-VMEM_BYTES = 40 * 1024 * 1024
+VMEM_BYTES = 26 * 1024 * 1024
 LIGHT = pl.CostEstimate(flops=0, bytes_accessed=0, transcendentals=0)
 
 

time: 315 us -> 315 us (level)
  local copies, waits for them, and re-layouts: 26.2 us -> 29.6 us
    unnamed x62 -> x66, local copies, waits for them, and re-layouts: 17.6 us -> 21 us
where the time goes in v15:
time: 315 us; the launch traced here: 314 us
  waiting for transfers between devices  188 us (60%)
  Pallas kernels  55.1 us (17%)
  local copies, waits for them, and re-layouts  29.6 us (9%)
  starting transfers between devices  27.5 us (9%)
  other arithmetic  13.5 us (4%)
    ppermute x12, waiting for transfers between devices, ring(): lax.ppermute(value, 'row', [(r, (r + 1) % row_count) for r in range(row_c...  169 us
    pallas_call x5, Pallas kernels, second_product(): pl.pallas_call(second_kernel, grid=(mpo_count,), in_specs=[pl.BlockSpec(m...  25.6 us
    pallas_call x1, Pallas kernels, first_product(): pl.pallas_call(functools.partial(first_kernel, w_local), grid=(rows // ro...  22.8 us
    unnamed x66, local copies, waits for them, and re-layouts  21 us
    ppermute x6, waiting for transfers between devices, send(): lax.ppermute(value, axes, [(place(r, 1 - c if turned else c, 1 - d if cro...  11.2 us
    ppermute x3, starting transfers between devices, turn_to_goal(): lax.ppermute(value, axes, [(place(r, 1 - c, d), place(r, c, d)) for r, (c...  9.5 us
    ppermute x6, starting transfers between devices, send(): lax.ppermute(value, axes, [(place(r, 1 - c if turned else c, 1 - d if cro...  8.02 us
    ppermute x4, waiting for transfers between devices, swap(): return lax.ppermute(value, 'depth', [(0, 1), (1, 0)])  6.86 us
  transfers between devices with their start and end apart: 26, of which 17 were waited for; matrix products, arithmetic and copies ran while one was open for 6% of the time, Pallas kernels for 17%

profile of v15, /device:TPU:1, one launch (start us, length us, event | category | flops | bytes accessed | tf_op | source)
XLA Modules:
  0.0 314.1 jit_solution(16682926842962476952)
XLA Ops:
  0.0 2.7 constant_dynamic-slice_fusion
  2.8 2.7 collective-permute-start.3
  5.6 3.9 %copy.9 = bf16[2,512,2,1024]{3,1,2,0:T(8,128)(2,1)S(1)} copy(bf16[2,512,2,1024]{3,2,1,0:T(2,128)(2,1)} %param.4) | data formatting | bytes 8388608 | tf_op jit(solution)/shard_map/optimization_barrier | solution.py:206
  9.5 0.2 dynamic-slice_bitcast_fusion
  9.7 2.4 collective-permute-start.1
  12.1 1.3 collective-permute-start.2
  13.4 17.7 %collective-permute-done.3.refs_2_ = bf16[1,2,512,512]{3,2,1,0:T(8,128)(2,1)S(1)} collective-permute-done((bf16[1,2,512,512]{3,2,1,0:T(8,128)(2,1)S(1)}, bf16[1,2,512,512]{3,2,1,0:T(8,128)(2,1)S(1)}, u32[]{:S(2)}, u32[]{:S(2)}) %collective-permute-start.3) | collective-permute-done | bytes 1048608 | tf_op jit(solution)/shard_map/ppermute | solution.py:269
  31.1 1.0 copy-done.13
  32.1 21.6 %collective-permute-done.2.refs_3_ = bf16[1,2,512,512]{3,2,1,0:T(8,128)(2,1)} collective-permute-done((bf16[1,2,512,512]{3,2,1,0:T(8,128)(2,1)S(1)}, bf16[1,2,512,512]{3,2,1,0:T(8,128)(2,1)}, u32[]{:S(2)}, u32[]{:S(2)}) %collective-permute-start.2) | collective-permute-done | bytes 1048608 | tf_op jit(solution)/shard_map/ppermute | solution.py:269
  53.6 22.4 %collective-permute-done.4.refs_4_ = bf16[1,2,512,512]{3,2,1,0:T(8,128)(2,1)S(1)} collective-permute-done((bf16[1,2,512,512]{3,2,1,0:T(8,128)(2,1)S(1)}, bf16[1,2,512,512]{3,2,1,0:T(8,128)(2,1)S(1)}, u32[]{:S(2)}, u32[]{:S(2)}) %collective-permute-start.4) | collective-permute-done | bytes 1048608 | tf_op jit(solution)/shard_map/ppermute | solution.py:269
  76.0 1.0 copy-done.15
  77.0 0.6 collective-permute-start.5
  77.6 1.8 fusion
  79.4 0.8 collective-permute-start.7
  80.2 24.2 %collective-permute-done.6.refs_5_ = bf16[1,2,512,512]{3,2,1,0:T(8,128)(2,1)} collective-permute-done((bf16[1,2,512,512]{3,2,1,0:T(8,128)(2,1)}, bf16[1,2,512,512]{3,2,1,0:T(8,128)(2,1)}, u32[]{:S(2)}, u32[]{:S(2)}) %collective-permute-start.6) | collective-permute-done | bytes 1048608 | tf_op jit(solution)/shard_map/ppermute | solution.py:269
  104.5 5.5 %maximum_select_fusion.1 = bf16[1,2,2,512,1024]{4,3,2,1,0:T(8,128)(2,1)S(1)} fusion(bf16[1,2,2,256,1024]{4,3,2,1,0:T(8,128)(2,1)} %bitcast.10, bf16[1,2,2,256,1024]{4,3,2,1,0:T(8,128)(2,1)} %bitcast.9, pred[]{:T(512)S(6)} %eq.23), kind=kLoop, calls=%fused_computation.1 | loop fusion | flops 18874368 | bytes 8388609 | tf_op jit(solution)/shard_map/jit(_where)/select_n | solution.py:273
  109.9 4.1 %maximum_select_fusion.site_ref = bf16[2,2,2,512,1024]{4,3,2,1,0:T(8,128)(2,1)} fusion(bf16[1,2,2,512,1024]{4,3,2,1,0:T(8,128)(2,1)S(1)} %maximum_select_fusion.1, bf16[1,2,2,512,1024]{4,3,2,1,0:T(8,128)(2,1)S(1)} %bitcast.15, pred[]{:T(512)S(6)} %eq.22), kind=kLoop, calls=%fused_computation | loop fusion | flops 12582912 | bytes 16777216 | tf_op jit(solution)/shard_map/jit(_where)/select_n | solution.py:290
  114.0 12.8 %collective-permute-done.7.refs_6_ = bf16[1,2,512,512]{3,2,1,0:T(8,128)(2,1)S(1)} collective-permute-done((bf16[1,2,512,512]{3,2,1,0:T(8,128)(2,1)}, bf16[1,2,512,512]{3,2,1,0:T(8,128)(2,1)S(1)}, u32[]{:S(2)}, u32[]{:S(2)}) %collective-permute-start.7) | collective-permute-done | bytes 1048608 | tf_op jit(solution)/shard_map/ppermute | solution.py:269
  126.8 1.0 copy-done.17
  127.8 21.5 %collective-permute-done.8.refs_7_ = bf16[1,2,512,512]{3,2,1,0:T(8,128)(2,1)S(1)} collective-permute-done((bf16[1,2,512,512]{3,2,1,0:T(8,128)(2,1)}, bf16[1,2,512,512]{3,2,1,0:T(8,128)(2,1)S(1)}, u32[]{:S(2)}, u32[]{:S(2)}) %collective-permute-start.8) | collective-permute-done | bytes 1048608 | tf_op jit(solution)/shard_map/ppermute | solution.py:269
  149.3 1.0 copy-done.19
  150.3 0.1 pad_add_fusion.1.block_ref
  150.4 3.4 %copy-done.5 = bf16[2,2,2,512,1024]{4,3,2,1,0:T(8,128)(2,1)S(1)} copy-done((bf16[2,2,2,512,1024]{4,3,2,1,0:T(8,128)(2,1)S(1)}, bf16[2,2,2,512,1024]{4,3,2,1,0:T(8,128)(2,1)}, u32[]{:S(2)}) %copy-start.5) | copy-done | bytes 8388632
  153.8 1.2 copy-done.12
  155.0 1.2 copy-done.14
  156.2 1.2 copy-done.16
  157.4 1.2 copy-done.18
  158.7 1.2 copy-done.20
  159.9 22.8 %first_product.1.own_ref = bf16[2,2,2,512,512]{4,3,2,1,0:T(8,128)(2,1)S(1)} custom-call(s32[4]{0:T(128)S(1)} %pad_add_fusion.1.block_ref, f32[2,2,2,2]{3,2,1,0:T(2,128)S(1)} %pad_maximum_fusion.mpo_ref, bf16[2,2,2,512,1024]{4,3,2,1,0:T(8,128)(2,1)S(1)} %copy-done.5, bf16[1,2,512,512]{3,2,1,0:T(8,128)(2,1)S(1)} %get-tuple-element.31.refs_0_, ...), custom_call_target="tpu_custom_call" | custom-call | tf_op jit(solution)/shard_map/first_product/pallas_call | solution.py:67
  182.7 11.6 %collective-permute-done.10.refs_1_ = bf16[2,2,128,1024]{3,2,1,0:T(8,128)(2,1)} collective-permute-done((bf16[2,2,128,1024]{3,2,1,0:T(8,128)(2,1)S(1)}, bf16[2,2,128,1024]{3,2,1,0:T(8,128)(2,1)}, u32[]{:S(2)}, u32[]{:S(2)}) %collective-permute-start.10) | collective-permute-done | bytes 1048608 | tf_op jit(solution)/shard_map/ppermute | solution.py:269
  194.3 0.8 collective-permute-start.11
  195.2 6.8 %collective-permute-done.11.sib_ref = bf16[2,2,2,512,512]{4,3,2,1,0:T(8,128)(2,1)S(1)} collective-permute-done((bf16[2,2,2,512,512]{4,3,2,1,0:T(8,128)(2,1)S(1)}, bf16[2,2,2,512,512]{4,3,2,1,0:T(8,128)(2,1)S(1)}, u32[]{:S(2)}, u32[]{:S(2)}) %collective-permute-start.11) | collective-permute-done | bytes 4194336 | tf_op jit(solution)/shard_map/ppermute | solution.py:210
  202.0 4.8 %second_product.5 = bf16[2,2,512,256]{3,2,1,0:T(8,128)(2,1)S(1)} custom-call(s32[1]{0:T(128)} %bitcast.1.pick_ref, bf16[2,2,2,512,512]{4,3,2,1,0:T(8,128)(2,1)S(1)} %first_product.1.own_ref, bf16[2,2,2,512,512]{4,3,2,1,0:T(8,128)(2,1)S(1)} %collective-permute-done.11.sib_ref, bf16[2,2,128,1024]{3,2,1,0:T(8,128)(2,1)S(1)} %get-tuple-element.17.refs_0_, ...), custom_call_target="tpu_custom_call" | custom-call | tf_op jit(solution)/shard_map/second_product/pallas_call | solution.py:104
  206.7 1.3 collective-permute-start.13
  208.1 14.0 %collective-permute-done.12.refs_0_ = bf16[2,2,128,1024]{3,2,1,0:T(8,128)(2,1)} collective-permute-done((bf16[2,2,128,1024]{3,2,1,0:T(8,128)(2,1)}, bf16[2,2,128,1024]{3,2,1,0:T(8,128)(2,1)}, u32[]{:S(2)}, u32[]{:S(2)}) %collective-permute-start.12) | collective-permute-done | bytes 1048608 | tf_op jit(solution)/shard_map/ppermute | solution.py:269
  222.1 6.3 %second_product.6 = bf16[2,2,512,256]{3,2,1,0:T(8,128)(2,1)S(1)} custom-call(s32[1]{0:T(128)} %bitcast.1.pick_ref, bf16[2,2,2,512,512]{4,3,2,1,0:T(8,128)(2,1)S(1)} %first_product.1.own_ref, bf16[2,2,2,512,512]{4,3,2,1,0:T(8,128)(2,1)S(1)} %collective-permute-done.11.sib_ref, bf16[2,2,128,1024]{3,2,1,0:T(8,128)(2,1)} %collective-permute-done.9.refs_0_, ...), custom_call_target="tpu_custom_call" | custom-call | tf_op jit(solution)/shard_map/second_product/pallas_call | solution.py:104
  228.4 4.1 %collective-permute-start.19 = (bf16[2,2,512,256]{3,2,1,0:T(8,128)(2,1)S(1)}, bf16[2,2,512,256]{3,2,1,0:T(8,128)(2,1)}, u32[]{:S(2)}, u32[]{:S(2)}) collective-permute-start(bf16[2,2,512,256]{3,2,1,0:T(8,128)(2,1)S(1)} %second_product.6), channel_id=1, source_target_pairs={{0,2},{1,3},{6,4},{7,5},{10,8},{11,9},{12,14},{13,15},{16,18},{17,... | collective-permute-start | bytes 3145736 | tf_op jit(solution)/shard_map/ppermute | solution.py:312
  232.5 0.6 collective-permute-done.13
  233.1 11.4 %collective-permute-done.14.refs_1_ = bf16[2,2,128,1024]{3,2,1,0:T(8,128)(2,1)} collective-permute-done((bf16[2,2,128,1024]{3,2,1,0:T(8,128)(2,1)}, bf16[2,2,128,1024]{3,2,1,0:T(8,128)(2,1)}, u32[]{:S(2)}, u32[]{:S(2)}) %collective-permute-start.14) | collective-permute-done | bytes 1048608 | tf_op jit(solution)/shard_map/ppermute | solution.py:269
  244.6 6.3 %second_product.7 = bf16[2,2,512,256]{3,2,1,0:T(8,128)(2,1)S(1)} custom-call(s32[1]{0:T(128)} %bitcast.1.pick_ref, bf16[2,2,2,512,512]{4,3,2,1,0:T(8,128)(2,1)S(1)} %first_product.1.own_ref, bf16[2,2,2,512,512]{4,3,2,1,0:T(8,128)(2,1)S(1)} %collective-permute-done.11.sib_ref, bf16[2,2,128,1024]{3,2,1,0:T(8,128)(2,1)} %collective-permute-done.12.refs_0_, ...), custom_call_target="tpu_custom_call" | custom-call | tf_op jit(solution)/shard_map/second_product/pallas_call | solution.py:104
  250.9 4.1 %collective-permute-start.20 = (bf16[2,2,512,256]{3,2,1,0:T(8,128)(2,1)S(1)}, bf16[2,2,512,256]{3,2,1,0:T(8,128)(2,1)}, u32[]{:S(2)}, u32[]{:S(2)}) collective-permute-start(bf16[2,2,512,256]{3,2,1,0:T(8,128)(2,1)S(1)} %second_product.7), channel_id=1, source_target_pairs={{0,2},{1,3},{4,6},{5,7},{10,8},{11,9},{14,12},{15,13},{16,18},{17,... | collective-permute-start | bytes 3145736 | tf_op jit(solution)/shard_map/ppermute | solution.py:312
  255.0 12.0 %collective-permute-done.15.refs_0_ = bf16[2,2,128,1024]{3,2,1,0:T(8,128)(2,1)} collective-permute-done((bf16[2,2,128,1024]{3,2,1,0:T(8,128)(2,1)}, bf16[2,2,128,1024]{3,2,1,0:T(8,128)(2,1)}, u32[]{:S(2)}, u32[]{:S(2)}) %collective-permute-start.15) | collective-permute-done | bytes 1048608 | tf_op jit(solution)/shard_map/ppermute | solution.py:269
  267.0 2.2 copy-done.1
  269.2 2.2 copy-done.4
  271.4 4.0 %second_product.8.refs_0_ = bf16[2,2,512,128]{3,2,1,0:T(8,128)(2,1)S(1)} custom-call(s32[1]{0:T(128)} %bitcast.1.pick_ref, bf16[2,2,2,512,512]{4,3,2,1,0:T(8,128)(2,1)S(1)} %copy-done.1, bf16[2,2,2,512,512]{4,3,2,1,0:T(8,128)(2,1)S(1)} %copy-done.4, bf16[2,2,128,1024]{3,2,1,0:T(8,128)(2,1)} %collective-permute-done.15.refs_0_), custom_call_target="tpu_custom_call" | custom-call | tf_op jit(solution)/shard_map/second_product/pallas_call | solution.py:104
  275.4 1.6 collective-permute-start.16
  277.0 1.3 collective-permute-start.17
  278.3 1.3 collective-permute-start.18
  279.6 3.8 %select_convert_fusion = (bf16[2,2,512,256]{3,2,1,0:T(8,128)(2,1)}, f32[2,2,512,256]{3,2,1,0:T(8,128)S(1)}) fusion(bf16[2,2,512,256]{3,2,1,0:T(8,128)(2,1)S(1)} %copy-done.31, bf16[2,2,512,256]{3,2,1,0:T(8,128)(2,1)S(1)} %second_product.5, bf16[2,2,512,256]{3,2,1,0:T(8,128)(2,1)} %collective-permute-done.19, bf16[2,2,512,256]{3,2,1,0:T(8,128)(2,1)S(1)} %copy-done.7, ...), kind=kLoop, calls=%fused_computation.2 | loop fusion | flops 7340032 | bytes 9437188 | tf_op jit(solution)/shard_map/convert_element_type | solution.py:346
  283.4 1.2 collective-permute-start.25
  284.6 5.1 %collective-permute-done.16.refs_1_ = bf16[2,2,512,128]{3,2,1,0:T(8,128)(2,1)S(1)} collective-permute-done((bf16[2,2,512,128]{3,2,1,0:T(8,128)(2,1)S(1)}, bf16[2,2,512,128]{3,2,1,0:T(8,128)(2,1)S(1)}, u32[]{:S(2)}, u32[]{:S(2)}) %collective-permute-start.16) | collective-permute-done | bytes 524320 | tf_op jit(solution)/shard_map/ppermute | solution.py:319
  289.7 1.5 collective-permute-done.17.refs_2_
  291.3 4.3 %second_product.9.refs_0_ = bf16[2,2,512,128]{3,2,1,0:T(8,128)(2,1)S(1)} custom-call(s32[1]{0:T(128)} %bitcast.1.pick_ref, bf16[2,2,2,512,512]{4,3,2,1,0:T(8,128)(2,1)S(1)} %copy-done.2, bf16[2,2,2,512,512]{4,3,2,1,0:T(8,128)(2,1)S(1)} %copy-done.4, bf16[2,2,128,1024]{3,2,1,0:T(8,128)(2,1)} %collective-permute-done.21.refs_0_), custom_call_target="tpu_custom_call" | custom-call | tf_op jit(solution)/shard_map/second_product/pallas_call | solution.py:104
  295.6 1.3 collective-permute-start.22
  296.9 1.3 collective-permute-start.23
  298.2 1.3 collective-permute-start.24
  299.5 0.1 pad_add_fusion.pick_ref
  299.5 1.0 copy-done.22
  300.6 1.0 copy-done.24
  301.6 1.0 copy-done.26
  302.7 4.0 %finish.1.refs_4_ = f32[2,2,512,512]{3,2,1,0:T(8,128)} custom-call(s32[2]{0:T(128)S(1)} %pad_add_fusion.pick_ref, f32[2,2,512,256]{3,2,1,0:T(8,128)S(1)} %get-tuple-element.26.mine_ref, bf16[2,2,512,256]{3,2,1,0:T(8,128)(2,1)} %collective-permute-done.25.siblings_ref, bf16[2,2,512,128]{3,2,1,0:T(8,128)(2,1)S(1)} %copy-done.10, ...), custom_call_target="tpu_custom_call" | custom-call | tf_op jit(solution)/shard_map/finish/pallas_call | solution.py:145
  306.6 2.6 collective-permute-done.22.refs_1_
  309.3 1.9 collective-permute-done.23.refs_2_
  311.2 2.8 finish_last.1
  (73 shorter events, 0.3 us)
Async XLA Ops:
  2.7 2.9 collective-permute-start
  2.8 28.3 %collective-permute-start.3 = (bf16[1,2,512,512]{3,2,1,0:T(8,128)(2,1)S(1)}, bf16[1,2,512,512]{3,2,1,0:T(8,128)(2,1)S(1)}, u32[]{:S(2)}, u32[]{:S(2)}) collective-permute-start(bf16[1,2,512,512]{3,2,1,0:T(8,128)(2,1)S(1)} %get-tuple-element.31.refs_0_), channel_id=1, source_target_pairs={{0,4},{4,8},{8,12},{12,0},{1,5},{5,9},{9,13},{13,1},{2,6},{6,10},{... | collective-permute-start | bytes 3145736 | tf_op jit(solution)/shard_map/ppermute | solution.py:269
  5.6 6.5 %copy-start.11 = (bf16[1,2,512,512]{3,2,1,0:T(8,128)(2,1)}, bf16[1,2,512,512]{3,2,1,0:T(8,128)(2,1)S(1)}, u32[]{:S(2)}) copy-start(bf16[1,2,512,512]{3,2,1,0:T(8,128)(2,1)S(1)} %collective-permute-done.refs_1_) | copy-start | bytes 3145732
  9.5 67.5 %copy-start.27 = (bf16[2,512,2,1024]{3,1,2,0:T(8,128)(2,1)}, bf16[2,512,2,1024]{3,1,2,0:T(8,128)(2,1)S(1)}, u32[]{:S(2)}) copy-start(bf16[2,512,2,1024]{3,1,2,0:T(8,128)(2,1)S(1)} %copy.9) | copy-start | bytes 12582916
  9.7 67.9 %copy-start.29 = (bf16[2,2,256,1024]{3,2,1,0:T(8,128)(2,1)}, bf16[2,2,256,1024]{3,2,1,0:T(8,128)(2,1)S(1)}, u32[]{:S(2)}) copy-start(bf16[2,2,256,1024]{3,2,1,0:T(8,128)(2,1)S(1)} %dynamic-slice_bitcast_fusion) | copy-start | bytes 6291460
  9.7 67.3 %collective-permute-start.1 = (bf16[2,2,256,1024]{3,2,1,0:T(8,128)(2,1)S(1)}, bf16[2,2,256,1024]{3,2,1,0:T(8,128)(2,1)}, u32[]{:S(2)}, u32[]{:S(2)}) collective-permute-start(bf16[2,2,256,1024]{3,2,1,0:T(8,128)(2,1)S(1)} %dynamic-slice_bitcast_fusion), channel_id=1, source_target_pairs={{0,2},{2,0},{1,3},{3,1},{4,6},{6,4},{5,7},{7,5},{8,10},{10,8},{9,1... | collective-permute-start | bytes 6291464 | tf_op jit(solution)/shard_map/ppermute | solution.py:272
  12.1 41.5 %collective-permute-start.2 = (bf16[1,2,512,512]{3,2,1,0:T(8,128)(2,1)S(1)}, bf16[1,2,512,512]{3,2,1,0:T(8,128)(2,1)}, u32[]{:S(2)}, u32[]{:S(2)}) collective-permute-start(bf16[1,2,512,512]{3,2,1,0:T(8,128)(2,1)S(1)} %collective-permute-done.refs_1_), channel_id=1, source_target_pairs={{0,4},{4,8},{8,12},{12,0},{1,5},{5,9},{9,13},{13,1},{2,6},{6,10},{... | collective-permute-start | bytes 3145736 | tf_op jit(solution)/shard_map/ppermute | solution.py:269
  31.1 44.9 %collective-permute-start.4 = (bf16[1,2,512,512]{3,2,1,0:T(8,128)(2,1)S(1)}, bf16[1,2,512,512]{3,2,1,0:T(8,128)(2,1)S(1)}, u32[]{:S(2)}, u32[]{:S(2)}) collective-permute-start(bf16[1,2,512,512]{3,2,1,0:T(8,128)(2,1)S(1)} %collective-permute-done.3.refs_2_), channel_id=1, source_target_pairs={{0,4},{4,8},{8,12},{12,0},{1,5},{5,9},{9,13},{13,1},{2,6},{6,10},{... | collective-permute-start | bytes 3145736 | tf_op jit(solution)/shard_map/ppermute | solution.py:269
  31.1 1.0 copy-start.13
  76.0 1.0 copy-start.15
  77.0 27.4 %collective-permute-start.5 = (bf16[2,2,256,1024]{3,2,1,0:T(8,128)(2,1)}, bf16[2,2,256,1024]{3,2,1,0:T(8,128)(2,1)}, u32[]{:S(2)}, u32[]{:S(2)}) collective-permute-start(bf16[2,2,256,1024]{3,2,1,0:T(8,128)(2,1)} %collective-permute-done.1), channel_id=1, source_target_pairs={{0,1},{1,0},{2,3},{3,2},{4,5},{5,4},{6,7},{7,6},{8,9},{9,8},{10,11... | collective-permute-start | bytes 6291464 | tf_op jit(solution)/shard_map/ppermute | solution.py:210
  77.6 26.8 %collective-permute-start.6 = (bf16[1,2,512,512]{3,2,1,0:T(8,128)(2,1)}, bf16[1,2,512,512]{3,2,1,0:T(8,128)(2,1)}, u32[]{:S(2)}, u32[]{:S(2)}) collective-permute-start(bf16[1,2,512,512]{3,2,1,0:T(8,128)(2,1)} %collective-permute-done.2.refs_3_), channel_id=1, source_target_pairs={{0,4},{4,8},{8,12},{12,0},{1,5},{5,9},{9,13},{13,1},{2,6},{6,10},{... | collective-permute-start | bytes 3145736 | tf_op jit(solution)/shard_map/ppermute | solution.py:269
  79.4 47.4 %collective-permute-start.7 = (bf16[1,2,512,512]{3,2,1,0:T(8,128)(2,1)}, bf16[1,2,512,512]{3,2,1,0:T(8,128)(2,1)S(1)}, u32[]{:S(2)}, u32[]{:S(2)}) collective-permute-start(bf16[1,2,512,512]{3,2,1,0:T(8,128)(2,1)} %copy-done.15), channel_id=1, source_target_pairs={{0,4},{4,8},{8,12},{12,0},{1,5},{5,9},{9,13},{13,1},{2,6},{6,10},{... | collective-permute-start | bytes 3145736 | tf_op jit(solution)/shard_map/ppermute | solution.py:269
  104.4 44.8 %collective-permute-start.8 = (bf16[1,2,512,512]{3,2,1,0:T(8,128)(2,1)}, bf16[1,2,512,512]{3,2,1,0:T(8,128)(2,1)S(1)}, u32[]{:S(2)}, u32[]{:S(2)}) collective-permute-start(bf16[1,2,512,512]{3,2,1,0:T(8,128)(2,1)} %collective-permute-done.6.refs_5_), channel_id=1, source_target_pairs={{0,4},{4,8},{8,12},{12,0},{1,5},{5,9},{9,13},{13,1},{2,6},{6,10},{... | collective-permute-start | bytes 3145736 | tf_op jit(solution)/shard_map/ppermute | solution.py:269
  104.4 5.5 %copy-start.28 = (bf16[2,512,2,1024]{3,1,2,0:T(8,128)(2,1)S(1)}, bf16[2,512,2,1024]{3,1,2,0:T(8,128)(2,1)}, u32[]{:S(2)}) copy-start(bf16[2,512,2,1024]{3,1,2,0:T(8,128)(2,1)} %copy-done.27) | copy-start | bytes 12582916
  109.9 40.4 %copy-start.32 = (f32[2,2,2,2]{3,2,1,0:T(2,128)S(1)}, f32[2,2,2,2]{3,2,1,0:T(2,128)}, u32[]{:S(2)}) copy-start(f32[2,2,2,2]{3,2,1,0:T(2,128)} %param.5) | copy-start | bytes 196
  126.8 1.0 copy-start.17
  127.8 54.9 %collective-permute-start.9 = (bf16[2,2,128,1024]{3,2,1,0:T(8,128)(2,1)S(1)}, bf16[2,2,128,1024]{3,2,1,0:T(8,128)(2,1)}, u32[]{:S(2)}, u32[]{:S(2)}) collective-permute-start(bf16[2,2,128,1024]{3,2,1,0:T(8,128)(2,1)S(1)} %get-tuple-element.17.refs_0_), channel_id=1, source_target_pairs={{0,4},{4,8},{8,12},{12,0},{1,5},{5,9},{9,13},{13,1},{2,6},{6,10},{... | collective-permute-start | bytes 3145736 | tf_op jit(solution)/shard_map/ppermute | solution.py:269
  149.3 1.0 copy-start.19
  150.3 44.0 %collective-permute-start.10 = (bf16[2,2,128,1024]{3,2,1,0:T(8,128)(2,1)S(1)}, bf16[2,2,128,1024]{3,2,1,0:T(8,128)(2,1)}, u32[]{:S(2)}, u32[]{:S(2)}) collective-permute-start(bf16[2,2,128,1024]{3,2,1,0:T(8,128)(2,1)S(1)} %get-tuple-element.18.refs_1_), channel_id=1, source_target_pairs={{0,4},{4,8},{8,12},{12,0},{1,5},{5,9},{9,13},{13,1},{2,6},{6,10},{... | collective-permute-start | bytes 3145736 | tf_op jit(solution)/shard_map/ppermute | solution.py:269
  150.4 3.4 %copy-start.5 = (bf16[2,2,2,512,1024]{4,3,2,1,0:T(8,128)(2,1)S(1)}, bf16[2,2,2,512,1024]{4,3,2,1,0:T(8,128)(2,1)}, u32[]{:S(2)}) copy-start(bf16[2,2,2,512,1024]{4,3,2,1,0:T(8,128)(2,1)} %maximum_select_fusion.site_ref) | copy-start | bytes 25165828
  153.8 1.2 copy-start.12
  155.0 1.2 copy-start.14
  156.2 1.2 copy-start.16
  157.4 1.2 copy-start.18
  158.7 1.2 copy-start.20
  182.7 61.9 %copy-start = (bf16[2,2,2,512,512]{4,3,2,1,0:T(8,128)(2,1)}, bf16[2,2,2,512,512]{4,3,2,1,0:T(8,128)(2,1)S(1)}, u32[]{:S(2)}) copy-start(bf16[2,2,2,512,512]{4,3,2,1,0:T(8,128)(2,1)S(1)} %first_product.1.own_ref) | copy-start | bytes 12582916
  194.3 7.6 %collective-permute-start.11 = (bf16[2,2,2,512,512]{4,3,2,1,0:T(8,128)(2,1)S(1)}, bf16[2,2,2,512,512]{4,3,2,1,0:T(8,128)(2,1)S(1)}, u32[]{:S(2)}, u32[]{:S(2)}) collective-permute-start(bf16[2,2,2,512,512]{4,3,2,1,0:T(8,128)(2,1)S(1)} %first_product.1.own_ref), channel_id=1, source_target_pairs={{0,1},{1,0},{2,3},{3,2},{4,5},{5,4},{6,7},{7,6},{8,9},{9,8},{10,11... | collective-permute-start | bytes 12582920 | tf_op jit(solution)/shard_map/ppermute | solution.py:210
  195.2 26.9 %collective-permute-start.12 = (bf16[2,2,128,1024]{3,2,1,0:T(8,128)(2,1)}, bf16[2,2,128,1024]{3,2,1,0:T(8,128)(2,1)}, u32[]{:S(2)}, u32[]{:S(2)}) collective-permute-start(bf16[2,2,128,1024]{3,2,1,0:T(8,128)(2,1)} %collective-permute-done.9.refs_0_), channel_id=1, source_target_pairs={{0,4},{4,8},{8,12},{12,0},{1,5},{5,9},{9,13},{13,1},{2,6},{6,10},{... | collective-permute-start | bytes 3145736 | tf_op jit(solution)/shard_map/ppermute | solution.py:269
  202.0 42.6 %copy-start.3 = (bf16[2,2,2,512,512]{4,3,2,1,0:T(8,128)(2,1)}, bf16[2,2,2,512,512]{4,3,2,1,0:T(8,128)(2,1)S(1)}, u32[]{:S(2)}) copy-start(bf16[2,2,2,512,512]{4,3,2,1,0:T(8,128)(2,1)S(1)} %collective-permute-done.11.sib_ref) | copy-start | bytes 12582916
  206.7 26.4 %collective-permute-start.13 = (bf16[2,2,512,256]{3,2,1,0:T(8,128)(2,1)S(1)}, bf16[2,2,512,256]{3,2,1,0:T(8,128)(2,1)S(1)}, u32[]{:S(2)}, u32[]{:S(2)}) collective-permute-start(bf16[2,2,512,256]{3,2,1,0:T(8,128)(2,1)S(1)} %second_product.5), channel_id=1, source_target_pairs={{2,0},{3,1},{6,4},{7,5},{8,10},{9,11},{12,14},{13,15},{18,16},{19,... | collective-permute-start | bytes 3145736 | tf_op jit(solution)/shard_map/ppermute | solution.py:312
  208.0 36.5 %collective-permute-start.14 = (bf16[2,2,128,1024]{3,2,1,0:T(8,128)(2,1)}, bf16[2,2,128,1024]{3,2,1,0:T(8,128)(2,1)}, u32[]{:S(2)}, u32[]{:S(2)}) collective-permute-start(bf16[2,2,128,1024]{3,2,1,0:T(8,128)(2,1)} %collective-permute-done.10.refs_1_), channel_id=1, source_target_pairs={{0,4},{4,8},{8,12},{12,0},{1,5},{5,9},{9,13},{13,1},{2,6},{6,10},{... | collective-permute-start | bytes 3145736 | tf_op jit(solution)/shard_map/ppermute | solution.py:269
  222.1 44.9 %collective-permute-start.15 = (bf16[2,2,128,1024]{3,2,1,0:T(8,128)(2,1)}, bf16[2,2,128,1024]{3,2,1,0:T(8,128)(2,1)}, u32[]{:S(2)}, u32[]{:S(2)}) collective-permute-start(bf16[2,2,128,1024]{3,2,1,0:T(8,128)(2,1)} %collective-permute-done.12.refs_0_), channel_id=1, source_target_pairs={{0,4},{4,8},{8,12},{12,0},{1,5},{5,9},{9,13},{13,1},{2,6},{6,10},{... | collective-permute-start | bytes 3145736 | tf_op jit(solution)/shard_map/ppermute | solution.py:269
  228.4 22.5 %copy-start.6 = (bf16[2,2,512,256]{3,2,1,0:T(8,128)(2,1)}, bf16[2,2,512,256]{3,2,1,0:T(8,128)(2,1)S(1)}, u32[]{:S(2)}) copy-start(bf16[2,2,512,256]{3,2,1,0:T(8,128)(2,1)S(1)} %second_product.6) | copy-start | bytes 3145732
  228.4 49.9 %collective-permute-start.19 = (bf16[2,2,512,256]{3,2,1,0:T(8,128)(2,1)S(1)}, bf16[2,2,512,256]{3,2,1,0:T(8,128)(2,1)}, u32[]{:S(2)}, u32[]{:S(2)}) collective-permute-start(bf16[2,2,512,256]{3,2,1,0:T(8,128)(2,1)S(1)} %second_product.6), channel_id=1, source_target_pairs={{0,2},{1,3},{6,4},{7,5},{10,8},{11,9},{12,14},{13,15},{16,18},{17,... | collective-permute-start | bytes 3145736 | tf_op jit(solution)/shard_map/ppermute | solution.py:312
  233.1 17.8 %copy-start.30 = (bf16[2,2,512,256]{3,2,1,0:T(8,128)(2,1)}, bf16[2,2,512,256]{3,2,1,0:T(8,128)(2,1)S(1)}, u32[]{:S(2)}) copy-start(bf16[2,2,512,256]{3,2,1,0:T(8,128)(2,1)S(1)} %collective-permute-done.13) | copy-start | bytes 3145732
  250.9 24.5 %copy-start.8 = (bf16[2,2,512,256]{3,2,1,0:T(8,128)(2,1)}, bf16[2,2,512,256]{3,2,1,0:T(8,128)(2,1)S(1)}, u32[]{:S(2)}) copy-start(bf16[2,2,512,256]{3,2,1,0:T(8,128)(2,1)S(1)} %second_product.7) | copy-start | bytes 3145732
  250.9 28.7 %collective-permute-start.20 = (bf16[2,2,512,256]{3,2,1,0:T(8,128)(2,1)S(1)}, bf16[2,2,512,256]{3,2,1,0:T(8,128)(2,1)}, u32[]{:S(2)}, u32[]{:S(2)}) collective-permute-start(bf16[2,2,512,256]{3,2,1,0:T(8,128)(2,1)S(1)} %second_product.7), channel_id=1, source_target_pairs={{0,2},{1,3},{4,6},{5,7},{10,8},{11,9},{14,12},{15,13},{16,18},{17,... | collective-permute-start | bytes 3145736 | tf_op jit(solution)/shard_map/ppermute | solution.py:312
  255.0 36.2 %collective-permute-start.21 = (bf16[2,2,128,1024]{3,2,1,0:T(8,128)(2,1)}, bf16[2,2,128,1024]{3,2,1,0:T(8,128)(2,1)}, u32[]{:S(2)}, u32[]{:S(2)}) collective-permute-start(bf16[2,2,128,1024]{3,2,1,0:T(8,128)(2,1)} %collective-permute-done.14.refs_1_), channel_id=1, source_target_pairs={{0,4},{4,8},{8,12},{12,0},{1,5},{5,9},{9,13},{13,1},{2,6},{6,10},{... | collective-permute-start | bytes 3145736 | tf_op jit(solution)/shard_map/ppermute | solution.py:269
  267.0 2.2 copy-start.1
  269.2 2.2 copy-start.4
  271.4 8.2 %copy-start.7 = (bf16[2,2,512,256]{3,2,1,0:T(8,128)(2,1)S(1)}, bf16[2,2,512,256]{3,2,1,0:T(8,128)(2,1)}, u32[]{:S(2)}) copy-start(bf16[2,2,512,256]{3,2,1,0:T(8,128)(2,1)} %copy-done.6) | copy-start | bytes 3145732
  271.4 8.2 %copy-start.31 = (bf16[2,2,512,256]{3,2,1,0:T(8,128)(2,1)S(1)}, bf16[2,2,512,256]{3,2,1,0:T(8,128)(2,1)}, u32[]{:S(2)}) copy-start(bf16[2,2,512,256]{3,2,1,0:T(8,128)(2,1)} %copy-done.30) | copy-start | bytes 3145732
  275.4 8.0 %copy-start.9 = (bf16[2,2,512,128]{3,2,1,0:T(8,128)(2,1)}, bf16[2,2,512,128]{3,2,1,0:T(8,128)(2,1)S(1)}, u32[]{:S(2)}) copy-start(bf16[2,2,512,128]{3,2,1,0:T(8,128)(2,1)S(1)} %second_product.8.refs_0_) | copy-start | bytes 1572868
  275.4 15.8 %copy-start.2 = (bf16[2,2,2,512,512]{4,3,2,1,0:T(8,128)(2,1)S(1)}, bf16[2,2,2,512,512]{4,3,2,1,0:T(8,128)(2,1)}, u32[]{:S(2)}) copy-start(bf16[2,2,2,512,512]{4,3,2,1,0:T(8,128)(2,1)} %copy-done) | copy-start | bytes 12582916
  275.4 14.3 %collective-permute-start.16 = (bf16[2,2,512,128]{3,2,1,0:T(8,128)(2,1)S(1)}, bf16[2,2,512,128]{3,2,1,0:T(8,128)(2,1)S(1)}, u32[]{:S(2)}, u32[]{:S(2)}) collective-permute-start(bf16[2,2,512,128]{3,2,1,0:T(8,128)(2,1)S(1)} %second_product.8.refs_0_), channel_id=1, source_target_pairs={{3,1},{4,6},{9,11},{14,12},{19,17},{20,22},{25,27},{30,28}} | collective-permute-start | bytes 1572872 | tf_op jit(solution)/shard_map/ppermute | solution.py:319
  277.0 14.2 %collective-permute-start.17 = (bf16[2,2,512,128]{3,2,1,0:T(8,128)(2,1)S(1)}, bf16[2,2,512,128]{3,2,1,0:T(8,128)(2,1)S(1)}, u32[]{:S(2)}, u32[]{:S(2)}) collective-permute-start(bf16[2,2,512,128]{3,2,1,0:T(8,128)(2,1)S(1)} %second_product.8.refs_0_), channel_id=1, source_target_pairs={{2,1},{5,6},{8,11},{15,12},{18,17},{21,22},{24,27},{31,28}} | collective-permute-start | bytes 1572872 | tf_op jit(solution)/shard_map/ppermute | solution.py:319
  278.3 12.9 %collective-permute-start.18 = (bf16[2,2,512,128]{3,2,1,0:T(8,128)(2,1)S(1)}, bf16[2,2,512,128]{3,2,1,0:T(8,128)(2,1)S(1)}, u32[]{:S(2)}, u32[]{:S(2)}) collective-permute-start(bf16[2,2,512,128]{3,2,1,0:T(8,128)(2,1)S(1)} %second_product.8.refs_0_), channel_id=1, source_target_pairs={{0,1},{7,6},{10,11},{13,12},{16,17},{23,22},{26,27},{29,28}} | collective-permute-start | bytes 1572872 | tf_op jit(solution)/shard_map/ppermute | solution.py:319
  283.4 16.1 %collective-permute-start.25 = (bf16[2,2,512,256]{3,2,1,0:T(8,128)(2,1)}, bf16[2,2,512,256]{3,2,1,0:T(8,128)(2,1)}, u32[]{:S(2)}, u32[]{:S(2)}) collective-permute-start(bf16[2,2,512,256]{3,2,1,0:T(8,128)(2,1)} %get-tuple-element.25), channel_id=1, source_target_pairs={{0,1},{1,0},{2,3},{3,2},{4,5},{5,4},{6,7},{7,6},{8,9},{9,8},{10,11... | collective-permute-start | bytes 3145736 | tf_op jit(solution)/shard_map/ppermute | solution.py:210
  289.7 5.8 %copy-start.21 = (bf16[2,2,512,128]{3,2,1,0:T(8,128)(2,1)}, bf16[2,2,512,128]{3,2,1,0:T(8,128)(2,1)S(1)}, u32[]{:S(2)}) copy-start(bf16[2,2,512,128]{3,2,1,0:T(8,128)(2,1)S(1)} %collective-permute-done.16.refs_1_) | copy-start | bytes 1572868
  291.2 4.3 %copy-start.23 = (bf16[2,2,512,128]{3,2,1,0:T(8,128)(2,1)}, bf16[2,2,512,128]{3,2,1,0:T(8,128)(2,1)S(1)}, u32[]{:S(2)}) copy-start(bf16[2,2,512,128]{3,2,1,0:T(8,128)(2,1)S(1)} %collective-permute-done.17.refs_2_) | copy-start | bytes 1572868
  291.2 4.3 %copy-start.25 = (bf16[2,2,512,128]{3,2,1,0:T(8,128)(2,1)}, bf16[2,2,512,128]{3,2,1,0:T(8,128)(2,1)S(1)}, u32[]{:S(2)}) copy-start(bf16[2,2,512,128]{3,2,1,0:T(8,128)(2,1)S(1)} %collective-permute-done.18.refs_3_) | copy-start | bytes 1572868
  291.2 8.3 %copy-start.10 = (bf16[2,2,512,128]{3,2,1,0:T(8,128)(2,1)S(1)}, bf16[2,2,512,128]{3,2,1,0:T(8,128)(2,1)}, u32[]{:S(2)}) copy-start(bf16[2,2,512,128]{3,2,1,0:T(8,128)(2,1)} %copy-done.9) | copy-start | bytes 1572868
  295.6 13.7 %collective-permute-start.22 = (bf16[2,2,512,128]{3,2,1,0:T(8,128)(2,1)S(1)}, bf16[2,2,512,128]{3,2,1,0:T(8,128)(2,1)}, u32[]{:S(2)}, u32[]{:S(2)}) collective-permute-start(bf16[2,2,512,128]{3,2,1,0:T(8,128)(2,1)S(1)} %second_product.9.refs_0_), channel_id=1, source_target_pairs={{3,1},{4,6},{9,11},{14,12},{19,17},{20,22},{25,27},{30,28}} | collective-permute-start | bytes 1572872 | tf_op jit(solution)/shard_map/ppermute | solution.py:319
  296.9 14.3 %collective-permute-start.23 = (bf16[2,2,512,128]{3,2,1,0:T(8,128)(2,1)S(1)}, bf16[2,2,512,128]{3,2,1,0:T(8,128)(2,1)}, u32[]{:S(2)}, u32[]{:S(2)}) collective-permute-start(bf16[2,2,512,128]{3,2,1,0:T(8,128)(2,1)S(1)} %second_product.9.refs_0_), channel_id=1, source_target_pairs={{2,1},{5,6},{8,11},{15,12},{18,17},{21,22},{24,27},{31,28}} | collective-permute-start | bytes 1572872 | tf_op jit(solution)/shard_map/ppermute | solution.py:319
  298.2 13.1 %collective-permute-start.24 = (bf16[2,2,512,128]{3,2,1,0:T(8,128)(2,1)S(1)}, bf16[2,2,512,128]{3,2,1,0:T(8,128)(2,1)}, u32[]{:S(2)}, u32[]{:S(2)}) collective-permute-start(bf16[2,2,512,128]{3,2,1,0:T(8,128)(2,1)S(1)} %second_product.9.refs_0_), channel_id=1, source_target_pairs={{0,1},{7,6},{10,11},{13,12},{16,17},{23,22},{26,27},{29,28}} | collective-permute-start | bytes 1572872 | tf_op jit(solution)/shard_map/ppermute | solution.py:319
  299.5 1.0 copy-start.22
  300.6 1.0 copy-start.24
  301.6 1.0 copy-start.26

commit v16 on v14

--- a/solution.py
+++ b/solution.py
@@ -38,7 +38,7 @@
             for number in range(len(env_refs) // 2):
                 block = block_ref[number]
                 piece = pl.ds(pl.multiple_of((block % per_col) * depth, depth), depth)
-                left = site_ref[block // per_col, :, :, :, piece].reshape(phys * 2 * rows, depth)
+                left = site_ref[block // per_col, 0, :, :, :, piece].reshape(phys * 2 * rows, depth)
                 env_ref = env_refs[number * 2 + which]
                 more_real, more_imag = mul(left, env_ref[w, 0]), mul(left, env_ref[w, 1])
                 with_real = more_real if with_real is None else with_real + more_real
@@ -59,23 +59,23 @@
                 q_ref[v, t, part] = total.astype(BF16)
 
 
-def first_product(blocks, mpo, site, envs, row_tile, col_tile):
-    col_count, phys, _, rows, wide = site.shape
+def first_product(blocks, mpo, site, envs, col_tile):
+    col_count, tiles, phys, _, rows, wide = site.shape
     w_local, _, depth, cols = envs[0].shape
     mpo_count = mpo.shape[1]
     smem = pl.BlockSpec(memory_space=pltpu.SMEM)
     return pl.pallas_call(
         functools.partial(first_kernel, w_local),
-        grid=(rows // row_tile, cols // col_tile),
+        grid=(tiles, cols // col_tile),
         in_specs=[
             smem,
             smem,
-            pl.BlockSpec((col_count, phys, 2, row_tile, wide), lambda i, j: (0, 0, 0, i, 0)),
+            pl.BlockSpec((col_count, 1, phys, 2, rows, wide), lambda i, j: (0, i, 0, 0, 0, 0)),
         ]
         + [pl.BlockSpec((w_local, 2, depth, col_tile), lambda i, j: (0, 0, 0, j))] * len(envs),
-        out_specs=pl.BlockSpec((mpo_count, phys, 2, row_tile, col_tile), lambda i, j: (0, 0, 0, i, j)),
-        out_shape=jax.ShapeDtypeStruct((mpo_count, phys, 2, rows, cols), BF16),
-        scratch_shapes=[pltpu.VMEM((2 * w_local, 2, phys * row_tile, col_tile), F32)],
+        out_specs=pl.BlockSpec((mpo_count, phys, 2, rows, col_tile), lambda i, j: (0, 0, 0, i, j)),
+        out_shape=jax.ShapeDtypeStruct((mpo_count, phys, 2, tiles * rows, cols), BF16),
+        scratch_shapes=[pltpu.VMEM((2 * w_local, 2, phys * rows, col_tile), F32)],
         compiler_params=params(2),
         cost_estimate=LIGHT,
         name="first_product",
@@ -269,13 +269,6 @@
     shift = lambda value: lax.ppermute(
         value, "row", [(r, (r + 1) % row_count) for r in range(row_count)]
     )
-    turn = lambda value: lax.ppermute(value, "col", [(0, 1), (1, 0)])
-    in_order = lambda mine, sibling, axis: jnp.where(
-        depth == 0,
-        jnp.concatenate([mine, sibling], axis=axis),
-        jnp.concatenate([sibling, mine], axis=axis),
-    )
-
     env_own, env_sib, mpo_mine = split_inputs(environment, mpo)
     envs = [env_own, env_sib]
     for _ in range(row_count - 1):
@@ -285,18 +278,16 @@
     rows = planar.shape[2]
     half = rows // 2
     mine = lax.dynamic_slice_in_dim(planar, depth * half, half, 2)
-    other = turn(mine)
-    other = in_order(other, swap(after(other, envs[3], envs[4])), 2)
-    site = jnp.where(col == 0, jnp.stack([planar, other]), jnp.stack([other, planar]))
+    site = lax.all_gather(after(mine, envs[2]), ("col", "depth"), axis=0).reshape((col_count, 2) + mine.shape)
 
     parts = [mine[:, :, : half // 2], mine[:, :, half // 2 :]]
-    travelling = [[shift(after(part, env, site)) for part, env in zip(parts, envs[-2:])]]
+    travelling = [[shift(after(part, env)) for part, env in zip(parts, envs[-2:])]]
     for _ in range(row_count - 2):
         travelling.append([shift(part) for part in travelling[-1]])
 
     blocks = jnp.stack([lax.rem(row - k + row_count, row_count) for k in range(row_count)])
     blocks = blocks.astype(jnp.int32)
-    q = first_product(blocks, mpo_mine, site, envs, half, half)
+    q = first_product(blocks, mpo_mine, site, envs, half)
     q_sib = swap(after(q, *travelling[0]))
 
     goals = [

time: 315 us -> 327 us (1.038)
  between operations: 0.53 us -> 13.7 us
  other arithmetic: 13.4 us -> 3.96 us
  waiting for transfers between devices: 191 us -> 200 us
  local copies, waits for them, and re-layouts: 26.2 us -> 30.3 us
  starting transfers between devices: 27.2 us -> 23.1 us
    select_n x2 -> x0, other arithmetic: 9.4 us -> none  [the longest x1 5.33 us: ring(): jnp.where(depth == 0, jnp.concatenate([mine, sibling], axis=axis), jnp.co...]
    ppermute x12, waiting for transfers between devices: 172 us -> 181 us  [ring(): lax.ppermute(value, 'row', [(r, (r + 1) % row_count) for r in range(row_c...]
    unnamed x62 -> x64, local copies, waits for them, and re-layouts: 17.6 us -> 20 us
    ppermute x4 -> x3, waiting for transfers between devices: 6.86 us -> 6.85 us  [swap(): return lax.ppermute(value, 'depth', [(0, 1), (1, 0)])]
  transfers between devices with their start and end apart: 26 -> 25, of which waited for: 17 -> 17; matrix products, arithmetic and copies ran while one was open for 6% -> 4% of each run, Pallas kernels for 17% -> 16%
where the time goes in v16:
time: 327 us; the launch traced here: 326 us
  waiting for transfers between devices  200 us (61%)
  Pallas kernels  55.4 us (17%)
  local copies, waits for them, and re-layouts  30.3 us (9%)
  starting transfers between devices  23.1 us (7%)
  between operations  13.7 us (4%)
  other arithmetic  3.96 us (1%)
    ppermute x12, waiting for transfers between devices, ring(): lax.ppermute(value, 'row', [(r, (r + 1) % row_count) for r in range(row_c...  181 us
    pallas_call x5, Pallas kernels, second_product(): pl.pallas_call(second_kernel, grid=(mpo_count,), in_specs=[pl.BlockSpec(m...  25.4 us
    pallas_call x1, Pallas kernels, first_product(): pl.pallas_call(functools.partial(first_kernel, w_local), grid=(tiles, col...  23.2 us
    unnamed x64, local copies, waits for them, and re-layouts  20 us
    ppermute x6, waiting for transfers between devices, send(): lax.ppermute(value, axes, [(place(r, 1 - c if turned else c, 1 - d if cro...  11.2 us
    ppermute x3, starting transfers between devices, turn_to_goal(): lax.ppermute(value, axes, [(place(r, 1 - c, d), place(r, c, d)) for r, (c...  9.23 us
    ppermute x6, starting transfers between devices, send(): lax.ppermute(value, axes, [(place(r, 1 - c if turned else c, 1 - d if cro...  7.75 us
    ppermute x3, waiting for transfers between devices, swap(): return lax.ppermute(value, 'depth', [(0, 1), (1, 0)])  6.85 us
  transfers between devices with their start and end apart: 25, of which 17 were waited for; matrix products, arithmetic and copies ran while one was open for 4% of the time, Pallas kernels for 16%

profile of v16, /device:TPU:1, one launch (start us, length us, event | category | flops | bytes accessed | tf_op | source)
XLA Modules:
  0.0 326.0 jit_solution(407624061612947898)
XLA Ops:
  6.5 2.7 constant_dynamic-slice_fusion
  9.2 0.1 collective-permute-start
  9.3 2.7 collective-permute-start.1
  12.0 0.1 collective-permute-done.refs_1_
  12.1 3.9 %copy.6 = bf16[2,512,2,1024]{3,1,2,0:T(8,128)(2,1)S(1)} copy(bf16[2,512,2,1024]{3,2,1,0:T(2,128)(2,1)} %param.4) | data formatting | bytes 8388608 | tf_op jit(solution)/shard_map/optimization_barrier | solution.py:206
  16.0 1.5 dynamic-slice_bitcast_fusion
  17.5 20.1 %collective-permute-done.1.refs_2_ = bf16[1,2,512,512]{3,2,1,0:T(8,128)(2,1)S(1)} collective-permute-done((bf16[1,2,512,512]{3,2,1,0:T(8,128)(2,1)S(1)}, bf16[1,2,512,512]{3,2,1,0:T(8,128)(2,1)S(1)}, u32[]{:S(2)}, u32[]{:S(2)}) %collective-permute-start.1) | collective-permute-done | bytes 1048608 | tf_op jit(solution)/shard_map/ppermute | solution.py:269
  37.6 0.1 collective-permute-start.2
  37.7 0.5 collective-permute-start.3
  38.3 25.4 %collective-permute-done.2.refs_3_ = bf16[1,2,512,512]{3,2,1,0:T(8,128)(2,1)S(1)} collective-permute-done((bf16[1,2,512,512]{3,2,1,0:T(8,128)(2,1)S(1)}, bf16[1,2,512,512]{3,2,1,0:T(8,128)(2,1)S(1)}, u32[]{:S(2)}, u32[]{:S(2)}) %collective-permute-start.2) | collective-permute-done | bytes 1048608 | tf_op jit(solution)/shard_map/ppermute | solution.py:269
  63.6 1.0 copy-done.13
  64.6 21.5 %collective-permute-done.3.refs_4_ = bf16[1,2,512,512]{3,2,1,0:T(8,128)(2,1)S(1)} collective-permute-done((bf16[1,2,512,512]{3,2,1,0:T(8,128)(2,1)S(1)}, bf16[1,2,512,512]{3,2,1,0:T(8,128)(2,1)S(1)}, u32[]{:S(2)}, u32[]{:S(2)}) %collective-permute-start.3) | collective-permute-done | bytes 1048608 | tf_op jit(solution)/shard_map/ppermute | solution.py:269
  86.1 22.5 %collective-permute-done.4.refs_5_ = bf16[1,2,512,512]{3,2,1,0:T(8,128)(2,1)S(1)} collective-permute-done((bf16[1,2,512,512]{3,2,1,0:T(8,128)(2,1)S(1)}, bf16[1,2,512,512]{3,2,1,0:T(8,128)(2,1)S(1)}, u32[]{:S(2)}, u32[]{:S(2)}) %collective-permute-start.4) | collective-permute-done | bytes 1048608 | tf_op jit(solution)/shard_map/ppermute | solution.py:269
  108.6 2.2 fusion
  110.8 20.2 %collective-permute-done.5.refs_6_ = bf16[1,2,512,512]{3,2,1,0:T(8,128)(2,1)S(1)} collective-permute-done((bf16[1,2,512,512]{3,2,1,0:T(8,128)(2,1)S(1)}, bf16[1,2,512,512]{3,2,1,0:T(8,128)(2,1)S(1)}, u32[]{:S(2)}, u32[]{:S(2)}) %collective-permute-start.5) | collective-permute-done | bytes 1048608 | tf_op jit(solution)/shard_map/ppermute | solution.py:269
  131.0 1.0 copy-done.19
  132.1 21.5 %collective-permute-done.6.refs_7_ = bf16[1,2,512,512]{3,2,1,0:T(8,128)(2,1)S(1)} collective-permute-done((bf16[1,2,512,512]{3,2,1,0:T(8,128)(2,1)S(1)}, bf16[1,2,512,512]{3,2,1,0:T(8,128)(2,1)S(1)}, u32[]{:S(2)}, u32[]{:S(2)}) %collective-permute-start.6) | collective-permute-done | bytes 1048608 | tf_op jit(solution)/shard_map/ppermute | solution.py:269
  153.5 1.0 copy-done.21
  154.6 0.1 pad_add_fusion.1.block_ref
  154.7 1.2 copy-done.10
  155.9 1.2 copy-done.12
  157.1 1.2 copy-done.14
  158.4 1.2 copy-done.16
  159.6 1.2 copy-done.18
  160.8 1.2 copy-done.20
  162.0 1.2 copy-done.22
  163.3 23.2 %first_product.1.own_ref = bf16[2,2,2,512,512]{4,3,2,1,0:T(8,128)(2,1)S(1)} custom-call(s32[4]{0:T(128)S(1)} %pad_add_fusion.1.block_ref, f32[2,2,2,2]{3,2,1,0:T(2,128)S(1)} %pad_maximum_fusion.mpo_ref, bf16[2,2,2,2,256,1024]{5,4,3,2,1,0:T(8,128)(2,1)} %bitcast.9, bf16[1,2,512,512]{3,2,1,0:T(8,128)(2,1)S(1)} %get-tuple-element.29.refs_0_, ...), custom_call_target="tpu_custom_call" | custom-call | tf_op jit(solution)/shard_map/first_product/pallas_call | solution.py:67
  186.5 12.0 %collective-permute-done.8.refs_1_ = bf16[2,2,128,1024]{3,2,1,0:T(8,128)(2,1)} collective-permute-done((bf16[2,2,128,1024]{3,2,1,0:T(8,128)(2,1)S(1)}, bf16[2,2,128,1024]{3,2,1,0:T(8,128)(2,1)}, u32[]{:S(2)}, u32[]{:S(2)}) %collective-permute-start.8) | collective-permute-done | bytes 1048608 | tf_op jit(solution)/shard_map/ppermute | solution.py:269
  198.6 1.4 collective-permute-start.9
  200.0 6.8 %collective-permute-done.9.sib_ref = bf16[2,2,2,512,512]{4,3,2,1,0:T(8,128)(2,1)S(1)} collective-permute-done((bf16[2,2,2,512,512]{4,3,2,1,0:T(8,128)(2,1)S(1)}, bf16[2,2,2,512,512]{4,3,2,1,0:T(8,128)(2,1)S(1)}, u32[]{:S(2)}, u32[]{:S(2)}) %collective-permute-start.9) | collective-permute-done | bytes 4194336 | tf_op jit(solution)/shard_map/ppermute | solution.py:210
  206.8 4.8 %second_product.5 = bf16[2,2,512,256]{3,2,1,0:T(8,128)(2,1)S(1)} custom-call(s32[1]{0:T(128)} %bitcast.1.pick_ref, bf16[2,2,2,512,512]{4,3,2,1,0:T(8,128)(2,1)S(1)} %first_product.1.own_ref, bf16[2,2,2,512,512]{4,3,2,1,0:T(8,128)(2,1)S(1)} %collective-permute-done.9.sib_ref, bf16[2,2,128,1024]{3,2,1,0:T(8,128)(2,1)S(1)} %get-tuple-element.17.refs_0_, ...), custom_call_target="tpu_custom_call" | custom-call | tf_op jit(solution)/shard_map/second_product/pallas_call | solution.py:104
  211.6 1.3 collective-permute-start.11
  212.9 0.1 collective-permute-start.12
  212.9 14.0 %collective-permute-done.10.refs_0_ = bf16[2,2,128,1024]{3,2,1,0:T(8,128)(2,1)} collective-permute-done((bf16[2,2,128,1024]{3,2,1,0:T(8,128)(2,1)}, bf16[2,2,128,1024]{3,2,1,0:T(8,128)(2,1)}, u32[]{:S(2)}, u32[]{:S(2)}) %collective-permute-start.10) | collective-permute-done | bytes 1048608 | tf_op jit(solution)/shard_map/ppermute | solution.py:269
  226.9 6.3 %second_product.6 = bf16[2,2,512,256]{3,2,1,0:T(8,128)(2,1)S(1)} custom-call(s32[1]{0:T(128)} %bitcast.1.pick_ref, bf16[2,2,2,512,512]{4,3,2,1,0:T(8,128)(2,1)S(1)} %first_product.1.own_ref, bf16[2,2,2,512,512]{4,3,2,1,0:T(8,128)(2,1)S(1)} %collective-permute-done.9.sib_ref, bf16[2,2,128,1024]{3,2,1,0:T(8,128)(2,1)} %collective-permute-done.7.refs_0_, ...), custom_call_target="tpu_custom_call" | custom-call | tf_op jit(solution)/shard_map/second_product/pallas_call | solution.py:104
  233.2 4.0 %collective-permute-start.17 = (bf16[2,2,512,256]{3,2,1,0:T(8,128)(2,1)S(1)}, bf16[2,2,512,256]{3,2,1,0:T(8,128)(2,1)}, u32[]{:S(2)}, u32[]{:S(2)}) collective-permute-start(bf16[2,2,512,256]{3,2,1,0:T(8,128)(2,1)S(1)} %second_product.6), channel_id=1, source_target_pairs={{0,2},{1,3},{6,4},{7,5},{10,8},{11,9},{12,14},{13,15},{16,18},{17,... | collective-permute-start | bytes 3145736 | tf_op jit(solution)/shard_map/ppermute | solution.py:303
  237.2 0.7 collective-permute-done.11
  237.9 11.4 %collective-permute-done.12.refs_1_ = bf16[2,2,128,1024]{3,2,1,0:T(8,128)(2,1)} collective-permute-done((bf16[2,2,128,1024]{3,2,1,0:T(8,128)(2,1)}, bf16[2,2,128,1024]{3,2,1,0:T(8,128)(2,1)}, u32[]{:S(2)}, u32[]{:S(2)}) %collective-permute-start.12) | collective-permute-done | bytes 1048608 | tf_op jit(solution)/shard_map/ppermute | solution.py:269
  249.4 6.3 %second_product.7 = bf16[2,2,512,256]{3,2,1,0:T(8,128)(2,1)S(1)} custom-call(s32[1]{0:T(128)} %bitcast.1.pick_ref, bf16[2,2,2,512,512]{4,3,2,1,0:T(8,128)(2,1)S(1)} %first_product.1.own_ref, bf16[2,2,2,512,512]{4,3,2,1,0:T(8,128)(2,1)S(1)} %collective-permute-done.9.sib_ref, bf16[2,2,128,1024]{3,2,1,0:T(8,128)(2,1)} %collective-permute-done.10.refs_0_, ...), custom_call_target="tpu_custom_call" | custom-call | tf_op jit(solution)/shard_map/second_product/pallas_call | solution.py:104
  255.7 4.0 %collective-permute-start.18 = (bf16[2,2,512,256]{3,2,1,0:T(8,128)(2,1)S(1)}, bf16[2,2,512,256]{3,2,1,0:T(8,128)(2,1)}, u32[]{:S(2)}, u32[]{:S(2)}) collective-permute-start(bf16[2,2,512,256]{3,2,1,0:T(8,128)(2,1)S(1)} %second_product.7), channel_id=1, source_target_pairs={{0,2},{1,3},{4,6},{5,7},{10,8},{11,9},{14,12},{15,13},{16,18},{17,... | collective-permute-start | bytes 3145736 | tf_op jit(solution)/shard_map/ppermute | solution.py:303
  259.7 12.1 %collective-permute-done.13.refs_0_ = bf16[2,2,128,1024]{3,2,1,0:T(8,128)(2,1)} collective-permute-done((bf16[2,2,128,1024]{3,2,1,0:T(8,128)(2,1)}, bf16[2,2,128,1024]{3,2,1,0:T(8,128)(2,1)}, u32[]{:S(2)}, u32[]{:S(2)}) %collective-permute-start.13) | collective-permute-done | bytes 1048608 | tf_op jit(solution)/shard_map/ppermute | solution.py:269
  271.9 2.2 copy-done.1
  274.0 2.2 copy-done.3
  276.2 4.0 %second_product.8.refs_0_ = bf16[2,2,512,128]{3,2,1,0:T(8,128)(2,1)S(1)} custom-call(s32[1]{0:T(128)} %bitcast.1.pick_ref, bf16[2,2,2,512,512]{4,3,2,1,0:T(8,128)(2,1)S(1)} %copy-done.1, bf16[2,2,2,512,512]{4,3,2,1,0:T(8,128)(2,1)S(1)} %copy-done.3, bf16[2,2,128,1024]{3,2,1,0:T(8,128)(2,1)} %collective-permute-done.13.refs_0_), custom_call_target="tpu_custom_call" | custom-call | tf_op jit(solution)/shard_map/second_product/pallas_call | solution.py:104
  280.2 1.3 collective-permute-start.14
  281.5 1.3 collective-permute-start.15
  282.8 1.3 collective-permute-start.16
  284.2 3.8 %select_convert_fusion = (bf16[2,2,512,256]{3,2,1,0:T(8,128)(2,1)}, f32[2,2,512,256]{3,2,1,0:T(8,128)S(1)}) fusion(bf16[2,2,512,256]{3,2,1,0:T(8,128)(2,1)S(1)} %copy-done.30, bf16[2,2,512,256]{3,2,1,0:T(8,128)(2,1)S(1)} %second_product.5, bf16[2,2,512,256]{3,2,1,0:T(8,128)(2,1)} %collective-permute-done.17, bf16[2,2,512,256]{3,2,1,0:T(8,128)(2,1)S(1)} %copy-done.5, ...), kind=kLoop, calls=%fused_computation | loop fusion | flops 7340032 | bytes 9437188 | tf_op jit(solution)/shard_map/convert_element_type | solution.py:337
  288.0 1.2 collective-permute-start.23
  289.1 5.1 %collective-permute-done.14.refs_1_ = bf16[2,2,512,128]{3,2,1,0:T(8,128)(2,1)S(1)} collective-permute-done((bf16[2,2,512,128]{3,2,1,0:T(8,128)(2,1)S(1)}, bf16[2,2,512,128]{3,2,1,0:T(8,128)(2,1)S(1)}, u32[]{:S(2)}, u32[]{:S(2)}) %collective-permute-start.14) | collective-permute-done | bytes 524320 | tf_op jit(solution)/shard_map/ppermute | solution.py:310
  294.2 1.5 collective-permute-done.15.refs_2_
  295.8 0.8 copy-done.25
  296.6 4.1 %second_product.9.refs_0_ = bf16[2,2,512,128]{3,2,1,0:T(8,128)(2,1)S(1)} custom-call(s32[1]{0:T(128)} %bitcast.1.pick_ref, bf16[2,2,2,512,512]{4,3,2,1,0:T(8,128)(2,1)S(1)} %copy-done.1, bf16[2,2,2,512,512]{4,3,2,1,0:T(8,128)(2,1)S(1)} %copy-done.3, bf16[2,2,128,1024]{3,2,1,0:T(8,128)(2,1)} %collective-permute-done.19.refs_0_), custom_call_target="tpu_custom_call" | custom-call | tf_op jit(solution)/shard_map/second_product/pallas_call | solution.py:104
  300.7 1.3 collective-permute-start.20
  302.0 1.3 collective-permute-start.21
  303.3 1.3 collective-permute-start.22
  304.6 0.1 pad_add_fusion.pick_ref
  304.7 1.0 copy-done.24
  305.7 1.0 copy-done.26
  306.8 1.0 copy-done.28
  307.8 4.0 %finish.1.refs_4_ = f32[2,2,512,512]{3,2,1,0:T(8,128)} custom-call(s32[2]{0:T(128)S(1)} %pad_add_fusion.pick_ref, f32[2,2,512,256]{3,2,1,0:T(8,128)S(1)} %get-tuple-element.26.mine_ref, bf16[2,2,512,256]{3,2,1,0:T(8,128)(2,1)} %collective-permute-done.23.siblings_ref, bf16[2,2,512,128]{3,2,1,0:T(8,128)(2,1)S(1)} %copy-done.8, ...), custom_call_target="tpu_custom_call" | custom-call | tf_op jit(solution)/shard_map/finish/pallas_call | solution.py:145
  311.8 2.6 collective-permute-done.20.refs_1_
  314.4 1.9 collective-permute-done.21.refs_2_
  316.3 2.8 finish_last.1
  (68 shorter events, 0.2 us)
Async XLA Ops:
  6.5 148.1 %all-gather.3.cloned.1.call-start = ((), (), s32[]{:S(2)}) async-start(), calls=%async_computation | async-start | bytes 10485760 | tf_op jit(solution)/shard_map/all_gather | solution.py:281
  9.2 2.9 collective-permute-start
  9.3 28.3 %collective-permute-start.1 = (bf16[1,2,512,512]{3,2,1,0:T(8,128)(2,1)S(1)}, bf16[1,2,512,512]{3,2,1,0:T(8,128)(2,1)S(1)}, u32[]{:S(2)}, u32[]{:S(2)}) collective-permute-start(bf16[1,2,512,512]{3,2,1,0:T(8,128)(2,1)S(1)} %get-tuple-element.29.refs_0_), channel_id=1, source_target_pairs={{0,4},{4,8},{8,12},{12,0},{1,5},{5,9},{9,13},{13,1},{2,6},{6,10},{... | collective-permute-start | bytes 3145736 | tf_op jit(solution)/shard_map/ppermute | solution.py:269
  12.1 25.5 %copy-start.9 = (bf16[1,2,512,512]{3,2,1,0:T(8,128)(2,1)}, bf16[1,2,512,512]{3,2,1,0:T(8,128)(2,1)S(1)}, u32[]{:S(2)}) copy-start(bf16[1,2,512,512]{3,2,1,0:T(8,128)(2,1)S(1)} %collective-permute-done.refs_1_) | copy-start | bytes 3145732
  37.6 71.0 %copy-start.11 = (bf16[1,2,512,512]{3,2,1,0:T(8,128)(2,1)}, bf16[1,2,512,512]{3,2,1,0:T(8,128)(2,1)S(1)}, u32[]{:S(2)}) copy-start(bf16[1,2,512,512]{3,2,1,0:T(8,128)(2,1)S(1)} %collective-permute-done.1.refs_2_) | copy-start | bytes 3145732
  37.6 117.0 %copy-start.31 = (f32[2,2,2,2]{3,2,1,0:T(2,128)S(1)}, f32[2,2,2,2]{3,2,1,0:T(2,128)}, u32[]{:S(2)}) copy-start(f32[2,2,2,2]{3,2,1,0:T(2,128)} %param.5) | copy-start | bytes 196
  37.6 26.0 %collective-permute-start.2 = (bf16[1,2,512,512]{3,2,1,0:T(8,128)(2,1)S(1)}, bf16[1,2,512,512]{3,2,1,0:T(8,128)(2,1)S(1)}, u32[]{:S(2)}, u32[]{:S(2)}) collective-permute-start(bf16[1,2,512,512]{3,2,1,0:T(8,128)(2,1)S(1)} %collective-permute-done.refs_1_), channel_id=1, source_target_pairs={{0,4},{4,8},{8,12},{12,0},{1,5},{5,9},{9,13},{13,1},{2,6},{6,10},{... | collective-permute-start | bytes 3145736 | tf_op jit(solution)/shard_map/ppermute | solution.py:269
  37.7 48.4 %collective-permute-start.3 = (bf16[1,2,512,512]{3,2,1,0:T(8,128)(2,1)S(1)}, bf16[1,2,512,512]{3,2,1,0:T(8,128)(2,1)S(1)}, u32[]{:S(2)}, u32[]{:S(2)}) collective-permute-start(bf16[1,2,512,512]{3,2,1,0:T(8,128)(2,1)S(1)} %collective-permute-done.1.refs_2_), channel_id=1, source_target_pairs={{0,4},{4,8},{8,12},{12,0},{1,5},{5,9},{9,13},{13,1},{2,6},{6,10},{... | collective-permute-start | bytes 3145736 | tf_op jit(solution)/shard_map/ppermute | solution.py:269
  63.6 44.9 %collective-permute-start.4 = (bf16[1,2,512,512]{3,2,1,0:T(8,128)(2,1)S(1)}, bf16[1,2,512,512]{3,2,1,0:T(8,128)(2,1)S(1)}, u32[]{:S(2)}, u32[]{:S(2)}) collective-permute-start(bf16[1,2,512,512]{3,2,1,0:T(8,128)(2,1)S(1)} %collective-permute-done.2.refs_3_), channel_id=1, source_target_pairs={{0,4},{4,8},{8,12},{12,0},{1,5},{5,9},{9,13},{13,1},{2,6},{6,10},{... | collective-permute-start | bytes 3145736 | tf_op jit(solution)/shard_map/ppermute | solution.py:269
  63.6 1.0 copy-start.13
  86.1 45.9 %copy-start.15 = (bf16[1,2,512,512]{3,2,1,0:T(8,128)(2,1)}, bf16[1,2,512,512]{3,2,1,0:T(8,128)(2,1)S(1)}, u32[]{:S(2)}) copy-start(bf16[1,2,512,512]{3,2,1,0:T(8,128)(2,1)S(1)} %collective-permute-done.3.refs_4_) | copy-start | bytes 3145732
  86.1 44.9 %collective-permute-start.5 = (bf16[1,2,512,512]{3,2,1,0:T(8,128)(2,1)S(1)}, bf16[1,2,512,512]{3,2,1,0:T(8,128)(2,1)S(1)}, u32[]{:S(2)}, u32[]{:S(2)}) collective-permute-start(bf16[1,2,512,512]{3,2,1,0:T(8,128)(2,1)S(1)} %collective-permute-done.3.refs_4_), channel_id=1, source_target_pairs={{0,4},{4,8},{8,12},{12,0},{1,5},{5,9},{9,13},{13,1},{2,6},{6,10},{... | collective-permute-start | bytes 3145736 | tf_op jit(solution)/shard_map/ppermute | solution.py:269
  108.6 23.5 %copy-start.17 = (bf16[1,2,512,512]{3,2,1,0:T(8,128)(2,1)}, bf16[1,2,512,512]{3,2,1,0:T(8,128)(2,1)S(1)}, u32[]{:S(2)}) copy-start(bf16[1,2,512,512]{3,2,1,0:T(8,128)(2,1)S(1)} %collective-permute-done.4.refs_5_) | copy-start | bytes 3145732
  108.6 44.9 %collective-permute-start.6 = (bf16[1,2,512,512]{3,2,1,0:T(8,128)(2,1)S(1)}, bf16[1,2,512,512]{3,2,1,0:T(8,128)(2,1)S(1)}, u32[]{:S(2)}, u32[]{:S(2)}) collective-permute-start(bf16[1,2,512,512]{3,2,1,0:T(8,128)(2,1)S(1)} %collective-permute-done.4.refs_5_), channel_id=1, source_target_pairs={{0,4},{4,8},{8,12},{12,0},{1,5},{5,9},{9,13},{13,1},{2,6},{6,10},{... | collective-permute-start | bytes 3145736 | tf_op jit(solution)/shard_map/ppermute | solution.py:269
  131.0 1.0 copy-start.19
  132.0 54.5 %collective-permute-start.7 = (bf16[2,2,128,1024]{3,2,1,0:T(8,128)(2,1)S(1)}, bf16[2,2,128,1024]{3,2,1,0:T(8,128)(2,1)}, u32[]{:S(2)}, u32[]{:S(2)}) collective-permute-start(bf16[2,2,128,1024]{3,2,1,0:T(8,128)(2,1)S(1)} %get-tuple-element.17.refs_0_), channel_id=1, source_target_pairs={{0,4},{4,8},{8,12},{12,0},{1,5},{5,9},{9,13},{13,1},{2,6},{6,10},{... | collective-permute-start | bytes 3145736 | tf_op jit(solution)/shard_map/ppermute | solution.py:269
  153.5 1.0 copy-start.21
  154.6 44.0 %collective-permute-start.8 = (bf16[2,2,128,1024]{3,2,1,0:T(8,128)(2,1)S(1)}, bf16[2,2,128,1024]{3,2,1,0:T(8,128)(2,1)}, u32[]{:S(2)}, u32[]{:S(2)}) collective-permute-start(bf16[2,2,128,1024]{3,2,1,0:T(8,128)(2,1)S(1)} %get-tuple-element.18.refs_1_), channel_id=1, source_target_pairs={{0,4},{4,8},{8,12},{12,0},{1,5},{5,9},{9,13},{13,1},{2,6},{6,10},{... | collective-permute-start | bytes 3145736 | tf_op jit(solution)/shard_map/ppermute | solution.py:269
  154.7 1.2 copy-start.10
  155.9 1.2 copy-start.12
  157.1 1.2 copy-start.14
  158.4 1.2 copy-start.16
  159.6 1.2 copy-start.18
  160.8 1.2 copy-start.20
  162.0 1.2 copy-start.22
  186.5 62.9 %copy-start = (bf16[2,2,2,512,512]{4,3,2,1,0:T(8,128)(2,1)}, bf16[2,2,2,512,512]{4,3,2,1,0:T(8,128)(2,1)S(1)}, u32[]{:S(2)}) copy-start(bf16[2,2,2,512,512]{4,3,2,1,0:T(8,128)(2,1)S(1)} %first_product.1.own_ref) | copy-start | bytes 12582916
  198.6 8.2 %collective-permute-start.9 = (bf16[2,2,2,512,512]{4,3,2,1,0:T(8,128)(2,1)S(1)}, bf16[2,2,2,512,512]{4,3,2,1,0:T(8,128)(2,1)S(1)}, u32[]{:S(2)}, u32[]{:S(2)}) collective-permute-start(bf16[2,2,2,512,512]{4,3,2,1,0:T(8,128)(2,1)S(1)} %first_product.1.own_ref), channel_id=1, source_target_pairs={{0,1},{1,0},{2,3},{3,2},{4,5},{5,4},{6,7},{7,6},{8,9},{9,8},{10,11... | collective-permute-start | bytes 12582920 | tf_op jit(solution)/shard_map/ppermute | solution.py:210
  200.0 26.9 %collective-permute-start.10 = (bf16[2,2,128,1024]{3,2,1,0:T(8,128)(2,1)}, bf16[2,2,128,1024]{3,2,1,0:T(8,128)(2,1)}, u32[]{:S(2)}, u32[]{:S(2)}) collective-permute-start(bf16[2,2,128,1024]{3,2,1,0:T(8,128)(2,1)} %collective-permute-done.7.refs_0_), channel_id=1, source_target_pairs={{0,4},{4,8},{8,12},{12,0},{1,5},{5,9},{9,13},{13,1},{2,6},{6,10},{... | collective-permute-start | bytes 3145736 | tf_op jit(solution)/shard_map/ppermute | solution.py:269
  206.8 42.6 %copy-start.2 = (bf16[2,2,2,512,512]{4,3,2,1,0:T(8,128)(2,1)}, bf16[2,2,2,512,512]{4,3,2,1,0:T(8,128)(2,1)S(1)}, u32[]{:S(2)}) copy-start(bf16[2,2,2,512,512]{4,3,2,1,0:T(8,128)(2,1)S(1)} %collective-permute-done.9.sib_ref) | copy-start | bytes 12582916
  211.6 26.4 %collective-permute-start.11 = (bf16[2,2,512,256]{3,2,1,0:T(8,128)(2,1)S(1)}, bf16[2,2,512,256]{3,2,1,0:T(8,128)(2,1)S(1)}, u32[]{:S(2)}, u32[]{:S(2)}) collective-permute-start(bf16[2,2,512,256]{3,2,1,0:T(8,128)(2,1)S(1)} %second_product.5), channel_id=1, source_target_pairs={{2,0},{3,1},{6,4},{7,5},{8,10},{9,11},{12,14},{13,15},{18,16},{19,... | collective-permute-start | bytes 3145736 | tf_op jit(solution)/shard_map/ppermute | solution.py:303
  212.9 36.5 %collective-permute-start.12 = (bf16[2,2,128,1024]{3,2,1,0:T(8,128)(2,1)}, bf16[2,2,128,1024]{3,2,1,0:T(8,128)(2,1)}, u32[]{:S(2)}, u32[]{:S(2)}) collective-permute-start(bf16[2,2,128,1024]{3,2,1,0:T(8,128)(2,1)} %collective-permute-done.8.refs_1_), channel_id=1, source_target_pairs={{0,4},{4,8},{8,12},{12,0},{1,5},{5,9},{9,13},{13,1},{2,6},{6,10},{... | collective-permute-start | bytes 3145736 | tf_op jit(solution)/shard_map/ppermute | solution.py:269
  226.9 44.9 %collective-permute-start.13 = (bf16[2,2,128,1024]{3,2,1,0:T(8,128)(2,1)}, bf16[2,2,128,1024]{3,2,1,0:T(8,128)(2,1)}, u32[]{:S(2)}, u32[]{:S(2)}) collective-permute-start(bf16[2,2,128,1024]{3,2,1,0:T(8,128)(2,1)} %collective-permute-done.10.refs_0_), channel_id=1, source_target_pairs={{0,4},{4,8},{8,12},{12,0},{1,5},{5,9},{9,13},{13,1},{2,6},{6,10},{... | collective-permute-start | bytes 3145736 | tf_op jit(solution)/shard_map/ppermute | solution.py:269
  233.2 22.5 %copy-start.4 = (bf16[2,2,512,256]{3,2,1,0:T(8,128)(2,1)}, bf16[2,2,512,256]{3,2,1,0:T(8,128)(2,1)S(1)}, u32[]{:S(2)}) copy-start(bf16[2,2,512,256]{3,2,1,0:T(8,128)(2,1)S(1)} %second_product.6) | copy-start | bytes 3145732
  233.2 49.6 %collective-permute-start.17 = (bf16[2,2,512,256]{3,2,1,0:T(8,128)(2,1)S(1)}, bf16[2,2,512,256]{3,2,1,0:T(8,128)(2,1)}, u32[]{:S(2)}, u32[]{:S(2)}) collective-permute-start(bf16[2,2,512,256]{3,2,1,0:T(8,128)(2,1)S(1)} %second_product.6), channel_id=1, source_target_pairs={{0,2},{1,3},{6,4},{7,5},{10,8},{11,9},{12,14},{13,15},{16,18},{17,... | collective-permute-start | bytes 3145736 | tf_op jit(solution)/shard_map/ppermute | solution.py:303
  237.9 17.8 %copy-start.29 = (bf16[2,2,512,256]{3,2,1,0:T(8,128)(2,1)}, bf16[2,2,512,256]{3,2,1,0:T(8,128)(2,1)S(1)}, u32[]{:S(2)}) copy-start(bf16[2,2,512,256]{3,2,1,0:T(8,128)(2,1)S(1)} %collective-permute-done.11) | copy-start | bytes 3145732
  255.7 24.5 %copy-start.6 = (bf16[2,2,512,256]{3,2,1,0:T(8,128)(2,1)}, bf16[2,2,512,256]{3,2,1,0:T(8,128)(2,1)S(1)}, u32[]{:S(2)}) copy-start(bf16[2,2,512,256]{3,2,1,0:T(8,128)(2,1)S(1)} %second_product.7) | copy-start | bytes 3145732
  255.7 28.4 %collective-permute-start.18 = (bf16[2,2,512,256]{3,2,1,0:T(8,128)(2,1)S(1)}, bf16[2,2,512,256]{3,2,1,0:T(8,128)(2,1)}, u32[]{:S(2)}, u32[]{:S(2)}) collective-permute-start(bf16[2,2,512,256]{3,2,1,0:T(8,128)(2,1)S(1)} %second_product.7), channel_id=1, source_target_pairs={{0,2},{1,3},{4,6},{5,7},{10,8},{11,9},{14,12},{15,13},{16,18},{17,... | collective-permute-start | bytes 3145736 | tf_op jit(solution)/shard_map/ppermute | solution.py:303
  259.7 36.9 %collective-permute-start.19 = (bf16[2,2,128,1024]{3,2,1,0:T(8,128)(2,1)}, bf16[2,2,128,1024]{3,2,1,0:T(8,128)(2,1)}, u32[]{:S(2)}, u32[]{:S(2)}) collective-permute-start(bf16[2,2,128,1024]{3,2,1,0:T(8,128)(2,1)} %collective-permute-done.12.refs_1_), channel_id=1, source_target_pairs={{0,4},{4,8},{8,12},{12,0},{1,5},{5,9},{9,13},{13,1},{2,6},{6,10},{... | collective-permute-start | bytes 3145736 | tf_op jit(solution)/shard_map/ppermute | solution.py:269
  271.9 2.2 copy-start.1
  274.0 2.2 copy-start.3
  276.2 7.9 %copy-start.5 = (bf16[2,2,512,256]{3,2,1,0:T(8,128)(2,1)S(1)}, bf16[2,2,512,256]{3,2,1,0:T(8,128)(2,1)}, u32[]{:S(2)}) copy-start(bf16[2,2,512,256]{3,2,1,0:T(8,128)(2,1)} %copy-done.4) | copy-start | bytes 3145732
  276.2 7.9 %copy-start.30 = (bf16[2,2,512,256]{3,2,1,0:T(8,128)(2,1)S(1)}, bf16[2,2,512,256]{3,2,1,0:T(8,128)(2,1)}, u32[]{:S(2)}) copy-start(bf16[2,2,512,256]{3,2,1,0:T(8,128)(2,1)} %copy-done.29) | copy-start | bytes 3145732
  280.2 7.7 %copy-start.7 = (bf16[2,2,512,128]{3,2,1,0:T(8,128)(2,1)}, bf16[2,2,512,128]{3,2,1,0:T(8,128)(2,1)S(1)}, u32[]{:S(2)}) copy-start(bf16[2,2,512,128]{3,2,1,0:T(8,128)(2,1)S(1)} %second_product.8.refs_0_) | copy-start | bytes 1572868
  280.2 14.0 %collective-permute-start.14 = (bf16[2,2,512,128]{3,2,1,0:T(8,128)(2,1)S(1)}, bf16[2,2,512,128]{3,2,1,0:T(8,128)(2,1)S(1)}, u32[]{:S(2)}, u32[]{:S(2)}) collective-permute-start(bf16[2,2,512,128]{3,2,1,0:T(8,128)(2,1)S(1)} %second_product.8.refs_0_), channel_id=1, source_target_pairs={{3,1},{4,6},{9,11},{14,12},{19,17},{20,22},{25,27},{30,28}} | collective-permute-start | bytes 1572872 | tf_op jit(solution)/shard_map/ppermute | solution.py:310
  281.5 14.2 %collective-permute-start.15 = (bf16[2,2,512,128]{3,2,1,0:T(8,128)(2,1)S(1)}, bf16[2,2,512,128]{3,2,1,0:T(8,128)(2,1)S(1)}, u32[]{:S(2)}, u32[]{:S(2)}) collective-permute-start(bf16[2,2,512,128]{3,2,1,0:T(8,128)(2,1)S(1)} %second_product.8.refs_0_), channel_id=1, source_target_pairs={{2,1},{5,6},{8,11},{15,12},{18,17},{21,22},{24,27},{31,28}} | collective-permute-start | bytes 1572872 | tf_op jit(solution)/shard_map/ppermute | solution.py:310
  282.8 13.8 %collective-permute-start.16 = (bf16[2,2,512,128]{3,2,1,0:T(8,128)(2,1)S(1)}, bf16[2,2,512,128]{3,2,1,0:T(8,128)(2,1)S(1)}, u32[]{:S(2)}, u32[]{:S(2)}) collective-permute-start(bf16[2,2,512,128]{3,2,1,0:T(8,128)(2,1)S(1)} %second_product.8.refs_0_), channel_id=1, source_target_pairs={{0,1},{7,6},{10,11},{13,12},{16,17},{23,22},{26,27},{29,28}} | collective-permute-start | bytes 1572872 | tf_op jit(solution)/shard_map/ppermute | solution.py:310
  288.0 16.7 %collective-permute-start.23 = (bf16[2,2,512,256]{3,2,1,0:T(8,128)(2,1)}, bf16[2,2,512,256]{3,2,1,0:T(8,128)(2,1)}, u32[]{:S(2)}, u32[]{:S(2)}) collective-permute-start(bf16[2,2,512,256]{3,2,1,0:T(8,128)(2,1)} %get-tuple-element.25), channel_id=1, source_target_pairs={{0,1},{1,0},{2,3},{3,2},{4,5},{5,4},{6,7},{7,6},{8,9},{9,8},{10,11... | collective-permute-start | bytes 3145736 | tf_op jit(solution)/shard_map/ppermute | solution.py:210
  294.2 6.4 %copy-start.23 = (bf16[2,2,512,128]{3,2,1,0:T(8,128)(2,1)}, bf16[2,2,512,128]{3,2,1,0:T(8,128)(2,1)S(1)}, u32[]{:S(2)}) copy-start(bf16[2,2,512,128]{3,2,1,0:T(8,128)(2,1)S(1)} %collective-permute-done.14.refs_1_) | copy-start | bytes 1572868
  295.8 0.8 copy-start.25
  296.6 4.1 %copy-start.27 = (bf16[2,2,512,128]{3,2,1,0:T(8,128)(2,1)}, bf16[2,2,512,128]{3,2,1,0:T(8,128)(2,1)S(1)}, u32[]{:S(2)}) copy-start(bf16[2,2,512,128]{3,2,1,0:T(8,128)(2,1)S(1)} %collective-permute-done.16.refs_3_) | copy-start | bytes 1572868
  296.6 8.1 %copy-start.8 = (bf16[2,2,512,128]{3,2,1,0:T(8,128)(2,1)S(1)}, bf16[2,2,512,128]{3,2,1,0:T(8,128)(2,1)}, u32[]{:S(2)}) copy-start(bf16[2,2,512,128]{3,2,1,0:T(8,128)(2,1)} %copy-done.7) | copy-start | bytes 1572868
  300.7 13.7 %collective-permute-start.20 = (bf16[2,2,512,128]{3,2,1,0:T(8,128)(2,1)S(1)}, bf16[2,2,512,128]{3,2,1,0:T(8,128)(2,1)}, u32[]{:S(2)}, u32[]{:S(2)}) collective-permute-start(bf16[2,2,512,128]{3,2,1,0:T(8,128)(2,1)S(1)} %second_product.9.refs_0_), channel_id=1, source_target_pairs={{3,1},{4,6},{9,11},{14,12},{19,17},{20,22},{25,27},{30,28}} | collective-permute-start | bytes 1572872 | tf_op jit(solution)/shard_map/ppermute | solution.py:310
  302.0 14.3 %collective-permute-start.21 = (bf16[2,2,512,128]{3,2,1,0:T(8,128)(2,1)S(1)}, bf16[2,2,512,128]{3,2,1,0:T(8,128)(2,1)}, u32[]{:S(2)}, u32[]{:S(2)}) collective-permute-start(bf16[2,2,512,128]{3,2,1,0:T(8,128)(2,1)S(1)} %second_product.9.refs_0_), channel_id=1, source_target_pairs={{2,1},{5,6},{8,11},{15,12},{18,17},{21,22},{24,27},{31,28}} | collective-permute-start | bytes 1572872 | tf_op jit(solution)/shard_map/ppermute | solution.py:310
  303.3 13.1 %collective-permute-start.22 = (bf16[2,2,512,128]{3,2,1,0:T(8,128)(2,1)S(1)}, bf16[2,2,512,128]{3,2,1,0:T(8,128)(2,1)}, u32[]{:S(2)}, u32[]{:S(2)}) collective-permute-start(bf16[2,2,512,128]{3,2,1,0:T(8,128)(2,1)S(1)} %second_product.9.refs_0_), channel_id=1, source_target_pairs={{0,1},{7,6},{10,11},{13,12},{16,17},{23,22},{26,27},{29,28}} | collective-permute-start | bytes 1572872 | tf_op jit(solution)/shard_map/ppermute | solution.py:310
  304.7 1.0 copy-start.24
  305.7 1.0 copy-start.26
  306.8 1.0 copy-start.28
Sparse Core Ops, SparseCore 0:
  37.7 57.9 all-gather.2

commit v17 on v15

--- a/solution.py
+++ b/solution.py
@@ -8,13 +8,13 @@
 
 F32 = jnp.float32
 BF16 = jnp.bfloat16
-VMEM_BYTES = 26 * 1024 * 1024
+MIB = 1024 * 1024
 LIGHT = pl.CostEstimate(flops=0, bytes_accessed=0, transcendentals=0)
 
 
-def params(steps):
+def params(steps, mib):
     return pltpu.CompilerParams(
-        dimension_semantics=("arbitrary",) * steps, vmem_limit_bytes=VMEM_BYTES
+        dimension_semantics=("arbitrary",) * steps, vmem_limit_bytes=mib * MIB
     )
 
 
@@ -76,7 +76,7 @@
         out_specs=pl.BlockSpec((mpo_count, phys, 2, row_tile, col_tile), lambda i, j: (0, 0, 0, i, j)),
         out_shape=jax.ShapeDtypeStruct((mpo_count, phys, 2, rows, cols), BF16),
         scratch_shapes=[pltpu.VMEM((2 * w_local, 2, phys * row_tile, col_tile), F32)],
-        compiler_params=params(2),
+        compiler_params=params(2, 28),
         cost_estimate=LIGHT,
         name="first_product",
     )(blocks, mpo, site, *envs)
@@ -108,7 +108,7 @@
         + [pl.BlockSpec(site.shape, lambda v: (0, 0, 0, 0)) for site in sites],
         out_specs=pl.BlockSpec((1, 2, rows, y_rows), lambda v: (v, 0, 0, 0)),
         out_shape=jax.ShapeDtypeStruct((mpo_count, 2, rows, y_rows), BF16),
-        compiler_params=params(1),
+        compiler_params=params(1, 20),
         cost_estimate=LIGHT,
         name="second_product",
     )(pick, own, sib, *sites)
@@ -151,7 +151,7 @@
             out_specs=pl.BlockSpec((1, 1, rows, 2 * half), lambda v, p, pick: (v, p, 0, 0)),
         ),
         out_shape=jax.ShapeDtypeStruct((mpo_count, 2, rows, 2 * half), F32),
-        compiler_params=params(2),
+        compiler_params=params(2, 16),
         cost_estimate=LIGHT,
         name="finish",
     )(pick, mine, siblings, *part)
@@ -196,7 +196,7 @@
             pltpu.VMEM((2, mpo_count, 2, rows, width), F32),
             pltpu.SemaphoreType.DMA((2, mpo_count, 2)),
         ],
-        compiler_params=pltpu.CompilerParams(vmem_limit_bytes=VMEM_BYTES),
+        compiler_params=pltpu.CompilerParams(vmem_limit_bytes=12 * MIB),
         cost_estimate=LIGHT,
         name="finish_last",
     )(pick, *part, out)

time: 315 us -> 315 us (level)
    unnamed x66 -> x68, local copies, waits for them, and re-layouts: 21 us -> 21 us
where the time goes in v17:
time: 315 us; the launch traced here: 314 us
  waiting for transfers between devices  188 us (60%)
  Pallas kernels  55.1 us (17%)
  local copies, waits for them, and re-layouts  29.6 us (9%)
  starting transfers between devices  27.7 us (9%)
  other arithmetic  13.6 us (4%)
    ppermute x12, waiting for transfers between devices, ring(): lax.ppermute(value, 'row', [(r, (r + 1) % row_count) for r in range(row_c...  169 us
    pallas_call x5, Pallas kernels, second_product(): pl.pallas_call(second_kernel, grid=(mpo_count,), in_specs=[pl.BlockSpec(m...  25.6 us
    pallas_call x1, Pallas kernels, first_product(): pl.pallas_call(functools.partial(first_kernel, w_local), grid=(rows // ro...  22.8 us
    unnamed x68, local copies, waits for them, and re-layouts  21 us
    ppermute x6, waiting for transfers between devices, send(): lax.ppermute(value, axes, [(place(r, 1 - c if turned else c, 1 - d if cro...  11 us
    ppermute x3, starting transfers between devices, turn_to_goal(): lax.ppermute(value, axes, [(place(r, 1 - c, d), place(r, c, d)) for r, (c...  9.49 us
    ppermute x6, starting transfers between devices, send(): lax.ppermute(value, axes, [(place(r, 1 - c if turned else c, 1 - d if cro...  8.28 us
    ppermute x4, waiting for transfers between devices, swap(): return lax.ppermute(value, 'depth', [(0, 1), (1, 0)])  6.86 us
  transfers between devices with their start and end apart: 26, of which 17 were waited for; matrix products, arithmetic and copies ran while one was open for 6% of the time, Pallas kernels for 17%

profile of v17, /device:TPU:1, one launch (start us, length us, event | category | flops | bytes accessed | tf_op | source)
XLA Modules:
  0.0 314.3 jit_solution(6028364513736329969)
XLA Ops:
  0.0 2.7 constant_dynamic-slice_fusion
  2.8 2.7 collective-permute-start.3
  5.6 3.9 %copy.9 = bf16[2,512,2,1024]{3,1,2,0:T(8,128)(2,1)S(1)} copy(bf16[2,512,2,1024]{3,2,1,0:T(2,128)(2,1)} %param.4) | data formatting | bytes 8388608 | tf_op jit(solution)/shard_map/optimization_barrier | solution.py:206
  9.5 0.2 dynamic-slice_bitcast_fusion
  9.7 2.4 collective-permute-start.1
  12.1 1.3 collective-permute-start.2
  13.4 17.7 %collective-permute-done.3.refs_2_ = bf16[1,2,512,512]{3,2,1,0:T(8,128)(2,1)S(1)} collective-permute-done((bf16[1,2,512,512]{3,2,1,0:T(8,128)(2,1)S(1)}, bf16[1,2,512,512]{3,2,1,0:T(8,128)(2,1)S(1)}, u32[]{:S(2)}, u32[]{:S(2)}) %collective-permute-start.3) | collective-permute-done | bytes 1048608 | tf_op jit(solution)/shard_map/ppermute | solution.py:269
  31.1 1.0 copy-done.14
  32.0 21.6 %collective-permute-done.2.refs_3_ = bf16[1,2,512,512]{3,2,1,0:T(8,128)(2,1)} collective-permute-done((bf16[1,2,512,512]{3,2,1,0:T(8,128)(2,1)S(1)}, bf16[1,2,512,512]{3,2,1,0:T(8,128)(2,1)}, u32[]{:S(2)}, u32[]{:S(2)}) %collective-permute-start.2) | collective-permute-done | bytes 1048608 | tf_op jit(solution)/shard_map/ppermute | solution.py:269
  53.6 22.4 %collective-permute-done.4.refs_4_ = bf16[1,2,512,512]{3,2,1,0:T(8,128)(2,1)S(1)} collective-permute-done((bf16[1,2,512,512]{3,2,1,0:T(8,128)(2,1)S(1)}, bf16[1,2,512,512]{3,2,1,0:T(8,128)(2,1)S(1)}, u32[]{:S(2)}, u32[]{:S(2)}) %collective-permute-start.4) | collective-permute-done | bytes 1048608 | tf_op jit(solution)/shard_map/ppermute | solution.py:269
  76.0 1.0 copy-done.16
  77.0 0.6 collective-permute-start.5
  77.6 1.8 fusion
  79.4 0.8 collective-permute-start.7
  80.2 24.2 %collective-permute-done.6.refs_5_ = bf16[1,2,512,512]{3,2,1,0:T(8,128)(2,1)} collective-permute-done((bf16[1,2,512,512]{3,2,1,0:T(8,128)(2,1)}, bf16[1,2,512,512]{3,2,1,0:T(8,128)(2,1)}, u32[]{:S(2)}, u32[]{:S(2)}) %collective-permute-start.6) | collective-permute-done | bytes 1048608 | tf_op jit(solution)/shard_map/ppermute | solution.py:269
  104.4 5.5 %maximum_select_fusion.1 = bf16[1,2,2,512,1024]{4,3,2,1,0:T(8,128)(2,1)S(1)} fusion(bf16[1,2,2,256,1024]{4,3,2,1,0:T(8,128)(2,1)} %bitcast.10, bf16[1,2,2,256,1024]{4,3,2,1,0:T(8,128)(2,1)} %bitcast.9, pred[]{:T(512)S(6)} %eq.23), kind=kLoop, calls=%fused_computation.1 | loop fusion | flops 18874368 | bytes 8388609 | tf_op jit(solution)/shard_map/jit(_where)/select_n | solution.py:273
  109.9 4.1 %maximum_select_fusion.site_ref = bf16[2,2,2,512,1024]{4,3,2,1,0:T(8,128)(2,1)} fusion(bf16[1,2,2,512,1024]{4,3,2,1,0:T(8,128)(2,1)S(1)} %maximum_select_fusion.1, bf16[1,2,2,512,1024]{4,3,2,1,0:T(8,128)(2,1)S(1)} %bitcast.15, pred[]{:T(512)S(6)} %eq.22), kind=kLoop, calls=%fused_computation | loop fusion | flops 12582912 | bytes 16777216 | tf_op jit(solution)/shard_map/jit(_where)/select_n | solution.py:290
  114.0 12.8 %collective-permute-done.7.refs_6_ = bf16[1,2,512,512]{3,2,1,0:T(8,128)(2,1)S(1)} collective-permute-done((bf16[1,2,512,512]{3,2,1,0:T(8,128)(2,1)}, bf16[1,2,512,512]{3,2,1,0:T(8,128)(2,1)S(1)}, u32[]{:S(2)}, u32[]{:S(2)}) %collective-permute-start.7) | collective-permute-done | bytes 1048608 | tf_op jit(solution)/shard_map/ppermute | solution.py:269
  126.8 1.0 copy-done.18
  127.8 21.5 %collective-permute-done.8.refs_7_ = bf16[1,2,512,512]{3,2,1,0:T(8,128)(2,1)S(1)} collective-permute-done((bf16[1,2,512,512]{3,2,1,0:T(8,128)(2,1)}, bf16[1,2,512,512]{3,2,1,0:T(8,128)(2,1)S(1)}, u32[]{:S(2)}, u32[]{:S(2)}) %collective-permute-start.8) | collective-permute-done | bytes 1048608 | tf_op jit(solution)/shard_map/ppermute | solution.py:269
  149.3 1.0 copy-done.20
  150.3 0.1 pad_add_fusion.1.block_ref
  150.4 3.4 %copy-done.6 = bf16[2,2,2,512,1024]{4,3,2,1,0:T(8,128)(2,1)S(1)} copy-done((bf16[2,2,2,512,1024]{4,3,2,1,0:T(8,128)(2,1)S(1)}, bf16[2,2,2,512,1024]{4,3,2,1,0:T(8,128)(2,1)}, u32[]{:S(2)}) %copy-start.6) | copy-done | bytes 8388632
  153.7 1.2 copy-done.13
  155.0 1.2 copy-done.15
  156.2 1.2 copy-done.17
  157.4 1.2 copy-done.19
  158.6 1.2 copy-done.21
  159.9 22.8 %first_product.1.own_ref = bf16[2,2,2,512,512]{4,3,2,1,0:T(8,128)(2,1)S(1)} custom-call(s32[4]{0:T(128)S(1)} %pad_add_fusion.1.block_ref, f32[2,2,2,2]{3,2,1,0:T(2,128)S(1)} %pad_maximum_fusion.mpo_ref, bf16[2,2,2,512,1024]{4,3,2,1,0:T(8,128)(2,1)S(1)} %copy-done.6, bf16[1,2,512,512]{3,2,1,0:T(8,128)(2,1)S(1)} %get-tuple-element.31.refs_0_, ...), custom_call_target="tpu_custom_call" | custom-call | tf_op jit(solution)/shard_map/first_product/pallas_call | solution.py:67
  182.7 11.7 %collective-permute-done.10.refs_1_ = bf16[2,2,128,1024]{3,2,1,0:T(8,128)(2,1)} collective-permute-done((bf16[2,2,128,1024]{3,2,1,0:T(8,128)(2,1)S(1)}, bf16[2,2,128,1024]{3,2,1,0:T(8,128)(2,1)}, u32[]{:S(2)}, u32[]{:S(2)}) %collective-permute-start.10) | collective-permute-done | bytes 1048608 | tf_op jit(solution)/shard_map/ppermute | solution.py:269
  194.3 0.8 collective-permute-start.11
  195.2 6.8 %collective-permute-done.11.sib_ref = bf16[2,2,2,512,512]{4,3,2,1,0:T(8,128)(2,1)S(1)} collective-permute-done((bf16[2,2,2,512,512]{4,3,2,1,0:T(8,128)(2,1)S(1)}, bf16[2,2,2,512,512]{4,3,2,1,0:T(8,128)(2,1)S(1)}, u32[]{:S(2)}, u32[]{:S(2)}) %collective-permute-start.11) | collective-permute-done | bytes 4194336 | tf_op jit(solution)/shard_map/ppermute | solution.py:210
  202.0 4.8 %second_product.5 = bf16[2,2,512,256]{3,2,1,0:T(8,128)(2,1)S(1)} custom-call(s32[1]{0:T(128)} %bitcast.1.pick_ref, bf16[2,2,2,512,512]{4,3,2,1,0:T(8,128)(2,1)S(1)} %first_product.1.own_ref, bf16[2,2,2,512,512]{4,3,2,1,0:T(8,128)(2,1)S(1)} %collective-permute-done.11.sib_ref, bf16[2,2,128,1024]{3,2,1,0:T(8,128)(2,1)S(1)} %get-tuple-element.17.refs_0_, ...), custom_call_target="tpu_custom_call" | custom-call | tf_op jit(solution)/shard_map/second_product/pallas_call | solution.py:104
  206.7 1.3 collective-permute-start.13
  208.1 14.0 %collective-permute-done.12.refs_0_ = bf16[2,2,128,1024]{3,2,1,0:T(8,128)(2,1)} collective-permute-done((bf16[2,2,128,1024]{3,2,1,0:T(8,128)(2,1)}, bf16[2,2,128,1024]{3,2,1,0:T(8,128)(2,1)}, u32[]{:S(2)}, u32[]{:S(2)}) %collective-permute-start.12) | collective-permute-done | bytes 1048608 | tf_op jit(solution)/shard_map/ppermute | solution.py:269
  222.1 6.3 %second_product.6 = bf16[2,2,512,256]{3,2,1,0:T(8,128)(2,1)S(1)} custom-call(s32[1]{0:T(128)} %bitcast.1.pick_ref, bf16[2,2,2,512,512]{4,3,2,1,0:T(8,128)(2,1)S(1)} %first_product.1.own_ref, bf16[2,2,2,512,512]{4,3,2,1,0:T(8,128)(2,1)S(1)} %collective-permute-done.11.sib_ref, bf16[2,2,128,1024]{3,2,1,0:T(8,128)(2,1)} %collective-permute-done.9.refs_0_, ...), custom_call_target="tpu_custom_call" | custom-call | tf_op jit(solution)/shard_map/second_product/pallas_call | solution.py:104
  228.4 4.1 %collective-permute-start.19 = (bf16[2,2,512,256]{3,2,1,0:T(8,128)(2,1)S(1)}, bf16[2,2,512,256]{3,2,1,0:T(8,128)(2,1)}, u32[]{:S(2)}, u32[]{:S(2)}) collective-permute-start(bf16[2,2,512,256]{3,2,1,0:T(8,128)(2,1)S(1)} %second_product.6), channel_id=1, source_target_pairs={{0,2},{1,3},{6,4},{7,5},{10,8},{11,9},{12,14},{13,15},{16,18},{17,... | collective-permute-start | bytes 3145736 | tf_op jit(solution)/shard_map/ppermute | solution.py:312
  232.5 0.6 collective-permute-done.13
  233.1 11.4 %collective-permute-done.14.refs_1_ = bf16[2,2,128,1024]{3,2,1,0:T(8,128)(2,1)} collective-permute-done((bf16[2,2,128,1024]{3,2,1,0:T(8,128)(2,1)}, bf16[2,2,128,1024]{3,2,1,0:T(8,128)(2,1)}, u32[]{:S(2)}, u32[]{:S(2)}) %collective-permute-start.14) | collective-permute-done | bytes 1048608 | tf_op jit(solution)/shard_map/ppermute | solution.py:269
  244.5 6.3 %second_product.7 = bf16[2,2,512,256]{3,2,1,0:T(8,128)(2,1)S(1)} custom-call(s32[1]{0:T(128)} %bitcast.1.pick_ref, bf16[2,2,2,512,512]{4,3,2,1,0:T(8,128)(2,1)S(1)} %first_product.1.own_ref, bf16[2,2,2,512,512]{4,3,2,1,0:T(8,128)(2,1)S(1)} %collective-permute-done.11.sib_ref, bf16[2,2,128,1024]{3,2,1,0:T(8,128)(2,1)} %collective-permute-done.12.refs_0_, ...), custom_call_target="tpu_custom_call" | custom-call | tf_op jit(solution)/shard_map/second_product/pallas_call | solution.py:104
  250.9 4.1 %collective-permute-start.20 = (bf16[2,2,512,256]{3,2,1,0:T(8,128)(2,1)S(1)}, bf16[2,2,512,256]{3,2,1,0:T(8,128)(2,1)}, u32[]{:S(2)}, u32[]{:S(2)}) collective-permute-start(bf16[2,2,512,256]{3,2,1,0:T(8,128)(2,1)S(1)} %second_product.7), channel_id=1, source_target_pairs={{0,2},{1,3},{4,6},{5,7},{10,8},{11,9},{14,12},{15,13},{16,18},{17,... | collective-permute-start | bytes 3145736 | tf_op jit(solution)/shard_map/ppermute | solution.py:312
  255.0 12.0 %collective-permute-done.15.refs_0_ = bf16[2,2,128,1024]{3,2,1,0:T(8,128)(2,1)} collective-permute-done((bf16[2,2,128,1024]{3,2,1,0:T(8,128)(2,1)}, bf16[2,2,128,1024]{3,2,1,0:T(8,128)(2,1)}, u32[]{:S(2)}, u32[]{:S(2)}) %collective-permute-start.15) | collective-permute-done | bytes 1048608 | tf_op jit(solution)/shard_map/ppermute | solution.py:269
  267.0 2.2 copy-done.1
  269.2 2.2 copy-done.4
  271.4 4.0 %second_product.8.refs_0_ = bf16[2,2,512,128]{3,2,1,0:T(8,128)(2,1)S(1)} custom-call(s32[1]{0:T(128)} %bitcast.1.pick_ref, bf16[2,2,2,512,512]{4,3,2,1,0:T(8,128)(2,1)S(1)} %copy-done.1, bf16[2,2,2,512,512]{4,3,2,1,0:T(8,128)(2,1)S(1)} %copy-done.4, bf16[2,2,128,1024]{3,2,1,0:T(8,128)(2,1)} %collective-permute-done.15.refs_0_), custom_call_target="tpu_custom_call" | custom-call | tf_op jit(solution)/shard_map/second_product/pallas_call | solution.py:104
  275.4 1.6 collective-permute-start.16
  277.0 1.6 collective-permute-start.17
  278.6 1.3 collective-permute-start.18
  279.9 3.9 %select_convert_fusion = (bf16[2,2,512,256]{3,2,1,0:T(8,128)(2,1)}, f32[2,2,512,256]{3,2,1,0:T(8,128)S(1)}) fusion(bf16[2,2,512,256]{3,2,1,0:T(8,128)(2,1)S(1)} %copy-done.32, bf16[2,2,512,256]{3,2,1,0:T(8,128)(2,1)S(1)} %second_product.5, bf16[2,2,512,256]{3,2,1,0:T(8,128)(2,1)} %collective-permute-done.19, bf16[2,2,512,256]{3,2,1,0:T(8,128)(2,1)S(1)} %copy-done.8, ...), kind=kLoop, calls=%fused_computation.2 | loop fusion | flops 7340032 | bytes 9437188 | tf_op jit(solution)/shard_map/convert_element_type | solution.py:346
  283.8 1.2 collective-permute-start.25
  284.9 4.6 %collective-permute-done.16.refs_1_ = bf16[2,2,512,128]{3,2,1,0:T(8,128)(2,1)S(1)} collective-permute-done((bf16[2,2,512,128]{3,2,1,0:T(8,128)(2,1)S(1)}, bf16[2,2,512,128]{3,2,1,0:T(8,128)(2,1)S(1)}, u32[]{:S(2)}, u32[]{:S(2)}) %collective-permute-start.16) | collective-permute-done | bytes 524320 | tf_op jit(solution)/shard_map/ppermute | solution.py:319
  289.6 1.8 collective-permute-done.17.refs_2_
  291.4 4.3 %second_product.9.refs_0_ = bf16[2,2,512,128]{3,2,1,0:T(8,128)(2,1)S(1)} custom-call(s32[1]{0:T(128)} %bitcast.1.pick_ref, bf16[2,2,2,512,512]{4,3,2,1,0:T(8,128)(2,1)S(1)} %copy-done.2, bf16[2,2,2,512,512]{4,3,2,1,0:T(8,128)(2,1)S(1)} %copy-done.5, bf16[2,2,128,1024]{3,2,1,0:T(8,128)(2,1)} %collective-permute-done.21.refs_0_), custom_call_target="tpu_custom_call" | custom-call | tf_op jit(solution)/shard_map/second_product/pallas_call | solution.py:104
  295.7 1.3 collective-permute-start.22
  297.0 1.3 collective-permute-start.23
  298.3 1.3 collective-permute-start.24
  299.6 0.1 pad_add_fusion.pick_ref
  299.7 1.0 copy-done.23
  300.7 1.0 copy-done.25
  301.8 1.0 copy-done.27
  302.8 4.0 %finish.1.refs_4_ = f32[2,2,512,512]{3,2,1,0:T(8,128)} custom-call(s32[2]{0:T(128)S(1)} %pad_add_fusion.pick_ref, f32[2,2,512,256]{3,2,1,0:T(8,128)S(1)} %get-tuple-element.26.mine_ref, bf16[2,2,512,256]{3,2,1,0:T(8,128)(2,1)} %collective-permute-done.25.siblings_ref, bf16[2,2,512,128]{3,2,1,0:T(8,128)(2,1)S(1)} %copy-done.11, ...), custom_call_target="tpu_custom_call" | custom-call | tf_op jit(solution)/shard_map/finish/pallas_call | solution.py:145
  306.8 2.6 collective-permute-done.22.refs_1_
  309.4 1.9 collective-permute-done.23.refs_2_
  311.4 2.8 finish_last.1
  (75 shorter events, 0.3 us)
Async XLA Ops:
  2.7 2.9 collective-permute-start
  2.8 28.3 %collective-permute-start.3 = (bf16[1,2,512,512]{3,2,1,0:T(8,128)(2,1)S(1)}, bf16[1,2,512,512]{3,2,1,0:T(8,128)(2,1)S(1)}, u32[]{:S(2)}, u32[]{:S(2)}) collective-permute-start(bf16[1,2,512,512]{3,2,1,0:T(8,128)(2,1)S(1)} %get-tuple-element.31.refs_0_), channel_id=1, source_target_pairs={{0,4},{4,8},{8,12},{12,0},{1,5},{5,9},{9,13},{13,1},{2,6},{6,10},{... | collective-permute-start | bytes 3145736 | tf_op jit(solution)/shard_map/ppermute | solution.py:269
  5.6 6.5 %copy-start.12 = (bf16[1,2,512,512]{3,2,1,0:T(8,128)(2,1)}, bf16[1,2,512,512]{3,2,1,0:T(8,128)(2,1)S(1)}, u32[]{:S(2)}) copy-start(bf16[1,2,512,512]{3,2,1,0:T(8,128)(2,1)S(1)} %collective-permute-done.refs_1_) | copy-start | bytes 3145732
  9.5 67.5 %copy-start.28 = (bf16[2,512,2,1024]{3,1,2,0:T(8,128)(2,1)}, bf16[2,512,2,1024]{3,1,2,0:T(8,128)(2,1)S(1)}, u32[]{:S(2)}) copy-start(bf16[2,512,2,1024]{3,1,2,0:T(8,128)(2,1)S(1)} %copy.9) | copy-start | bytes 12582916
  9.7 67.9 %copy-start.30 = (bf16[2,2,256,1024]{3,2,1,0:T(8,128)(2,1)}, bf16[2,2,256,1024]{3,2,1,0:T(8,128)(2,1)S(1)}, u32[]{:S(2)}) copy-start(bf16[2,2,256,1024]{3,2,1,0:T(8,128)(2,1)S(1)} %dynamic-slice_bitcast_fusion) | copy-start | bytes 6291460
  9.7 67.3 %collective-permute-start.1 = (bf16[2,2,256,1024]{3,2,1,0:T(8,128)(2,1)S(1)}, bf16[2,2,256,1024]{3,2,1,0:T(8,128)(2,1)}, u32[]{:S(2)}, u32[]{:S(2)}) collective-permute-start(bf16[2,2,256,1024]{3,2,1,0:T(8,128)(2,1)S(1)} %dynamic-slice_bitcast_fusion), channel_id=1, source_target_pairs={{0,2},{2,0},{1,3},{3,1},{4,6},{6,4},{5,7},{7,5},{8,10},{10,8},{9,1... | collective-permute-start | bytes 6291464 | tf_op jit(solution)/shard_map/ppermute | solution.py:272
  12.1 41.5 %collective-permute-start.2 = (bf16[1,2,512,512]{3,2,1,0:T(8,128)(2,1)S(1)}, bf16[1,2,512,512]{3,2,1,0:T(8,128)(2,1)}, u32[]{:S(2)}, u32[]{:S(2)}) collective-permute-start(bf16[1,2,512,512]{3,2,1,0:T(8,128)(2,1)S(1)} %collective-permute-done.refs_1_), channel_id=1, source_target_pairs={{0,4},{4,8},{8,12},{12,0},{1,5},{5,9},{9,13},{13,1},{2,6},{6,10},{... | collective-permute-start | bytes 3145736 | tf_op jit(solution)/shard_map/ppermute | solution.py:269
  31.1 44.9 %collective-permute-start.4 = (bf16[1,2,512,512]{3,2,1,0:T(8,128)(2,1)S(1)}, bf16[1,2,512,512]{3,2,1,0:T(8,128)(2,1)S(1)}, u32[]{:S(2)}, u32[]{:S(2)}) collective-permute-start(bf16[1,2,512,512]{3,2,1,0:T(8,128)(2,1)S(1)} %collective-permute-done.3.refs_2_), channel_id=1, source_target_pairs={{0,4},{4,8},{8,12},{12,0},{1,5},{5,9},{9,13},{13,1},{2,6},{6,10},{... | collective-permute-start | bytes 3145736 | tf_op jit(solution)/shard_map/ppermute | solution.py:269
  31.1 1.0 copy-start.14
  76.0 1.0 copy-start.16
  77.0 27.4 %collective-permute-start.5 = (bf16[2,2,256,1024]{3,2,1,0:T(8,128)(2,1)}, bf16[2,2,256,1024]{3,2,1,0:T(8,128)(2,1)}, u32[]{:S(2)}, u32[]{:S(2)}) collective-permute-start(bf16[2,2,256,1024]{3,2,1,0:T(8,128)(2,1)} %collective-permute-done.1), channel_id=1, source_target_pairs={{0,1},{1,0},{2,3},{3,2},{4,5},{5,4},{6,7},{7,6},{8,9},{9,8},{10,11... | collective-permute-start | bytes 6291464 | tf_op jit(solution)/shard_map/ppermute | solution.py:210
  77.6 26.8 %collective-permute-start.6 = (bf16[1,2,512,512]{3,2,1,0:T(8,128)(2,1)}, bf16[1,2,512,512]{3,2,1,0:T(8,128)(2,1)}, u32[]{:S(2)}, u32[]{:S(2)}) collective-permute-start(bf16[1,2,512,512]{3,2,1,0:T(8,128)(2,1)} %collective-permute-done.2.refs_3_), channel_id=1, source_target_pairs={{0,4},{4,8},{8,12},{12,0},{1,5},{5,9},{9,13},{13,1},{2,6},{6,10},{... | collective-permute-start | bytes 3145736 | tf_op jit(solution)/shard_map/ppermute | solution.py:269
  79.4 47.4 %collective-permute-start.7 = (bf16[1,2,512,512]{3,2,1,0:T(8,128)(2,1)}, bf16[1,2,512,512]{3,2,1,0:T(8,128)(2,1)S(1)}, u32[]{:S(2)}, u32[]{:S(2)}) collective-permute-start(bf16[1,2,512,512]{3,2,1,0:T(8,128)(2,1)} %copy-done.16), channel_id=1, source_target_pairs={{0,4},{4,8},{8,12},{12,0},{1,5},{5,9},{9,13},{13,1},{2,6},{6,10},{... | collective-permute-start | bytes 3145736 | tf_op jit(solution)/shard_map/ppermute | solution.py:269
  104.4 44.8 %collective-permute-start.8 = (bf16[1,2,512,512]{3,2,1,0:T(8,128)(2,1)}, bf16[1,2,512,512]{3,2,1,0:T(8,128)(2,1)S(1)}, u32[]{:S(2)}, u32[]{:S(2)}) collective-permute-start(bf16[1,2,512,512]{3,2,1,0:T(8,128)(2,1)} %collective-permute-done.6.refs_5_), channel_id=1, source_target_pairs={{0,4},{4,8},{8,12},{12,0},{1,5},{5,9},{9,13},{13,1},{2,6},{6,10},{... | collective-permute-start | bytes 3145736 | tf_op jit(solution)/shard_map/ppermute | solution.py:269
  104.4 5.5 %copy-start.29 = (bf16[2,512,2,1024]{3,1,2,0:T(8,128)(2,1)S(1)}, bf16[2,512,2,1024]{3,1,2,0:T(8,128)(2,1)}, u32[]{:S(2)}) copy-start(bf16[2,512,2,1024]{3,1,2,0:T(8,128)(2,1)} %copy-done.28) | copy-start | bytes 12582916
  109.9 40.4 %copy-start.33 = (f32[2,2,2,2]{3,2,1,0:T(2,128)S(1)}, f32[2,2,2,2]{3,2,1,0:T(2,128)}, u32[]{:S(2)}) copy-start(f32[2,2,2,2]{3,2,1,0:T(2,128)} %param.5) | copy-start | bytes 196
  126.8 1.0 copy-start.18
  127.8 54.9 %collective-permute-start.9 = (bf16[2,2,128,1024]{3,2,1,0:T(8,128)(2,1)S(1)}, bf16[2,2,128,1024]{3,2,1,0:T(8,128)(2,1)}, u32[]{:S(2)}, u32[]{:S(2)}) collective-permute-start(bf16[2,2,128,1024]{3,2,1,0:T(8,128)(2,1)S(1)} %get-tuple-element.17.refs_0_), channel_id=1, source_target_pairs={{0,4},{4,8},{8,12},{12,0},{1,5},{5,9},{9,13},{13,1},{2,6},{6,10},{... | collective-permute-start | bytes 3145736 | tf_op jit(solution)/shard_map/ppermute | solution.py:269
  149.3 1.0 copy-start.20
  150.3 44.1 %collective-permute-start.10 = (bf16[2,2,128,1024]{3,2,1,0:T(8,128)(2,1)S(1)}, bf16[2,2,128,1024]{3,2,1,0:T(8,128)(2,1)}, u32[]{:S(2)}, u32[]{:S(2)}) collective-permute-start(bf16[2,2,128,1024]{3,2,1,0:T(8,128)(2,1)S(1)} %get-tuple-element.18.refs_1_), channel_id=1, source_target_pairs={{0,4},{4,8},{8,12},{12,0},{1,5},{5,9},{9,13},{13,1},{2,6},{6,10},{... | collective-permute-start | bytes 3145736 | tf_op jit(solution)/shard_map/ppermute | solution.py:269
  150.4 3.4 %copy-start.6 = (bf16[2,2,2,512,1024]{4,3,2,1,0:T(8,128)(2,1)S(1)}, bf16[2,2,2,512,1024]{4,3,2,1,0:T(8,128)(2,1)}, u32[]{:S(2)}) copy-start(bf16[2,2,2,512,1024]{4,3,2,1,0:T(8,128)(2,1)} %maximum_select_fusion.site_ref) | copy-start | bytes 25165828
  153.7 1.2 copy-start.13
  155.0 1.2 copy-start.15
  156.2 1.2 copy-start.17
  157.4 1.2 copy-start.19
  158.6 1.2 copy-start.21
  182.6 61.9 %copy-start = (bf16[2,2,2,512,512]{4,3,2,1,0:T(8,128)(2,1)}, bf16[2,2,2,512,512]{4,3,2,1,0:T(8,128)(2,1)S(1)}, u32[]{:S(2)}) copy-start(bf16[2,2,2,512,512]{4,3,2,1,0:T(8,128)(2,1)S(1)} %first_product.1.own_ref) | copy-start | bytes 12582916
  194.3 7.6 %collective-permute-start.11 = (bf16[2,2,2,512,512]{4,3,2,1,0:T(8,128)(2,1)S(1)}, bf16[2,2,2,512,512]{4,3,2,1,0:T(8,128)(2,1)S(1)}, u32[]{:S(2)}, u32[]{:S(2)}) collective-permute-start(bf16[2,2,2,512,512]{4,3,2,1,0:T(8,128)(2,1)S(1)} %first_product.1.own_ref), channel_id=1, source_target_pairs={{0,1},{1,0},{2,3},{3,2},{4,5},{5,4},{6,7},{7,6},{8,9},{9,8},{10,11... | collective-permute-start | bytes 12582920 | tf_op jit(solution)/shard_map/ppermute | solution.py:210
  195.2 26.9 %collective-permute-start.12 = (bf16[2,2,128,1024]{3,2,1,0:T(8,128)(2,1)}, bf16[2,2,128,1024]{3,2,1,0:T(8,128)(2,1)}, u32[]{:S(2)}, u32[]{:S(2)}) collective-permute-start(bf16[2,2,128,1024]{3,2,1,0:T(8,128)(2,1)} %collective-permute-done.9.refs_0_), channel_id=1, source_target_pairs={{0,4},{4,8},{8,12},{12,0},{1,5},{5,9},{9,13},{13,1},{2,6},{6,10},{... | collective-permute-start | bytes 3145736 | tf_op jit(solution)/shard_map/ppermute | solution.py:269
  202.0 42.6 %copy-start.3 = (bf16[2,2,2,512,512]{4,3,2,1,0:T(8,128)(2,1)}, bf16[2,2,2,512,512]{4,3,2,1,0:T(8,128)(2,1)S(1)}, u32[]{:S(2)}) copy-start(bf16[2,2,2,512,512]{4,3,2,1,0:T(8,128)(2,1)S(1)} %collective-permute-done.11.sib_ref) | copy-start | bytes 12582916
  206.7 26.4 %collective-permute-start.13 = (bf16[2,2,512,256]{3,2,1,0:T(8,128)(2,1)S(1)}, bf16[2,2,512,256]{3,2,1,0:T(8,128)(2,1)S(1)}, u32[]{:S(2)}, u32[]{:S(2)}) collective-permute-start(bf16[2,2,512,256]{3,2,1,0:T(8,128)(2,1)S(1)} %second_product.5), channel_id=1, source_target_pairs={{2,0},{3,1},{6,4},{7,5},{8,10},{9,11},{12,14},{13,15},{18,16},{19,... | collective-permute-start | bytes 3145736 | tf_op jit(solution)/shard_map/ppermute | solution.py:312
  208.0 36.5 %collective-permute-start.14 = (bf16[2,2,128,1024]{3,2,1,0:T(8,128)(2,1)}, bf16[2,2,128,1024]{3,2,1,0:T(8,128)(2,1)}, u32[]{:S(2)}, u32[]{:S(2)}) collective-permute-start(bf16[2,2,128,1024]{3,2,1,0:T(8,128)(2,1)} %collective-permute-done.10.refs_1_), channel_id=1, source_target_pairs={{0,4},{4,8},{8,12},{12,0},{1,5},{5,9},{9,13},{13,1},{2,6},{6,10},{... | collective-permute-start | bytes 3145736 | tf_op jit(solution)/shard_map/ppermute | solution.py:269
  222.1 44.9 %collective-permute-start.15 = (bf16[2,2,128,1024]{3,2,1,0:T(8,128)(2,1)}, bf16[2,2,128,1024]{3,2,1,0:T(8,128)(2,1)}, u32[]{:S(2)}, u32[]{:S(2)}) collective-permute-start(bf16[2,2,128,1024]{3,2,1,0:T(8,128)(2,1)} %collective-permute-done.12.refs_0_), channel_id=1, source_target_pairs={{0,4},{4,8},{8,12},{12,0},{1,5},{5,9},{9,13},{13,1},{2,6},{6,10},{... | collective-permute-start | bytes 3145736 | tf_op jit(solution)/shard_map/ppermute | solution.py:269
  228.4 22.5 %copy-start.7 = (bf16[2,2,512,256]{3,2,1,0:T(8,128)(2,1)}, bf16[2,2,512,256]{3,2,1,0:T(8,128)(2,1)S(1)}, u32[]{:S(2)}) copy-start(bf16[2,2,512,256]{3,2,1,0:T(8,128)(2,1)S(1)} %second_product.6) | copy-start | bytes 3145732
  228.4 50.1 %collective-permute-start.19 = (bf16[2,2,512,256]{3,2,1,0:T(8,128)(2,1)S(1)}, bf16[2,2,512,256]{3,2,1,0:T(8,128)(2,1)}, u32[]{:S(2)}, u32[]{:S(2)}) collective-permute-start(bf16[2,2,512,256]{3,2,1,0:T(8,128)(2,1)S(1)} %second_product.6), channel_id=1, source_target_pairs={{0,2},{1,3},{6,4},{7,5},{10,8},{11,9},{12,14},{13,15},{16,18},{17,... | collective-permute-start | bytes 3145736 | tf_op jit(solution)/shard_map/ppermute | solution.py:312
  233.1 17.8 %copy-start.31 = (bf16[2,2,512,256]{3,2,1,0:T(8,128)(2,1)}, bf16[2,2,512,256]{3,2,1,0:T(8,128)(2,1)S(1)}, u32[]{:S(2)}) copy-start(bf16[2,2,512,256]{3,2,1,0:T(8,128)(2,1)S(1)} %collective-permute-done.13) | copy-start | bytes 3145732
  250.9 24.5 %copy-start.9 = (bf16[2,2,512,256]{3,2,1,0:T(8,128)(2,1)}, bf16[2,2,512,256]{3,2,1,0:T(8,128)(2,1)S(1)}, u32[]{:S(2)}) copy-start(bf16[2,2,512,256]{3,2,1,0:T(8,128)(2,1)S(1)} %second_product.7) | copy-start | bytes 3145732
  250.9 29.0 %collective-permute-start.20 = (bf16[2,2,512,256]{3,2,1,0:T(8,128)(2,1)S(1)}, bf16[2,2,512,256]{3,2,1,0:T(8,128)(2,1)}, u32[]{:S(2)}, u32[]{:S(2)}) collective-permute-start(bf16[2,2,512,256]{3,2,1,0:T(8,128)(2,1)S(1)} %second_product.7), channel_id=1, source_target_pairs={{0,2},{1,3},{4,6},{5,7},{10,8},{11,9},{14,12},{15,13},{16,18},{17,... | collective-permute-start | bytes 3145736 | tf_op jit(solution)/shard_map/ppermute | solution.py:312
  255.0 36.4 %collective-permute-start.21 = (bf16[2,2,128,1024]{3,2,1,0:T(8,128)(2,1)}, bf16[2,2,128,1024]{3,2,1,0:T(8,128)(2,1)}, u32[]{:S(2)}, u32[]{:S(2)}) collective-permute-start(bf16[2,2,128,1024]{3,2,1,0:T(8,128)(2,1)} %collective-permute-done.14.refs_1_), channel_id=1, source_target_pairs={{0,4},{4,8},{8,12},{12,0},{1,5},{5,9},{9,13},{13,1},{2,6},{6,10},{... | collective-permute-start | bytes 3145736 | tf_op jit(solution)/shard_map/ppermute | solution.py:269
  267.0 2.2 copy-start.1
  269.2 2.2 copy-start.4
  271.4 8.5 %copy-start.8 = (bf16[2,2,512,256]{3,2,1,0:T(8,128)(2,1)S(1)}, bf16[2,2,512,256]{3,2,1,0:T(8,128)(2,1)}, u32[]{:S(2)}) copy-start(bf16[2,2,512,256]{3,2,1,0:T(8,128)(2,1)} %copy-done.7) | copy-start | bytes 3145732
  271.4 8.5 %copy-start.32 = (bf16[2,2,512,256]{3,2,1,0:T(8,128)(2,1)S(1)}, bf16[2,2,512,256]{3,2,1,0:T(8,128)(2,1)}, u32[]{:S(2)}) copy-start(bf16[2,2,512,256]{3,2,1,0:T(8,128)(2,1)} %copy-done.31) | copy-start | bytes 3145732
  275.4 8.4 %copy-start.10 = (bf16[2,2,512,128]{3,2,1,0:T(8,128)(2,1)}, bf16[2,2,512,128]{3,2,1,0:T(8,128)(2,1)S(1)}, u32[]{:S(2)}) copy-start(bf16[2,2,512,128]{3,2,1,0:T(8,128)(2,1)S(1)} %second_product.8.refs_0_) | copy-start | bytes 1572868
  275.4 16.0 %copy-start.2 = (bf16[2,2,2,512,512]{4,3,2,1,0:T(8,128)(2,1)S(1)}, bf16[2,2,2,512,512]{4,3,2,1,0:T(8,128)(2,1)}, u32[]{:S(2)}) copy-start(bf16[2,2,2,512,512]{4,3,2,1,0:T(8,128)(2,1)} %copy-done) | copy-start | bytes 12582916
  275.4 16.0 %copy-start.5 = (bf16[2,2,2,512,512]{4,3,2,1,0:T(8,128)(2,1)S(1)}, bf16[2,2,2,512,512]{4,3,2,1,0:T(8,128)(2,1)}, u32[]{:S(2)}) copy-start(bf16[2,2,2,512,512]{4,3,2,1,0:T(8,128)(2,1)} %copy-done.3) | copy-start | bytes 12582916
  275.4 14.1 %collective-permute-start.16 = (bf16[2,2,512,128]{3,2,1,0:T(8,128)(2,1)S(1)}, bf16[2,2,512,128]{3,2,1,0:T(8,128)(2,1)S(1)}, u32[]{:S(2)}, u32[]{:S(2)}) collective-permute-start(bf16[2,2,512,128]{3,2,1,0:T(8,128)(2,1)S(1)} %second_product.8.refs_0_), channel_id=1, source_target_pairs={{3,1},{4,6},{9,11},{14,12},{19,17},{20,22},{25,27},{30,28}} | collective-permute-start | bytes 1572872 | tf_op jit(solution)/shard_map/ppermute | solution.py:319
  277.0 14.4 %collective-permute-start.17 = (bf16[2,2,512,128]{3,2,1,0:T(8,128)(2,1)S(1)}, bf16[2,2,512,128]{3,2,1,0:T(8,128)(2,1)S(1)}, u32[]{:S(2)}, u32[]{:S(2)}) collective-permute-start(bf16[2,2,512,128]{3,2,1,0:T(8,128)(2,1)S(1)} %second_product.8.refs_0_), channel_id=1, source_target_pairs={{2,1},{5,6},{8,11},{15,12},{18,17},{21,22},{24,27},{31,28}} | collective-permute-start | bytes 1572872 | tf_op jit(solution)/shard_map/ppermute | solution.py:319
  278.6 12.8 %collective-permute-start.18 = (bf16[2,2,512,128]{3,2,1,0:T(8,128)(2,1)S(1)}, bf16[2,2,512,128]{3,2,1,0:T(8,128)(2,1)S(1)}, u32[]{:S(2)}, u32[]{:S(2)}) collective-permute-start(bf16[2,2,512,128]{3,2,1,0:T(8,128)(2,1)S(1)} %second_product.8.refs_0_), channel_id=1, source_target_pairs={{0,1},{7,6},{10,11},{13,12},{16,17},{23,22},{26,27},{29,28}} | collective-permute-start | bytes 1572872 | tf_op jit(solution)/shard_map/ppermute | solution.py:319
  283.8 15.9 %collective-permute-start.25 = (bf16[2,2,512,256]{3,2,1,0:T(8,128)(2,1)}, bf16[2,2,512,256]{3,2,1,0:T(8,128)(2,1)}, u32[]{:S(2)}, u32[]{:S(2)}) collective-permute-start(bf16[2,2,512,256]{3,2,1,0:T(8,128)(2,1)} %get-tuple-element.25), channel_id=1, source_target_pairs={{0,1},{1,0},{2,3},{3,2},{4,5},{5,4},{6,7},{7,6},{8,9},{9,8},{10,11... | collective-permute-start | bytes 3145736 | tf_op jit(solution)/shard_map/ppermute | solution.py:210
  289.6 6.1 %copy-start.22 = (bf16[2,2,512,128]{3,2,1,0:T(8,128)(2,1)}, bf16[2,2,512,128]{3,2,1,0:T(8,128)(2,1)S(1)}, u32[]{:S(2)}) copy-start(bf16[2,2,512,128]{3,2,1,0:T(8,128)(2,1)S(1)} %collective-permute-done.16.refs_1_) | copy-start | bytes 1572868
  291.4 4.3 %copy-start.24 = (bf16[2,2,512,128]{3,2,1,0:T(8,128)(2,1)}, bf16[2,2,512,128]{3,2,1,0:T(8,128)(2,1)S(1)}, u32[]{:S(2)}) copy-start(bf16[2,2,512,128]{3,2,1,0:T(8,128)(2,1)S(1)} %collective-permute-done.17.refs_2_) | copy-start | bytes 1572868
  291.4 4.3 %copy-start.26 = (bf16[2,2,512,128]{3,2,1,0:T(8,128)(2,1)}, bf16[2,2,512,128]{3,2,1,0:T(8,128)(2,1)S(1)}, u32[]{:S(2)}) copy-start(bf16[2,2,512,128]{3,2,1,0:T(8,128)(2,1)S(1)} %collective-permute-done.18.refs_3_) | copy-start | bytes 1572868
  291.4 8.3 %copy-start.11 = (bf16[2,2,512,128]{3,2,1,0:T(8,128)(2,1)S(1)}, bf16[2,2,512,128]{3,2,1,0:T(8,128)(2,1)}, u32[]{:S(2)}) copy-start(bf16[2,2,512,128]{3,2,1,0:T(8,128)(2,1)} %copy-done.10) | copy-start | bytes 1572868
  295.7 13.7 %collective-permute-start.22 = (bf16[2,2,512,128]{3,2,1,0:T(8,128)(2,1)S(1)}, bf16[2,2,512,128]{3,2,1,0:T(8,128)(2,1)}, u32[]{:S(2)}, u32[]{:S(2)}) collective-permute-start(bf16[2,2,512,128]{3,2,1,0:T(8,128)(2,1)S(1)} %second_product.9.refs_0_), channel_id=1, source_target_pairs={{3,1},{4,6},{9,11},{14,12},{19,17},{20,22},{25,27},{30,28}} | collective-permute-start | bytes 1572872 | tf_op jit(solution)/shard_map/ppermute | solution.py:319
  297.0 14.3 %collective-permute-start.23 = (bf16[2,2,512,128]{3,2,1,0:T(8,128)(2,1)S(1)}, bf16[2,2,512,128]{3,2,1,0:T(8,128)(2,1)}, u32[]{:S(2)}, u32[]{:S(2)}) collective-permute-start(bf16[2,2,512,128]{3,2,1,0:T(8,128)(2,1)S(1)} %second_product.9.refs_0_), channel_id=1, source_target_pairs={{2,1},{5,6},{8,11},{15,12},{18,17},{21,22},{24,27},{31,28}} | collective-permute-start | bytes 1572872 | tf_op jit(solution)/shard_map/ppermute | solution.py:319
  298.3 13.1 %collective-permute-start.24 = (bf16[2,2,512,128]{3,2,1,0:T(8,128)(2,1)S(1)}, bf16[2,2,512,128]{3,2,1,0:T(8,128)(2,1)}, u32[]{:S(2)}, u32[]{:S(2)}) collective-permute-start(bf16[2,2,512,128]{3,2,1,0:T(8,128)(2,1)S(1)} %second_product.9.refs_0_), channel_id=1, source_target_pairs={{0,1},{7,6},{10,11},{13,12},{16,17},{23,22},{26,27},{29,28}} | collective-permute-start | bytes 1572872 | tf_op jit(solution)/shard_map/ppermute | solution.py:319
  299.7 1.0 copy-start.23
  300.7 1.0 copy-start.25
  301.8 1.0 copy-start.27

commit v18 on v14

--- a/solution.py
+++ b/solution.py
@@ -9,12 +9,13 @@
 F32 = jnp.float32
 BF16 = jnp.bfloat16
 VMEM_BYTES = 40 * 1024 * 1024
+ALL_VMEM_BYTES = 64 * 1024 * 1024
 LIGHT = pl.CostEstimate(flops=0, bytes_accessed=0, transcendentals=0)
 
 
-def params(steps):
+def params(steps, vmem_bytes=VMEM_BYTES):
     return pltpu.CompilerParams(
-        dimension_semantics=("arbitrary",) * steps, vmem_limit_bytes=VMEM_BYTES
+        dimension_semantics=("arbitrary",) * steps, vmem_limit_bytes=vmem_bytes
     )
 
 
@@ -97,7 +98,7 @@
     out_ref[0, 1] = (total[:rows, width:] + total[rows:, :width]).astype(BF16)
 
 
-def second_product(pick, own, sib, sites):
+def second_product(pick, own, sib, sites, vmem_bytes):
     mpo_count, phys, _, rows, cols = own.shape
     y_rows = sum(site.shape[2] for site in sites)
     q_spec = pl.BlockSpec((1, phys, 2, rows, cols), lambda v: (v, 0, 0, 0, 0))
@@ -108,7 +109,7 @@
         + [pl.BlockSpec(site.shape, lambda v: (0, 0, 0, 0)) for site in sites],
         out_specs=pl.BlockSpec((1, 2, rows, y_rows), lambda v: (v, 0, 0, 0)),
         out_shape=jax.ShapeDtypeStruct((mpo_count, 2, rows, y_rows), BF16),
-        compiler_params=params(1),
+        compiler_params=params(1, vmem_bytes),
         cost_estimate=LIGHT,
         name="second_product",
     )(pick, own, sib, *sites)
@@ -305,8 +306,8 @@
     ]
     pick = depth.astype(jnp.int32).reshape(1)
 
-    def second(sites, *earlier):
-        return second_product(after(pick, *earlier), q, q_sib, sites)
+    def second(sites, *earlier, vmem_bytes=VMEM_BYTES):
+        return second_product(after(pick, *earlier), q, q_sib, sites, vmem_bytes)
 
     def turn_to_goal(value, goal):
         return lax.ppermute(
@@ -338,7 +339,8 @@
         return jnp.where(step == 0, totals[0], jnp.where(step == 1, totals[1], totals[2]))
 
     def last_part(number, *earlier):
-        low = second([travelling[2][number]], *earlier)
+        vmem_bytes = VMEM_BYTES if number else ALL_VMEM_BYTES
+        low = second([travelling[2][number]], *earlier, vmem_bytes=vmem_bytes)
         ways = ((True, False), (True, True), (False, True))
         return [low] + [send(low, goals[3], *way) for way in ways]
 

time: 315 us -> 314 us (level)
    unnamed x62 -> x54, local copies, waits for them, and re-layouts: 17.6 us -> 15.7 us
  transfers between devices with their start and end apart: 26 -> 26, of which waited for: 17 -> 16; matrix products, arithmetic and copies ran while one was open for 6% -> 6% of each run, Pallas kernels for 17% -> 18%
where the time goes in v18:
time: 314 us
  waiting for transfers between devices  188 us (60%)
  Pallas kernels  58.5 us (19%)
  starting transfers between devices  27.8 us (9%)
  local copies, waits for them, and re-layouts  24.3 us (8%)
  other arithmetic  14.2 us (5%)
    ppermute x12, waiting for transfers between devices, ring(): lax.ppermute(value, 'row', [(r, (r + 1) % row_count) for r in range(row_c...  171 us
    pallas_call x5, Pallas kernels, second_product(): pl.pallas_call(second_kernel, grid=(mpo_count,), in_specs=[pl.BlockSpec(m...  28.4 us
    pallas_call x1, Pallas kernels, first_product(): pl.pallas_call(functools.partial(first_kernel, w_local), grid=(rows // ro...  23.4 us
    unnamed x54, local copies, waits for them, and re-layouts  15.7 us
    ppermute x6, waiting for transfers between devices, send(): lax.ppermute(value, axes, [(place(r, 1 - c if turned else c, 1 - d if cro...  9.96 us
    ppermute x3, starting transfers between devices, turn_to_goal(): lax.ppermute(value, axes, [(place(r, 1 - c, d), place(r, c, d)) for r, (c...  9.61 us
    ppermute x6, starting transfers between devices, send(): lax.ppermute(value, axes, [(place(r, 1 - c if turned else c, 1 - d if cro...  8.27 us
    ppermute x4, waiting for transfers between devices, swap(): return lax.ppermute(value, 'depth', [(0, 1), (1, 0)])  6.86 us
  transfers between devices with their start and end apart: 26, of which 16 were waited for; matrix products, arithmetic and copies ran while one was open for 6% of the time, Pallas kernels for 18%

profile of v18, /device:TPU:1, one launch (start us, length us, event | category | flops | bytes accessed | tf_op | source)
XLA Modules:
  0.0 313.6 jit_solution(5792868542099251297)
XLA Ops:
  0.0 2.7 constant_dynamic-slice_fusion
  2.8 2.7 collective-permute-start.3
  5.5 0.1 collective-permute-done.refs_1_
  5.6 3.9 %copy.9 = bf16[2,512,2,1024]{3,1,2,0:T(8,128)(2,1)S(1)} copy(bf16[2,512,2,1024]{3,2,1,0:T(2,128)(2,1)} %param.4) | data formatting | bytes 8388608 | tf_op jit(solution)/shard_map/optimization_barrier | solution.py:207
  9.5 0.2 dynamic-slice_bitcast_fusion
  9.7 2.4 collective-permute-start.1
  12.1 1.3 collective-permute-start.2
  13.4 17.7 %collective-permute-done.3.refs_2_ = bf16[1,2,512,512]{3,2,1,0:T(8,128)(2,1)S(1)} collective-permute-done((bf16[1,2,512,512]{3,2,1,0:T(8,128)(2,1)S(1)}, bf16[1,2,512,512]{3,2,1,0:T(8,128)(2,1)S(1)}, u32[]{:S(2)}, u32[]{:S(2)}) %collective-permute-start.3) | collective-permute-done | bytes 1048608 | tf_op jit(solution)/shard_map/ppermute | solution.py:270
  31.1 1.0 copy-done.8
  32.0 21.6 %collective-permute-done.2.refs_3_ = bf16[1,2,512,512]{3,2,1,0:T(8,128)(2,1)} collective-permute-done((bf16[1,2,512,512]{3,2,1,0:T(8,128)(2,1)S(1)}, bf16[1,2,512,512]{3,2,1,0:T(8,128)(2,1)}, u32[]{:S(2)}, u32[]{:S(2)}) %collective-permute-start.2) | collective-permute-done | bytes 1048608 | tf_op jit(solution)/shard_map/ppermute | solution.py:270
  53.6 22.4 %collective-permute-done.4.refs_4_ = bf16[1,2,512,512]{3,2,1,0:T(8,128)(2,1)S(1)} collective-permute-done((bf16[1,2,512,512]{3,2,1,0:T(8,128)(2,1)S(1)}, bf16[1,2,512,512]{3,2,1,0:T(8,128)(2,1)S(1)}, u32[]{:S(2)}, u32[]{:S(2)}) %collective-permute-start.4) | collective-permute-done | bytes 1048608 | tf_op jit(solution)/shard_map/ppermute | solution.py:270
  76.0 1.0 copy-done.10
  77.0 0.6 collective-permute-start.5
  77.6 1.8 fusion
  79.4 0.8 collective-permute-start.7
  80.2 24.2 %collective-permute-done.6.refs_5_ = bf16[1,2,512,512]{3,2,1,0:T(8,128)(2,1)} collective-permute-done((bf16[1,2,512,512]{3,2,1,0:T(8,128)(2,1)}, bf16[1,2,512,512]{3,2,1,0:T(8,128)(2,1)}, u32[]{:S(2)}, u32[]{:S(2)}) %collective-permute-start.6) | collective-permute-done | bytes 1048608 | tf_op jit(solution)/shard_map/ppermute | solution.py:270
  104.4 5.3 %maximum_select_fusion.1 = bf16[1,2,2,512,1024]{4,3,2,1,0:T(8,128)(2,1)S(1)} fusion(bf16[1,2,2,256,1024]{4,3,2,1,0:T(8,128)(2,1)} %bitcast.10, bf16[1,2,2,256,1024]{4,3,2,1,0:T(8,128)(2,1)} %bitcast.9, pred[]{:T(512)S(6)} %eq.23), kind=kLoop, calls=%fused_computation.1 | loop fusion | flops 18874368 | bytes 8388609 | tf_op jit(solution)/shard_map/jit(_where)/select_n | solution.py:274
  109.8 4.0 %maximum_select_fusion.site_ref = bf16[2,2,2,512,1024]{4,3,2,1,0:T(8,128)(2,1)} fusion(bf16[1,2,2,512,1024]{4,3,2,1,0:T(8,128)(2,1)S(1)} %maximum_select_fusion.1, bf16[1,2,2,512,1024]{4,3,2,1,0:T(8,128)(2,1)S(1)} %bitcast.15, pred[]{:T(512)S(6)} %eq.22), kind=kLoop, calls=%fused_computation | loop fusion | flops 12582912 | bytes 16777216 | tf_op jit(solution)/shard_map/jit(_where)/select_n | solution.py:291
  113.8 13.0 %collective-permute-done.7.refs_6_ = bf16[1,2,512,512]{3,2,1,0:T(8,128)(2,1)S(1)} collective-permute-done((bf16[1,2,512,512]{3,2,1,0:T(8,128)(2,1)}, bf16[1,2,512,512]{3,2,1,0:T(8,128)(2,1)S(1)}, u32[]{:S(2)}, u32[]{:S(2)}) %collective-permute-start.7) | collective-permute-done | bytes 1048608 | tf_op jit(solution)/shard_map/ppermute | solution.py:270
  126.8 1.0 copy-done.12
  127.8 21.5 %collective-permute-done.8.refs_7_ = bf16[1,2,512,512]{3,2,1,0:T(8,128)(2,1)S(1)} collective-permute-done((bf16[1,2,512,512]{3,2,1,0:T(8,128)(2,1)}, bf16[1,2,512,512]{3,2,1,0:T(8,128)(2,1)S(1)}, u32[]{:S(2)}, u32[]{:S(2)}) %collective-permute-start.8) | collective-permute-done | bytes 1048608 | tf_op jit(solution)/shard_map/ppermute | solution.py:270
  149.3 1.0 copy-done.14
  150.2 0.1 pad_add_fusion.1.block_ref
  150.3 1.2 copy-done.7
  151.6 1.2 copy-done.9
  152.8 1.2 copy-done.11
  154.0 1.2 copy-done.13
  155.2 1.2 copy-done.15
  156.5 23.4 %first_product.1.own_ref = bf16[2,2,2,512,512]{4,3,2,1,0:T(8,128)(2,1)S(1)} custom-call(s32[4]{0:T(128)S(1)} %pad_add_fusion.1.block_ref, f32[2,2,2,2]{3,2,1,0:T(2,128)S(1)} %pad_maximum_fusion.mpo_ref, bf16[2,2,2,512,1024]{4,3,2,1,0:T(8,128)(2,1)} %maximum_select_fusion.site_ref, bf16[1,2,512,512]{3,2,1,0:T(8,128)(2,1)S(1)} %get-tuple-element.31.refs_0_, ...), custom_call_target="tpu_custom_call" | custom-call | tf_op jit(solution)/shard_map/first_product/pallas_call | solution.py:68
  179.9 14.4 %collective-permute-done.10.refs_1_ = bf16[2,2,128,1024]{3,2,1,0:T(8,128)(2,1)} collective-permute-done((bf16[2,2,128,1024]{3,2,1,0:T(8,128)(2,1)S(1)}, bf16[2,2,128,1024]{3,2,1,0:T(8,128)(2,1)}, u32[]{:S(2)}, u32[]{:S(2)}) %collective-permute-start.10) | collective-permute-done | bytes 1048608 | tf_op jit(solution)/shard_map/ppermute | solution.py:270
  194.3 0.8 collective-permute-start.11
  195.2 6.8 %collective-permute-done.11.sib_ref = bf16[2,2,2,512,512]{4,3,2,1,0:T(8,128)(2,1)S(1)} collective-permute-done((bf16[2,2,2,512,512]{4,3,2,1,0:T(8,128)(2,1)S(1)}, bf16[2,2,2,512,512]{4,3,2,1,0:T(8,128)(2,1)S(1)}, u32[]{:S(2)}, u32[]{:S(2)}) %collective-permute-start.11) | collective-permute-done | bytes 4194336 | tf_op jit(solution)/shard_map/ppermute | solution.py:211
  202.0 4.8 %second_product.5 = bf16[2,2,512,256]{3,2,1,0:T(8,128)(2,1)S(1)} custom-call(s32[1]{0:T(128)} %bitcast.1.pick_ref, bf16[2,2,2,512,512]{4,3,2,1,0:T(8,128)(2,1)S(1)} %first_product.1.own_ref, bf16[2,2,2,512,512]{4,3,2,1,0:T(8,128)(2,1)S(1)} %collective-permute-done.11.sib_ref, bf16[2,2,128,1024]{3,2,1,0:T(8,128)(2,1)S(1)} %get-tuple-element.17.refs_0_, ...), custom_call_target="tpu_custom_call" | custom-call | tf_op jit(solution)/shard_map/second_product/pallas_call | solution.py:105
  206.7 1.3 collective-permute-start.13
  208.1 13.9 %collective-permute-done.12.refs_0_ = bf16[2,2,128,1024]{3,2,1,0:T(8,128)(2,1)S(1)} collective-permute-done((bf16[2,2,128,1024]{3,2,1,0:T(8,128)(2,1)}, bf16[2,2,128,1024]{3,2,1,0:T(8,128)(2,1)S(1)}, u32[]{:S(2)}, u32[]{:S(2)}) %collective-permute-start.12) | collective-permute-done | bytes 1048608 | tf_op jit(solution)/shard_map/ppermute | solution.py:270
  222.0 7.1 %second_product.6 = bf16[2,2,512,256]{3,2,1,0:T(8,128)(2,1)} custom-call(s32[1]{0:T(128)} %bitcast.1.pick_ref, bf16[2,2,2,512,512]{4,3,2,1,0:T(8,128)(2,1)S(1)} %first_product.1.own_ref, bf16[2,2,2,512,512]{4,3,2,1,0:T(8,128)(2,1)S(1)} %collective-permute-done.11.sib_ref, bf16[2,2,128,1024]{3,2,1,0:T(8,128)(2,1)} %collective-permute-done.9.refs_0_, ...), custom_call_target="tpu_custom_call" | custom-call | tf_op jit(solution)/shard_map/second_product/pallas_call | solution.py:105
  229.1 4.2 %collective-permute-start.19 = (bf16[2,2,512,256]{3,2,1,0:T(8,128)(2,1)}, bf16[2,2,512,256]{3,2,1,0:T(8,128)(2,1)}, u32[]{:S(2)}, u32[]{:S(2)}) collective-permute-start(bf16[2,2,512,256]{3,2,1,0:T(8,128)(2,1)} %second_product.6), channel_id=1, source_target_pairs={{0,2},{1,3},{6,4},{7,5},{10,8},{11,9},{12,14},{13,15},{16,18},{17,... | collective-permute-start | bytes 3145736 | tf_op jit(solution)/shard_map/ppermute | solution.py:313
  233.2 11.3 %collective-permute-done.14.refs_1_ = bf16[2,2,128,1024]{3,2,1,0:T(8,128)(2,1)} collective-permute-done((bf16[2,2,128,1024]{3,2,1,0:T(8,128)(2,1)}, bf16[2,2,128,1024]{3,2,1,0:T(8,128)(2,1)}, u32[]{:S(2)}, u32[]{:S(2)}) %collective-permute-start.14) | collective-permute-done | bytes 1048608 | tf_op jit(solution)/shard_map/ppermute | solution.py:270
  244.5 6.8 %second_product.7 = bf16[2,2,512,256]{3,2,1,0:T(8,128)(2,1)} custom-call(s32[1]{0:T(128)} %bitcast.1.pick_ref, bf16[2,2,2,512,512]{4,3,2,1,0:T(8,128)(2,1)S(1)} %first_product.1.own_ref, bf16[2,2,2,512,512]{4,3,2,1,0:T(8,128)(2,1)S(1)} %collective-permute-done.11.sib_ref, bf16[2,2,128,1024]{3,2,1,0:T(8,128)(2,1)S(1)} %collective-permute-done.12.refs_0_, ...), custom_call_target="tpu_custom_call" | custom-call | tf_op jit(solution)/shard_map/second_product/pallas_call | solution.py:105
  251.3 4.2 %collective-permute-start.20 = (bf16[2,2,512,256]{3,2,1,0:T(8,128)(2,1)}, bf16[2,2,512,256]{3,2,1,0:T(8,128)(2,1)}, u32[]{:S(2)}, u32[]{:S(2)}) collective-permute-start(bf16[2,2,512,256]{3,2,1,0:T(8,128)(2,1)} %second_product.7), channel_id=1, source_target_pairs={{0,2},{1,3},{4,6},{5,7},{10,8},{11,9},{14,12},{15,13},{16,18},{17,... | collective-permute-start | bytes 3145736 | tf_op jit(solution)/shard_map/ppermute | solution.py:313
  255.5 11.5 %collective-permute-done.15.refs_0_ = bf16[2,2,128,1024]{3,2,1,0:T(8,128)(2,1)} collective-permute-done((bf16[2,2,128,1024]{3,2,1,0:T(8,128)(2,1)S(1)}, bf16[2,2,128,1024]{3,2,1,0:T(8,128)(2,1)}, u32[]{:S(2)}, u32[]{:S(2)}) %collective-permute-start.15) | collective-permute-done | bytes 1048608 | tf_op jit(solution)/shard_map/ppermute | solution.py:270
  267.0 5.8 %second_product.8.refs_0_ = bf16[2,2,512,128]{3,2,1,0:T(8,128)(2,1)} custom-call(s32[1]{0:T(128)} %bitcast.1.pick_ref, bf16[2,2,2,512,512]{4,3,2,1,0:T(8,128)(2,1)} %copy-done, bf16[2,2,2,512,512]{4,3,2,1,0:T(8,128)(2,1)} %copy-done.2, bf16[2,2,128,1024]{3,2,1,0:T(8,128)(2,1)} %collective-permute-done.15.refs_0_), custom_call_target="tpu_custom_call" | custom-call | tf_op jit(solution)/shard_map/second_product/pallas_call | solution.py:105
  272.8 1.5 collective-permute-start.16
  274.4 1.6 collective-permute-start.17
  276.0 1.3 collective-permute-start.18
  277.3 4.7 %select_convert_fusion = (bf16[2,2,512,256]{3,2,1,0:T(8,128)(2,1)}, f32[2,2,512,256]{3,2,1,0:T(8,128)S(1)}) fusion(bf16[2,2,512,256]{3,2,1,0:T(8,128)(2,1)} %copy-done.25, bf16[2,2,512,256]{3,2,1,0:T(8,128)(2,1)} %copy-done.4, bf16[2,2,512,256]{3,2,1,0:T(8,128)(2,1)} %collective-permute-done.19, bf16[2,2,512,256]{3,2,1,0:T(8,128)(2,1)} %second_product.6, ...), kind=kLoop, calls=%fused_computation.2 | loop fusion | flops 7340032 | bytes 9437188 | tf_op jit(solution)/shard_map/convert_element_type | solution.py:348
  282.0 1.2 collective-permute-start.25
  283.2 4.1 %collective-permute-done.16.refs_1_ = bf16[2,2,512,128]{3,2,1,0:T(8,128)(2,1)S(1)} collective-permute-done((bf16[2,2,512,128]{3,2,1,0:T(8,128)(2,1)}, bf16[2,2,512,128]{3,2,1,0:T(8,128)(2,1)S(1)}, u32[]{:S(2)}, u32[]{:S(2)}) %collective-permute-start.16) | collective-permute-done | bytes 524320 | tf_op jit(solution)/shard_map/ppermute | solution.py:320
  287.3 0.8 copy-done.16
  288.1 1.2 collective-permute-done.17.refs_2_
  289.4 0.9 copy-done.18
  290.2 0.8 copy-done.20
  291.1 3.9 %second_product.9.refs_0_ = bf16[2,2,512,128]{3,2,1,0:T(8,128)(2,1)S(1)} custom-call(s32[1]{0:T(128)} %bitcast.1.pick_ref, bf16[2,2,2,512,512]{4,3,2,1,0:T(8,128)(2,1)S(1)} %copy-done.1, bf16[2,2,2,512,512]{4,3,2,1,0:T(8,128)(2,1)S(1)} %copy-done.3, bf16[2,2,128,1024]{3,2,1,0:T(8,128)(2,1)} %collective-permute-done.21.refs_0_), custom_call_target="tpu_custom_call" | custom-call | tf_op jit(solution)/shard_map/second_product/pallas_call | solution.py:105
  295.0 1.3 collective-permute-start.22
  296.3 1.3 collective-permute-start.23
  297.6 1.3 collective-permute-start.24
  298.9 0.1 pad_add_fusion.pick_ref
  299.0 1.0 copy-done.17
  300.0 1.0 copy-done.19
  301.1 1.0 copy-done.21
  302.1 4.0 %finish.1.refs_4_ = f32[2,2,512,512]{3,2,1,0:T(8,128)} custom-call(s32[2]{0:T(128)S(1)} %pad_add_fusion.pick_ref, f32[2,2,512,256]{3,2,1,0:T(8,128)S(1)} %get-tuple-element.26.mine_ref, bf16[2,2,512,256]{3,2,1,0:T(8,128)(2,1)} %collective-permute-done.25.siblings_ref, bf16[2,2,512,128]{3,2,1,0:T(8,128)(2,1)S(1)} %copy-done.5, ...), custom_call_target="tpu_custom_call" | custom-call | tf_op jit(solution)/shard_map/finish/pallas_call | solution.py:146
  306.1 2.6 collective-permute-done.22.refs_1_
  308.7 1.9 collective-permute-done.23.refs_2_
  310.6 2.8 finish_last.1
  (61 shorter events, 0.3 us)
Async XLA Ops:
  2.7 2.9 collective-permute-start
  2.8 28.3 %collective-permute-start.3 = (bf16[1,2,512,512]{3,2,1,0:T(8,128)(2,1)S(1)}, bf16[1,2,512,512]{3,2,1,0:T(8,128)(2,1)S(1)}, u32[]{:S(2)}, u32[]{:S(2)}) collective-permute-start(bf16[1,2,512,512]{3,2,1,0:T(8,128)(2,1)S(1)} %get-tuple-element.31.refs_0_), channel_id=1, source_target_pairs={{0,4},{4,8},{8,12},{12,0},{1,5},{5,9},{9,13},{13,1},{2,6},{6,10},{... | collective-permute-start | bytes 3145736 | tf_op jit(solution)/shard_map/ppermute | solution.py:270
  5.6 6.5 %copy-start.6 = (bf16[1,2,512,512]{3,2,1,0:T(8,128)(2,1)}, bf16[1,2,512,512]{3,2,1,0:T(8,128)(2,1)S(1)}, u32[]{:S(2)}) copy-start(bf16[1,2,512,512]{3,2,1,0:T(8,128)(2,1)S(1)} %collective-permute-done.refs_1_) | copy-start | bytes 3145732
  9.5 67.5 %copy-start.22 = (bf16[2,512,2,1024]{3,1,2,0:T(8,128)(2,1)}, bf16[2,512,2,1024]{3,1,2,0:T(8,128)(2,1)S(1)}, u32[]{:S(2)}) copy-start(bf16[2,512,2,1024]{3,1,2,0:T(8,128)(2,1)S(1)} %copy.9) | copy-start | bytes 12582916
  9.7 67.9 %copy-start.24 = (bf16[2,2,256,1024]{3,2,1,0:T(8,128)(2,1)}, bf16[2,2,256,1024]{3,2,1,0:T(8,128)(2,1)S(1)}, u32[]{:S(2)}) copy-start(bf16[2,2,256,1024]{3,2,1,0:T(8,128)(2,1)S(1)} %dynamic-slice_bitcast_fusion) | copy-start | bytes 6291460
  9.7 67.3 %collective-permute-start.1 = (bf16[2,2,256,1024]{3,2,1,0:T(8,128)(2,1)S(1)}, bf16[2,2,256,1024]{3,2,1,0:T(8,128)(2,1)}, u32[]{:S(2)}, u32[]{:S(2)}) collective-permute-start(bf16[2,2,256,1024]{3,2,1,0:T(8,128)(2,1)S(1)} %dynamic-slice_bitcast_fusion), channel_id=1, source_target_pairs={{0,2},{2,0},{1,3},{3,1},{4,6},{6,4},{5,7},{7,5},{8,10},{10,8},{9,1... | collective-permute-start | bytes 6291464 | tf_op jit(solution)/shard_map/ppermute | solution.py:273
  12.1 41.5 %collective-permute-start.2 = (bf16[1,2,512,512]{3,2,1,0:T(8,128)(2,1)S(1)}, bf16[1,2,512,512]{3,2,1,0:T(8,128)(2,1)}, u32[]{:S(2)}, u32[]{:S(2)}) collective-permute-start(bf16[1,2,512,512]{3,2,1,0:T(8,128)(2,1)S(1)} %collective-permute-done.refs_1_), channel_id=1, source_target_pairs={{0,4},{4,8},{8,12},{12,0},{1,5},{5,9},{9,13},{13,1},{2,6},{6,10},{... | collective-permute-start | bytes 3145736 | tf_op jit(solution)/shard_map/ppermute | solution.py:270
  31.1 44.9 %collective-permute-start.4 = (bf16[1,2,512,512]{3,2,1,0:T(8,128)(2,1)S(1)}, bf16[1,2,512,512]{3,2,1,0:T(8,128)(2,1)S(1)}, u32[]{:S(2)}, u32[]{:S(2)}) collective-permute-start(bf16[1,2,512,512]{3,2,1,0:T(8,128)(2,1)S(1)} %collective-permute-done.3.refs_2_), channel_id=1, source_target_pairs={{0,4},{4,8},{8,12},{12,0},{1,5},{5,9},{9,13},{13,1},{2,6},{6,10},{... | collective-permute-start | bytes 3145736 | tf_op jit(solution)/shard_map/ppermute | solution.py:270
  31.1 1.0 copy-start.8
  76.0 1.0 copy-start.10
  77.0 27.4 %collective-permute-start.5 = (bf16[2,2,256,1024]{3,2,1,0:T(8,128)(2,1)}, bf16[2,2,256,1024]{3,2,1,0:T(8,128)(2,1)}, u32[]{:S(2)}, u32[]{:S(2)}) collective-permute-start(bf16[2,2,256,1024]{3,2,1,0:T(8,128)(2,1)} %collective-permute-done.1), channel_id=1, source_target_pairs={{0,1},{1,0},{2,3},{3,2},{4,5},{5,4},{6,7},{7,6},{8,9},{9,8},{10,11... | collective-permute-start | bytes 6291464 | tf_op jit(solution)/shard_map/ppermute | solution.py:211
  77.6 26.8 %collective-permute-start.6 = (bf16[1,2,512,512]{3,2,1,0:T(8,128)(2,1)}, bf16[1,2,512,512]{3,2,1,0:T(8,128)(2,1)}, u32[]{:S(2)}, u32[]{:S(2)}) collective-permute-start(bf16[1,2,512,512]{3,2,1,0:T(8,128)(2,1)} %collective-permute-done.2.refs_3_), channel_id=1, source_target_pairs={{0,4},{4,8},{8,12},{12,0},{1,5},{5,9},{9,13},{13,1},{2,6},{6,10},{... | collective-permute-start | bytes 3145736 | tf_op jit(solution)/shard_map/ppermute | solution.py:270
  79.4 47.4 %collective-permute-start.7 = (bf16[1,2,512,512]{3,2,1,0:T(8,128)(2,1)}, bf16[1,2,512,512]{3,2,1,0:T(8,128)(2,1)S(1)}, u32[]{:S(2)}, u32[]{:S(2)}) collective-permute-start(bf16[1,2,512,512]{3,2,1,0:T(8,128)(2,1)} %copy-done.10), channel_id=1, source_target_pairs={{0,4},{4,8},{8,12},{12,0},{1,5},{5,9},{9,13},{13,1},{2,6},{6,10},{... | collective-permute-start | bytes 3145736 | tf_op jit(solution)/shard_map/ppermute | solution.py:270
  104.4 44.8 %collective-permute-start.8 = (bf16[1,2,512,512]{3,2,1,0:T(8,128)(2,1)}, bf16[1,2,512,512]{3,2,1,0:T(8,128)(2,1)S(1)}, u32[]{:S(2)}, u32[]{:S(2)}) collective-permute-start(bf16[1,2,512,512]{3,2,1,0:T(8,128)(2,1)} %collective-permute-done.6.refs_5_), channel_id=1, source_target_pairs={{0,4},{4,8},{8,12},{12,0},{1,5},{5,9},{9,13},{13,1},{2,6},{6,10},{... | collective-permute-start | bytes 3145736 | tf_op jit(solution)/shard_map/ppermute | solution.py:270
  104.4 5.3 %copy-start.23 = (bf16[2,512,2,1024]{3,1,2,0:T(8,128)(2,1)S(1)}, bf16[2,512,2,1024]{3,1,2,0:T(8,128)(2,1)}, u32[]{:S(2)}) copy-start(bf16[2,512,2,1024]{3,1,2,0:T(8,128)(2,1)} %copy-done.22) | copy-start | bytes 12582916
  109.8 40.6 %copy-start.26 = (f32[2,2,2,2]{3,2,1,0:T(2,128)S(1)}, f32[2,2,2,2]{3,2,1,0:T(2,128)}, u32[]{:S(2)}) copy-start(f32[2,2,2,2]{3,2,1,0:T(2,128)} %param.5) | copy-start | bytes 196
  126.8 1.0 copy-start.12
  127.8 52.1 %collective-permute-start.9 = (bf16[2,2,128,1024]{3,2,1,0:T(8,128)(2,1)S(1)}, bf16[2,2,128,1024]{3,2,1,0:T(8,128)(2,1)}, u32[]{:S(2)}, u32[]{:S(2)}) collective-permute-start(bf16[2,2,128,1024]{3,2,1,0:T(8,128)(2,1)S(1)} %get-tuple-element.17.refs_0_), channel_id=1, source_target_pairs={{0,4},{4,8},{8,12},{12,0},{1,5},{5,9},{9,13},{13,1},{2,6},{6,10},{... | collective-permute-start | bytes 3145736 | tf_op jit(solution)/shard_map/ppermute | solution.py:270
  149.3 1.0 copy-start.14
  150.2 44.1 %collective-permute-start.10 = (bf16[2,2,128,1024]{3,2,1,0:T(8,128)(2,1)S(1)}, bf16[2,2,128,1024]{3,2,1,0:T(8,128)(2,1)}, u32[]{:S(2)}, u32[]{:S(2)}) collective-permute-start(bf16[2,2,128,1024]{3,2,1,0:T(8,128)(2,1)S(1)} %get-tuple-element.18.refs_1_), channel_id=1, source_target_pairs={{0,4},{4,8},{8,12},{12,0},{1,5},{5,9},{9,13},{13,1},{2,6},{6,10},{... | collective-permute-start | bytes 3145736 | tf_op jit(solution)/shard_map/ppermute | solution.py:270
  150.3 1.2 copy-start.7
  151.6 1.2 copy-start.9
  152.8 1.2 copy-start.11
  154.0 1.2 copy-start.13
  155.2 1.2 copy-start.15
  179.9 64.7 %copy-start = (bf16[2,2,2,512,512]{4,3,2,1,0:T(8,128)(2,1)}, bf16[2,2,2,512,512]{4,3,2,1,0:T(8,128)(2,1)S(1)}, u32[]{:S(2)}) copy-start(bf16[2,2,2,512,512]{4,3,2,1,0:T(8,128)(2,1)S(1)} %first_product.1.own_ref) | copy-start | bytes 12582916
  194.3 7.6 %collective-permute-start.11 = (bf16[2,2,2,512,512]{4,3,2,1,0:T(8,128)(2,1)S(1)}, bf16[2,2,2,512,512]{4,3,2,1,0:T(8,128)(2,1)S(1)}, u32[]{:S(2)}, u32[]{:S(2)}) collective-permute-start(bf16[2,2,2,512,512]{4,3,2,1,0:T(8,128)(2,1)S(1)} %first_product.1.own_ref), channel_id=1, source_target_pairs={{0,1},{1,0},{2,3},{3,2},{4,5},{5,4},{6,7},{7,6},{8,9},{9,8},{10,11... | collective-permute-start | bytes 12582920 | tf_op jit(solution)/shard_map/ppermute | solution.py:211
  195.2 26.8 %collective-permute-start.12 = (bf16[2,2,128,1024]{3,2,1,0:T(8,128)(2,1)}, bf16[2,2,128,1024]{3,2,1,0:T(8,128)(2,1)S(1)}, u32[]{:S(2)}, u32[]{:S(2)}) collective-permute-start(bf16[2,2,128,1024]{3,2,1,0:T(8,128)(2,1)} %collective-permute-done.9.refs_0_), channel_id=1, source_target_pairs={{0,4},{4,8},{8,12},{12,0},{1,5},{5,9},{9,13},{13,1},{2,6},{6,10},{... | collective-permute-start | bytes 3145736 | tf_op jit(solution)/shard_map/ppermute | solution.py:270
  202.0 42.6 %copy-start.2 = (bf16[2,2,2,512,512]{4,3,2,1,0:T(8,128)(2,1)}, bf16[2,2,2,512,512]{4,3,2,1,0:T(8,128)(2,1)S(1)}, u32[]{:S(2)}) copy-start(bf16[2,2,2,512,512]{4,3,2,1,0:T(8,128)(2,1)S(1)} %collective-permute-done.11.sib_ref) | copy-start | bytes 12582916
  206.7 22.3 %copy-start.4 = (bf16[2,2,512,256]{3,2,1,0:T(8,128)(2,1)}, bf16[2,2,512,256]{3,2,1,0:T(8,128)(2,1)S(1)}, u32[]{:S(2)}) copy-start(bf16[2,2,512,256]{3,2,1,0:T(8,128)(2,1)S(1)} %second_product.5) | copy-start | bytes 3145732
  206.7 26.5 %collective-permute-start.13 = (bf16[2,2,512,256]{3,2,1,0:T(8,128)(2,1)S(1)}, bf16[2,2,512,256]{3,2,1,0:T(8,128)(2,1)S(1)}, u32[]{:S(2)}, u32[]{:S(2)}) collective-permute-start(bf16[2,2,512,256]{3,2,1,0:T(8,128)(2,1)S(1)} %second_product.5), channel_id=1, source_target_pairs={{2,0},{3,1},{6,4},{7,5},{8,10},{9,11},{12,14},{13,15},{18,16},{19,... | collective-permute-start | bytes 3145736 | tf_op jit(solution)/shard_map/ppermute | solution.py:313
  208.0 36.5 %collective-permute-start.14 = (bf16[2,2,128,1024]{3,2,1,0:T(8,128)(2,1)}, bf16[2,2,128,1024]{3,2,1,0:T(8,128)(2,1)}, u32[]{:S(2)}, u32[]{:S(2)}) collective-permute-start(bf16[2,2,128,1024]{3,2,1,0:T(8,128)(2,1)} %collective-permute-done.10.refs_1_), channel_id=1, source_target_pairs={{0,4},{4,8},{8,12},{12,0},{1,5},{5,9},{9,13},{13,1},{2,6},{6,10},{... | collective-permute-start | bytes 3145736 | tf_op jit(solution)/shard_map/ppermute | solution.py:270
  222.0 45.0 %collective-permute-start.15 = (bf16[2,2,128,1024]{3,2,1,0:T(8,128)(2,1)S(1)}, bf16[2,2,128,1024]{3,2,1,0:T(8,128)(2,1)}, u32[]{:S(2)}, u32[]{:S(2)}) collective-permute-start(bf16[2,2,128,1024]{3,2,1,0:T(8,128)(2,1)S(1)} %collective-permute-done.12.refs_0_), channel_id=1, source_target_pairs={{0,4},{4,8},{8,12},{12,0},{1,5},{5,9},{9,13},{13,1},{2,6},{6,10},{... | collective-permute-start | bytes 3145736 | tf_op jit(solution)/shard_map/ppermute | solution.py:270
  229.1 46.9 %collective-permute-start.19 = (bf16[2,2,512,256]{3,2,1,0:T(8,128)(2,1)}, bf16[2,2,512,256]{3,2,1,0:T(8,128)(2,1)}, u32[]{:S(2)}, u32[]{:S(2)}) collective-permute-start(bf16[2,2,512,256]{3,2,1,0:T(8,128)(2,1)} %second_product.6), channel_id=1, source_target_pairs={{0,2},{1,3},{6,4},{7,5},{10,8},{11,9},{12,14},{13,15},{16,18},{17,... | collective-permute-start | bytes 3145736 | tf_op jit(solution)/shard_map/ppermute | solution.py:313
  233.2 18.1 %copy-start.25 = (bf16[2,2,512,256]{3,2,1,0:T(8,128)(2,1)}, bf16[2,2,512,256]{3,2,1,0:T(8,128)(2,1)S(1)}, u32[]{:S(2)}) copy-start(bf16[2,2,512,256]{3,2,1,0:T(8,128)(2,1)S(1)} %collective-permute-done.13) | copy-start | bytes 3145732
  251.3 25.9 %collective-permute-start.20 = (bf16[2,2,512,256]{3,2,1,0:T(8,128)(2,1)}, bf16[2,2,512,256]{3,2,1,0:T(8,128)(2,1)}, u32[]{:S(2)}, u32[]{:S(2)}) collective-permute-start(bf16[2,2,512,256]{3,2,1,0:T(8,128)(2,1)} %second_product.7), channel_id=1, source_target_pairs={{0,2},{1,3},{4,6},{5,7},{10,8},{11,9},{14,12},{15,13},{16,18},{17,... | collective-permute-start | bytes 3145736 | tf_op jit(solution)/shard_map/ppermute | solution.py:313
  255.5 35.6 %collective-permute-start.21 = (bf16[2,2,128,1024]{3,2,1,0:T(8,128)(2,1)}, bf16[2,2,128,1024]{3,2,1,0:T(8,128)(2,1)}, u32[]{:S(2)}, u32[]{:S(2)}) collective-permute-start(bf16[2,2,128,1024]{3,2,1,0:T(8,128)(2,1)} %collective-permute-done.14.refs_1_), channel_id=1, source_target_pairs={{0,4},{4,8},{8,12},{12,0},{1,5},{5,9},{9,13},{13,1},{2,6},{6,10},{... | collective-permute-start | bytes 3145736 | tf_op jit(solution)/shard_map/ppermute | solution.py:270
  272.8 18.2 %copy-start.1 = (bf16[2,2,2,512,512]{4,3,2,1,0:T(8,128)(2,1)S(1)}, bf16[2,2,2,512,512]{4,3,2,1,0:T(8,128)(2,1)}, u32[]{:S(2)}) copy-start(bf16[2,2,2,512,512]{4,3,2,1,0:T(8,128)(2,1)} %copy-done) | copy-start | bytes 12582916
  272.8 18.2 %copy-start.3 = (bf16[2,2,2,512,512]{4,3,2,1,0:T(8,128)(2,1)S(1)}, bf16[2,2,2,512,512]{4,3,2,1,0:T(8,128)(2,1)}, u32[]{:S(2)}) copy-start(bf16[2,2,2,512,512]{4,3,2,1,0:T(8,128)(2,1)} %copy-done.2) | copy-start | bytes 12582916
  272.8 14.5 %collective-permute-start.16 = (bf16[2,2,512,128]{3,2,1,0:T(8,128)(2,1)}, bf16[2,2,512,128]{3,2,1,0:T(8,128)(2,1)S(1)}, u32[]{:S(2)}, u32[]{:S(2)}) collective-permute-start(bf16[2,2,512,128]{3,2,1,0:T(8,128)(2,1)} %second_product.8.refs_0_), channel_id=1, source_target_pairs={{3,1},{4,6},{9,11},{14,12},{19,17},{20,22},{25,27},{30,28}} | collective-permute-start | bytes 1572872 | tf_op jit(solution)/shard_map/ppermute | solution.py:320
  274.4 15.0 %collective-permute-start.17 = (bf16[2,2,512,128]{3,2,1,0:T(8,128)(2,1)}, bf16[2,2,512,128]{3,2,1,0:T(8,128)(2,1)S(1)}, u32[]{:S(2)}, u32[]{:S(2)}) collective-permute-start(bf16[2,2,512,128]{3,2,1,0:T(8,128)(2,1)} %second_product.8.refs_0_), channel_id=1, source_target_pairs={{2,1},{5,6},{8,11},{15,12},{18,17},{21,22},{24,27},{31,28}} | collective-permute-start | bytes 1572872 | tf_op jit(solution)/shard_map/ppermute | solution.py:320
  276.0 14.3 %collective-permute-start.18 = (bf16[2,2,512,128]{3,2,1,0:T(8,128)(2,1)}, bf16[2,2,512,128]{3,2,1,0:T(8,128)(2,1)S(1)}, u32[]{:S(2)}, u32[]{:S(2)}) collective-permute-start(bf16[2,2,512,128]{3,2,1,0:T(8,128)(2,1)} %second_product.8.refs_0_), channel_id=1, source_target_pairs={{0,1},{7,6},{10,11},{13,12},{16,17},{23,22},{26,27},{29,28}} | collective-permute-start | bytes 1572872 | tf_op jit(solution)/shard_map/ppermute | solution.py:320
  282.0 17.0 %collective-permute-start.25 = (bf16[2,2,512,256]{3,2,1,0:T(8,128)(2,1)}, bf16[2,2,512,256]{3,2,1,0:T(8,128)(2,1)}, u32[]{:S(2)}, u32[]{:S(2)}) collective-permute-start(bf16[2,2,512,256]{3,2,1,0:T(8,128)(2,1)} %get-tuple-element.25), channel_id=1, source_target_pairs={{0,1},{1,0},{2,3},{3,2},{4,5},{5,4},{6,7},{7,6},{8,9},{9,8},{10,11... | collective-permute-start | bytes 3145736 | tf_op jit(solution)/shard_map/ppermute | solution.py:211
  287.3 0.8 copy-start.16
  289.4 0.9 copy-start.18
  290.2 0.8 copy-start.20
  291.1 7.9 %copy-start.5 = (bf16[2,2,512,128]{3,2,1,0:T(8,128)(2,1)S(1)}, bf16[2,2,512,128]{3,2,1,0:T(8,128)(2,1)}, u32[]{:S(2)}) copy-start(bf16[2,2,512,128]{3,2,1,0:T(8,128)(2,1)} %second_product.8.refs_0_) | copy-start | bytes 1572868
  295.0 13.7 %collective-permute-start.22 = (bf16[2,2,512,128]{3,2,1,0:T(8,128)(2,1)S(1)}, bf16[2,2,512,128]{3,2,1,0:T(8,128)(2,1)}, u32[]{:S(2)}, u32[]{:S(2)}) collective-permute-start(bf16[2,2,512,128]{3,2,1,0:T(8,128)(2,1)S(1)} %second_product.9.refs_0_), channel_id=1, source_target_pairs={{3,1},{4,6},{9,11},{14,12},{19,17},{20,22},{25,27},{30,28}} | collective-permute-start | bytes 1572872 | tf_op jit(solution)/shard_map/ppermute | solution.py:320
  296.3 14.3 %collective-permute-start.23 = (bf16[2,2,512,128]{3,2,1,0:T(8,128)(2,1)S(1)}, bf16[2,2,512,128]{3,2,1,0:T(8,128)(2,1)}, u32[]{:S(2)}, u32[]{:S(2)}) collective-permute-start(bf16[2,2,512,128]{3,2,1,0:T(8,128)(2,1)S(1)} %second_product.9.refs_0_), channel_id=1, source_target_pairs={{2,1},{5,6},{8,11},{15,12},{18,17},{21,22},{24,27},{31,28}} | collective-permute-start | bytes 1572872 | tf_op jit(solution)/shard_map/ppermute | solution.py:320
  297.6 13.1 %collective-permute-start.24 = (bf16[2,2,512,128]{3,2,1,0:T(8,128)(2,1)S(1)}, bf16[2,2,512,128]{3,2,1,0:T(8,128)(2,1)}, u32[]{:S(2)}, u32[]{:S(2)}) collective-permute-start(bf16[2,2,512,128]{3,2,1,0:T(8,128)(2,1)S(1)} %second_product.9.refs_0_), channel_id=1, source_target_pairs={{0,1},{7,6},{10,11},{13,12},{16,17},{23,22},{26,27},{29,28}} | collective-permute-start | bytes 1572872 | tf_op jit(solution)/shard_map/ppermute | solution.py:320
  299.0 1.0 copy-start.17
  300.0 1.0 copy-start.19
  301.1 1.0 copy-start.21

commit v19 on v14

--- a/solution.py
+++ b/solution.py
@@ -286,11 +286,11 @@
     half = rows // 2
     mine = lax.dynamic_slice_in_dim(planar, depth * half, half, 2)
     other = turn(mine)
-    other = in_order(other, swap(after(other, envs[3], envs[4])), 2)
+    other = in_order(other, swap(after(other, envs[6], envs[7])), 2)
     site = jnp.where(col == 0, jnp.stack([planar, other]), jnp.stack([other, planar]))
 
     parts = [mine[:, :, : half // 2], mine[:, :, half // 2 :]]
-    travelling = [[shift(after(part, env, site)) for part, env in zip(parts, envs[-2:])]]
+    travelling = [[shift(after(part, env)) for part, env in zip(parts, envs[-2:])]]
     for _ in range(row_count - 2):
         travelling.append([shift(part) for part in travelling[-1]])
 

time: 315 us -> 316 us (level)
  waiting for transfers between devices: 191 us -> 200 us
  local copies, waits for them, and re-layouts: 26.2 us -> 19.5 us
    ppermute x12, waiting for transfers between devices: 172 us -> 178 us  [ring(): lax.ppermute(value, 'row', [(r, (r + 1) % row_count) for r in range(row_c...]
    unnamed x62 -> x58, local copies, waits for them, and re-layouts: 17.6 us -> 12.3 us
  transfers between devices with their start and end apart: 26 -> 26, of which waited for: 17 -> 17; matrix products, arithmetic and copies ran while one was open for 6% -> 6% of each run, Pallas kernels for 17% -> 16%
where the time goes in v19:
time: 316 us; the launch traced here: 315 us
  waiting for transfers between devices  200 us (63%)
  Pallas kernels  54 us (17%)
  starting transfers between devices  27.1 us (9%)
  local copies, waits for them, and re-layouts  19.5 us (6%)
  other arithmetic  13.6 us (4%)
    ppermute x12, waiting for transfers between devices, ring(): lax.ppermute(value, 'row', [(r, (r + 1) % row_count) for r in range(row_c...  178 us
    pallas_call x5, Pallas kernels, second_product(): pl.pallas_call(second_kernel, grid=(mpo_count,), in_specs=[pl.BlockSpec(m...  23.9 us
    pallas_call x1, Pallas kernels, first_product(): pl.pallas_call(functools.partial(first_kernel, w_local), grid=(rows // ro...  23.3 us
    unnamed x58, local copies, waits for them, and re-layouts  12.3 us
    ppermute x6, waiting for transfers between devices, send(): lax.ppermute(value, axes, [(place(r, 1 - c if turned else c, 1 - d if cro...  11.2 us
    ppermute x3, starting transfers between devices, turn_to_goal(): lax.ppermute(value, axes, [(place(r, 1 - c, d), place(r, c, d)) for r, (c...  9.5 us
    ppermute x4, waiting for transfers between devices, swap(): return lax.ppermute(value, 'depth', [(0, 1), (1, 0)])  8.31 us
    ppermute x6, starting transfers between devices, send(): lax.ppermute(value, axes, [(place(r, 1 - c if turned else c, 1 - d if cro...  7.75 us
  transfers between devices with their start and end apart: 26, of which 17 were waited for; matrix products, arithmetic and copies ran while one was open for 6% of the time, Pallas kernels for 16%

profile of v19, /device:TPU:1, one launch (start us, length us, event | category | flops | bytes accessed | tf_op | source)
XLA Modules:
  0.0 314.8 jit_solution(8816174481391844413)
XLA Ops:
  0.0 1.7 constant_dynamic-slice_fusion
  1.7 0.1 collective-permute-start
  1.9 2.7 collective-permute-start.2
  4.6 2.3 collective-permute-start.5
  6.9 3.5 %copy.9 = bf16[2,512,2,1024]{3,1,2,0:T(8,128)(2,1)S(1)} copy(bf16[2,512,2,1024]{3,2,1,0:T(2,128)(2,1)} %param.4) | data formatting | bytes 8388608 | tf_op jit(solution)/shard_map/optimization_barrier | solution.py:206
  10.4 0.0 copy-start.28
  10.4 0.2 dynamic-slice_bitcast_fusion
  10.6 1.3 collective-permute-start.1
  11.9 18.2 %collective-permute-done.2.refs_2_ = bf16[1,2,512,512]{3,2,1,0:T(8,128)(2,1)S(1)} collective-permute-done((bf16[1,2,512,512]{3,2,1,0:T(8,128)(2,1)S(1)}, bf16[1,2,512,512]{3,2,1,0:T(8,128)(2,1)S(1)}, u32[]{:S(2)}, u32[]{:S(2)}) %collective-permute-start.2) | collective-permute-done | bytes 1048608 | tf_op jit(solution)/shard_map/ppermute | solution.py:269
  30.1 22.6 %collective-permute-done.5.refs_3_ = bf16[1,2,512,512]{3,2,1,0:T(8,128)(2,1)} collective-permute-done((bf16[1,2,512,512]{3,2,1,0:T(8,128)(2,1)S(1)}, bf16[1,2,512,512]{3,2,1,0:T(8,128)(2,1)}, u32[]{:S(2)}, u32[]{:S(2)}) %collective-permute-start.5) | collective-permute-done | bytes 1048608 | tf_op jit(solution)/shard_map/ppermute | solution.py:269
  52.7 22.4 %collective-permute-done.3.refs_4_ = bf16[1,2,512,512]{3,2,1,0:T(8,128)(2,1)S(1)} collective-permute-done((bf16[1,2,512,512]{3,2,1,0:T(8,128)(2,1)S(1)}, bf16[1,2,512,512]{3,2,1,0:T(8,128)(2,1)S(1)}, u32[]{:S(2)}, u32[]{:S(2)}) %collective-permute-start.3) | collective-permute-done | bytes 1048608 | tf_op jit(solution)/shard_map/ppermute | solution.py:269
  75.0 1.0 copy-done.9
  76.0 21.5 %collective-permute-done.6.refs_5_ = bf16[1,2,512,512]{3,2,1,0:T(8,128)(2,1)S(1)} collective-permute-done((bf16[1,2,512,512]{3,2,1,0:T(8,128)(2,1)}, bf16[1,2,512,512]{3,2,1,0:T(8,128)(2,1)S(1)}, u32[]{:S(2)}, u32[]{:S(2)}) %collective-permute-start.6) | collective-permute-done | bytes 1048608 | tf_op jit(solution)/shard_map/ppermute | solution.py:269
  97.5 1.0 copy-done.11
  98.5 21.5 %collective-permute-done.4.refs_6_ = bf16[1,2,512,512]{3,2,1,0:T(8,128)(2,1)S(1)} collective-permute-done((bf16[1,2,512,512]{3,2,1,0:T(8,128)(2,1)S(1)}, bf16[1,2,512,512]{3,2,1,0:T(8,128)(2,1)S(1)}, u32[]{:S(2)}, u32[]{:S(2)}) %collective-permute-start.4) | collective-permute-done | bytes 1048608 | tf_op jit(solution)/shard_map/ppermute | solution.py:269
  120.0 1.0 copy-done.13
  121.0 21.4 %collective-permute-done.7.refs_7_ = bf16[1,2,512,512]{3,2,1,0:T(8,128)(2,1)S(1)} collective-permute-done((bf16[1,2,512,512]{3,2,1,0:T(8,128)(2,1)S(1)}, bf16[1,2,512,512]{3,2,1,0:T(8,128)(2,1)S(1)}, u32[]{:S(2)}, u32[]{:S(2)}) %collective-permute-start.7) | collective-permute-done | bytes 1048608 | tf_op jit(solution)/shard_map/ppermute | solution.py:269
  142.5 1.0 copy-done.15
  143.4 0.6 collective-permute-start.8
  144.1 0.1 pad_add_fusion.1.block_ref
  144.2 1.7 fusion
  145.9 0.1 collective-permute-start.9
  146.0 0.7 collective-permute-start.10
  146.7 1.5 collective-permute-done.8
  148.2 5.4 %maximum_select_fusion.1 = bf16[1,2,2,512,1024]{4,3,2,1,0:T(8,128)(2,1)S(1)} fusion(bf16[1,2,2,256,1024]{4,3,2,1,0:T(8,128)(2,1)} %bitcast.10, bf16[1,2,2,256,1024]{4,3,2,1,0:T(8,128)(2,1)} %bitcast.9, pred[]{:T(512)S(6)} %eq.23), kind=kLoop, calls=%fused_computation.1 | loop fusion | flops 18874368 | bytes 8388609 | tf_op jit(solution)/shard_map/jit(_where)/select_n | solution.py:273
  153.7 4.2 %maximum_select_fusion.site_ref = bf16[2,2,2,512,1024]{4,3,2,1,0:T(8,128)(2,1)} fusion(bf16[1,2,2,512,1024]{4,3,2,1,0:T(8,128)(2,1)S(1)} %maximum_select_fusion.1, bf16[1,2,2,512,1024]{4,3,2,1,0:T(8,128)(2,1)S(1)} %bitcast.15, pred[]{:T(512)S(6)} %eq.22), kind=kLoop, calls=%fused_computation | loop fusion | flops 12582912 | bytes 16777216 | tf_op jit(solution)/shard_map/jit(_where)/select_n | solution.py:290
  157.9 23.3 %first_product.1.own_ref = bf16[2,2,2,512,512]{4,3,2,1,0:T(8,128)(2,1)S(1)} custom-call(s32[4]{0:T(128)S(1)} %pad_add_fusion.1.block_ref, f32[2,2,2,2]{3,2,1,0:T(2,128)S(1)} %pad_maximum_fusion.mpo_ref, bf16[2,2,2,512,1024]{4,3,2,1,0:T(8,128)(2,1)} %maximum_select_fusion.site_ref, bf16[1,2,512,512]{3,2,1,0:T(8,128)(2,1)S(1)} %get-tuple-element.31.refs_0_, ...), custom_call_target="tpu_custom_call" | custom-call | tf_op jit(solution)/shard_map/first_product/pallas_call | solution.py:67
  181.3 13.7 %collective-permute-done.10.refs_1_ = bf16[2,2,128,1024]{3,2,1,0:T(8,128)(2,1)S(1)} collective-permute-done((bf16[2,2,128,1024]{3,2,1,0:T(8,128)(2,1)S(1)}, bf16[2,2,128,1024]{3,2,1,0:T(8,128)(2,1)S(1)}, u32[]{:S(2)}, u32[]{:S(2)}) %collective-permute-start.10) | collective-permute-done | bytes 1048608 | tf_op jit(solution)/shard_map/ppermute | solution.py:269
  195.0 0.8 collective-permute-start.11
  195.8 6.8 %collective-permute-done.11.sib_ref = bf16[2,2,2,512,512]{4,3,2,1,0:T(8,128)(2,1)S(1)} collective-permute-done((bf16[2,2,2,512,512]{4,3,2,1,0:T(8,128)(2,1)S(1)}, bf16[2,2,2,512,512]{4,3,2,1,0:T(8,128)(2,1)S(1)}, u32[]{:S(2)}, u32[]{:S(2)}) %collective-permute-start.11) | collective-permute-done | bytes 4194336 | tf_op jit(solution)/shard_map/ppermute | solution.py:210
  202.6 4.8 %second_product.5 = bf16[2,2,512,256]{3,2,1,0:T(8,128)(2,1)S(1)} custom-call(s32[1]{0:T(128)} %bitcast.1.pick_ref, bf16[2,2,2,512,512]{4,3,2,1,0:T(8,128)(2,1)S(1)} %first_product.1.own_ref, bf16[2,2,2,512,512]{4,3,2,1,0:T(8,128)(2,1)S(1)} %collective-permute-done.11.sib_ref, bf16[2,2,128,1024]{3,2,1,0:T(8,128)(2,1)S(1)} %get-tuple-element.17.refs_0_, ...), custom_call_target="tpu_custom_call" | custom-call | tf_op jit(solution)/shard_map/second_product/pallas_call | solution.py:104
  207.4 1.3 collective-permute-start.13
  208.7 0.1 collective-permute-start.14
  208.7 13.8 %collective-permute-done.12.refs_0_ = bf16[2,2,128,1024]{3,2,1,0:T(8,128)(2,1)} collective-permute-done((bf16[2,2,128,1024]{3,2,1,0:T(8,128)(2,1)S(1)}, bf16[2,2,128,1024]{3,2,1,0:T(8,128)(2,1)}, u32[]{:S(2)}, u32[]{:S(2)}) %collective-permute-start.12) | collective-permute-done | bytes 1048608 | tf_op jit(solution)/shard_map/ppermute | solution.py:269
  222.5 4.8 %second_product.6 = bf16[2,2,512,256]{3,2,1,0:T(8,128)(2,1)S(1)} custom-call(s32[1]{0:T(128)} %bitcast.1.pick_ref, bf16[2,2,2,512,512]{4,3,2,1,0:T(8,128)(2,1)S(1)} %first_product.1.own_ref, bf16[2,2,2,512,512]{4,3,2,1,0:T(8,128)(2,1)S(1)} %collective-permute-done.11.sib_ref, bf16[2,2,128,1024]{3,2,1,0:T(8,128)(2,1)S(1)} %collective-permute-done.9.refs_0_, ...), custom_call_target="tpu_custom_call" | custom-call | tf_op jit(solution)/shard_map/second_product/pallas_call | solution.py:104
  227.3 4.1 %collective-permute-start.19 = (bf16[2,2,512,256]{3,2,1,0:T(8,128)(2,1)S(1)}, bf16[2,2,512,256]{3,2,1,0:T(8,128)(2,1)}, u32[]{:S(2)}, u32[]{:S(2)}) collective-permute-start(bf16[2,2,512,256]{3,2,1,0:T(8,128)(2,1)S(1)} %second_product.6), channel_id=1, source_target_pairs={{0,2},{1,3},{6,4},{7,5},{10,8},{11,9},{12,14},{13,15},{16,18},{17,... | collective-permute-start | bytes 3145736 | tf_op jit(solution)/shard_map/ppermute | solution.py:312
  231.4 2.3 collective-permute-done.13
  233.7 11.2 %collective-permute-done.14.refs_1_ = bf16[2,2,128,1024]{3,2,1,0:T(8,128)(2,1)} collective-permute-done((bf16[2,2,128,1024]{3,2,1,0:T(8,128)(2,1)S(1)}, bf16[2,2,128,1024]{3,2,1,0:T(8,128)(2,1)}, u32[]{:S(2)}, u32[]{:S(2)}) %collective-permute-start.14) | collective-permute-done | bytes 1048608 | tf_op jit(solution)/shard_map/ppermute | solution.py:269
  245.0 6.3 %second_product.7 = bf16[2,2,512,256]{3,2,1,0:T(8,128)(2,1)S(1)} custom-call(s32[1]{0:T(128)} %bitcast.1.pick_ref, bf16[2,2,2,512,512]{4,3,2,1,0:T(8,128)(2,1)S(1)} %first_product.1.own_ref, bf16[2,2,2,512,512]{4,3,2,1,0:T(8,128)(2,1)S(1)} %collective-permute-done.11.sib_ref, bf16[2,2,128,1024]{3,2,1,0:T(8,128)(2,1)} %collective-permute-done.12.refs_0_, ...), custom_call_target="tpu_custom_call" | custom-call | tf_op jit(solution)/shard_map/second_product/pallas_call | solution.py:104
  251.3 4.1 %collective-permute-start.20 = (bf16[2,2,512,256]{3,2,1,0:T(8,128)(2,1)S(1)}, bf16[2,2,512,256]{3,2,1,0:T(8,128)(2,1)}, u32[]{:S(2)}, u32[]{:S(2)}) collective-permute-start(bf16[2,2,512,256]{3,2,1,0:T(8,128)(2,1)S(1)} %second_product.7), channel_id=1, source_target_pairs={{0,2},{1,3},{4,6},{5,7},{10,8},{11,9},{14,12},{15,13},{16,18},{17,... | collective-permute-start | bytes 3145736 | tf_op jit(solution)/shard_map/ppermute | solution.py:312
  255.4 12.0 %collective-permute-done.15.refs_0_ = bf16[2,2,128,1024]{3,2,1,0:T(8,128)(2,1)} collective-permute-done((bf16[2,2,128,1024]{3,2,1,0:T(8,128)(2,1)}, bf16[2,2,128,1024]{3,2,1,0:T(8,128)(2,1)}, u32[]{:S(2)}, u32[]{:S(2)}) %collective-permute-start.15) | collective-permute-done | bytes 1048608 | tf_op jit(solution)/shard_map/ppermute | solution.py:269
  267.4 2.2 copy-done.1
  269.6 2.2 copy-done.3
  271.8 4.0 %second_product.8.refs_0_ = bf16[2,2,512,128]{3,2,1,0:T(8,128)(2,1)S(1)} custom-call(s32[1]{0:T(128)} %bitcast.1.pick_ref, bf16[2,2,2,512,512]{4,3,2,1,0:T(8,128)(2,1)S(1)} %copy-done.1, bf16[2,2,2,512,512]{4,3,2,1,0:T(8,128)(2,1)S(1)} %copy-done.3, bf16[2,2,128,1024]{3,2,1,0:T(8,128)(2,1)} %collective-permute-done.15.refs_0_), custom_call_target="tpu_custom_call" | custom-call | tf_op jit(solution)/shard_map/second_product/pallas_call | solution.py:104
  275.8 1.3 collective-permute-start.16
  277.1 1.3 collective-permute-start.17
  278.4 1.3 collective-permute-start.18
  279.7 3.8 %select_convert_fusion = (bf16[2,2,512,256]{3,2,1,0:T(8,128)(2,1)}, f32[2,2,512,256]{3,2,1,0:T(8,128)S(1)}) fusion(bf16[2,2,512,256]{3,2,1,0:T(8,128)(2,1)S(1)} %copy-done.27, bf16[2,2,512,256]{3,2,1,0:T(8,128)(2,1)S(1)} %second_product.5, bf16[2,2,512,256]{3,2,1,0:T(8,128)(2,1)} %collective-permute-done.19, bf16[2,2,512,256]{3,2,1,0:T(8,128)(2,1)S(1)} %copy-done.5, ...), kind=kLoop, calls=%fused_computation.2 | loop fusion | flops 7340032 | bytes 9437188 | tf_op jit(solution)/shard_map/convert_element_type | solution.py:346
  283.5 1.2 collective-permute-start.25
  284.7 5.1 %collective-permute-done.16.refs_1_ = bf16[2,2,512,128]{3,2,1,0:T(8,128)(2,1)S(1)} collective-permute-done((bf16[2,2,512,128]{3,2,1,0:T(8,128)(2,1)S(1)}, bf16[2,2,512,128]{3,2,1,0:T(8,128)(2,1)S(1)}, u32[]{:S(2)}, u32[]{:S(2)}) %collective-permute-start.16) | collective-permute-done | bytes 524320 | tf_op jit(solution)/shard_map/ppermute | solution.py:319
  289.8 1.5 collective-permute-done.17.refs_2_
  291.4 0.8 copy-done.19
  292.2 4.1 %second_product.9.refs_0_ = bf16[2,2,512,128]{3,2,1,0:T(8,128)(2,1)S(1)} custom-call(s32[1]{0:T(128)} %bitcast.1.pick_ref, bf16[2,2,2,512,512]{4,3,2,1,0:T(8,128)(2,1)S(1)} %copy-done.1, bf16[2,2,2,512,512]{4,3,2,1,0:T(8,128)(2,1)S(1)} %copy-done.3, bf16[2,2,128,1024]{3,2,1,0:T(8,128)(2,1)} %collective-permute-done.21.refs_0_), custom_call_target="tpu_custom_call" | custom-call | tf_op jit(solution)/shard_map/second_product/pallas_call | solution.py:104
  296.2 1.3 collective-permute-start.22
  297.5 1.3 collective-permute-start.23
  298.8 1.3 collective-permute-start.24
  300.2 0.1 pad_add_fusion.pick_ref
  300.2 1.0 copy-done.18
  301.3 1.0 copy-done.20
  302.3 1.0 copy-done.22
  303.4 4.0 %finish.1.refs_4_ = f32[2,2,512,512]{3,2,1,0:T(8,128)} custom-call(s32[2]{0:T(128)S(1)} %pad_add_fusion.pick_ref, f32[2,2,512,256]{3,2,1,0:T(8,128)S(1)} %get-tuple-element.26.mine_ref, bf16[2,2,512,256]{3,2,1,0:T(8,128)(2,1)} %collective-permute-done.25.siblings_ref, bf16[2,2,512,128]{3,2,1,0:T(8,128)(2,1)S(1)} %copy-done.8, ...), custom_call_target="tpu_custom_call" | custom-call | tf_op jit(solution)/shard_map/finish/pallas_call | solution.py:145
  307.3 2.6 collective-permute-done.22.refs_1_
  310.0 1.9 collective-permute-done.23.refs_2_
  311.9 2.8 finish_last.1
  (65 shorter events, 0.1 us)
Async XLA Ops:
  1.7 2.9 collective-permute-start
  1.9 28.2 %collective-permute-start.2 = (bf16[1,2,512,512]{3,2,1,0:T(8,128)(2,1)S(1)}, bf16[1,2,512,512]{3,2,1,0:T(8,128)(2,1)S(1)}, u32[]{:S(2)}, u32[]{:S(2)}) collective-permute-start(bf16[1,2,512,512]{3,2,1,0:T(8,128)(2,1)S(1)} %get-tuple-element.31.refs_0_), channel_id=1, source_target_pairs={{0,4},{4,8},{8,12},{12,0},{1,5},{5,9},{9,13},{13,1},{2,6},{6,10},{... | collective-permute-start | bytes 3145736 | tf_op jit(solution)/shard_map/ppermute | solution.py:269
  4.6 48.1 %collective-permute-start.5 = (bf16[1,2,512,512]{3,2,1,0:T(8,128)(2,1)S(1)}, bf16[1,2,512,512]{3,2,1,0:T(8,128)(2,1)}, u32[]{:S(2)}, u32[]{:S(2)}) collective-permute-start(bf16[1,2,512,512]{3,2,1,0:T(8,128)(2,1)S(1)} %collective-permute-done.refs_1_), channel_id=1, source_target_pairs={{0,4},{4,8},{8,12},{12,0},{1,5},{5,9},{9,13},{13,1},{2,6},{6,10},{... | collective-permute-start | bytes 3145736 | tf_op jit(solution)/shard_map/ppermute | solution.py:269
  10.4 132.0 %copy-start.23 = (bf16[2,512,2,1024]{3,1,2,0:T(8,128)(2,1)}, bf16[2,512,2,1024]{3,1,2,0:T(8,128)(2,1)S(1)}, u32[]{:S(2)}) copy-start(bf16[2,512,2,1024]{3,1,2,0:T(8,128)(2,1)S(1)} %copy.9) | copy-start | bytes 12582916
  10.4 133.7 %copy-start.28 = (f32[2,2,2,2]{3,2,1,0:T(2,128)S(1)}, f32[2,2,2,2]{3,2,1,0:T(2,128)}, u32[]{:S(2)}) copy-start(f32[2,2,2,2]{3,2,1,0:T(2,128)} %param.5) | copy-start | bytes 196
  10.6 131.8 %copy-start.25 = (bf16[2,2,256,1024]{3,2,1,0:T(8,128)(2,1)}, bf16[2,2,256,1024]{3,2,1,0:T(8,128)(2,1)S(1)}, u32[]{:S(2)}) copy-start(bf16[2,2,256,1024]{3,2,1,0:T(8,128)(2,1)S(1)} %dynamic-slice_bitcast_fusion) | copy-start | bytes 6291460
  10.6 87.8 %collective-permute-start.1 = (bf16[2,2,256,1024]{3,2,1,0:T(8,128)(2,1)S(1)}, bf16[2,2,256,1024]{3,2,1,0:T(8,128)(2,1)}, u32[]{:S(2)}, u32[]{:S(2)}) collective-permute-start(bf16[2,2,256,1024]{3,2,1,0:T(8,128)(2,1)S(1)} %dynamic-slice_bitcast_fusion), channel_id=1, source_target_pairs={{0,2},{2,0},{1,3},{3,1},{4,6},{6,4},{5,7},{7,5},{8,10},{10,8},{9,1... | collective-permute-start | bytes 6291464 | tf_op jit(solution)/shard_map/ppermute | solution.py:272
  30.1 44.9 %collective-permute-start.3 = (bf16[1,2,512,512]{3,2,1,0:T(8,128)(2,1)S(1)}, bf16[1,2,512,512]{3,2,1,0:T(8,128)(2,1)S(1)}, u32[]{:S(2)}, u32[]{:S(2)}) collective-permute-start(bf16[1,2,512,512]{3,2,1,0:T(8,128)(2,1)S(1)} %collective-permute-done.2.refs_2_), channel_id=1, source_target_pairs={{0,4},{4,8},{8,12},{12,0},{1,5},{5,9},{9,13},{13,1},{2,6},{6,10},{... | collective-permute-start | bytes 3145736 | tf_op jit(solution)/shard_map/ppermute | solution.py:269
  52.7 44.8 %collective-permute-start.6 = (bf16[1,2,512,512]{3,2,1,0:T(8,128)(2,1)}, bf16[1,2,512,512]{3,2,1,0:T(8,128)(2,1)S(1)}, u32[]{:S(2)}, u32[]{:S(2)}) collective-permute-start(bf16[1,2,512,512]{3,2,1,0:T(8,128)(2,1)} %collective-permute-done.5.refs_3_), channel_id=1, source_target_pairs={{0,4},{4,8},{8,12},{12,0},{1,5},{5,9},{9,13},{13,1},{2,6},{6,10},{... | collective-permute-start | bytes 3145736 | tf_op jit(solution)/shard_map/ppermute | solution.py:269
  75.0 44.9 %collective-permute-start.4 = (bf16[1,2,512,512]{3,2,1,0:T(8,128)(2,1)S(1)}, bf16[1,2,512,512]{3,2,1,0:T(8,128)(2,1)S(1)}, u32[]{:S(2)}, u32[]{:S(2)}) collective-permute-start(bf16[1,2,512,512]{3,2,1,0:T(8,128)(2,1)S(1)} %collective-permute-done.3.refs_4_), channel_id=1, source_target_pairs={{0,4},{4,8},{8,12},{12,0},{1,5},{5,9},{9,13},{13,1},{2,6},{6,10},{... | collective-permute-start | bytes 3145736 | tf_op jit(solution)/shard_map/ppermute | solution.py:269
  75.0 1.0 copy-start.9
  97.5 44.9 %collective-permute-start.7 = (bf16[1,2,512,512]{3,2,1,0:T(8,128)(2,1)S(1)}, bf16[1,2,512,512]{3,2,1,0:T(8,128)(2,1)S(1)}, u32[]{:S(2)}, u32[]{:S(2)}) collective-permute-start(bf16[1,2,512,512]{3,2,1,0:T(8,128)(2,1)S(1)} %collective-permute-done.6.refs_5_), channel_id=1, source_target_pairs={{0,4},{4,8},{8,12},{12,0},{1,5},{5,9},{9,13},{13,1},{2,6},{6,10},{... | collective-permute-start | bytes 3145736 | tf_op jit(solution)/shard_map/ppermute | solution.py:269
  97.5 1.0 copy-start.11
  120.0 1.0 copy-start.13
  142.5 1.0 copy-start.15
  143.4 4.8 %collective-permute-start.8 = (bf16[2,2,256,1024]{3,2,1,0:T(8,128)(2,1)}, bf16[2,2,256,1024]{3,2,1,0:T(8,128)(2,1)}, u32[]{:S(2)}, u32[]{:S(2)}) collective-permute-start(bf16[2,2,256,1024]{3,2,1,0:T(8,128)(2,1)} %collective-permute-done.1), channel_id=1, source_target_pairs={{0,1},{1,0},{2,3},{3,2},{4,5},{5,4},{6,7},{7,6},{8,9},{9,8},{10,11... | collective-permute-start | bytes 6291464 | tf_op jit(solution)/shard_map/ppermute | solution.py:210
  145.9 35.4 %collective-permute-start.9 = (bf16[2,2,128,1024]{3,2,1,0:T(8,128)(2,1)S(1)}, bf16[2,2,128,1024]{3,2,1,0:T(8,128)(2,1)S(1)}, u32[]{:S(2)}, u32[]{:S(2)}) collective-permute-start(bf16[2,2,128,1024]{3,2,1,0:T(8,128)(2,1)S(1)} %get-tuple-element.17.refs_0_), channel_id=1, source_target_pairs={{0,4},{4,8},{8,12},{12,0},{1,5},{5,9},{9,13},{13,1},{2,6},{6,10},{... | collective-permute-start | bytes 3145736 | tf_op jit(solution)/shard_map/ppermute | solution.py:269
  146.0 49.0 %collective-permute-start.10 = (bf16[2,2,128,1024]{3,2,1,0:T(8,128)(2,1)S(1)}, bf16[2,2,128,1024]{3,2,1,0:T(8,128)(2,1)S(1)}, u32[]{:S(2)}, u32[]{:S(2)}) collective-permute-start(bf16[2,2,128,1024]{3,2,1,0:T(8,128)(2,1)S(1)} %get-tuple-element.18.refs_1_), channel_id=1, source_target_pairs={{0,4},{4,8},{8,12},{12,0},{1,5},{5,9},{9,13},{13,1},{2,6},{6,10},{... | collective-permute-start | bytes 3145736 | tf_op jit(solution)/shard_map/ppermute | solution.py:269
  148.2 5.4 %copy-start.24 = (bf16[2,512,2,1024]{3,1,2,0:T(8,128)(2,1)S(1)}, bf16[2,512,2,1024]{3,1,2,0:T(8,128)(2,1)}, u32[]{:S(2)}) copy-start(bf16[2,512,2,1024]{3,1,2,0:T(8,128)(2,1)} %copy-done.23) | copy-start | bytes 12582916
  153.6 4.3 %copy-start.10 = (bf16[1,2,512,512]{3,2,1,0:T(8,128)(2,1)S(1)}, bf16[1,2,512,512]{3,2,1,0:T(8,128)(2,1)}, u32[]{:S(2)}) copy-start(bf16[1,2,512,512]{3,2,1,0:T(8,128)(2,1)} %copy-done.9) | copy-start | bytes 3145732
  153.6 4.3 %copy-start.12 = (bf16[1,2,512,512]{3,2,1,0:T(8,128)(2,1)S(1)}, bf16[1,2,512,512]{3,2,1,0:T(8,128)(2,1)}, u32[]{:S(2)}) copy-start(bf16[1,2,512,512]{3,2,1,0:T(8,128)(2,1)} %copy-done.11) | copy-start | bytes 3145732
  153.7 4.3 %copy-start.14 = (bf16[1,2,512,512]{3,2,1,0:T(8,128)(2,1)S(1)}, bf16[1,2,512,512]{3,2,1,0:T(8,128)(2,1)}, u32[]{:S(2)}) copy-start(bf16[1,2,512,512]{3,2,1,0:T(8,128)(2,1)} %copy-done.13) | copy-start | bytes 3145732
  153.7 4.3 %copy-start.16 = (bf16[1,2,512,512]{3,2,1,0:T(8,128)(2,1)S(1)}, bf16[1,2,512,512]{3,2,1,0:T(8,128)(2,1)}, u32[]{:S(2)}) copy-start(bf16[1,2,512,512]{3,2,1,0:T(8,128)(2,1)} %copy-done.15) | copy-start | bytes 3145732
  181.3 63.7 %copy-start = (bf16[2,2,2,512,512]{4,3,2,1,0:T(8,128)(2,1)}, bf16[2,2,2,512,512]{4,3,2,1,0:T(8,128)(2,1)S(1)}, u32[]{:S(2)}) copy-start(bf16[2,2,2,512,512]{4,3,2,1,0:T(8,128)(2,1)S(1)} %first_product.1.own_ref) | copy-start | bytes 12582916
  195.0 7.6 %collective-permute-start.11 = (bf16[2,2,2,512,512]{4,3,2,1,0:T(8,128)(2,1)S(1)}, bf16[2,2,2,512,512]{4,3,2,1,0:T(8,128)(2,1)S(1)}, u32[]{:S(2)}, u32[]{:S(2)}) collective-permute-start(bf16[2,2,2,512,512]{4,3,2,1,0:T(8,128)(2,1)S(1)} %first_product.1.own_ref), channel_id=1, source_target_pairs={{0,1},{1,0},{2,3},{3,2},{4,5},{5,4},{6,7},{7,6},{8,9},{9,8},{10,11... | collective-permute-start | bytes 12582920 | tf_op jit(solution)/shard_map/ppermute | solution.py:210
  195.8 26.7 %collective-permute-start.12 = (bf16[2,2,128,1024]{3,2,1,0:T(8,128)(2,1)S(1)}, bf16[2,2,128,1024]{3,2,1,0:T(8,128)(2,1)}, u32[]{:S(2)}, u32[]{:S(2)}) collective-permute-start(bf16[2,2,128,1024]{3,2,1,0:T(8,128)(2,1)S(1)} %collective-permute-done.9.refs_0_), channel_id=1, source_target_pairs={{0,4},{4,8},{8,12},{12,0},{1,5},{5,9},{9,13},{13,1},{2,6},{6,10},{... | collective-permute-start | bytes 3145736 | tf_op jit(solution)/shard_map/ppermute | solution.py:269
  202.6 42.4 %copy-start.2 = (bf16[2,2,2,512,512]{4,3,2,1,0:T(8,128)(2,1)}, bf16[2,2,2,512,512]{4,3,2,1,0:T(8,128)(2,1)S(1)}, u32[]{:S(2)}) copy-start(bf16[2,2,2,512,512]{4,3,2,1,0:T(8,128)(2,1)S(1)} %collective-permute-done.11.sib_ref) | copy-start | bytes 12582916
  207.4 26.4 %collective-permute-start.13 = (bf16[2,2,512,256]{3,2,1,0:T(8,128)(2,1)S(1)}, bf16[2,2,512,256]{3,2,1,0:T(8,128)(2,1)S(1)}, u32[]{:S(2)}, u32[]{:S(2)}) collective-permute-start(bf16[2,2,512,256]{3,2,1,0:T(8,128)(2,1)S(1)} %second_product.5), channel_id=1, source_target_pairs={{2,0},{3,1},{6,4},{7,5},{8,10},{9,11},{12,14},{13,15},{18,16},{19,... | collective-permute-start | bytes 3145736 | tf_op jit(solution)/shard_map/ppermute | solution.py:312
  208.7 36.3 %collective-permute-start.14 = (bf16[2,2,128,1024]{3,2,1,0:T(8,128)(2,1)S(1)}, bf16[2,2,128,1024]{3,2,1,0:T(8,128)(2,1)}, u32[]{:S(2)}, u32[]{:S(2)}) collective-permute-start(bf16[2,2,128,1024]{3,2,1,0:T(8,128)(2,1)S(1)} %collective-permute-done.10.refs_1_), channel_id=1, source_target_pairs={{0,4},{4,8},{8,12},{12,0},{1,5},{5,9},{9,13},{13,1},{2,6},{6,10},{... | collective-permute-start | bytes 3145736 | tf_op jit(solution)/shard_map/ppermute | solution.py:269
  222.5 44.9 %collective-permute-start.15 = (bf16[2,2,128,1024]{3,2,1,0:T(8,128)(2,1)}, bf16[2,2,128,1024]{3,2,1,0:T(8,128)(2,1)}, u32[]{:S(2)}, u32[]{:S(2)}) collective-permute-start(bf16[2,2,128,1024]{3,2,1,0:T(8,128)(2,1)} %collective-permute-done.12.refs_0_), channel_id=1, source_target_pairs={{0,4},{4,8},{8,12},{12,0},{1,5},{5,9},{9,13},{13,1},{2,6},{6,10},{... | collective-permute-start | bytes 3145736 | tf_op jit(solution)/shard_map/ppermute | solution.py:269
  227.3 24.0 %copy-start.4 = (bf16[2,2,512,256]{3,2,1,0:T(8,128)(2,1)}, bf16[2,2,512,256]{3,2,1,0:T(8,128)(2,1)S(1)}, u32[]{:S(2)}) copy-start(bf16[2,2,512,256]{3,2,1,0:T(8,128)(2,1)S(1)} %second_product.6) | copy-start | bytes 3145732
  227.3 51.1 %collective-permute-start.19 = (bf16[2,2,512,256]{3,2,1,0:T(8,128)(2,1)S(1)}, bf16[2,2,512,256]{3,2,1,0:T(8,128)(2,1)}, u32[]{:S(2)}, u32[]{:S(2)}) collective-permute-start(bf16[2,2,512,256]{3,2,1,0:T(8,128)(2,1)S(1)} %second_product.6), channel_id=1, source_target_pairs={{0,2},{1,3},{6,4},{7,5},{10,8},{11,9},{12,14},{13,15},{16,18},{17,... | collective-permute-start | bytes 3145736 | tf_op jit(solution)/shard_map/ppermute | solution.py:312
  233.7 17.6 %copy-start.26 = (bf16[2,2,512,256]{3,2,1,0:T(8,128)(2,1)}, bf16[2,2,512,256]{3,2,1,0:T(8,128)(2,1)S(1)}, u32[]{:S(2)}) copy-start(bf16[2,2,512,256]{3,2,1,0:T(8,128)(2,1)S(1)} %collective-permute-done.13) | copy-start | bytes 3145732
  251.3 24.5 %copy-start.6 = (bf16[2,2,512,256]{3,2,1,0:T(8,128)(2,1)}, bf16[2,2,512,256]{3,2,1,0:T(8,128)(2,1)S(1)}, u32[]{:S(2)}) copy-start(bf16[2,2,512,256]{3,2,1,0:T(8,128)(2,1)S(1)} %second_product.7) | copy-start | bytes 3145732
  251.3 28.4 %collective-permute-start.20 = (bf16[2,2,512,256]{3,2,1,0:T(8,128)(2,1)S(1)}, bf16[2,2,512,256]{3,2,1,0:T(8,128)(2,1)}, u32[]{:S(2)}, u32[]{:S(2)}) collective-permute-start(bf16[2,2,512,256]{3,2,1,0:T(8,128)(2,1)S(1)} %second_product.7), channel_id=1, source_target_pairs={{0,2},{1,3},{4,6},{5,7},{10,8},{11,9},{14,12},{15,13},{16,18},{17,... | collective-permute-start | bytes 3145736 | tf_op jit(solution)/shard_map/ppermute | solution.py:312
  255.4 36.8 %collective-permute-start.21 = (bf16[2,2,128,1024]{3,2,1,0:T(8,128)(2,1)}, bf16[2,2,128,1024]{3,2,1,0:T(8,128)(2,1)}, u32[]{:S(2)}, u32[]{:S(2)}) collective-permute-start(bf16[2,2,128,1024]{3,2,1,0:T(8,128)(2,1)} %collective-permute-done.14.refs_1_), channel_id=1, source_target_pairs={{0,4},{4,8},{8,12},{12,0},{1,5},{5,9},{9,13},{13,1},{2,6},{6,10},{... | collective-permute-start | bytes 3145736 | tf_op jit(solution)/shard_map/ppermute | solution.py:269
  267.4 2.2 copy-start.1
  269.6 2.2 copy-start.3
  271.8 7.9 %copy-start.5 = (bf16[2,2,512,256]{3,2,1,0:T(8,128)(2,1)S(1)}, bf16[2,2,512,256]{3,2,1,0:T(8,128)(2,1)}, u32[]{:S(2)}) copy-start(bf16[2,2,512,256]{3,2,1,0:T(8,128)(2,1)} %copy-done.4) | copy-start | bytes 3145732
  271.8 7.9 %copy-start.27 = (bf16[2,2,512,256]{3,2,1,0:T(8,128)(2,1)S(1)}, bf16[2,2,512,256]{3,2,1,0:T(8,128)(2,1)}, u32[]{:S(2)}) copy-start(bf16[2,2,512,256]{3,2,1,0:T(8,128)(2,1)} %copy-done.26) | copy-start | bytes 3145732
  275.8 7.7 %copy-start.7 = (bf16[2,2,512,128]{3,2,1,0:T(8,128)(2,1)}, bf16[2,2,512,128]{3,2,1,0:T(8,128)(2,1)S(1)}, u32[]{:S(2)}) copy-start(bf16[2,2,512,128]{3,2,1,0:T(8,128)(2,1)S(1)} %second_product.8.refs_0_) | copy-start | bytes 1572868
  275.8 14.0 %collective-permute-start.16 = (bf16[2,2,512,128]{3,2,1,0:T(8,128)(2,1)S(1)}, bf16[2,2,512,128]{3,2,1,0:T(8,128)(2,1)S(1)}, u32[]{:S(2)}, u32[]{:S(2)}) collective-permute-start(bf16[2,2,512,128]{3,2,1,0:T(8,128)(2,1)S(1)} %second_product.8.refs_0_), channel_id=1, source_target_pairs={{3,1},{4,6},{9,11},{14,12},{19,17},{20,22},{25,27},{30,28}} | collective-permute-start | bytes 1572872 | tf_op jit(solution)/shard_map/ppermute | solution.py:319
  277.1 14.2 %collective-permute-start.17 = (bf16[2,2,512,128]{3,2,1,0:T(8,128)(2,1)S(1)}, bf16[2,2,512,128]{3,2,1,0:T(8,128)(2,1)S(1)}, u32[]{:S(2)}, u32[]{:S(2)}) collective-permute-start(bf16[2,2,512,128]{3,2,1,0:T(8,128)(2,1)S(1)} %second_product.8.refs_0_), channel_id=1, source_target_pairs={{2,1},{5,6},{8,11},{15,12},{18,17},{21,22},{24,27},{31,28}} | collective-permute-start | bytes 1572872 | tf_op jit(solution)/shard_map/ppermute | solution.py:319
  278.4 13.7 %collective-permute-start.18 = (bf16[2,2,512,128]{3,2,1,0:T(8,128)(2,1)S(1)}, bf16[2,2,512,128]{3,2,1,0:T(8,128)(2,1)S(1)}, u32[]{:S(2)}, u32[]{:S(2)}) collective-permute-start(bf16[2,2,512,128]{3,2,1,0:T(8,128)(2,1)S(1)} %second_product.8.refs_0_), channel_id=1, source_target_pairs={{0,1},{7,6},{10,11},{13,12},{16,17},{23,22},{26,27},{29,28}} | collective-permute-start | bytes 1572872 | tf_op jit(solution)/shard_map/ppermute | solution.py:319
  283.5 16.7 %collective-permute-start.25 = (bf16[2,2,512,256]{3,2,1,0:T(8,128)(2,1)}, bf16[2,2,512,256]{3,2,1,0:T(8,128)(2,1)}, u32[]{:S(2)}, u32[]{:S(2)}) collective-permute-start(bf16[2,2,512,256]{3,2,1,0:T(8,128)(2,1)} %get-tuple-element.25), channel_id=1, source_target_pairs={{0,1},{1,0},{2,3},{3,2},{4,5},{5,4},{6,7},{7,6},{8,9},{9,8},{10,11... | collective-permute-start | bytes 3145736 | tf_op jit(solution)/shard_map/ppermute | solution.py:210
  289.8 6.4 %copy-start.17 = (bf16[2,2,512,128]{3,2,1,0:T(8,128)(2,1)}, bf16[2,2,512,128]{3,2,1,0:T(8,128)(2,1)S(1)}, u32[]{:S(2)}) copy-start(bf16[2,2,512,128]{3,2,1,0:T(8,128)(2,1)S(1)} %collective-permute-done.16.refs_1_) | copy-start | bytes 1572868
  291.4 0.8 copy-start.19
  292.2 4.1 %copy-start.21 = (bf16[2,2,512,128]{3,2,1,0:T(8,128)(2,1)}, bf16[2,2,512,128]{3,2,1,0:T(8,128)(2,1)S(1)}, u32[]{:S(2)}) copy-start(bf16[2,2,512,128]{3,2,1,0:T(8,128)(2,1)S(1)} %collective-permute-done.18.refs_3_) | copy-start | bytes 1572868
  292.2 8.1 %copy-start.8 = (bf16[2,2,512,128]{3,2,1,0:T(8,128)(2,1)S(1)}, bf16[2,2,512,128]{3,2,1,0:T(8,128)(2,1)}, u32[]{:S(2)}) copy-start(bf16[2,2,512,128]{3,2,1,0:T(8,128)(2,1)} %copy-done.7) | copy-start | bytes 1572868
  296.2 13.7 %collective-permute-start.22 = (bf16[2,2,512,128]{3,2,1,0:T(8,128)(2,1)S(1)}, bf16[2,2,512,128]{3,2,1,0:T(8,128)(2,1)}, u32[]{:S(2)}, u32[]{:S(2)}) collective-permute-start(bf16[2,2,512,128]{3,2,1,0:T(8,128)(2,1)S(1)} %second_product.9.refs_0_), channel_id=1, source_target_pairs={{3,1},{4,6},{9,11},{14,12},{19,17},{20,22},{25,27},{30,28}} | collective-permute-start | bytes 1572872 | tf_op jit(solution)/shard_map/ppermute | solution.py:319
  297.5 14.3 %collective-permute-start.23 = (bf16[2,2,512,128]{3,2,1,0:T(8,128)(2,1)S(1)}, bf16[2,2,512,128]{3,2,1,0:T(8,128)(2,1)}, u32[]{:S(2)}, u32[]{:S(2)}) collective-permute-start(bf16[2,2,512,128]{3,2,1,0:T(8,128)(2,1)S(1)} %second_product.9.refs_0_), channel_id=1, source_target_pairs={{2,1},{5,6},{8,11},{15,12},{18,17},{21,22},{24,27},{31,28}} | collective-permute-start | bytes 1572872 | tf_op jit(solution)/shard_map/ppermute | solution.py:319
  298.8 13.1 %collective-permute-start.24 = (bf16[2,2,512,128]{3,2,1,0:T(8,128)(2,1)S(1)}, bf16[2,2,512,128]{3,2,1,0:T(8,128)(2,1)}, u32[]{:S(2)}, u32[]{:S(2)}) collective-permute-start(bf16[2,2,512,128]{3,2,1,0:T(8,128)(2,1)S(1)} %second_product.9.refs_0_), channel_id=1, source_target_pairs={{0,1},{7,6},{10,11},{13,12},{16,17},{23,22},{26,27},{29,28}} | collective-permute-start | bytes 1572872 | tf_op jit(solution)/shard_map/ppermute | solution.py:319
  300.2 1.0 copy-start.18
  301.3 1.0 copy-start.20
  302.3 1.0 copy-start.22

commit v20 on v19

--- a/solution.py
+++ b/solution.py
@@ -286,7 +286,7 @@
     half = rows // 2
     mine = lax.dynamic_slice_in_dim(planar, depth * half, half, 2)
     other = turn(mine)
-    other = in_order(other, swap(after(other, envs[6], envs[7])), 2)
+    other = in_order(other, swap(after(other, envs[5], envs[6])), 2)
     site = jnp.where(col == 0, jnp.stack([planar, other]), jnp.stack([other, planar]))
 
     parts = [mine[:, :, : half // 2], mine[:, :, half // 2 :]]

time: 316 us -> 315 us (level)
    unnamed x58 -> x54, local copies, waits for them, and re-layouts: 12.3 us -> 11.3 us
where the time goes in v20:
time: 315 us; the launch traced here: 314 us
  waiting for transfers between devices  199 us (63%)
  Pallas kernels  54.3 us (17%)
  starting transfers between devices  27.1 us (9%)
  local copies, waits for them, and re-layouts  19.5 us (6%)
  other arithmetic  13.4 us (4%)
    ppermute x12, waiting for transfers between devices, ring(): lax.ppermute(value, 'row', [(r, (r + 1) % row_count) for r in range(row_c...  179 us
    pallas_call x5, Pallas kernels, second_product(): pl.pallas_call(second_kernel, grid=(mpo_count,), in_specs=[pl.BlockSpec(m...  24.1 us
    pallas_call x1, Pallas kernels, first_product(): pl.pallas_call(functools.partial(first_kernel, w_local), grid=(rows // ro...  23.5 us
    unnamed x54, local copies, waits for them, and re-layouts  11.3 us
    ppermute x6, waiting for transfers between devices, send(): lax.ppermute(value, axes, [(place(r, 1 - c if turned else c, 1 - d if cro...  11.2 us
    ppermute x3, starting transfers between devices, turn_to_goal(): lax.ppermute(value, axes, [(place(r, 1 - c, d), place(r, c, d)) for r, (c...  9.48 us
    ppermute x6, starting transfers between devices, send(): lax.ppermute(value, axes, [(place(r, 1 - c if turned else c, 1 - d if cro...  7.75 us
    ppermute x4, waiting for transfers between devices, swap(): return lax.ppermute(value, 'depth', [(0, 1), (1, 0)])  6.86 us
  transfers between devices with their start and end apart: 26, of which 17 were waited for; matrix products, arithmetic and copies ran while one was open for 6% of the time, Pallas kernels for 16%

profile of v20, /device:TPU:1, one launch (start us, length us, event | category | flops | bytes accessed | tf_op | source)
XLA Modules:
  0.0 314.1 jit_solution(9746619002760741805)
XLA Ops:
  0.0 2.7 constant_dynamic-slice_fusion
  2.7 0.1 collective-permute-start
  2.8 2.7 collective-permute-start.4
  5.5 0.1 collective-permute-done.refs_1_
  5.6 3.5 %copy.9 = bf16[2,512,2,1024]{3,1,2,0:T(8,128)(2,1)S(1)} copy(bf16[2,512,2,1024]{3,2,1,0:T(2,128)(2,1)} %param.4) | data formatting | bytes 8388608 | tf_op jit(solution)/shard_map/optimization_barrier | solution.py:206
  9.1 0.0 copy-start.21
  9.1 0.0 copy-start.26
  9.1 0.2 dynamic-slice_bitcast_fusion
  9.3 2.4 collective-permute-start.1
  11.7 1.3 collective-permute-start.2
  13.0 18.0 %collective-permute-done.4.refs_2_ = bf16[1,2,512,512]{3,2,1,0:T(8,128)(2,1)S(1)} collective-permute-done((bf16[1,2,512,512]{3,2,1,0:T(8,128)(2,1)S(1)}, bf16[1,2,512,512]{3,2,1,0:T(8,128)(2,1)S(1)}, u32[]{:S(2)}, u32[]{:S(2)}) %collective-permute-start.4) | collective-permute-done | bytes 1048608 | tf_op jit(solution)/shard_map/ppermute | solution.py:269
  31.1 22.5 %collective-permute-done.2.refs_3_ = bf16[1,2,512,512]{3,2,1,0:T(8,128)(2,1)S(1)} collective-permute-done((bf16[1,2,512,512]{3,2,1,0:T(8,128)(2,1)S(1)}, bf16[1,2,512,512]{3,2,1,0:T(8,128)(2,1)S(1)}, u32[]{:S(2)}, u32[]{:S(2)}) %collective-permute-start.2) | collective-permute-done | bytes 1048608 | tf_op jit(solution)/shard_map/ppermute | solution.py:269
  53.5 1.0 copy-done.9
  54.5 21.5 %collective-permute-done.5.refs_4_ = bf16[1,2,512,512]{3,2,1,0:T(8,128)(2,1)S(1)} collective-permute-done((bf16[1,2,512,512]{3,2,1,0:T(8,128)(2,1)S(1)}, bf16[1,2,512,512]{3,2,1,0:T(8,128)(2,1)S(1)}, u32[]{:S(2)}, u32[]{:S(2)}) %collective-permute-start.5) | collective-permute-done | bytes 1048608 | tf_op jit(solution)/shard_map/ppermute | solution.py:269
  76.0 1.0 copy-done.11
  77.0 21.6 %collective-permute-done.3.refs_5_ = bf16[1,2,512,512]{3,2,1,0:T(8,128)(2,1)} collective-permute-done((bf16[1,2,512,512]{3,2,1,0:T(8,128)(2,1)S(1)}, bf16[1,2,512,512]{3,2,1,0:T(8,128)(2,1)}, u32[]{:S(2)}, u32[]{:S(2)}) %collective-permute-start.3) | collective-permute-done | bytes 1048608 | tf_op jit(solution)/shard_map/ppermute | solution.py:269
  98.6 22.4 %collective-permute-done.6.refs_6_ = bf16[1,2,512,512]{3,2,1,0:T(8,128)(2,1)S(1)} collective-permute-done((bf16[1,2,512,512]{3,2,1,0:T(8,128)(2,1)S(1)}, bf16[1,2,512,512]{3,2,1,0:T(8,128)(2,1)S(1)}, u32[]{:S(2)}, u32[]{:S(2)}) %collective-permute-start.6) | collective-permute-done | bytes 1048608 | tf_op jit(solution)/shard_map/ppermute | solution.py:269
  121.0 1.0 copy-done.13
  122.0 0.6 collective-permute-start.7
  122.6 0.1 pad_add_fusion.1.block_ref
  122.7 1.7 fusion
  124.4 0.8 collective-permute-start.9
  125.2 24.3 %collective-permute-done.8.refs_7_ = bf16[1,2,512,512]{3,2,1,0:T(8,128)(2,1)} collective-permute-done((bf16[1,2,512,512]{3,2,1,0:T(8,128)(2,1)}, bf16[1,2,512,512]{3,2,1,0:T(8,128)(2,1)}, u32[]{:S(2)}, u32[]{:S(2)}) %collective-permute-start.8) | collective-permute-done | bytes 1048608 | tf_op jit(solution)/shard_map/ppermute | solution.py:269
  149.5 5.3 %maximum_select_fusion.1 = bf16[1,2,2,512,1024]{4,3,2,1,0:T(8,128)(2,1)S(1)} fusion(bf16[1,2,2,256,1024]{4,3,2,1,0:T(8,128)(2,1)} %bitcast.10, bf16[1,2,2,256,1024]{4,3,2,1,0:T(8,128)(2,1)} %bitcast.9, pred[]{:T(512)S(6)} %eq.23), kind=kLoop, calls=%fused_computation.1 | loop fusion | flops 18874368 | bytes 8388609 | tf_op jit(solution)/shard_map/jit(_where)/select_n | solution.py:273
  154.8 4.1 %maximum_select_fusion.site_ref = bf16[2,2,2,512,1024]{4,3,2,1,0:T(8,128)(2,1)} fusion(bf16[1,2,2,512,1024]{4,3,2,1,0:T(8,128)(2,1)S(1)} %maximum_select_fusion.1, bf16[1,2,2,512,1024]{4,3,2,1,0:T(8,128)(2,1)S(1)} %bitcast.15, pred[]{:T(512)S(6)} %eq.22), kind=kLoop, calls=%fused_computation | loop fusion | flops 12582912 | bytes 16777216 | tf_op jit(solution)/shard_map/jit(_where)/select_n | solution.py:290
  159.0 23.5 %first_product.1.own_ref = bf16[2,2,2,512,512]{4,3,2,1,0:T(8,128)(2,1)S(1)} custom-call(s32[4]{0:T(128)S(1)} %pad_add_fusion.1.block_ref, f32[2,2,2,2]{3,2,1,0:T(2,128)S(1)} %pad_maximum_fusion.mpo_ref, bf16[2,2,2,512,1024]{4,3,2,1,0:T(8,128)(2,1)} %maximum_select_fusion.site_ref, bf16[1,2,512,512]{3,2,1,0:T(8,128)(2,1)S(1)} %get-tuple-element.31.refs_0_, ...), custom_call_target="tpu_custom_call" | custom-call | tf_op jit(solution)/shard_map/first_product/pallas_call | solution.py:67
  182.5 0.0 copy-start
  182.5 11.8 %collective-permute-done.10.refs_1_ = bf16[2,2,128,1024]{3,2,1,0:T(8,128)(2,1)S(1)} collective-permute-done((bf16[2,2,128,1024]{3,2,1,0:T(8,128)(2,1)S(1)}, bf16[2,2,128,1024]{3,2,1,0:T(8,128)(2,1)S(1)}, u32[]{:S(2)}, u32[]{:S(2)}) %collective-permute-start.10) | collective-permute-done | bytes 1048608 | tf_op jit(solution)/shard_map/ppermute | solution.py:269
  194.3 0.8 collective-permute-start.11
  195.1 6.8 %collective-permute-done.11.sib_ref = bf16[2,2,2,512,512]{4,3,2,1,0:T(8,128)(2,1)S(1)} collective-permute-done((bf16[2,2,2,512,512]{4,3,2,1,0:T(8,128)(2,1)S(1)}, bf16[2,2,2,512,512]{4,3,2,1,0:T(8,128)(2,1)S(1)}, u32[]{:S(2)}, u32[]{:S(2)}) %collective-permute-start.11) | collective-permute-done | bytes 4194336 | tf_op jit(solution)/shard_map/ppermute | solution.py:210
  201.9 4.8 %second_product.5 = bf16[2,2,512,256]{3,2,1,0:T(8,128)(2,1)S(1)} custom-call(s32[1]{0:T(128)} %bitcast.1.pick_ref, bf16[2,2,2,512,512]{4,3,2,1,0:T(8,128)(2,1)S(1)} %first_product.1.own_ref, bf16[2,2,2,512,512]{4,3,2,1,0:T(8,128)(2,1)S(1)} %collective-permute-done.11.sib_ref, bf16[2,2,128,1024]{3,2,1,0:T(8,128)(2,1)S(1)} %get-tuple-element.17.refs_0_, ...), custom_call_target="tpu_custom_call" | custom-call | tf_op jit(solution)/shard_map/second_product/pallas_call | solution.py:104
  206.7 1.3 collective-permute-start.13
  208.0 0.1 collective-permute-start.14
  208.1 13.7 %collective-permute-done.12.refs_0_ = bf16[2,2,128,1024]{3,2,1,0:T(8,128)(2,1)} collective-permute-done((bf16[2,2,128,1024]{3,2,1,0:T(8,128)(2,1)S(1)}, bf16[2,2,128,1024]{3,2,1,0:T(8,128)(2,1)}, u32[]{:S(2)}, u32[]{:S(2)}) %collective-permute-start.12) | collective-permute-done | bytes 1048608 | tf_op jit(solution)/shard_map/ppermute | solution.py:269
  221.8 4.9 %second_product.6 = bf16[2,2,512,256]{3,2,1,0:T(8,128)(2,1)S(1)} custom-call(s32[1]{0:T(128)} %bitcast.1.pick_ref, bf16[2,2,2,512,512]{4,3,2,1,0:T(8,128)(2,1)S(1)} %first_product.1.own_ref, bf16[2,2,2,512,512]{4,3,2,1,0:T(8,128)(2,1)S(1)} %collective-permute-done.11.sib_ref, bf16[2,2,128,1024]{3,2,1,0:T(8,128)(2,1)S(1)} %collective-permute-done.9.refs_0_, ...), custom_call_target="tpu_custom_call" | custom-call | tf_op jit(solution)/shard_map/second_product/pallas_call | solution.py:104
  226.7 4.1 %collective-permute-start.19 = (bf16[2,2,512,256]{3,2,1,0:T(8,128)(2,1)S(1)}, bf16[2,2,512,256]{3,2,1,0:T(8,128)(2,1)}, u32[]{:S(2)}, u32[]{:S(2)}) collective-permute-start(bf16[2,2,512,256]{3,2,1,0:T(8,128)(2,1)S(1)} %second_product.6), channel_id=1, source_target_pairs={{0,2},{1,3},{6,4},{7,5},{10,8},{11,9},{12,14},{13,15},{16,18},{17,... | collective-permute-start | bytes 3145736 | tf_op jit(solution)/shard_map/ppermute | solution.py:312
  230.8 2.3 collective-permute-done.13
  233.1 11.1 %collective-permute-done.14.refs_1_ = bf16[2,2,128,1024]{3,2,1,0:T(8,128)(2,1)} collective-permute-done((bf16[2,2,128,1024]{3,2,1,0:T(8,128)(2,1)S(1)}, bf16[2,2,128,1024]{3,2,1,0:T(8,128)(2,1)}, u32[]{:S(2)}, u32[]{:S(2)}) %collective-permute-start.14) | collective-permute-done | bytes 1048608 | tf_op jit(solution)/shard_map/ppermute | solution.py:269
  244.3 6.4 %second_product.7 = bf16[2,2,512,256]{3,2,1,0:T(8,128)(2,1)S(1)} custom-call(s32[1]{0:T(128)} %bitcast.1.pick_ref, bf16[2,2,2,512,512]{4,3,2,1,0:T(8,128)(2,1)S(1)} %first_product.1.own_ref, bf16[2,2,2,512,512]{4,3,2,1,0:T(8,128)(2,1)S(1)} %collective-permute-done.11.sib_ref, bf16[2,2,128,1024]{3,2,1,0:T(8,128)(2,1)} %collective-permute-done.12.refs_0_, ...), custom_call_target="tpu_custom_call" | custom-call | tf_op jit(solution)/shard_map/second_product/pallas_call | solution.py:104
  250.7 4.1 %collective-permute-start.20 = (bf16[2,2,512,256]{3,2,1,0:T(8,128)(2,1)S(1)}, bf16[2,2,512,256]{3,2,1,0:T(8,128)(2,1)}, u32[]{:S(2)}, u32[]{:S(2)}) collective-permute-start(bf16[2,2,512,256]{3,2,1,0:T(8,128)(2,1)S(1)} %second_product.7), channel_id=1, source_target_pairs={{0,2},{1,3},{4,6},{5,7},{10,8},{11,9},{14,12},{15,13},{16,18},{17,... | collective-permute-start | bytes 3145736 | tf_op jit(solution)/shard_map/ppermute | solution.py:312
  254.8 11.9 %collective-permute-done.15.refs_0_ = bf16[2,2,128,1024]{3,2,1,0:T(8,128)(2,1)} collective-permute-done((bf16[2,2,128,1024]{3,2,1,0:T(8,128)(2,1)}, bf16[2,2,128,1024]{3,2,1,0:T(8,128)(2,1)}, u32[]{:S(2)}, u32[]{:S(2)}) %collective-permute-start.15) | collective-permute-done | bytes 1048608 | tf_op jit(solution)/shard_map/ppermute | solution.py:269
  266.7 2.2 copy-done.1
  268.9 2.2 copy-done.3
  271.1 4.0 %second_product.8.refs_0_ = bf16[2,2,512,128]{3,2,1,0:T(8,128)(2,1)S(1)} custom-call(s32[1]{0:T(128)} %bitcast.1.pick_ref, bf16[2,2,2,512,512]{4,3,2,1,0:T(8,128)(2,1)S(1)} %copy-done.1, bf16[2,2,2,512,512]{4,3,2,1,0:T(8,128)(2,1)S(1)} %copy-done.3, bf16[2,2,128,1024]{3,2,1,0:T(8,128)(2,1)} %collective-permute-done.15.refs_0_), custom_call_target="tpu_custom_call" | custom-call | tf_op jit(solution)/shard_map/second_product/pallas_call | solution.py:104
  275.1 1.3 collective-permute-start.16
  276.4 1.3 collective-permute-start.17
  277.7 1.3 collective-permute-start.18
  279.1 3.8 %select_convert_fusion = (bf16[2,2,512,256]{3,2,1,0:T(8,128)(2,1)}, f32[2,2,512,256]{3,2,1,0:T(8,128)S(1)}) fusion(bf16[2,2,512,256]{3,2,1,0:T(8,128)(2,1)S(1)} %copy-done.25, bf16[2,2,512,256]{3,2,1,0:T(8,128)(2,1)S(1)} %second_product.5, bf16[2,2,512,256]{3,2,1,0:T(8,128)(2,1)} %collective-permute-done.19, bf16[2,2,512,256]{3,2,1,0:T(8,128)(2,1)S(1)} %copy-done.5, ...), kind=kLoop, calls=%fused_computation.2 | loop fusion | flops 7340032 | bytes 9437188 | tf_op jit(solution)/shard_map/convert_element_type | solution.py:346
  282.9 1.2 collective-permute-start.25
  284.0 5.1 %collective-permute-done.16.refs_1_ = bf16[2,2,512,128]{3,2,1,0:T(8,128)(2,1)S(1)} collective-permute-done((bf16[2,2,512,128]{3,2,1,0:T(8,128)(2,1)S(1)}, bf16[2,2,512,128]{3,2,1,0:T(8,128)(2,1)S(1)}, u32[]{:S(2)}, u32[]{:S(2)}) %collective-permute-start.16) | collective-permute-done | bytes 524320 | tf_op jit(solution)/shard_map/ppermute | solution.py:319
  289.1 1.5 collective-permute-done.17.refs_2_
  290.7 0.8 copy-done.17
  291.5 4.1 %second_product.9.refs_0_ = bf16[2,2,512,128]{3,2,1,0:T(8,128)(2,1)S(1)} custom-call(s32[1]{0:T(128)} %bitcast.1.pick_ref, bf16[2,2,2,512,512]{4,3,2,1,0:T(8,128)(2,1)S(1)} %copy-done.1, bf16[2,2,2,512,512]{4,3,2,1,0:T(8,128)(2,1)S(1)} %copy-done.3, bf16[2,2,128,1024]{3,2,1,0:T(8,128)(2,1)} %collective-permute-done.21.refs_0_), custom_call_target="tpu_custom_call" | custom-call | tf_op jit(solution)/shard_map/second_product/pallas_call | solution.py:104
  295.6 1.3 collective-permute-start.22
  296.9 1.3 collective-permute-start.23
  298.2 1.3 collective-permute-start.24
  299.5 0.1 pad_add_fusion.pick_ref
  299.6 1.0 copy-done.16
  300.6 1.0 copy-done.18
  301.6 1.0 copy-done.20
  302.7 4.0 %finish.1.refs_4_ = f32[2,2,512,512]{3,2,1,0:T(8,128)} custom-call(s32[2]{0:T(128)S(1)} %pad_add_fusion.pick_ref, f32[2,2,512,256]{3,2,1,0:T(8,128)S(1)} %get-tuple-element.26.mine_ref, bf16[2,2,512,256]{3,2,1,0:T(8,128)(2,1)} %collective-permute-done.25.siblings_ref, bf16[2,2,512,128]{3,2,1,0:T(8,128)(2,1)S(1)} %copy-done.8, ...), custom_call_target="tpu_custom_call" | custom-call | tf_op jit(solution)/shard_map/finish/pallas_call | solution.py:145
  306.6 2.6 collective-permute-done.22.refs_1_
  309.3 1.9 collective-permute-done.23.refs_2_
  311.2 2.8 finish_last.1
  (61 shorter events, 0.1 us)
Async XLA Ops:
  2.7 2.9 collective-permute-start
  2.8 28.3 %collective-permute-start.4 = (bf16[1,2,512,512]{3,2,1,0:T(8,128)(2,1)S(1)}, bf16[1,2,512,512]{3,2,1,0:T(8,128)(2,1)S(1)}, u32[]{:S(2)}, u32[]{:S(2)}) collective-permute-start(bf16[1,2,512,512]{3,2,1,0:T(8,128)(2,1)S(1)} %get-tuple-element.31.refs_0_), channel_id=1, source_target_pairs={{0,4},{4,8},{8,12},{12,0},{1,5},{5,9},{9,13},{13,1},{2,6},{6,10},{... | collective-permute-start | bytes 3145736 | tf_op jit(solution)/shard_map/ppermute | solution.py:269
  9.1 111.9 %copy-start.21 = (bf16[2,512,2,1024]{3,1,2,0:T(8,128)(2,1)}, bf16[2,512,2,1024]{3,1,2,0:T(8,128)(2,1)S(1)}, u32[]{:S(2)}) copy-start(bf16[2,512,2,1024]{3,1,2,0:T(8,128)(2,1)S(1)} %copy.9) | copy-start | bytes 12582916
  9.1 113.6 %copy-start.26 = (f32[2,2,2,2]{3,2,1,0:T(2,128)S(1)}, f32[2,2,2,2]{3,2,1,0:T(2,128)}, u32[]{:S(2)}) copy-start(f32[2,2,2,2]{3,2,1,0:T(2,128)} %param.5) | copy-start | bytes 196
  9.3 113.3 %copy-start.23 = (bf16[2,2,256,1024]{3,2,1,0:T(8,128)(2,1)}, bf16[2,2,256,1024]{3,2,1,0:T(8,128)(2,1)S(1)}, u32[]{:S(2)}) copy-start(bf16[2,2,256,1024]{3,2,1,0:T(8,128)(2,1)S(1)} %dynamic-slice_bitcast_fusion) | copy-start | bytes 6291460
  9.3 67.7 %collective-permute-start.1 = (bf16[2,2,256,1024]{3,2,1,0:T(8,128)(2,1)S(1)}, bf16[2,2,256,1024]{3,2,1,0:T(8,128)(2,1)}, u32[]{:S(2)}, u32[]{:S(2)}) collective-permute-start(bf16[2,2,256,1024]{3,2,1,0:T(8,128)(2,1)S(1)} %dynamic-slice_bitcast_fusion), channel_id=1, source_target_pairs={{0,2},{2,0},{1,3},{3,1},{4,6},{6,4},{5,7},{7,5},{8,10},{10,8},{9,1... | collective-permute-start | bytes 6291464 | tf_op jit(solution)/shard_map/ppermute | solution.py:272
  11.7 41.8 %collective-permute-start.2 = (bf16[1,2,512,512]{3,2,1,0:T(8,128)(2,1)S(1)}, bf16[1,2,512,512]{3,2,1,0:T(8,128)(2,1)S(1)}, u32[]{:S(2)}, u32[]{:S(2)}) collective-permute-start(bf16[1,2,512,512]{3,2,1,0:T(8,128)(2,1)S(1)} %collective-permute-done.refs_1_), channel_id=1, source_target_pairs={{0,4},{4,8},{8,12},{12,0},{1,5},{5,9},{9,13},{13,1},{2,6},{6,10},{... | collective-permute-start | bytes 3145736 | tf_op jit(solution)/shard_map/ppermute | solution.py:269
  31.1 44.9 %collective-permute-start.5 = (bf16[1,2,512,512]{3,2,1,0:T(8,128)(2,1)S(1)}, bf16[1,2,512,512]{3,2,1,0:T(8,128)(2,1)S(1)}, u32[]{:S(2)}, u32[]{:S(2)}) collective-permute-start(bf16[1,2,512,512]{3,2,1,0:T(8,128)(2,1)S(1)} %collective-permute-done.4.refs_2_), channel_id=1, source_target_pairs={{0,4},{4,8},{8,12},{12,0},{1,5},{5,9},{9,13},{13,1},{2,6},{6,10},{... | collective-permute-start | bytes 3145736 | tf_op jit(solution)/shard_map/ppermute | solution.py:269
  53.5 45.0 %collective-permute-start.3 = (bf16[1,2,512,512]{3,2,1,0:T(8,128)(2,1)S(1)}, bf16[1,2,512,512]{3,2,1,0:T(8,128)(2,1)}, u32[]{:S(2)}, u32[]{:S(2)}) collective-permute-start(bf16[1,2,512,512]{3,2,1,0:T(8,128)(2,1)S(1)} %collective-permute-done.2.refs_3_), channel_id=1, source_target_pairs={{0,4},{4,8},{8,12},{12,0},{1,5},{5,9},{9,13},{13,1},{2,6},{6,10},{... | collective-permute-start | bytes 3145736 | tf_op jit(solution)/shard_map/ppermute | solution.py:269
  53.5 1.0 copy-start.9
  76.0 44.9 %collective-permute-start.6 = (bf16[1,2,512,512]{3,2,1,0:T(8,128)(2,1)S(1)}, bf16[1,2,512,512]{3,2,1,0:T(8,128)(2,1)S(1)}, u32[]{:S(2)}, u32[]{:S(2)}) collective-permute-start(bf16[1,2,512,512]{3,2,1,0:T(8,128)(2,1)S(1)} %collective-permute-done.5.refs_4_), channel_id=1, source_target_pairs={{0,4},{4,8},{8,12},{12,0},{1,5},{5,9},{9,13},{13,1},{2,6},{6,10},{... | collective-permute-start | bytes 3145736 | tf_op jit(solution)/shard_map/ppermute | solution.py:269
  76.0 1.0 copy-start.11
  120.9 1.0 copy-start.13
  122.0 27.5 %collective-permute-start.7 = (bf16[2,2,256,1024]{3,2,1,0:T(8,128)(2,1)}, bf16[2,2,256,1024]{3,2,1,0:T(8,128)(2,1)}, u32[]{:S(2)}, u32[]{:S(2)}) collective-permute-start(bf16[2,2,256,1024]{3,2,1,0:T(8,128)(2,1)} %collective-permute-done.1), channel_id=1, source_target_pairs={{0,1},{1,0},{2,3},{3,2},{4,5},{5,4},{6,7},{7,6},{8,9},{9,8},{10,11... | collective-permute-start | bytes 6291464 | tf_op jit(solution)/shard_map/ppermute | solution.py:210
  122.6 26.9 %collective-permute-start.8 = (bf16[1,2,512,512]{3,2,1,0:T(8,128)(2,1)}, bf16[1,2,512,512]{3,2,1,0:T(8,128)(2,1)}, u32[]{:S(2)}, u32[]{:S(2)}) collective-permute-start(bf16[1,2,512,512]{3,2,1,0:T(8,128)(2,1)} %collective-permute-done.3.refs_5_), channel_id=1, source_target_pairs={{0,4},{4,8},{8,12},{12,0},{1,5},{5,9},{9,13},{13,1},{2,6},{6,10},{... | collective-permute-start | bytes 3145736 | tf_op jit(solution)/shard_map/ppermute | solution.py:269
  124.4 58.1 %collective-permute-start.9 = (bf16[2,2,128,1024]{3,2,1,0:T(8,128)(2,1)S(1)}, bf16[2,2,128,1024]{3,2,1,0:T(8,128)(2,1)S(1)}, u32[]{:S(2)}, u32[]{:S(2)}) collective-permute-start(bf16[2,2,128,1024]{3,2,1,0:T(8,128)(2,1)S(1)} %get-tuple-element.17.refs_0_), channel_id=1, source_target_pairs={{0,4},{4,8},{8,12},{12,0},{1,5},{5,9},{9,13},{13,1},{2,6},{6,10},{... | collective-permute-start | bytes 3145736 | tf_op jit(solution)/shard_map/ppermute | solution.py:269
  149.5 44.8 %collective-permute-start.10 = (bf16[2,2,128,1024]{3,2,1,0:T(8,128)(2,1)S(1)}, bf16[2,2,128,1024]{3,2,1,0:T(8,128)(2,1)S(1)}, u32[]{:S(2)}, u32[]{:S(2)}) collective-permute-start(bf16[2,2,128,1024]{3,2,1,0:T(8,128)(2,1)S(1)} %get-tuple-element.18.refs_1_), channel_id=1, source_target_pairs={{0,4},{4,8},{8,12},{12,0},{1,5},{5,9},{9,13},{13,1},{2,6},{6,10},{... | collective-permute-start | bytes 3145736 | tf_op jit(solution)/shard_map/ppermute | solution.py:269
  149.5 5.3 %copy-start.22 = (bf16[2,512,2,1024]{3,1,2,0:T(8,128)(2,1)S(1)}, bf16[2,512,2,1024]{3,1,2,0:T(8,128)(2,1)}, u32[]{:S(2)}) copy-start(bf16[2,512,2,1024]{3,1,2,0:T(8,128)(2,1)} %copy-done.21) | copy-start | bytes 12582916
  154.8 4.2 %copy-start.10 = (bf16[1,2,512,512]{3,2,1,0:T(8,128)(2,1)S(1)}, bf16[1,2,512,512]{3,2,1,0:T(8,128)(2,1)}, u32[]{:S(2)}) copy-start(bf16[1,2,512,512]{3,2,1,0:T(8,128)(2,1)} %copy-done.9) | copy-start | bytes 3145732
  154.8 4.2 %copy-start.12 = (bf16[1,2,512,512]{3,2,1,0:T(8,128)(2,1)S(1)}, bf16[1,2,512,512]{3,2,1,0:T(8,128)(2,1)}, u32[]{:S(2)}) copy-start(bf16[1,2,512,512]{3,2,1,0:T(8,128)(2,1)} %copy-done.11) | copy-start | bytes 3145732
  154.8 4.2 %copy-start.14 = (bf16[1,2,512,512]{3,2,1,0:T(8,128)(2,1)S(1)}, bf16[1,2,512,512]{3,2,1,0:T(8,128)(2,1)}, u32[]{:S(2)}) copy-start(bf16[1,2,512,512]{3,2,1,0:T(8,128)(2,1)} %copy-done.13) | copy-start | bytes 3145732
  182.5 61.8 %copy-start = (bf16[2,2,2,512,512]{4,3,2,1,0:T(8,128)(2,1)}, bf16[2,2,2,512,512]{4,3,2,1,0:T(8,128)(2,1)S(1)}, u32[]{:S(2)}) copy-start(bf16[2,2,2,512,512]{4,3,2,1,0:T(8,128)(2,1)S(1)} %first_product.1.own_ref) | copy-start | bytes 12582916
  194.3 7.6 %collective-permute-start.11 = (bf16[2,2,2,512,512]{4,3,2,1,0:T(8,128)(2,1)S(1)}, bf16[2,2,2,512,512]{4,3,2,1,0:T(8,128)(2,1)S(1)}, u32[]{:S(2)}, u32[]{:S(2)}) collective-permute-start(bf16[2,2,2,512,512]{4,3,2,1,0:T(8,128)(2,1)S(1)} %first_product.1.own_ref), channel_id=1, source_target_pairs={{0,1},{1,0},{2,3},{3,2},{4,5},{5,4},{6,7},{7,6},{8,9},{9,8},{10,11... | collective-permute-start | bytes 12582920 | tf_op jit(solution)/shard_map/ppermute | solution.py:210
  195.1 26.7 %collective-permute-start.12 = (bf16[2,2,128,1024]{3,2,1,0:T(8,128)(2,1)S(1)}, bf16[2,2,128,1024]{3,2,1,0:T(8,128)(2,1)}, u32[]{:S(2)}, u32[]{:S(2)}) collective-permute-start(bf16[2,2,128,1024]{3,2,1,0:T(8,128)(2,1)S(1)} %collective-permute-done.9.refs_0_), channel_id=1, source_target_pairs={{0,4},{4,8},{8,12},{12,0},{1,5},{5,9},{9,13},{13,1},{2,6},{6,10},{... | collective-permute-start | bytes 3145736 | tf_op jit(solution)/shard_map/ppermute | solution.py:269
  201.9 42.4 %copy-start.2 = (bf16[2,2,2,512,512]{4,3,2,1,0:T(8,128)(2,1)}, bf16[2,2,2,512,512]{4,3,2,1,0:T(8,128)(2,1)S(1)}, u32[]{:S(2)}) copy-start(bf16[2,2,2,512,512]{4,3,2,1,0:T(8,128)(2,1)S(1)} %collective-permute-done.11.sib_ref) | copy-start | bytes 12582916
  206.7 26.4 %collective-permute-start.13 = (bf16[2,2,512,256]{3,2,1,0:T(8,128)(2,1)S(1)}, bf16[2,2,512,256]{3,2,1,0:T(8,128)(2,1)S(1)}, u32[]{:S(2)}, u32[]{:S(2)}) collective-permute-start(bf16[2,2,512,256]{3,2,1,0:T(8,128)(2,1)S(1)} %second_product.5), channel_id=1, source_target_pairs={{2,0},{3,1},{6,4},{7,5},{8,10},{9,11},{12,14},{13,15},{18,16},{19,... | collective-permute-start | bytes 3145736 | tf_op jit(solution)/shard_map/ppermute | solution.py:312
  208.0 36.2 %collective-permute-start.14 = (bf16[2,2,128,1024]{3,2,1,0:T(8,128)(2,1)S(1)}, bf16[2,2,128,1024]{3,2,1,0:T(8,128)(2,1)}, u32[]{:S(2)}, u32[]{:S(2)}) collective-permute-start(bf16[2,2,128,1024]{3,2,1,0:T(8,128)(2,1)S(1)} %collective-permute-done.10.refs_1_), channel_id=1, source_target_pairs={{0,4},{4,8},{8,12},{12,0},{1,5},{5,9},{9,13},{13,1},{2,6},{6,10},{... | collective-permute-start | bytes 3145736 | tf_op jit(solution)/shard_map/ppermute | solution.py:269
  221.8 44.9 %collective-permute-start.15 = (bf16[2,2,128,1024]{3,2,1,0:T(8,128)(2,1)}, bf16[2,2,128,1024]{3,2,1,0:T(8,128)(2,1)}, u32[]{:S(2)}, u32[]{:S(2)}) collective-permute-start(bf16[2,2,128,1024]{3,2,1,0:T(8,128)(2,1)} %collective-permute-done.12.refs_0_), channel_id=1, source_target_pairs={{0,4},{4,8},{8,12},{12,0},{1,5},{5,9},{9,13},{13,1},{2,6},{6,10},{... | collective-permute-start | bytes 3145736 | tf_op jit(solution)/shard_map/ppermute | solution.py:269
  226.7 24.0 %copy-start.4 = (bf16[2,2,512,256]{3,2,1,0:T(8,128)(2,1)}, bf16[2,2,512,256]{3,2,1,0:T(8,128)(2,1)S(1)}, u32[]{:S(2)}) copy-start(bf16[2,2,512,256]{3,2,1,0:T(8,128)(2,1)S(1)} %second_product.6) | copy-start | bytes 3145732
  226.7 51.1 %collective-permute-start.19 = (bf16[2,2,512,256]{3,2,1,0:T(8,128)(2,1)S(1)}, bf16[2,2,512,256]{3,2,1,0:T(8,128)(2,1)}, u32[]{:S(2)}, u32[]{:S(2)}) collective-permute-start(bf16[2,2,512,256]{3,2,1,0:T(8,128)(2,1)S(1)} %second_product.6), channel_id=1, source_target_pairs={{0,2},{1,3},{6,4},{7,5},{10,8},{11,9},{12,14},{13,15},{16,18},{17,... | collective-permute-start | bytes 3145736 | tf_op jit(solution)/shard_map/ppermute | solution.py:312
  233.1 17.6 %copy-start.24 = (bf16[2,2,512,256]{3,2,1,0:T(8,128)(2,1)}, bf16[2,2,512,256]{3,2,1,0:T(8,128)(2,1)S(1)}, u32[]{:S(2)}) copy-start(bf16[2,2,512,256]{3,2,1,0:T(8,128)(2,1)S(1)} %collective-permute-done.13) | copy-start | bytes 3145732
  250.7 24.4 %copy-start.6 = (bf16[2,2,512,256]{3,2,1,0:T(8,128)(2,1)}, bf16[2,2,512,256]{3,2,1,0:T(8,128)(2,1)S(1)}, u32[]{:S(2)}) copy-start(bf16[2,2,512,256]{3,2,1,0:T(8,128)(2,1)S(1)} %second_product.7) | copy-start | bytes 3145732
  250.7 28.3 %collective-permute-start.20 = (bf16[2,2,512,256]{3,2,1,0:T(8,128)(2,1)S(1)}, bf16[2,2,512,256]{3,2,1,0:T(8,128)(2,1)}, u32[]{:S(2)}, u32[]{:S(2)}) collective-permute-start(bf16[2,2,512,256]{3,2,1,0:T(8,128)(2,1)S(1)} %second_product.7), channel_id=1, source_target_pairs={{0,2},{1,3},{4,6},{5,7},{10,8},{11,9},{14,12},{15,13},{16,18},{17,... | collective-permute-start | bytes 3145736 | tf_op jit(solution)/shard_map/ppermute | solution.py:312
  254.8 36.7 %collective-permute-start.21 = (bf16[2,2,128,1024]{3,2,1,0:T(8,128)(2,1)}, bf16[2,2,128,1024]{3,2,1,0:T(8,128)(2,1)}, u32[]{:S(2)}, u32[]{:S(2)}) collective-permute-start(bf16[2,2,128,1024]{3,2,1,0:T(8,128)(2,1)} %collective-permute-done.14.refs_1_), channel_id=1, source_target_pairs={{0,4},{4,8},{8,12},{12,0},{1,5},{5,9},{9,13},{13,1},{2,6},{6,10},{... | collective-permute-start | bytes 3145736 | tf_op jit(solution)/shard_map/ppermute | solution.py:269
  266.7 2.2 copy-start.1
  268.9 2.2 copy-start.3
  271.1 7.9 %copy-start.5 = (bf16[2,2,512,256]{3,2,1,0:T(8,128)(2,1)S(1)}, bf16[2,2,512,256]{3,2,1,0:T(8,128)(2,1)}, u32[]{:S(2)}) copy-start(bf16[2,2,512,256]{3,2,1,0:T(8,128)(2,1)} %copy-done.4) | copy-start | bytes 3145732
  271.1 7.9 %copy-start.25 = (bf16[2,2,512,256]{3,2,1,0:T(8,128)(2,1)S(1)}, bf16[2,2,512,256]{3,2,1,0:T(8,128)(2,1)}, u32[]{:S(2)}) copy-start(bf16[2,2,512,256]{3,2,1,0:T(8,128)(2,1)} %copy-done.24) | copy-start | bytes 3145732
  275.1 7.7 %copy-start.7 = (bf16[2,2,512,128]{3,2,1,0:T(8,128)(2,1)}, bf16[2,2,512,128]{3,2,1,0:T(8,128)(2,1)S(1)}, u32[]{:S(2)}) copy-start(bf16[2,2,512,128]{3,2,1,0:T(8,128)(2,1)S(1)} %second_product.8.refs_0_) | copy-start | bytes 1572868
  275.1 14.0 %collective-permute-start.16 = (bf16[2,2,512,128]{3,2,1,0:T(8,128)(2,1)S(1)}, bf16[2,2,512,128]{3,2,1,0:T(8,128)(2,1)S(1)}, u32[]{:S(2)}, u32[]{:S(2)}) collective-permute-start(bf16[2,2,512,128]{3,2,1,0:T(8,128)(2,1)S(1)} %second_product.8.refs_0_), channel_id=1, source_target_pairs={{3,1},{4,6},{9,11},{14,12},{19,17},{20,22},{25,27},{30,28}} | collective-permute-start | bytes 1572872 | tf_op jit(solution)/shard_map/ppermute | solution.py:319
  276.4 14.2 %collective-permute-start.17 = (bf16[2,2,512,128]{3,2,1,0:T(8,128)(2,1)S(1)}, bf16[2,2,512,128]{3,2,1,0:T(8,128)(2,1)S(1)}, u32[]{:S(2)}, u32[]{:S(2)}) collective-permute-start(bf16[2,2,512,128]{3,2,1,0:T(8,128)(2,1)S(1)} %second_product.8.refs_0_), channel_id=1, source_target_pairs={{2,1},{5,6},{8,11},{15,12},{18,17},{21,22},{24,27},{31,28}} | collective-permute-start | bytes 1572872 | tf_op jit(solution)/shard_map/ppermute | solution.py:319
  277.7 13.7 %collective-permute-start.18 = (bf16[2,2,512,128]{3,2,1,0:T(8,128)(2,1)S(1)}, bf16[2,2,512,128]{3,2,1,0:T(8,128)(2,1)S(1)}, u32[]{:S(2)}, u32[]{:S(2)}) collective-permute-start(bf16[2,2,512,128]{3,2,1,0:T(8,128)(2,1)S(1)} %second_product.8.refs_0_), channel_id=1, source_target_pairs={{0,1},{7,6},{10,11},{13,12},{16,17},{23,22},{26,27},{29,28}} | collective-permute-start | bytes 1572872 | tf_op jit(solution)/shard_map/ppermute | solution.py:319
  282.9 16.7 %collective-permute-start.25 = (bf16[2,2,512,256]{3,2,1,0:T(8,128)(2,1)}, bf16[2,2,512,256]{3,2,1,0:T(8,128)(2,1)}, u32[]{:S(2)}, u32[]{:S(2)}) collective-permute-start(bf16[2,2,512,256]{3,2,1,0:T(8,128)(2,1)} %get-tuple-element.25), channel_id=1, source_target_pairs={{0,1},{1,0},{2,3},{3,2},{4,5},{5,4},{6,7},{7,6},{8,9},{9,8},{10,11... | collective-permute-start | bytes 3145736 | tf_op jit(solution)/shard_map/ppermute | solution.py:210
  289.1 6.4 %copy-start.15 = (bf16[2,2,512,128]{3,2,1,0:T(8,128)(2,1)}, bf16[2,2,512,128]{3,2,1,0:T(8,128)(2,1)S(1)}, u32[]{:S(2)}) copy-start(bf16[2,2,512,128]{3,2,1,0:T(8,128)(2,1)S(1)} %collective-permute-done.16.refs_1_) | copy-start | bytes 1572868
  290.7 0.8 copy-start.17
  291.5 4.1 %copy-start.19 = (bf16[2,2,512,128]{3,2,1,0:T(8,128)(2,1)}, bf16[2,2,512,128]{3,2,1,0:T(8,128)(2,1)S(1)}, u32[]{:S(2)}) copy-start(bf16[2,2,512,128]{3,2,1,0:T(8,128)(2,1)S(1)} %collective-permute-done.18.refs_3_) | copy-start | bytes 1572868
  291.5 8.1 %copy-start.8 = (bf16[2,2,512,128]{3,2,1,0:T(8,128)(2,1)S(1)}, bf16[2,2,512,128]{3,2,1,0:T(8,128)(2,1)}, u32[]{:S(2)}) copy-start(bf16[2,2,512,128]{3,2,1,0:T(8,128)(2,1)} %copy-done.7) | copy-start | bytes 1572868
  295.6 13.7 %collective-permute-start.22 = (bf16[2,2,512,128]{3,2,1,0:T(8,128)(2,1)S(1)}, bf16[2,2,512,128]{3,2,1,0:T(8,128)(2,1)}, u32[]{:S(2)}, u32[]{:S(2)}) collective-permute-start(bf16[2,2,512,128]{3,2,1,0:T(8,128)(2,1)S(1)} %second_product.9.refs_0_), channel_id=1, source_target_pairs={{3,1},{4,6},{9,11},{14,12},{19,17},{20,22},{25,27},{30,28}} | collective-permute-start | bytes 1572872 | tf_op jit(solution)/shard_map/ppermute | solution.py:319
  296.9 14.3 %collective-permute-start.23 = (bf16[2,2,512,128]{3,2,1,0:T(8,128)(2,1)S(1)}, bf16[2,2,512,128]{3,2,1,0:T(8,128)(2,1)}, u32[]{:S(2)}, u32[]{:S(2)}) collective-permute-start(bf16[2,2,512,128]{3,2,1,0:T(8,128)(2,1)S(1)} %second_product.9.refs_0_), channel_id=1, source_target_pairs={{2,1},{5,6},{8,11},{15,12},{18,17},{21,22},{24,27},{31,28}} | collective-permute-start | bytes 1572872 | tf_op jit(solution)/shard_map/ppermute | solution.py:319
  298.2 13.1 %collective-permute-start.24 = (bf16[2,2,512,128]{3,2,1,0:T(8,128)(2,1)S(1)}, bf16[2,2,512,128]{3,2,1,0:T(8,128)(2,1)}, u32[]{:S(2)}, u32[]{:S(2)}) collective-permute-start(bf16[2,2,512,128]{3,2,1,0:T(8,128)(2,1)S(1)} %second_product.9.refs_0_), channel_id=1, source_target_pairs={{0,1},{7,6},{10,11},{13,12},{16,17},{23,22},{26,27},{29,28}} | collective-permute-start | bytes 1572872 | tf_op jit(solution)/shard_map/ppermute | solution.py:319
  299.6 1.0 copy-start.16
  300.6 1.0 copy-start.18
  301.6 1.0 copy-start.20
